TPU v7x, 32 devices: a whole 2x2x4 slice. The times are simulated.
32 devices in a mesh: ctx: 8 (over z, core), head: 4 (over y, x).
Axes of the slice: x: 2, y: 2, z: 4, core: 2. Of those that a mesh axis runs over, the one named last changes fastest.
Arguments:
- activations: bfloat16 [2048, 4096], P('ctx', 'head'), may hold values from -40 to 40
- positions: int32 [2048], P('ctx'), may hold values from 0 to 6143, as said below
- w_query: bfloat16 [4096, 4096], P('ctx', 'head'), may hold values from -0.09375 to 0.09375
- w_key: bfloat16 [4096, 4096], P('ctx', 'head'), may hold values from -0.09375 to 0.09375
- w_value: bfloat16 [4096, 4096], P('ctx', 'head'), may hold values from -0.09375 to 0.09375
- conv_kernel: float32 [32, 66], P('head'), may hold values from -0.6 to 0.6
- head_mix: float32 [32, 4], P('head'), may hold values from -0.45 to 1.45
- out_gain: float32 [4096], P('head'), may hold values from 0.1 to 1.9
- w_out: bfloat16 [4096, 4096], P('head', 'ctx'), may hold values from -0.09375 to 0.09375
Outputs:
- attended: bfloat16 [2048, 4096], P('ctx', 'head')
Inputs may be any that keep to these rules, and one draw needn't show every extreme that they name: `positions`: strictly increasing along the tokens; the first token's is 0 and the last token's is 6143.
All inputs are finite; a program needn't handle non-finite values.
Results may differ from a plain program's by a relative error of at most 0.018.
Values may be sent and summed in bfloat16 or wider, within the bound.
No kernel may reach another device: no remote copies, remote signals or barrier semaphores. Data moves between devices by JAX's collectives and lax.ppermute only.
A program may use at most 128 MiB of HBM per device.

v0:
```python
import math

import jax
import jax.numpy as jnp
from jax import lax
from jax.experimental import pallas as pl
from jax.experimental.pallas import tpu as pltpu
from jax.sharding import PartitionSpec as P

HD = 128
GROUP = 4
CQ = 6
CK = 11
KB = 512


def passed_along(value, axis, steps):
    count = lax.axis_size(axis)
    leading, last = (max(0, -steps), min(count, count - steps))
    return lax.ppermute(value, axis, [(source, source + steps) for source in range(leading, last)])


def rope(projected, positions):
    row_count = projected.shape[0]
    head_count = projected.shape[1] // HD
    shaped = projected.reshape(row_count, head_count, HD)
    half_size = HD // 2
    exponents = jnp.arange(half_size, dtype=jnp.float32) * (2.0 / HD)
    inverse = jnp.exp(-exponents * math.log(500000.0))
    angle = (positions.astype(jnp.float32) * 0.25)[:, None, None] * inverse[None, None, :]
    cosine = jnp.cos(angle)
    sine = jnp.sin(angle)
    lower_half = shaped[..., :half_size]
    upper_half = shaped[..., half_size:]
    rotated_rows = jnp.concatenate(
        [lower_half * cosine - upper_half * sine, upper_half * cosine + lower_half * sine], -1
    )
    return rotated_rows.reshape(row_count, head_count * HD)


def convolve(masked, kernel, row_count, col_count):
    summed = jnp.zeros((masked.shape[0], row_count, col_count), jnp.float32)
    for lag_q in range(CQ):
        for lag_k in range(CK):
            weight = kernel[:, lag_q * CK + lag_k][:, None, None]
            window = masked[
                :,
                CQ - 1 - lag_q : CQ - 1 - lag_q + row_count,
                CK - 1 - lag_k : CK - 1 - lag_k + col_count,
            ]
            summed = summed + weight * window
    return summed


def add_rows(left, piece):
    return jnp.dot(left, piece, preferred_element_type=jnp.float32)


def share_keys(key, value):
    return (
        lax.all_gather(key, "ctx", axis=0, tiled=True),
        lax.all_gather(value, "ctx", axis=0, tiled=True),
    )


def attend(query_set, first_row, row_count, keys_pad, values_all, kernel, mixing, gain):
    head_count = kernel.shape[0]
    ext_rows = row_count + CQ - 1
    query_heads = query_set.reshape(ext_rows, head_count, HD)
    token_total = values_all.shape[0]
    block_count = token_total // KB
    last_row = first_row + row_count - 1
    scale = 1.0 / math.sqrt(HD)
    prow = first_row - (CQ - 1) + jnp.arange(ext_rows, dtype=jnp.int32)
    irow = first_row + jnp.arange(row_count, dtype=jnp.int32)

    def logits_of(block):
        key_start = block * KB
        key_block = lax.dynamic_slice_in_dim(keys_pad, key_start, KB + CK - 1, 0).reshape(
            KB + CK - 1, head_count, HD
        )
        scores = (
            jnp.einsum("rhd,khd->hrk", query_heads, key_block, preferred_element_type=jnp.float32)
            * scale
        )
        kcol = key_start - CK // 2 + jnp.arange(KB + CK - 1, dtype=jnp.int32)
        valid = (kcol[None, :] <= prow[:, None]) & (prow[:, None] >= 0)
        masked = jnp.where(valid[None], scores, 0.0)
        conv = convolve(masked, kernel, row_count, KB)
        jcol = key_start + jnp.arange(KB, dtype=jnp.int32)
        return jnp.where((jcol[None, :] <= irow[:, None])[None], conv, -jnp.inf)

    def first_pass(block, carry_in):

        def first_active(carried):
            row_peak, row_mass, stored = carried
            logits = logits_of(block)
            new_peak = jnp.maximum(row_peak, jnp.max(logits, axis=-1))
            new_mass = row_mass * jnp.exp(row_peak - new_peak) + jnp.sum(
                jnp.exp(logits - new_peak[..., None]), axis=-1
            )
            stored = lax.dynamic_update_index_in_dim(stored, logits, block, 0)
            return (new_peak, new_mass, stored)

        return lax.cond(block * KB <= last_row, first_active, lambda carried: carried, carry_in)

    peak_start = jnp.full((head_count, row_count), -jnp.inf, jnp.float32)
    mass_start = jnp.zeros((head_count, row_count), jnp.float32)
    store_start = jnp.zeros((block_count, head_count, row_count, KB), jnp.float32)
    row_peak, row_mass, stored = lax.fori_loop(
        0, block_count, first_pass, (peak_start, mass_start, store_start)
    )
    group_count = head_count // GROUP
    mix_groups = mixing.reshape(group_count, GROUP, GROUP)

    def second_pass(block, carry_in):

        def second_active(summed):
            logits = lax.dynamic_index_in_dim(stored, block, 0, keepdims=False)
            probs = jnp.exp(logits - row_peak[..., None]) / row_mass[..., None]
            grouped = probs.reshape(group_count, GROUP, row_count, KB)
            mixed_scores = (
                jnp.einsum("gab,gbrk->gark", mix_groups, grouped)
                .reshape(head_count, row_count, KB)
                .astype(jnp.bfloat16)
            )
            value_block = lax.dynamic_slice_in_dim(values_all, block * KB, KB, 0).reshape(
                KB, head_count, HD
            )
            return summed + jnp.einsum(
                "hrk,khd->rhd", mixed_scores, value_block, preferred_element_type=jnp.float32
            )

        return lax.cond(block * KB <= last_row, second_active, lambda summed: summed, carry_in)

    summed = lax.fori_loop(
        0, block_count, second_pass, jnp.zeros((row_count, head_count, HD), jnp.float32)
    )
    rms = jnp.sqrt(jnp.mean(summed * summed, axis=-1, keepdims=True) + 1e-05)
    normed = (summed / rms * gain.reshape(head_count, HD)).astype(jnp.bfloat16)
    return normed.reshape(row_count, head_count * HD)


def per_device(
    activations, positions, w_query, w_key, w_value, conv_kernel, head_mix, out_gain, w_out
):
    row_count = activations.shape[0]
    ctx_place = lax.axis_index("ctx")
    features = lax.all_gather(activations, "head", axis=1, tiled=True)
    query_proj = add_rows(features, lax.all_gather(w_query, "ctx", axis=0, tiled=True))
    key_proj = add_rows(features, lax.all_gather(w_key, "ctx", axis=0, tiled=True))
    value_proj = add_rows(features, lax.all_gather(w_value, "ctx", axis=0, tiled=True))
    key = rope(key_proj, positions).astype(jnp.bfloat16)
    value = value_proj.astype(jnp.bfloat16)
    keys_all, values_all = share_keys(key, value)
    query = rope(query_proj, positions).astype(jnp.bfloat16)
    rim_rows = passed_along(query[row_count - (CQ - 1) :], "ctx", 1)
    query_ext = jnp.concatenate([rim_rows, query], 0)
    keys_pad = jnp.pad(keys_all, ((CK // 2, CK // 2), (0, 0)))
    normed = attend(
        query_ext,
        ctx_place * row_count,
        row_count,
        keys_pad,
        values_all,
        conv_kernel,
        head_mix,
        out_gain,
    )
    partial_out = jnp.dot(
        normed, lax.all_gather(w_out, "ctx", axis=1, tiled=True), preferred_element_type=jnp.float32
    )
    return lax.psum_scatter(
        partial_out.astype(jnp.bfloat16), "head", scatter_dimension=1, tiled=True
    )


ROWS = 256
BAND = 128
LANES = 128
SUB = 64
VMEM_BYTES = 56 * 1024 * 1024


def kernel_params():
    return pltpu.CompilerParams(vmem_limit_bytes=VMEM_BYTES)


def whole(memory_space):
    return pl.BlockSpec(memory_space=memory_space)


def project_kernel(place, *refs):
    a_own, a_x, a_y = refs[:4], refs[4:9], refs[9:14]
    weights = refs[14:20]
    cos_ref, sin_ref = refs[20:22]
    mine, theirs, v_out = refs[22:25]
    abuf, wbuf, sem_a, sem_w = refs[25:]
    turn, core = place[0], place[1]
    rows, depth = a_own[0].shape
    half, pair = weights[0].shape[1:]
    first_rows, last_rows = pl.ds(0, rows // 2), pl.ds(rows // 2, rows // 2)

    def copies_a(t, b):
        cols = pl.ds(t * depth, depth)
        if t < 3:
            source = (a_own, a_x, a_y)[t][b].at[pl.ds(0, rows)]
            return [pltpu.make_async_copy(source, abuf.at[b, :, cols], sem_a.at[t, b])]
        late = pl.ds(rows if b < 3 else 0, rows // 2)
        return [
            pltpu.make_async_copy(
                a_y[b + 1].at[late], abuf.at[b, first_rows, cols], sem_a.at[3, b]
            ),
            pltpu.make_async_copy(
                a_x[b + 1].at[late], abuf.at[b, last_rows, cols], sem_a.at[4, b]
            ),
        ]

    def copy_w(t, i):
        side = core if i % 2 == 0 else 1 - core
        start = pl.multiple_of(t * depth + side * half, half)
        return pltpu.make_async_copy(
            weights[i].at[lax.bitwise_xor(turn, t)],
            wbuf.at[pl.ds(start, half), pl.ds((i // 2) * pair, pair)],
            sem_w.at[t, i],
        )

    for t in range(4):
        for copy in copies_a(t, 0):
            copy.start()
        for i in range(6):
            copy_w(t, i).start()
    for b in range(1, 4):
        for t in range(4):
            for copy in copies_a(t, b):
                copy.start()
    for t in range(4):
        for i in range(6):
            copy_w(t, i).wait()
    first = core == 0
    for b in range(4):
        for t in range(4):
            for copy in copies_a(t, b):
                copy.wait()
        total = jnp.dot(abuf[b], wbuf[...], preferred_element_type=jnp.float32)
        cosine, sine = cos_ref[b], sin_ref[b]
        at = place[5 + b]
        for col, out in ((0, 0), (2 * HD, HD)):
            heads = []
            for start in (col, col + HD):
                x = total[:, start : start + HD]
                x = x * cosine + pltpu.roll(x, HD // 2, 1) * sine
                heads.append(x.astype(jnp.bfloat16))
            mine[at, :, out : out + HD] = jnp.where(first, heads[0], heads[1])
            theirs[at, :, out : out + HD] = jnp.where(first, heads[1], heads[0])
        v_out[at] = total[:, 4 * HD :].astype(jnp.bfloat16)


def project(place, a_own, a_x, a_y, weights, cosine, sine):
    rows, depth = a_own[0].shape
    width = 3 * weights[0].shape[2]
    out = jax.ShapeDtypeStruct((4, rows, 2 * HD), jnp.bfloat16)
    return pl.pallas_call(
        project_kernel,
        out_shape=(out, out, out),
        in_specs=[whole(pltpu.SMEM)] + [whole(pl.ANY)] * 20 + [whole(pltpu.VMEM)] * 2,
        out_specs=[whole(pltpu.VMEM)] * 3,
        scratch_shapes=[
            pltpu.VMEM((4, rows, 4 * depth), jnp.bfloat16),
            pltpu.VMEM((4 * depth, width), jnp.bfloat16),
            pltpu.SemaphoreType.DMA((5, 4)),
            pltpu.SemaphoreType.DMA((4, 6)),
        ],
        compiler_params=kernel_params(),
        cost_estimate=pl.CostEstimate(
            flops=8 * rows * 4 * depth * width, bytes_accessed=16 * 2**20, transcendentals=0
        ),
    )(place, *a_own, *a_x, *a_y, *weights, cosine, sine)


def prepare_kernel(place, weights, mine, other, even_ref, odd_ref, q_out, k_out, corr, qf, kf, lags):
    core = place[1]
    total = q_out.shape[0]
    qf[0:8] = jnp.zeros((8, HD), jnp.float32)
    kf[0:8] = jnp.zeros((8, HD), jnp.float32)
    kf[8 + total :] = jnp.zeros((kf.shape[0] - 8 - total, HD), jnp.float32)
    for i in range(total // (2 * ROWS)):
        for ref, parity in ((mine, core), (other, 1 - core)):
            start = pl.multiple_of(8 + (2 * i + parity) * ROWS, 8)
            block = ref[i].astype(jnp.float32)
            qf[pl.ds(start, ROWS)] = block[:, :HD]
            kf[pl.ds(start, ROWS)] = block[:, HD:]

    ahead = lax.broadcasted_iota(jnp.int32, (SUB + 8, LANES), 1) - lax.broadcasted_iota(
        jnp.int32, (SUB + 8, LANES), 0
    )
    near = (ahead >= 1) & (ahead < CQ + CK // 2)

    def block_step(b, carry):
        corr[b] = jnp.zeros(corr.shape[1:], jnp.float32)
        for m in range(ROWS // SUB):
            base = pl.multiple_of(b * ROWS + m * SUB, SUB)
            qwin = qf[pl.ds(base, SUB + 8)]
            kwin = kf[pl.ds(base, LANES)]
            scores = lax.dot_general(
                qwin.astype(jnp.bfloat16),
                kwin.astype(jnp.bfloat16),
                (((1,), (1,)), ((), ())),
                preferred_element_type=jnp.float32,
            )
            future = jnp.where(near, scores, 0.0)
            rows = pl.ds(pl.multiple_of((2 * b + m // 2) * SUB, SUB), SUB)
            for a in range(CQ):
                lags[m % 2, rows, a * LANES : (a + 1) * LANES] = future[
                    8 - a : 8 - a + SUB
                ].astype(jnp.bfloat16)
            for a in range(CQ):
                q_out[pl.ds(base, SUB), a * HD : (a + 1) * HD] = qwin[8 - a : 8 - a + SUB].astype(
                    jnp.bfloat16
                )
            sums = [None] * CQ
            for c in range(CK):
                off = 8 + CK // 2 - c
                window = kwin[off : off + SUB]
                for a in range(CQ):
                    term = weights[a * CK + c] * window
                    sums[a] = term if c == 0 else sums[a] + term
            for a in range(CQ):
                k_out[pl.ds(base, SUB), a * HD : (a + 1) * HD] = sums[a].astype(jnp.bfloat16)
        return carry

    lax.fori_loop(0, total // ROWS, block_step, 0)
    for odd, taps in enumerate((even_ref, odd_ref)):
        for b in range(0, total // ROWS, 2):
            fix = jnp.dot(
                lags[odd, 2 * b * SUB : (2 * b + 4) * SUB],
                taps[...],
                preferred_element_type=jnp.float32,
            )
            for n in range(4):
                m = 2 * (n % 2) + odd
                col = LANES * ((m + 1) // 2)
                corr[b + n // 2, m * SUB : (m + 1) * SUB, col : col + taps.shape[1]] = fix[
                    n * SUB : (n + 1) * SUB
                ]


def prepare(place, weights, mine, other, even, odd):
    total = mine.shape[0] * 2 * ROWS
    return pl.pallas_call(
        prepare_kernel,
        out_shape=(
            jax.ShapeDtypeStruct((total, CQ * HD), jnp.bfloat16),
            jax.ShapeDtypeStruct((total, CQ * HD), jnp.bfloat16),
            jax.ShapeDtypeStruct((total // ROWS, ROWS, BAND + ROWS), jnp.float32),
        ),
        in_specs=[whole(pltpu.SMEM)] * 2 + [whole(pltpu.VMEM)] * 4,
        out_specs=[whole(pltpu.VMEM)] * 3,
        scratch_shapes=[
            pltpu.VMEM((8 + total, HD), jnp.float32),
            pltpu.VMEM((8 + total + LANES, HD), jnp.float32),
            pltpu.VMEM((2, total // 2, CQ * LANES), jnp.bfloat16),
        ],
        compiler_params=kernel_params(),
        cost_estimate=pl.CostEstimate(flops=2**31, bytes_accessed=12 * 2**20, transcendentals=0),
    )(place, weights, mine, other, even, odd)


def band_taps(weights, first, lanes):
    lag = jnp.arange(CQ)[:, None, None]
    tap = (first + jnp.arange(lanes))[None, None, :] + CK // 2 + 8 - jnp.arange(LANES)[None, :, None]
    band = jnp.zeros((CQ, LANES, lanes), jnp.float32)
    for c in range(CK):
        band = band + jnp.where(tap == c, weights[:, c][:, None, None], 0.0)
    return band.astype(jnp.bfloat16).reshape(CQ * LANES, lanes)


def attend_kernel(place, mix, q_ref, k_ref, corr, va, vb, vc, vd, mine, theirs, v_all):
    side, core = place[2], place[1]
    b = pl.program_id(0)
    count = k_ref.shape[0] // ROWS

    @pl.when(b == 0)
    def _():
        for i in range(count // 2):
            for parity, near, far in ((core, va, vb), (1 - core, vc, vd)):
                rows = pl.ds(pl.multiple_of((2 * i + parity) * ROWS, ROWS), ROWS)
                first, last = near[i], far[i]
                v_all[rows, : 2 * HD] = jnp.where(side == 0, first, last)
                v_all[rows, 2 * HD :] = jnp.where(side == 0, last, first)

    row = lax.broadcasted_iota(jnp.int32, (ROWS, ROWS), 0)
    col = lax.broadcasted_iota(jnp.int32, (ROWS, ROWS), 1)
    seen = col <= row

    for step in range(count):

        @pl.when(b == step)
        def _():
            pieces = []
            for j in range(step + 1):
                part = lax.dot_general(
                    q_ref[...],
                    k_ref[j * ROWS : (j + 1) * ROWS],
                    (((1,), (1,)), ((), ())),
                    preferred_element_type=jnp.float32,
                )
                if j == step:
                    part = jnp.where(seen, part - corr[0, :, BAND:], -jnp.inf)
                elif j == step - 1:
                    part = jnp.concatenate(
                        [part[:, : ROWS - BAND], part[:, ROWS - BAND :] - corr[0, :, :BAND]], 1
                    )
                pieces.append(part)
            peak = pieces[0]
            for part in pieces[1:]:
                peak = jnp.maximum(peak, part)
            peak = jnp.max(peak, axis=1, keepdims=True)
            mass = jnp.zeros((ROWS, ROWS), jnp.float32)
            probs = []
            for part in pieces:
                part = jnp.exp2(part - peak)
                mass = mass + part
                probs.append(part.astype(jnp.bfloat16))
            summed = jnp.dot(
                jnp.concatenate(probs, 1),
                v_all[: (step + 1) * ROWS],
                preferred_element_type=jnp.float32,
            )
            inverse = 1.0 / jnp.sum(mass, axis=1, keepdims=True)
            out = jnp.concatenate(
                [summed[:, g * HD : (g + 1) * HD] * (inverse * mix[g]) for g in range(GROUP)], 1
            ).astype(jnp.bfloat16)

            @pl.when(core == step % 2)
            def _():
                mine[0] = out

            @pl.when(core != step % 2)
            def _():
                theirs[0] = out


def attend_head(place, mix, q_wide, k_wide, corr, va, vb, vc, vd):
    total, depth = k_wide.shape
    count = total // ROWS
    out = jax.ShapeDtypeStruct((count // 2, ROWS, GROUP * HD), jnp.bfloat16)
    out_spec = pl.BlockSpec((1, ROWS, GROUP * HD), lambda b: (b // 2, 0, 0))
    v_spec = pl.BlockSpec(va.shape, lambda b: (0, 0, 0))
    return pl.pallas_call(
        attend_kernel,
        grid=(count,),
        out_shape=(out, out),
        in_specs=[
            whole(pltpu.SMEM),
            whole(pltpu.SMEM),
            pl.BlockSpec((ROWS, depth), lambda b: (b, 0)),
            pl.BlockSpec((total, depth), lambda b: (0, 0)),
            pl.BlockSpec((1, ROWS, BAND + ROWS), lambda b: (b, 0, 0)),
        ]
        + [v_spec] * 4,
        out_specs=[out_spec, out_spec],
        scratch_shapes=[pltpu.VMEM((total, GROUP * HD), jnp.bfloat16)],
        compiler_params=kernel_params(),
        cost_estimate=pl.CostEstimate(
            flops=total * total * (depth + GROUP * HD),
            bytes_accessed=16 * 2**20,
            transcendentals=total * total // 2,
        ),
    )(place, mix, q_wide, k_wide, corr, va, vb, vc, vd)


def finish_kernel(place, own, r1, r2, r3, gain, w_any, out, normed, w_buf, sem):
    blocks, _, width = w_buf.shape
    per = blocks // 4
    order = [(t, i) for t in (3, 2, 1, 0) for i in range(per)]

    def copy_w(n):
        t, i = order[n]
        source = per * lax.bitwise_xor(place[4], t) + i
        return pltpu.make_async_copy(w_any.at[source], w_buf.at[n], sem.at[n])

    for n in range(blocks):
        copy_w(n).start()
    near = own[...] + r1[...].astype(jnp.float32)
    far = r2[...].astype(jnp.float32) + r3[...].astype(jnp.float32)
    low = place[3] == 0
    for g in range(2 * GROUP):
        cols = slice((g % GROUP) * HD, (g % GROUP + 1) * HD)
        first = low if g < GROUP else jnp.logical_not(low)
        x = jnp.where(first, near[:, cols], far[:, cols])
        scale = lax.rsqrt(jnp.mean(x * x, axis=1, keepdims=True) + 1e-05)
        normed[:, g * HD : (g + 1) * HD] = (
            x * scale * gain[:, g * HD : (g + 1) * HD]
        ).astype(jnp.bfloat16)
    for n in range(blocks):
        t, i = order[n]
        copy_w(n).wait()
        out[t, :, i * width : (i + 1) * width] = jnp.dot(
            normed[...], w_buf[n], preferred_element_type=jnp.float32
        ).astype(jnp.bfloat16)


def finish(place, own, r1, r2, r3, gain, w_all):
    rows = own.shape[0]
    blocks, depth, width = w_all.shape
    return pl.pallas_call(
        finish_kernel,
        in_specs=[whole(pltpu.SMEM)] + [whole(pltpu.VMEM)] * 5 + [whole(pl.ANY)],
        out_specs=whole(pltpu.VMEM),
        out_shape=jax.ShapeDtypeStruct((4, rows, blocks // 4 * width), jnp.bfloat16),
        scratch_shapes=[
            pltpu.VMEM((rows, depth), jnp.bfloat16),
            pltpu.VMEM((blocks, depth, width), jnp.bfloat16),
            pltpu.SemaphoreType.DMA((blocks,)),
        ],
        compiler_params=kernel_params(),
        cost_estimate=pl.CostEstimate(
            flops=2 * rows * depth * blocks * width, bytes_accessed=11 * 2**20, transcendentals=0
        ),
    )(place, own, r1, r2, r3, gain, w_all)


def swapped(value, axis, mask):
    count = lax.axis_size(axis)
    return lax.ppermute(value, axis, [(i, i ^ mask) for i in range(count)])


def per_device_one_head(
    activations, positions, w_query, w_key, w_value, conv_kernel, head_mix, out_gain, w_out
):
    ctx, head = lax.axis_index("ctx"), lax.axis_index("head")
    z, core = ctx // 2, ctx % 2
    pair = 2 * HD
    same_core = [[i for i in range(8) if i % 2 == k] for k in range(2)]

    def columns(w):
        return lax.all_to_all(
            w.reshape(w.shape[0], 4, pair).transpose(1, 0, 2),
            "ctx",
            0,
            0,
            axis_index_groups=same_core,
        )

    middle = [(2, 4), (3, 5), (4, 2), (5, 3)]
    outward = [(2, 0), (3, 1), (4, 6), (5, 7)]
    inner = (z == 1) | (z == 2)
    rows = activations.shape[0]
    half = rows // 2

    def plane(block, x_before, y_before):
        to_x = jnp.concatenate([block, y_before[half:rows]])
        to_y = jnp.concatenate([block, x_before[:half]])
        return swapped(to_x, "head", 1), swapped(to_y, "head", 2)

    barrier = lax.optimization_barrier
    near = swapped(activations, "ctx", 2)
    across = lax.ppermute(activations, "ctx", middle)
    x0, y0 = swapped(activations, "head", 1), swapped(activations, "head", 2)
    place_near = swapped(positions, "ctx", 2)
    near, across, x0, y0, place_near, w_value, w_key, w_query = barrier(
        (near, across, x0, y0, place_near, w_value, w_key, w_query)
    )
    across_next = lax.ppermute(near, "ctx", middle)
    passed = lax.ppermute(across, "ctx", outward)
    x1, y1 = plane(near, x0, y0)
    place_far = swapped(jnp.stack([positions, place_near]), "ctx", 4)
    v_same = columns(w_value)
    across_next, passed, x1, y1, place_far, v_same, w_key, w_query = barrier(
        (across_next, passed, x1, y1, place_far, v_same, w_key, w_query)
    )
    far_a = across + passed
    passed_next = lax.ppermute(across_next, "ctx", outward)
    x2, y2 = plane(far_a, x1, y1)
    k_same = columns(w_key)
    v_swap = swapped(v_same, "ctx", 1)
    passed_next, x2, y2, k_same, v_swap, w_query, w_out = barrier(
        (passed_next, x2, y2, k_same, v_swap, w_query, w_out)
    )
    far_b = across_next + passed_next
    x3, y3 = plane(far_b, x2, y2)
    q_same = columns(w_query)
    k_swap = swapped(k_same, "ctx", 1)
    x3, y3, q_same, k_swap = barrier((x3, y3, q_same, k_swap))
    x4, y4 = swapped(y3[half:rows], "head", 1), swapped(x3[:half], "head", 2)
    q_swap = swapped(q_same, "ctx", 1)

    place_far = jnp.where(inner, place_far[::-1], place_far)
    place_of = jnp.concatenate([jnp.stack([positions, place_near]), place_far])
    order = jnp.where(inner, z ^ 3, z ^ 2), jnp.where(inner, z ^ 2, z ^ 3)
    place = jnp.stack([head, core, z % 2, z // 2, head, z, z ^ 1, *order]).astype(jnp.int32)

    exponents = jnp.arange(HD // 2, dtype=jnp.float32) * (2.0 / HD)
    inverse = jnp.exp(-exponents * math.log(500000.0))
    angle = (place_of.astype(jnp.float32) * 0.25)[:, :, None] * inverse
    cosine, sine = jnp.cos(angle), jnp.sin(angle)
    mine, theirs, v_pair = project(
        place,
        (activations, near, far_a, far_b),
        (x0, x1, x2, x3, x4),
        (y0, y1, y2, y3, y4),
        (q_same, q_swap, k_same, k_swap, v_same, v_swap),
        jnp.concatenate([cosine, cosine], -1),
        jnp.concatenate([-sine, sine], -1),
    )
    other = swapped(theirs, "ctx", 1)
    v_next = swapped(v_pair, "ctx", 2)
    v_pair_other = swapped(v_pair, "ctx", 1)
    v_next_other = swapped(v_next, "ctx", 1)

    weights = lax.dynamic_index_in_dim(conv_kernel, ctx, 0, keepdims=False)
    weights = weights * (math.log2(math.e) / math.sqrt(HD))
    taps = weights.reshape(CQ, CK)
    even, odd = band_taps(taps, -BAND, 2 * LANES), band_taps(taps, -SUB, LANES)
    even, odd, _ = lax.optimization_barrier((even, odd, positions))
    q_wide, k_wide, corr = prepare(place, weights, mine, other, even, odd)
    group_rows = lax.dynamic_slice_in_dim(head_mix, GROUP * (ctx // GROUP), GROUP, 0)
    mix = lax.dynamic_index_in_dim(group_rows, ctx % GROUP, 1, keepdims=False)
    out_mine, out_theirs = attend_head(
        place, mix, q_wide, k_wide, corr, v_pair, v_next, v_pair_other, v_next_other
    )
    summed = out_mine.astype(jnp.float32) + swapped(out_theirs, "ctx", 1).astype(jnp.float32)
    own = lax.dynamic_index_in_dim(summed, z, 0, keepdims=False)
    r1, r2, r3 = [
        swapped(
            lax.dynamic_index_in_dim(summed, z ^ s, 0, keepdims=False).astype(jnp.bfloat16),
            "ctx",
            2 * s,
        )
        for s in (1, 2, 3)
    ]

    w_all = lax.all_gather(w_out, "ctx", axis=0)
    shares = finish(place, own, r1, r2, r3, out_gain.reshape(1, -1), w_all)
    total = shares[0].astype(jnp.float32)
    for t in (1, 2, 3):
        total = total + swapped(shares[t], "head", t).astype(jnp.float32)
    return total.astype(jnp.bfloat16)


def solution(mesh):
    one_head_each = mesh.shape["ctx"] == 8 and mesh.shape["head"] == 4
    body = per_device_one_head if one_head_each else per_device
    return jax.shard_map(
        body,
        mesh=mesh,
        in_specs=(
            P("ctx", "head"),
            P("ctx"),
            P("ctx", "head"),
            P("ctx", "head"),
            P("ctx", "head"),
            P("head", None),
            P("head", None),
            P("head"),
            P("head", "ctx"),
        ),
        out_specs=P("ctx", "head"),
        check_vma=False,
    )
```

profile of v0, /device:TPU:17, one launch (start us, length us, event | category | flops | bytes accessed | tf_op | source)
XLA Modules:
  0.0 329.6 jit_solution(16961887215852779405)
XLA Ops:
  6.5 1.3 collective-permute-start
  7.8 1.9 collective-permute-start.1
  9.8 1.3 collective-permute-start.2
  11.0 1.2 collective-permute-start.3
  12.3 7.3 %collective-permute-done.4 = s32[256]{0:T(256)S(1)} collective-permute-done((s32[256]{0:T(256)}, s32[256]{0:T(256)S(1)}, u32[]{:S(2)}, u32[]{:S(2)}) %collective-permute-start.4) | collective-permute-done | bytes 1056 | tf_op jit(solution)/shard_map/ppermute | solution.py:526
  19.6 2.8 collective-permute-done.1
  22.5 0.9 collective-permute-done.3.refs_9_
  23.4 1.7 copy.10
  25.1 1.3 copy.11
  26.4 4.4 %all-to-all-start = ((bf16[4,512,256]{2,1,0:T(8,128)(2,1)}), bf16[4,512,256]{2,1,0:T(8,128)(2,1)}, u32[]{:S(2)}, u32[]{:S(2)}) async-start(bf16[4,512,256]{2,1,0:T(8,128)(2,1)} %bitcast.13), calls=%async_computation | async-start | bytes 2097152 | tf_op jit(solution)/shard_map/all_to_all | solution.py:538
  31.6 1.2 collective-permute-start.8
  32.9 3.0 collective-permute-start.5
  35.9 1.3 collective-permute-start.6
  37.4 27.5 %collective-permute-done.9 = s32[2,256]{1,0:T(2,128)S(1)} collective-permute-done((s32[2,256]{1,0:T(2,128)S(1)}, s32[2,256]{1,0:T(2,128)S(1)}, u32[]{:S(2)}, u32[]{:S(2)}) %collective-permute-start.9) | collective-permute-done | bytes 2080 | tf_op jit(solution)/shard_map/ppermute | solution.py:526
  66.7 1.3 copy.13
  68.0 5.9 %all-to-all-start.1 = ((bf16[4,512,256]{2,1,0:T(8,128)(2,1)}), bf16[4,512,256]{2,1,0:T(8,128)(2,1)S(1)}, u32[]{:S(2)}, u32[]{:S(2)}) async-start(bf16[4,512,256]{2,1,0:T(8,128)(2,1)} %bitcast.15), calls=%async_computation.1 | async-start | bytes 2097152 | tf_op jit(solution)/shard_map/all_to_all | solution.py:538
  74.0 1.6 collective-permute-start.13
  75.8 1.1 slice.83
  76.9 1.0 slice.82
  78.6 1.2 collective-permute-start.12
  79.9 3.1 collective-permute-start.10
  83.0 18.9 %collective-permute-done.10 = bf16[256,1024]{1,0:T(8,128)(2,1)S(1)} collective-permute-done((bf16[256,1024]{1,0:T(8,128)(2,1)S(1)}, bf16[256,1024]{1,0:T(8,128)(2,1)S(1)}, u32[]{:S(2)}, u32[]{:S(2)}) %collective-permute-start.10) | collective-permute-done | bytes 524320 | tf_op jit(solution)/shard_map/ppermute | solution.py:574
  101.9 0.9 copy-done.18
  102.8 0.9 copy-done.19
  103.7 1.0 copy-done.6
  105.3 1.3 copy.15
  106.6 5.7 %all-to-all-start.2 = ((bf16[4,512,256]{2,1,0:T(8,128)(2,1)}), bf16[4,512,256]{2,1,0:T(8,128)(2,1)S(1)}, u32[]{:S(2)}, u32[]{:S(2)}) async-start(bf16[4,512,256]{2,1,0:T(8,128)(2,1)} %bitcast.17), calls=%async_computation.2 | async-start | bytes 2097152 | tf_op jit(solution)/shard_map/all_to_all | solution.py:538
  112.3 1.3 fusion.31
  114.0 1.9 collective-permute-start.16
  116.1 1.2 slice.85
  117.3 1.0 slice.84
  118.3 1.1 pad_maximum_fusion.4
  119.9 1.3 collective-permute-start.15
  122.0 17.0 %collective-permute-done.14.refs_7_ = bf16[384,1024]{1,0:T(8,128)(2,1)} collective-permute-done((bf16[384,1024]{1,0:T(8,128)(2,1)}, bf16[384,1024]{1,0:T(8,128)(2,1)}, u32[]{:S(2)}, u32[]{:S(2)}) %collective-permute-start.14) | collective-permute-done | bytes 786464 | tf_op jit(solution)/shard_map/ppermute | solution.py:526
  138.9 18.8 %all-to-all-done.2.refs_14_ = bf16[4,512,256]{2,1,0:T(8,128)(2,1)S(1)} async-done(((bf16[4,512,256]{2,1,0:T(8,128)(2,1)}), bf16[4,512,256]{2,1,0:T(8,128)(2,1)S(1)}, u32[]{:S(2)}, u32[]{:S(2)}) %all-to-all-start.2) | async-done | bytes 1048608 | tf_op jit(solution)/shard_map/all_to_all | solution.py:538
  157.7 6.4 %collective-permute-start.19 = (bf16[4,512,256]{2,1,0:T(8,128)(2,1)S(1)}, bf16[4,512,256]{2,1,0:T(8,128)(2,1)S(1)}, u32[]{:S(2)}, u32[]{:S(2)}) collective-permute-start(bf16[4,512,256]{2,1,0:T(8,128)(2,1)S(1)} %all-to-all-done.2.refs_14_), channel_id=1, source_target_pairs={{0,4},{4,0},{8,12},{12,8},{16,20},{20,16},{24,28},{28,24},{1,5},{5... | collective-permute-start | bytes 3145736 | tf_op jit(solution)/shard_map/ppermute | solution.py:526
  164.7 1.0 slice.86
  166.3 1.0 slice.87
  167.2 1.3 collective-permute-start.18
  168.5 1.9 fusion.6
  170.4 1.3 pad_maximum_fusion.6
  171.8 1.9 collective-permute-done.17.refs_8_
  173.7 1.3 collective-permute-done.18.refs_13_
  176.0 16.9 %shard_map.91 = (bf16[4,256,256]{2,1,0:T(8,128)(2,1)}, bf16[4,256,256]{2,1,0:T(8,128)(2,1)}, bf16[4,256,256]{2,1,0:T(8,128)(2,1)}) custom-call(s32[9]{0:T(128)} %stack.47.place, bf16[256,1024]{1,0:T(8,128)(2,1)} %refs_0_.1, bf16[256,1024]{1,0:T(8,128)(2,1)} %copy-done.9, bf16[256,1024]{1,0:T(8,128)(2,1)} %copy-done.2, bf16[256,1024]{1,0:T(8,128)(2,1)} %copy-done.3, ...), custom_call_target="tpu_custom_call" | custom-call | flops 6442450944 | bytes 16777216 | tf_op jit(solution)/shard_map/pallas_call | solution.py:263
  193.7 1.2 collective-permute-start.20
  194.9 2.4 add_convert_fusion.even_ref
  197.3 16.4 %collective-permute-done.21.vb = bf16[4,256,256]{2,1,0:T(8,128)(2,1)S(1)} collective-permute-done((bf16[4,256,256]{2,1,0:T(8,128)(2,1)}, bf16[4,256,256]{2,1,0:T(8,128)(2,1)S(1)}, u32[]{:S(2)}, u32[]{:S(2)}) %collective-permute-start.21) | collective-permute-done | bytes 524320 | tf_op jit(solution)/shard_map/ppermute | solution.py:526
  213.7 0.8 collective-permute-start.23
  214.7 2.2 add_convert_fusion.1.odd_ref
  218.3 18.9 %shard_map.92 = (bf16[2048,768]{1,0:T(8,128)(2,1)}, bf16[2048,768]{1,0:T(8,128)(2,1)}, f32[8,256,384]{2,1,0:T(8,128)}) custom-call(s32[9]{0:T(128)} %stack.47.place, f32[66]{0:T(128)} %get-tuple-element.106.weights, bf16[4,256,256]{2,1,0:T(8,128)(2,1)} %get-tuple-element.68.mine, bf16[4,256,256]{2,1,0:T(8,128)(2,1)} %copy-done.23, ...), custom_call_target="tpu_custom_call" | custom-call | flops 2147483648 | bytes 12582912 | tf_op jit(solution)/shard_map/pallas_call | solution.py:350
  238.2 14.8 %shard_map.93 = (bf16[4,256,512]{2,1,0:T(8,128)(2,1)}, bf16[4,256,512]{2,1,0:T(8,128)(2,1)}) custom-call(s32[9]{0:T(128)} %stack.47.place, f32[4]{0:T(128)} %dynamic-slice_bitcast_fusion.1.mix, bf16[2048,768]{1,0:T(8,128)(2,1)} %get-tuple-element.72.q_ref, bf16[2048,768]{1,0:T(8,128)(2,1)} %get-tuple-element.73.k_ref, ...), custom_call_target="tpu_custom_call" | custom-call | flops 5368709120 | bytes 16777216 | tf_op jit(solution)/shard_map/pallas_call | solution.py:450
  253.1 2.8 collective-permute-done.24
  255.9 1.6 convert_add_fusion
  258.4 2.1 collective-permute-start.25
  260.4 1.0 collective-permute-start.26
  262.5 9.1 %collective-permute-done.25.r1 = bf16[256,512]{1,0:T(8,128)(2,1)S(1)} collective-permute-done((bf16[256,512]{1,0:T(8,128)(2,1)}, bf16[256,512]{1,0:T(8,128)(2,1)S(1)}, u32[]{:S(2)}, u32[]{:S(2)}) %collective-permute-start.25) | collective-permute-done | bytes 262176 | tf_op jit(solution)/shard_map/ppermute | solution.py:526
  271.7 6.5 %collective-permute-done.26.r2 = bf16[256,512]{1,0:T(8,128)(2,1)S(1)} collective-permute-done((bf16[256,512]{1,0:T(8,128)(2,1)S(1)}, bf16[256,512]{1,0:T(8,128)(2,1)S(1)}, u32[]{:S(2)}, u32[]{:S(2)}) %collective-permute-start.26) | collective-permute-done | bytes 262176 | tf_op jit(solution)/shard_map/ppermute | solution.py:526
  278.1 6.8 %collective-permute-done.27.r3 = bf16[256,512]{1,0:T(8,128)(2,1)S(1)} collective-permute-done((bf16[256,512]{1,0:T(8,128)(2,1)S(1)}, bf16[256,512]{1,0:T(8,128)(2,1)S(1)}, u32[]{:S(2)}, u32[]{:S(2)}) %collective-permute-start.27) | collective-permute-done | bytes 262176 | tf_op jit(solution)/shard_map/ppermute | solution.py:526
  285.6 7.4 %shard_map.94 = bf16[4,256,1024]{2,1,0:T(8,128)(2,1)} custom-call(s32[9]{0:T(128)} %stack.47.place, f32[256,512]{1,0:T(8,128)} %dynamic-slice_bitcast_fusion.own, bf16[256,512]{1,0:T(8,128)(2,1)} %copy-done.12, bf16[256,512]{1,0:T(8,128)(2,1)} %copy-done.13, bf16[256,512]{1,0:T(8,128)(2,1)} %copy-done.14, f32[1,1024]{1,0:T(1,128)} %bitcast.111, ...), custom_call_target="tpu_custom_call" | custom-call | flops 2147483648 | bytes 11534336 | tf_op jit(solution)/shard_map/pallas_call | solution.py:507
  293.0 1.5 slice_bitcast_fusion.2
  294.5 1.8 collective-permute-start.30
  297.2 10.8 %collective-permute-done.30 = bf16[256,1024]{1,0:T(8,128)(2,1)S(1)} collective-permute-done((bf16[256,1024]{1,0:T(8,128)(2,1)S(1)}, bf16[256,1024]{1,0:T(8,128)(2,1)S(1)}, u32[]{:S(2)}, u32[]{:S(2)}) %collective-permute-start.30) | collective-permute-done | bytes 524320 | tf_op jit(solution)/shard_map/ppermute | solution.py:526
  308.0 12.6 %collective-permute-done.29 = bf16[256,1024]{1,0:T(8,128)(2,1)S(1)} collective-permute-done((bf16[256,1024]{1,0:T(8,128)(2,1)S(1)}, bf16[256,1024]{1,0:T(8,128)(2,1)S(1)}, u32[]{:S(2)}, u32[]{:S(2)}) %collective-permute-start.29) | collective-permute-done | bytes 524320 | tf_op jit(solution)/shard_map/ppermute | solution.py:526
  320.5 2.2 fusion.2
  (115 shorter events, 15.4 us)
Async XLA Ops:
  6.5 210.4 %copy-start = (f32[8,4]{0,1:T(4,128)S(1)}, f32[8,4]{0,1:T(4,128)}, u32[]{:S(2)}) copy-start(f32[8,4]{0,1:T(4,128)} %param.15) | copy-start | bytes 388
  6.5 13.0 %collective-permute-start = (bf16[256,1024]{1,0:T(8,128)(2,1)}, bf16[256,1024]{1,0:T(8,128)(2,1)S(1)}, u32[]{:S(2)}, u32[]{:S(2)}) collective-permute-start(bf16[256,1024]{1,0:T(8,128)(2,1)} %refs_0_.1), channel_id=1, source_target_pairs={{0,8},{4,12},{8,0},{12,4},{16,24},{20,28},{24,16},{28,20},{1,9},{5... | collective-permute-start | bytes 1572872 | tf_op jit(solution)/shard_map/ppermute | solution.py:526
  7.8 14.6 %collective-permute-start.1 = (bf16[256,1024]{1,0:T(8,128)(2,1)}, bf16[256,1024]{1,0:T(8,128)(2,1)S(1)}, u32[]{:S(2)}, u32[]{:S(2)}) collective-permute-start(bf16[256,1024]{1,0:T(8,128)(2,1)} %refs_0_.1), channel_id=1, source_target_pairs={{8,16},{12,20},{16,8},{20,12},{9,17},{13,21},{17,9},{21,13},{10,18... | collective-permute-start | bytes 1572872 | tf_op jit(solution)/shard_map/ppermute | solution.py:559
  9.8 12.7 %collective-permute-start.2 = (bf16[256,1024]{1,0:T(8,128)(2,1)}, bf16[256,1024]{1,0:T(8,128)(2,1)S(1)}, u32[]{:S(2)}, u32[]{:S(2)}) collective-permute-start(bf16[256,1024]{1,0:T(8,128)(2,1)} %refs_0_.1), channel_id=1, source_target_pairs={{0,1},{1,0},{2,3},{3,2},{4,5},{5,4},{6,7},{7,6},{8,9},{9,8},{10,11... | collective-permute-start | bytes 1572872 | tf_op jit(solution)/shard_map/ppermute | solution.py:526
  11.0 12.4 %collective-permute-start.3 = (bf16[256,1024]{1,0:T(8,128)(2,1)}, bf16[256,1024]{1,0:T(8,128)(2,1)S(1)}, u32[]{:S(2)}, u32[]{:S(2)}) collective-permute-start(bf16[256,1024]{1,0:T(8,128)(2,1)} %refs_0_.1), channel_id=1, source_target_pairs={{0,2},{1,3},{2,0},{3,1},{4,6},{5,7},{6,4},{7,5},{8,10},{9,11},{10,... | collective-permute-start | bytes 1572872 | tf_op jit(solution)/shard_map/ppermute | solution.py:526
  12.3 7.3 %collective-permute-start.4 = (s32[256]{0:T(256)}, s32[256]{0:T(256)S(1)}, u32[]{:S(2)}, u32[]{:S(2)}) collective-permute-start(s32[256]{0:T(256)} %param.10), channel_id=1, source_target_pairs={{0,8},{4,12},{8,0},{12,4},{16,24},{20,28},{24,16},{28,20},{1,9},{5... | collective-permute-start | bytes 3080 | tf_op jit(solution)/shard_map/ppermute | solution.py:526
  19.6 13.3 %copy-start.9 = (bf16[256,1024]{1,0:T(8,128)(2,1)}, bf16[256,1024]{1,0:T(8,128)(2,1)S(1)}, u32[]{:S(2)}) copy-start(bf16[256,1024]{1,0:T(8,128)(2,1)S(1)} %collective-permute-done.refs_1_) | copy-start | bytes 1572868
  22.5 8.3 %copy-start.15 = (bf16[256,1024]{1,0:T(8,128)(2,1)}, bf16[256,1024]{1,0:T(8,128)(2,1)S(1)}, u32[]{:S(2)}) copy-start(bf16[256,1024]{1,0:T(8,128)(2,1)S(1)} %collective-permute-done.2.refs_4_) | copy-start | bytes 1572868
  23.4 3.0 copy-start.16
  26.4 4.4 %copy-start.17 = (bf16[256,1024]{1,0:T(8,128)(2,1)S(1)}, bf16[256,1024]{1,0:T(8,128)(2,1)}, u32[]{:S(2)}) copy-start(bf16[256,1024]{1,0:T(8,128)(2,1)} %copy-done.16) | copy-start | bytes 1572868
  26.4 39.7 %all-to-all-start = ((bf16[4,512,256]{2,1,0:T(8,128)(2,1)}), bf16[4,512,256]{2,1,0:T(8,128)(2,1)}, u32[]{:S(2)}, u32[]{:S(2)}) async-start(bf16[4,512,256]{2,1,0:T(8,128)(2,1)} %bitcast.13), calls=%async_computation | async-start | bytes 2097152 | tf_op jit(solution)/shard_map/all_to_all | solution.py:538
  30.9 6.4 %copy-start.20 = (s32[256]{0:T(256)S(1)}, s32[256]{0:T(256)}, u32[]{:S(2)}) copy-start(s32[256]{0:T(256)} %param.10) | copy-start | bytes 3076
  30.9 35.3 %copy-start.4 = (bf16[512,1024]{1,0:T(8,128)(2,1)S(1)}, bf16[512,1024]{1,0:T(8,128)(2,1)}, u32[]{:S(2)}) copy-start(bf16[512,1024]{1,0:T(8,128)(2,1)} %param.12) | copy-start | bytes 3145732
  31.1 34.3 %collective-permute-start.7 = (bf16[384,1024]{1,0:T(8,128)(2,1)S(1)}, bf16[384,1024]{1,0:T(8,128)(2,1)}, u32[]{:S(2)}, u32[]{:S(2)}) collective-permute-start(bf16[384,1024]{1,0:T(8,128)(2,1)S(1)} %get-tuple-element.101), channel_id=1, source_target_pairs={{0,1},{1,0},{2,3},{3,2},{4,5},{5,4},{6,7},{7,6},{8,9},{9,8},{10,11... | collective-permute-start | bytes 2359304 | tf_op jit(solution)/shard_map/ppermute | solution.py:526
  31.6 33.7 %collective-permute-start.8 = (bf16[384,1024]{1,0:T(8,128)(2,1)S(1)}, bf16[384,1024]{1,0:T(8,128)(2,1)}, u32[]{:S(2)}, u32[]{:S(2)}) collective-permute-start(bf16[384,1024]{1,0:T(8,128)(2,1)S(1)} %get-tuple-element.100), channel_id=1, source_target_pairs={{0,2},{1,3},{2,0},{3,1},{4,6},{5,7},{6,4},{7,5},{8,10},{9,11},{10,... | collective-permute-start | bytes 2359304 | tf_op jit(solution)/shard_map/ppermute | solution.py:526
  32.9 32.5 %collective-permute-start.5 = (bf16[256,1024]{1,0:T(8,128)(2,1)S(1)}, bf16[256,1024]{1,0:T(8,128)(2,1)S(1)}, u32[]{:S(2)}, u32[]{:S(2)}) collective-permute-start(bf16[256,1024]{1,0:T(8,128)(2,1)S(1)} %collective-permute-done.refs_1_), channel_id=1, source_target_pairs={{8,16},{12,20},{16,8},{20,12},{9,17},{13,21},{17,9},{21,13},{10,18... | collective-permute-start | bytes 1572872 | tf_op jit(solution)/shard_map/ppermute | solution.py:565
  35.9 29.4 %collective-permute-start.6 = (bf16[256,1024]{1,0:T(8,128)(2,1)S(1)}, bf16[256,1024]{1,0:T(8,128)(2,1)S(1)}, u32[]{:S(2)}, u32[]{:S(2)}) collective-permute-start(bf16[256,1024]{1,0:T(8,128)(2,1)S(1)} %collective-permute-done.1), channel_id=1, source_target_pairs={{8,0},{12,4},{16,24},{20,28},{9,1},{13,5},{17,25},{21,29},{10,2},{... | collective-permute-start | bytes 1572872 | tf_op jit(solution)/shard_map/ppermute | solution.py:566
  37.3 27.6 %collective-permute-start.9 = (s32[2,256]{1,0:T(2,128)S(1)}, s32[2,256]{1,0:T(2,128)S(1)}, u32[]{:S(2)}, u32[]{:S(2)}) collective-permute-start(s32[2,256]{1,0:T(2,128)S(1)} %pad_add_fusion), channel_id=1, source_target_pairs={{0,16},{4,20},{8,24},{12,28},{16,0},{20,4},{24,8},{28,12},{1,17},{... | collective-permute-start | bytes 6152 | tf_op jit(solution)/shard_map/ppermute | solution.py:526
  65.4 0.8 copy-start.10
  68.0 7.5 %copy-start.11 = (bf16[256,1024]{1,0:T(8,128)(2,1)S(1)}, bf16[256,1024]{1,0:T(8,128)(2,1)}, u32[]{:S(2)}) copy-start(bf16[256,1024]{1,0:T(8,128)(2,1)} %copy-done.10) | copy-start | bytes 1572868
  68.0 35.7 %all-to-all-start.1 = ((bf16[4,512,256]{2,1,0:T(8,128)(2,1)}), bf16[4,512,256]{2,1,0:T(8,128)(2,1)S(1)}, u32[]{:S(2)}, u32[]{:S(2)}) async-start(bf16[4,512,256]{2,1,0:T(8,128)(2,1)} %bitcast.15), calls=%async_computation.1 | async-start | bytes 2097152 | tf_op jit(solution)/shard_map/all_to_all | solution.py:538
  74.0 210.9 %all-gather.3.cloned.1.call-start = ((), (), s32[]{:S(2)}) async-start(), calls=%async_computation.3 | async-start | bytes 9437184 | tf_op jit(solution)/shard_map/all_gather | solution.py:634
  74.0 29.7 %collective-permute-start.13 = (bf16[4,512,256]{2,1,0:T(8,128)(2,1)}, bf16[4,512,256]{2,1,0:T(8,128)(2,1)}, u32[]{:S(2)}, u32[]{:S(2)}) collective-permute-start(bf16[4,512,256]{2,1,0:T(8,128)(2,1)} %all-to-all-done.refs_18_), channel_id=1, source_target_pairs={{0,4},{4,0},{8,12},{12,8},{16,20},{20,16},{24,28},{28,24},{1,5},{5... | collective-permute-start | bytes 3145736 | tf_op jit(solution)/shard_map/ppermute | solution.py:526
  75.8 2.3 copy-start.2
  77.9 26.8 %copy-start.5 = (bf16[512,1024]{1,0:T(8,128)(2,1)S(1)}, bf16[512,1024]{1,0:T(8,128)(2,1)}, u32[]{:S(2)}) copy-start(bf16[512,1024]{1,0:T(8,128)(2,1)} %param.11) | copy-start | bytes 3145732
  78.1 23.8 %collective-permute-start.11 = (bf16[384,1024]{1,0:T(8,128)(2,1)S(1)}, bf16[384,1024]{1,0:T(8,128)(2,1)S(1)}, u32[]{:S(2)}, u32[]{:S(2)}) collective-permute-start(bf16[384,1024]{1,0:T(8,128)(2,1)S(1)} %get-tuple-element.99), channel_id=1, source_target_pairs={{0,1},{1,0},{2,3},{3,2},{4,5},{5,4},{6,7},{7,6},{8,9},{9,8},{10,11... | collective-permute-start | bytes 2359304 | tf_op jit(solution)/shard_map/ppermute | solution.py:526
  78.6 23.3 %collective-permute-start.12 = (bf16[384,1024]{1,0:T(8,128)(2,1)S(1)}, bf16[384,1024]{1,0:T(8,128)(2,1)S(1)}, u32[]{:S(2)}, u32[]{:S(2)}) collective-permute-start(bf16[384,1024]{1,0:T(8,128)(2,1)S(1)} %get-tuple-element.98), channel_id=1, source_target_pairs={{0,2},{1,3},{2,0},{3,1},{4,6},{5,7},{6,4},{7,5},{8,10},{9,11},{10,... | collective-permute-start | bytes 2359304 | tf_op jit(solution)/shard_map/ppermute | solution.py:526
  79.9 22.0 %collective-permute-start.10 = (bf16[256,1024]{1,0:T(8,128)(2,1)S(1)}, bf16[256,1024]{1,0:T(8,128)(2,1)S(1)}, u32[]{:S(2)}, u32[]{:S(2)}) collective-permute-start(bf16[256,1024]{1,0:T(8,128)(2,1)S(1)} %collective-permute-done.5), channel_id=1, source_target_pairs={{8,0},{12,4},{16,24},{20,28},{9,1},{13,5},{17,25},{21,29},{10,2},{... | collective-permute-start | bytes 1572872 | tf_op jit(solution)/shard_map/ppermute | solution.py:574
  101.9 0.9 copy-start.18
  102.8 0.9 copy-start.19
  103.7 1.0 copy-start.6
  106.6 7.4 %copy-start.7 = (bf16[4,512,256]{2,1,0:T(8,128)(2,1)S(1)}, bf16[4,512,256]{2,1,0:T(8,128)(2,1)}, u32[]{:S(2)}) copy-start(bf16[4,512,256]{2,1,0:T(8,128)(2,1)} %copy-done.6) | copy-start | bytes 3145732
  106.6 51.1 %all-to-all-start.2 = ((bf16[4,512,256]{2,1,0:T(8,128)(2,1)}), bf16[4,512,256]{2,1,0:T(8,128)(2,1)S(1)}, u32[]{:S(2)}, u32[]{:S(2)}) async-start(bf16[4,512,256]{2,1,0:T(8,128)(2,1)} %bitcast.17), calls=%async_computation.2 | async-start | bytes 2097152 | tf_op jit(solution)/shard_map/all_to_all | solution.py:538
  114.0 25.0 %collective-permute-start.16 = (bf16[4,512,256]{2,1,0:T(8,128)(2,1)S(1)}, bf16[4,512,256]{2,1,0:T(8,128)(2,1)}, u32[]{:S(2)}, u32[]{:S(2)}) collective-permute-start(bf16[4,512,256]{2,1,0:T(8,128)(2,1)S(1)} %copy-done.7), channel_id=1, source_target_pairs={{0,4},{4,0},{8,12},{12,8},{16,20},{20,16},{24,28},{28,24},{1,5},{5... | collective-permute-start | bytes 3145736 | tf_op jit(solution)/shard_map/ppermute | solution.py:526
  116.1 3.3 copy-start.3
  119.4 19.5 %collective-permute-start.14 = (bf16[384,1024]{1,0:T(8,128)(2,1)}, bf16[384,1024]{1,0:T(8,128)(2,1)}, u32[]{:S(2)}, u32[]{:S(2)}) collective-permute-start(bf16[384,1024]{1,0:T(8,128)(2,1)} %get-tuple-element.97), channel_id=1, source_target_pairs={{0,1},{1,0},{2,3},{3,2},{4,5},{5,4},{6,7},{7,6},{8,9},{9,8},{10,11... | collective-permute-start | bytes 2359304 | tf_op jit(solution)/shard_map/ppermute | solution.py:526
  119.9 19.0 %collective-permute-start.15 = (bf16[384,1024]{1,0:T(8,128)(2,1)S(1)}, bf16[384,1024]{1,0:T(8,128)(2,1)}, u32[]{:S(2)}, u32[]{:S(2)}) collective-permute-start(bf16[384,1024]{1,0:T(8,128)(2,1)S(1)} %get-tuple-element.96), channel_id=1, source_target_pairs={{0,2},{1,3},{2,0},{3,1},{4,6},{5,7},{6,4},{7,5},{8,10},{9,11},{10,... | collective-permute-start | bytes 2359304 | tf_op jit(solution)/shard_map/ppermute | solution.py:526
  157.7 14.0 %copy-start.8 = (bf16[4,512,256]{2,1,0:T(8,128)(2,1)}, bf16[4,512,256]{2,1,0:T(8,128)(2,1)S(1)}, u32[]{:S(2)}) copy-start(bf16[4,512,256]{2,1,0:T(8,128)(2,1)S(1)} %all-to-all-done.2.refs_14_) | copy-start | bytes 3145732
  157.7 17.3 %collective-permute-start.19 = (bf16[4,512,256]{2,1,0:T(8,128)(2,1)S(1)}, bf16[4,512,256]{2,1,0:T(8,128)(2,1)S(1)}, u32[]{:S(2)}, u32[]{:S(2)}) collective-permute-start(bf16[4,512,256]{2,1,0:T(8,128)(2,1)S(1)} %all-to-all-done.2.refs_14_), channel_id=1, source_target_pairs={{0,4},{4,0},{8,12},{12,8},{16,20},{20,16},{24,28},{28,24},{1,5},{5... | collective-permute-start | bytes 3145736 | tf_op jit(solution)/shard_map/ppermute | solution.py:526
  165.7 8.0 %collective-permute-start.17 = (bf16[128,1024]{1,0:T(8,128)(2,1)S(1)}, bf16[128,1024]{1,0:T(8,128)(2,1)S(1)}, u32[]{:S(2)}, u32[]{:S(2)}) collective-permute-start(bf16[128,1024]{1,0:T(8,128)(2,1)S(1)} %slice.86), channel_id=1, source_target_pairs={{0,1},{1,0},{2,3},{3,2},{4,5},{5,4},{6,7},{7,6},{8,9},{9,8},{10,11... | collective-permute-start | bytes 786440 | tf_op jit(solution)/shard_map/ppermute | solution.py:526
  167.2 7.8 %collective-permute-start.18 = (bf16[128,1024]{1,0:T(8,128)(2,1)S(1)}, bf16[128,1024]{1,0:T(8,128)(2,1)S(1)}, u32[]{:S(2)}, u32[]{:S(2)}) collective-permute-start(bf16[128,1024]{1,0:T(8,128)(2,1)S(1)} %slice.87), channel_id=1, source_target_pairs={{0,2},{1,3},{2,0},{3,1},{4,6},{5,7},{6,4},{7,5},{8,10},{9,11},{10,... | collective-permute-start | bytes 786440 | tf_op jit(solution)/shard_map/ppermute | solution.py:526
  173.7 1.3 copy-start.26
  175.0 0.7 copy-start.27
  175.0 1.0 copy-start.21
  192.9 20.8 %collective-permute-start.21 = (bf16[4,256,256]{2,1,0:T(8,128)(2,1)}, bf16[4,256,256]{2,1,0:T(8,128)(2,1)S(1)}, u32[]{:S(2)}, u32[]{:S(2)}) collective-permute-start(bf16[4,256,256]{2,1,0:T(8,128)(2,1)} %get-tuple-element.75.va), channel_id=1, source_target_pairs={{0,8},{4,12},{8,0},{12,4},{16,24},{20,28},{24,16},{28,20},{1,9},{5... | collective-permute-start | bytes 1572872 | tf_op jit(solution)/shard_map/ppermute | solution.py:526
  193.7 23.9 %collective-permute-start.20 = (bf16[4,256,256]{2,1,0:T(8,128)(2,1)}, bf16[4,256,256]{2,1,0:T(8,128)(2,1)S(1)}, u32[]{:S(2)}, u32[]{:S(2)}) collective-permute-start(bf16[4,256,256]{2,1,0:T(8,128)(2,1)} %get-tuple-element.69), channel_id=1, source_target_pairs={{0,4},{4,0},{8,12},{12,8},{16,20},{20,16},{24,28},{28,24},{1,5},{5... | collective-permute-start | bytes 1572872 | tf_op jit(solution)/shard_map/ppermute | solution.py:526
  197.3 39.9 %collective-permute-start.22 = (bf16[4,256,256]{2,1,0:T(8,128)(2,1)}, bf16[4,256,256]{2,1,0:T(8,128)(2,1)S(1)}, u32[]{:S(2)}, u32[]{:S(2)}) collective-permute-start(bf16[4,256,256]{2,1,0:T(8,128)(2,1)} %get-tuple-element.75.va), channel_id=1, source_target_pairs={{0,4},{4,0},{8,12},{12,8},{16,20},{20,16},{24,28},{28,24},{1,5},{5... | collective-permute-start | bytes 1572872 | tf_op jit(solution)/shard_map/ppermute | solution.py:526
  213.7 23.5 %copy-start.22 = (bf16[4,256,256]{2,1,0:T(8,128)(2,1)}, bf16[4,256,256]{2,1,0:T(8,128)(2,1)S(1)}, u32[]{:S(2)}) copy-start(bf16[4,256,256]{2,1,0:T(8,128)(2,1)S(1)} %collective-permute-done.21.vb) | copy-start | bytes 1572868
  213.7 23.5 %collective-permute-start.23 = (bf16[4,256,256]{2,1,0:T(8,128)(2,1)S(1)}, bf16[4,256,256]{2,1,0:T(8,128)(2,1)S(1)}, u32[]{:S(2)}, u32[]{:S(2)}) collective-permute-start(bf16[4,256,256]{2,1,0:T(8,128)(2,1)S(1)} %collective-permute-done.21.vb), channel_id=1, source_target_pairs={{0,4},{4,0},{8,12},{12,8},{16,20},{20,16},{24,28},{28,24},{1,5},{5... | collective-permute-start | bytes 1572872 | tf_op jit(solution)/shard_map/ppermute | solution.py:526
  217.5 0.8 copy-start.23
  237.2 0.8 copy-start.24
  237.3 0.9 copy-start.25
  253.0 2.9 collective-permute-start.24
  258.4 13.3 %collective-permute-start.25 = (bf16[256,512]{1,0:T(8,128)(2,1)}, bf16[256,512]{1,0:T(8,128)(2,1)S(1)}, u32[]{:S(2)}, u32[]{:S(2)}) collective-permute-start(bf16[256,512]{1,0:T(8,128)(2,1)} %get-tuple-element.95), channel_id=1, source_target_pairs={{0,8},{4,12},{8,0},{12,4},{16,24},{20,28},{24,16},{28,20},{1,9},{5... | collective-permute-start | bytes 786440 | tf_op jit(solution)/shard_map/ppermute | solution.py:526
  260.4 17.7 %collective-permute-start.26 = (bf16[256,512]{1,0:T(8,128)(2,1)S(1)}, bf16[256,512]{1,0:T(8,128)(2,1)S(1)}, u32[]{:S(2)}, u32[]{:S(2)}) collective-permute-start(bf16[256,512]{1,0:T(8,128)(2,1)S(1)} %get-tuple-element.94), channel_id=1, source_target_pairs={{0,16},{4,20},{8,24},{12,28},{16,0},{20,4},{24,8},{28,12},{1,17},{... | collective-permute-start | bytes 786440 | tf_op jit(solution)/shard_map/ppermute | solution.py:526
  261.4 23.5 %collective-permute-start.27 = (bf16[256,512]{1,0:T(8,128)(2,1)S(1)}, bf16[256,512]{1,0:T(8,128)(2,1)S(1)}, u32[]{:S(2)}, u32[]{:S(2)}) collective-permute-start(bf16[256,512]{1,0:T(8,128)(2,1)S(1)} %get-tuple-element.93), channel_id=1, source_target_pairs={{0,24},{4,28},{8,16},{12,20},{16,8},{20,12},{24,0},{28,4},{1,25},{... | collective-permute-start | bytes 786440 | tf_op jit(solution)/shard_map/ppermute | solution.py:526
  271.7 13.2 %copy-start.12 = (bf16[256,512]{1,0:T(8,128)(2,1)}, bf16[256,512]{1,0:T(8,128)(2,1)S(1)}, u32[]{:S(2)}) copy-start(bf16[256,512]{1,0:T(8,128)(2,1)S(1)} %collective-permute-done.25.r1) | copy-start | bytes 786436
  278.1 6.8 %copy-start.13 = (bf16[256,512]{1,0:T(8,128)(2,1)}, bf16[256,512]{1,0:T(8,128)(2,1)S(1)}, u32[]{:S(2)}) copy-start(bf16[256,512]{1,0:T(8,128)(2,1)S(1)} %collective-permute-done.26.r2) | copy-start | bytes 786436
  284.9 0.7 copy-start.14
  293.0 29.8 %copy-start.1 = (f32[8,4]{0,1:T(4,128)S(1)}, f32[8,4]{0,1:T(4,128)}, u32[]{:S(2)}) copy-start(f32[8,4]{0,1:T(4,128)} %param.15) | copy-start | bytes 388
  294.5 13.5 %collective-permute-start.30 = (bf16[256,1024]{1,0:T(8,128)(2,1)S(1)}, bf16[256,1024]{1,0:T(8,128)(2,1)S(1)}, u32[]{:S(2)}, u32[]{:S(2)}) collective-permute-start(bf16[256,1024]{1,0:T(8,128)(2,1)S(1)} %get-tuple-element.91), channel_id=1, source_target_pairs={{0,3},{1,2},{2,1},{3,0},{4,7},{5,6},{6,5},{7,4},{8,11},{9,10},{10,... | collective-permute-start | bytes 1572872 | tf_op jit(solution)/shard_map/ppermute | solution.py:526
  296.3 24.3 %collective-permute-start.29 = (bf16[256,1024]{1,0:T(8,128)(2,1)S(1)}, bf16[256,1024]{1,0:T(8,128)(2,1)S(1)}, u32[]{:S(2)}, u32[]{:S(2)}) collective-permute-start(bf16[256,1024]{1,0:T(8,128)(2,1)S(1)} %get-tuple-element.92), channel_id=1, source_target_pairs={{0,2},{1,3},{2,0},{3,1},{4,6},{5,7},{6,4},{7,5},{8,10},{9,11},{10,... | collective-permute-start | bytes 1572872 | tf_op jit(solution)/shard_map/ppermute | solution.py:526
  296.5 24.1 %collective-permute-start.28 = (bf16[256,1024]{1,0:T(8,128)(2,1)S(1)}, bf16[256,1024]{1,0:T(8,128)(2,1)S(1)}, u32[]{:S(2)}, u32[]{:S(2)}) collective-permute-start(bf16[256,1024]{1,0:T(8,128)(2,1)S(1)} %get-tuple-element.90), channel_id=1, source_target_pairs={{0,1},{1,0},{2,3},{3,2},{4,5},{5,4},{6,7},{7,6},{8,9},{9,8},{10,11... | collective-permute-start | bytes 1572872 | tf_op jit(solution)/shard_map/ppermute | solution.py:526
Sparse Core Ops, SparseCore 0:
  104.8 99.7 all-gather.2
where the time goes:
time: 331 us; the launch traced here: 330 us
  waiting for transfers between devices  162 us (49%)
  Pallas kernels  58 us (18%)
  starting transfers between devices  55.1 us (17%)
  local copies, waits for them, and re-layouts  25.5 us (8%)
  other arithmetic  15.1 us (5%)
  between operations  13.8 us (4%)
    ppermute x27, waiting for transfers between devices, swapped(): return lax.ppermute(value, axis, [(i, i ^ mask) for i in range(count)])  121 us
    ppermute x27, starting transfers between devices, swapped(): return lax.ppermute(value, axis, [(i, i ^ mask) for i in range(count)])  29.7 us
    ppermute x1, waiting for transfers between devices, per_device_one_head(): passed_next = lax.ppermute(across_next, 'ctx', outward)  18.9 us
    pallas_call x1, Pallas kernels, prepare(): pl.pallas_call(prepare_kernel, out_shape=(jax.ShapeDtypeStruct((total, CQ...  18.9 us
    all_to_all x3, waiting for transfers between devices, columns(): lax.all_to_all(w.reshape(w.shape[0], 4, pair).transpose(1, 0, 2), 'ctx',...  18.8 us
    pallas_call x1, Pallas kernels, project(): pl.pallas_call(project_kernel, out_shape=(out, out, out), in_specs=[whole...  16.9 us
    all_to_all x3, starting transfers between devices, columns(): lax.all_to_all(w.reshape(w.shape[0], 4, pair).transpose(1, 0, 2), 'ctx',...  16 us
    pallas_call x1, Pallas kernels, attend_head(): pl.pallas_call(attend_kernel, grid=(count,), out_shape=(out, out), in_spe...  14.8 us
  transfers between devices with their start and end apart: 35, of which 18 were waited for; matrix products, arithmetic and copies ran while one was open for 8% of the time, Pallas kernels for 15%

commit v1 on v0

--- a/solution.py
+++ b/solution.py
@@ -179,6 +179,7 @@
 BAND = 128
 LANES = 128
 SUB = 64
+AHEAD = 16
 VMEM_BYTES = 56 * 1024 * 1024
 
 
@@ -192,60 +193,58 @@
 
 def project_kernel(place, *refs):
     a_own, a_x, a_y = refs[:4], refs[4:9], refs[9:14]
-    weights = refs[14:20]
-    cos_ref, sin_ref = refs[20:22]
-    mine, theirs, v_out = refs[22:25]
-    abuf, wbuf, sem_a, sem_w = refs[25:]
+    weights = refs[14:18]
+    cos_ref, sin_ref = refs[18:20]
+    mine, theirs, v_out = refs[20:23]
+    abuf, wbuf, acc, sem_a, sem_w = refs[23:]
     turn, core = place[0], place[1]
     rows, depth = a_own[0].shape
-    half, pair = weights[0].shape[1:]
-    first_rows, last_rows = pl.ds(0, rows // 2), pl.ds(rows // 2, rows // 2)
-
-    def copies_a(t, b):
-        cols = pl.ds(t * depth, depth)
-        if t < 3:
-            source = (a_own, a_x, a_y)[t][b].at[pl.ds(0, rows)]
-            return [pltpu.make_async_copy(source, abuf.at[b, :, cols], sem_a.at[t, b])]
-        late = pl.ds(rows if b < 3 else 0, rows // 2)
-        return [
-            pltpu.make_async_copy(
-                a_y[b + 1].at[late], abuf.at[b, first_rows, cols], sem_a.at[3, b]
-            ),
-            pltpu.make_async_copy(
-                a_x[b + 1].at[late], abuf.at[b, last_rows, cols], sem_a.at[4, b]
-            ),
-        ]
-
-    def copy_w(t, i):
-        side = core if i % 2 == 0 else 1 - core
-        start = pl.multiple_of(t * depth + side * half, half)
-        return pltpu.make_async_copy(
-            weights[i].at[lax.bitwise_xor(turn, t)],
-            wbuf.at[pl.ds(start, half), pl.ds((i // 2) * pair, pair)],
-            sem_w.at[t, i],
-        )
+    half = weights[0].shape[1]
+
+    def copies(t):
+        out = []
+        start = 0
+        for i in range(4):
+            width = weights[i].shape[2]
+            side = core if i % 2 == 0 else 1 - core
+            out.append(
+                pltpu.make_async_copy(
+                    weights[i].at[lax.bitwise_xor(turn, t)],
+                    wbuf.at[
+                        t, pl.ds(pl.multiple_of(side * half, half), half), pl.ds(start, width)
+                    ],
+                    sem_w.at[t, i],
+                )
+            )
+            start += width * (i % 2)
+        for b in range(4):
+            if t < 3:
+                source = (a_own, a_x, a_y)[t][b].at[pl.ds(0, rows)]
+                target = abuf.at[t, pl.ds(b * rows, rows)]
+                out.append(pltpu.make_async_copy(source, target, sem_a.at[t, b]))
+                continue
+            late = pl.ds(rows if b < 3 else 0, rows // 2)
+            for n, part in enumerate((a_y, a_x)):
+                target = abuf.at[t, pl.ds(b * rows + n * (rows // 2), rows // 2)]
+                out.append(
+                    pltpu.make_async_copy(part[b + 1].at[late], target, sem_a.at[t + n, b])
+                )
+        return out
 
     for t in range(4):
-        for copy in copies_a(t, 0):
+        for copy in copies(t):
             copy.start()
-        for i in range(6):
-            copy_w(t, i).start()
-    for b in range(1, 4):
-        for t in range(4):
-            for copy in copies_a(t, b):
-                copy.start()
     for t in range(4):
-        for i in range(6):
-            copy_w(t, i).wait()
+        for copy in copies(t):
+            copy.wait()
+        part = jnp.dot(abuf[t], wbuf[t], preferred_element_type=jnp.float32)
+        acc[...] = part if t == 0 else acc[...] + part
     first = core == 0
     for b in range(4):
-        for t in range(4):
-            for copy in copies_a(t, b):
-                copy.wait()
-        total = jnp.dot(abuf[b], wbuf[...], preferred_element_type=jnp.float32)
+        total = acc[b * rows : (b + 1) * rows]
         cosine, sine = cos_ref[b], sin_ref[b]
         at = place[5 + b]
-        for col, out in ((0, 0), (2 * HD, HD)):
+        for col, out in ((0, 0), (4 * HD, HD)):
             heads = []
             for start in (col, col + HD):
                 x = total[:, start : start + HD]
@@ -253,23 +252,24 @@
                 heads.append(x.astype(jnp.bfloat16))
             mine[at, :, out : out + HD] = jnp.where(first, heads[0], heads[1])
             theirs[at, :, out : out + HD] = jnp.where(first, heads[1], heads[0])
-        v_out[at] = total[:, 4 * HD :].astype(jnp.bfloat16)
+        v_out[at] = total[:, 2 * HD : 4 * HD].astype(jnp.bfloat16)
 
 
 def project(place, a_own, a_x, a_y, weights, cosine, sine):
     rows, depth = a_own[0].shape
-    width = 3 * weights[0].shape[2]
+    width = weights[0].shape[2] + weights[2].shape[2]
     out = jax.ShapeDtypeStruct((4, rows, 2 * HD), jnp.bfloat16)
     return pl.pallas_call(
         project_kernel,
         out_shape=(out, out, out),
-        in_specs=[whole(pltpu.SMEM)] + [whole(pl.ANY)] * 20 + [whole(pltpu.VMEM)] * 2,
+        in_specs=[whole(pltpu.SMEM)] + [whole(pl.ANY)] * 18 + [whole(pltpu.VMEM)] * 2,
         out_specs=[whole(pltpu.VMEM)] * 3,
         scratch_shapes=[
-            pltpu.VMEM((4, rows, 4 * depth), jnp.bfloat16),
-            pltpu.VMEM((4 * depth, width), jnp.bfloat16),
+            pltpu.VMEM((4, 4 * rows, depth), jnp.bfloat16),
+            pltpu.VMEM((4, depth, width), jnp.bfloat16),
+            pltpu.VMEM((4 * rows, width), jnp.float32),
             pltpu.SemaphoreType.DMA((5, 4)),
-            pltpu.SemaphoreType.DMA((4, 6)),
+            pltpu.SemaphoreType.DMA((4, 4)),
         ],
         compiler_params=kernel_params(),
         cost_estimate=pl.CostEstimate(
@@ -278,30 +278,34 @@
     )(place, *a_own, *a_x, *a_y, *weights, cosine, sine)
 
 
-def prepare_kernel(place, weights, mine, other, even_ref, odd_ref, q_out, k_out, corr, qf, kf, lags):
+def prepare_kernel(place, mine, other, key_ref, even_ref, odd_ref, q_out, k_out, corr, *scratch):
+    qf, kf, lags, turned = scratch
     core = place[1]
     total = q_out.shape[0]
     qf[0:8] = jnp.zeros((8, HD), jnp.float32)
-    kf[0:8] = jnp.zeros((8, HD), jnp.float32)
-    kf[8 + total :] = jnp.zeros((kf.shape[0] - 8 - total, HD), jnp.float32)
+    kf[0:AHEAD] = jnp.zeros((AHEAD, HD), jnp.float32)
+    kf[AHEAD + total :] = jnp.zeros((kf.shape[0] - AHEAD - total, HD), jnp.float32)
+    corr[...] = jnp.zeros(corr.shape, jnp.float32)
     for i in range(total // (2 * ROWS)):
         for ref, parity in ((mine, core), (other, 1 - core)):
-            start = pl.multiple_of(8 + (2 * i + parity) * ROWS, 8)
+            start = pl.multiple_of((2 * i + parity) * ROWS, ROWS)
             block = ref[i].astype(jnp.float32)
-            qf[pl.ds(start, ROWS)] = block[:, :HD]
-            kf[pl.ds(start, ROWS)] = block[:, HD:]
+            qf[pl.ds(8 + start, ROWS)] = block[:, :HD]
+            kf[pl.ds(AHEAD + start, ROWS)] = block[:, HD:]
 
     ahead = lax.broadcasted_iota(jnp.int32, (SUB + 8, LANES), 1) - lax.broadcasted_iota(
         jnp.int32, (SUB + 8, LANES), 0
     )
     near = (ahead >= 1) & (ahead < CQ + CK // 2)
-
-    def block_step(b, carry):
-        corr[b] = jnp.zeros(corr.shape[1:], jnp.float32)
-        for m in range(ROWS // SUB):
-            base = pl.multiple_of(b * ROWS + m * SUB, SUB)
-            qwin = qf[pl.ds(base, SUB + 8)]
-            kwin = kf[pl.ds(base, LANES)]
+    steps = total // LANES
+    for w in range(steps):
+        base = w * LANES
+        window = kf[base : base + 2 * LANES].T
+        turned[base : base + LANES] = window.astype(jnp.bfloat16)
+        for odd in range(2):
+            at = base + odd * SUB
+            qwin = qf[at : at + SUB + 8]
+            kwin = kf[at + AHEAD - 8 : at + AHEAD - 8 + LANES]
             scores = lax.dot_general(
                 qwin.astype(jnp.bfloat16),
                 kwin.astype(jnp.bfloat16),
@@ -309,61 +313,63 @@
                 preferred_element_type=jnp.float32,
             )
             future = jnp.where(near, scores, 0.0)
-            rows = pl.ds(pl.multiple_of((2 * b + m // 2) * SUB, SUB), SUB)
             for a in range(CQ):
-                lags[m % 2, rows, a * LANES : (a + 1) * LANES] = future[
-                    8 - a : 8 - a + SUB
-                ].astype(jnp.bfloat16)
-            for a in range(CQ):
-                q_out[pl.ds(base, SUB), a * HD : (a + 1) * HD] = qwin[8 - a : 8 - a + SUB].astype(
+                cols = slice(a * LANES, (a + 1) * LANES)
+                lags[odd, w * SUB : (w + 1) * SUB, cols] = future[8 - a : 8 - a + SUB].astype(
                     jnp.bfloat16
                 )
-            sums = [None] * CQ
-            for c in range(CK):
-                off = 8 + CK // 2 - c
-                window = kwin[off : off + SUB]
-                for a in range(CQ):
-                    term = weights[a * CK + c] * window
-                    sums[a] = term if c == 0 else sums[a] + term
+                q_out[at : at + SUB, cols] = qwin[8 - a : 8 - a + SUB].astype(jnp.bfloat16)
+    for w in range(0, steps, 4):
+        wide = jnp.dot(
+            turned[w * LANES : (w + 4) * LANES], key_ref[...], preferred_element_type=jnp.float32
+        )
+        for n in range(4):
+            cols = slice((w + n) * LANES, (w + n + 1) * LANES)
             for a in range(CQ):
-                k_out[pl.ds(base, SUB), a * HD : (a + 1) * HD] = sums[a].astype(jnp.bfloat16)
-        return carry
-
-    lax.fori_loop(0, total // ROWS, block_step, 0)
+                k_out[a * HD : (a + 1) * HD, cols] = wide[
+                    n * LANES : (n + 1) * LANES, a * LANES : (a + 1) * LANES
+                ].astype(jnp.bfloat16)
     for odd, taps in enumerate((even_ref, odd_ref)):
-        for b in range(0, total // ROWS, 2):
+        for w in range(0, steps, 8):
             fix = jnp.dot(
-                lags[odd, 2 * b * SUB : (2 * b + 4) * SUB],
-                taps[...],
-                preferred_element_type=jnp.float32,
-            )
-            for n in range(4):
-                m = 2 * (n % 2) + odd
+                lags[odd, w * SUB : (w + 8) * SUB], taps[...], preferred_element_type=jnp.float32
+            )
+            for n in range(8):
+                m = 2 * ((w + n) % 2) + odd
                 col = LANES * ((m + 1) // 2)
-                corr[b + n // 2, m * SUB : (m + 1) * SUB, col : col + taps.shape[1]] = fix[
+                corr[(w + n) // 2, m * SUB : (m + 1) * SUB, col : col + taps.shape[1]] = fix[
                     n * SUB : (n + 1) * SUB
                 ]
 
 
-def prepare(place, weights, mine, other, even, odd):
+def prepare(place, mine, other, key_taps, even, odd):
     total = mine.shape[0] * 2 * ROWS
     return pl.pallas_call(
         prepare_kernel,
         out_shape=(
             jax.ShapeDtypeStruct((total, CQ * HD), jnp.bfloat16),
-            jax.ShapeDtypeStruct((total, CQ * HD), jnp.bfloat16),
+            jax.ShapeDtypeStruct((CQ * HD, total), jnp.bfloat16),
             jax.ShapeDtypeStruct((total // ROWS, ROWS, BAND + ROWS), jnp.float32),
         ),
-        in_specs=[whole(pltpu.SMEM)] * 2 + [whole(pltpu.VMEM)] * 4,
+        in_specs=[whole(pltpu.SMEM)] + [whole(pltpu.VMEM)] * 5,
         out_specs=[whole(pltpu.VMEM)] * 3,
         scratch_shapes=[
             pltpu.VMEM((8 + total, HD), jnp.float32),
-            pltpu.VMEM((8 + total + LANES, HD), jnp.float32),
+            pltpu.VMEM((AHEAD + total + LANES, HD), jnp.float32),
             pltpu.VMEM((2, total // 2, CQ * LANES), jnp.bfloat16),
+            pltpu.VMEM((total, 2 * LANES), jnp.bfloat16),
         ],
         compiler_params=kernel_params(),
         cost_estimate=pl.CostEstimate(flops=2**31, bytes_accessed=12 * 2**20, transcendentals=0),
-    )(place, weights, mine, other, even, odd)
+    )(place, mine, other, key_taps, even, odd)
+
+
+def key_taps_of(weights):
+    tap = jnp.arange(LANES)[None, None, :] + CK // 2 + AHEAD - jnp.arange(2 * LANES)[:, None, None]
+    out = jnp.zeros((2 * LANES, CQ, LANES), jnp.float32)
+    for c in range(CK):
+        out = out + jnp.where(tap == c, weights[:, c][None, :, None], 0.0)
+    return out.astype(jnp.bfloat16).reshape(2 * LANES, CQ * LANES)
 
 
 def band_taps(weights, first, lanes):
@@ -378,11 +384,11 @@
 def attend_kernel(place, mix, q_ref, k_ref, corr, va, vb, vc, vd, mine, theirs, v_all):
     side, core = place[2], place[1]
     b = pl.program_id(0)
-    count = k_ref.shape[0] // ROWS
+    count = k_ref.shape[1] // (2 * ROWS)
 
     @pl.when(b == 0)
     def _():
-        for i in range(count // 2):
+        for i in range(count):
             for parity, near, far in ((core, va, vb), (1 - core, vc, vd)):
                 rows = pl.ds(pl.multiple_of((2 * i + parity) * ROWS, ROWS), ROWS)
                 first, last = near[i], far[i]
@@ -392,60 +398,79 @@
     row = lax.broadcasted_iota(jnp.int32, (ROWS, ROWS), 0)
     col = lax.broadcasted_iota(jnp.int32, (ROWS, ROWS), 1)
     seen = col <= row
+    top, low = slice(0, ROWS), slice(ROWS, 2 * ROWS)
+
+    def fixed(part, n):
+        return jnp.concatenate([part[:, :BAND], part[:, BAND:] - corr[n, :, :BAND]], 1)
+
+    def rows_of(upper, lower):
+        return jnp.concatenate([upper, lower], 0)
+
+    def block(step):
+        parts = []
+        for j in range(2 * step + 1):
+            part = jnp.dot(
+                q_ref[...],
+                k_ref[:, j * ROWS : (j + 1) * ROWS],
+                preferred_element_type=jnp.float32,
+            )
+            if j == 2 * step:
+                diagonal = jnp.where(seen, part[top] - corr[0, :, BAND:], -jnp.inf)
+                part = rows_of(diagonal, fixed(part[low], 1))
+            elif j == 2 * step - 1:
+                part = rows_of(fixed(part[top], 0), part[low])
+            parts.append(part)
+        start = (2 * step + 1) * ROWS
+        last = jnp.dot(
+            q_ref[low], k_ref[:, start : start + ROWS], preferred_element_type=jnp.float32
+        )
+        last = jnp.where(seen, last - corr[1, :, BAND:], -jnp.inf)
+        peak = parts[0]
+        for part in parts[1:]:
+            peak = jnp.maximum(peak, part)
+        peak = rows_of(peak[top], jnp.maximum(peak[low], last))
+        peak = jnp.max(peak, axis=1, keepdims=True)
+        mass = jnp.zeros((2 * ROWS, ROWS), jnp.float32)
+        probs = []
+        for part in parts:
+            part = jnp.exp2(part - peak)
+            mass = mass + part
+            probs.append(part.astype(jnp.bfloat16))
+        last = jnp.exp2(last - peak[low])
+        mass = rows_of(mass[top], mass[low] + last)
+        summed = jnp.dot(
+            jnp.concatenate(probs, 1), v_all[:start], preferred_element_type=jnp.float32
+        )
+        extra = jnp.dot(
+            last.astype(jnp.bfloat16),
+            v_all[start : start + ROWS],
+            preferred_element_type=jnp.float32,
+        )
+        inverse = 1.0 / jnp.sum(mass, axis=1, keepdims=True)
+        halves = []
+        for rows, total in ((top, summed[top]), (low, summed[low] + extra)):
+            halves.append(
+                jnp.concatenate(
+                    [
+                        total[:, g * HD : (g + 1) * HD] * (inverse[rows] * mix[g])
+                        for g in range(GROUP)
+                    ],
+                    1,
+                ).astype(jnp.bfloat16)
+            )
+        mine[0] = jnp.where(core == 0, halves[0], halves[1])
+        theirs[0] = jnp.where(core == 0, halves[1], halves[0])
 
     for step in range(count):
-
-        @pl.when(b == step)
-        def _():
-            pieces = []
-            for j in range(step + 1):
-                part = lax.dot_general(
-                    q_ref[...],
-                    k_ref[j * ROWS : (j + 1) * ROWS],
-                    (((1,), (1,)), ((), ())),
-                    preferred_element_type=jnp.float32,
-                )
-                if j == step:
-                    part = jnp.where(seen, part - corr[0, :, BAND:], -jnp.inf)
-                elif j == step - 1:
-                    part = jnp.concatenate(
-                        [part[:, : ROWS - BAND], part[:, ROWS - BAND :] - corr[0, :, :BAND]], 1
-                    )
-                pieces.append(part)
-            peak = pieces[0]
-            for part in pieces[1:]:
-                peak = jnp.maximum(peak, part)
-            peak = jnp.max(peak, axis=1, keepdims=True)
-            mass = jnp.zeros((ROWS, ROWS), jnp.float32)
-            probs = []
-            for part in pieces:
-                part = jnp.exp2(part - peak)
-                mass = mass + part
-                probs.append(part.astype(jnp.bfloat16))
-            summed = jnp.dot(
-                jnp.concatenate(probs, 1),
-                v_all[: (step + 1) * ROWS],
-                preferred_element_type=jnp.float32,
-            )
-            inverse = 1.0 / jnp.sum(mass, axis=1, keepdims=True)
-            out = jnp.concatenate(
-                [summed[:, g * HD : (g + 1) * HD] * (inverse * mix[g]) for g in range(GROUP)], 1
-            ).astype(jnp.bfloat16)
-
-            @pl.when(core == step % 2)
-            def _():
-                mine[0] = out
-
-            @pl.when(core != step % 2)
-            def _():
-                theirs[0] = out
+        pl.when(b == step)(lambda step=step: block(step))
 
 
 def attend_head(place, mix, q_wide, k_wide, corr, va, vb, vc, vd):
-    total, depth = k_wide.shape
-    count = total // ROWS
-    out = jax.ShapeDtypeStruct((count // 2, ROWS, GROUP * HD), jnp.bfloat16)
-    out_spec = pl.BlockSpec((1, ROWS, GROUP * HD), lambda b: (b // 2, 0, 0))
+    depth, total = k_wide.shape
+    rows = 2 * ROWS
+    count = total // rows
+    out = jax.ShapeDtypeStruct((count, ROWS, GROUP * HD), jnp.bfloat16)
+    out_spec = pl.BlockSpec((1, ROWS, GROUP * HD), lambda b: (b, 0, 0))
     v_spec = pl.BlockSpec(va.shape, lambda b: (0, 0, 0))
     return pl.pallas_call(
         attend_kernel,
@@ -454,9 +479,9 @@
         in_specs=[
             whole(pltpu.SMEM),
             whole(pltpu.SMEM),
-            pl.BlockSpec((ROWS, depth), lambda b: (b, 0)),
-            pl.BlockSpec((total, depth), lambda b: (0, 0)),
-            pl.BlockSpec((1, ROWS, BAND + ROWS), lambda b: (b, 0, 0)),
+            pl.BlockSpec((rows, depth), lambda b: (b, 0)),
+            pl.BlockSpec((depth, total), lambda b: (0, 0)),
+            pl.BlockSpec((2, ROWS, BAND + ROWS), lambda b: (b, 0, 0)),
         ]
         + [v_spec] * 4,
         out_specs=[out_spec, out_spec],
@@ -470,7 +495,7 @@
     )(place, mix, q_wide, k_wide, corr, va, vb, vc, vd)
 
 
-def finish_kernel(place, own, r1, r2, r3, gain, w_any, out, normed, w_buf, sem):
+def finish_kernel(place, own, r1, r2, r3, gain, w_any, o0, o1, o2, o3, normed, w_buf, sem):
     blocks, _, width = w_buf.shape
     per = blocks // 4
     order = [(t, i) for t in (3, 2, 1, 0) for i in range(per)]
@@ -496,7 +521,7 @@
     for n in range(blocks):
         t, i = order[n]
         copy_w(n).wait()
-        out[t, :, i * width : (i + 1) * width] = jnp.dot(
+        (o0, o1, o2, o3)[t][:, i * width : (i + 1) * width] = jnp.dot(
             normed[...], w_buf[n], preferred_element_type=jnp.float32
         ).astype(jnp.bfloat16)
 
@@ -507,8 +532,8 @@
     return pl.pallas_call(
         finish_kernel,
         in_specs=[whole(pltpu.SMEM)] + [whole(pltpu.VMEM)] * 5 + [whole(pl.ANY)],
-        out_specs=whole(pltpu.VMEM),
-        out_shape=jax.ShapeDtypeStruct((4, rows, blocks // 4 * width), jnp.bfloat16),
+        out_specs=[whole(pltpu.VMEM)] * 4,
+        out_shape=[jax.ShapeDtypeStruct((rows, blocks // 4 * width), jnp.bfloat16)] * 4,
         scratch_shapes=[
             pltpu.VMEM((rows, depth), jnp.bfloat16),
             pltpu.VMEM((blocks, depth, width), jnp.bfloat16),
@@ -534,9 +559,10 @@
     pair = 2 * HD
     same_core = [[i for i in range(8) if i % 2 == k] for k in range(2)]
 
-    def columns(w):
+    def columns(*weights):
+        shaped = [w.reshape(w.shape[0], 4, pair) for w in weights]
         return lax.all_to_all(
-            w.reshape(w.shape[0], 4, pair).transpose(1, 0, 2),
+            jnp.concatenate(shaped, -1).transpose(1, 0, 2),
             "ctx",
             0,
             0,
@@ -559,30 +585,21 @@
     across = lax.ppermute(activations, "ctx", middle)
     x0, y0 = swapped(activations, "head", 1), swapped(activations, "head", 2)
     place_near = swapped(positions, "ctx", 2)
-    near, across, x0, y0, place_near, w_value, w_key, w_query = barrier(
-        (near, across, x0, y0, place_near, w_value, w_key, w_query)
-    )
+    vk_same, q_same = columns(w_value, w_key), columns(w_query)
+    near, across, x0, y0 = barrier((near, across, x0, y0))
     across_next = lax.ppermute(near, "ctx", middle)
     passed = lax.ppermute(across, "ctx", outward)
     x1, y1 = plane(near, x0, y0)
-    place_far = swapped(jnp.stack([positions, place_near]), "ctx", 4)
-    v_same = columns(w_value)
-    across_next, passed, x1, y1, place_far, v_same, w_key, w_query = barrier(
-        (across_next, passed, x1, y1, place_far, v_same, w_key, w_query)
-    )
+    across_next, passed, x1, y1, place_near = barrier((across_next, passed, x1, y1, place_near))
     far_a = across + passed
     passed_next = lax.ppermute(across_next, "ctx", outward)
     x2, y2 = plane(far_a, x1, y1)
-    k_same = columns(w_key)
-    v_swap = swapped(v_same, "ctx", 1)
-    passed_next, x2, y2, k_same, v_swap, w_query, w_out = barrier(
-        (passed_next, x2, y2, k_same, v_swap, w_query, w_out)
-    )
+    place_far = swapped(jnp.stack([positions, place_near]), "ctx", 4)
+    passed_next, x2, y2, place_far, vk_same = barrier((passed_next, x2, y2, place_far, vk_same))
     far_b = across_next + passed_next
     x3, y3 = plane(far_b, x2, y2)
-    q_same = columns(w_query)
-    k_swap = swapped(k_same, "ctx", 1)
-    x3, y3, q_same, k_swap = barrier((x3, y3, q_same, k_swap))
+    vk_swap = swapped(vk_same, "ctx", 1)
+    x3, y3, vk_swap, q_same, w_out = barrier((x3, y3, vk_swap, q_same, w_out))
     x4, y4 = swapped(y3[half:rows], "head", 1), swapped(x3[:half], "head", 2)
     q_swap = swapped(q_same, "ctx", 1)
 
@@ -600,21 +617,21 @@
         (activations, near, far_a, far_b),
         (x0, x1, x2, x3, x4),
         (y0, y1, y2, y3, y4),
-        (q_same, q_swap, k_same, k_swap, v_same, v_swap),
+        (q_same, q_swap, vk_same, vk_swap),
         jnp.concatenate([cosine, cosine], -1),
         jnp.concatenate([-sine, sine], -1),
     )
     other = swapped(theirs, "ctx", 1)
     v_next = swapped(v_pair, "ctx", 2)
     v_pair_other = swapped(v_pair, "ctx", 1)
-    v_next_other = swapped(v_next, "ctx", 1)
 
     weights = lax.dynamic_index_in_dim(conv_kernel, ctx, 0, keepdims=False)
     weights = weights * (math.log2(math.e) / math.sqrt(HD))
     taps = weights.reshape(CQ, CK)
-    even, odd = band_taps(taps, -BAND, 2 * LANES), band_taps(taps, -SUB, LANES)
-    even, odd, _ = lax.optimization_barrier((even, odd, positions))
-    q_wide, k_wide, corr = prepare(place, weights, mine, other, even, odd)
+    tables = key_taps_of(taps), band_taps(taps, -BAND, 2 * LANES), band_taps(taps, -SUB, LANES)
+    q_wide, k_wide, corr = prepare(place, mine, other, *tables)
+    v_next, q_wide = barrier((v_next, q_wide))
+    v_next_other = swapped(v_next, "ctx", 1)
     group_rows = lax.dynamic_slice_in_dim(head_mix, GROUP * (ctx // GROUP), GROUP, 0)
     mix = lax.dynamic_index_in_dim(group_rows, ctx % GROUP, 1, keepdims=False)
     out_mine, out_theirs = attend_head(

time: 331 us -> 326 us (0.985); the launches traced: 330 us -> 320 us
  Pallas kernels: 58 us -> 42.9 us
  waiting for transfers between devices: 162 us -> 176 us
  starting transfers between devices: 55.1 us -> 47.4 us
  local copies, waits for them, and re-layouts: 25.5 us -> 22 us
    ppermute x27 -> x26, waiting for transfers between devices: 121 us -> 144 us  [swapped(): return lax.ppermute(value, axis, [(i, i ^ mask) for i in range(count)])]
    ppermute x1, waiting for transfers between devices: 18.9 us -> 4.28 us  [per_device_one_head(): passed_next = lax.ppermute(across_next, 'ctx', outward)]
    pallas_call x1, Pallas kernels: 18.9 us -> 7.58 us  [prepare(): pl.pallas_call(prepare_kernel, out_shape=(jax.ShapeDtypeStruct((total, CQ...]
    ppermute x1, waiting for transfers between devices: 2.84 us -> 10.2 us  [per_device_one_head(): across = lax.ppermute(activations, 'ctx', middle)]
    all_to_all x3 -> x2, starting transfers between devices: 16 us -> 9.24 us  [columns(): lax.all_to_all(jnp.concatenate(shaped, -1).transpose(1, 0, 2), 'ctx', 0,...]
    broadcast_in_dim x6 -> x28, local copies, waits for them, and re-layouts: 0.42 us -> 4.88 us  [key_taps_of(): out = out + jnp.where(tap == c, weights[:, c][None, :, None], 0.0)]
    all_to_all x3 -> x2, waiting for transfers between devices: 18.8 us -> 17.8 us  [columns(): lax.all_to_all(jnp.concatenate(shaped, -1).transpose(1, 0, 2), 'ctx', 0,...]
    ppermute x27 -> x26, starting transfers between devices: 29.7 us -> 30 us  [swapped(): return lax.ppermute(value, axis, [(i, i ^ mask) for i in range(count)])]
  transfers between devices with their start and end apart: 35 -> 33, of which waited for: 18 -> 20; matrix products, arithmetic and copies ran while one was open for 8% -> 9% of each run, Pallas kernels for 15% -> 11%
where the time goes in v1:
time: 326 us; the launch traced here: 320 us
  waiting for transfers between devices  176 us (54%)
  starting transfers between devices  47.4 us (15%)
  Pallas kernels  42.9 us (13%)
  local copies, waits for them, and re-layouts  22 us (7%)
  other arithmetic  17.1 us (5%)
  between operations  14.4 us (4%)
    ppermute x26, waiting for transfers between devices, swapped(): return lax.ppermute(value, axis, [(i, i ^ mask) for i in range(count)])  144 us
    ppermute x26, starting transfers between devices, swapped(): return lax.ppermute(value, axis, [(i, i ^ mask) for i in range(count)])  30 us
    all_to_all x2, waiting for transfers between devices, columns(): lax.all_to_all(jnp.concatenate(shaped, -1).transpose(1, 0, 2), 'ctx', 0,...  17.8 us
    pallas_call x1, Pallas kernels, project(): pl.pallas_call(project_kernel, out_shape=(out, out, out), in_specs=[whole...  15.6 us
    pallas_call x1, Pallas kernels, attend_head(): pl.pallas_call(attend_kernel, grid=(count,), out_shape=(out, out), in_spe...  12.7 us
    ppermute x1, waiting for transfers between devices, per_device_one_head(): across = lax.ppermute(activations, 'ctx', middle)  10.2 us
    all_to_all x2, starting transfers between devices, columns(): lax.all_to_all(jnp.concatenate(shaped, -1).transpose(1, 0, 2), 'ctx', 0,...  9.24 us
    pallas_call x1, Pallas kernels, prepare(): pl.pallas_call(prepare_kernel, out_shape=(jax.ShapeDtypeStruct((total, CQ...  7.58 us
  transfers between devices with their start and end apart: 33, of which 20 were waited for; matrix products, arithmetic and copies ran while one was open for 9% of the time, Pallas kernels for 11%

profile of v1, /device:TPU:17, one launch (start us, length us, event | category | flops | bytes accessed | tf_op | source)
XLA Modules:
  0.0 319.8 jit_solution(8096135133236374693)
XLA Ops:
  6.5 1.6 copy.11
  9.8 1.5 maximum_bitcast_fusion
  11.3 4.8 %all-to-all-start = ((bf16[4,512,512]{2,1,0:T(8,128)(2,1)}), bf16[4,512,512]{2,1,0:T(8,128)(2,1)}, u32[]{:S(2)}, u32[]{:S(2)}) async-start(bf16[4,512,512]{2,1,0:T(8,128)(2,1)} %maximum_bitcast_fusion), calls=%async_computation | async-start | bytes 4194304 | tf_op jit(solution)/shard_map/all_to_all | solution.py:564
  16.1 1.2 collective-permute-start
  17.3 1.9 collective-permute-start.1
  19.2 1.3 collective-permute-start.2
  20.5 1.2 collective-permute-start.3
  21.7 40.6 %collective-permute-done.refs_1_ = bf16[256,1024]{1,0:T(8,128)(2,1)S(1)} collective-permute-done((bf16[256,1024]{1,0:T(8,128)(2,1)S(1)}, bf16[256,1024]{1,0:T(8,128)(2,1)S(1)}, u32[]{:S(2)}, u32[]{:S(2)}) %collective-permute-start) | collective-permute-done | bytes 524320 | tf_op jit(solution)/shard_map/ppermute | solution.py:551
  62.3 10.2 %collective-permute-done.1 = bf16[256,1024]{1,0:T(8,128)(2,1)S(1)} collective-permute-done((bf16[256,1024]{1,0:T(8,128)(2,1)S(1)}, bf16[256,1024]{1,0:T(8,128)(2,1)S(1)}, u32[]{:S(2)}, u32[]{:S(2)}) %collective-permute-start.1) | collective-permute-done | bytes 524320 | tf_op jit(solution)/shard_map/ppermute | solution.py:585
  72.5 0.8 copy-done.12
  73.3 0.8 copy-done.13
  74.3 1.3 collective-permute-start.6
  75.6 1.2 collective-permute-start.7
  76.9 3.5 %collective-permute-start.4 = (bf16[256,1024]{1,0:T(8,128)(2,1)S(1)}, bf16[256,1024]{1,0:T(8,128)(2,1)S(1)}, u32[]{:S(2)}, u32[]{:S(2)}) collective-permute-start(bf16[256,1024]{1,0:T(8,128)(2,1)S(1)} %collective-permute-done.refs_1_), channel_id=1, source_target_pairs={{8,16},{12,20},{16,8},{20,12},{9,17},{13,21},{17,9},{21,13},{10,18... | collective-permute-start | bytes 1572872 | tf_op jit(solution)/shard_map/ppermute | solution.py:590
  80.4 1.3 collective-permute-start.5
  81.8 9.1 %collective-permute-done.8 = s32[256]{0:T(256)S(1)} collective-permute-done((s32[256]{0:T(256)S(1)}, s32[256]{0:T(256)S(1)}, u32[]{:S(2)}, u32[]{:S(2)}) %collective-permute-start.8) | collective-permute-done | bytes 1056 | tf_op jit(solution)/shard_map/ppermute | solution.py:551
  91.6 0.9 collective-permute-done.7.refs_10_
  94.2 1.2 collective-permute-start.11
  95.5 1.5 collective-permute-start.9
  97.0 3.3 %collective-permute-done.12 = s32[2,256]{1,0:T(2,128)S(1)} collective-permute-done((s32[2,256]{1,0:T(2,128)S(1)}, s32[2,256]{1,0:T(2,128)S(1)}, u32[]{:S(2)}, u32[]{:S(2)}) %collective-permute-start.12) | collective-permute-done | bytes 2080 | tf_op jit(solution)/shard_map/ppermute | solution.py:551
  100.3 4.3 %collective-permute-done.9 = bf16[256,1024]{1,0:T(8,128)(2,1)S(1)} collective-permute-done((bf16[256,1024]{1,0:T(8,128)(2,1)S(1)}, bf16[256,1024]{1,0:T(8,128)(2,1)S(1)}, u32[]{:S(2)}, u32[]{:S(2)}) %collective-permute-start.9) | collective-permute-done | bytes 524320 | tf_op jit(solution)/shard_map/ppermute | solution.py:595
  104.6 5.1 %collective-permute-done.10.refs_6_ = bf16[384,1024]{1,0:T(8,128)(2,1)} collective-permute-done((bf16[384,1024]{1,0:T(8,128)(2,1)S(1)}, bf16[384,1024]{1,0:T(8,128)(2,1)}, u32[]{:S(2)}, u32[]{:S(2)}) %collective-permute-start.10) | collective-permute-done | bytes 786464 | tf_op jit(solution)/shard_map/ppermute | solution.py:551
  110.3 4.0 %collective-permute-start.15 = (bf16[4,512,512]{2,1,0:T(8,128)(2,1)}, bf16[4,512,512]{2,1,0:T(8,128)(2,1)}, u32[]{:S(2)}, u32[]{:S(2)}) collective-permute-start(bf16[4,512,512]{2,1,0:T(8,128)(2,1)} %all-to-all-done.refs_16_), channel_id=1, source_target_pairs={{0,4},{4,0},{8,12},{12,8},{16,20},{20,16},{24,28},{28,24},{1,5},{5... | collective-permute-start | bytes 6291464 | tf_op jit(solution)/shard_map/ppermute | solution.py:551
  114.9 1.3 copy.15
  116.2 4.5 %all-to-all-start.1 = ((bf16[4,512,256]{2,1,0:T(8,128)(2,1)}), bf16[4,512,256]{2,1,0:T(8,128)(2,1)S(1)}, u32[]{:S(2)}, u32[]{:S(2)}) async-start(bf16[4,512,256]{2,1,0:T(8,128)(2,1)} %bitcast.15), calls=%async_computation.1 | async-start | bytes 2097152 | tf_op jit(solution)/shard_map/all_to_all | solution.py:564
  120.9 1.1 slice.84
  122.0 1.0 slice.83
  123.2 1.0 collective-permute-start.13
  124.2 1.2 collective-permute-start.14
  125.4 17.8 %all-to-all-done.1.refs_14_ = bf16[4,512,256]{2,1,0:T(8,128)(2,1)S(1)} async-done(((bf16[4,512,256]{2,1,0:T(8,128)(2,1)}), bf16[4,512,256]{2,1,0:T(8,128)(2,1)S(1)}, u32[]{:S(2)}, u32[]{:S(2)}) %all-to-all-start.1) | async-done | bytes 1048608 | tf_op jit(solution)/shard_map/all_to_all | solution.py:564
  145.9 1.2 collective-permute-start.18
  147.6 1.0 slice.85
  148.6 1.0 collective-permute-start.16
  149.6 1.0 slice.86
  150.6 1.3 collective-permute-start.17
  151.9 1.9 fusion.3
  153.8 1.3 pad_maximum_fusion.6
  155.1 1.6 collective-permute-done.16.refs_8_
  156.7 1.6 collective-permute-done.17.refs_13_
  159.1 15.6 %shard_map.91 = (bf16[4,256,256]{2,1,0:T(8,128)(2,1)}, bf16[4,256,256]{2,1,0:T(8,128)(2,1)}, bf16[4,256,256]{2,1,0:T(8,128)(2,1)}) custom-call(s32[9]{0:T(128)} %stack.47.place, bf16[256,1024]{1,0:T(8,128)(2,1)} %refs_0_.1, bf16[256,1024]{1,0:T(8,128)(2,1)} %copy-done.6, bf16[256,1024]{1,0:T(8,128)(2,1)} %copy-done.1, bf16[256,1024]{1,0:T(8,128)(2,1)} %copy-done.2, ...), custom_call_target="tpu_custom_call" | custom-call | flops 6442450944 | bytes 16777216 | tf_op jit(solution)/shard_map/pallas_call | solution.py:262
  174.7 1.1 collective-permute-start.20
  180.4 2.4 add_convert_fusion.1.even_ref
  182.8 2.0 add_convert_fusion.3.odd_ref
  184.8 3.0 collective-permute-start.19
  187.8 1.9 add_convert_fusion.2.key_ref
  190.0 7.6 %shard_map.92 = (bf16[2048,768]{1,0:T(8,128)(2,1)}, bf16[768,2048]{1,0:T(8,128)(2,1)}, f32[8,256,384]{2,1,0:T(8,128)}) custom-call(s32[9]{0:T(128)} %stack.47.place, bf16[4,256,256]{2,1,0:T(8,128)(2,1)} %get-tuple-element.57.mine, bf16[4,256,256]{2,1,0:T(8,128)(2,1)} %collective-permute-done.20.other, bf16[256,768]{1,0:T(8,128)(2,1)} %add_convert_fusion.2.key_ref, ...), custom_call_target="tpu_custom_call" | custom-call | flops 2147483648 | bytes 12582912 | tf_op jit(solution)/shard_map/pallas_call | solution.py:347
  197.5 31.0 %collective-permute-done.19.vb = bf16[4,256,256]{2,1,0:T(8,128)(2,1)S(1)} collective-permute-done((bf16[4,256,256]{2,1,0:T(8,128)(2,1)S(1)}, bf16[4,256,256]{2,1,0:T(8,128)(2,1)S(1)}, u32[]{:S(2)}, u32[]{:S(2)}) %collective-permute-start.19) | collective-permute-done | bytes 524320 | tf_op jit(solution)/shard_map/ppermute | solution.py:551
  229.6 0.9 collective-permute-done.22.vd
  230.5 0.8 copy-done.21
  231.3 12.7 %shard_map.93 = (bf16[4,256,512]{2,1,0:T(8,128)(2,1)}, bf16[4,256,512]{2,1,0:T(8,128)(2,1)}) custom-call(s32[9]{0:T(128)} %stack.47.place, f32[4]{0:T(128)} %dynamic-slice_bitcast_fusion.1.mix, bf16[2048,768]{1,0:T(8,128)(2,1)} %get-tuple-element.60.q_ref, bf16[768,2048]{1,0:T(8,128)(2,1)} %get-tuple-element.61.k_ref, ...), custom_call_target="tpu_custom_call" | custom-call | flops 5368709120 | bytes 16777216 | tf_op jit(solution)/shard_map/pallas_call | solution.py:475
  244.4 2.5 collective-permute-done.23
  246.9 1.5 convert_add_fusion
  248.4 0.8 fusion.2
  249.3 2.3 collective-permute-start.24
  251.5 1.6 collective-permute-start.25
  253.4 0.8 dynamic-slice_bitcast_fusion.own
  254.2 8.1 %collective-permute-done.24.r1 = bf16[256,512]{1,0:T(8,128)(2,1)S(1)} collective-permute-done((bf16[256,512]{1,0:T(8,128)(2,1)}, bf16[256,512]{1,0:T(8,128)(2,1)S(1)}, u32[]{:S(2)}, u32[]{:S(2)}) %collective-permute-start.24) | collective-permute-done | bytes 262176 | tf_op jit(solution)/shard_map/ppermute | solution.py:551
  262.4 7.3 %collective-permute-done.25.r2 = bf16[256,512]{1,0:T(8,128)(2,1)S(1)} collective-permute-done((bf16[256,512]{1,0:T(8,128)(2,1)S(1)}, bf16[256,512]{1,0:T(8,128)(2,1)S(1)}, u32[]{:S(2)}, u32[]{:S(2)}) %collective-permute-start.25) | collective-permute-done | bytes 262176 | tf_op jit(solution)/shard_map/ppermute | solution.py:551
  269.7 6.6 %collective-permute-done.26.r3 = bf16[256,512]{1,0:T(8,128)(2,1)S(1)} collective-permute-done((bf16[256,512]{1,0:T(8,128)(2,1)S(1)}, bf16[256,512]{1,0:T(8,128)(2,1)S(1)}, u32[]{:S(2)}, u32[]{:S(2)}) %collective-permute-start.26) | collective-permute-done | bytes 262176 | tf_op jit(solution)/shard_map/ppermute | solution.py:551
  277.1 7.0 %shard_map.94 = (bf16[256,1024]{1,0:T(8,128)(2,1)}, bf16[256,1024]{1,0:T(8,128)(2,1)}, bf16[256,1024]{1,0:T(8,128)(2,1)}, bf16[256,1024]{1,0:T(8,128)(2,1)}) custom-call(s32[9]{0:T(128)} %stack.47.place, f32[256,512]{1,0:T(8,128)} %dynamic-slice_bitcast_fusion.own, bf16[256,512]{1,0:T(8,128)(2,1)} %copy-done.9, bf16[256,512]{1,0:T(8,128)(2,1)} %copy-done.10, ...), custom_call_target="tpu_custom_call" | custom-call | flops 2147483648 | bytes 11534336 | tf_op jit(solution)/shard_map/pallas_call | solution.py:532
  284.1 1.7 collective-permute-start.29
  286.8 10.7 %collective-permute-done.29 = bf16[256,1024]{1,0:T(8,128)(2,1)S(1)} collective-permute-done((bf16[256,1024]{1,0:T(8,128)(2,1)}, bf16[256,1024]{1,0:T(8,128)(2,1)S(1)}, u32[]{:S(2)}, u32[]{:S(2)}) %collective-permute-start.29) | collective-permute-done | bytes 524320 | tf_op jit(solution)/shard_map/ppermute | solution.py:551
  297.5 12.8 %collective-permute-done.28 = bf16[256,1024]{1,0:T(8,128)(2,1)S(1)} collective-permute-done((bf16[256,1024]{1,0:T(8,128)(2,1)}, bf16[256,1024]{1,0:T(8,128)(2,1)S(1)}, u32[]{:S(2)}, u32[]{:S(2)}) %collective-permute-start.28) | collective-permute-done | bytes 524320 | tf_op jit(solution)/shard_map/ppermute | solution.py:551
  310.3 2.2 add_convert_fusion
  (128 shorter events, 17.9 us)
Async XLA Ops:
  6.5 222.4 %copy-start = (f32[8,4]{0,1:T(4,128)S(1)}, f32[8,4]{0,1:T(4,128)}, u32[]{:S(2)}) copy-start(f32[8,4]{0,1:T(4,128)} %param.15) | copy-start | bytes 388
  6.5 2.1 copy-start.3
  11.3 4.8 %copy-start.17 = (bf16[256,1024]{1,0:T(8,128)(2,1)S(1)}, bf16[256,1024]{1,0:T(8,128)(2,1)}, u32[]{:S(2)}) copy-start(bf16[256,1024]{1,0:T(8,128)(2,1)} %refs_0_.1) | copy-start | bytes 1572868
  11.3 99.0 %all-to-all-start = ((bf16[4,512,512]{2,1,0:T(8,128)(2,1)}), bf16[4,512,512]{2,1,0:T(8,128)(2,1)}, u32[]{:S(2)}, u32[]{:S(2)}) async-start(bf16[4,512,512]{2,1,0:T(8,128)(2,1)} %maximum_bitcast_fusion), calls=%async_computation | async-start | bytes 4194304 | tf_op jit(solution)/shard_map/all_to_all | solution.py:564
  16.1 65.6 %copy-start.16 = (s32[256]{0:T(256)S(1)}, s32[256]{0:T(256)}, u32[]{:S(2)}) copy-start(s32[256]{0:T(256)} %param.10) | copy-start | bytes 3076
  16.1 46.2 %collective-permute-start = (bf16[256,1024]{1,0:T(8,128)(2,1)S(1)}, bf16[256,1024]{1,0:T(8,128)(2,1)S(1)}, u32[]{:S(2)}, u32[]{:S(2)}) collective-permute-start(bf16[256,1024]{1,0:T(8,128)(2,1)S(1)} %copy-done.17), channel_id=1, source_target_pairs={{0,8},{4,12},{8,0},{12,4},{16,24},{20,28},{24,16},{28,20},{1,9},{5... | collective-permute-start | bytes 1572872 | tf_op jit(solution)/shard_map/ppermute | solution.py:551
  17.3 55.2 %collective-permute-start.1 = (bf16[256,1024]{1,0:T(8,128)(2,1)S(1)}, bf16[256,1024]{1,0:T(8,128)(2,1)S(1)}, u32[]{:S(2)}, u32[]{:S(2)}) collective-permute-start(bf16[256,1024]{1,0:T(8,128)(2,1)S(1)} %copy-done.17), channel_id=1, source_target_pairs={{8,16},{12,20},{16,8},{20,12},{9,17},{13,21},{17,9},{21,13},{10,18... | collective-permute-start | bytes 1572872 | tf_op jit(solution)/shard_map/ppermute | solution.py:585
  19.2 53.3 %collective-permute-start.2 = (bf16[256,1024]{1,0:T(8,128)(2,1)S(1)}, bf16[256,1024]{1,0:T(8,128)(2,1)S(1)}, u32[]{:S(2)}, u32[]{:S(2)}) collective-permute-start(bf16[256,1024]{1,0:T(8,128)(2,1)S(1)} %copy-done.17), channel_id=1, source_target_pairs={{0,1},{1,0},{2,3},{3,2},{4,5},{5,4},{6,7},{7,6},{8,9},{9,8},{10,11... | collective-permute-start | bytes 1572872 | tf_op jit(solution)/shard_map/ppermute | solution.py:551
  20.5 52.1 %collective-permute-start.3 = (bf16[256,1024]{1,0:T(8,128)(2,1)S(1)}, bf16[256,1024]{1,0:T(8,128)(2,1)S(1)}, u32[]{:S(2)}, u32[]{:S(2)}) collective-permute-start(bf16[256,1024]{1,0:T(8,128)(2,1)S(1)} %copy-done.17), channel_id=1, source_target_pairs={{0,2},{1,3},{2,0},{3,1},{4,6},{5,7},{6,4},{7,5},{8,10},{9,11},{10,... | collective-permute-start | bytes 1572872 | tf_op jit(solution)/shard_map/ppermute | solution.py:551
  62.3 30.4 %copy-start.6 = (bf16[256,1024]{1,0:T(8,128)(2,1)}, bf16[256,1024]{1,0:T(8,128)(2,1)S(1)}, u32[]{:S(2)}) copy-start(bf16[256,1024]{1,0:T(8,128)(2,1)S(1)} %collective-permute-done.refs_1_) | copy-start | bytes 1572868
  72.5 0.8 copy-start.12
  73.3 0.8 copy-start.13
  74.3 17.2 %collective-permute-start.6 = (bf16[384,1024]{1,0:T(8,128)(2,1)S(1)}, bf16[384,1024]{1,0:T(8,128)(2,1)S(1)}, u32[]{:S(2)}, u32[]{:S(2)}) collective-permute-start(bf16[384,1024]{1,0:T(8,128)(2,1)S(1)} %get-tuple-element.90), channel_id=1, source_target_pairs={{0,1},{1,0},{2,3},{3,2},{4,5},{5,4},{6,7},{7,6},{8,9},{9,8},{10,11... | collective-permute-start | bytes 2359304 | tf_op jit(solution)/shard_map/ppermute | solution.py:551
  75.6 16.9 %collective-permute-start.7 = (bf16[384,1024]{1,0:T(8,128)(2,1)S(1)}, bf16[384,1024]{1,0:T(8,128)(2,1)S(1)}, u32[]{:S(2)}, u32[]{:S(2)}) collective-permute-start(bf16[384,1024]{1,0:T(8,128)(2,1)S(1)} %get-tuple-element.89), channel_id=1, source_target_pairs={{0,2},{1,3},{2,0},{3,1},{4,6},{5,7},{6,4},{7,5},{8,10},{9,11},{10,... | collective-permute-start | bytes 2359304 | tf_op jit(solution)/shard_map/ppermute | solution.py:551
  76.9 14.0 %collective-permute-start.4 = (bf16[256,1024]{1,0:T(8,128)(2,1)S(1)}, bf16[256,1024]{1,0:T(8,128)(2,1)S(1)}, u32[]{:S(2)}, u32[]{:S(2)}) collective-permute-start(bf16[256,1024]{1,0:T(8,128)(2,1)S(1)} %collective-permute-done.refs_1_), channel_id=1, source_target_pairs={{8,16},{12,20},{16,8},{20,12},{9,17},{13,21},{17,9},{21,13},{10,18... | collective-permute-start | bytes 1572872 | tf_op jit(solution)/shard_map/ppermute | solution.py:590
  80.4 10.5 %collective-permute-start.5 = (bf16[256,1024]{1,0:T(8,128)(2,1)S(1)}, bf16[256,1024]{1,0:T(8,128)(2,1)S(1)}, u32[]{:S(2)}, u32[]{:S(2)}) collective-permute-start(bf16[256,1024]{1,0:T(8,128)(2,1)S(1)} %collective-permute-done.1), channel_id=1, source_target_pairs={{8,0},{12,4},{16,24},{20,28},{9,1},{13,5},{17,25},{21,29},{10,2},{... | collective-permute-start | bytes 1572872 | tf_op jit(solution)/shard_map/ppermute | solution.py:591
  81.7 9.2 %collective-permute-start.8 = (s32[256]{0:T(256)S(1)}, s32[256]{0:T(256)S(1)}, u32[]{:S(2)}, u32[]{:S(2)}) collective-permute-start(s32[256]{0:T(256)S(1)} %copy-done.16), channel_id=1, source_target_pairs={{0,8},{4,12},{8,0},{12,4},{16,24},{20,28},{24,16},{28,20},{1,9},{5... | collective-permute-start | bytes 3080 | tf_op jit(solution)/shard_map/ppermute | solution.py:551
  91.6 1.2 copy-start.14
  92.5 0.9 copy-start.15
  92.7 22.1 %copy-start.1 = (bf16[256,1024]{1,0:T(8,128)(2,1)}, bf16[256,1024]{1,0:T(8,128)(2,1)S(1)}, u32[]{:S(2)}) copy-start(bf16[256,1024]{1,0:T(8,128)(2,1)S(1)} %add.295.refs_2_) | copy-start | bytes 1572868
  92.7 21.6 %copy-start.4 = (bf16[512,1024]{1,0:T(8,128)(2,1)S(1)}, bf16[512,1024]{1,0:T(8,128)(2,1)}, u32[]{:S(2)}) copy-start(bf16[512,1024]{1,0:T(8,128)(2,1)} %param.11) | copy-start | bytes 3145732
  93.6 16.1 %collective-permute-start.10 = (bf16[384,1024]{1,0:T(8,128)(2,1)S(1)}, bf16[384,1024]{1,0:T(8,128)(2,1)}, u32[]{:S(2)}, u32[]{:S(2)}) collective-permute-start(bf16[384,1024]{1,0:T(8,128)(2,1)S(1)} %get-tuple-element.88), channel_id=1, source_target_pairs={{0,1},{1,0},{2,3},{3,2},{4,5},{5,4},{6,7},{7,6},{8,9},{9,8},{10,11... | collective-permute-start | bytes 2359304 | tf_op jit(solution)/shard_map/ppermute | solution.py:551
  94.2 16.1 %collective-permute-start.11 = (bf16[384,1024]{1,0:T(8,128)(2,1)S(1)}, bf16[384,1024]{1,0:T(8,128)(2,1)}, u32[]{:S(2)}, u32[]{:S(2)}) collective-permute-start(bf16[384,1024]{1,0:T(8,128)(2,1)S(1)} %get-tuple-element.87), channel_id=1, source_target_pairs={{0,2},{1,3},{2,0},{3,1},{4,6},{5,7},{6,4},{7,5},{8,10},{9,11},{10,... | collective-permute-start | bytes 2359304 | tf_op jit(solution)/shard_map/ppermute | solution.py:551
  95.5 9.2 %collective-permute-start.9 = (bf16[256,1024]{1,0:T(8,128)(2,1)S(1)}, bf16[256,1024]{1,0:T(8,128)(2,1)S(1)}, u32[]{:S(2)}, u32[]{:S(2)}) collective-permute-start(bf16[256,1024]{1,0:T(8,128)(2,1)S(1)} %collective-permute-done.4), channel_id=1, source_target_pairs={{8,0},{12,4},{16,24},{20,28},{9,1},{13,5},{17,25},{21,29},{10,2},{... | collective-permute-start | bytes 1572872 | tf_op jit(solution)/shard_map/ppermute | solution.py:595
  96.9 3.4 %collective-permute-start.12 = (s32[2,256]{1,0:T(2,128)S(1)}, s32[2,256]{1,0:T(2,128)S(1)}, u32[]{:S(2)}, u32[]{:S(2)}) collective-permute-start(s32[2,256]{1,0:T(2,128)S(1)} %pad_add_fusion), channel_id=1, source_target_pairs={{0,16},{4,20},{8,24},{12,28},{16,0},{20,4},{24,8},{28,12},{1,17},{... | collective-permute-start | bytes 6152 | tf_op jit(solution)/shard_map/ppermute | solution.py:551
  104.6 5.7 %copy-start.7 = (bf16[256,1024]{1,0:T(8,128)(2,1)}, bf16[256,1024]{1,0:T(8,128)(2,1)S(1)}, u32[]{:S(2)}) copy-start(bf16[256,1024]{1,0:T(8,128)(2,1)S(1)} %collective-permute-done.9) | copy-start | bytes 1572868
  110.3 32.9 %collective-permute-start.15 = (bf16[4,512,512]{2,1,0:T(8,128)(2,1)}, bf16[4,512,512]{2,1,0:T(8,128)(2,1)}, u32[]{:S(2)}, u32[]{:S(2)}) collective-permute-start(bf16[4,512,512]{2,1,0:T(8,128)(2,1)} %all-to-all-done.refs_16_), channel_id=1, source_target_pairs={{0,4},{4,0},{8,12},{12,8},{16,20},{20,16},{24,28},{28,24},{1,5},{5... | collective-permute-start | bytes 6291464 | tf_op jit(solution)/shard_map/ppermute | solution.py:551
  114.8 5.8 %copy-start.8 = (bf16[256,1024]{1,0:T(8,128)(2,1)S(1)}, bf16[256,1024]{1,0:T(8,128)(2,1)}, u32[]{:S(2)}) copy-start(bf16[256,1024]{1,0:T(8,128)(2,1)} %copy-done.7) | copy-start | bytes 1572868
  116.2 27.0 %all-to-all-start.1 = ((bf16[4,512,256]{2,1,0:T(8,128)(2,1)}), bf16[4,512,256]{2,1,0:T(8,128)(2,1)S(1)}, u32[]{:S(2)}, u32[]{:S(2)}) async-start(bf16[4,512,256]{2,1,0:T(8,128)(2,1)} %bitcast.15), calls=%async_computation.1 | async-start | bytes 2097152 | tf_op jit(solution)/shard_map/all_to_all | solution.py:564
  120.7 155.7 %all-gather.3.cloned.1.call-start = ((), (), s32[]{:S(2)}) async-start(), calls=%async_computation.2 | async-start | bytes 9437184 | tf_op jit(solution)/shard_map/all_gather | solution.py:651
  120.9 22.4 %copy-start.2 = (bf16[256,1024]{1,0:T(8,128)(2,1)}, bf16[256,1024]{1,0:T(8,128)(2,1)S(1)}, u32[]{:S(2)}) copy-start(bf16[256,1024]{1,0:T(8,128)(2,1)S(1)} %add.296.refs_3_) | copy-start | bytes 1572868
  123.2 20.0 %collective-permute-start.13 = (bf16[384,1024]{1,0:T(8,128)(2,1)S(1)}, bf16[384,1024]{1,0:T(8,128)(2,1)}, u32[]{:S(2)}, u32[]{:S(2)}) collective-permute-start(bf16[384,1024]{1,0:T(8,128)(2,1)S(1)} %get-tuple-element.86), channel_id=1, source_target_pairs={{0,1},{1,0},{2,3},{3,2},{4,5},{5,4},{6,7},{7,6},{8,9},{9,8},{10,11... | collective-permute-start | bytes 2359304 | tf_op jit(solution)/shard_map/ppermute | solution.py:551
  124.2 19.1 %collective-permute-start.14 = (bf16[384,1024]{1,0:T(8,128)(2,1)S(1)}, bf16[384,1024]{1,0:T(8,128)(2,1)}, u32[]{:S(2)}, u32[]{:S(2)}) collective-permute-start(bf16[384,1024]{1,0:T(8,128)(2,1)S(1)} %get-tuple-element.85), channel_id=1, source_target_pairs={{0,2},{1,3},{2,0},{3,1},{4,6},{5,7},{6,4},{7,5},{8,10},{9,11},{10,... | collective-permute-start | bytes 2359304 | tf_op jit(solution)/shard_map/ppermute | solution.py:551
  143.2 10.6 %copy-start.5 = (bf16[4,512,256]{2,1,0:T(8,128)(2,1)}, bf16[4,512,256]{2,1,0:T(8,128)(2,1)S(1)}, u32[]{:S(2)}) copy-start(bf16[4,512,256]{2,1,0:T(8,128)(2,1)S(1)} %all-to-all-done.1.refs_14_) | copy-start | bytes 3145732
  145.9 12.5 %collective-permute-start.18 = (bf16[4,512,256]{2,1,0:T(8,128)(2,1)S(1)}, bf16[4,512,256]{2,1,0:T(8,128)(2,1)}, u32[]{:S(2)}, u32[]{:S(2)}) collective-permute-start(bf16[4,512,256]{2,1,0:T(8,128)(2,1)S(1)} %all-to-all-done.1.refs_14_), channel_id=1, source_target_pairs={{0,4},{4,0},{8,12},{12,8},{16,20},{20,16},{24,28},{28,24},{1,5},{5... | collective-permute-start | bytes 3145736 | tf_op jit(solution)/shard_map/ppermute | solution.py:551
  148.6 8.1 %collective-permute-start.16 = (bf16[128,1024]{1,0:T(8,128)(2,1)S(1)}, bf16[128,1024]{1,0:T(8,128)(2,1)S(1)}, u32[]{:S(2)}, u32[]{:S(2)}) collective-permute-start(bf16[128,1024]{1,0:T(8,128)(2,1)S(1)} %slice.85), channel_id=1, source_target_pairs={{0,1},{1,0},{2,3},{3,2},{4,5},{5,4},{6,7},{7,6},{8,9},{9,8},{10,11... | collective-permute-start | bytes 786440 | tf_op jit(solution)/shard_map/ppermute | solution.py:551
  150.6 7.8 %collective-permute-start.17 = (bf16[128,1024]{1,0:T(8,128)(2,1)S(1)}, bf16[128,1024]{1,0:T(8,128)(2,1)S(1)}, u32[]{:S(2)}, u32[]{:S(2)}) collective-permute-start(bf16[128,1024]{1,0:T(8,128)(2,1)S(1)} %slice.86), channel_id=1, source_target_pairs={{0,2},{1,3},{2,0},{3,1},{4,6},{5,7},{6,4},{7,5},{8,10},{9,11},{10,... | collective-permute-start | bytes 786440 | tf_op jit(solution)/shard_map/ppermute | solution.py:551
  156.7 1.6 copy-start.22
  158.3 0.7 copy-start.23
  174.7 15.3 %collective-permute-start.20 = (bf16[4,256,256]{2,1,0:T(8,128)(2,1)}, bf16[4,256,256]{2,1,0:T(8,128)(2,1)}, u32[]{:S(2)}, u32[]{:S(2)}) collective-permute-start(bf16[4,256,256]{2,1,0:T(8,128)(2,1)} %get-tuple-element.58), channel_id=1, source_target_pairs={{0,4},{4,0},{8,12},{12,8},{16,20},{20,16},{24,28},{28,24},{1,5},{5... | collective-permute-start | bytes 1572872 | tf_op jit(solution)/shard_map/ppermute | solution.py:551
  178.3 6.5 %copy-start.18 = (bf16[4,256,256]{2,1,0:T(8,128)(2,1)S(1)}, bf16[4,256,256]{2,1,0:T(8,128)(2,1)}, u32[]{:S(2)}) copy-start(bf16[4,256,256]{2,1,0:T(8,128)(2,1)} %get-tuple-element.56.va) | copy-start | bytes 1572868
  184.8 43.8 %collective-permute-start.19 = (bf16[4,256,256]{2,1,0:T(8,128)(2,1)S(1)}, bf16[4,256,256]{2,1,0:T(8,128)(2,1)S(1)}, u32[]{:S(2)}, u32[]{:S(2)}) collective-permute-start(bf16[4,256,256]{2,1,0:T(8,128)(2,1)S(1)} %copy-done.18), channel_id=1, source_target_pairs={{0,8},{4,12},{8,0},{12,4},{16,24},{20,28},{24,16},{28,20},{1,9},{5... | collective-permute-start | bytes 1572872 | tf_op jit(solution)/shard_map/ppermute | solution.py:551
  189.7 39.9 %collective-permute-start.21 = (bf16[4,256,256]{2,1,0:T(8,128)(2,1)S(1)}, bf16[4,256,256]{2,1,0:T(8,128)(2,1)S(1)}, u32[]{:S(2)}, u32[]{:S(2)}) collective-permute-start(bf16[4,256,256]{2,1,0:T(8,128)(2,1)S(1)} %copy-done.18), channel_id=1, source_target_pairs={{0,4},{4,0},{8,12},{12,8},{16,20},{20,16},{24,28},{28,24},{1,5},{5... | collective-permute-start | bytes 1572872 | tf_op jit(solution)/shard_map/ppermute | solution.py:551
  228.6 1.9 copy-start.19
  228.6 1.9 collective-permute-start.22
  229.6 0.9 copy-start.20
  230.5 0.8 copy-start.21
  244.0 2.9 collective-permute-start.23
  249.3 13.1 %collective-permute-start.24 = (bf16[256,512]{1,0:T(8,128)(2,1)}, bf16[256,512]{1,0:T(8,128)(2,1)S(1)}, u32[]{:S(2)}, u32[]{:S(2)}) collective-permute-start(bf16[256,512]{1,0:T(8,128)(2,1)} %get-tuple-element.84), channel_id=1, source_target_pairs={{0,8},{4,12},{8,0},{12,4},{16,24},{20,28},{24,16},{28,20},{1,9},{5... | collective-permute-start | bytes 786440 | tf_op jit(solution)/shard_map/ppermute | solution.py:551
  251.5 18.2 %collective-permute-start.25 = (bf16[256,512]{1,0:T(8,128)(2,1)S(1)}, bf16[256,512]{1,0:T(8,128)(2,1)S(1)}, u32[]{:S(2)}, u32[]{:S(2)}) collective-permute-start(bf16[256,512]{1,0:T(8,128)(2,1)S(1)} %get-tuple-element.83), channel_id=1, source_target_pairs={{0,16},{4,20},{8,24},{12,28},{16,0},{20,4},{24,8},{28,12},{1,17},{... | collective-permute-start | bytes 786440 | tf_op jit(solution)/shard_map/ppermute | solution.py:551
  253.1 23.2 %collective-permute-start.26 = (bf16[256,512]{1,0:T(8,128)(2,1)S(1)}, bf16[256,512]{1,0:T(8,128)(2,1)S(1)}, u32[]{:S(2)}, u32[]{:S(2)}) collective-permute-start(bf16[256,512]{1,0:T(8,128)(2,1)S(1)} %get-tuple-element.82), channel_id=1, source_target_pairs={{0,24},{4,28},{8,16},{12,20},{16,8},{20,12},{24,0},{28,4},{1,25},{... | collective-permute-start | bytes 786440 | tf_op jit(solution)/shard_map/ppermute | solution.py:551
  262.4 14.0 %copy-start.9 = (bf16[256,512]{1,0:T(8,128)(2,1)}, bf16[256,512]{1,0:T(8,128)(2,1)S(1)}, u32[]{:S(2)}) copy-start(bf16[256,512]{1,0:T(8,128)(2,1)S(1)} %collective-permute-done.24.r1) | copy-start | bytes 786436
  269.7 6.6 %copy-start.10 = (bf16[256,512]{1,0:T(8,128)(2,1)}, bf16[256,512]{1,0:T(8,128)(2,1)S(1)}, u32[]{:S(2)}) copy-start(bf16[256,512]{1,0:T(8,128)(2,1)S(1)} %collective-permute-done.25.r2) | copy-start | bytes 786436
  276.4 0.7 copy-start.11
  284.1 13.4 %collective-permute-start.29 = (bf16[256,1024]{1,0:T(8,128)(2,1)}, bf16[256,1024]{1,0:T(8,128)(2,1)S(1)}, u32[]{:S(2)}, u32[]{:S(2)}) collective-permute-start(bf16[256,1024]{1,0:T(8,128)(2,1)} %get-tuple-element.70), channel_id=1, source_target_pairs={{0,3},{1,2},{2,1},{3,0},{4,7},{5,6},{6,5},{7,4},{8,11},{9,10},{10,... | collective-permute-start | bytes 1572872 | tf_op jit(solution)/shard_map/ppermute | solution.py:551
  285.8 24.6 %collective-permute-start.28 = (bf16[256,1024]{1,0:T(8,128)(2,1)}, bf16[256,1024]{1,0:T(8,128)(2,1)S(1)}, u32[]{:S(2)}, u32[]{:S(2)}) collective-permute-start(bf16[256,1024]{1,0:T(8,128)(2,1)} %get-tuple-element.69), channel_id=1, source_target_pairs={{0,2},{1,3},{2,0},{3,1},{4,6},{5,7},{6,4},{7,5},{8,10},{9,11},{10,... | collective-permute-start | bytes 1572872 | tf_op jit(solution)/shard_map/ppermute | solution.py:551
  286.0 24.3 %collective-permute-start.27 = (bf16[256,1024]{1,0:T(8,128)(2,1)}, bf16[256,1024]{1,0:T(8,128)(2,1)S(1)}, u32[]{:S(2)}, u32[]{:S(2)}) collective-permute-start(bf16[256,1024]{1,0:T(8,128)(2,1)} %get-tuple-element.68), channel_id=1, source_target_pairs={{0,1},{1,0},{2,3},{3,2},{4,5},{5,4},{6,7},{7,6},{8,9},{9,8},{10,11... | collective-permute-start | bytes 1572872 | tf_op jit(solution)/shard_map/ppermute | solution.py:551
Sparse Core Ops, SparseCore 0:
  143.4 94.7 all-gather.2

commit v2 on v1

--- a/solution.py
+++ b/solution.py
@@ -1,3 +1,4 @@
+import functools
 import math
 
 import jax
@@ -191,14 +192,14 @@
     return pl.BlockSpec(memory_space=memory_space)
 
 
-def project_kernel(place, *refs):
+def project_kernel(rows, place, *refs):
     a_own, a_x, a_y = refs[:4], refs[4:9], refs[9:14]
     weights = refs[14:18]
     cos_ref, sin_ref = refs[18:20]
     mine, theirs, v_out = refs[20:23]
     abuf, wbuf, acc, sem_a, sem_w = refs[23:]
     turn, core = place[0], place[1]
-    rows, depth = a_own[0].shape
+    depth = a_own[0].shape[1]
     half = weights[0].shape[1]
 
     def copies(t):
@@ -244,7 +245,7 @@
         total = acc[b * rows : (b + 1) * rows]
         cosine, sine = cos_ref[b], sin_ref[b]
         at = place[5 + b]
-        for col, out in ((0, 0), (4 * HD, HD)):
+        for col, out in ((4 * HD, 0), (2 * HD, HD)):
             heads = []
             for start in (col, col + HD):
                 x = total[:, start : start + HD]
@@ -252,7 +253,7 @@
                 heads.append(x.astype(jnp.bfloat16))
             mine[at, :, out : out + HD] = jnp.where(first, heads[0], heads[1])
             theirs[at, :, out : out + HD] = jnp.where(first, heads[1], heads[0])
-        v_out[at] = total[:, 2 * HD : 4 * HD].astype(jnp.bfloat16)
+        v_out[at] = total[:, : 2 * HD].astype(jnp.bfloat16)
 
 
 def project(place, a_own, a_x, a_y, weights, cosine, sine):
@@ -260,7 +261,7 @@
     width = weights[0].shape[2] + weights[2].shape[2]
     out = jax.ShapeDtypeStruct((4, rows, 2 * HD), jnp.bfloat16)
     return pl.pallas_call(
-        project_kernel,
+        functools.partial(project_kernel, rows),
         out_shape=(out, out, out),
         in_specs=[whole(pltpu.SMEM)] + [whole(pl.ANY)] * 18 + [whole(pltpu.VMEM)] * 2,
         out_specs=[whole(pltpu.VMEM)] * 3,
@@ -495,17 +496,19 @@
     )(place, mix, q_wide, k_wide, corr, va, vb, vc, vd)
 
 
-def finish_kernel(place, own, r1, r2, r3, gain, w_any, o0, o1, o2, o3, normed, w_buf, sem):
-    blocks, _, width = w_buf.shape
-    per = blocks // 4
-    order = [(t, i) for t in (3, 2, 1, 0) for i in range(per)]
+def finish_kernel(place, own, r1, r2, r3, gain, *refs):
+    w_parts, outs = refs[:8], refs[8:12]
+    normed, w_buf, sem = refs[12:]
+    width = w_parts[0].shape[1]
+    core, head = place[1], place[0]
 
     def copy_w(n):
-        t, i = order[n]
-        source = per * lax.bitwise_xor(place[4], t) + i
-        return pltpu.make_async_copy(w_any.at[source], w_buf.at[n], sem.at[n])
-
-    for n in range(blocks):
+        side = core if n % 2 == 0 else 1 - core
+        cols = pl.ds(pl.multiple_of(side * width, width), width)
+        target = w_buf.at[lax.bitwise_xor(place[5 + n // 2], head), :, cols]
+        return pltpu.make_async_copy(w_parts[n], target, sem.at[n])
+
+    for n in range(8):
         copy_w(n).start()
     near = own[...] + r1[...].astype(jnp.float32)
     far = r2[...].astype(jnp.float32) + r3[...].astype(jnp.float32)
@@ -518,32 +521,32 @@
         normed[:, g * HD : (g + 1) * HD] = (
             x * scale * gain[:, g * HD : (g + 1) * HD]
         ).astype(jnp.bfloat16)
-    for n in range(blocks):
-        t, i = order[n]
+    for n in range(8):
         copy_w(n).wait()
-        (o0, o1, o2, o3)[t][:, i * width : (i + 1) * width] = jnp.dot(
-            normed[...], w_buf[n], preferred_element_type=jnp.float32
+    for t in (3, 2, 1, 0):
+        outs[t][...] = jnp.dot(
+            normed[...], w_buf[t], preferred_element_type=jnp.float32
         ).astype(jnp.bfloat16)
 
 
-def finish(place, own, r1, r2, r3, gain, w_all):
+def finish(place, own, r1, r2, r3, gain, w_parts):
     rows = own.shape[0]
-    blocks, depth, width = w_all.shape
+    depth, width = w_parts[0].shape
     return pl.pallas_call(
         finish_kernel,
-        in_specs=[whole(pltpu.SMEM)] + [whole(pltpu.VMEM)] * 5 + [whole(pl.ANY)],
+        in_specs=[whole(pltpu.SMEM)] + [whole(pltpu.VMEM)] * 5 + [whole(pl.ANY)] * 8,
         out_specs=[whole(pltpu.VMEM)] * 4,
-        out_shape=[jax.ShapeDtypeStruct((rows, blocks // 4 * width), jnp.bfloat16)] * 4,
+        out_shape=[jax.ShapeDtypeStruct((rows, 2 * width), jnp.bfloat16)] * 4,
         scratch_shapes=[
             pltpu.VMEM((rows, depth), jnp.bfloat16),
-            pltpu.VMEM((blocks, depth, width), jnp.bfloat16),
-            pltpu.SemaphoreType.DMA((blocks,)),
+            pltpu.VMEM((4, depth, 2 * width), jnp.bfloat16),
+            pltpu.SemaphoreType.DMA((8,)),
         ],
         compiler_params=kernel_params(),
         cost_estimate=pl.CostEstimate(
-            flops=2 * rows * depth * blocks * width, bytes_accessed=11 * 2**20, transcendentals=0
+            flops=2 * rows * depth * 8 * width, bytes_accessed=11 * 2**20, transcendentals=0
         ),
-    )(place, own, r1, r2, r3, gain, w_all)
+    )(place, own, r1, r2, r3, gain, *w_parts)
 
 
 def swapped(value, axis, mask):
@@ -574,69 +577,89 @@
     inner = (z == 1) | (z == 2)
     rows = activations.shape[0]
     half = rows // 2
+    barrier = lax.optimization_barrier
 
     def plane(block, x_before, y_before):
-        to_x = jnp.concatenate([block, y_before[half:rows]])
-        to_y = jnp.concatenate([block, x_before[:half]])
+        to_x = jnp.concatenate([block[:rows], y_before[half:rows]])
+        to_y = jnp.concatenate([block[:rows], x_before[:half]])
         return swapped(to_x, "head", 1), swapped(to_y, "head", 2)
 
-    barrier = lax.optimization_barrier
-    near = swapped(activations, "ctx", 2)
-    across = lax.ppermute(activations, "ctx", middle)
+    digits = jnp.stack([positions // 256, positions % 256]).astype(jnp.bfloat16)
+    digits = jnp.pad(digits, ((0, 14), (0, activations.shape[1] - rows)))
+    block = jnp.concatenate([activations, digits])
+    near = swapped(block, "ctx", 2)
+    across = lax.ppermute(block, "ctx", middle)
     x0, y0 = swapped(activations, "head", 1), swapped(activations, "head", 2)
-    place_near = swapped(positions, "ctx", 2)
-    vk_same, q_same = columns(w_value, w_key), columns(w_query)
-    near, across, x0, y0 = barrier((near, across, x0, y0))
+    near, across, x0, y0, w_value, w_key, w_query = barrier(
+        (near, across, x0, y0, w_value, w_key, w_query)
+    )
+    v_same, kq_same = columns(w_value), columns(w_key, w_query)
     across_next = lax.ppermute(near, "ctx", middle)
     passed = lax.ppermute(across, "ctx", outward)
     x1, y1 = plane(near, x0, y0)
-    across_next, passed, x1, y1, place_near = barrier((across_next, passed, x1, y1, place_near))
+    across_next, passed, x1, y1 = barrier((across_next, passed, x1, y1))
     far_a = across + passed
     passed_next = lax.ppermute(across_next, "ctx", outward)
     x2, y2 = plane(far_a, x1, y1)
-    place_far = swapped(jnp.stack([positions, place_near]), "ctx", 4)
-    passed_next, x2, y2, place_far, vk_same = barrier((passed_next, x2, y2, place_far, vk_same))
+    weights = lax.dynamic_index_in_dim(conv_kernel, ctx, 0, keepdims=False)
+    weights = weights * (math.log2(math.e) / math.sqrt(HD))
+    taps = weights.reshape(CQ, CK)
+    tables = key_taps_of(taps), band_taps(taps, -BAND, 2 * LANES), band_taps(taps, -SUB, LANES)
+    passed_next, x2, y2, v_same, tables = barrier((passed_next, x2, y2, v_same, tables))
     far_b = across_next + passed_next
     x3, y3 = plane(far_b, x2, y2)
-    vk_swap = swapped(vk_same, "ctx", 1)
-    x3, y3, vk_swap, q_same, w_out = barrier((x3, y3, vk_swap, q_same, w_out))
+    v_swap = swapped(v_same, "ctx", 1)
+    x3, y3, v_swap, kq_same, w_out = barrier((x3, y3, v_swap, kq_same, w_out))
     x4, y4 = swapped(y3[half:rows], "head", 1), swapped(x3[:half], "head", 2)
-    q_swap = swapped(q_same, "ctx", 1)
-
-    place_far = jnp.where(inner, place_far[::-1], place_far)
-    place_of = jnp.concatenate([jnp.stack([positions, place_near]), place_far])
+    kq_swap = swapped(kq_same, "ctx", 1)
+    w_near = swapped(w_out, "ctx", 2)
+    w_across = lax.ppermute(w_out, "ctx", middle)
+    x4, y4, kq_swap, w_near, w_across = barrier((x4, y4, kq_swap, w_near, w_across))
+    w_across_next = lax.ppermute(w_near, "ctx", middle)
+    w_passed = lax.ppermute(w_across, "ctx", outward)
+
+    tokens = (block, near, far_a, far_b)
+    place_of = jnp.stack(
+        [a[rows, :rows].astype(jnp.float32) * 256.0 + a[rows + 1, :rows].astype(jnp.float32) for a in tokens]
+    )
     order = jnp.where(inner, z ^ 3, z ^ 2), jnp.where(inner, z ^ 2, z ^ 3)
     place = jnp.stack([head, core, z % 2, z // 2, head, z, z ^ 1, *order]).astype(jnp.int32)
 
     exponents = jnp.arange(HD // 2, dtype=jnp.float32) * (2.0 / HD)
     inverse = jnp.exp(-exponents * math.log(500000.0))
-    angle = (place_of.astype(jnp.float32) * 0.25)[:, :, None] * inverse
+    angle = (place_of * 0.25)[:, :, None] * inverse
     cosine, sine = jnp.cos(angle), jnp.sin(angle)
     mine, theirs, v_pair = project(
         place,
         (activations, near, far_a, far_b),
         (x0, x1, x2, x3, x4),
         (y0, y1, y2, y3, y4),
-        (q_same, q_swap, vk_same, vk_swap),
+        (v_same, v_swap, kq_same, kq_swap),
         jnp.concatenate([cosine, cosine], -1),
         jnp.concatenate([-sine, sine], -1),
+    )
+    mine, theirs, v_pair, w_across_next, w_passed = barrier(
+        (mine, theirs, v_pair, w_across_next, w_passed)
     )
     other = swapped(theirs, "ctx", 1)
     v_next = swapped(v_pair, "ctx", 2)
     v_pair_other = swapped(v_pair, "ctx", 1)
-
-    weights = lax.dynamic_index_in_dim(conv_kernel, ctx, 0, keepdims=False)
-    weights = weights * (math.log2(math.e) / math.sqrt(HD))
-    taps = weights.reshape(CQ, CK)
-    tables = key_taps_of(taps), band_taps(taps, -BAND, 2 * LANES), band_taps(taps, -SUB, LANES)
+    w_passed_next = lax.ppermute(w_across_next, "ctx", outward)
     q_wide, k_wide, corr = prepare(place, mine, other, *tables)
     v_next, q_wide = barrier((v_next, q_wide))
     v_next_other = swapped(v_next, "ctx", 1)
+    w_own_swap, w_near_swap = swapped(w_out, "ctx", 1), swapped(w_near, "ctx", 1)
+    w_far_a = w_across + w_passed
     group_rows = lax.dynamic_slice_in_dim(head_mix, GROUP * (ctx // GROUP), GROUP, 0)
     mix = lax.dynamic_index_in_dim(group_rows, ctx % GROUP, 1, keepdims=False)
     out_mine, out_theirs = attend_head(
         place, mix, q_wide, k_wide, corr, v_pair, v_next, v_pair_other, v_next_other
     )
+    out_mine, out_theirs, w_own_swap, w_near_swap, w_passed_next = barrier(
+        (out_mine, out_theirs, w_own_swap, w_near_swap, w_passed_next)
+    )
+    w_far_b = w_across_next + w_passed_next
+    w_far_a_swap, w_far_b_swap = swapped(w_far_a, "ctx", 1), swapped(w_far_b, "ctx", 1)
     summed = out_mine.astype(jnp.float32) + swapped(out_theirs, "ctx", 1).astype(jnp.float32)
     own = lax.dynamic_index_in_dim(summed, z, 0, keepdims=False)
     r1, r2, r3 = [
@@ -648,8 +671,9 @@
         for s in (1, 2, 3)
     ]
 
-    w_all = lax.all_gather(w_out, "ctx", axis=0)
-    shares = finish(place, own, r1, r2, r3, out_gain.reshape(1, -1), w_all)
+    w_parts = (w_out, w_own_swap, w_near, w_near_swap)
+    w_parts += (w_far_a, w_far_a_swap, w_far_b, w_far_b_swap)
+    shares = finish(place, own, r1, r2, r3, out_gain.reshape(1, -1), w_parts)
     total = shares[0].astype(jnp.float32)
     for t in (1, 2, 3):
         total = total + swapped(shares[t], "head", t).astype(jnp.float32)

time: 326 us -> 357 us (1.095)
  starting transfers between devices: 47.4 us -> 69.7 us
  local copies, waits for them, and re-layouts: 22 us -> 39.7 us
  other arithmetic: 17.1 us -> 31.7 us
  between operations: 14.4 us -> 0.88 us
  waiting for transfers between devices: 176 us -> 165 us
    ppermute x26 -> x29, waiting for transfers between devices: 144 us -> 93.1 us  [swapped(): return lax.ppermute(value, axis, [(i, i ^ mask) for i in range(count)])]
    ppermute x1, waiting for transfers between devices: 0.01 us -> 48.9 us  [per_device_one_head(): across_next = lax.ppermute(near, 'ctx', middle)]
    ppermute x1 -> x5, starting transfers between devices: 1.91 us -> 23.6 us  [the longest x1 13.6 us: per_device_one_head(): w_passed_next = lax.ppermute(w_across_next, 'ctx', outward)]
    broadcast_in_dim x28, local copies, waits for them, and re-layouts: 4.88 us -> 22.7 us  [key_taps_of(): out = out + jnp.where(tap == c, weights[:, c][None, :, None], 0.0)]
    ppermute x1 -> x5, waiting for transfers between devices: 10.2 us -> 4.83 us  [the longest x1 2.9 us: per_device_one_head(): w_across = lax.ppermute(w_out, 'ctx', middle)]
    add x0 -> x5, other arithmetic: none -> 4.58 us  [the longest x1 2.8 us: per_device_one_head(): w_far_b = w_across_next + w_passed_next]
    all_to_all x2, waiting for transfers between devices: 17.8 us -> 13.7 us  [columns(): lax.all_to_all(jnp.concatenate(shaped, -1).transpose(1, 0, 2), 'ctx', 0,...]
    optimization_barrier x0 -> x3, local copies, waits for them, and re-layouts: none -> 4.02 us  [per_device_one_head(): barrier((near, across, x0, y0, w_value, w_key, w_query))]
  transfers between devices with their start and end apart: 33 -> 39, of which waited for: 20 -> 19; matrix products, arithmetic and copies ran while one was open for 9% -> 17% of each run, Pallas kernels for 11% -> 10%
where the time goes in v2:
time: 357 us; the launch traced here: 350 us
  waiting for transfers between devices  165 us (46%)
  starting transfers between devices  69.7 us (20%)
  Pallas kernels  43.7 us (12%)
  local copies, waits for them, and re-layouts  39.7 us (11%)
  other arithmetic  31.7 us (9%)
    ppermute x29, waiting for transfers between devices, swapped(): return lax.ppermute(value, axis, [(i, i ^ mask) for i in range(count)])  93.1 us
    ppermute x1, waiting for transfers between devices, per_device_one_head(): across_next = lax.ppermute(near, 'ctx', middle)  48.9 us
    ppermute x29, starting transfers between devices, swapped(): return lax.ppermute(value, axis, [(i, i ^ mask) for i in range(count)])  29 us
    broadcast_in_dim x28, local copies, waits for them, and re-layouts, key_taps_of(): out = out + jnp.where(tap == c, weights[:, c][None, :, None], 0.0)  22.7 us
    pallas_call x1, Pallas kernels, project(): pl.pallas_call(functools.partial(project_kernel, rows), out_shape=(out, o...  15.7 us
    all_to_all x2, waiting for transfers between devices, columns(): lax.all_to_all(jnp.concatenate(shaped, -1).transpose(1, 0, 2), 'ctx', 0,...  13.7 us
    ppermute x1, starting transfers between devices, per_device_one_head(): w_passed_next = lax.ppermute(w_across_next, 'ctx', outward)  13.6 us
    pallas_call x1, Pallas kernels, attend_head(): pl.pallas_call(attend_kernel, grid=(count,), out_shape=(out, out), in_spe...  12.5 us
  transfers between devices with their start and end apart: 39, of which 19 were waited for; matrix products, arithmetic and copies ran while one was open for 17% of the time, Pallas kernels for 10%

profile of v2, /device:TPU:17, one launch (start us, length us, event | category | flops | bytes accessed | tf_op | source)
XLA Modules:
  0.0 350.3 jit_solution(1996189098085108876)
XLA Ops:
  2.4 1.4 collective-permute-start
  3.8 1.9 collective-permute-start.1
  5.7 1.3 collective-permute-start.2
  6.9 1.2 collective-permute-start.3
  8.2 10.3 %collective-permute-done.2.refs_4_ = bf16[256,1024]{1,0:T(8,128)(2,1)S(1)} collective-permute-done((bf16[256,1024]{1,0:T(8,128)(2,1)}, bf16[256,1024]{1,0:T(8,128)(2,1)S(1)}, u32[]{:S(2)}, u32[]{:S(2)}) %collective-permute-start.2) | collective-permute-done | bytes 524320 | tf_op jit(solution)/shard_map/ppermute | solution.py:554
  19.5 1.9 copy.10
  21.4 1.3 copy.11
  22.7 4.2 %all-to-all-start = ((bf16[4,512,256]{2,1,0:T(8,128)(2,1)}), bf16[4,512,256]{2,1,0:T(8,128)(2,1)}, u32[]{:S(2)}, u32[]{:S(2)}) async-start(bf16[4,512,256]{2,1,0:T(8,128)(2,1)} %bitcast.10), calls=%async_computation | async-start | bytes 2097152 | tf_op jit(solution)/shard_map/all_to_all | solution.py:567
  31.2 1.6 copy.24
  34.4 1.5 maximum_bitcast_fusion
  36.0 13.7 %all-to-all-done.refs_14_ = bf16[4,512,256]{2,1,0:T(8,128)(2,1)} async-done(((bf16[4,512,256]{2,1,0:T(8,128)(2,1)}), bf16[4,512,256]{2,1,0:T(8,128)(2,1)}, u32[]{:S(2)}, u32[]{:S(2)}) %all-to-all-start) | async-done | bytes 1048608 | tf_op jit(solution)/shard_map/all_to_all | solution.py:567
  49.7 7.5 %all-to-all-start.1 = ((bf16[4,512,512]{2,1,0:T(8,128)(2,1)}), bf16[4,512,512]{2,1,0:T(8,128)(2,1)}, u32[]{:S(2)}, u32[]{:S(2)}) async-start(bf16[4,512,512]{2,1,0:T(8,128)(2,1)} %maximum_bitcast_fusion), calls=%async_computation.1 | async-start | bytes 4194304 | tf_op jit(solution)/shard_map/all_to_all | solution.py:567
  58.0 1.2 collective-permute-start.7
  59.9 2.2 collective-permute-start.4
  62.1 1.6 collective-permute-start.5
  65.6 48.9 %collective-permute-done.4 = bf16[272,1024]{1,0:T(8,128)(2,1)S(1)} collective-permute-done((bf16[272,1024]{1,0:T(8,128)(2,1)S(1)}, bf16[272,1024]{1,0:T(8,128)(2,1)S(1)}, u32[]{:S(2)}, u32[]{:S(2)}) %collective-permute-start.4) | collective-permute-done | bytes 557088 | tf_op jit(solution)/shard_map/ppermute | solution.py:597
  115.3 1.5 add.327.refs_2_
  117.0 1.3 pad_maximum_fusion.2
  123.8 1.5 broadcast_in_dim.555
  125.4 1.2 copy.16
  126.6 1.5 broadcast_in_dim.549
  128.1 1.9 copy.15
  130.0 1.5 broadcast_in_dim.543
  131.5 1.9 copy.14
  133.3 1.5 broadcast_in_dim.537
  134.8 1.9 copy.13
  136.7 1.5 broadcast_in_dim.530
  138.2 1.9 copy.12
  140.1 3.3 add_convert_fusion.1.even_ref
  143.4 1.6 collective-permute-start.8
  145.1 2.7 add_convert_fusion.3.odd_ref
  147.8 3.1 add_convert_fusion.2.key_ref
  150.9 3.9 %collective-permute-done.8 = bf16[272,1024]{1,0:T(8,128)(2,1)S(1)} collective-permute-done((bf16[272,1024]{1,0:T(8,128)(2,1)}, bf16[272,1024]{1,0:T(8,128)(2,1)S(1)}, u32[]{:S(2)}, u32[]{:S(2)}) %collective-permute-start.8) | collective-permute-done | bytes 557088 | tf_op jit(solution)/shard_map/ppermute | solution.py:602
  155.7 3.0 collective-permute-start.13
  161.6 18.0 %collective-permute-done.11.refs_7_ = bf16[384,1024]{1,0:T(8,128)(2,1)S(1)} collective-permute-done((bf16[384,1024]{1,0:T(8,128)(2,1)S(1)}, bf16[384,1024]{1,0:T(8,128)(2,1)S(1)}, u32[]{:S(2)}, u32[]{:S(2)}) %collective-permute-start.11) | collective-permute-done | bytes 786464 | tf_op jit(solution)/shard_map/ppermute | solution.py:554
  182.3 2.1 collective-permute-start.17
  184.4 3.4 collective-permute-start.18
  191.7 5.1 %collective-permute-done.14.refs_8_ = bf16[128,1024]{1,0:T(8,128)(2,1)S(1)} collective-permute-done((bf16[128,1024]{1,0:T(8,128)(2,1)S(1)}, bf16[128,1024]{1,0:T(8,128)(2,1)S(1)}, u32[]{:S(2)}, u32[]{:S(2)}) %collective-permute-start.14) | collective-permute-done | bytes 262176 | tf_op jit(solution)/shard_map/ppermute | solution.py:554
  196.9 1.6 collective-permute-done.15.refs_13_
  198.5 9.4 %collective-permute-done.17.refs_2_ = bf16[1024,512]{1,0:T(8,128)(2,1)} collective-permute-done((bf16[1024,512]{1,0:T(8,128)(2,1)S(1)}, bf16[1024,512]{1,0:T(8,128)(2,1)}, u32[]{:S(2)}, u32[]{:S(2)}) %collective-permute-start.17) | collective-permute-done | bytes 1048608 | tf_op jit(solution)/shard_map/ppermute | solution.py:554
  207.9 2.9 collective-permute-done.18
  210.8 3.3 collective-permute-start.19
  214.2 1.4 collective-permute-start.20
  215.5 1.9 fusion.3
  219.4 15.7 %shard_map.91 = (bf16[4,256,256]{2,1,0:T(8,128)(2,1)}, bf16[4,256,256]{2,1,0:T(8,128)(2,1)}, bf16[4,256,256]{2,1,0:T(8,128)(2,1)}) custom-call(s32[9]{0:T(128)} %stack.55.place, bf16[256,1024]{1,0:T(8,128)(2,1)} %refs_0_.1, bf16[272,1024]{1,0:T(8,128)(2,1)} %copy-done.4, bf16[272,1024]{1,0:T(8,128)(2,1)} %copy-done.2, bf16[272,1024]{1,0:T(8,128)(2,1)} %copy-done.3, ...), custom_call_target="tpu_custom_call" | custom-call | flops 6442450944 | bytes 16777216 | tf_op jit(solution)/shard_map/pallas_call | solution.py:263
  235.1 1.4 collective-permute-done.19
  237.0 2.1 collective-permute-start.22
  239.1 2.1 collective-permute-start.21
  241.2 1.3 collective-permute-start.25
  243.0 13.6 %collective-permute-start.27 = (bf16[1024,512]{1,0:T(8,128)(2,1)}, bf16[1024,512]{1,0:T(8,128)(2,1)}, u32[]{:S(2)}, u32[]{:S(2)}) collective-permute-start(bf16[1024,512]{1,0:T(8,128)(2,1)} %collective-permute-done.19), channel_id=1, source_target_pairs={{8,0},{12,4},{16,24},{20,28},{9,1},{13,5},{17,25},{21,29},{10,2},{... | collective-permute-start | bytes 3145736 | tf_op jit(solution)/shard_map/ppermute | solution.py:647
  256.6 7.6 %shard_map.92 = (bf16[2048,768]{1,0:T(8,128)(2,1)}, bf16[768,2048]{1,0:T(8,128)(2,1)}, f32[8,256,384]{2,1,0:T(8,128)}) custom-call(s32[9]{0:T(128)} %stack.55.place, bf16[4,256,256]{2,1,0:T(8,128)(2,1)} %get-tuple-element.86.mine, bf16[4,256,256]{2,1,0:T(8,128)(2,1)} %copy-done.30, bf16[256,768]{1,0:T(8,128)(2,1)} %add_convert_fusion.2.key_ref, ...), custom_call_target="tpu_custom_call" | custom-call | flops 2147483648 | bytes 12582912 | tf_op jit(solution)/shard_map/pallas_call | solution.py:348
  265.5 1.3 collective-permute-done.24.vd
  266.8 12.5 %shard_map.93 = (bf16[4,256,512]{2,1,0:T(8,128)(2,1)}, bf16[4,256,512]{2,1,0:T(8,128)(2,1)}) custom-call(s32[9]{0:T(128)} %stack.55.place, f32[4]{0:T(128)} %dynamic-slice_bitcast_fusion.1.mix, bf16[2048,768]{1,0:T(8,128)(2,1)} %get-tuple-element.92.q_ref, bf16[768,2048]{1,0:T(8,128)(2,1)} %get-tuple-element.93.k_ref, ...), custom_call_target="tpu_custom_call" | custom-call | flops 5368709120 | bytes 16777216 | tf_op jit(solution)/shard_map/pallas_call | solution.py:476
  279.8 1.8 add.375.refs_4_
  282.1 2.8 add.376.refs_6_
  285.2 1.9 convert_add_fusion
  289.3 1.4 collective-permute-start.31
  291.5 6.9 %collective-permute-done.29.r1 = bf16[256,512]{1,0:T(8,128)(2,1)S(1)} collective-permute-done((bf16[256,512]{1,0:T(8,128)(2,1)}, bf16[256,512]{1,0:T(8,128)(2,1)S(1)}, u32[]{:S(2)}, u32[]{:S(2)}) %collective-permute-start.29) | collective-permute-done | bytes 262176 | tf_op jit(solution)/shard_map/ppermute | solution.py:554
  298.4 3.0 collective-permute-done.30.r2
  301.5 12.4 %collective-permute-done.31.r3 = bf16[256,512]{1,0:T(8,128)(2,1)} collective-permute-done((bf16[256,512]{1,0:T(8,128)(2,1)}, bf16[256,512]{1,0:T(8,128)(2,1)}, u32[]{:S(2)}, u32[]{:S(2)}) %collective-permute-start.31) | collective-permute-done | bytes 262176 | tf_op jit(solution)/shard_map/ppermute | solution.py:554
  313.8 7.9 %shard_map.94 = (bf16[256,1024]{1,0:T(8,128)(2,1)}, bf16[256,1024]{1,0:T(8,128)(2,1)}, bf16[256,1024]{1,0:T(8,128)(2,1)}, bf16[256,1024]{1,0:T(8,128)(2,1)}) custom-call(s32[9]{0:T(128)} %stack.55.place, f32[256,512]{1,0:T(8,128)} %dynamic-slice_bitcast_fusion.own, bf16[256,512]{1,0:T(8,128)(2,1)} %copy-done.17, ...), custom_call_target="tpu_custom_call" | custom-call | flops 2147483648 | bytes 11534336 | tf_op jit(solution)/shard_map/pallas_call | solution.py:535
  324.5 10.6 %collective-permute-done.36 = bf16[256,1024]{1,0:T(8,128)(2,1)S(1)} collective-permute-done((bf16[256,1024]{1,0:T(8,128)(2,1)}, bf16[256,1024]{1,0:T(8,128)(2,1)S(1)}, u32[]{:S(2)}, u32[]{:S(2)}) %collective-permute-start.36) | collective-permute-done | bytes 524320 | tf_op jit(solution)/shard_map/ppermute | solution.py:554
  335.1 12.8 %collective-permute-done.35 = bf16[256,1024]{1,0:T(8,128)(2,1)S(1)} collective-permute-done((bf16[256,1024]{1,0:T(8,128)(2,1)}, bf16[256,1024]{1,0:T(8,128)(2,1)S(1)}, u32[]{:S(2)}, u32[]{:S(2)}) %collective-permute-start.35) | collective-permute-done | bytes 524320 | tf_op jit(solution)/shard_map/ppermute | solution.py:554
  347.9 2.2 add_convert_fusion
  (172 shorter events, 40.4 us)
Async XLA Ops:
  0.0 264.9 %copy-start = (f32[8,4]{0,1:T(4,128)S(1)}, f32[8,4]{0,1:T(4,128)}, u32[]{:S(2)}) copy-start(f32[8,4]{0,1:T(4,128)} %param.15) | copy-start | bytes 388
  2.4 17.1 %collective-permute-start = (bf16[272,1024]{1,0:T(8,128)(2,1)S(1)}, bf16[272,1024]{1,0:T(8,128)(2,1)S(1)}, u32[]{:S(2)}, u32[]{:S(2)}) collective-permute-start(bf16[272,1024]{1,0:T(8,128)(2,1)S(1)} %pad_maximum_fusion.6), channel_id=1, source_target_pairs={{0,8},{4,12},{8,0},{12,4},{16,24},{20,28},{24,16},{28,20},{1,9},{5... | collective-permute-start | bytes 1671176 | tf_op jit(solution)/shard_map/ppermute | solution.py:554
  3.8 15.7 %collective-permute-start.1 = (bf16[272,1024]{1,0:T(8,128)(2,1)S(1)}, bf16[272,1024]{1,0:T(8,128)(2,1)}, u32[]{:S(2)}, u32[]{:S(2)}) collective-permute-start(bf16[272,1024]{1,0:T(8,128)(2,1)S(1)} %pad_maximum_fusion.6), channel_id=1, source_target_pairs={{8,16},{12,20},{16,8},{20,12},{9,17},{13,21},{17,9},{21,13},{10,18... | collective-permute-start | bytes 1671176 | tf_op jit(solution)/shard_map/ppermute | solution.py:591
  5.7 12.9 %collective-permute-start.2 = (bf16[256,1024]{1,0:T(8,128)(2,1)}, bf16[256,1024]{1,0:T(8,128)(2,1)S(1)}, u32[]{:S(2)}, u32[]{:S(2)}) collective-permute-start(bf16[256,1024]{1,0:T(8,128)(2,1)} %refs_0_.1), channel_id=1, source_target_pairs={{0,1},{1,0},{2,3},{3,2},{4,5},{5,4},{6,7},{7,6},{8,9},{9,8},{10,11... | collective-permute-start | bytes 1572872 | tf_op jit(solution)/shard_map/ppermute | solution.py:554
  6.9 12.5 %collective-permute-start.3 = (bf16[256,1024]{1,0:T(8,128)(2,1)}, bf16[256,1024]{1,0:T(8,128)(2,1)S(1)}, u32[]{:S(2)}, u32[]{:S(2)}) collective-permute-start(bf16[256,1024]{1,0:T(8,128)(2,1)} %refs_0_.1), channel_id=1, source_target_pairs={{0,2},{1,3},{2,0},{3,1},{4,6},{5,7},{6,4},{7,5},{8,10},{9,11},{10,... | collective-permute-start | bytes 1572872 | tf_op jit(solution)/shard_map/ppermute | solution.py:554
  18.5 12.7 %copy-start.11 = (bf16[256,1024]{1,0:T(8,128)(2,1)}, bf16[256,1024]{1,0:T(8,128)(2,1)S(1)}, u32[]{:S(2)}) copy-start(bf16[256,1024]{1,0:T(8,128)(2,1)S(1)} %collective-permute-done.2.refs_4_) | copy-start | bytes 1572868
  19.4 11.8 %copy-start.12 = (bf16[256,1024]{1,0:T(8,128)(2,1)}, bf16[256,1024]{1,0:T(8,128)(2,1)S(1)}, u32[]{:S(2)}) copy-start(bf16[256,1024]{1,0:T(8,128)(2,1)S(1)} %collective-permute-done.3.refs_9_) | copy-start | bytes 1572868
  19.4 11.8 %copy-start.4 = (bf16[272,1024]{1,0:T(8,128)(2,1)}, bf16[272,1024]{1,0:T(8,128)(2,1)S(1)}, u32[]{:S(2)}) copy-start(bf16[272,1024]{1,0:T(8,128)(2,1)S(1)} %collective-permute-done.refs_1_) | copy-start | bytes 1671172
  22.7 27.0 %all-to-all-start = ((bf16[4,512,256]{2,1,0:T(8,128)(2,1)}), bf16[4,512,256]{2,1,0:T(8,128)(2,1)}, u32[]{:S(2)}, u32[]{:S(2)}) async-start(bf16[4,512,256]{2,1,0:T(8,128)(2,1)} %bitcast.10), calls=%async_computation | async-start | bytes 2097152 | tf_op jit(solution)/shard_map/all_to_all | solution.py:567
  36.0 21.2 %slice-start = ((bf16[272,1024]{1,0:T(8,128)(2,1)}), bf16[256,1024]{1,0:T(8,128)(2,1)S(1)}, s32[]{:S(2)}) async-start(bf16[272,1024]{1,0:T(8,128)(2,1)} %copy-done.4), calls=%async_computation.2 | async-start | bytes 1048576 | tf_op jit(solution)/shard_map/slice | solution.py:583
  36.0 21.2 %slice-start.1 = ((bf16[256,1024]{1,0:T(8,128)(2,1)}), bf16[128,1024]{1,0:T(8,128)(2,1)S(1)}, s32[]{:S(2)}) async-start(bf16[256,1024]{1,0:T(8,128)(2,1)} %copy-done.11), calls=%async_computation.3 | async-start | bytes 524288 | tf_op jit(solution)/shard_map/slice | solution.py:584
  36.0 21.2 %slice-start.2 = ((bf16[256,1024]{1,0:T(8,128)(2,1)}), bf16[128,1024]{1,0:T(8,128)(2,1)S(1)}, s32[]{:S(2)}) async-start(bf16[256,1024]{1,0:T(8,128)(2,1)} %copy-done.12), calls=%async_computation.4 | async-start | bytes 524288 | tf_op jit(solution)/shard_map/slice | solution.py:583
  49.7 131.7 %all-to-all-start.1 = ((bf16[4,512,512]{2,1,0:T(8,128)(2,1)}), bf16[4,512,512]{2,1,0:T(8,128)(2,1)}, u32[]{:S(2)}, u32[]{:S(2)}) async-start(bf16[4,512,512]{2,1,0:T(8,128)(2,1)} %maximum_bitcast_fusion), calls=%async_computation.1 | async-start | bytes 4194304 | tf_op jit(solution)/shard_map/all_to_all | solution.py:567
  57.2 7.5 %copy-start.29 = (s32[256]{0:T(256)S(1)}, s32[256]{0:T(256)}, u32[]{:S(2)}) copy-start(s32[256]{0:T(256)} %iota_add_fusion) | copy-start | bytes 3076
  57.5 57.0 %collective-permute-start.6 = (bf16[384,1024]{1,0:T(8,128)(2,1)S(1)}, bf16[384,1024]{1,0:T(8,128)(2,1)S(1)}, u32[]{:S(2)}, u32[]{:S(2)}) collective-permute-start(bf16[384,1024]{1,0:T(8,128)(2,1)S(1)} %get-tuple-element.128), channel_id=1, source_target_pairs={{0,1},{1,0},{2,3},{3,2},{4,5},{5,4},{6,7},{7,6},{8,9},{9,8},{10,11... | collective-permute-start | bytes 2359304 | tf_op jit(solution)/shard_map/ppermute | solution.py:554
  58.0 56.5 %collective-permute-start.7 = (bf16[384,1024]{1,0:T(8,128)(2,1)S(1)}, bf16[384,1024]{1,0:T(8,128)(2,1)S(1)}, u32[]{:S(2)}, u32[]{:S(2)}) collective-permute-start(bf16[384,1024]{1,0:T(8,128)(2,1)S(1)} %get-tuple-element.127), channel_id=1, source_target_pairs={{0,2},{1,3},{2,0},{3,1},{4,6},{5,7},{6,4},{7,5},{8,10},{9,11},{10,... | collective-permute-start | bytes 2359304 | tf_op jit(solution)/shard_map/ppermute | solution.py:554
  59.9 54.6 %collective-permute-start.4 = (bf16[272,1024]{1,0:T(8,128)(2,1)S(1)}, bf16[272,1024]{1,0:T(8,128)(2,1)S(1)}, u32[]{:S(2)}, u32[]{:S(2)}) collective-permute-start(bf16[272,1024]{1,0:T(8,128)(2,1)S(1)} %copy-done.5), channel_id=1, source_target_pairs={{8,16},{12,20},{16,8},{20,12},{9,17},{13,21},{17,9},{21,13},{10,18... | collective-permute-start | bytes 1671176 | tf_op jit(solution)/shard_map/ppermute | solution.py:597
  62.1 52.4 %collective-permute-start.5 = (bf16[272,1024]{1,0:T(8,128)(2,1)}, bf16[272,1024]{1,0:T(8,128)(2,1)S(1)}, u32[]{:S(2)}, u32[]{:S(2)}) collective-permute-start(bf16[272,1024]{1,0:T(8,128)(2,1)} %collective-permute-done.1), channel_id=1, source_target_pairs={{8,0},{12,4},{16,24},{20,28},{9,1},{13,5},{17,25},{21,29},{10,2},{... | collective-permute-start | bytes 1671176 | tf_op jit(solution)/shard_map/ppermute | solution.py:598
  116.9 71.6 %copy-start.2 = (bf16[272,1024]{1,0:T(8,128)(2,1)}, bf16[272,1024]{1,0:T(8,128)(2,1)S(1)}, u32[]{:S(2)}) copy-start(bf16[272,1024]{1,0:T(8,128)(2,1)S(1)} %add.327.refs_2_) | copy-start | bytes 1671172
  116.9 3.1 copy-start.24
  118.3 36.6 %collective-permute-start.9 = (bf16[384,1024]{1,0:T(8,128)(2,1)}, bf16[384,1024]{1,0:T(8,128)(2,1)S(1)}, u32[]{:S(2)}, u32[]{:S(2)}) collective-permute-start(bf16[384,1024]{1,0:T(8,128)(2,1)} %get-tuple-element.126), channel_id=1, source_target_pairs={{0,1},{1,0},{2,3},{3,2},{4,5},{5,4},{6,7},{7,6},{8,9},{9,8},{10,11... | collective-permute-start | bytes 2359304 | tf_op jit(solution)/shard_map/ppermute | solution.py:554
  118.8 36.1 %collective-permute-start.10 = (bf16[384,1024]{1,0:T(8,128)(2,1)}, bf16[384,1024]{1,0:T(8,128)(2,1)}, u32[]{:S(2)}, u32[]{:S(2)}) collective-permute-start(bf16[384,1024]{1,0:T(8,128)(2,1)} %get-tuple-element.125), channel_id=1, source_target_pairs={{0,2},{1,3},{2,0},{3,1},{4,6},{5,7},{6,4},{7,5},{8,10},{9,11},{10,... | collective-permute-start | bytes 2359304 | tf_op jit(solution)/shard_map/ppermute | solution.py:554
  122.3 17.8 %copy-start.18 = (pred[128,256]{1,0:T(8,128)(4,1)S(1)}, pred[128,256]{1,0:T(8,128)(4,1)}, u32[]{:S(2)}) copy-start(pred[128,256]{1,0:T(8,128)(4,1)} %get-tuple-element.138) | copy-start | bytes 98308
  122.3 17.7 %copy-start.19 = (pred[128,256]{1,0:T(8,128)(4,1)S(1)}, pred[128,256]{1,0:T(8,128)(4,1)}, u32[]{:S(2)}) copy-start(pred[128,256]{1,0:T(8,128)(4,1)} %get-tuple-element.139) | copy-start | bytes 98308
  140.1 18.6 %copy-start.16 = (bf16[272,1024]{1,0:T(8,128)(2,1)S(1)}, bf16[272,1024]{1,0:T(8,128)(2,1)}, u32[]{:S(2)}) copy-start(bf16[272,1024]{1,0:T(8,128)(2,1)} %copy-done.15) | copy-start | bytes 1671172
  143.4 11.5 %collective-permute-start.8 = (bf16[272,1024]{1,0:T(8,128)(2,1)}, bf16[272,1024]{1,0:T(8,128)(2,1)S(1)}, u32[]{:S(2)}, u32[]{:S(2)}) collective-permute-start(bf16[272,1024]{1,0:T(8,128)(2,1)} %copy-done.15), channel_id=1, source_target_pairs={{8,0},{12,4},{16,24},{20,28},{9,1},{13,5},{17,25},{21,29},{10,2},{... | collective-permute-start | bytes 1671176 | tf_op jit(solution)/shard_map/ppermute | solution.py:602
  155.7 25.7 %collective-permute-start.13 = (bf16[4,512,256]{2,1,0:T(8,128)(2,1)}, bf16[4,512,256]{2,1,0:T(8,128)(2,1)}, u32[]{:S(2)}, u32[]{:S(2)}) collective-permute-start(bf16[4,512,256]{2,1,0:T(8,128)(2,1)} %all-to-all-done.refs_14_), channel_id=1, source_target_pairs={{0,4},{4,0},{8,12},{12,8},{16,20},{20,16},{24,28},{28,24},{1,5},{5... | collective-permute-start | bytes 3145736 | tf_op jit(solution)/shard_map/ppermute | solution.py:554
  158.9 32.8 %copy-start.3 = (bf16[272,1024]{1,0:T(8,128)(2,1)}, bf16[272,1024]{1,0:T(8,128)(2,1)S(1)}, u32[]{:S(2)}) copy-start(bf16[272,1024]{1,0:T(8,128)(2,1)S(1)} %add.365.refs_3_) | copy-start | bytes 1671172
  159.0 23.3 %copy-start.6 = (bf16[1024,512]{1,0:T(8,128)(2,1)S(1)}, bf16[1024,512]{1,0:T(8,128)(2,1)}, u32[]{:S(2)}) copy-start(bf16[1024,512]{1,0:T(8,128)(2,1)} %refs_0_.2) | copy-start | bytes 3145732
  159.0 29.5 %copy-start.26 = (bf16[256]{0:T(256)(128)(2,1)S(1)}, bf16[256]{0:T(256)(128)(2,1)}, u32[]{:S(2)}) copy-start(bf16[256]{0:T(256)(128)(2,1)} %copy-done.25) | copy-start | bytes 1540
  159.0 29.5 %copy-start.28 = (bf16[256]{0:T(256)(128)(2,1)S(1)}, bf16[256]{0:T(256)(128)(2,1)}, u32[]{:S(2)}) copy-start(bf16[256]{0:T(256)(128)(2,1)} %copy-done.27) | copy-start | bytes 1540
  160.3 19.2 %collective-permute-start.11 = (bf16[384,1024]{1,0:T(8,128)(2,1)S(1)}, bf16[384,1024]{1,0:T(8,128)(2,1)S(1)}, u32[]{:S(2)}, u32[]{:S(2)}) collective-permute-start(bf16[384,1024]{1,0:T(8,128)(2,1)S(1)} %get-tuple-element.124), channel_id=1, source_target_pairs={{0,1},{1,0},{2,3},{3,2},{4,5},{5,4},{6,7},{7,6},{8,9},{9,8},{10,11... | collective-permute-start | bytes 2359304 | tf_op jit(solution)/shard_map/ppermute | solution.py:554
  161.4 18.9 %collective-permute-start.12 = (bf16[384,1024]{1,0:T(8,128)(2,1)S(1)}, bf16[384,1024]{1,0:T(8,128)(2,1)S(1)}, u32[]{:S(2)}, u32[]{:S(2)}) collective-permute-start(bf16[384,1024]{1,0:T(8,128)(2,1)S(1)} %get-tuple-element.123), channel_id=1, source_target_pairs={{0,2},{1,3},{2,0},{3,1},{4,6},{5,7},{6,4},{7,5},{8,10},{9,11},{10,... | collective-permute-start | bytes 2359304 | tf_op jit(solution)/shard_map/ppermute | solution.py:554
  181.4 29.4 %collective-permute-start.16 = (bf16[4,512,512]{2,1,0:T(8,128)(2,1)}, bf16[4,512,512]{2,1,0:T(8,128)(2,1)}, u32[]{:S(2)}, u32[]{:S(2)}) collective-permute-start(bf16[4,512,512]{2,1,0:T(8,128)(2,1)} %all-to-all-done.1.refs_16_), channel_id=1, source_target_pairs={{0,4},{4,0},{8,12},{12,8},{16,20},{20,16},{24,28},{28,24},{1,5},{5... | collective-permute-start | bytes 6291464 | tf_op jit(solution)/shard_map/ppermute | solution.py:554
  182.3 25.6 %collective-permute-start.17 = (bf16[1024,512]{1,0:T(8,128)(2,1)S(1)}, bf16[1024,512]{1,0:T(8,128)(2,1)}, u32[]{:S(2)}, u32[]{:S(2)}) collective-permute-start(bf16[1024,512]{1,0:T(8,128)(2,1)S(1)} %copy-done.6), channel_id=1, source_target_pairs={{0,8},{4,12},{8,0},{12,4},{16,24},{20,28},{24,16},{28,20},{1,9},{5... | collective-permute-start | bytes 3145736 | tf_op jit(solution)/shard_map/ppermute | solution.py:554
  184.4 26.4 %collective-permute-start.18 = (bf16[1024,512]{1,0:T(8,128)(2,1)S(1)}, bf16[1024,512]{1,0:T(8,128)(2,1)}, u32[]{:S(2)}, u32[]{:S(2)}) collective-permute-start(bf16[1024,512]{1,0:T(8,128)(2,1)S(1)} %copy-done.6), channel_id=1, source_target_pairs={{8,16},{12,20},{16,8},{20,12},{9,17},{13,21},{17,9},{21,13},{10,18... | collective-permute-start | bytes 3145736 | tf_op jit(solution)/shard_map/ppermute | solution.py:616
  189.5 7.4 %collective-permute-start.14 = (bf16[128,1024]{1,0:T(8,128)(2,1)S(1)}, bf16[128,1024]{1,0:T(8,128)(2,1)S(1)}, u32[]{:S(2)}, u32[]{:S(2)}) collective-permute-start(bf16[128,1024]{1,0:T(8,128)(2,1)S(1)} %slice.133), channel_id=1, source_target_pairs={{0,1},{1,0},{2,3},{3,2},{4,5},{5,4},{6,7},{7,6},{8,9},{9,8},{10,11... | collective-permute-start | bytes 786440 | tf_op jit(solution)/shard_map/ppermute | solution.py:554
  191.4 7.1 %collective-permute-start.15 = (bf16[128,1024]{1,0:T(8,128)(2,1)S(1)}, bf16[128,1024]{1,0:T(8,128)(2,1)S(1)}, u32[]{:S(2)}, u32[]{:S(2)}) collective-permute-start(bf16[128,1024]{1,0:T(8,128)(2,1)S(1)} %slice.134), channel_id=1, source_target_pairs={{0,2},{1,3},{2,0},{3,1},{4,6},{5,7},{6,4},{7,5},{8,10},{9,11},{10,... | collective-permute-start | bytes 786440 | tf_op jit(solution)/shard_map/ppermute | solution.py:554
  196.9 22.6 %copy-start.31 = (bf16[128,1024]{1,0:T(8,128)(2,1)}, bf16[128,1024]{1,0:T(8,128)(2,1)S(1)}, u32[]{:S(2)}) copy-start(bf16[128,1024]{1,0:T(8,128)(2,1)S(1)} %collective-permute-done.14.refs_8_) | copy-start | bytes 786436
  198.5 20.9 %copy-start.32 = (bf16[128,1024]{1,0:T(8,128)(2,1)}, bf16[128,1024]{1,0:T(8,128)(2,1)S(1)}, u32[]{:S(2)}) copy-start(bf16[128,1024]{1,0:T(8,128)(2,1)S(1)} %collective-permute-done.15.refs_13_) | copy-start | bytes 786436
  210.8 25.7 %collective-permute-start.19 = (bf16[1024,512]{1,0:T(8,128)(2,1)}, bf16[1024,512]{1,0:T(8,128)(2,1)}, u32[]{:S(2)}, u32[]{:S(2)}) collective-permute-start(bf16[1024,512]{1,0:T(8,128)(2,1)} %collective-permute-done.17.refs_2_), channel_id=1, source_target_pairs={{8,16},{12,20},{16,8},{20,12},{9,17},{13,21},{17,9},{21,13},{10,18... | collective-permute-start | bytes 3145736 | tf_op jit(solution)/shard_map/ppermute | solution.py:618
  214.2 22.9 %collective-permute-start.20 = (bf16[1024,512]{1,0:T(8,128)(2,1)}, bf16[1024,512]{1,0:T(8,128)(2,1)S(1)}, u32[]{:S(2)}, u32[]{:S(2)}) collective-permute-start(bf16[1024,512]{1,0:T(8,128)(2,1)} %collective-permute-done.18), channel_id=1, source_target_pairs={{8,0},{12,4},{16,24},{20,28},{9,1},{13,5},{17,25},{21,29},{10,2},{... | collective-permute-start | bytes 3145736 | tf_op jit(solution)/shard_map/ppermute | solution.py:619
  237.0 6.0 %collective-permute-start.22 = (bf16[4,256,256]{2,1,0:T(8,128)(2,1)}, bf16[4,256,256]{2,1,0:T(8,128)(2,1)S(1)}, u32[]{:S(2)}, u32[]{:S(2)}) collective-permute-start(bf16[4,256,256]{2,1,0:T(8,128)(2,1)} %get-tuple-element.87), channel_id=1, source_target_pairs={{0,4},{4,0},{8,12},{12,8},{16,20},{20,16},{24,28},{28,24},{1,5},{5... | collective-permute-start | bytes 1572872 | tf_op jit(solution)/shard_map/ppermute | solution.py:554
  239.1 25.1 %collective-permute-start.21 = (bf16[4,256,256]{2,1,0:T(8,128)(2,1)}, bf16[4,256,256]{2,1,0:T(8,128)(2,1)}, u32[]{:S(2)}, u32[]{:S(2)}) collective-permute-start(bf16[4,256,256]{2,1,0:T(8,128)(2,1)} %get-tuple-element.85.va), channel_id=1, source_target_pairs={{0,8},{4,12},{8,0},{12,4},{16,24},{20,28},{24,16},{28,20},{1,9},{5... | collective-permute-start | bytes 1572872 | tf_op jit(solution)/shard_map/ppermute | solution.py:554
  241.2 38.1 %collective-permute-start.25 = (bf16[1024,512]{1,0:T(8,128)(2,1)S(1)}, bf16[1024,512]{1,0:T(8,128)(2,1)S(1)}, u32[]{:S(2)}, u32[]{:S(2)}) collective-permute-start(bf16[1024,512]{1,0:T(8,128)(2,1)S(1)} %copy-done.6), channel_id=1, source_target_pairs={{0,4},{4,0},{8,12},{12,8},{16,20},{20,16},{24,28},{28,24},{1,5},{5... | collective-permute-start | bytes 3145736 | tf_op jit(solution)/shard_map/ppermute | solution.py:554
  242.5 36.9 %collective-permute-start.26 = (bf16[1024,512]{1,0:T(8,128)(2,1)}, bf16[1024,512]{1,0:T(8,128)(2,1)S(1)}, u32[]{:S(2)}, u32[]{:S(2)}) collective-permute-start(bf16[1024,512]{1,0:T(8,128)(2,1)} %collective-permute-done.17.refs_2_), channel_id=1, source_target_pairs={{0,4},{4,0},{8,12},{12,8},{16,20},{20,16},{24,28},{28,24},{1,5},{5... | collective-permute-start | bytes 3145736 | tf_op jit(solution)/shard_map/ppermute | solution.py:554
  242.5 23.0 %collective-permute-start.23 = (bf16[4,256,256]{2,1,0:T(8,128)(2,1)}, bf16[4,256,256]{2,1,0:T(8,128)(2,1)}, u32[]{:S(2)}, u32[]{:S(2)}) collective-permute-start(bf16[4,256,256]{2,1,0:T(8,128)(2,1)} %get-tuple-element.85.va), channel_id=1, source_target_pairs={{0,4},{4,0},{8,12},{12,8},{16,20},{20,16},{24,28},{28,24},{1,5},{5... | collective-permute-start | bytes 1572872 | tf_op jit(solution)/shard_map/ppermute | solution.py:554
  243.0 13.6 %copy-start.30 = (bf16[4,256,256]{2,1,0:T(8,128)(2,1)}, bf16[4,256,256]{2,1,0:T(8,128)(2,1)S(1)}, u32[]{:S(2)}) copy-start(bf16[4,256,256]{2,1,0:T(8,128)(2,1)S(1)} %collective-permute-done.22.other) | copy-start | bytes 1572868
  243.0 36.4 %collective-permute-start.27 = (bf16[1024,512]{1,0:T(8,128)(2,1)}, bf16[1024,512]{1,0:T(8,128)(2,1)}, u32[]{:S(2)}, u32[]{:S(2)}) collective-permute-start(bf16[1024,512]{1,0:T(8,128)(2,1)} %collective-permute-done.19), channel_id=1, source_target_pairs={{8,0},{12,4},{16,24},{20,28},{9,1},{13,5},{17,25},{21,29},{10,2},{... | collective-permute-start | bytes 3145736 | tf_op jit(solution)/shard_map/ppermute | solution.py:647
  264.3 2.5 collective-permute-start.24
  266.8 13.0 %copy-start.10 = (bf16[1024,512]{1,0:T(8,128)(2,1)S(1)}, bf16[1024,512]{1,0:T(8,128)(2,1)}, u32[]{:S(2)}) copy-start(bf16[1024,512]{1,0:T(8,128)(2,1)} %copy-done.9) | copy-start | bytes 3145732
  279.4 5.5 %copy-start.7 = (bf16[1024,512]{1,0:T(8,128)(2,1)}, bf16[1024,512]{1,0:T(8,128)(2,1)S(1)}, u32[]{:S(2)}) copy-start(bf16[1024,512]{1,0:T(8,128)(2,1)S(1)} %collective-permute-done.25.refs_1_) | copy-start | bytes 3145732
  279.4 5.5 %copy-start.8 = (bf16[1024,512]{1,0:T(8,128)(2,1)}, bf16[1024,512]{1,0:T(8,128)(2,1)S(1)}, u32[]{:S(2)}) copy-start(bf16[1024,512]{1,0:T(8,128)(2,1)S(1)} %collective-permute-done.26.refs_3_) | copy-start | bytes 3145732
  279.4 5.8 %collective-permute-start.28 = (bf16[4,256,512]{2,1,0:T(8,128)(2,1)}, bf16[4,256,512]{2,1,0:T(8,128)(2,1)}, u32[]{:S(2)}, u32[]{:S(2)}) collective-permute-start(bf16[4,256,512]{2,1,0:T(8,128)(2,1)} %get-tuple-element.100), channel_id=1, source_target_pairs={{0,4},{4,0},{8,12},{12,8},{16,20},{20,16},{24,28},{28,24},{1,5},{5... | collective-permute-start | bytes 3145736 | tf_op jit(solution)/shard_map/ppermute | solution.py:554
  281.6 5.5 %copy-start.1 = (bf16[1024,512]{1,0:T(8,128)(2,1)}, bf16[1024,512]{1,0:T(8,128)(2,1)S(1)}, u32[]{:S(2)}) copy-start(bf16[1024,512]{1,0:T(8,128)(2,1)S(1)} %add.375.refs_4_) | copy-start | bytes 3145732
  281.6 9.9 %collective-permute-start.32 = (bf16[1024,512]{1,0:T(8,128)(2,1)S(1)}, bf16[1024,512]{1,0:T(8,128)(2,1)}, u32[]{:S(2)}, u32[]{:S(2)}) collective-permute-start(bf16[1024,512]{1,0:T(8,128)(2,1)S(1)} %add.375.refs_4_), channel_id=1, source_target_pairs={{0,4},{4,0},{8,12},{12,8},{16,20},{20,16},{24,28},{28,24},{1,5},{5... | collective-permute-start | bytes 3145736 | tf_op jit(solution)/shard_map/ppermute | solution.py:554
  284.9 6.6 %collective-permute-start.33 = (bf16[1024,512]{1,0:T(8,128)(2,1)}, bf16[1024,512]{1,0:T(8,128)(2,1)}, u32[]{:S(2)}, u32[]{:S(2)}) collective-permute-start(bf16[1024,512]{1,0:T(8,128)(2,1)} %add.376.refs_6_), channel_id=1, source_target_pairs={{0,4},{4,0},{8,12},{12,8},{16,20},{20,16},{24,28},{28,24},{1,5},{5... | collective-permute-start | bytes 3145736 | tf_op jit(solution)/shard_map/ppermute | solution.py:554
  288.0 10.4 %collective-permute-start.29 = (bf16[256,512]{1,0:T(8,128)(2,1)}, bf16[256,512]{1,0:T(8,128)(2,1)S(1)}, u32[]{:S(2)}, u32[]{:S(2)}) collective-permute-start(bf16[256,512]{1,0:T(8,128)(2,1)} %get-tuple-element.122), channel_id=1, source_target_pairs={{0,8},{4,12},{8,0},{12,4},{16,24},{20,28},{24,16},{28,20},{1,9},{5... | collective-permute-start | bytes 786440 | tf_op jit(solution)/shard_map/ppermute | solution.py:554
  288.0 13.4 %collective-permute-start.30 = (bf16[256,512]{1,0:T(8,128)(2,1)}, bf16[256,512]{1,0:T(8,128)(2,1)}, u32[]{:S(2)}, u32[]{:S(2)}) collective-permute-start(bf16[256,512]{1,0:T(8,128)(2,1)} %get-tuple-element.121), channel_id=1, source_target_pairs={{0,16},{4,20},{8,24},{12,28},{16,0},{20,4},{24,8},{28,12},{1,17},{... | collective-permute-start | bytes 786440 | tf_op jit(solution)/shard_map/ppermute | solution.py:554
  289.3 24.6 %collective-permute-start.31 = (bf16[256,512]{1,0:T(8,128)(2,1)}, bf16[256,512]{1,0:T(8,128)(2,1)}, u32[]{:S(2)}, u32[]{:S(2)}) collective-permute-start(bf16[256,512]{1,0:T(8,128)(2,1)} %get-tuple-element.120), channel_id=1, source_target_pairs={{0,24},{4,28},{8,16},{12,20},{16,8},{20,12},{24,0},{28,4},{1,25},{... | collective-permute-start | bytes 786440 | tf_op jit(solution)/shard_map/ppermute | solution.py:554
  298.4 15.4 %copy-start.17 = (bf16[256,512]{1,0:T(8,128)(2,1)}, bf16[256,512]{1,0:T(8,128)(2,1)S(1)}, u32[]{:S(2)}) copy-start(bf16[256,512]{1,0:T(8,128)(2,1)S(1)} %collective-permute-done.29.r1) | copy-start | bytes 786436
  321.8 13.4 %collective-permute-start.36 = (bf16[256,1024]{1,0:T(8,128)(2,1)}, bf16[256,1024]{1,0:T(8,128)(2,1)S(1)}, u32[]{:S(2)}, u32[]{:S(2)}) collective-permute-start(bf16[256,1024]{1,0:T(8,128)(2,1)} %get-tuple-element.108), channel_id=1, source_target_pairs={{0,3},{1,2},{2,1},{3,0},{4,7},{5,6},{6,5},{7,4},{8,11},{9,10},{10,... | collective-permute-start | bytes 1572872 | tf_op jit(solution)/shard_map/ppermute | solution.py:554
  322.7 25.2 %collective-permute-start.35 = (bf16[256,1024]{1,0:T(8,128)(2,1)}, bf16[256,1024]{1,0:T(8,128)(2,1)S(1)}, u32[]{:S(2)}, u32[]{:S(2)}) collective-permute-start(bf16[256,1024]{1,0:T(8,128)(2,1)} %get-tuple-element.107), channel_id=1, source_target_pairs={{0,2},{1,3},{2,0},{3,1},{4,6},{5,7},{6,4},{7,5},{8,10},{9,11},{10,... | collective-permute-start | bytes 1572872 | tf_op jit(solution)/shard_map/ppermute | solution.py:554
  323.9 24.0 %collective-permute-start.34 = (bf16[256,1024]{1,0:T(8,128)(2,1)}, bf16[256,1024]{1,0:T(8,128)(2,1)S(1)}, u32[]{:S(2)}, u32[]{:S(2)}) collective-permute-start(bf16[256,1024]{1,0:T(8,128)(2,1)} %get-tuple-element.106), channel_id=1, source_target_pairs={{0,1},{1,0},{2,3},{3,2},{4,5},{5,4},{6,7},{7,6},{8,9},{9,8},{10,11... | collective-permute-start | bytes 1572872 | tf_op jit(solution)/shard_map/ppermute | solution.py:554
  (12 other events, 17.1 us)

commit v3 on v1

--- a/solution.py
+++ b/solution.py
@@ -1,3 +1,4 @@
+import functools
 import math
 
 import jax
@@ -191,49 +192,53 @@
     return pl.BlockSpec(memory_space=memory_space)
 
 
-def project_kernel(place, *refs):
-    a_own, a_x, a_y = refs[:4], refs[4:9], refs[9:14]
-    weights = refs[14:18]
-    cos_ref, sin_ref = refs[18:20]
-    mine, theirs, v_out = refs[20:23]
-    abuf, wbuf, acc, sem_a, sem_w = refs[23:]
-    turn, core = place[0], place[1]
-    rows, depth = a_own[0].shape
-    half = weights[0].shape[1]
+def project_kernel(rows, place, *refs):
+    a_own, (x0, x_rest, y0, y_rest, d_rest) = refs[:4], refs[4:9]
+    w_same, w_swap = refs[9:13], refs[13:17]
+    cos_ref, sin_ref = refs[17:19]
+    mine, theirs, v_out = refs[19:22]
+    abuf, wbuf, acc, sem_a, sem_w = refs[22:]
+    turn, core = place[4], place[1]
+    half = w_same[0].shape[0]
+    rest = pl.ds(rows, 3 * rows)
+
+    def copies_a(t):
+        if t == 0:
+            pairs = [(a_own[b], 0, b * rows, rows) for b in range(4)]
+        elif t < 3:
+            first, others = ((x0, x_rest), (y0, y_rest))[t - 1]
+            pairs = [(first, 0, 0, rows), (others, 0, rows, 3 * rows)]
+        else:
+            late, mid = 3 * rows, rows // 2
+            pairs = [(y_rest, late, 0, mid), (x_rest, late, mid, mid), (d_rest, 0, rows, 3 * rows)]
+        return [
+            pltpu.make_async_copy(
+                ref.at[pl.ds(source, size)], abuf.at[t, pl.ds(target, size)], sem_a.at[t, n]
+            )
+            for n, (ref, source, target, size) in enumerate(pairs)
+        ]
+
+    def copies_w(t, s):
+        out = []
+        for n, (ref, side) in enumerate(((w_same[s], core), (w_swap[s], 1 - core))):
+            target = wbuf.at[t, pl.ds(pl.multiple_of(side * half, half), half)]
+            out.append(pltpu.make_async_copy(ref, target, sem_w.at[t, n]))
+        return out
+
+    for t in range(4):
+        for s in range(4):
+
+            @pl.when(s == lax.bitwise_xor(turn, t))
+            def _():
+                for copy in copies_w(t, s):
+                    copy.start()
+
+        for copy in copies_a(t):
+            copy.start()
 
     def copies(t):
-        out = []
-        start = 0
-        for i in range(4):
-            width = weights[i].shape[2]
-            side = core if i % 2 == 0 else 1 - core
-            out.append(
-                pltpu.make_async_copy(
-                    weights[i].at[lax.bitwise_xor(turn, t)],
-                    wbuf.at[
-                        t, pl.ds(pl.multiple_of(side * half, half), half), pl.ds(start, width)
-                    ],
-                    sem_w.at[t, i],
-                )
-            )
-            start += width * (i % 2)
-        for b in range(4):
-            if t < 3:
-                source = (a_own, a_x, a_y)[t][b].at[pl.ds(0, rows)]
-                target = abuf.at[t, pl.ds(b * rows, rows)]
-                out.append(pltpu.make_async_copy(source, target, sem_a.at[t, b]))
-                continue
-            late = pl.ds(rows if b < 3 else 0, rows // 2)
-            for n, part in enumerate((a_y, a_x)):
-                target = abuf.at[t, pl.ds(b * rows + n * (rows // 2), rows // 2)]
-                out.append(
-                    pltpu.make_async_copy(part[b + 1].at[late], target, sem_a.at[t + n, b])
-                )
-        return out
-
-    for t in range(4):
-        for copy in copies(t):
-            copy.start()
+        return copies_w(t, 0) + copies_a(t)
+
     for t in range(4):
         for copy in copies(t):
             copy.wait()
@@ -244,7 +249,7 @@
         total = acc[b * rows : (b + 1) * rows]
         cosine, sine = cos_ref[b], sin_ref[b]
         at = place[5 + b]
-        for col, out in ((0, 0), (4 * HD, HD)):
+        for col, out in ((0, 0), (2 * HD, HD)):
             heads = []
             for start in (col, col + HD):
                 x = total[:, start : start + HD]
@@ -252,30 +257,30 @@
                 heads.append(x.astype(jnp.bfloat16))
             mine[at, :, out : out + HD] = jnp.where(first, heads[0], heads[1])
             theirs[at, :, out : out + HD] = jnp.where(first, heads[1], heads[0])
-        v_out[at] = total[:, 2 * HD : 4 * HD].astype(jnp.bfloat16)
-
-
-def project(place, a_own, a_x, a_y, weights, cosine, sine):
+        v_out[at] = total[:, 4 * HD :].astype(jnp.bfloat16)
+
+
+def project(place, a_own, a_plane, w_same, w_swap, cosine, sine):
     rows, depth = a_own[0].shape
-    width = weights[0].shape[2] + weights[2].shape[2]
+    width = w_same[0].shape[1]
     out = jax.ShapeDtypeStruct((4, rows, 2 * HD), jnp.bfloat16)
     return pl.pallas_call(
-        project_kernel,
+        functools.partial(project_kernel, rows),
         out_shape=(out, out, out),
-        in_specs=[whole(pltpu.SMEM)] + [whole(pl.ANY)] * 18 + [whole(pltpu.VMEM)] * 2,
+        in_specs=[whole(pltpu.SMEM)] + [whole(pl.ANY)] * 17 + [whole(pltpu.VMEM)] * 2,
         out_specs=[whole(pltpu.VMEM)] * 3,
         scratch_shapes=[
             pltpu.VMEM((4, 4 * rows, depth), jnp.bfloat16),
             pltpu.VMEM((4, depth, width), jnp.bfloat16),
             pltpu.VMEM((4 * rows, width), jnp.float32),
-            pltpu.SemaphoreType.DMA((5, 4)),
             pltpu.SemaphoreType.DMA((4, 4)),
+            pltpu.SemaphoreType.DMA((4, 2)),
         ],
         compiler_params=kernel_params(),
         cost_estimate=pl.CostEstimate(
             flops=8 * rows * 4 * depth * width, bytes_accessed=16 * 2**20, transcendentals=0
         ),
-    )(place, *a_own, *a_x, *a_y, *weights, cosine, sine)
+    )(place, *a_own, *a_plane, *w_same, *w_swap, cosine, sine)
 
 
 def prepare_kernel(place, mine, other, key_ref, even_ref, odd_ref, q_out, k_out, corr, *scratch):
@@ -364,21 +369,40 @@
     )(place, mine, other, key_taps, even, odd)
 
 
-def key_taps_of(weights):
-    tap = jnp.arange(LANES)[None, None, :] + CK // 2 + AHEAD - jnp.arange(2 * LANES)[:, None, None]
-    out = jnp.zeros((2 * LANES, CQ, LANES), jnp.float32)
-    for c in range(CK):
-        out = out + jnp.where(tap == c, weights[:, c][None, :, None], 0.0)
-    return out.astype(jnp.bfloat16).reshape(2 * LANES, CQ * LANES)
-
-
-def band_taps(weights, first, lanes):
-    lag = jnp.arange(CQ)[:, None, None]
-    tap = (first + jnp.arange(lanes))[None, None, :] + CK // 2 + 8 - jnp.arange(LANES)[None, :, None]
-    band = jnp.zeros((CQ, LANES, lanes), jnp.float32)
-    for c in range(CK):
-        band = band + jnp.where(tap == c, weights[:, c][:, None, None], 0.0)
-    return band.astype(jnp.bfloat16).reshape(CQ * LANES, lanes)
+def tables_kernel(weights, key_ref, even_ref, odd_ref):
+    def fill(ref, origin, swap):
+        height = ref.shape[0] if swap else ref.shape[0] // CQ
+        width = ref.shape[1] // CQ if swap else ref.shape[1]
+        shape = (height, width)
+        tap = lax.broadcasted_iota(jnp.int32, shape, 1) - lax.broadcasted_iota(jnp.int32, shape, 0)
+        for a in range(CQ):
+            value = jnp.zeros(shape, jnp.float32)
+            for c in range(CK):
+                value = jnp.where(tap == c - origin, weights[a * CK + c], value)
+            value = value.astype(jnp.bfloat16)
+            if swap:
+                ref[:, a * width : (a + 1) * width] = value
+            else:
+                ref[a * height : (a + 1) * height, :] = value
+
+    fill(key_ref, CK // 2 + AHEAD, True)
+    fill(even_ref, CK // 2 + 8 - BAND, False)
+    fill(odd_ref, CK // 2 + 8 - SUB, False)
+
+
+def tables_of(weights):
+    return pl.pallas_call(
+        tables_kernel,
+        out_shape=(
+            jax.ShapeDtypeStruct((2 * LANES, CQ * LANES), jnp.bfloat16),
+            jax.ShapeDtypeStruct((CQ * LANES, 2 * LANES), jnp.bfloat16),
+            jax.ShapeDtypeStruct((CQ * LANES, LANES), jnp.bfloat16),
+        ),
+        in_specs=[whole(pltpu.SMEM)],
+        out_specs=[whole(pltpu.VMEM)] * 3,
+        compiler_params=pltpu.CompilerParams(vmem_limit_bytes=8 * 1024 * 1024),
+        cost_estimate=pl.CostEstimate(flops=2**23, bytes_accessed=2**20, transcendentals=0),
+    )(weights)
 
 
 def attend_kernel(place, mix, q_ref, k_ref, corr, va, vb, vc, vd, mine, theirs, v_all):
@@ -502,7 +526,7 @@
 
     def copy_w(n):
         t, i = order[n]
-        source = per * lax.bitwise_xor(place[4], t) + i
+        source = per * lax.bitwise_xor(place[0], t) + i
         return pltpu.make_async_copy(w_any.at[source], w_buf.at[n], sem.at[n])
 
     for n in range(blocks):
@@ -556,79 +580,67 @@
 ):
     ctx, head = lax.axis_index("ctx"), lax.axis_index("head")
     z, core = ctx // 2, ctx % 2
-    pair = 2 * HD
-    same_core = [[i for i in range(8) if i % 2 == k] for k in range(2)]
-
-    def columns(*weights):
-        shaped = [w.reshape(w.shape[0], 4, pair) for w in weights]
-        return lax.all_to_all(
-            jnp.concatenate(shaped, -1).transpose(1, 0, 2),
-            "ctx",
-            0,
-            0,
-            axis_index_groups=same_core,
-        )
-
-    middle = [(2, 4), (3, 5), (4, 2), (5, 3)]
-    outward = [(2, 0), (3, 1), (4, 6), (5, 7)]
-    inner = (z == 1) | (z == 2)
     rows = activations.shape[0]
     half = rows // 2
-
-    def plane(block, x_before, y_before):
-        to_x = jnp.concatenate([block, y_before[half:rows]])
-        to_y = jnp.concatenate([block, x_before[:half]])
-        return swapped(to_x, "head", 1), swapped(to_y, "head", 2)
-
     barrier = lax.optimization_barrier
-    near = swapped(activations, "ctx", 2)
-    across = lax.ppermute(activations, "ctx", middle)
+    pair = 2 * HD
+
+    def columns(target):
+        parts = [
+            lax.dynamic_slice_in_dim(w, target * pair, pair, 1) for w in (w_query, w_key, w_value)
+        ]
+        return jnp.concatenate(parts, 1)
+
+    digits = jnp.stack([positions // 256, positions % 256]).astype(jnp.bfloat16)
+    digits = jnp.pad(digits, ((0, 14), (0, activations.shape[1] - rows)))
+    block = jnp.concatenate([activations, digits])
+    w_pieces = [columns(z ^ s) for s in range(4)]
+    w_near = swapped(w_pieces[1], "ctx", 2)
+    far = [swapped(block, "ctx", 2 * s) for s in (1, 2, 3)]
     x0, y0 = swapped(activations, "head", 1), swapped(activations, "head", 2)
-    place_near = swapped(positions, "ctx", 2)
-    vk_same, q_same = columns(w_value, w_key), columns(w_query)
-    near, across, x0, y0 = barrier((near, across, x0, y0))
-    across_next = lax.ppermute(near, "ctx", middle)
-    passed = lax.ppermute(across, "ctx", outward)
-    x1, y1 = plane(near, x0, y0)
-    across_next, passed, x1, y1, place_near = barrier((across_next, passed, x1, y1, place_near))
-    far_a = across + passed
-    passed_next = lax.ppermute(across_next, "ctx", outward)
-    x2, y2 = plane(far_a, x1, y1)
-    place_far = swapped(jnp.stack([positions, place_near]), "ctx", 4)
-    passed_next, x2, y2, place_far, vk_same = barrier((passed_next, x2, y2, place_far, vk_same))
-    far_b = across_next + passed_next
-    x3, y3 = plane(far_b, x2, y2)
-    vk_swap = swapped(vk_same, "ctx", 1)
-    x3, y3, vk_swap, q_same, w_out = barrier((x3, y3, vk_swap, q_same, w_out))
-    x4, y4 = swapped(y3[half:rows], "head", 1), swapped(x3[:half], "head", 2)
-    q_swap = swapped(q_same, "ctx", 1)
-
-    place_far = jnp.where(inner, place_far[::-1], place_far)
-    place_of = jnp.concatenate([jnp.stack([positions, place_near]), place_far])
-    order = jnp.where(inner, z ^ 3, z ^ 2), jnp.where(inner, z ^ 2, z ^ 3)
-    place = jnp.stack([head, core, z % 2, z // 2, head, z, z ^ 1, *order]).astype(jnp.int32)
-
+    far, x0, y0, w_near, w_pieces = barrier((far, x0, y0, w_near, w_pieces))
+
+    w_far = [swapped(w_pieces[s], "ctx", 2 * s) for s in (2, 3)]
+    inner = [a[:rows] for a in far]
+    x_rest = swapped(jnp.concatenate(inner + [y0[half:]]), "head", 1)
+    y_rest = swapped(jnp.concatenate(inner + [x0[:half]]), "head", 2)
+    d_rest = swapped(jnp.concatenate(inner), "head", 3)
+    place_of = jnp.stack(
+        [
+            a[rows, :rows].astype(jnp.float32) * 256.0 + a[rows + 1, :rows].astype(jnp.float32)
+            for a in [block] + far
+        ]
+    )
     exponents = jnp.arange(HD // 2, dtype=jnp.float32) * (2.0 / HD)
     inverse = jnp.exp(-exponents * math.log(500000.0))
-    angle = (place_of.astype(jnp.float32) * 0.25)[:, :, None] * inverse
+    angle = (place_of * 0.25)[:, :, None] * inverse
     cosine, sine = jnp.cos(angle), jnp.sin(angle)
+    cosine = jnp.concatenate([cosine, cosine], -1)
+    sine = jnp.concatenate([-sine, sine], -1)
+    weights = lax.dynamic_index_in_dim(conv_kernel, ctx, 0, keepdims=False)
+    tables = tables_of(weights * (math.log2(math.e) / math.sqrt(HD)))
+    place = jnp.stack([head, core, z % 2, z // 2, z ^ head, z, z ^ 1, z ^ 2, z ^ 3])
+    place = place.astype(jnp.int32)
+    w_far, x_rest, y_rest, d_rest, cosine, sine, tables, place = barrier(
+        (w_far, x_rest, y_rest, d_rest, cosine, sine, tables, place)
+    )
+    w_same = [w_pieces[0], w_near] + list(w_far)
+    w_swap = [swapped(w, "ctx", 1) for w in w_same]
+    w_all = lax.all_gather(w_out, "ctx", axis=0)
+
     mine, theirs, v_pair = project(
         place,
-        (activations, near, far_a, far_b),
-        (x0, x1, x2, x3, x4),
-        (y0, y1, y2, y3, y4),
-        (q_same, q_swap, vk_same, vk_swap),
-        jnp.concatenate([cosine, cosine], -1),
-        jnp.concatenate([-sine, sine], -1),
-    )
+        [activations] + list(far),
+        (x0, x_rest, y0, y_rest, d_rest),
+        w_same,
+        w_swap,
+        cosine,
+        sine,
+    )
+    mine, theirs, v_pair, w_all = barrier((mine, theirs, v_pair, w_all))
     other = swapped(theirs, "ctx", 1)
     v_next = swapped(v_pair, "ctx", 2)
     v_pair_other = swapped(v_pair, "ctx", 1)
-
-    weights = lax.dynamic_index_in_dim(conv_kernel, ctx, 0, keepdims=False)
-    weights = weights * (math.log2(math.e) / math.sqrt(HD))
-    taps = weights.reshape(CQ, CK)
-    tables = key_taps_of(taps), band_taps(taps, -BAND, 2 * LANES), band_taps(taps, -SUB, LANES)
     q_wide, k_wide, corr = prepare(place, mine, other, *tables)
     v_next, q_wide = barrier((v_next, q_wide))
     v_next_other = swapped(v_next, "ctx", 1)
@@ -648,7 +660,6 @@
         for s in (1, 2, 3)
     ]
 
-    w_all = lax.all_gather(w_out, "ctx", axis=0)
     shares = finish(place, own, r1, r2, r3, out_gain.reshape(1, -1), w_all)
     total = shares[0].astype(jnp.float32)
     for t in (1, 2, 3):

time: 326 us -> 323 us (level); the launches traced: 320 us -> 321 us
  waiting for transfers between devices: 176 us -> 204 us
  starting transfers between devices: 47.4 us -> 31.8 us
  local copies, waits for them, and re-layouts: 22 us -> 11 us
    ppermute x26, waiting for transfers between devices: 144 us -> 203 us  [swapped(): return lax.ppermute(value, axis, [(i, i ^ mask) for i in range(count)])]
    all_to_all x2 -> x0, waiting for transfers between devices: 17.8 us -> none  [columns(): lax.all_to_all(jnp.concatenate(shaped, -1).transpose(1, 0, 2), 'ctx', 0,...]
    ppermute x4 -> x0, waiting for transfers between devices: 14.5 us -> none  [the longest x1 10.2 us: per_device_one_head(): across = lax.ppermute(activations, 'ctx', middle)]
    all_to_all x2 -> x0, starting transfers between devices: 9.24 us -> none  [columns(): lax.all_to_all(jnp.concatenate(shaped, -1).transpose(1, 0, 2), 'ctx', 0,...]
    ppermute x4 -> x0, starting transfers between devices: 8.19 us -> none  [the longest x1 3.5 us: per_device_one_head(): across_next = lax.ppermute(near, 'ctx', middle)]
    convert_element_type x3 -> x0, other arithmetic: 6.26 us -> none  [the longest x2 4.4 us: band_taps(): return band.astype(jnp.bfloat16).reshape(CQ * LANES, lanes)]
    concatenate x4 -> x9, other arithmetic: 1.88 us -> 7.74 us  [the longest x4 2.86 us: columns(): return jnp.concatenate(parts, 1)]
    broadcast_in_dim x28 -> x0, local copies, waits for them, and re-layouts: 4.88 us -> none  [key_taps_of(): out = out + jnp.where(tap == c, weights[:, c][None, :, None], 0.0)]
  transfers between devices with their start and end apart: 33 -> 27, of which waited for: 20 -> 18; matrix products, arithmetic and copies ran while one was open for 9% -> 5% of each run, Pallas kernels for 11% -> 8%
where the time goes in v3:
time: 323 us; the launch traced here: 321 us
  waiting for transfers between devices  204 us (63%)
  Pallas kernels  44.1 us (14%)
  starting transfers between devices  31.8 us (10%)
  other arithmetic  16.4 us (5%)
  between operations  13.7 us (4%)
  local copies, waits for them, and re-layouts  11 us (3%)
    ppermute x26, waiting for transfers between devices, swapped(): return lax.ppermute(value, axis, [(i, i ^ mask) for i in range(count)])  203 us
    ppermute x26, starting transfers between devices, swapped(): return lax.ppermute(value, axis, [(i, i ^ mask) for i in range(count)])  31.8 us
    pallas_call x1, Pallas kernels, project(): pl.pallas_call(functools.partial(project_kernel, rows), out_shape=(out, o...  15.6 us
    pallas_call x1, Pallas kernels, attend_head(): pl.pallas_call(attend_kernel, grid=(count,), out_shape=(out, out), in_spe...  12.4 us
    pallas_call x1, Pallas kernels, prepare(): pl.pallas_call(prepare_kernel, out_shape=(jax.ShapeDtypeStruct((total, CQ...  7.73 us
    pallas_call x1, Pallas kernels, finish(): pl.pallas_call(finish_kernel, in_specs=[whole(pltpu.SMEM)] + [whole(pltpu...  6.99 us
    unnamed x58, local copies, waits for them, and re-layouts  6.66 us
  transfers between devices with their start and end apart: 27, of which 18 were waited for; matrix products, arithmetic and copies ran while one was open for 5% of the time, Pallas kernels for 8%

profile of v3, /device:TPU:17, one launch (start us, length us, event | category | flops | bytes accessed | tf_op | source)
XLA Modules:
  0.0 320.6 jit_solution(13581232271018959461)
XLA Ops:
  6.6 0.7 all-gather.3.cloned.1.call-update
  7.3 1.3 collective-permute-start.3
  9.1 1.4 collective-permute-start.5
  10.6 0.9 collective-permute-start
  11.5 1.7 collective-permute-start.2
  13.3 7.2 %collective-permute-done.3.refs_4_ = bf16[256,1024]{1,0:T(8,128)(2,1)} collective-permute-done((bf16[256,1024]{1,0:T(8,128)(2,1)}, bf16[256,1024]{1,0:T(8,128)(2,1)}, u32[]{:S(2)}, u32[]{:S(2)}) %collective-permute-start.3) | collective-permute-done | bytes 524320 | tf_op jit(solution)/shard_map/ppermute | solution.py:575
  20.4 1.2 collective-permute-start.4
  21.7 0.9 pad_maximum_fusion.5.refs_9_
  22.6 0.9 pad_maximum_fusion.6
  23.6 0.9 pad_maximum_fusion.7
  24.5 7.9 %collective-permute-done.4.refs_6_ = bf16[256,1024]{1,0:T(8,128)(2,1)S(1)} collective-permute-done((bf16[256,1024]{1,0:T(8,128)(2,1)S(1)}, bf16[256,1024]{1,0:T(8,128)(2,1)S(1)}, u32[]{:S(2)}, u32[]{:S(2)}) %collective-permute-start.4) | collective-permute-done | bytes 524320 | tf_op jit(solution)/shard_map/ppermute | solution.py:575
  32.4 78.8 %collective-permute-done.refs_1_ = bf16[272,1024]{1,0:T(8,128)(2,1)S(1)} collective-permute-done((bf16[272,1024]{1,0:T(8,128)(2,1)S(1)}, bf16[272,1024]{1,0:T(8,128)(2,1)S(1)}, u32[]{:S(2)}, u32[]{:S(2)}) %collective-permute-start) | collective-permute-done | bytes 557088 | tf_op jit(solution)/shard_map/ppermute | solution.py:575
  112.7 1.0 slice.41
  113.7 1.5 pad_maximum_fusion.2
  115.2 1.0 collective-permute-start.8
  116.2 1.2 collective-permute-start.9
  117.4 1.3 pad_maximum_fusion.3
  119.1 0.7 fusion.13.weights
  120.4 1.4 shard_map.91
  121.7 0.8 copy-done.1
  122.5 0.8 copy-done.2
  123.3 0.7 copy-done.3
  123.9 2.3 collective-permute-start.6
  126.2 4.3 %collective-permute-start.7 = (bf16[512,768]{1,0:T(8,128)(2,1)}, bf16[512,768]{1,0:T(8,128)(2,1)S(1)}, u32[]{:S(2)}, u32[]{:S(2)}) collective-permute-start(bf16[512,768]{1,0:T(8,128)(2,1)} %pad_maximum_fusion.7), channel_id=1, source_target_pairs={{0,24},{4,28},{8,16},{12,20},{16,8},{20,12},{24,0},{28,4},{1,25},{... | collective-permute-start | bytes 2359304 | tf_op jit(solution)/shard_map/ppermute | solution.py:575
  130.5 0.8 convert_add_fusion.1
  131.2 0.8 convert_add_fusion.2
  132.0 0.8 convert_add_fusion.3
  132.8 1.9 fusion.3
  134.7 1.0 pad_maximum_fusion.9.refs_17_
  135.7 1.1 pad_maximum_fusion.10.refs_18_
  136.8 39.3 %collective-permute-done.6.refs_11_ = bf16[512,768]{1,0:T(8,128)(2,1)S(1)} collective-permute-done((bf16[512,768]{1,0:T(8,128)(2,1)}, bf16[512,768]{1,0:T(8,128)(2,1)S(1)}, u32[]{:S(2)}, u32[]{:S(2)}) %collective-permute-start.6) | collective-permute-done | bytes 786464 | tf_op jit(solution)/shard_map/ppermute | solution.py:575
  176.1 6.0 %collective-permute-start.11 = (bf16[512,768]{1,0:T(8,128)(2,1)S(1)}, bf16[512,768]{1,0:T(8,128)(2,1)S(1)}, u32[]{:S(2)}, u32[]{:S(2)}) collective-permute-start(bf16[512,768]{1,0:T(8,128)(2,1)S(1)} %copy-done.7), channel_id=1, source_target_pairs={{0,4},{4,0},{8,12},{12,8},{16,20},{20,16},{24,28},{28,24},{1,5},{5... | collective-permute-start | bytes 2359304 | tf_op jit(solution)/shard_map/ppermute | solution.py:575
  182.1 14.3 %collective-permute-done.7.refs_12_ = bf16[512,768]{1,0:T(8,128)(2,1)S(1)} collective-permute-done((bf16[512,768]{1,0:T(8,128)(2,1)}, bf16[512,768]{1,0:T(8,128)(2,1)S(1)}, u32[]{:S(2)}, u32[]{:S(2)}) %collective-permute-start.7) | collective-permute-done | bytes 786464 | tf_op jit(solution)/shard_map/ppermute | solution.py:575
  196.5 1.9 collective-permute-start.12
  199.0 1.3 collective-permute-done.12.refs_14_
  200.3 1.1 collective-permute-done.13.refs_15_
  201.4 1.1 collective-permute-done.14.refs_16_
  202.6 0.9 copy-done.24
  203.4 15.6 %shard_map.92 = (bf16[4,256,256]{2,1,0:T(8,128)(2,1)}, bf16[4,256,256]{2,1,0:T(8,128)(2,1)}, bf16[4,256,256]{2,1,0:T(8,128)(2,1)}) custom-call(s32[9]{0:T(128)} %stack.62.place, bf16[256,1024]{1,0:T(8,128)(2,1)} %refs_0_.1, bf16[272,1024]{1,0:T(8,128)(2,1)} %copy-done.9, bf16[272,1024]{1,0:T(8,128)(2,1)} %copy-done.10, bf16[272,1024]{1,0:T(8,128)(2,1)} %copy-done.11, ...), custom_call_target="tpu_custom_call" | custom-call | flops 6442450944 | bytes 16777216 | tf_op jit(solution)/shard_map/pallas_call | solution.py:267
  219.7 1.6 collective-permute-done.16.other
  221.3 0.8 copy-done.28
  222.0 7.7 %shard_map.93 = (bf16[2048,768]{1,0:T(8,128)(2,1)}, bf16[768,2048]{1,0:T(8,128)(2,1)}, f32[8,256,384]{2,1,0:T(8,128)}) custom-call(s32[9]{0:T(128)} %stack.62.place, bf16[4,256,256]{2,1,0:T(8,128)(2,1)} %get-tuple-element.70.mine, bf16[4,256,256]{2,1,0:T(8,128)(2,1)} %copy-done.28, bf16[256,768]{1,0:T(8,128)(2,1)} %copy-done.1, bf16[768,256]{1,0:T(8,128)(2,1)} %copy-done.2, ...), custom_call_target="tpu_custom_call" | custom-call | flops 2147483648 | bytes 12582912 | tf_op jit(solution)/shard_map/pallas_call | solution.py:352
  229.8 3.3 %collective-permute-done.15.vb = bf16[4,256,256]{2,1,0:T(8,128)(2,1)S(1)} collective-permute-done((bf16[4,256,256]{2,1,0:T(8,128)(2,1)}, bf16[4,256,256]{2,1,0:T(8,128)(2,1)S(1)}, u32[]{:S(2)}, u32[]{:S(2)}) %collective-permute-start.15) | collective-permute-done | bytes 524320 | tf_op jit(solution)/shard_map/ppermute | solution.py:575
  233.1 0.9 collective-permute-start.18
  234.7 0.9 collective-permute-done.18.vd
  235.6 0.8 copy-done.27
  236.4 12.4 %shard_map.94 = (bf16[4,256,512]{2,1,0:T(8,128)(2,1)}, bf16[4,256,512]{2,1,0:T(8,128)(2,1)}) custom-call(s32[9]{0:T(128)} %stack.62.place, f32[4]{0:T(128)} %dynamic-slice_bitcast_fusion.1.mix, bf16[2048,768]{1,0:T(8,128)(2,1)} %get-tuple-element.76.q_ref, bf16[768,2048]{1,0:T(8,128)(2,1)} %get-tuple-element.77.k_ref, ...), custom_call_target="tpu_custom_call" | custom-call | flops 5368709120 | bytes 16777216 | tf_op jit(solution)/shard_map/pallas_call | solution.py:499
  249.2 2.5 collective-permute-done.19
  251.7 1.6 convert_add_fusion
  253.3 0.8 fusion.2
  254.1 1.1 collective-permute-start.21
  255.2 1.6 collective-permute-start.22
  256.8 0.8 dynamic-slice_bitcast_fusion.own
  257.6 6.5 %collective-permute-done.20.r1 = bf16[256,512]{1,0:T(8,128)(2,1)S(1)} collective-permute-done((bf16[256,512]{1,0:T(8,128)(2,1)}, bf16[256,512]{1,0:T(8,128)(2,1)S(1)}, u32[]{:S(2)}, u32[]{:S(2)}) %collective-permute-start.20) | collective-permute-done | bytes 262176 | tf_op jit(solution)/shard_map/ppermute | solution.py:575
  264.1 3.0 collective-permute-done.21.r2
  267.2 12.3 %collective-permute-done.22.r3 = bf16[256,512]{1,0:T(8,128)(2,1)S(1)} collective-permute-done((bf16[256,512]{1,0:T(8,128)(2,1)S(1)}, bf16[256,512]{1,0:T(8,128)(2,1)S(1)}, u32[]{:S(2)}, u32[]{:S(2)}) %collective-permute-start.22) | collective-permute-done | bytes 262176 | tf_op jit(solution)/shard_map/ppermute | solution.py:575
  279.5 0.7 copy-done.14
  280.2 7.0 %shard_map.95 = (bf16[256,1024]{1,0:T(8,128)(2,1)}, bf16[256,1024]{1,0:T(8,128)(2,1)}, bf16[256,1024]{1,0:T(8,128)(2,1)}, bf16[256,1024]{1,0:T(8,128)(2,1)}) custom-call(s32[9]{0:T(128)} %stack.62.place, f32[256,512]{1,0:T(8,128)} %dynamic-slice_bitcast_fusion.own, bf16[256,512]{1,0:T(8,128)(2,1)} %copy-done.12, bf16[256,512]{1,0:T(8,128)(2,1)} %copy-done.13, ...), custom_call_target="tpu_custom_call" | custom-call | flops 2147483648 | bytes 11534336 | tf_op jit(solution)/shard_map/pallas_call | solution.py:556
  287.2 1.7 collective-permute-start.23
  288.8 1.0 collective-permute-start.24
  290.1 9.6 %collective-permute-done.23 = bf16[256,1024]{1,0:T(8,128)(2,1)S(1)} collective-permute-done((bf16[256,1024]{1,0:T(8,128)(2,1)}, bf16[256,1024]{1,0:T(8,128)(2,1)S(1)}, u32[]{:S(2)}, u32[]{:S(2)}) %collective-permute-start.23) | collective-permute-done | bytes 524320 | tf_op jit(solution)/shard_map/ppermute | solution.py:575
  299.6 1.4 collective-permute-done.24
  301.1 10.5 %collective-permute-done.25 = bf16[256,1024]{1,0:T(8,128)(2,1)S(1)} collective-permute-done((bf16[256,1024]{1,0:T(8,128)(2,1)}, bf16[256,1024]{1,0:T(8,128)(2,1)S(1)}, u32[]{:S(2)}, u32[]{:S(2)}) %collective-permute-start.25) | collective-permute-done | bytes 524320 | tf_op jit(solution)/shard_map/ppermute | solution.py:575
  311.6 2.2 add_convert_fusion
  (88 shorter events, 5.5 us)
Async XLA Ops:
  6.5 227.5 %copy-start = (f32[8,4]{0,1:T(4,128)S(1)}, f32[8,4]{0,1:T(4,128)}, u32[]{:S(2)}) copy-start(f32[8,4]{0,1:T(4,128)} %param.15) | copy-start | bytes 388
  6.5 2.0 copy-start.4
  6.5 2.2 copy-start.6
  6.5 2.2 copy-start.5
  6.5 212.5 %all-gather.3.cloned.1.call-start = ((), (), s32[]{:S(2)}) async-start(), calls=%async_computation | async-start | bytes 9437184 | tf_op jit(solution)/shard_map/all_gather | solution.py:629
  7.3 13.2 %collective-permute-start.3 = (bf16[256,1024]{1,0:T(8,128)(2,1)}, bf16[256,1024]{1,0:T(8,128)(2,1)}, u32[]{:S(2)}, u32[]{:S(2)}) collective-permute-start(bf16[256,1024]{1,0:T(8,128)(2,1)} %refs_0_.1), channel_id=1, source_target_pairs={{0,1},{1,0},{2,3},{3,2},{4,5},{5,4},{6,7},{7,6},{8,9},{9,8},{10,11... | collective-permute-start | bytes 1572872 | tf_op jit(solution)/shard_map/ppermute | solution.py:575
  8.7 1.7 copy-start.16
  9.0 1.5 copy-start.8
  9.1 102.2 %collective-permute-start.5 = (bf16[512,768]{1,0:T(8,128)(2,1)S(1)}, bf16[512,768]{1,0:T(8,128)(2,1)S(1)}, u32[]{:S(2)}, u32[]{:S(2)}) collective-permute-start(bf16[512,768]{1,0:T(8,128)(2,1)S(1)} %pad_maximum_fusion.4), channel_id=1, source_target_pairs={{0,8},{4,12},{8,0},{12,4},{16,24},{20,28},{24,16},{28,20},{1,9},{5... | collective-permute-start | bytes 2359304 | tf_op jit(solution)/shard_map/ppermute | solution.py:575
  10.6 100.7 %collective-permute-start = (bf16[272,1024]{1,0:T(8,128)(2,1)S(1)}, bf16[272,1024]{1,0:T(8,128)(2,1)S(1)}, u32[]{:S(2)}, u32[]{:S(2)}) collective-permute-start(bf16[272,1024]{1,0:T(8,128)(2,1)S(1)} %pad_maximum_fusion.8), channel_id=1, source_target_pairs={{0,8},{4,12},{8,0},{12,4},{16,24},{20,28},{24,16},{28,20},{1,9},{5... | collective-permute-start | bytes 1671176 | tf_op jit(solution)/shard_map/ppermute | solution.py:575
  11.5 99.8 %collective-permute-start.1 = (bf16[272,1024]{1,0:T(8,128)(2,1)S(1)}, bf16[272,1024]{1,0:T(8,128)(2,1)S(1)}, u32[]{:S(2)}, u32[]{:S(2)}) collective-permute-start(bf16[272,1024]{1,0:T(8,128)(2,1)S(1)} %pad_maximum_fusion.8), channel_id=1, source_target_pairs={{0,16},{4,20},{8,24},{12,28},{16,0},{20,4},{24,8},{28,12},{1,17},{... | collective-permute-start | bytes 1671176 | tf_op jit(solution)/shard_map/ppermute | solution.py:575
  11.5 99.7 %collective-permute-start.2 = (bf16[272,1024]{1,0:T(8,128)(2,1)S(1)}, bf16[272,1024]{1,0:T(8,128)(2,1)S(1)}, u32[]{:S(2)}, u32[]{:S(2)}) collective-permute-start(bf16[272,1024]{1,0:T(8,128)(2,1)S(1)} %pad_maximum_fusion.8), channel_id=1, source_target_pairs={{0,24},{4,28},{8,16},{12,20},{16,8},{20,12},{24,0},{28,4},{1,25},{... | collective-permute-start | bytes 1671176 | tf_op jit(solution)/shard_map/ppermute | solution.py:575
  20.4 12.0 %collective-permute-start.4 = (bf16[256,1024]{1,0:T(8,128)(2,1)S(1)}, bf16[256,1024]{1,0:T(8,128)(2,1)S(1)}, u32[]{:S(2)}, u32[]{:S(2)}) collective-permute-start(bf16[256,1024]{1,0:T(8,128)(2,1)S(1)} %copy-done.8), channel_id=1, source_target_pairs={{0,2},{1,3},{2,0},{3,1},{4,6},{5,7},{6,4},{7,5},{8,10},{9,11},{10,... | collective-permute-start | bytes 1572872 | tf_op jit(solution)/shard_map/ppermute | solution.py:575
  32.4 79.0 %copy-start.15 = (bf16[256,1024]{1,0:T(8,128)(2,1)}, bf16[256,1024]{1,0:T(8,128)(2,1)S(1)}, u32[]{:S(2)}) copy-start(bf16[256,1024]{1,0:T(8,128)(2,1)S(1)} %collective-permute-done.4.refs_6_) | copy-start | bytes 1572868
  111.3 0.8 copy-start.9
  111.3 1.0 copy-start.10
  111.3 1.2 copy-start.11
  111.3 1.4 copy-start.17
  115.2 83.2 %collective-permute-start.8 = (bf16[896,1024]{1,0:T(8,128)(2,1)}, bf16[896,1024]{1,0:T(8,128)(2,1)}, u32[]{:S(2)}, u32[]{:S(2)}) collective-permute-start(bf16[896,1024]{1,0:T(8,128)(2,1)} %get-tuple-element.91), channel_id=1, source_target_pairs={{0,1},{1,0},{2,3},{3,2},{4,5},{5,4},{6,7},{7,6},{8,9},{9,8},{10,11... | collective-permute-start | bytes 5505032 | tf_op jit(solution)/shard_map/ppermute | solution.py:575
  116.2 82.2 %collective-permute-start.9 = (bf16[896,1024]{1,0:T(8,128)(2,1)S(1)}, bf16[896,1024]{1,0:T(8,128)(2,1)}, u32[]{:S(2)}, u32[]{:S(2)}) collective-permute-start(bf16[896,1024]{1,0:T(8,128)(2,1)S(1)} %get-tuple-element.90), channel_id=1, source_target_pairs={{0,2},{1,3},{2,0},{3,1},{4,6},{5,7},{6,4},{7,5},{8,10},{9,11},{10,... | collective-permute-start | bytes 5505032 | tf_op jit(solution)/shard_map/ppermute | solution.py:575
  118.7 79.6 %collective-permute-start.10 = (bf16[768,1024]{1,0:T(8,128)(2,1)}, bf16[768,1024]{1,0:T(8,128)(2,1)}, u32[]{:S(2)}, u32[]{:S(2)}) collective-permute-start(bf16[768,1024]{1,0:T(8,128)(2,1)} %pad_maximum_fusion.3), channel_id=1, source_target_pairs={{0,3},{1,2},{2,1},{3,0},{4,7},{5,6},{6,5},{7,4},{8,11},{9,10},{10,... | collective-permute-start | bytes 4718600 | tf_op jit(solution)/shard_map/ppermute | solution.py:575
  121.7 0.8 copy-start.1
  122.5 0.8 copy-start.2
  123.3 0.7 copy-start.3
  123.9 52.1 %collective-permute-start.6 = (bf16[512,768]{1,0:T(8,128)(2,1)}, bf16[512,768]{1,0:T(8,128)(2,1)S(1)}, u32[]{:S(2)}, u32[]{:S(2)}) collective-permute-start(bf16[512,768]{1,0:T(8,128)(2,1)} %pad_maximum_fusion.6), channel_id=1, source_target_pairs={{0,16},{4,20},{8,24},{12,28},{16,0},{20,4},{24,8},{28,12},{1,17},{... | collective-permute-start | bytes 2359304 | tf_op jit(solution)/shard_map/ppermute | solution.py:575
  126.2 70.3 %collective-permute-start.7 = (bf16[512,768]{1,0:T(8,128)(2,1)}, bf16[512,768]{1,0:T(8,128)(2,1)S(1)}, u32[]{:S(2)}, u32[]{:S(2)}) collective-permute-start(bf16[512,768]{1,0:T(8,128)(2,1)} %pad_maximum_fusion.7), channel_id=1, source_target_pairs={{0,24},{4,28},{8,16},{12,20},{16,8},{20,12},{24,0},{28,4},{1,25},{... | collective-permute-start | bytes 2359304 | tf_op jit(solution)/shard_map/ppermute | solution.py:575
  132.8 43.3 %copy-start.7 = (bf16[512,768]{1,0:T(8,128)(2,1)S(1)}, bf16[512,768]{1,0:T(8,128)(2,1)}, u32[]{:S(2)}) copy-start(bf16[512,768]{1,0:T(8,128)(2,1)} %pad_maximum_fusion.5.refs_9_) | copy-start | bytes 2359300
  132.8 63.7 %copy-start.18 = (bf16[512,768]{1,0:T(8,128)(2,1)S(1)}, bf16[512,768]{1,0:T(8,128)(2,1)}, u32[]{:S(2)}) copy-start(bf16[512,768]{1,0:T(8,128)(2,1)} %copy-done.17) | copy-start | bytes 2359300
  176.1 26.4 %copy-start.19 = (bf16[512,768]{1,0:T(8,128)(2,1)}, bf16[512,768]{1,0:T(8,128)(2,1)S(1)}, u32[]{:S(2)}) copy-start(bf16[512,768]{1,0:T(8,128)(2,1)S(1)} %collective-permute-done.6.refs_11_) | copy-start | bytes 2359300
  176.1 22.9 %collective-permute-start.11 = (bf16[512,768]{1,0:T(8,128)(2,1)S(1)}, bf16[512,768]{1,0:T(8,128)(2,1)S(1)}, u32[]{:S(2)}, u32[]{:S(2)}) collective-permute-start(bf16[512,768]{1,0:T(8,128)(2,1)S(1)} %copy-done.7), channel_id=1, source_target_pairs={{0,4},{4,0},{8,12},{12,8},{16,20},{20,16},{24,28},{28,24},{1,5},{5... | collective-permute-start | bytes 2359304 | tf_op jit(solution)/shard_map/ppermute | solution.py:575
  196.5 6.0 %copy-start.20 = (bf16[512,768]{1,0:T(8,128)(2,1)}, bf16[512,768]{1,0:T(8,128)(2,1)S(1)}, u32[]{:S(2)}) copy-start(bf16[512,768]{1,0:T(8,128)(2,1)S(1)} %collective-permute-done.7.refs_12_) | copy-start | bytes 2359300
  196.5 3.8 %collective-permute-start.12 = (bf16[512,768]{1,0:T(8,128)(2,1)S(1)}, bf16[512,768]{1,0:T(8,128)(2,1)S(1)}, u32[]{:S(2)}, u32[]{:S(2)}) collective-permute-start(bf16[512,768]{1,0:T(8,128)(2,1)S(1)} %copy-done.18), channel_id=1, source_target_pairs={{0,4},{4,0},{8,12},{12,8},{16,20},{20,16},{24,28},{28,24},{1,5},{5... | collective-permute-start | bytes 2359304 | tf_op jit(solution)/shard_map/ppermute | solution.py:575
  198.4 3.0 collective-permute-start.13
  198.5 4.1 %collective-permute-start.14 = (bf16[512,768]{1,0:T(8,128)(2,1)S(1)}, bf16[512,768]{1,0:T(8,128)(2,1)S(1)}, u32[]{:S(2)}, u32[]{:S(2)}) collective-permute-start(bf16[512,768]{1,0:T(8,128)(2,1)S(1)} %collective-permute-done.7.refs_12_), channel_id=1, source_target_pairs={{0,4},{4,0},{8,12},{12,8},{16,20},{20,16},{24,28},{28,24},{1,5},{5... | collective-permute-start | bytes 2359304 | tf_op jit(solution)/shard_map/ppermute | solution.py:575
  198.9 3.6 %copy-start.21 = (bf16[512,768]{1,0:T(8,128)(2,1)}, bf16[512,768]{1,0:T(8,128)(2,1)S(1)}, u32[]{:S(2)}) copy-start(bf16[512,768]{1,0:T(8,128)(2,1)S(1)} %collective-permute-done.11.refs_13_) | copy-start | bytes 2359300
  200.3 2.3 copy-start.22
  201.4 1.1 copy-start.23
  202.5 0.9 copy-start.24
  219.1 2.2 collective-permute-start.16
  219.5 13.6 %collective-permute-start.15 = (bf16[4,256,256]{2,1,0:T(8,128)(2,1)}, bf16[4,256,256]{2,1,0:T(8,128)(2,1)S(1)}, u32[]{:S(2)}, u32[]{:S(2)}) collective-permute-start(bf16[4,256,256]{2,1,0:T(8,128)(2,1)} %get-tuple-element.69.va), channel_id=1, source_target_pairs={{0,8},{4,12},{8,0},{12,4},{16,24},{20,28},{24,16},{28,20},{1,9},{5... | collective-permute-start | bytes 1572872 | tf_op jit(solution)/shard_map/ppermute | solution.py:575
  219.5 15.2 %collective-permute-start.17 = (bf16[4,256,256]{2,1,0:T(8,128)(2,1)}, bf16[4,256,256]{2,1,0:T(8,128)(2,1)S(1)}, u32[]{:S(2)}, u32[]{:S(2)}) collective-permute-start(bf16[4,256,256]{2,1,0:T(8,128)(2,1)} %get-tuple-element.69.va), channel_id=1, source_target_pairs={{0,4},{4,0},{8,12},{12,8},{16,20},{20,16},{24,28},{28,24},{1,5},{5... | collective-permute-start | bytes 1572872 | tf_op jit(solution)/shard_map/ppermute | solution.py:575
  221.2 0.8 copy-start.28
  233.1 2.5 copy-start.25
  233.1 2.5 collective-permute-start.18
  234.7 0.9 copy-start.26
  235.6 0.8 copy-start.27
  248.9 2.9 collective-permute-start.19
  254.1 10.0 %collective-permute-start.20 = (bf16[256,512]{1,0:T(8,128)(2,1)}, bf16[256,512]{1,0:T(8,128)(2,1)S(1)}, u32[]{:S(2)}, u32[]{:S(2)}) collective-permute-start(bf16[256,512]{1,0:T(8,128)(2,1)} %get-tuple-element.89), channel_id=1, source_target_pairs={{0,8},{4,12},{8,0},{12,4},{16,24},{20,28},{24,16},{28,20},{1,9},{5... | collective-permute-start | bytes 786440 | tf_op jit(solution)/shard_map/ppermute | solution.py:575
  254.1 13.0 %collective-permute-start.21 = (bf16[256,512]{1,0:T(8,128)(2,1)S(1)}, bf16[256,512]{1,0:T(8,128)(2,1)S(1)}, u32[]{:S(2)}, u32[]{:S(2)}) collective-permute-start(bf16[256,512]{1,0:T(8,128)(2,1)S(1)} %get-tuple-element.88), channel_id=1, source_target_pairs={{0,16},{4,20},{8,24},{12,28},{16,0},{20,4},{24,8},{28,12},{1,17},{... | collective-permute-start | bytes 786440 | tf_op jit(solution)/shard_map/ppermute | solution.py:575
  255.2 24.2 %collective-permute-start.22 = (bf16[256,512]{1,0:T(8,128)(2,1)S(1)}, bf16[256,512]{1,0:T(8,128)(2,1)S(1)}, u32[]{:S(2)}, u32[]{:S(2)}) collective-permute-start(bf16[256,512]{1,0:T(8,128)(2,1)S(1)} %get-tuple-element.87), channel_id=1, source_target_pairs={{0,24},{4,28},{8,16},{12,20},{16,8},{20,12},{24,0},{28,4},{1,25},{... | collective-permute-start | bytes 786440 | tf_op jit(solution)/shard_map/ppermute | solution.py:575
  264.1 15.4 %copy-start.12 = (bf16[256,512]{1,0:T(8,128)(2,1)}, bf16[256,512]{1,0:T(8,128)(2,1)S(1)}, u32[]{:S(2)}) copy-start(bf16[256,512]{1,0:T(8,128)(2,1)S(1)} %collective-permute-done.20.r1) | copy-start | bytes 786436
  267.2 12.3 %copy-start.13 = (bf16[256,512]{1,0:T(8,128)(2,1)}, bf16[256,512]{1,0:T(8,128)(2,1)S(1)}, u32[]{:S(2)}) copy-start(bf16[256,512]{1,0:T(8,128)(2,1)S(1)} %collective-permute-done.21.r2) | copy-start | bytes 786436
  279.5 0.7 copy-start.14
  287.2 12.5 %collective-permute-start.23 = (bf16[256,1024]{1,0:T(8,128)(2,1)}, bf16[256,1024]{1,0:T(8,128)(2,1)S(1)}, u32[]{:S(2)}, u32[]{:S(2)}) collective-permute-start(bf16[256,1024]{1,0:T(8,128)(2,1)} %get-tuple-element.84), channel_id=1, source_target_pairs={{0,1},{1,0},{2,3},{3,2},{4,5},{5,4},{6,7},{7,6},{8,9},{9,8},{10,11... | collective-permute-start | bytes 1572872 | tf_op jit(solution)/shard_map/ppermute | solution.py:575
  288.8 12.3 %collective-permute-start.24 = (bf16[256,1024]{1,0:T(8,128)(2,1)}, bf16[256,1024]{1,0:T(8,128)(2,1)S(1)}, u32[]{:S(2)}, u32[]{:S(2)}) collective-permute-start(bf16[256,1024]{1,0:T(8,128)(2,1)} %get-tuple-element.85), channel_id=1, source_target_pairs={{0,2},{1,3},{2,0},{3,1},{4,6},{5,7},{6,4},{7,5},{8,10},{9,11},{10,... | collective-permute-start | bytes 1572872 | tf_op jit(solution)/shard_map/ppermute | solution.py:575
  289.8 21.8 %collective-permute-start.25 = (bf16[256,1024]{1,0:T(8,128)(2,1)}, bf16[256,1024]{1,0:T(8,128)(2,1)S(1)}, u32[]{:S(2)}, u32[]{:S(2)}) collective-permute-start(bf16[256,1024]{1,0:T(8,128)(2,1)} %get-tuple-element.86), channel_id=1, source_target_pairs={{0,3},{1,2},{2,1},{3,0},{4,7},{5,6},{6,5},{7,4},{8,11},{9,10},{10,... | collective-permute-start | bytes 1572872 | tf_op jit(solution)/shard_map/ppermute | solution.py:575
Sparse Core Ops, SparseCore 0:
  9.0 125.4 all-gather.2

commit v4 on v3

--- a/solution.py
+++ b/solution.py
@@ -181,11 +181,10 @@
 LANES = 128
 SUB = 64
 AHEAD = 16
-VMEM_BYTES = 56 * 1024 * 1024
-
-
-def kernel_params():
-    return pltpu.CompilerParams(vmem_limit_bytes=VMEM_BYTES)
+
+
+def kernel_params(mebibytes):
+    return pltpu.CompilerParams(vmem_limit_bytes=mebibytes * 1024 * 1024)
 
 
 def whole(memory_space):
@@ -276,7 +275,7 @@
             pltpu.SemaphoreType.DMA((4, 4)),
             pltpu.SemaphoreType.DMA((4, 2)),
         ],
-        compiler_params=kernel_params(),
+        compiler_params=kernel_params(24),
         cost_estimate=pl.CostEstimate(
             flops=8 * rows * 4 * depth * width, bytes_accessed=16 * 2**20, transcendentals=0
         ),
@@ -364,7 +363,7 @@
             pltpu.VMEM((2, total // 2, CQ * LANES), jnp.bfloat16),
             pltpu.VMEM((total, 2 * LANES), jnp.bfloat16),
         ],
-        compiler_params=kernel_params(),
+        compiler_params=kernel_params(22),
         cost_estimate=pl.CostEstimate(flops=2**31, bytes_accessed=12 * 2**20, transcendentals=0),
     )(place, mine, other, key_taps, even, odd)
 
@@ -400,7 +399,7 @@
         ),
         in_specs=[whole(pltpu.SMEM)],
         out_specs=[whole(pltpu.VMEM)] * 3,
-        compiler_params=pltpu.CompilerParams(vmem_limit_bytes=8 * 1024 * 1024),
+        compiler_params=kernel_params(8),
         cost_estimate=pl.CostEstimate(flops=2**23, bytes_accessed=2**20, transcendentals=0),
     )(weights)
 
@@ -510,7 +509,7 @@
         + [v_spec] * 4,
         out_specs=[out_spec, out_spec],
         scratch_shapes=[pltpu.VMEM((total, GROUP * HD), jnp.bfloat16)],
-        compiler_params=kernel_params(),
+        compiler_params=kernel_params(30),
         cost_estimate=pl.CostEstimate(
             flops=total * total * (depth + GROUP * HD),
             bytes_accessed=16 * 2**20,
@@ -563,7 +562,7 @@
             pltpu.VMEM((blocks, depth, width), jnp.bfloat16),
             pltpu.SemaphoreType.DMA((blocks,)),
         ],
-        compiler_params=kernel_params(),
+        compiler_params=kernel_params(14),
         cost_estimate=pl.CostEstimate(
             flops=2 * rows * depth * blocks * width, bytes_accessed=11 * 2**20, transcendentals=0
         ),
@@ -598,7 +597,13 @@
     w_near = swapped(w_pieces[1], "ctx", 2)
     far = [swapped(block, "ctx", 2 * s) for s in (1, 2, 3)]
     x0, y0 = swapped(activations, "head", 1), swapped(activations, "head", 2)
-    far, x0, y0, w_near, w_pieces = barrier((far, x0, y0, w_near, w_pieces))
+    weights = lax.dynamic_index_in_dim(conv_kernel, ctx, 0, keepdims=False)
+    tables = tables_of(weights * (math.log2(math.e) / math.sqrt(HD)))
+    place = jnp.stack([head, core, z % 2, z // 2, z ^ head, z, z ^ 1, z ^ 2, z ^ 3])
+    place = place.astype(jnp.int32)
+    far, x0, y0, w_near, w_pieces, tables, place, w_out = barrier(
+        (far, x0, y0, w_near, w_pieces, tables, place, w_out)
+    )
 
     w_far = [swapped(w_pieces[s], "ctx", 2 * s) for s in (2, 3)]
     inner = [a[:rows] for a in far]
@@ -617,12 +622,8 @@
     cosine, sine = jnp.cos(angle), jnp.sin(angle)
     cosine = jnp.concatenate([cosine, cosine], -1)
     sine = jnp.concatenate([-sine, sine], -1)
-    weights = lax.dynamic_index_in_dim(conv_kernel, ctx, 0, keepdims=False)
-    tables = tables_of(weights * (math.log2(math.e) / math.sqrt(HD)))
-    place = jnp.stack([head, core, z % 2, z // 2, z ^ head, z, z ^ 1, z ^ 2, z ^ 3])
-    place = place.astype(jnp.int32)
-    w_far, x_rest, y_rest, d_rest, cosine, sine, tables, place = barrier(
-        (w_far, x_rest, y_rest, d_rest, cosine, sine, tables, place)
+    w_far, x_rest, y_rest, d_rest, cosine, sine = barrier(
+        (w_far, x_rest, y_rest, d_rest, cosine, sine)
     )
     w_same = [w_pieces[0], w_near] + list(w_far)
     w_swap = [swapped(w, "ctx", 1) for w in w_same]

time: 323 us -> 338 us (1.046)
  local copies, waits for them, and re-layouts: 11 us -> 31.8 us
  Pallas kernels: 44.1 us -> 33.1 us
  waiting for transfers between devices: 204 us -> 211 us
    unnamed x58 -> x60, local copies, waits for them, and re-layouts: 6.66 us -> 26.2 us
    ppermute x26, waiting for transfers between devices: 203 us -> 211 us  [swapped(): return lax.ppermute(value, axis, [(i, i ^ mask) for i in range(count)])]
  transfers between devices with their start and end apart: 27 -> 27, of which waited for: 18 -> 18; matrix products, arithmetic and copies ran while one was open for 5% -> 5% of each run, Pallas kernels for 8% -> 6%
where the time goes in v4:
time: 338 us; the launch traced here: 336 us
  waiting for transfers between devices  211 us (62%)
  Pallas kernels  33.1 us (10%)
  starting transfers between devices  32.3 us (10%)
  local copies, waits for them, and re-layouts  31.8 us (9%)
  between operations  13.7 us (4%)
  other arithmetic  13.5 us (4%)
    ppermute x26, waiting for transfers between devices, swapped(): return lax.ppermute(value, axis, [(i, i ^ mask) for i in range(count)])  211 us
    ppermute x26, starting transfers between devices, swapped(): return lax.ppermute(value, axis, [(i, i ^ mask) for i in range(count)])  32.3 us
    unnamed x60, local copies, waits for them, and re-layouts  26.2 us
    pallas_call x1, Pallas kernels, project(): pl.pallas_call(functools.partial(project_kernel, rows), out_shape=(out, o...  12.4 us
    pallas_call x1, Pallas kernels, attend_head(): pl.pallas_call(attend_kernel, grid=(count,), out_shape=(out, out), in_spe...  9.3 us
  transfers between devices with their start and end apart: 27, of which 18 were waited for; matrix products, arithmetic and copies ran while one was open for 5% of the time, Pallas kernels for 6%

profile of v4, /device:TPU:17, one launch (start us, length us, event | category | flops | bytes accessed | tf_op | source)
XLA Modules:
  0.0 335.7 jit_solution(12333314234820021062)
XLA Ops:
  6.5 1.3 collective-permute-start.3
  7.8 2.1 constant_dynamic-slice_fusion.3
  9.9 1.2 constant_dynamic-slice_fusion.1
  11.2 1.0 pad_maximum_fusion.4
  12.2 1.3 collective-permute-start.5
  13.5 0.9 pad_maximum_fusion.8
  14.7 2.4 collective-permute-start.2
  17.0 2.7 collective-permute-done.3.refs_4_
  19.7 1.2 collective-permute-start.4
  21.0 0.7 fusion.13.weights
  21.7 1.4 shard_map.91
  23.1 0.7 copy-done.11
  23.9 0.8 copy-done.13
  25.3 1.2 pad_maximum_fusion.5.refs_9_
  26.5 2.1 pad_maximum_fusion.6
  28.6 2.0 pad_maximum_fusion.7
  30.6 1.2 collective-permute-done.4.refs_6_
  31.8 21.7 %collective-permute-done.refs_1_ = bf16[272,1024]{1,0:T(8,128)(2,1)S(1)} collective-permute-done((bf16[272,1024]{1,0:T(8,128)(2,1)}, bf16[272,1024]{1,0:T(8,128)(2,1)S(1)}, u32[]{:S(2)}, u32[]{:S(2)}) %collective-permute-start) | collective-permute-done | bytes 557088 | tf_op jit(solution)/shard_map/ppermute | solution.py:574
  54.4 1.0 slice.40
  56.6 1.2 collective-permute-start.9
  57.9 0.9 collective-permute-start.10
  58.8 14.2 %collective-permute-start.6 = (bf16[512,768]{1,0:T(8,128)(2,1)S(1)}, bf16[512,768]{1,0:T(8,128)(2,1)S(1)}, u32[]{:S(2)}, u32[]{:S(2)}) collective-permute-start(bf16[512,768]{1,0:T(8,128)(2,1)S(1)} %copy-done.28), channel_id=1, source_target_pairs={{0,16},{4,20},{8,24},{12,28},{16,0},{20,4},{24,8},{28,12},{1,17},{... | collective-permute-start | bytes 2359304 | tf_op jit(solution)/shard_map/ppermute | solution.py:574
  73.2 1.9 fusion.3
  75.6 89.1 %collective-permute-done.6.refs_11_ = bf16[512,768]{1,0:T(8,128)(2,1)S(1)} collective-permute-done((bf16[512,768]{1,0:T(8,128)(2,1)S(1)}, bf16[512,768]{1,0:T(8,128)(2,1)S(1)}, u32[]{:S(2)}, u32[]{:S(2)}) %collective-permute-start.6) | collective-permute-done | bytes 786464 | tf_op jit(solution)/shard_map/ppermute | solution.py:574
  164.7 0.8 collective-permute-start.11
  165.5 43.4 %collective-permute-done.7.refs_12_ = bf16[512,768]{1,0:T(8,128)(2,1)S(1)} collective-permute-done((bf16[512,768]{1,0:T(8,128)(2,1)S(1)}, bf16[512,768]{1,0:T(8,128)(2,1)S(1)}, u32[]{:S(2)}, u32[]{:S(2)}) %collective-permute-start.7) | collective-permute-done | bytes 786464 | tf_op jit(solution)/shard_map/ppermute | solution.py:574
  210.1 1.8 collective-permute-done.12.refs_14_
  212.6 1.1 collective-permute-done.14.refs_16_
  213.7 12.4 %shard_map.92 = (bf16[4,256,256]{2,1,0:T(8,128)(2,1)S(1)}, bf16[4,256,256]{2,1,0:T(8,128)(2,1)S(1)}, bf16[4,256,256]{2,1,0:T(8,128)(2,1)S(1)}) custom-call(s32[9]{0:T(128)S(1)} %stack.61.place, bf16[256,1024]{1,0:T(8,128)(2,1)S(1)} %copy-done.2, bf16[272,1024]{1,0:T(8,128)(2,1)S(1)} %collective-permute-done.refs_1_, ...), custom_call_target="tpu_custom_call" | custom-call | flops 6442450944 | bytes 16777216 | tf_op jit(solution)/shard_map/pallas_call | solution.py:266
  226.1 0.8 copy-done.4
  226.9 0.8 copy-done.10
  227.7 0.8 copy-done.23
  229.0 1.6 collective-permute-done.16.other
  230.6 1.0 copy-done.12
  231.6 1.0 copy-done.14
  232.6 0.9 copy-done.16
  233.5 1.0 copy-done.24
  234.6 4.9 %shard_map.93 = (bf16[2048,768]{1,0:T(8,128)(2,1)S(1)}, bf16[768,2048]{1,0:T(8,128)(2,1)S(1)}, f32[8,256,384]{2,1,0:T(8,128)S(1)}) custom-call(s32[9]{0:T(128)S(1)} %stack.61.place, bf16[4,256,256]{2,1,0:T(8,128)(2,1)S(1)} %copy-done.24, bf16[4,256,256]{2,1,0:T(8,128)(2,1)S(1)} %collective-permute-done.16.other, bf16[256,768]{1,0:T(8,128)(2,1)S(1)} %copy-done.12, ...), custom_call_target="tpu_custom_call" | custom-call | flops 2147483648 | bytes 12582912 | tf_op jit(solution)/shard_map/pallas_call | solution.py:351
  239.5 1.6 copy-done.17
  241.1 1.6 copy-done.19
  242.7 1.6 copy-done.21
  244.8 0.8 copy-done.6
  246.3 0.8 copy-done.8
  247.1 1.0 copy-done.7
  248.1 1.0 copy-done.9
  249.2 1.9 copy-done.18
  251.1 1.9 copy-done.20
  253.0 1.9 copy-done.22
  254.9 9.3 %shard_map.94 = (bf16[4,256,512]{2,1,0:T(8,128)(2,1)S(1)}, bf16[4,256,512]{2,1,0:T(8,128)(2,1)S(1)}) custom-call(s32[9]{0:T(128)S(1)} %stack.61.place, f32[4]{0:T(128)S(1)} %dynamic-slice_bitcast_fusion.1.mix, bf16[2048,768]{1,0:T(8,128)(2,1)S(1)} %copy-done.18, bf16[768,2048]{1,0:T(8,128)(2,1)S(1)} %copy-done.20, f32[8,256,384]{2,1,0:T(8,128)S(1)} %copy-done.22, ...), custom_call_target="tpu_custom_call" | custom-call | flops 5368709120 | bytes 16777216 | tf_op jit(solution)/shard_map/pallas_call | solution.py:498
  264.6 2.4 collective-permute-done.19
  267.0 1.5 convert_add_fusion
  268.6 0.9 fusion.2
  269.6 1.2 collective-permute-start.21
  270.8 1.3 collective-permute-start.22
  272.1 7.7 %collective-permute-done.20.r1 = bf16[256,512]{1,0:T(8,128)(2,1)S(1)} collective-permute-done((bf16[256,512]{1,0:T(8,128)(2,1)}, bf16[256,512]{1,0:T(8,128)(2,1)S(1)}, u32[]{:S(2)}, u32[]{:S(2)}) %collective-permute-start.20) | collective-permute-done | bytes 262176 | tf_op jit(solution)/shard_map/ppermute | solution.py:574
  279.9 2.9 collective-permute-done.21.r2
  282.7 12.3 %collective-permute-done.22.r3 = bf16[256,512]{1,0:T(8,128)(2,1)S(1)} collective-permute-done((bf16[256,512]{1,0:T(8,128)(2,1)S(1)}, bf16[256,512]{1,0:T(8,128)(2,1)S(1)}, u32[]{:S(2)}, u32[]{:S(2)}) %collective-permute-start.22) | collective-permute-done | bytes 262176 | tf_op jit(solution)/shard_map/ppermute | solution.py:574
  295.0 3.4 %copy-done.1 = bf16[8192,512]{1,0:T(8,128)(2,1)S(1)} copy-done((bf16[8192,512]{1,0:T(8,128)(2,1)S(1)}, bf16[8192,512]{1,0:T(8,128)(2,1)}, u32[]{:S(2)}) %copy-start.1) | copy-done | bytes 8388632
  298.4 5.1 %shard_map.95 = (bf16[256,1024]{1,0:T(8,128)(2,1)S(1)}, bf16[256,1024]{1,0:T(8,128)(2,1)S(1)}, bf16[256,1024]{1,0:T(8,128)(2,1)S(1)}, bf16[256,1024]{1,0:T(8,128)(2,1)S(1)}) custom-call(s32[9]{0:T(128)S(1)} %stack.61.place, f32[256,512]{1,0:T(8,128)S(1)} %dynamic-slice_bitcast_fusion.own, bf16[256,512]{1,0:T(8,128)(2,1)S(1)} %collective-permute-done.20.r1, ...), custom_call_target="tpu_custom_call" | custom-call | flops 2147483648 | bytes 11534336 | tf_op jit(solution)/shard_map/pallas_call | solution.py:555
  304.2 1.2 collective-permute-start.24
  305.4 0.8 collective-permute-start.25
  306.3 9.3 %collective-permute-done.23 = bf16[256,1024]{1,0:T(8,128)(2,1)S(1)} collective-permute-done((bf16[256,1024]{1,0:T(8,128)(2,1)S(1)}, bf16[256,1024]{1,0:T(8,128)(2,1)S(1)}, u32[]{:S(2)}, u32[]{:S(2)}) %collective-permute-start.23) | collective-permute-done | bytes 524320 | tf_op jit(solution)/shard_map/ppermute | solution.py:574
  315.8 11.9 %collective-permute-done.25 = bf16[256,1024]{1,0:T(8,128)(2,1)S(1)} collective-permute-done((bf16[256,1024]{1,0:T(8,128)(2,1)S(1)}, bf16[256,1024]{1,0:T(8,128)(2,1)S(1)}, u32[]{:S(2)}, u32[]{:S(2)}) %collective-permute-start.25) | collective-permute-done | bytes 524320 | tf_op jit(solution)/shard_map/ppermute | solution.py:574
  327.7 1.2 add_convert_fusion
  (90 shorter events, 9.0 us)
Async XLA Ops:
  6.5 238.2 %copy-start = (f32[8,4]{0,1:T(4,128)S(1)}, f32[8,4]{0,1:T(4,128)}, u32[]{:S(2)}) copy-start(f32[8,4]{0,1:T(4,128)} %param.15) | copy-start | bytes 388
  6.5 3.4 %copy-start.26 = (bf16[512,1024]{1,0:T(8,128)(2,1)S(1)}, bf16[512,1024]{1,0:T(8,128)(2,1)}, u32[]{:S(2)}) copy-start(bf16[512,1024]{1,0:T(8,128)(2,1)} %param.12) | copy-start | bytes 3145732
  6.5 3.4 %copy-start.25 = (bf16[512,1024]{1,0:T(8,128)(2,1)S(1)}, bf16[512,1024]{1,0:T(8,128)(2,1)}, u32[]{:S(2)}) copy-start(bf16[512,1024]{1,0:T(8,128)(2,1)} %param.13) | copy-start | bytes 3145732
  6.5 221.9 %all-gather.3.cloned.1.call-start = ((), (), s32[]{:S(2)}) async-start(), calls=%async_computation | async-start | bytes 9437184 | tf_op jit(solution)/shard_map/all_gather | solution.py:630
  6.5 13.2 %collective-permute-start.3 = (bf16[256,1024]{1,0:T(8,128)(2,1)}, bf16[256,1024]{1,0:T(8,128)(2,1)S(1)}, u32[]{:S(2)}, u32[]{:S(2)}) collective-permute-start(bf16[256,1024]{1,0:T(8,128)(2,1)} %refs_0_.1), channel_id=1, source_target_pairs={{0,1},{1,0},{2,3},{3,2},{4,5},{5,4},{6,7},{7,6},{8,9},{9,8},{10,11... | collective-permute-start | bytes 1572872 | tf_op jit(solution)/shard_map/ppermute | solution.py:574
  9.9 3.5 %copy-start.29 = (s32[256]{0:T(256)S(1)}, s32[256]{0:T(256)}, u32[]{:S(2)}) copy-start(s32[256]{0:T(256)} %param.10) | copy-start | bytes 3076
  11.2 2.3 copy-start.2
  12.2 42.1 %collective-permute-start.5 = (bf16[512,768]{1,0:T(8,128)(2,1)}, bf16[512,768]{1,0:T(8,128)(2,1)}, u32[]{:S(2)}, u32[]{:S(2)}) collective-permute-start(bf16[512,768]{1,0:T(8,128)(2,1)} %pad_maximum_fusion.4), channel_id=1, source_target_pairs={{0,8},{4,12},{8,0},{12,4},{16,24},{20,28},{24,16},{28,20},{1,9},{5... | collective-permute-start | bytes 2359304 | tf_op jit(solution)/shard_map/ppermute | solution.py:574
  14.4 39.1 %collective-permute-start = (bf16[272,1024]{1,0:T(8,128)(2,1)}, bf16[272,1024]{1,0:T(8,128)(2,1)S(1)}, u32[]{:S(2)}, u32[]{:S(2)}) collective-permute-start(bf16[272,1024]{1,0:T(8,128)(2,1)} %pad_maximum_fusion.8), channel_id=1, source_target_pairs={{0,8},{4,12},{8,0},{12,4},{16,24},{20,28},{24,16},{28,20},{1,9},{5... | collective-permute-start | bytes 1671176 | tf_op jit(solution)/shard_map/ppermute | solution.py:574
  14.6 39.6 %collective-permute-start.1 = (bf16[272,1024]{1,0:T(8,128)(2,1)}, bf16[272,1024]{1,0:T(8,128)(2,1)S(1)}, u32[]{:S(2)}, u32[]{:S(2)}) collective-permute-start(bf16[272,1024]{1,0:T(8,128)(2,1)} %pad_maximum_fusion.8), channel_id=1, source_target_pairs={{0,16},{4,20},{8,24},{12,28},{16,0},{20,4},{24,8},{28,12},{1,17},{... | collective-permute-start | bytes 1671176 | tf_op jit(solution)/shard_map/ppermute | solution.py:574
  14.7 39.6 %collective-permute-start.2 = (bf16[272,1024]{1,0:T(8,128)(2,1)}, bf16[272,1024]{1,0:T(8,128)(2,1)S(1)}, u32[]{:S(2)}, u32[]{:S(2)}) collective-permute-start(bf16[272,1024]{1,0:T(8,128)(2,1)} %pad_maximum_fusion.8), channel_id=1, source_target_pairs={{0,24},{4,28},{8,16},{12,20},{16,8},{20,12},{24,0},{28,4},{1,25},{... | collective-permute-start | bytes 1671176 | tf_op jit(solution)/shard_map/ppermute | solution.py:574
  19.7 12.1 %collective-permute-start.4 = (bf16[256,1024]{1,0:T(8,128)(2,1)S(1)}, bf16[256,1024]{1,0:T(8,128)(2,1)}, u32[]{:S(2)}, u32[]{:S(2)}) collective-permute-start(bf16[256,1024]{1,0:T(8,128)(2,1)S(1)} %copy-done.2), channel_id=1, source_target_pairs={{0,2},{1,3},{2,0},{3,1},{4,6},{5,7},{6,4},{7,5},{8,10},{9,11},{10,... | collective-permute-start | bytes 1572872 | tf_op jit(solution)/shard_map/ppermute | solution.py:574
  23.1 0.8 copy-start.11
  23.9 0.8 copy-start.13
  24.6 0.7 copy-start.15
  55.9 2.9 copy-start.28
  55.9 17.1 %copy-start.27 = (bf16[512,768]{1,0:T(8,128)(2,1)S(1)}, bf16[512,768]{1,0:T(8,128)(2,1)}, u32[]{:S(2)}) copy-start(bf16[512,768]{1,0:T(8,128)(2,1)} %pad_maximum_fusion.7) | copy-start | bytes 2359300
  55.9 153.6 %collective-permute-start.8 = (bf16[896,1024]{1,0:T(8,128)(2,1)S(1)}, bf16[896,1024]{1,0:T(8,128)(2,1)S(1)}, u32[]{:S(2)}, u32[]{:S(2)}) collective-permute-start(bf16[896,1024]{1,0:T(8,128)(2,1)S(1)} %get-tuple-element.93), channel_id=1, source_target_pairs={{0,1},{1,0},{2,3},{3,2},{4,5},{5,4},{6,7},{7,6},{8,9},{9,8},{10,11... | collective-permute-start | bytes 5505032 | tf_op jit(solution)/shard_map/ppermute | solution.py:574
  56.6 153.0 %collective-permute-start.9 = (bf16[896,1024]{1,0:T(8,128)(2,1)S(1)}, bf16[896,1024]{1,0:T(8,128)(2,1)S(1)}, u32[]{:S(2)}, u32[]{:S(2)}) collective-permute-start(bf16[896,1024]{1,0:T(8,128)(2,1)S(1)} %get-tuple-element.92), channel_id=1, source_target_pairs={{0,2},{1,3},{2,0},{3,1},{4,6},{5,7},{6,4},{7,5},{8,10},{9,11},{10,... | collective-permute-start | bytes 5505032 | tf_op jit(solution)/shard_map/ppermute | solution.py:574
  57.9 151.6 %collective-permute-start.10 = (bf16[768,1024]{1,0:T(8,128)(2,1)S(1)}, bf16[768,1024]{1,0:T(8,128)(2,1)S(1)}, u32[]{:S(2)}, u32[]{:S(2)}) collective-permute-start(bf16[768,1024]{1,0:T(8,128)(2,1)S(1)} %pad_maximum_fusion.3), channel_id=1, source_target_pairs={{0,3},{1,2},{2,1},{3,0},{4,7},{5,6},{6,5},{7,4},{8,11},{9,10},{10,... | collective-permute-start | bytes 4718600 | tf_op jit(solution)/shard_map/ppermute | solution.py:574
  58.8 105.9 %collective-permute-start.6 = (bf16[512,768]{1,0:T(8,128)(2,1)S(1)}, bf16[512,768]{1,0:T(8,128)(2,1)S(1)}, u32[]{:S(2)}, u32[]{:S(2)}) collective-permute-start(bf16[512,768]{1,0:T(8,128)(2,1)S(1)} %copy-done.28), channel_id=1, source_target_pairs={{0,16},{4,20},{8,24},{12,28},{16,0},{20,4},{24,8},{28,12},{1,17},{... | collective-permute-start | bytes 2359304 | tf_op jit(solution)/shard_map/ppermute | solution.py:574
  73.0 135.8 %collective-permute-start.7 = (bf16[512,768]{1,0:T(8,128)(2,1)S(1)}, bf16[512,768]{1,0:T(8,128)(2,1)S(1)}, u32[]{:S(2)}, u32[]{:S(2)}) collective-permute-start(bf16[512,768]{1,0:T(8,128)(2,1)S(1)} %copy-done.27), channel_id=1, source_target_pairs={{0,24},{4,28},{8,16},{12,20},{16,8},{20,12},{24,0},{28,4},{1,25},{... | collective-permute-start | bytes 2359304 | tf_op jit(solution)/shard_map/ppermute | solution.py:574
  164.7 45.4 %collective-permute-start.11 = (bf16[512,768]{1,0:T(8,128)(2,1)S(1)}, bf16[512,768]{1,0:T(8,128)(2,1)S(1)}, u32[]{:S(2)}, u32[]{:S(2)}) collective-permute-start(bf16[512,768]{1,0:T(8,128)(2,1)S(1)} %pad_maximum_fusion.5.refs_9_), channel_id=1, source_target_pairs={{0,4},{4,0},{8,12},{12,8},{16,20},{20,16},{24,28},{28,24},{1,5},{5... | collective-permute-start | bytes 2359304 | tf_op jit(solution)/shard_map/ppermute | solution.py:574
  208.8 3.0 collective-permute-start.12
  209.5 3.0 collective-permute-start.13
  209.6 4.1 %collective-permute-start.14 = (bf16[512,768]{1,0:T(8,128)(2,1)S(1)}, bf16[512,768]{1,0:T(8,128)(2,1)S(1)}, u32[]{:S(2)}, u32[]{:S(2)}) collective-permute-start(bf16[512,768]{1,0:T(8,128)(2,1)S(1)} %collective-permute-done.7.refs_12_), channel_id=1, source_target_pairs={{0,4},{4,0},{8,12},{12,8},{16,20},{20,16},{24,28},{28,24},{1,5},{5... | collective-permute-start | bytes 2359304 | tf_op jit(solution)/shard_map/ppermute | solution.py:574
  226.1 0.8 copy-start.4
  226.9 0.8 copy-start.10
  227.7 0.8 copy-start.23
  228.5 18.6 %copy-start.5 = (bf16[4,256,256]{2,1,0:T(8,128)(2,1)S(1)}, bf16[4,256,256]{2,1,0:T(8,128)(2,1)}, u32[]{:S(2)}) copy-start(bf16[4,256,256]{2,1,0:T(8,128)(2,1)} %copy-done.4) | copy-start | bytes 1572868
  228.5 2.1 collective-permute-start.16
  228.9 15.5 %collective-permute-start.15 = (bf16[4,256,256]{2,1,0:T(8,128)(2,1)}, bf16[4,256,256]{2,1,0:T(8,128)(2,1)S(1)}, u32[]{:S(2)}, u32[]{:S(2)}) collective-permute-start(bf16[4,256,256]{2,1,0:T(8,128)(2,1)} %copy-done.4), channel_id=1, source_target_pairs={{0,8},{4,12},{8,0},{12,4},{16,24},{20,28},{24,16},{28,20},{1,9},{5... | collective-permute-start | bytes 1572872 | tf_op jit(solution)/shard_map/ppermute | solution.py:574
  228.9 16.0 %collective-permute-start.17 = (bf16[4,256,256]{2,1,0:T(8,128)(2,1)}, bf16[4,256,256]{2,1,0:T(8,128)(2,1)S(1)}, u32[]{:S(2)}, u32[]{:S(2)}) collective-permute-start(bf16[4,256,256]{2,1,0:T(8,128)(2,1)} %copy-done.4), channel_id=1, source_target_pairs={{0,4},{4,0},{8,12},{12,8},{16,20},{20,16},{24,28},{28,24},{1,5},{5... | collective-permute-start | bytes 1572872 | tf_op jit(solution)/shard_map/ppermute | solution.py:574
  230.6 1.0 copy-start.12
  231.6 1.0 copy-start.14
  232.6 0.9 copy-start.16
  233.5 1.0 copy-start.24
  239.4 1.6 copy-start.17
  241.1 1.6 copy-start.19
  242.7 1.7 copy-start.21
  244.4 1.9 collective-permute-start.18
  244.8 0.8 copy-start.6
  246.3 0.8 copy-start.8
  247.1 1.0 copy-start.7
  248.1 1.0 copy-start.9
  249.2 1.9 copy-start.18
  251.1 1.9 copy-start.20
  253.0 1.9 copy-start.22
  264.2 2.9 collective-permute-start.19
  268.6 26.5 %copy-start.3 = (f32[1024]{0:T(1024)S(1)}, f32[1024]{0:T(1024)}, u32[]{:S(2)}) copy-start(f32[1024]{0:T(1024)} %param.16) | copy-start | bytes 12292
  269.5 10.4 %collective-permute-start.20 = (bf16[256,512]{1,0:T(8,128)(2,1)}, bf16[256,512]{1,0:T(8,128)(2,1)S(1)}, u32[]{:S(2)}, u32[]{:S(2)}) collective-permute-start(bf16[256,512]{1,0:T(8,128)(2,1)} %get-tuple-element.91), channel_id=1, source_target_pairs={{0,8},{4,12},{8,0},{12,4},{16,24},{20,28},{24,16},{28,20},{1,9},{5... | collective-permute-start | bytes 786440 | tf_op jit(solution)/shard_map/ppermute | solution.py:574
  269.6 13.1 %collective-permute-start.21 = (bf16[256,512]{1,0:T(8,128)(2,1)}, bf16[256,512]{1,0:T(8,128)(2,1)S(1)}, u32[]{:S(2)}, u32[]{:S(2)}) collective-permute-start(bf16[256,512]{1,0:T(8,128)(2,1)} %get-tuple-element.90), channel_id=1, source_target_pairs={{0,16},{4,20},{8,24},{12,28},{16,0},{20,4},{24,8},{28,12},{1,17},{... | collective-permute-start | bytes 786440 | tf_op jit(solution)/shard_map/ppermute | solution.py:574
  270.8 24.2 %collective-permute-start.22 = (bf16[256,512]{1,0:T(8,128)(2,1)S(1)}, bf16[256,512]{1,0:T(8,128)(2,1)S(1)}, u32[]{:S(2)}, u32[]{:S(2)}) collective-permute-start(bf16[256,512]{1,0:T(8,128)(2,1)S(1)} %get-tuple-element.89), channel_id=1, source_target_pairs={{0,24},{4,28},{8,16},{12,20},{16,8},{20,12},{24,0},{28,4},{1,25},{... | collective-permute-start | bytes 786440 | tf_op jit(solution)/shard_map/ppermute | solution.py:574
  295.0 3.4 %copy-start.1 = (bf16[8192,512]{1,0:T(8,128)(2,1)S(1)}, bf16[8192,512]{1,0:T(8,128)(2,1)}, u32[]{:S(2)}) copy-start(bf16[8192,512]{1,0:T(8,128)(2,1)} %all-gather.3.cloned.1.call-done) | copy-start | bytes 25165828
  303.5 12.0 %collective-permute-start.23 = (bf16[256,1024]{1,0:T(8,128)(2,1)S(1)}, bf16[256,1024]{1,0:T(8,128)(2,1)S(1)}, u32[]{:S(2)}, u32[]{:S(2)}) collective-permute-start(bf16[256,1024]{1,0:T(8,128)(2,1)S(1)} %get-tuple-element.86), channel_id=1, source_target_pairs={{0,1},{1,0},{2,3},{3,2},{4,5},{5,4},{6,7},{7,6},{8,9},{9,8},{10,11... | collective-permute-start | bytes 1572872 | tf_op jit(solution)/shard_map/ppermute | solution.py:574
  304.2 11.7 %collective-permute-start.24 = (bf16[256,1024]{1,0:T(8,128)(2,1)S(1)}, bf16[256,1024]{1,0:T(8,128)(2,1)S(1)}, u32[]{:S(2)}, u32[]{:S(2)}) collective-permute-start(bf16[256,1024]{1,0:T(8,128)(2,1)S(1)} %get-tuple-element.87), channel_id=1, source_target_pairs={{0,2},{1,3},{2,0},{3,1},{4,6},{5,7},{6,4},{7,5},{8,10},{9,11},{10,... | collective-permute-start | bytes 1572872 | tf_op jit(solution)/shard_map/ppermute | solution.py:574
  305.4 22.3 %collective-permute-start.25 = (bf16[256,1024]{1,0:T(8,128)(2,1)S(1)}, bf16[256,1024]{1,0:T(8,128)(2,1)S(1)}, u32[]{:S(2)}, u32[]{:S(2)}) collective-permute-start(bf16[256,1024]{1,0:T(8,128)(2,1)S(1)} %get-tuple-element.88), channel_id=1, source_target_pairs={{0,3},{1,2},{2,1},{3,0},{4,7},{5,6},{6,5},{7,4},{8,11},{9,10},{10,... | collective-permute-start | bytes 1572872 | tf_op jit(solution)/shard_map/ppermute | solution.py:574
Sparse Core Ops, SparseCore 0:
  54.4 152.7 all-gather.2

commit v5 on v4

--- a/solution.py
+++ b/solution.py
@@ -191,15 +191,13 @@
     return pl.BlockSpec(memory_space=memory_space)
 
 
-def project_kernel(rows, place, *refs):
+def project_kernel(rows, first_col, place, *refs):
     a_own, (x0, x_rest, y0, y_rest, d_rest) = refs[:4], refs[4:9]
     w_same, w_swap = refs[9:13], refs[13:17]
-    cos_ref, sin_ref = refs[17:19]
-    mine, theirs, v_out = refs[19:22]
-    abuf, wbuf, acc, sem_a, sem_w = refs[22:]
+    abuf, wbuf, acc, sem_a, sem_w = refs[-5:]
     turn, core = place[4], place[1]
     half = w_same[0].shape[0]
-    rest = pl.ds(rows, 3 * rows)
+    width = wbuf.shape[2]
 
     def copies_a(t):
         if t == 0:
@@ -220,8 +218,9 @@
     def copies_w(t, s):
         out = []
         for n, (ref, side) in enumerate(((w_same[s], core), (w_swap[s], 1 - core))):
+            source = ref.at[:, pl.ds(first_col, width)]
             target = wbuf.at[t, pl.ds(pl.multiple_of(side * half, half), half)]
-            out.append(pltpu.make_async_copy(ref, target, sem_w.at[t, n]))
+            out.append(pltpu.make_async_copy(source, target, sem_w.at[t, n]))
         return out
 
     for t in range(4):
@@ -234,15 +233,17 @@
 
         for copy in copies_a(t):
             copy.start()
-
-    def copies(t):
-        return copies_w(t, 0) + copies_a(t)
-
     for t in range(4):
-        for copy in copies(t):
+        for copy in copies_w(t, 0) + copies_a(t):
             copy.wait()
         part = jnp.dot(abuf[t], wbuf[t], preferred_element_type=jnp.float32)
         acc[...] = part if t == 0 else acc[...] + part
+    if first_col:
+        v_out = refs[17]
+        for b in range(4):
+            v_out[place[5 + b]] = acc[b * rows : (b + 1) * rows].astype(jnp.bfloat16)
+        return
+    cos_ref, sin_ref, mine, theirs = refs[17:21]
     first = core == 0
     for b in range(4):
         total = acc[b * rows : (b + 1) * rows]
@@ -256,18 +257,20 @@
                 heads.append(x.astype(jnp.bfloat16))
             mine[at, :, out : out + HD] = jnp.where(first, heads[0], heads[1])
             theirs[at, :, out : out + HD] = jnp.where(first, heads[1], heads[0])
-        v_out[at] = total[:, 4 * HD :].astype(jnp.bfloat16)
-
-
-def project(place, a_own, a_plane, w_same, w_swap, cosine, sine):
+
+
+def project(place, a_own, a_plane, w_same, w_swap, angles=()):
     rows, depth = a_own[0].shape
-    width = w_same[0].shape[1]
+    first_col, width = (0, 4 * HD) if angles else (4 * HD, 2 * HD)
     out = jax.ShapeDtypeStruct((4, rows, 2 * HD), jnp.bfloat16)
+    count = 2 if angles else 1
     return pl.pallas_call(
-        functools.partial(project_kernel, rows),
-        out_shape=(out, out, out),
-        in_specs=[whole(pltpu.SMEM)] + [whole(pl.ANY)] * 17 + [whole(pltpu.VMEM)] * 2,
-        out_specs=[whole(pltpu.VMEM)] * 3,
+        functools.partial(project_kernel, rows, first_col),
+        out_shape=[out] * count,
+        in_specs=[whole(pltpu.SMEM)]
+        + [whole(pl.ANY)] * 17
+        + [whole(pltpu.VMEM)] * len(angles),
+        out_specs=[whole(pltpu.VMEM)] * count,
         scratch_shapes=[
             pltpu.VMEM((4, 4 * rows, depth), jnp.bfloat16),
             pltpu.VMEM((4, depth, width), jnp.bfloat16),
@@ -275,16 +278,15 @@
             pltpu.SemaphoreType.DMA((4, 4)),
             pltpu.SemaphoreType.DMA((4, 2)),
         ],
-        compiler_params=kernel_params(24),
+        compiler_params=kernel_params(20),
         cost_estimate=pl.CostEstimate(
             flops=8 * rows * 4 * depth * width, bytes_accessed=16 * 2**20, transcendentals=0
         ),
-    )(place, *a_own, *a_plane, *w_same, *w_swap, cosine, sine)
-
-
-def prepare_kernel(place, mine, other, key_ref, even_ref, odd_ref, q_out, k_out, corr, *scratch):
+    )(place, *a_own, *a_plane, *w_same, *w_swap, *angles)
+
+
+def prepare(core, mine, other, key_ref, even_ref, odd_ref, q_out, k_out, corr, *scratch):
     qf, kf, lags, turned = scratch
-    core = place[1]
     total = q_out.shape[0]
     qf[0:8] = jnp.zeros((8, HD), jnp.float32)
     kf[0:AHEAD] = jnp.zeros((AHEAD, HD), jnp.float32)
@@ -346,28 +348,6 @@
                 ]
 
 
-def prepare(place, mine, other, key_taps, even, odd):
-    total = mine.shape[0] * 2 * ROWS
-    return pl.pallas_call(
-        prepare_kernel,
-        out_shape=(
-            jax.ShapeDtypeStruct((total, CQ * HD), jnp.bfloat16),
-            jax.ShapeDtypeStruct((CQ * HD, total), jnp.bfloat16),
-            jax.ShapeDtypeStruct((total // ROWS, ROWS, BAND + ROWS), jnp.float32),
-        ),
-        in_specs=[whole(pltpu.SMEM)] + [whole(pltpu.VMEM)] * 5,
-        out_specs=[whole(pltpu.VMEM)] * 3,
-        scratch_shapes=[
-            pltpu.VMEM((8 + total, HD), jnp.float32),
-            pltpu.VMEM((AHEAD + total + LANES, HD), jnp.float32),
-            pltpu.VMEM((2, total // 2, CQ * LANES), jnp.bfloat16),
-            pltpu.VMEM((total, 2 * LANES), jnp.bfloat16),
-        ],
-        compiler_params=kernel_params(22),
-        cost_estimate=pl.CostEstimate(flops=2**31, bytes_accessed=12 * 2**20, transcendentals=0),
-    )(place, mine, other, key_taps, even, odd)
-
-
 def tables_kernel(weights, key_ref, even_ref, odd_ref):
     def fill(ref, origin, swap):
         height = ref.shape[0] if swap else ref.shape[0] // CQ
@@ -404,13 +384,16 @@
     )(weights)
 
 
-def attend_kernel(place, mix, q_ref, k_ref, corr, va, vb, vc, vd, mine, theirs, v_all):
+def attend_kernel(place, mix, *refs):
+    qk_refs, (va, vb, vc, vd), (mine, theirs) = refs[:5], refs[5:9], refs[9:11]
+    v_all, q_wide, k_ref, corr = refs[11:15]
     side, core = place[2], place[1]
     b = pl.program_id(0)
     count = k_ref.shape[1] // (2 * ROWS)
 
     @pl.when(b == 0)
     def _():
+        prepare(core, *qk_refs, q_wide, k_ref, corr, *refs[15:])
         for i in range(count):
             for parity, near, far in ((core, va, vb), (1 - core, vc, vd)):
                 rows = pl.ds(pl.multiple_of((2 * i + parity) * ROWS, ROWS), ROWS)
@@ -430,24 +413,25 @@
         return jnp.concatenate([upper, lower], 0)
 
     def block(step):
+        q_rows = q_wide[2 * step * ROWS : (2 * step + 2) * ROWS]
         parts = []
         for j in range(2 * step + 1):
             part = jnp.dot(
-                q_ref[...],
+                q_rows,
                 k_ref[:, j * ROWS : (j + 1) * ROWS],
                 preferred_element_type=jnp.float32,
             )
             if j == 2 * step:
-                diagonal = jnp.where(seen, part[top] - corr[0, :, BAND:], -jnp.inf)
-                part = rows_of(diagonal, fixed(part[low], 1))
+                diagonal = jnp.where(seen, part[top] - corr[2 * step, :, BAND:], -jnp.inf)
+                part = rows_of(diagonal, fixed(part[low], 2 * step + 1))
             elif j == 2 * step - 1:
-                part = rows_of(fixed(part[top], 0), part[low])
+                part = rows_of(fixed(part[top], 2 * step), part[low])
             parts.append(part)
         start = (2 * step + 1) * ROWS
         last = jnp.dot(
-            q_ref[low], k_ref[:, start : start + ROWS], preferred_element_type=jnp.float32
+            q_rows[low], k_ref[:, start : start + ROWS], preferred_element_type=jnp.float32
         )
-        last = jnp.where(seen, last - corr[1, :, BAND:], -jnp.inf)
+        last = jnp.where(seen, last - corr[2 * step + 1, :, BAND:], -jnp.inf)
         peak = parts[0]
         for part in parts[1:]:
             peak = jnp.maximum(peak, part)
@@ -488,48 +472,62 @@
         pl.when(b == step)(lambda step=step: block(step))
 
 
-def attend_head(place, mix, q_wide, k_wide, corr, va, vb, vc, vd):
-    depth, total = k_wide.shape
-    rows = 2 * ROWS
-    count = total // rows
+def attend_head(place, mix, mine, other, tables, values):
+    total = 2 * mine.shape[0] * ROWS
+    count = total // (2 * ROWS)
+    depth = CQ * HD
     out = jax.ShapeDtypeStruct((count, ROWS, GROUP * HD), jnp.bfloat16)
     out_spec = pl.BlockSpec((1, ROWS, GROUP * HD), lambda b: (b, 0, 0))
-    v_spec = pl.BlockSpec(va.shape, lambda b: (0, 0, 0))
     return pl.pallas_call(
         attend_kernel,
         grid=(count,),
         out_shape=(out, out),
-        in_specs=[
-            whole(pltpu.SMEM),
-            whole(pltpu.SMEM),
-            pl.BlockSpec((rows, depth), lambda b: (b, 0)),
-            pl.BlockSpec((depth, total), lambda b: (0, 0)),
-            pl.BlockSpec((2, ROWS, BAND + ROWS), lambda b: (b, 0, 0)),
-        ]
-        + [v_spec] * 4,
+        in_specs=[whole(pltpu.SMEM)] * 2 + [whole(pltpu.VMEM)] * 9,
         out_specs=[out_spec, out_spec],
-        scratch_shapes=[pltpu.VMEM((total, GROUP * HD), jnp.bfloat16)],
-        compiler_params=kernel_params(30),
+        scratch_shapes=[
+            pltpu.VMEM((total, GROUP * HD), jnp.bfloat16),
+            pltpu.VMEM((total, depth), jnp.bfloat16),
+            pltpu.VMEM((depth, total), jnp.bfloat16),
+            pltpu.VMEM((total // ROWS, ROWS, BAND + ROWS), jnp.float32),
+            pltpu.VMEM((8 + total, HD), jnp.float32),
+            pltpu.VMEM((AHEAD + total + LANES, HD), jnp.float32),
+            pltpu.VMEM((2, total // 2, CQ * LANES), jnp.bfloat16),
+            pltpu.VMEM((total, 2 * LANES), jnp.bfloat16),
+        ],
+        compiler_params=kernel_params(36),
         cost_estimate=pl.CostEstimate(
             flops=total * total * (depth + GROUP * HD),
             bytes_accessed=16 * 2**20,
             transcendentals=total * total // 2,
         ),
-    )(place, mix, q_wide, k_wide, corr, va, vb, vc, vd)
-
-
-def finish_kernel(place, own, r1, r2, r3, gain, w_any, o0, o1, o2, o3, normed, w_buf, sem):
-    blocks, _, width = w_buf.shape
-    per = blocks // 4
-    order = [(t, i) for t in (3, 2, 1, 0) for i in range(per)]
-
-    def copy_w(n):
-        t, i = order[n]
-        source = per * lax.bitwise_xor(place[0], t) + i
-        return pltpu.make_async_copy(w_any.at[source], w_buf.at[n], sem.at[n])
-
-    for n in range(blocks):
-        copy_w(n).start()
+    )(place, mix, mine, other, *tables, *values)
+
+
+def finish_kernel(place, own, r1, r2, r3, gain, *refs):
+    w_parts, outs = refs[:12], refs[12:16]
+    normed, w_buf, sem = refs[16:]
+    width = w_parts[0].shape[1]
+    core, head, inner = place[1], place[0], place[9]
+
+    def copy_w(n, source):
+        side = core if n % 2 == 0 else 1 - core
+        cols = pl.ds(pl.multiple_of(side * width, width), width)
+        target = w_buf.at[lax.bitwise_xor(place[5 + n // 2], head), :, cols]
+        return pltpu.make_async_copy(w_parts[source], target, sem.at[n])
+
+    for n in range(4):
+        copy_w(n, n).start()
+    for n in range(4, 8):
+        straight = n if n < 6 else n + 2
+
+        @pl.when(inner == 1)
+        def _():
+            copy_w(n, straight).start()
+
+        @pl.when(inner == 0)
+        def _():
+            copy_w(n, straight + 2).start()
+
     near = own[...] + r1[...].astype(jnp.float32)
     far = r2[...].astype(jnp.float32) + r3[...].astype(jnp.float32)
     low = place[3] == 0
@@ -541,32 +539,32 @@
         normed[:, g * HD : (g + 1) * HD] = (
             x * scale * gain[:, g * HD : (g + 1) * HD]
         ).astype(jnp.bfloat16)
-    for n in range(blocks):
-        t, i = order[n]
-        copy_w(n).wait()
-        (o0, o1, o2, o3)[t][:, i * width : (i + 1) * width] = jnp.dot(
-            normed[...], w_buf[n], preferred_element_type=jnp.float32
+    for n in range(8):
+        copy_w(n, n).wait()
+    for t in (3, 2, 1, 0):
+        outs[t][...] = jnp.dot(
+            normed[...], w_buf[t], preferred_element_type=jnp.float32
         ).astype(jnp.bfloat16)
 
 
-def finish(place, own, r1, r2, r3, gain, w_all):
+def finish(place, own, r1, r2, r3, gain, w_parts):
     rows = own.shape[0]
-    blocks, depth, width = w_all.shape
+    depth, width = w_parts[0].shape
     return pl.pallas_call(
         finish_kernel,
-        in_specs=[whole(pltpu.SMEM)] + [whole(pltpu.VMEM)] * 5 + [whole(pl.ANY)],
+        in_specs=[whole(pltpu.SMEM)] + [whole(pltpu.VMEM)] * 5 + [whole(pl.ANY)] * 12,
         out_specs=[whole(pltpu.VMEM)] * 4,
-        out_shape=[jax.ShapeDtypeStruct((rows, blocks // 4 * width), jnp.bfloat16)] * 4,
+        out_shape=[jax.ShapeDtypeStruct((rows, 2 * width), jnp.bfloat16)] * 4,
         scratch_shapes=[
             pltpu.VMEM((rows, depth), jnp.bfloat16),
-            pltpu.VMEM((blocks, depth, width), jnp.bfloat16),
-            pltpu.SemaphoreType.DMA((blocks,)),
+            pltpu.VMEM((4, depth, 2 * width), jnp.bfloat16),
+            pltpu.SemaphoreType.DMA((8,)),
         ],
         compiler_params=kernel_params(14),
         cost_estimate=pl.CostEstimate(
-            flops=2 * rows * depth * blocks * width, bytes_accessed=11 * 2**20, transcendentals=0
+            flops=2 * rows * depth * 8 * width, bytes_accessed=11 * 2**20, transcendentals=0
         ),
-    )(place, own, r1, r2, r3, gain, w_all)
+    )(place, own, r1, r2, r3, gain, *w_parts)
 
 
 def swapped(value, axis, mask):
@@ -594,9 +592,9 @@
     digits = jnp.pad(digits, ((0, 14), (0, activations.shape[1] - rows)))
     block = jnp.concatenate([activations, digits])
     w_pieces = [columns(z ^ s) for s in range(4)]
-    w_near = swapped(w_pieces[1], "ctx", 2)
     far = [swapped(block, "ctx", 2 * s) for s in (1, 2, 3)]
     x0, y0 = swapped(activations, "head", 1), swapped(activations, "head", 2)
+    w_near = swapped(w_pieces[1], "ctx", 2)
     weights = lax.dynamic_index_in_dim(conv_kernel, ctx, 0, keepdims=False)
     tables = tables_of(weights * (math.log2(math.e) / math.sqrt(HD)))
     place = jnp.stack([head, core, z % 2, z // 2, z ^ head, z, z ^ 1, z ^ 2, z ^ 3])
@@ -622,34 +620,41 @@
     cosine, sine = jnp.cos(angle), jnp.sin(angle)
     cosine = jnp.concatenate([cosine, cosine], -1)
     sine = jnp.concatenate([-sine, sine], -1)
-    w_far, x_rest, y_rest, d_rest, cosine, sine = barrier(
-        (w_far, x_rest, y_rest, d_rest, cosine, sine)
+    w_far, x_rest, y_rest, d_rest, cosine, sine, w_out = barrier(
+        (w_far, x_rest, y_rest, d_rest, cosine, sine, w_out)
     )
     w_same = [w_pieces[0], w_near] + list(w_far)
     w_swap = [swapped(w, "ctx", 1) for w in w_same]
-    w_all = lax.all_gather(w_out, "ctx", axis=0)
-
-    mine, theirs, v_pair = project(
-        place,
-        [activations] + list(far),
-        (x0, x_rest, y0, y_rest, d_rest),
-        w_same,
-        w_swap,
-        cosine,
-        sine,
-    )
-    mine, theirs, v_pair, w_all = barrier((mine, theirs, v_pair, w_all))
-    other = swapped(theirs, "ctx", 1)
+    middle = [(2, 4), (3, 5), (4, 2), (5, 3)]
+    outward = [(2, 0), (3, 1), (4, 6), (5, 7)]
+    out_near = swapped(w_out, "ctx", 2)
+    out_across = lax.ppermute(w_out, "ctx", middle)
+    sources = place, [activations] + list(far), (x0, x_rest, y0, y_rest, d_rest), w_same, w_swap
+    (v_pair,) = project(*sources)
     v_next = swapped(v_pair, "ctx", 2)
     v_pair_other = swapped(v_pair, "ctx", 1)
-    q_wide, k_wide, corr = prepare(place, mine, other, *tables)
-    v_next, q_wide = barrier((v_next, q_wide))
+    out_own_swap = swapped(w_out, "ctx", 1)
+    place, v_pair = barrier((place, v_pair))
+    mine, theirs = project(place, *sources[1:], (cosine, sine))
+    mine, theirs, v_next, v_pair_other, out_near, out_across, out_own_swap = barrier(
+        (mine, theirs, v_next, v_pair_other, out_near, out_across, out_own_swap)
+    )
+    out_near_swap, out_across_swap = swapped(out_near, "ctx", 1), swapped(out_across, "ctx", 1)
+    other = swapped(theirs, "ctx", 1)
     v_next_other = swapped(v_next, "ctx", 1)
+    out_across_next = lax.ppermute(out_near, "ctx", middle)
+    out_passed = lax.ppermute(out_across, "ctx", outward)
     group_rows = lax.dynamic_slice_in_dim(head_mix, GROUP * (ctx // GROUP), GROUP, 0)
     mix = lax.dynamic_index_in_dim(group_rows, ctx % GROUP, 1, keepdims=False)
     out_mine, out_theirs = attend_head(
-        place, mix, q_wide, k_wide, corr, v_pair, v_next, v_pair_other, v_next_other
-    )
+        place, mix, mine, other, tables, (v_pair, v_next, v_pair_other, v_next_other)
+    )
+    out_mine, out_theirs, out_across_next, out_passed, out_near_swap, out_across_swap = barrier(
+        (out_mine, out_theirs, out_across_next, out_passed, out_near_swap, out_across_swap)
+    )
+    out_passed_next = lax.ppermute(out_across_next, "ctx", outward)
+    out_parts = [w_out, out_own_swap, out_near, out_near_swap, out_across, out_across_swap]
+    out_parts += [p for w in (out_passed, out_across_next) for p in (w, swapped(w, "ctx", 1))]
     summed = out_mine.astype(jnp.float32) + swapped(out_theirs, "ctx", 1).astype(jnp.float32)
     own = lax.dynamic_index_in_dim(summed, z, 0, keepdims=False)
     r1, r2, r3 = [
@@ -661,7 +666,14 @@
         for s in (1, 2, 3)
     ]
 
-    shares = finish(place, own, r1, r2, r3, out_gain.reshape(1, -1), w_all)
+    r1, r2, r3, out_passed_next = barrier((r1, r2, r3, out_passed_next))
+    out_parts += [out_passed_next, swapped(out_passed_next, "ctx", 1)]
+    inner = (z == 1) | (z == 2)
+    out_places = jnp.stack(
+        [z, z ^ 1, jnp.where(inner, z ^ 3, z ^ 2), jnp.where(inner, z ^ 2, z ^ 3), inner]
+    )
+    where = jnp.concatenate([place[:5], out_places.astype(jnp.int32)])
+    shares = finish(where, own, r1, r2, r3, out_gain.reshape(1, -1), out_parts)
     total = shares[0].astype(jnp.float32)
     for t in (1, 2, 3):
         total = total + swapped(shares[t], "head", t).astype(jnp.float32)

time: 338 us -> 298 us (0.88)
  waiting for transfers between devices: 211 us -> 171 us
  starting transfers between devices: 32.3 us -> 47.9 us
  between operations: 13.7 us -> 0.44 us
  local copies, waits for them, and re-layouts: 31.8 us -> 26.3 us
    ppermute x26 -> x33, waiting for transfers between devices: 211 us -> 142 us  [swapped(): return lax.ppermute(value, axis, [(i, i ^ mask) for i in range(count)])]
    ppermute x0 -> x4, waiting for transfers between devices: none -> 29.5 us  [the longest x1 27 us: per_device_one_head(): out_passed_next = lax.ppermute(out_across_next, 'ctx', outward)]
    ppermute x0 -> x4, starting transfers between devices: none -> 9.93 us  [the longest x1 3.19 us: per_device_one_head(): out_across = lax.ppermute(w_out, 'ctx', middle)]
    unnamed x60 -> x72, local copies, waits for them, and re-layouts: 26.2 us -> 20.5 us
    ppermute x26 -> x33, starting transfers between devices: 32.3 us -> 38 us  [swapped(): return lax.ppermute(value, axis, [(i, i ^ mask) for i in range(count)])]
    pallas_call x1, Pallas kernels: 9.3 us -> 14.9 us  [attend_head(): pl.pallas_call(attend_kernel, grid=(count,), out_shape=(out, out), in_spe...]
    pallas_call x2, Pallas kernels: 17.3 us -> 13.1 us  [project(): pl.pallas_call(functools.partial(project_kernel, rows, first_col), out_sh...]
  transfers between devices with their start and end apart: 27 -> 37, of which waited for: 18 -> 16; matrix products, arithmetic and copies ran while one was open for 5% -> 5% of each run, Pallas kernels for 6% -> 10%
where the time goes in v5:
time: 298 us; the launch traced here: 293 us
  waiting for transfers between devices  171 us (57%)
  starting transfers between devices  47.9 us (16%)
  Pallas kernels  34.8 us (12%)
  local copies, waits for them, and re-layouts  26.3 us (9%)
  other arithmetic  11.6 us (4%)
    ppermute x33, waiting for transfers between devices, swapped(): return lax.ppermute(value, axis, [(i, i ^ mask) for i in range(count)])  142 us
    ppermute x33, starting transfers between devices, swapped(): return lax.ppermute(value, axis, [(i, i ^ mask) for i in range(count)])  38 us
    ppermute x1, waiting for transfers between devices, per_device_one_head(): out_passed_next = lax.ppermute(out_across_next, 'ctx', outward)  27 us
    unnamed x72, local copies, waits for them, and re-layouts  20.5 us
    pallas_call x1, Pallas kernels, attend_head(): pl.pallas_call(attend_kernel, grid=(count,), out_shape=(out, out), in_spe...  14.9 us
    pallas_call x2, Pallas kernels, project(): pl.pallas_call(functools.partial(project_kernel, rows, first_col), out_sh...  13.1 us
  transfers between devices with their start and end apart: 37, of which 16 were waited for; matrix products, arithmetic and copies ran while one was open for 5% of the time, Pallas kernels for 10%

profile of v5, /device:TPU:17, one launch (start us, length us, event | category | flops | bytes accessed | tf_op | source)
XLA Modules:
  0.0 292.6 jit_solution(13429692283467610629)
XLA Ops:
  0.0 1.2 collective-permute-start.3
  1.2 2.2 constant_dynamic-slice_fusion.3
  3.4 1.3 constant_dynamic-slice_fusion.1
  4.7 0.9 pad_maximum_fusion.4
  5.7 1.3 collective-permute-start.5
  7.0 0.9 pad_maximum_fusion.8
  8.2 2.4 collective-permute-start.2
  10.5 2.6 collective-permute-done.3.refs_4_
  13.1 1.2 collective-permute-start.4
  15.1 1.4 shard_map.91
  18.7 1.2 pad_maximum_fusion.5.refs_9_
  19.9 1.2 pad_maximum_fusion.6
  21.1 1.2 pad_maximum_fusion.7
  22.2 3.0 %collective-permute-done.4.refs_6_ = bf16[256,1024]{1,0:T(8,128)(2,1)S(1)} collective-permute-done((bf16[256,1024]{1,0:T(8,128)(2,1)S(1)}, bf16[256,1024]{1,0:T(8,128)(2,1)S(1)}, u32[]{:S(2)}, u32[]{:S(2)}) %collective-permute-start.4) | collective-permute-done | bytes 524320 | tf_op jit(solution)/shard_map/ppermute | solution.py:572
  25.2 21.8 %collective-permute-done.refs_1_ = bf16[272,1024]{1,0:T(8,128)(2,1)S(1)} collective-permute-done((bf16[272,1024]{1,0:T(8,128)(2,1)}, bf16[272,1024]{1,0:T(8,128)(2,1)S(1)}, u32[]{:S(2)}, u32[]{:S(2)}) %collective-permute-start) | collective-permute-done | bytes 557088 | tf_op jit(solution)/shard_map/ppermute | solution.py:572
  49.5 1.2 collective-permute-start.9
  50.9 1.2 collective-permute-start.10
  52.1 14.1 %collective-permute-start.6 = (bf16[512,768]{1,0:T(8,128)(2,1)S(1)}, bf16[512,768]{1,0:T(8,128)(2,1)S(1)}, u32[]{:S(2)}, u32[]{:S(2)}) collective-permute-start(bf16[512,768]{1,0:T(8,128)(2,1)S(1)} %pad_maximum_fusion.6), channel_id=1, source_target_pairs={{0,16},{4,20},{8,24},{12,28},{16,0},{20,4},{24,8},{28,12},{1,17},{... | collective-permute-start | bytes 2359304 | tf_op jit(solution)/shard_map/ppermute | solution.py:572
  66.5 49.4 %collective-permute-done.6.refs_11_ = bf16[512,768]{1,0:T(8,128)(2,1)S(1)} collective-permute-done((bf16[512,768]{1,0:T(8,128)(2,1)S(1)}, bf16[512,768]{1,0:T(8,128)(2,1)S(1)}, u32[]{:S(2)}, u32[]{:S(2)}) %collective-permute-start.6) | collective-permute-done | bytes 786464 | tf_op jit(solution)/shard_map/ppermute | solution.py:572
  116.5 18.3 %collective-permute-done.7.refs_12_ = bf16[512,768]{1,0:T(8,128)(2,1)S(1)} collective-permute-done((bf16[512,768]{1,0:T(8,128)(2,1)S(1)}, bf16[512,768]{1,0:T(8,128)(2,1)S(1)}, u32[]{:S(2)}, u32[]{:S(2)}) %collective-permute-start.7) | collective-permute-done | bytes 786464 | tf_op jit(solution)/shard_map/ppermute | solution.py:572
  135.3 1.9 fusion.3
  138.2 1.3 collective-permute-start.17
  139.5 3.2 %collective-permute-start.18 = (bf16[1024,512]{1,0:T(8,128)(2,1)S(1)}, bf16[1024,512]{1,0:T(8,128)(2,1)}, u32[]{:S(2)}, u32[]{:S(2)}) collective-permute-start(bf16[1024,512]{1,0:T(8,128)(2,1)S(1)} %copy-done.4), channel_id=1, source_target_pairs={{8,16},{12,20},{16,8},{20,12},{9,17},{13,21},{17,9},{21,13},{10,18... | collective-permute-start | bytes 3145736 | tf_op jit(solution)/shard_map/ppermute | solution.py:631
  142.7 1.1 collective-permute-start.19
  143.8 6.3 %shard_map.92.refs_5_ = bf16[4,256,256]{2,1,0:T(8,128)(2,1)S(1)} custom-call(s32[9]{0:T(128)S(1)} %stack.75.place, bf16[256,1024]{1,0:T(8,128)(2,1)S(1)} %copy-done.1, bf16[272,1024]{1,0:T(8,128)(2,1)S(1)} %collective-permute-done.refs_1_, bf16[272,1024]{1,0:T(8,128)(2,1)S(1)} %collective-permute-done.1.refs_2_, ...), custom_call_target="tpu_custom_call" | custom-call | flops 2147483648 | bytes 16777216 | tf_op jit(solution)/shard_map/pallas_call | solution.py:267
  150.3 6.8 %shard_map.93 = (bf16[4,256,256]{2,1,0:T(8,128)(2,1)S(1)}, bf16[4,256,256]{2,1,0:T(8,128)(2,1)S(1)}) custom-call(s32[9]{0:T(128)S(1)} %stack.75.place, bf16[256,1024]{1,0:T(8,128)(2,1)S(1)} %copy-done.1, bf16[272,1024]{1,0:T(8,128)(2,1)S(1)} %collective-permute-done.refs_1_, bf16[272,1024]{1,0:T(8,128)(2,1)S(1)} %collective-permute-done.1.refs_2_, ...), custom_call_target="tpu_custom_call" | custom-call | flops 4294967296 | bytes 16777216 | tf_op jit(solution)/shard_map/pallas_call | solution.py:267
  157.9 5.1 %collective-permute-done.17.refs_2_ = bf16[1024,512]{1,0:T(8,128)(2,1)} collective-permute-done((bf16[1024,512]{1,0:T(8,128)(2,1)S(1)}, bf16[1024,512]{1,0:T(8,128)(2,1)}, u32[]{:S(2)}, u32[]{:S(2)}) %collective-permute-start.17) | collective-permute-done | bytes 1048608 | tf_op jit(solution)/shard_map/ppermute | solution.py:572
  163.0 2.5 collective-permute-done.18.refs_4_
  165.5 1.0 copy-done.6
  166.5 7.8 %collective-permute-done.15.refs_6_ = bf16[4,256,256]{2,1,0:T(8,128)(2,1)} collective-permute-done((bf16[4,256,256]{2,1,0:T(8,128)(2,1)S(1)}, bf16[4,256,256]{2,1,0:T(8,128)(2,1)}, u32[]{:S(2)}, u32[]{:S(2)}) %collective-permute-start.15) | collective-permute-done | bytes 524320 | tf_op jit(solution)/shard_map/ppermute | solution.py:572
  175.1 0.8 collective-permute-start.20
  175.9 3.0 %collective-permute-start.22 = (bf16[1024,512]{1,0:T(8,128)(2,1)}, bf16[1024,512]{1,0:T(8,128)(2,1)S(1)}, u32[]{:S(2)}, u32[]{:S(2)}) collective-permute-start(bf16[1024,512]{1,0:T(8,128)(2,1)} %collective-permute-done.17.refs_2_), channel_id=1, source_target_pairs={{8,16},{12,20},{16,8},{20,12},{9,17},{13,21},{17,9},{21,13},{10,18... | collective-permute-start | bytes 3145736 | tf_op jit(solution)/shard_map/ppermute | solution.py:645
  179.0 1.4 collective-permute-start.23
  180.9 0.8 copy-done.22
  182.1 3.6 %collective-permute-done.21.refs_8_ = bf16[4,256,256]{2,1,0:T(8,128)(2,1)} collective-permute-done((bf16[4,256,256]{2,1,0:T(8,128)(2,1)}, bf16[4,256,256]{2,1,0:T(8,128)(2,1)}, u32[]{:S(2)}, u32[]{:S(2)}) %collective-permute-start.21) | collective-permute-done | bytes 524320 | tf_op jit(solution)/shard_map/ppermute | solution.py:572
  185.7 1.0 copy-done.14
  186.7 1.0 copy-done.21
  187.8 1.0 copy-done.23
  188.8 1.0 copy-done.25
  189.8 1.0 copy-done.27
  190.8 0.9 copy-done.29
  191.7 1.0 copy-done.31
  192.8 14.9 %shard_map.94 = (bf16[4,256,512]{2,1,0:T(8,128)(2,1)S(1)}, bf16[4,256,512]{2,1,0:T(8,128)(2,1)}) custom-call(s32[9]{0:T(128)S(1)} %stack.75.place, f32[4]{0:T(128)S(1)} %dynamic-slice_bitcast_fusion.1.mix, bf16[4,256,256]{2,1,0:T(8,128)(2,1)S(1)} %copy-done.31, bf16[4,256,256]{2,1,0:T(8,128)(2,1)S(1)} %copy-done.23, bf16[256,768]{1,0:T(8,128)(2,1)S(1)} %copy-done.25, ...), custom_call_target="tpu_custom_call" | custom-call | flops 5368709120 | bytes 16777216 | tf_op jit(solution)/shard_map/pallas_call | solution.py:481
  207.7 1.0 copy-done.12
  208.7 1.0 copy-done.10
  210.0 2.3 collective-permute-start.30
  212.6 1.5 convert_add_fusion
  214.3 2.1 collective-permute-start.28
  217.0 1.1 collective-permute-start.32
  218.1 27.0 %collective-permute-done.30.refs_10_ = bf16[1024,512]{1,0:T(8,128)(2,1)} collective-permute-done((bf16[1024,512]{1,0:T(8,128)(2,1)S(1)}, bf16[1024,512]{1,0:T(8,128)(2,1)}, u32[]{:S(2)}, u32[]{:S(2)}) %collective-permute-start.30) | collective-permute-done | bytes 1048608 | tf_op jit(solution)/shard_map/ppermute | solution.py:655
  245.1 1.0 collective-permute-start.31
  246.2 4.6 %collective-permute-done.27.r1 = bf16[256,512]{1,0:T(8,128)(2,1)S(1)} collective-permute-done((bf16[256,512]{1,0:T(8,128)(2,1)S(1)}, bf16[256,512]{1,0:T(8,128)(2,1)S(1)}, u32[]{:S(2)}, u32[]{:S(2)}) %collective-permute-start.27) | collective-permute-done | bytes 262176 | tf_op jit(solution)/shard_map/ppermute | solution.py:572
  253.0 1.1 dynamic-slice_bitcast_fusion.own
  254.1 1.4 collective-permute-done.33.refs_11_
  255.5 1.2 copy-done.9
  256.7 1.2 copy-done.11
  258.0 0.9 copy-done.16
  258.9 0.9 copy-done.18
  259.9 5.5 %shard_map.95 = (bf16[256,1024]{1,0:T(8,128)(2,1)S(1)}, bf16[256,1024]{1,0:T(8,128)(2,1)S(1)}, bf16[256,1024]{1,0:T(8,128)(2,1)S(1)}, bf16[256,1024]{1,0:T(8,128)(2,1)S(1)}) custom-call(s32[10]{0:T(128)S(1)} %concatenate.47.place, f32[256,512]{1,0:T(8,128)S(1)} %dynamic-slice_bitcast_fusion.own, bf16[256,512]{1,0:T(8,128)(2,1)S(1)} %collective-permute-done.27.r1, ...), custom_call_target="tpu_custom_call" | custom-call | flops 2147483648 | bytes 11534336 | tf_op jit(solution)/shard_map/pallas_call | solution.py:553
  265.3 1.5 collective-permute-start.36
  267.0 1.0 collective-permute-start.34
  268.1 11.4 %collective-permute-done.36 = bf16[256,1024]{1,0:T(8,128)(2,1)S(1)} collective-permute-done((bf16[256,1024]{1,0:T(8,128)(2,1)S(1)}, bf16[256,1024]{1,0:T(8,128)(2,1)S(1)}, u32[]{:S(2)}, u32[]{:S(2)}) %collective-permute-start.36) | collective-permute-done | bytes 524320 | tf_op jit(solution)/shard_map/ppermute | solution.py:572
  279.5 11.9 %collective-permute-done.35 = bf16[256,1024]{1,0:T(8,128)(2,1)S(1)} collective-permute-done((bf16[256,1024]{1,0:T(8,128)(2,1)S(1)}, bf16[256,1024]{1,0:T(8,128)(2,1)S(1)}, u32[]{:S(2)}, u32[]{:S(2)}) %collective-permute-start.35) | collective-permute-done | bytes 524320 | tf_op jit(solution)/shard_map/ppermute | solution.py:572
  291.4 1.2 add_convert_fusion
  (123 shorter events, 14.7 us)
Async XLA Ops:
  0.0 182.1 %copy-start = (f32[8,4]{0,1:T(4,128)S(1)}, f32[8,4]{0,1:T(4,128)}, u32[]{:S(2)}) copy-start(f32[8,4]{0,1:T(4,128)} %param.15) | copy-start | bytes 388
  0.0 3.4 %copy-start.33 = (bf16[512,1024]{1,0:T(8,128)(2,1)S(1)}, bf16[512,1024]{1,0:T(8,128)(2,1)}, u32[]{:S(2)}) copy-start(bf16[512,1024]{1,0:T(8,128)(2,1)} %param.13) | copy-start | bytes 3145732
  0.0 13.1 %collective-permute-start.3 = (bf16[256,1024]{1,0:T(8,128)(2,1)}, bf16[256,1024]{1,0:T(8,128)(2,1)S(1)}, u32[]{:S(2)}, u32[]{:S(2)}) collective-permute-start(bf16[256,1024]{1,0:T(8,128)(2,1)} %refs_0_.3), channel_id=1, source_target_pairs={{0,1},{1,0},{2,3},{3,2},{4,5},{5,4},{6,7},{7,6},{8,9},{9,8},{10,11... | collective-permute-start | bytes 1572872 | tf_op jit(solution)/shard_map/ppermute | solution.py:572
  1.2 2.2 copy-start.34
  3.4 3.5 %copy-start.35 = (s32[256]{0:T(256)S(1)}, s32[256]{0:T(256)}, u32[]{:S(2)}) copy-start(s32[256]{0:T(256)} %param.10) | copy-start | bytes 3076
  4.7 2.3 copy-start.1
  5.7 42.1 %collective-permute-start.5 = (bf16[512,768]{1,0:T(8,128)(2,1)}, bf16[512,768]{1,0:T(8,128)(2,1)}, u32[]{:S(2)}, u32[]{:S(2)}) collective-permute-start(bf16[512,768]{1,0:T(8,128)(2,1)} %pad_maximum_fusion.4), channel_id=1, source_target_pairs={{0,8},{4,12},{8,0},{12,4},{16,24},{20,28},{24,16},{28,20},{1,9},{5... | collective-permute-start | bytes 2359304 | tf_op jit(solution)/shard_map/ppermute | solution.py:572
  7.9 39.2 %collective-permute-start = (bf16[272,1024]{1,0:T(8,128)(2,1)}, bf16[272,1024]{1,0:T(8,128)(2,1)S(1)}, u32[]{:S(2)}, u32[]{:S(2)}) collective-permute-start(bf16[272,1024]{1,0:T(8,128)(2,1)} %pad_maximum_fusion.8), channel_id=1, source_target_pairs={{0,8},{4,12},{8,0},{12,4},{16,24},{20,28},{24,16},{28,20},{1,9},{5... | collective-permute-start | bytes 1671176 | tf_op jit(solution)/shard_map/ppermute | solution.py:572
  8.1 39.6 %collective-permute-start.1 = (bf16[272,1024]{1,0:T(8,128)(2,1)}, bf16[272,1024]{1,0:T(8,128)(2,1)S(1)}, u32[]{:S(2)}, u32[]{:S(2)}) collective-permute-start(bf16[272,1024]{1,0:T(8,128)(2,1)} %pad_maximum_fusion.8), channel_id=1, source_target_pairs={{0,16},{4,20},{8,24},{12,28},{16,0},{20,4},{24,8},{28,12},{1,17},{... | collective-permute-start | bytes 1671176 | tf_op jit(solution)/shard_map/ppermute | solution.py:572
  8.2 39.6 %collective-permute-start.2 = (bf16[272,1024]{1,0:T(8,128)(2,1)}, bf16[272,1024]{1,0:T(8,128)(2,1)S(1)}, u32[]{:S(2)}, u32[]{:S(2)}) collective-permute-start(bf16[272,1024]{1,0:T(8,128)(2,1)} %pad_maximum_fusion.8), channel_id=1, source_target_pairs={{0,24},{4,28},{8,16},{12,20},{16,8},{20,12},{24,0},{28,4},{1,25},{... | collective-permute-start | bytes 1671176 | tf_op jit(solution)/shard_map/ppermute | solution.py:572
  13.1 34.6 %copy-start.2 = (bf16[256,1024]{1,0:T(8,128)(2,1)}, bf16[256,1024]{1,0:T(8,128)(2,1)S(1)}, u32[]{:S(2)}) copy-start(bf16[256,1024]{1,0:T(8,128)(2,1)S(1)} %collective-permute-done.3.refs_4_) | copy-start | bytes 1572868
  13.1 12.1 %collective-permute-start.4 = (bf16[256,1024]{1,0:T(8,128)(2,1)S(1)}, bf16[256,1024]{1,0:T(8,128)(2,1)S(1)}, u32[]{:S(2)}, u32[]{:S(2)}) collective-permute-start(bf16[256,1024]{1,0:T(8,128)(2,1)S(1)} %copy-done.1), channel_id=1, source_target_pairs={{0,2},{1,3},{2,0},{3,1},{4,6},{5,7},{6,4},{7,5},{8,10},{9,11},{10,... | collective-permute-start | bytes 1572872 | tf_op jit(solution)/shard_map/ppermute | solution.py:572
  47.7 1.0 slice-start
  49.2 88.4 %collective-permute-start.8 = (bf16[896,1024]{1,0:T(8,128)(2,1)S(1)}, bf16[896,1024]{1,0:T(8,128)(2,1)S(1)}, u32[]{:S(2)}, u32[]{:S(2)}) collective-permute-start(bf16[896,1024]{1,0:T(8,128)(2,1)S(1)} %get-tuple-element.113), channel_id=1, source_target_pairs={{0,1},{1,0},{2,3},{3,2},{4,5},{5,4},{6,7},{7,6},{8,9},{9,8},{10,11... | collective-permute-start | bytes 5505032 | tf_op jit(solution)/shard_map/ppermute | solution.py:572
  49.5 88.1 %collective-permute-start.9 = (bf16[896,1024]{1,0:T(8,128)(2,1)S(1)}, bf16[896,1024]{1,0:T(8,128)(2,1)S(1)}, u32[]{:S(2)}, u32[]{:S(2)}) collective-permute-start(bf16[896,1024]{1,0:T(8,128)(2,1)S(1)} %get-tuple-element.112), channel_id=1, source_target_pairs={{0,2},{1,3},{2,0},{3,1},{4,6},{5,7},{6,4},{7,5},{8,10},{9,11},{10,... | collective-permute-start | bytes 5505032 | tf_op jit(solution)/shard_map/ppermute | solution.py:572
  50.9 86.7 %collective-permute-start.10 = (bf16[768,1024]{1,0:T(8,128)(2,1)S(1)}, bf16[768,1024]{1,0:T(8,128)(2,1)S(1)}, u32[]{:S(2)}, u32[]{:S(2)}) collective-permute-start(bf16[768,1024]{1,0:T(8,128)(2,1)S(1)} %pad_maximum_fusion.3), channel_id=1, source_target_pairs={{0,3},{1,2},{2,1},{3,0},{4,7},{5,6},{6,5},{7,4},{8,11},{9,10},{10,... | collective-permute-start | bytes 4718600 | tf_op jit(solution)/shard_map/ppermute | solution.py:572
  52.1 63.8 %collective-permute-start.6 = (bf16[512,768]{1,0:T(8,128)(2,1)S(1)}, bf16[512,768]{1,0:T(8,128)(2,1)S(1)}, u32[]{:S(2)}, u32[]{:S(2)}) collective-permute-start(bf16[512,768]{1,0:T(8,128)(2,1)S(1)} %pad_maximum_fusion.6), channel_id=1, source_target_pairs={{0,16},{4,20},{8,24},{12,28},{16,0},{20,4},{24,8},{28,12},{1,17},{... | collective-permute-start | bytes 2359304 | tf_op jit(solution)/shard_map/ppermute | solution.py:572
  66.2 68.6 %collective-permute-start.7 = (bf16[512,768]{1,0:T(8,128)(2,1)S(1)}, bf16[512,768]{1,0:T(8,128)(2,1)S(1)}, u32[]{:S(2)}, u32[]{:S(2)}) collective-permute-start(bf16[512,768]{1,0:T(8,128)(2,1)S(1)} %pad_maximum_fusion.7), channel_id=1, source_target_pairs={{0,24},{4,28},{8,16},{12,20},{16,8},{20,12},{24,0},{28,4},{1,25},{... | collective-permute-start | bytes 2359304 | tf_op jit(solution)/shard_map/ppermute | solution.py:572
  66.4 71.8 %copy-start.4 = (bf16[1024,512]{1,0:T(8,128)(2,1)S(1)}, bf16[1024,512]{1,0:T(8,128)(2,1)}, u32[]{:S(2)}) copy-start(bf16[1024,512]{1,0:T(8,128)(2,1)} %refs_0_.4) | copy-start | bytes 3145732
  66.5 77.4 %copy-start.3 = (bf16[256,1024]{1,0:T(8,128)(2,1)S(1)}, bf16[256,1024]{1,0:T(8,128)(2,1)}, u32[]{:S(2)}) copy-start(bf16[256,1024]{1,0:T(8,128)(2,1)} %copy-done.2) | copy-start | bytes 1572868
  115.9 23.6 %collective-permute-start.11 = (bf16[512,768]{1,0:T(8,128)(2,1)S(1)}, bf16[512,768]{1,0:T(8,128)(2,1)S(1)}, u32[]{:S(2)}, u32[]{:S(2)}) collective-permute-start(bf16[512,768]{1,0:T(8,128)(2,1)S(1)} %pad_maximum_fusion.5.refs_9_), channel_id=1, source_target_pairs={{0,4},{4,0},{8,12},{12,8},{16,20},{20,16},{24,28},{28,24},{1,5},{5... | collective-permute-start | bytes 2359304 | tf_op jit(solution)/shard_map/ppermute | solution.py:572
  134.8 8.0 %collective-permute-start.12 = (bf16[512,768]{1,0:T(8,128)(2,1)}, bf16[512,768]{1,0:T(8,128)(2,1)S(1)}, u32[]{:S(2)}, u32[]{:S(2)}) collective-permute-start(bf16[512,768]{1,0:T(8,128)(2,1)} %collective-permute-done.5.refs_10_), channel_id=1, source_target_pairs={{0,4},{4,0},{8,12},{12,8},{16,20},{20,16},{24,28},{28,24},{1,5},{5... | collective-permute-start | bytes 2359304 | tf_op jit(solution)/shard_map/ppermute | solution.py:572
  137.6 6.2 %collective-permute-start.13 = (bf16[512,768]{1,0:T(8,128)(2,1)S(1)}, bf16[512,768]{1,0:T(8,128)(2,1)S(1)}, u32[]{:S(2)}, u32[]{:S(2)}) collective-permute-start(bf16[512,768]{1,0:T(8,128)(2,1)S(1)} %collective-permute-done.6.refs_11_), channel_id=1, source_target_pairs={{0,4},{4,0},{8,12},{12,8},{16,20},{20,16},{24,28},{28,24},{1,5},{5... | collective-permute-start | bytes 2359304 | tf_op jit(solution)/shard_map/ppermute | solution.py:572
  137.7 6.1 %collective-permute-start.14 = (bf16[512,768]{1,0:T(8,128)(2,1)S(1)}, bf16[512,768]{1,0:T(8,128)(2,1)S(1)}, u32[]{:S(2)}, u32[]{:S(2)}) collective-permute-start(bf16[512,768]{1,0:T(8,128)(2,1)S(1)} %collective-permute-done.7.refs_12_), channel_id=1, source_target_pairs={{0,4},{4,0},{8,12},{12,8},{16,20},{20,16},{24,28},{28,24},{1,5},{5... | collective-permute-start | bytes 2359304 | tf_op jit(solution)/shard_map/ppermute | solution.py:572
  138.2 24.8 %collective-permute-start.17 = (bf16[1024,512]{1,0:T(8,128)(2,1)S(1)}, bf16[1024,512]{1,0:T(8,128)(2,1)}, u32[]{:S(2)}, u32[]{:S(2)}) collective-permute-start(bf16[1024,512]{1,0:T(8,128)(2,1)S(1)} %copy-done.4), channel_id=1, source_target_pairs={{0,8},{4,12},{8,0},{12,4},{16,24},{20,28},{24,16},{28,20},{1,9},{5... | collective-permute-start | bytes 3145736 | tf_op jit(solution)/shard_map/ppermute | solution.py:572
  139.5 26.0 %collective-permute-start.18 = (bf16[1024,512]{1,0:T(8,128)(2,1)S(1)}, bf16[1024,512]{1,0:T(8,128)(2,1)}, u32[]{:S(2)}, u32[]{:S(2)}) collective-permute-start(bf16[1024,512]{1,0:T(8,128)(2,1)S(1)} %copy-done.4), channel_id=1, source_target_pairs={{8,16},{12,20},{16,8},{20,12},{9,17},{13,21},{17,9},{21,13},{10,18... | collective-permute-start | bytes 3145736 | tf_op jit(solution)/shard_map/ppermute | solution.py:631
  142.7 22.8 %collective-permute-start.19 = (bf16[1024,512]{1,0:T(8,128)(2,1)S(1)}, bf16[1024,512]{1,0:T(8,128)(2,1)S(1)}, u32[]{:S(2)}, u32[]{:S(2)}) collective-permute-start(bf16[1024,512]{1,0:T(8,128)(2,1)S(1)} %copy-done.4), channel_id=1, source_target_pairs={{0,4},{4,0},{8,12},{12,8},{16,20},{20,16},{24,28},{28,24},{1,5},{5... | collective-permute-start | bytes 3145736 | tf_op jit(solution)/shard_map/ppermute | solution.py:572
  150.1 7.0 %copy-start.13 = (bf16[4,256,256]{2,1,0:T(8,128)(2,1)}, bf16[4,256,256]{2,1,0:T(8,128)(2,1)S(1)}, u32[]{:S(2)}) copy-start(bf16[4,256,256]{2,1,0:T(8,128)(2,1)S(1)} %shard_map.92.refs_5_) | copy-start | bytes 1572868
  150.1 24.2 %collective-permute-start.15 = (bf16[4,256,256]{2,1,0:T(8,128)(2,1)S(1)}, bf16[4,256,256]{2,1,0:T(8,128)(2,1)}, u32[]{:S(2)}, u32[]{:S(2)}) collective-permute-start(bf16[4,256,256]{2,1,0:T(8,128)(2,1)S(1)} %shard_map.92.refs_5_), channel_id=1, source_target_pairs={{0,8},{4,12},{8,0},{12,4},{16,24},{20,28},{24,16},{28,20},{1,9},{5... | collective-permute-start | bytes 1572872 | tf_op jit(solution)/shard_map/ppermute | solution.py:572
  150.2 24.1 %collective-permute-start.16 = (bf16[4,256,256]{2,1,0:T(8,128)(2,1)S(1)}, bf16[4,256,256]{2,1,0:T(8,128)(2,1)S(1)}, u32[]{:S(2)}, u32[]{:S(2)}) collective-permute-start(bf16[4,256,256]{2,1,0:T(8,128)(2,1)S(1)} %shard_map.92.refs_5_), channel_id=1, source_target_pairs={{0,4},{4,0},{8,12},{12,8},{16,20},{20,16},{24,28},{28,24},{1,5},{5... | collective-permute-start | bytes 1572872 | tf_op jit(solution)/shard_map/ppermute | solution.py:572
  165.5 1.0 copy-start.6
  175.1 5.8 %collective-permute-start.20 = (bf16[4,256,256]{2,1,0:T(8,128)(2,1)S(1)}, bf16[4,256,256]{2,1,0:T(8,128)(2,1)S(1)}, u32[]{:S(2)}, u32[]{:S(2)}) collective-permute-start(bf16[4,256,256]{2,1,0:T(8,128)(2,1)S(1)} %get-tuple-element.83), channel_id=1, source_target_pairs={{0,4},{4,0},{8,12},{12,8},{16,20},{20,16},{24,28},{28,24},{1,5},{5... | collective-permute-start | bytes 1572872 | tf_op jit(solution)/shard_map/ppermute | solution.py:572
  175.9 32.7 %collective-permute-start.22 = (bf16[1024,512]{1,0:T(8,128)(2,1)}, bf16[1024,512]{1,0:T(8,128)(2,1)S(1)}, u32[]{:S(2)}, u32[]{:S(2)}) collective-permute-start(bf16[1024,512]{1,0:T(8,128)(2,1)} %collective-permute-done.17.refs_2_), channel_id=1, source_target_pairs={{8,16},{12,20},{16,8},{20,12},{9,17},{13,21},{17,9},{21,13},{10,18... | collective-permute-start | bytes 3145736 | tf_op jit(solution)/shard_map/ppermute | solution.py:645
  179.0 29.7 %collective-permute-start.23 = (bf16[1024,512]{1,0:T(8,128)(2,1)}, bf16[1024,512]{1,0:T(8,128)(2,1)S(1)}, u32[]{:S(2)}, u32[]{:S(2)}) collective-permute-start(bf16[1024,512]{1,0:T(8,128)(2,1)} %collective-permute-done.18.refs_4_), channel_id=1, source_target_pairs={{8,0},{12,4},{16,24},{20,28},{9,1},{13,5},{17,25},{21,29},{10,2},{... | collective-permute-start | bytes 3145736 | tf_op jit(solution)/shard_map/ppermute | solution.py:646
  180.4 28.3 %collective-permute-start.24 = (bf16[1024,512]{1,0:T(8,128)(2,1)}, bf16[1024,512]{1,0:T(8,128)(2,1)S(1)}, u32[]{:S(2)}, u32[]{:S(2)}) collective-permute-start(bf16[1024,512]{1,0:T(8,128)(2,1)} %collective-permute-done.17.refs_2_), channel_id=1, source_target_pairs={{0,4},{4,0},{8,12},{12,8},{16,20},{20,16},{24,28},{28,24},{1,5},{5... | collective-permute-start | bytes 3145736 | tf_op jit(solution)/shard_map/ppermute | solution.py:572
  180.7 29.0 %collective-permute-start.25 = (bf16[1024,512]{1,0:T(8,128)(2,1)}, bf16[1024,512]{1,0:T(8,128)(2,1)}, u32[]{:S(2)}, u32[]{:S(2)}) collective-permute-start(bf16[1024,512]{1,0:T(8,128)(2,1)} %collective-permute-done.18.refs_4_), channel_id=1, source_target_pairs={{0,4},{4,0},{8,12},{12,8},{16,20},{20,16},{24,28},{28,24},{1,5},{5... | collective-permute-start | bytes 3145736 | tf_op jit(solution)/shard_map/ppermute | solution.py:572
  181.8 3.9 %collective-permute-start.21 = (bf16[4,256,256]{2,1,0:T(8,128)(2,1)}, bf16[4,256,256]{2,1,0:T(8,128)(2,1)}, u32[]{:S(2)}, u32[]{:S(2)}) collective-permute-start(bf16[4,256,256]{2,1,0:T(8,128)(2,1)} %collective-permute-done.15.refs_6_), channel_id=1, source_target_pairs={{0,4},{4,0},{8,12},{12,8},{16,20},{20,16},{24,28},{28,24},{1,5},{5... | collective-permute-start | bytes 1572872 | tf_op jit(solution)/shard_map/ppermute | solution.py:572
  185.7 1.0 copy-start.14
  186.7 1.0 copy-start.21
  187.8 1.0 copy-start.23
  188.8 1.0 copy-start.25
  189.8 1.0 copy-start.27
  191.7 1.0 copy-start.31
  207.7 1.0 copy-start.12
  208.7 3.9 %copy-start.8 = (bf16[1024,512]{1,0:T(8,128)(2,1)}, bf16[1024,512]{1,0:T(8,128)(2,1)S(1)}, u32[]{:S(2)}) copy-start(bf16[1024,512]{1,0:T(8,128)(2,1)S(1)} %collective-permute-done.23.refs_6_) | copy-start | bytes 3145732
  208.7 1.0 copy-start.10
  209.7 2.9 collective-permute-start.26
  210.0 35.2 %collective-permute-start.30 = (bf16[1024,512]{1,0:T(8,128)(2,1)S(1)}, bf16[1024,512]{1,0:T(8,128)(2,1)}, u32[]{:S(2)}, u32[]{:S(2)}) collective-permute-start(bf16[1024,512]{1,0:T(8,128)(2,1)S(1)} %collective-permute-done.22.refs_8_), channel_id=1, source_target_pairs={{8,0},{12,4},{16,24},{20,28},{9,1},{13,5},{17,25},{21,29},{10,2},{... | collective-permute-start | bytes 3145736 | tf_op jit(solution)/shard_map/ppermute | solution.py:655
  214.1 37.4 %copy-start.32 = (f32[4,256,512]{2,1,0:T(8,128)}, f32[4,256,512]{2,1,0:T(8,128)S(1)}, u32[]{:S(2)}) copy-start(f32[4,256,512]{2,1,0:T(8,128)S(1)} %convert_add_fusion) | copy-start | bytes 6291460
  214.1 41.4 %copy-start.5 = (bf16[1024,512]{1,0:T(8,128)(2,1)S(1)}, bf16[1024,512]{1,0:T(8,128)(2,1)}, u32[]{:S(2)}) copy-start(bf16[1024,512]{1,0:T(8,128)(2,1)} %refs_0_.4) | copy-start | bytes 3145732
  214.1 41.4 %copy-start.7 = (bf16[1024,512]{1,0:T(8,128)(2,1)S(1)}, bf16[1024,512]{1,0:T(8,128)(2,1)}, u32[]{:S(2)}) copy-start(bf16[1024,512]{1,0:T(8,128)(2,1)} %copy-done.6) | copy-start | bytes 3145732
  214.1 41.4 %copy-start.19 = (f32[1024]{0:T(1024)S(1)}, f32[1024]{0:T(1024)}, u32[]{:S(2)}) copy-start(f32[1024]{0:T(1024)} %param.16) | copy-start | bytes 12292
  214.2 36.5 %collective-permute-start.27 = (bf16[256,512]{1,0:T(8,128)(2,1)S(1)}, bf16[256,512]{1,0:T(8,128)(2,1)S(1)}, u32[]{:S(2)}, u32[]{:S(2)}) collective-permute-start(bf16[256,512]{1,0:T(8,128)(2,1)S(1)} %get-tuple-element.111), channel_id=1, source_target_pairs={{0,8},{4,12},{8,0},{12,4},{16,24},{20,28},{24,16},{28,20},{1,9},{5... | collective-permute-start | bytes 786440 | tf_op jit(solution)/shard_map/ppermute | solution.py:572
  214.3 36.4 %collective-permute-start.28 = (bf16[256,512]{1,0:T(8,128)(2,1)S(1)}, bf16[256,512]{1,0:T(8,128)(2,1)S(1)}, u32[]{:S(2)}, u32[]{:S(2)}) collective-permute-start(bf16[256,512]{1,0:T(8,128)(2,1)S(1)} %get-tuple-element.110), channel_id=1, source_target_pairs={{0,16},{4,20},{8,24},{12,28},{16,0},{20,4},{24,8},{28,12},{1,17},{... | collective-permute-start | bytes 786440 | tf_op jit(solution)/shard_map/ppermute | solution.py:572
  216.4 35.1 %collective-permute-start.29 = (bf16[256,512]{1,0:T(8,128)(2,1)S(1)}, bf16[256,512]{1,0:T(8,128)(2,1)S(1)}, u32[]{:S(2)}, u32[]{:S(2)}) collective-permute-start(bf16[256,512]{1,0:T(8,128)(2,1)S(1)} %get-tuple-element.109), channel_id=1, source_target_pairs={{0,24},{4,28},{8,16},{12,20},{16,8},{20,12},{24,0},{28,4},{1,25},{... | collective-permute-start | bytes 786440 | tf_op jit(solution)/shard_map/ppermute | solution.py:572
  217.0 37.1 %collective-permute-start.32 = (bf16[1024,512]{1,0:T(8,128)(2,1)S(1)}, bf16[1024,512]{1,0:T(8,128)(2,1)}, u32[]{:S(2)}, u32[]{:S(2)}) collective-permute-start(bf16[1024,512]{1,0:T(8,128)(2,1)S(1)} %collective-permute-done.22.refs_8_), channel_id=1, source_target_pairs={{0,4},{4,0},{8,12},{12,8},{16,20},{20,16},{24,28},{28,24},{1,5},{5... | collective-permute-start | bytes 3145736 | tf_op jit(solution)/shard_map/ppermute | solution.py:572
  245.1 8.9 %collective-permute-start.31 = (bf16[1024,512]{1,0:T(8,128)(2,1)}, bf16[1024,512]{1,0:T(8,128)(2,1)}, u32[]{:S(2)}, u32[]{:S(2)}) collective-permute-start(bf16[1024,512]{1,0:T(8,128)(2,1)} %copy-done.8), channel_id=1, source_target_pairs={{0,4},{4,0},{8,12},{12,8},{16,20},{20,16},{24,28},{28,24},{1,5},{5... | collective-permute-start | bytes 3145736 | tf_op jit(solution)/shard_map/ppermute | solution.py:572
  252.2 3.3 %collective-permute-start.33 = (bf16[1024,512]{1,0:T(8,128)(2,1)}, bf16[1024,512]{1,0:T(8,128)(2,1)}, u32[]{:S(2)}, u32[]{:S(2)}) collective-permute-start(bf16[1024,512]{1,0:T(8,128)(2,1)} %collective-permute-done.30.refs_10_), channel_id=1, source_target_pairs={{0,4},{4,0},{8,12},{12,8},{16,20},{20,16},{24,28},{28,24},{1,5},{5... | collective-permute-start | bytes 3145736 | tf_op jit(solution)/shard_map/ppermute | solution.py:572
  255.5 1.2 copy-start.9
  256.7 1.2 copy-start.11
  258.0 0.9 copy-start.16
  265.3 14.1 %collective-permute-start.36 = (bf16[256,1024]{1,0:T(8,128)(2,1)S(1)}, bf16[256,1024]{1,0:T(8,128)(2,1)S(1)}, u32[]{:S(2)}, u32[]{:S(2)}) collective-permute-start(bf16[256,1024]{1,0:T(8,128)(2,1)S(1)} %get-tuple-element.108), channel_id=1, source_target_pairs={{0,3},{1,2},{2,1},{3,0},{4,7},{5,6},{6,5},{7,4},{8,11},{9,10},{10,... | collective-permute-start | bytes 1572872 | tf_op jit(solution)/shard_map/ppermute | solution.py:572
  266.8 24.6 %collective-permute-start.35 = (bf16[256,1024]{1,0:T(8,128)(2,1)S(1)}, bf16[256,1024]{1,0:T(8,128)(2,1)S(1)}, u32[]{:S(2)}, u32[]{:S(2)}) collective-permute-start(bf16[256,1024]{1,0:T(8,128)(2,1)S(1)} %get-tuple-element.107), channel_id=1, source_target_pairs={{0,2},{1,3},{2,0},{3,1},{4,6},{5,7},{6,4},{7,5},{8,10},{9,11},{10,... | collective-permute-start | bytes 1572872 | tf_op jit(solution)/shard_map/ppermute | solution.py:572
  267.0 24.4 %collective-permute-start.34 = (bf16[256,1024]{1,0:T(8,128)(2,1)S(1)}, bf16[256,1024]{1,0:T(8,128)(2,1)S(1)}, u32[]{:S(2)}, u32[]{:S(2)}) collective-permute-start(bf16[256,1024]{1,0:T(8,128)(2,1)S(1)} %get-tuple-element.106), channel_id=1, source_target_pairs={{0,1},{1,0},{2,3},{3,2},{4,5},{5,4},{6,7},{7,6},{8,9},{9,8},{10,11... | collective-permute-start | bytes 1572872 | tf_op jit(solution)/shard_map/ppermute | solution.py:572
  (10 other events, 8.0 us)

commit v6 on v5

--- a/solution.py
+++ b/solution.py
@@ -193,10 +193,10 @@
 
 def project_kernel(rows, first_col, place, *refs):
     a_own, (x0, x_rest, y0, y_rest, d_rest) = refs[:4], refs[4:9]
-    w_same, w_swap = refs[9:13], refs[13:17]
+    w_same, w_swap = refs[9:11]
     abuf, wbuf, acc, sem_a, sem_w = refs[-5:]
-    turn, core = place[4], place[1]
-    half = w_same[0].shape[0]
+    turn, core = place[0], place[1]
+    half = w_same.shape[1]
     width = wbuf.shape[2]
 
     def copies_a(t):
@@ -215,35 +215,28 @@
             for n, (ref, source, target, size) in enumerate(pairs)
         ]
 
-    def copies_w(t, s):
+    def copies_w(t):
         out = []
-        for n, (ref, side) in enumerate(((w_same[s], core), (w_swap[s], 1 - core))):
-            source = ref.at[:, pl.ds(first_col, width)]
+        for n, (ref, side) in enumerate(((w_same, core), (w_swap, 1 - core))):
+            source = ref.at[lax.bitwise_xor(turn, t), :, pl.ds(first_col, width)]
             target = wbuf.at[t, pl.ds(pl.multiple_of(side * half, half), half)]
             out.append(pltpu.make_async_copy(source, target, sem_w.at[t, n]))
         return out
 
     for t in range(4):
-        for s in range(4):
-
-            @pl.when(s == lax.bitwise_xor(turn, t))
-            def _():
-                for copy in copies_w(t, s):
-                    copy.start()
-
-        for copy in copies_a(t):
+        for copy in copies_w(t) + copies_a(t):
             copy.start()
     for t in range(4):
-        for copy in copies_w(t, 0) + copies_a(t):
+        for copy in copies_w(t) + copies_a(t):
             copy.wait()
         part = jnp.dot(abuf[t], wbuf[t], preferred_element_type=jnp.float32)
         acc[...] = part if t == 0 else acc[...] + part
     if first_col:
-        v_out = refs[17]
+        v_out = refs[11]
         for b in range(4):
             v_out[place[5 + b]] = acc[b * rows : (b + 1) * rows].astype(jnp.bfloat16)
         return
-    cos_ref, sin_ref, mine, theirs = refs[17:21]
+    cos_ref, sin_ref, mine, theirs = refs[11:15]
     first = core == 0
     for b in range(4):
         total = acc[b * rows : (b + 1) * rows]
@@ -268,7 +261,7 @@
         functools.partial(project_kernel, rows, first_col),
         out_shape=[out] * count,
         in_specs=[whole(pltpu.SMEM)]
-        + [whole(pl.ANY)] * 17
+        + [whole(pl.ANY)] * 11
         + [whole(pltpu.VMEM)] * len(angles),
         out_specs=[whole(pltpu.VMEM)] * count,
         scratch_shapes=[
@@ -282,7 +275,7 @@
         cost_estimate=pl.CostEstimate(
             flops=8 * rows * 4 * depth * width, bytes_accessed=16 * 2**20, transcendentals=0
         ),
-    )(place, *a_own, *a_plane, *w_same, *w_swap, *angles)
+    )(place, *a_own, *a_plane, w_same, w_swap, *angles)
 
 
 def prepare(core, mine, other, key_ref, even_ref, odd_ref, q_out, k_out, corr, *scratch):
@@ -385,21 +378,37 @@
 
 
 def attend_kernel(place, mix, *refs):
-    qk_refs, (va, vb, vc, vd), (mine, theirs) = refs[:5], refs[5:9], refs[9:11]
+    qk_refs, table_refs, (va, vb, vc, vd), (mine, theirs) = refs[:2], refs[2:5], refs[5:9], refs[9:11]
     v_all, q_wide, k_ref, corr = refs[11:15]
+    tables, sem_v, sem_t = refs[19:22], refs[22], refs[23]
     side, core = place[2], place[1]
     b = pl.program_id(0)
     count = k_ref.shape[1] // (2 * ROWS)
 
     @pl.when(b == 0)
     def _():
-        prepare(core, *qk_refs, q_wide, k_ref, corr, *refs[15:])
-        for i in range(count):
-            for parity, near, far in ((core, va, vb), (1 - core, vc, vd)):
-                rows = pl.ds(pl.multiple_of((2 * i + parity) * ROWS, ROWS), ROWS)
-                first, last = near[i], far[i]
-                v_all[rows, : 2 * HD] = jnp.where(side == 0, first, last)
-                v_all[rows, 2 * HD :] = jnp.where(side == 0, last, first)
+        def copies_v():
+            out = []
+            for n, ref in enumerate((va, vb, vc, vd)):
+                parity = core if n < 2 else 1 - core
+                start = pl.multiple_of((side if n % 2 == 0 else 1 - side) * 2 * HD, 2 * HD)
+                for i in range(count):
+                    rows = pl.ds(pl.multiple_of((2 * i + parity) * ROWS, ROWS), ROWS)
+                    target = v_all.at[rows, pl.ds(start, 2 * HD)]
+                    out.append(pltpu.make_async_copy(ref.at[i], target, sem_v.at[n, i]))
+            return out
+
+        loads = [
+            pltpu.make_async_copy(ref, table, sem_t.at[n])
+            for n, (ref, table) in enumerate(zip(table_refs, tables))
+        ]
+        for copy in loads + copies_v():
+            copy.start()
+        for copy in loads:
+            copy.wait()
+        prepare(core, *qk_refs, *tables, q_wide, k_ref, corr, *refs[15:19])
+        for copy in copies_v():
+            copy.wait()
 
     row = lax.broadcasted_iota(jnp.int32, (ROWS, ROWS), 0)
     col = lax.broadcasted_iota(jnp.int32, (ROWS, ROWS), 1)
@@ -482,7 +491,7 @@
         attend_kernel,
         grid=(count,),
         out_shape=(out, out),
-        in_specs=[whole(pltpu.SMEM)] * 2 + [whole(pltpu.VMEM)] * 9,
+        in_specs=[whole(pltpu.SMEM)] * 2 + [whole(pltpu.VMEM)] * 2 + [whole(pl.ANY)] * 7,
         out_specs=[out_spec, out_spec],
         scratch_shapes=[
             pltpu.VMEM((total, GROUP * HD), jnp.bfloat16),
@@ -493,7 +502,9 @@
             pltpu.VMEM((AHEAD + total + LANES, HD), jnp.float32),
             pltpu.VMEM((2, total // 2, CQ * LANES), jnp.bfloat16),
             pltpu.VMEM((total, 2 * LANES), jnp.bfloat16),
-        ],
+        ]
+        + [pltpu.VMEM(table.shape, table.dtype) for table in tables]
+        + [pltpu.SemaphoreType.DMA((4, count)), pltpu.SemaphoreType.DMA((3,))],
         compiler_params=kernel_params(36),
         cost_estimate=pl.CostEstimate(
             flops=total * total * (depth + GROUP * HD),
@@ -560,7 +571,7 @@
             pltpu.VMEM((4, depth, 2 * width), jnp.bfloat16),
             pltpu.SemaphoreType.DMA((8,)),
         ],
-        compiler_params=kernel_params(14),
+        compiler_params=kernel_params(56),
         cost_estimate=pl.CostEstimate(
             flops=2 * rows * depth * 8 * width, bytes_accessed=11 * 2**20, transcendentals=0
         ),
@@ -591,19 +602,19 @@
     digits = jnp.stack([positions // 256, positions % 256]).astype(jnp.bfloat16)
     digits = jnp.pad(digits, ((0, 14), (0, activations.shape[1] - rows)))
     block = jnp.concatenate([activations, digits])
-    w_pieces = [columns(z ^ s) for s in range(4)]
+    w_pieces = jnp.stack([columns(target) for target in range(4)])
     far = [swapped(block, "ctx", 2 * s) for s in (1, 2, 3)]
     x0, y0 = swapped(activations, "head", 1), swapped(activations, "head", 2)
-    w_near = swapped(w_pieces[1], "ctx", 2)
     weights = lax.dynamic_index_in_dim(conv_kernel, ctx, 0, keepdims=False)
     tables = tables_of(weights * (math.log2(math.e) / math.sqrt(HD)))
-    place = jnp.stack([head, core, z % 2, z // 2, z ^ head, z, z ^ 1, z ^ 2, z ^ 3])
+    place = jnp.stack([head, core, z % 2, z // 2, head, z, z ^ 1, z ^ 2, z ^ 3])
     place = place.astype(jnp.int32)
-    far, x0, y0, w_near, w_pieces, tables, place, w_out = barrier(
-        (far, x0, y0, w_near, w_pieces, tables, place, w_out)
-    )
-
-    w_far = [swapped(w_pieces[s], "ctx", 2 * s) for s in (2, 3)]
+    far, x0, y0, w_pieces, tables, place, w_out = barrier(
+        (far, x0, y0, w_pieces, tables, place, w_out)
+    )
+
+    same_core = [[i for i in range(8) if i % 2 == k] for k in range(2)]
+    w_same = lax.all_to_all(w_pieces, "ctx", 0, 0, axis_index_groups=same_core)
     inner = [a[:rows] for a in far]
     x_rest = swapped(jnp.concatenate(inner + [y0[half:]]), "head", 1)
     y_rest = swapped(jnp.concatenate(inner + [x0[:half]]), "head", 2)
@@ -620,15 +631,16 @@
     cosine, sine = jnp.cos(angle), jnp.sin(angle)
     cosine = jnp.concatenate([cosine, cosine], -1)
     sine = jnp.concatenate([-sine, sine], -1)
-    w_far, x_rest, y_rest, d_rest, cosine, sine, w_out = barrier(
-        (w_far, x_rest, y_rest, d_rest, cosine, sine, w_out)
-    )
-    w_same = [w_pieces[0], w_near] + list(w_far)
-    w_swap = [swapped(w, "ctx", 1) for w in w_same]
     middle = [(2, 4), (3, 5), (4, 2), (5, 3)]
     outward = [(2, 0), (3, 1), (4, 6), (5, 7)]
     out_near = swapped(w_out, "ctx", 2)
     out_across = lax.ppermute(w_out, "ctx", middle)
+    w_same, x_rest, y_rest, d_rest, cosine, sine, out_near, out_across = barrier(
+        (w_same, x_rest, y_rest, d_rest, cosine, sine, out_near, out_across)
+    )
+    w_swap = swapped(w_same, "ctx", 1)
+    out_across_next = lax.ppermute(out_near, "ctx", middle)
+    out_passed = lax.ppermute(out_across, "ctx", outward)
     sources = place, [activations] + list(far), (x0, x_rest, y0, y_rest, d_rest), w_same, w_swap
     (v_pair,) = project(*sources)
     v_next = swapped(v_pair, "ctx", 2)
@@ -636,25 +648,24 @@
     out_own_swap = swapped(w_out, "ctx", 1)
     place, v_pair = barrier((place, v_pair))
     mine, theirs = project(place, *sources[1:], (cosine, sine))
-    mine, theirs, v_next, v_pair_other, out_near, out_across, out_own_swap = barrier(
-        (mine, theirs, v_next, v_pair_other, out_near, out_across, out_own_swap)
-    )
-    out_near_swap, out_across_swap = swapped(out_near, "ctx", 1), swapped(out_across, "ctx", 1)
+    mine, theirs, v_next, v_pair_other, out_across_next, out_passed, out_own_swap = barrier(
+        (mine, theirs, v_next, v_pair_other, out_across_next, out_passed, out_own_swap)
+    )
+    out_passed_next = lax.ppermute(out_across_next, "ctx", outward)
     other = swapped(theirs, "ctx", 1)
     v_next_other = swapped(v_next, "ctx", 1)
-    out_across_next = lax.ppermute(out_near, "ctx", middle)
-    out_passed = lax.ppermute(out_across, "ctx", outward)
+    out_near_swap, out_across_swap = swapped(out_near, "ctx", 1), swapped(out_across, "ctx", 1)
     group_rows = lax.dynamic_slice_in_dim(head_mix, GROUP * (ctx // GROUP), GROUP, 0)
     mix = lax.dynamic_index_in_dim(group_rows, ctx % GROUP, 1, keepdims=False)
     out_mine, out_theirs = attend_head(
         place, mix, mine, other, tables, (v_pair, v_next, v_pair_other, v_next_other)
     )
-    out_mine, out_theirs, out_across_next, out_passed, out_near_swap, out_across_swap = barrier(
-        (out_mine, out_theirs, out_across_next, out_passed, out_near_swap, out_across_swap)
-    )
-    out_passed_next = lax.ppermute(out_across_next, "ctx", outward)
+    out_mine, out_theirs, out_passed_next, out_near_swap, out_across_swap = barrier(
+        (out_mine, out_theirs, out_passed_next, out_near_swap, out_across_swap)
+    )
     out_parts = [w_out, out_own_swap, out_near, out_near_swap, out_across, out_across_swap]
-    out_parts += [p for w in (out_passed, out_across_next) for p in (w, swapped(w, "ctx", 1))]
+    for part in (out_passed, out_across_next, out_passed_next):
+        out_parts += [part, swapped(part, "ctx", 1)]
     summed = out_mine.astype(jnp.float32) + swapped(out_theirs, "ctx", 1).astype(jnp.float32)
     own = lax.dynamic_index_in_dim(summed, z, 0, keepdims=False)
     r1, r2, r3 = [
@@ -666,8 +677,6 @@
         for s in (1, 2, 3)
     ]
 
-    r1, r2, r3, out_passed_next = barrier((r1, r2, r3, out_passed_next))
-    out_parts += [out_passed_next, swapped(out_passed_next, "ctx", 1)]
     inner = (z == 1) | (z == 2)
     out_places = jnp.stack(
         [z, z ^ 1, jnp.where(inner, z ^ 3, z ^ 2), jnp.where(inner, z ^ 2, z ^ 3), inner]

time: 298 us -> 291 us (0.977); the launches traced: 293 us -> 290 us
  starting transfers between devices: 47.9 us -> 37.2 us
  local copies, waits for them, and re-layouts: 26.3 us -> 33.1 us
  waiting for transfers between devices: 171 us -> 165 us
  other arithmetic: 11.6 us -> 16.9 us
    ppermute x1, waiting for transfers between devices: 27 us -> 0.01 us  [per_device_one_head(): out_passed_next = lax.ppermute(out_across_next, 'ctx', outward)]
    ppermute x33 -> x27, starting transfers between devices: 38 us -> 21 us  [swapped(): return lax.ppermute(value, axis, [(i, i ^ mask) for i in range(count)])]
    ppermute x1, waiting for transfers between devices: 2.46 us -> 16.4 us  [per_device_one_head(): out_across = lax.ppermute(w_out, 'ctx', middle)]
    ppermute x33 -> x27, waiting for transfers between devices: 142 us -> 148 us  [swapped(): return lax.ppermute(value, axis, [(i, i ^ mask) for i in range(count)])]
    another operation x1 -> x4, other arithmetic: 0.01 us -> 5.2 us  [the longest x3 4.49 us: per_device_one_head(): w_pieces = jnp.stack([columns(target) for target in range(4)])]
    unnamed x72 -> x88, local copies, waits for them, and re-layouts: 20.5 us -> 25.1 us
    concatenate x4 -> x0, other arithmetic: 4.43 us -> none  [columns(): return jnp.concatenate(parts, 1)]
    all_to_all x0 -> x1, starting transfers between devices: none -> 3.69 us  [per_device_one_head(): w_same = lax.all_to_all(w_pieces, 'ctx', 0, 0, axis_index_groups=same_core)]
  transfers between devices with their start and end apart: 37 -> 32, of which waited for: 16 -> 15; matrix products, arithmetic and copies ran while one was open for 5% -> 7% of each run, Pallas kernels for 10% -> 10%
where the time goes in v6:
time: 291 us; the launch traced here: 290 us
  waiting for transfers between devices  165 us (57%)
  Pallas kernels  37.7 us (13%)
  starting transfers between devices  37.2 us (13%)
  local copies, waits for them, and re-layouts  33.1 us (11%)
  other arithmetic  16.9 us (6%)
    ppermute x27, waiting for transfers between devices, swapped(): return lax.ppermute(value, axis, [(i, i ^ mask) for i in range(count)])  148 us
    unnamed x88, local copies, waits for them, and re-layouts  25.1 us
    ppermute x27, starting transfers between devices, swapped(): return lax.ppermute(value, axis, [(i, i ^ mask) for i in range(count)])  21 us
    ppermute x1, waiting for transfers between devices, per_device_one_head(): out_across = lax.ppermute(w_out, 'ctx', middle)  16.4 us
    pallas_call x1, Pallas kernels, attend_head(): pl.pallas_call(attend_kernel, grid=(count,), out_shape=(out, out), in_spe...  14.7 us
    pallas_call x2, Pallas kernels, project(): pl.pallas_call(functools.partial(project_kernel, rows, first_col), out_sh...  13.6 us
    pallas_call x1, Pallas kernels, finish(): pl.pallas_call(finish_kernel, in_specs=[whole(pltpu.SMEM)] + [whole(pltpu...  7.95 us
  transfers between devices with their start and end apart: 32, of which 15 were waited for; matrix products, arithmetic and copies ran while one was open for 7% of the time, Pallas kernels for 10%

profile of v6, /device:TPU:17, one launch (start us, length us, event | category | flops | bytes accessed | tf_op | source)
XLA Modules:
  0.0 289.9 jit_solution(12446427002651910551)
XLA Ops:
  0.7 1.9 pad_maximum_fusion.5
  2.7 1.3 collective-permute-start
  4.0 1.3 collective-permute-start.2
  5.3 1.2 collective-permute-start.3
  6.5 1.2 collective-permute-start.4
  7.8 2.2 fusion.16
  10.0 1.0 fusion.15
  11.0 1.0 fusion.14
  12.7 1.4 shard_map.91
  16.4 1.5 maximum_bitcast_fusion.2
  17.9 1.1 maximum_bitcast_fusion
  19.0 1.9 pad_maximum_fusion
  20.9 5.3 %collective-permute-done.refs_1_ = bf16[272,1024]{1,0:T(8,128)(2,1)S(1)} collective-permute-done((bf16[272,1024]{1,0:T(8,128)(2,1)}, bf16[272,1024]{1,0:T(8,128)(2,1)S(1)}, u32[]{:S(2)}, u32[]{:S(2)}) %collective-permute-start) | collective-permute-done | bytes 557088 | tf_op jit(solution)/shard_map/ppermute | solution.py:583
  26.2 2.0 collective-permute-done.1.refs_2_
  28.2 24.9 %collective-permute-done.2.refs_3_ = bf16[272,1024]{1,0:T(8,128)(2,1)S(1)} collective-permute-done((bf16[272,1024]{1,0:T(8,128)(2,1)}, bf16[272,1024]{1,0:T(8,128)(2,1)S(1)}, u32[]{:S(2)}, u32[]{:S(2)}) %collective-permute-start.2) | collective-permute-done | bytes 557088 | tf_op jit(solution)/shard_map/ppermute | solution.py:583
  54.0 3.7 %all-to-all-start = ((bf16[4,512,768]{2,1,0:T(8,128)(2,1)}), bf16[4,512,768]{2,1,0:T(8,128)(2,1)S(1)}, u32[]{:S(2)}, u32[]{:S(2)}) async-start(bf16[4,512,768]{2,1,0:T(8,128)(2,1)} %pad_maximum_fusion), calls=%async_computation | async-start | bytes 6291456 | tf_op jit(solution)/shard_map/all_to_all | solution.py:617
  57.7 1.2 slice.42
  59.7 1.3 collective-permute-start.5
  60.9 1.2 collective-permute-start.6
  62.6 1.2 collective-permute-start.8
  63.8 1.9 collective-permute-start.9
  66.5 1.9 fusion.3
  69.4 1.0 pad_maximum_fusion.7.refs_12_
  70.4 60.5 %collective-permute-done.8.refs_2_ = bf16[1024,512]{1,0:T(8,128)(2,1)} collective-permute-done((bf16[1024,512]{1,0:T(8,128)(2,1)S(1)}, bf16[1024,512]{1,0:T(8,128)(2,1)}, u32[]{:S(2)}, u32[]{:S(2)}) %collective-permute-start.8) | collective-permute-done | bytes 1048608 | tf_op jit(solution)/shard_map/ppermute | solution.py:583
  130.9 16.4 %collective-permute-done.9.refs_4_ = bf16[1024,512]{1,0:T(8,128)(2,1)} collective-permute-done((bf16[1024,512]{1,0:T(8,128)(2,1)S(1)}, bf16[1024,512]{1,0:T(8,128)(2,1)}, u32[]{:S(2)}, u32[]{:S(2)}) %collective-permute-start.9) | collective-permute-done | bytes 1048608 | tf_op jit(solution)/shard_map/ppermute | solution.py:637
  147.3 1.2 copy-done.14
  148.5 1.3 copy-done.10
  149.8 1.3 copy-done.12
  151.1 2.5 collective-permute-start.10
  153.5 3.1 %collective-permute-start.13 = (bf16[1024,512]{1,0:T(8,128)(2,1)}, bf16[1024,512]{1,0:T(8,128)(2,1)}, u32[]{:S(2)}, u32[]{:S(2)}) collective-permute-start(bf16[1024,512]{1,0:T(8,128)(2,1)} %collective-permute-done.8.refs_2_), channel_id=1, source_target_pairs={{8,16},{12,20},{16,8},{20,12},{9,17},{13,21},{17,9},{21,13},{10,18... | collective-permute-start | bytes 3145736 | tf_op jit(solution)/shard_map/ppermute | solution.py:642
  156.7 2.3 collective-permute-start.14
  158.9 1.4 collective-permute-done.10.refs_10_
  160.3 1.1 copy-done.3
  161.4 1.1 copy-done.6
  162.4 1.1 copy-done.8
  163.5 1.0 copy-done.9
  164.5 1.5 copy-done.11
  166.0 1.5 copy-done.13
  167.5 1.4 copy-done.15
  168.9 1.0 copy-done.17
  170.0 1.0 copy-done.20
  171.0 6.2 %shard_map.92.refs_5_ = bf16[4,256,256]{2,1,0:T(8,128)(2,1)S(1)} custom-call(s32[9]{0:T(128)S(1)} %stack.92.place, bf16[256,1024]{1,0:T(8,128)(2,1)S(1)} %copy-done.9, bf16[272,1024]{1,0:T(8,128)(2,1)S(1)} %copy-done.3, bf16[272,1024]{1,0:T(8,128)(2,1)S(1)} %copy-done.6, bf16[272,1024]{1,0:T(8,128)(2,1)S(1)} %copy-done.8, bf16[256,1024]{1,0:T(8,128)(2,1)S(1)} %copy-done.17, ...), custom_call_target="tpu_custom_call" | custom-call | flops 2147483648 | bytes 16777216 | tf_op jit(solution)/shard_map/pallas_call | solution.py:260
  177.8 7.5 %shard_map.93 = (bf16[4,256,256]{2,1,0:T(8,128)(2,1)S(1)}, bf16[4,256,256]{2,1,0:T(8,128)(2,1)}) custom-call(s32[9]{0:T(128)S(1)} %stack.92.place, bf16[256,1024]{1,0:T(8,128)(2,1)S(1)} %copy-done.9, bf16[272,1024]{1,0:T(8,128)(2,1)S(1)} %copy-done.3, bf16[272,1024]{1,0:T(8,128)(2,1)S(1)} %copy-done.6, bf16[272,1024]{1,0:T(8,128)(2,1)S(1)} %copy-done.8, ...), custom_call_target="tpu_custom_call" | custom-call | flops 4294967296 | bytes 16777216 | tf_op jit(solution)/shard_map/pallas_call | solution.py:260
  186.6 4.8 %collective-permute-done.11.refs_6_ = bf16[4,256,256]{2,1,0:T(8,128)(2,1)} collective-permute-done((bf16[4,256,256]{2,1,0:T(8,128)(2,1)S(1)}, bf16[4,256,256]{2,1,0:T(8,128)(2,1)}, u32[]{:S(2)}, u32[]{:S(2)}) %collective-permute-start.11) | collective-permute-done | bytes 524320 | tf_op jit(solution)/shard_map/ppermute | solution.py:583
  192.2 5.2 %collective-permute-start.18 = (bf16[1024,512]{1,0:T(8,128)(2,1)}, bf16[1024,512]{1,0:T(8,128)(2,1)}, u32[]{:S(2)}, u32[]{:S(2)}) collective-permute-start(bf16[1024,512]{1,0:T(8,128)(2,1)} %collective-permute-done.13.refs_8_), channel_id=1, source_target_pairs={{8,0},{12,4},{16,24},{20,28},{9,1},{13,5},{17,25},{21,29},{10,2},{... | collective-permute-start | bytes 3145736 | tf_op jit(solution)/shard_map/ppermute | solution.py:654
  197.4 1.6 collective-permute-start.16
  199.1 1.7 collective-permute-done.16.refs_1_
  201.5 1.0 copy-done.22
  202.6 1.0 copy-done.26
  203.6 1.0 copy-done.28
  205.6 1.0 copy-done.34
  206.6 14.7 %shard_map.94 = (bf16[4,256,512]{2,1,0:T(8,128)(2,1)S(1)}, bf16[4,256,512]{2,1,0:T(8,128)(2,1)S(1)}) custom-call(s32[9]{0:T(128)S(1)} %stack.92.place, f32[4]{0:T(128)S(1)} %dynamic-slice_bitcast_fusion.1.mix, bf16[4,256,256]{2,1,0:T(8,128)(2,1)S(1)} %copy-done.34, bf16[4,256,256]{2,1,0:T(8,128)(2,1)S(1)} %collective-permute-done.16.refs_1_, ...), custom_call_target="tpu_custom_call" | custom-call | flops 5368709120 | bytes 16777216 | tf_op jit(solution)/shard_map/pallas_call | solution.py:490
  222.5 1.9 collective-permute-done.21
  224.3 1.6 convert_add_fusion
  226.8 1.8 collective-permute-start.22
  228.6 1.2 collective-permute-start.24
  231.2 7.7 %collective-permute-done.22.r1 = bf16[256,512]{1,0:T(8,128)(2,1)S(1)} collective-permute-done((bf16[256,512]{1,0:T(8,128)(2,1)}, bf16[256,512]{1,0:T(8,128)(2,1)S(1)}, u32[]{:S(2)}, u32[]{:S(2)}) %collective-permute-start.22) | collective-permute-done | bytes 262176 | tf_op jit(solution)/shard_map/ppermute | solution.py:583
  238.9 1.9 collective-permute-done.23.r2
  240.8 11.9 %collective-permute-done.24.r3 = bf16[256,512]{1,0:T(8,128)(2,1)S(1)} collective-permute-done((bf16[256,512]{1,0:T(8,128)(2,1)S(1)}, bf16[256,512]{1,0:T(8,128)(2,1)S(1)}, u32[]{:S(2)}, u32[]{:S(2)}) %collective-permute-start.24) | collective-permute-done | bytes 262176 | tf_op jit(solution)/shard_map/ppermute | solution.py:583
  253.4 7.9 %shard_map.95 = (bf16[256,1024]{1,0:T(8,128)(2,1)}, bf16[256,1024]{1,0:T(8,128)(2,1)}, bf16[256,1024]{1,0:T(8,128)(2,1)}, bf16[256,1024]{1,0:T(8,128)(2,1)}) custom-call(s32[10]{0:T(128)} %concatenate.47.place, f32[256,512]{1,0:T(8,128)} %dynamic-slice_bitcast_fusion.own, bf16[256,512]{1,0:T(8,128)(2,1)} %copy-done.41, bf16[256,512]{1,0:T(8,128)(2,1)} %copy-done.42, ...), custom_call_target="tpu_custom_call" | custom-call | flops 2147483648 | bytes 11534336 | tf_op jit(solution)/shard_map/pallas_call | solution.py:564
  261.4 2.2 collective-permute-start.30
  264.1 10.7 %collective-permute-done.30 = bf16[256,1024]{1,0:T(8,128)(2,1)S(1)} collective-permute-done((bf16[256,1024]{1,0:T(8,128)(2,1)}, bf16[256,1024]{1,0:T(8,128)(2,1)S(1)}, u32[]{:S(2)}, u32[]{:S(2)}) %collective-permute-start.30) | collective-permute-done | bytes 524320 | tf_op jit(solution)/shard_map/ppermute | solution.py:583
  274.8 12.8 %collective-permute-done.29 = bf16[256,1024]{1,0:T(8,128)(2,1)S(1)} collective-permute-done((bf16[256,1024]{1,0:T(8,128)(2,1)}, bf16[256,1024]{1,0:T(8,128)(2,1)S(1)}, u32[]{:S(2)}, u32[]{:S(2)}) %collective-permute-start.29) | collective-permute-done | bytes 524320 | tf_op jit(solution)/shard_map/ppermute | solution.py:583
  287.7 2.2 add_convert_fusion
  (130 shorter events, 16.6 us)
Async XLA Ops:
  0.0 199.0 %copy-start = (f32[8,4]{0,1:T(4,128)S(1)}, f32[8,4]{0,1:T(4,128)}, u32[]{:S(2)}) copy-start(f32[8,4]{0,1:T(4,128)} %param.15) | copy-start | bytes 388
  2.7 23.5 %collective-permute-start = (bf16[272,1024]{1,0:T(8,128)(2,1)}, bf16[272,1024]{1,0:T(8,128)(2,1)S(1)}, u32[]{:S(2)}, u32[]{:S(2)}) collective-permute-start(bf16[272,1024]{1,0:T(8,128)(2,1)} %pad_maximum_fusion.5), channel_id=1, source_target_pairs={{0,8},{4,12},{8,0},{12,4},{16,24},{20,28},{24,16},{28,20},{1,9},{5... | collective-permute-start | bytes 1671176 | tf_op jit(solution)/shard_map/ppermute | solution.py:583
  3.9 24.3 %collective-permute-start.1 = (bf16[272,1024]{1,0:T(8,128)(2,1)}, bf16[272,1024]{1,0:T(8,128)(2,1)S(1)}, u32[]{:S(2)}, u32[]{:S(2)}) collective-permute-start(bf16[272,1024]{1,0:T(8,128)(2,1)} %pad_maximum_fusion.5), channel_id=1, source_target_pairs={{0,16},{4,20},{8,24},{12,28},{16,0},{20,4},{24,8},{28,12},{1,17},{... | collective-permute-start | bytes 1671176 | tf_op jit(solution)/shard_map/ppermute | solution.py:583
  4.0 49.1 %collective-permute-start.2 = (bf16[272,1024]{1,0:T(8,128)(2,1)}, bf16[272,1024]{1,0:T(8,128)(2,1)S(1)}, u32[]{:S(2)}, u32[]{:S(2)}) collective-permute-start(bf16[272,1024]{1,0:T(8,128)(2,1)} %pad_maximum_fusion.5), channel_id=1, source_target_pairs={{0,24},{4,28},{8,16},{12,20},{16,8},{20,12},{24,0},{28,4},{1,25},{... | collective-permute-start | bytes 1671176 | tf_op jit(solution)/shard_map/ppermute | solution.py:583
  5.3 15.6 %collective-permute-start.3 = (bf16[256,1024]{1,0:T(8,128)(2,1)}, bf16[256,1024]{1,0:T(8,128)(2,1)S(1)}, u32[]{:S(2)}, u32[]{:S(2)}) collective-permute-start(bf16[256,1024]{1,0:T(8,128)(2,1)} %refs_0_.3), channel_id=1, source_target_pairs={{0,1},{1,0},{2,3},{3,2},{4,5},{5,4},{6,7},{7,6},{8,9},{9,8},{10,11... | collective-permute-start | bytes 1572872 | tf_op jit(solution)/shard_map/ppermute | solution.py:583
  6.5 14.4 %collective-permute-start.4 = (bf16[256,1024]{1,0:T(8,128)(2,1)}, bf16[256,1024]{1,0:T(8,128)(2,1)S(1)}, u32[]{:S(2)}, u32[]{:S(2)}) collective-permute-start(bf16[256,1024]{1,0:T(8,128)(2,1)} %refs_0_.3), channel_id=1, source_target_pairs={{0,2},{1,3},{2,0},{3,1},{4,6},{5,7},{6,4},{7,5},{8,10},{9,11},{10,... | collective-permute-start | bytes 1572872 | tf_op jit(solution)/shard_map/ppermute | solution.py:583
  7.8 2.2 copy-start.37
  7.8 3.2 %copy-start.38 = (bf16[512,1024]{1,0:T(8,128)(2,1)S(1)}, bf16[512,1024]{1,0:T(8,128)(2,1)}, u32[]{:S(2)}) copy-start(bf16[512,1024]{1,0:T(8,128)(2,1)} %param.11) | copy-start | bytes 3145732
  16.4 1.5 copy-start.39
  16.4 1.5 copy-start.40
  20.9 32.2 %copy-start.16 = (bf16[256,1024]{1,0:T(8,128)(2,1)}, bf16[256,1024]{1,0:T(8,128)(2,1)S(1)}, u32[]{:S(2)}) copy-start(bf16[256,1024]{1,0:T(8,128)(2,1)S(1)} %collective-permute-done.3.refs_4_) | copy-start | bytes 1572868
  20.9 32.2 %copy-start.19 = (bf16[256,1024]{1,0:T(8,128)(2,1)}, bf16[256,1024]{1,0:T(8,128)(2,1)S(1)}, u32[]{:S(2)}) copy-start(bf16[256,1024]{1,0:T(8,128)(2,1)S(1)} %collective-permute-done.4.refs_6_) | copy-start | bytes 1572868
  26.2 27.0 %copy-start.1 = (bf16[272,1024]{1,0:T(8,128)(2,1)}, bf16[272,1024]{1,0:T(8,128)(2,1)S(1)}, u32[]{:S(2)}) copy-start(bf16[272,1024]{1,0:T(8,128)(2,1)S(1)} %collective-permute-done.refs_1_) | copy-start | bytes 1671172
  28.2 24.9 %copy-start.4 = (bf16[272,1024]{1,0:T(8,128)(2,1)}, bf16[272,1024]{1,0:T(8,128)(2,1)S(1)}, u32[]{:S(2)}) copy-start(bf16[272,1024]{1,0:T(8,128)(2,1)S(1)} %collective-permute-done.1.refs_2_) | copy-start | bytes 1671172
  54.0 97.1 %all-to-all-start = ((bf16[4,512,768]{2,1,0:T(8,128)(2,1)}), bf16[4,512,768]{2,1,0:T(8,128)(2,1)S(1)}, u32[]{:S(2)}, u32[]{:S(2)}) async-start(bf16[4,512,768]{2,1,0:T(8,128)(2,1)} %pad_maximum_fusion), calls=%async_computation | async-start | bytes 6291456 | tf_op jit(solution)/shard_map/all_to_all | solution.py:617
  57.7 1.2 copy-start.5
  57.7 1.4 copy-start.2
  57.7 1.4 slice-start
  57.7 1.5 slice-start.1
  59.7 2.9 %copy-start.35 = (bf16[1024,512]{1,0:T(8,128)(2,1)S(1)}, bf16[1024,512]{1,0:T(8,128)(2,1)}, u32[]{:S(2)}) copy-start(bf16[1024,512]{1,0:T(8,128)(2,1)} %refs_0_.4) | copy-start | bytes 3145732
  59.7 88.9 %collective-permute-start.5 = (bf16[896,1024]{1,0:T(8,128)(2,1)S(1)}, bf16[896,1024]{1,0:T(8,128)(2,1)S(1)}, u32[]{:S(2)}, u32[]{:S(2)}) collective-permute-start(bf16[896,1024]{1,0:T(8,128)(2,1)S(1)} %get-tuple-element.97), channel_id=1, source_target_pairs={{0,1},{1,0},{2,3},{3,2},{4,5},{5,4},{6,7},{7,6},{8,9},{9,8},{10,11... | collective-permute-start | bytes 5505032 | tf_op jit(solution)/shard_map/ppermute | solution.py:583
  60.9 88.9 %collective-permute-start.6 = (bf16[896,1024]{1,0:T(8,128)(2,1)S(1)}, bf16[896,1024]{1,0:T(8,128)(2,1)S(1)}, u32[]{:S(2)}, u32[]{:S(2)}) collective-permute-start(bf16[896,1024]{1,0:T(8,128)(2,1)S(1)} %get-tuple-element.96), channel_id=1, source_target_pairs={{0,2},{1,3},{2,0},{3,1},{4,6},{5,7},{6,4},{7,5},{8,10},{9,11},{10,... | collective-permute-start | bytes 5505032 | tf_op jit(solution)/shard_map/ppermute | solution.py:583
  62.3 85.0 %collective-permute-start.7 = (bf16[768,1024]{1,0:T(8,128)(2,1)S(1)}, bf16[768,1024]{1,0:T(8,128)(2,1)S(1)}, u32[]{:S(2)}, u32[]{:S(2)}) collective-permute-start(bf16[768,1024]{1,0:T(8,128)(2,1)S(1)} %pad_maximum_fusion.4), channel_id=1, source_target_pairs={{0,3},{1,2},{2,1},{3,0},{4,7},{5,6},{6,5},{7,4},{8,11},{9,10},{10,... | collective-permute-start | bytes 4718600 | tf_op jit(solution)/shard_map/ppermute | solution.py:583
  62.6 68.3 %collective-permute-start.8 = (bf16[1024,512]{1,0:T(8,128)(2,1)S(1)}, bf16[1024,512]{1,0:T(8,128)(2,1)}, u32[]{:S(2)}, u32[]{:S(2)}) collective-permute-start(bf16[1024,512]{1,0:T(8,128)(2,1)S(1)} %copy-done.35), channel_id=1, source_target_pairs={{0,8},{4,12},{8,0},{12,4},{16,24},{20,28},{24,16},{28,20},{1,9},{5... | collective-permute-start | bytes 3145736 | tf_op jit(solution)/shard_map/ppermute | solution.py:583
  63.8 83.5 %collective-permute-start.9 = (bf16[1024,512]{1,0:T(8,128)(2,1)S(1)}, bf16[1024,512]{1,0:T(8,128)(2,1)}, u32[]{:S(2)}, u32[]{:S(2)}) collective-permute-start(bf16[1024,512]{1,0:T(8,128)(2,1)S(1)} %copy-done.35), channel_id=1, source_target_pairs={{8,16},{12,20},{16,8},{20,12},{9,17},{13,21},{17,9},{21,13},{10,18... | collective-permute-start | bytes 3145736 | tf_op jit(solution)/shard_map/ppermute | solution.py:637
  147.3 1.3 copy-start.14
  148.5 1.3 copy-start.10
  149.8 1.3 copy-start.12
  151.1 9.3 %collective-permute-start.10 = (bf16[4,512,768]{2,1,0:T(8,128)(2,1)S(1)}, bf16[4,512,768]{2,1,0:T(8,128)(2,1)S(1)}, u32[]{:S(2)}, u32[]{:S(2)}) collective-permute-start(bf16[4,512,768]{2,1,0:T(8,128)(2,1)S(1)} %all-to-all-done.refs_9_), channel_id=1, source_target_pairs={{0,4},{4,0},{8,12},{12,8},{16,20},{20,16},{24,28},{28,24},{1,5},{5... | collective-permute-start | bytes 9437192 | tf_op jit(solution)/shard_map/ppermute | solution.py:583
  153.5 32.6 %collective-permute-start.15 = (bf16[1024,512]{1,0:T(8,128)(2,1)}, bf16[1024,512]{1,0:T(8,128)(2,1)S(1)}, u32[]{:S(2)}, u32[]{:S(2)}) collective-permute-start(bf16[1024,512]{1,0:T(8,128)(2,1)} %refs_0_.4), channel_id=1, source_target_pairs={{0,4},{4,0},{8,12},{12,8},{16,20},{20,16},{24,28},{28,24},{1,5},{5... | collective-permute-start | bytes 3145736 | tf_op jit(solution)/shard_map/ppermute | solution.py:583
  153.5 32.7 %collective-permute-start.13 = (bf16[1024,512]{1,0:T(8,128)(2,1)}, bf16[1024,512]{1,0:T(8,128)(2,1)}, u32[]{:S(2)}, u32[]{:S(2)}) collective-permute-start(bf16[1024,512]{1,0:T(8,128)(2,1)} %collective-permute-done.8.refs_2_), channel_id=1, source_target_pairs={{8,16},{12,20},{16,8},{20,12},{9,17},{13,21},{17,9},{21,13},{10,18... | collective-permute-start | bytes 3145736 | tf_op jit(solution)/shard_map/ppermute | solution.py:642
  156.7 30.0 %collective-permute-start.14 = (bf16[1024,512]{1,0:T(8,128)(2,1)}, bf16[1024,512]{1,0:T(8,128)(2,1)}, u32[]{:S(2)}, u32[]{:S(2)}) collective-permute-start(bf16[1024,512]{1,0:T(8,128)(2,1)} %collective-permute-done.9.refs_4_), channel_id=1, source_target_pairs={{8,0},{12,4},{16,24},{20,28},{9,1},{13,5},{17,25},{21,29},{10,2},{... | collective-permute-start | bytes 3145736 | tf_op jit(solution)/shard_map/ppermute | solution.py:643
  160.3 1.1 copy-start.3
  161.4 1.1 copy-start.6
  162.4 1.1 copy-start.8
  164.5 1.5 copy-start.11
  166.0 1.5 copy-start.13
  167.5 1.4 copy-start.15
  171.0 6.7 %copy-start.18 = (bf16[256,1024]{1,0:T(8,128)(2,1)S(1)}, bf16[256,1024]{1,0:T(8,128)(2,1)}, u32[]{:S(2)}) copy-start(bf16[256,1024]{1,0:T(8,128)(2,1)} %copy-done.16) | copy-start | bytes 1572868
  171.0 6.7 %copy-start.23 = (f32[4,256,128]{2,1,0:T(8,128)S(1)}, f32[4,256,128]{2,1,0:T(8,128)}, u32[]{:S(2)}) copy-start(f32[4,256,128]{2,1,0:T(8,128)} %pad_maximum_fusion.7.refs_12_) | copy-start | bytes 1572868
  171.0 6.7 %copy-start.24 = (f32[4,256,128]{2,1,0:T(8,128)S(1)}, f32[4,256,128]{2,1,0:T(8,128)}, u32[]{:S(2)}) copy-start(f32[4,256,128]{2,1,0:T(8,128)} %pad_maximum_fusion.6.refs_11_) | copy-start | bytes 1572868
  177.2 8.0 %copy-start.21 = (bf16[4,256,256]{2,1,0:T(8,128)(2,1)}, bf16[4,256,256]{2,1,0:T(8,128)(2,1)S(1)}, u32[]{:S(2)}) copy-start(bf16[4,256,256]{2,1,0:T(8,128)(2,1)S(1)} %shard_map.92.refs_5_) | copy-start | bytes 1572868
  177.2 24.3 %copy-start.32 = (bf16[768,128]{1,0:T(8,128)(2,1)S(1)}, bf16[768,128]{1,0:T(8,128)(2,1)}, u32[]{:S(2)}) copy-start(bf16[768,128]{1,0:T(8,128)(2,1)} %copy-done.31) | copy-start | bytes 589828
  177.2 14.2 %collective-permute-start.11 = (bf16[4,256,256]{2,1,0:T(8,128)(2,1)S(1)}, bf16[4,256,256]{2,1,0:T(8,128)(2,1)}, u32[]{:S(2)}, u32[]{:S(2)}) collective-permute-start(bf16[4,256,256]{2,1,0:T(8,128)(2,1)S(1)} %shard_map.92.refs_5_), channel_id=1, source_target_pairs={{0,8},{4,12},{8,0},{12,4},{16,24},{20,28},{24,16},{28,20},{1,9},{5... | collective-permute-start | bytes 1572872 | tf_op jit(solution)/shard_map/ppermute | solution.py:583
  177.3 14.1 %collective-permute-start.12 = (bf16[4,256,256]{2,1,0:T(8,128)(2,1)S(1)}, bf16[4,256,256]{2,1,0:T(8,128)(2,1)S(1)}, u32[]{:S(2)}, u32[]{:S(2)}) collective-permute-start(bf16[4,256,256]{2,1,0:T(8,128)(2,1)S(1)} %shard_map.92.refs_5_), channel_id=1, source_target_pairs={{0,4},{4,0},{8,12},{12,8},{16,20},{20,16},{24,28},{28,24},{1,5},{5... | collective-permute-start | bytes 1572872 | tf_op jit(solution)/shard_map/ppermute | solution.py:583
  186.1 11.3 %copy-start.36 = (bf16[1024,512]{1,0:T(8,128)(2,1)}, bf16[1024,512]{1,0:T(8,128)(2,1)S(1)}, u32[]{:S(2)}) copy-start(bf16[1024,512]{1,0:T(8,128)(2,1)S(1)} %collective-permute-done.15.refs_1_) | copy-start | bytes 3145732
  186.1 35.2 %collective-permute-start.19 = (bf16[1024,512]{1,0:T(8,128)(2,1)}, bf16[1024,512]{1,0:T(8,128)(2,1)}, u32[]{:S(2)}, u32[]{:S(2)}) collective-permute-start(bf16[1024,512]{1,0:T(8,128)(2,1)} %collective-permute-done.8.refs_2_), channel_id=1, source_target_pairs={{0,4},{4,0},{8,12},{12,8},{16,20},{20,16},{24,28},{28,24},{1,5},{5... | collective-permute-start | bytes 3145736 | tf_op jit(solution)/shard_map/ppermute | solution.py:583
  186.2 35.1 %collective-permute-start.20 = (bf16[1024,512]{1,0:T(8,128)(2,1)}, bf16[1024,512]{1,0:T(8,128)(2,1)}, u32[]{:S(2)}, u32[]{:S(2)}) collective-permute-start(bf16[1024,512]{1,0:T(8,128)(2,1)} %collective-permute-done.9.refs_4_), channel_id=1, source_target_pairs={{0,4},{4,0},{8,12},{12,8},{16,20},{20,16},{24,28},{28,24},{1,5},{5... | collective-permute-start | bytes 3145736 | tf_op jit(solution)/shard_map/ppermute | solution.py:583
  192.2 29.2 %collective-permute-start.18 = (bf16[1024,512]{1,0:T(8,128)(2,1)}, bf16[1024,512]{1,0:T(8,128)(2,1)}, u32[]{:S(2)}, u32[]{:S(2)}) collective-permute-start(bf16[1024,512]{1,0:T(8,128)(2,1)} %collective-permute-done.13.refs_8_), channel_id=1, source_target_pairs={{8,0},{12,4},{16,24},{20,28},{9,1},{13,5},{17,25},{21,29},{10,2},{... | collective-permute-start | bytes 3145736 | tf_op jit(solution)/shard_map/ppermute | solution.py:654
  197.4 3.4 %collective-permute-start.16 = (bf16[4,256,256]{2,1,0:T(8,128)(2,1)}, bf16[4,256,256]{2,1,0:T(8,128)(2,1)S(1)}, u32[]{:S(2)}, u32[]{:S(2)}) collective-permute-start(bf16[4,256,256]{2,1,0:T(8,128)(2,1)} %get-tuple-element.72), channel_id=1, source_target_pairs={{0,4},{4,0},{8,12},{12,8},{16,20},{20,16},{24,28},{28,24},{1,5},{5... | collective-permute-start | bytes 1572872 | tf_op jit(solution)/shard_map/ppermute | solution.py:583
  199.0 2.5 collective-permute-start.17
  201.5 1.0 copy-start.22
  221.4 3.0 %collective-permute-start.21 = (bf16[4,256,512]{2,1,0:T(8,128)(2,1)S(1)}, bf16[4,256,512]{2,1,0:T(8,128)(2,1)}, u32[]{:S(2)}, u32[]{:S(2)}) collective-permute-start(bf16[4,256,512]{2,1,0:T(8,128)(2,1)S(1)} %get-tuple-element.83), channel_id=1, source_target_pairs={{0,4},{4,0},{8,12},{12,8},{16,20},{20,16},{24,28},{28,24},{1,5},{5... | collective-permute-start | bytes 3145736 | tf_op jit(solution)/shard_map/ppermute | solution.py:583
  221.8 6.8 %collective-permute-start.25 = (bf16[1024,512]{1,0:T(8,128)(2,1)}, bf16[1024,512]{1,0:T(8,128)(2,1)}, u32[]{:S(2)}, u32[]{:S(2)}) collective-permute-start(bf16[1024,512]{1,0:T(8,128)(2,1)} %collective-permute-done.14.refs_6_), channel_id=1, source_target_pairs={{0,4},{4,0},{8,12},{12,8},{16,20},{20,16},{24,28},{28,24},{1,5},{5... | collective-permute-start | bytes 3145736 | tf_op jit(solution)/shard_map/ppermute | solution.py:583
  222.0 9.2 %collective-permute-start.26 = (bf16[1024,512]{1,0:T(8,128)(2,1)}, bf16[1024,512]{1,0:T(8,128)(2,1)}, u32[]{:S(2)}, u32[]{:S(2)}) collective-permute-start(bf16[1024,512]{1,0:T(8,128)(2,1)} %collective-permute-done.13.refs_8_), channel_id=1, source_target_pairs={{0,4},{4,0},{8,12},{12,8},{16,20},{20,16},{24,28},{28,24},{1,5},{5... | collective-permute-start | bytes 3145736 | tf_op jit(solution)/shard_map/ppermute | solution.py:583
  222.3 8.9 %collective-permute-start.27 = (bf16[1024,512]{1,0:T(8,128)(2,1)}, bf16[1024,512]{1,0:T(8,128)(2,1)}, u32[]{:S(2)}, u32[]{:S(2)}) collective-permute-start(bf16[1024,512]{1,0:T(8,128)(2,1)} %collective-permute-done.18.refs_10_), channel_id=1, source_target_pairs={{0,4},{4,0},{8,12},{12,8},{16,20},{20,16},{24,28},{28,24},{1,5},{5... | collective-permute-start | bytes 3145736 | tf_op jit(solution)/shard_map/ppermute | solution.py:583
  226.8 12.2 %collective-permute-start.22 = (bf16[256,512]{1,0:T(8,128)(2,1)}, bf16[256,512]{1,0:T(8,128)(2,1)S(1)}, u32[]{:S(2)}, u32[]{:S(2)}) collective-permute-start(bf16[256,512]{1,0:T(8,128)(2,1)} %get-tuple-element.95), channel_id=1, source_target_pairs={{0,8},{4,12},{8,0},{12,4},{16,24},{20,28},{24,16},{28,20},{1,9},{5... | collective-permute-start | bytes 786440 | tf_op jit(solution)/shard_map/ppermute | solution.py:583
  228.6 12.2 %collective-permute-start.23 = (bf16[256,512]{1,0:T(8,128)(2,1)S(1)}, bf16[256,512]{1,0:T(8,128)(2,1)S(1)}, u32[]{:S(2)}, u32[]{:S(2)}) collective-permute-start(bf16[256,512]{1,0:T(8,128)(2,1)S(1)} %get-tuple-element.94), channel_id=1, source_target_pairs={{0,16},{4,20},{8,24},{12,28},{16,0},{20,4},{24,8},{28,12},{1,17},{... | collective-permute-start | bytes 786440 | tf_op jit(solution)/shard_map/ppermute | solution.py:583
  228.6 24.1 %collective-permute-start.24 = (bf16[256,512]{1,0:T(8,128)(2,1)S(1)}, bf16[256,512]{1,0:T(8,128)(2,1)S(1)}, u32[]{:S(2)}, u32[]{:S(2)}) collective-permute-start(bf16[256,512]{1,0:T(8,128)(2,1)S(1)} %get-tuple-element.93), channel_id=1, source_target_pairs={{0,24},{4,28},{8,16},{12,20},{16,8},{20,12},{24,0},{28,4},{1,25},{... | collective-permute-start | bytes 786440 | tf_op jit(solution)/shard_map/ppermute | solution.py:583
  238.9 13.8 %copy-start.41 = (bf16[256,512]{1,0:T(8,128)(2,1)}, bf16[256,512]{1,0:T(8,128)(2,1)S(1)}, u32[]{:S(2)}) copy-start(bf16[256,512]{1,0:T(8,128)(2,1)S(1)} %collective-permute-done.22.r1) | copy-start | bytes 786436
  240.8 11.9 %copy-start.42 = (bf16[256,512]{1,0:T(8,128)(2,1)}, bf16[256,512]{1,0:T(8,128)(2,1)S(1)}, u32[]{:S(2)}) copy-start(bf16[256,512]{1,0:T(8,128)(2,1)S(1)} %collective-permute-done.23.r2) | copy-start | bytes 786436
  261.4 13.4 %collective-permute-start.30 = (bf16[256,1024]{1,0:T(8,128)(2,1)}, bf16[256,1024]{1,0:T(8,128)(2,1)S(1)}, u32[]{:S(2)}, u32[]{:S(2)}) collective-permute-start(bf16[256,1024]{1,0:T(8,128)(2,1)} %get-tuple-element.92), channel_id=1, source_target_pairs={{0,3},{1,2},{2,1},{3,0},{4,7},{5,6},{6,5},{7,4},{8,11},{9,10},{10,... | collective-permute-start | bytes 1572872 | tf_op jit(solution)/shard_map/ppermute | solution.py:583
  263.6 24.0 %collective-permute-start.29 = (bf16[256,1024]{1,0:T(8,128)(2,1)}, bf16[256,1024]{1,0:T(8,128)(2,1)S(1)}, u32[]{:S(2)}, u32[]{:S(2)}) collective-permute-start(bf16[256,1024]{1,0:T(8,128)(2,1)} %get-tuple-element.91), channel_id=1, source_target_pairs={{0,2},{1,3},{2,0},{3,1},{4,6},{5,7},{6,4},{7,5},{8,10},{9,11},{10,... | collective-permute-start | bytes 1572872 | tf_op jit(solution)/shard_map/ppermute | solution.py:583
  263.8 23.8 %collective-permute-start.28 = (bf16[256,1024]{1,0:T(8,128)(2,1)}, bf16[256,1024]{1,0:T(8,128)(2,1)S(1)}, u32[]{:S(2)}, u32[]{:S(2)}) collective-permute-start(bf16[256,1024]{1,0:T(8,128)(2,1)} %get-tuple-element.90), channel_id=1, source_target_pairs={{0,1},{1,0},{2,3},{3,2},{4,5},{5,4},{6,7},{7,6},{8,9},{9,8},{10,11... | collective-permute-start | bytes 1572872 | tf_op jit(solution)/shard_map/ppermute | solution.py:583
  (14 other events, 12.6 us)

commit v7 on v6

--- a/solution.py
+++ b/solution.py
@@ -271,7 +271,7 @@
             pltpu.SemaphoreType.DMA((4, 4)),
             pltpu.SemaphoreType.DMA((4, 2)),
         ],
-        compiler_params=kernel_params(20),
+        compiler_params=kernel_params(56),
         cost_estimate=pl.CostEstimate(
             flops=8 * rows * 4 * depth * width, bytes_accessed=16 * 2**20, transcendentals=0
         ),
@@ -341,7 +341,7 @@
                 ]
 
 
-def tables_kernel(weights, key_ref, even_ref, odd_ref):
+def fill_tables(weights, key_ref, even_ref, odd_ref):
     def fill(ref, origin, swap):
         height = ref.shape[0] if swap else ref.shape[0] // CQ
         width = ref.shape[1] // CQ if swap else ref.shape[1]
@@ -362,25 +362,10 @@
     fill(odd_ref, CK // 2 + 8 - SUB, False)
 
 
-def tables_of(weights):
-    return pl.pallas_call(
-        tables_kernel,
-        out_shape=(
-            jax.ShapeDtypeStruct((2 * LANES, CQ * LANES), jnp.bfloat16),
-            jax.ShapeDtypeStruct((CQ * LANES, 2 * LANES), jnp.bfloat16),
-            jax.ShapeDtypeStruct((CQ * LANES, LANES), jnp.bfloat16),
-        ),
-        in_specs=[whole(pltpu.SMEM)],
-        out_specs=[whole(pltpu.VMEM)] * 3,
-        compiler_params=kernel_params(8),
-        cost_estimate=pl.CostEstimate(flops=2**23, bytes_accessed=2**20, transcendentals=0),
-    )(weights)
-
-
-def attend_kernel(place, mix, *refs):
-    qk_refs, table_refs, (va, vb, vc, vd), (mine, theirs) = refs[:2], refs[2:5], refs[5:9], refs[9:11]
-    v_all, q_wide, k_ref, corr = refs[11:15]
-    tables, sem_v, sem_t = refs[19:22], refs[22], refs[23]
+def attend_kernel(place, mix, weights, *refs):
+    qk_refs, (va, vb, vc, vd), (mine, theirs) = refs[:2], refs[2:6], refs[6:8]
+    v_all, q_wide, k_ref, corr = refs[8:12]
+    tables, sem_v = refs[16:19], refs[19]
     side, core = place[2], place[1]
     b = pl.program_id(0)
     count = k_ref.shape[1] // (2 * ROWS)
@@ -398,15 +383,10 @@
                     out.append(pltpu.make_async_copy(ref.at[i], target, sem_v.at[n, i]))
             return out
 
-        loads = [
-            pltpu.make_async_copy(ref, table, sem_t.at[n])
-            for n, (ref, table) in enumerate(zip(table_refs, tables))
-        ]
-        for copy in loads + copies_v():
+        for copy in copies_v():
             copy.start()
-        for copy in loads:
-            copy.wait()
-        prepare(core, *qk_refs, *tables, q_wide, k_ref, corr, *refs[15:19])
+        fill_tables(weights, *tables)
+        prepare(core, *qk_refs, *tables, q_wide, k_ref, corr, *refs[12:16])
         for copy in copies_v():
             copy.wait()
 
@@ -481,7 +461,7 @@
         pl.when(b == step)(lambda step=step: block(step))
 
 
-def attend_head(place, mix, mine, other, tables, values):
+def attend_head(place, mix, weights, mine, other, values):
     total = 2 * mine.shape[0] * ROWS
     count = total // (2 * ROWS)
     depth = CQ * HD
@@ -491,7 +471,7 @@
         attend_kernel,
         grid=(count,),
         out_shape=(out, out),
-        in_specs=[whole(pltpu.SMEM)] * 2 + [whole(pltpu.VMEM)] * 2 + [whole(pl.ANY)] * 7,
+        in_specs=[whole(pltpu.SMEM)] * 3 + [whole(pltpu.VMEM)] * 2 + [whole(pl.ANY)] * 4,
         out_specs=[out_spec, out_spec],
         scratch_shapes=[
             pltpu.VMEM((total, GROUP * HD), jnp.bfloat16),
@@ -503,15 +483,18 @@
             pltpu.VMEM((2, total // 2, CQ * LANES), jnp.bfloat16),
             pltpu.VMEM((total, 2 * LANES), jnp.bfloat16),
         ]
-        + [pltpu.VMEM(table.shape, table.dtype) for table in tables]
-        + [pltpu.SemaphoreType.DMA((4, count)), pltpu.SemaphoreType.DMA((3,))],
-        compiler_params=kernel_params(36),
+        + [
+            pltpu.VMEM(shape, jnp.bfloat16)
+            for shape in ((2 * LANES, depth), (CQ * LANES, 2 * LANES), (CQ * LANES, LANES))
+        ]
+        + [pltpu.SemaphoreType.DMA((4, count))],
+        compiler_params=kernel_params(56),
         cost_estimate=pl.CostEstimate(
             flops=total * total * (depth + GROUP * HD),
             bytes_accessed=16 * 2**20,
             transcendentals=total * total // 2,
         ),
-    )(place, mix, mine, other, *tables, *values)
+    )(place, mix, weights, mine, other, *values)
 
 
 def finish_kernel(place, own, r1, r2, r3, gain, *refs):
@@ -606,11 +589,11 @@
     far = [swapped(block, "ctx", 2 * s) for s in (1, 2, 3)]
     x0, y0 = swapped(activations, "head", 1), swapped(activations, "head", 2)
     weights = lax.dynamic_index_in_dim(conv_kernel, ctx, 0, keepdims=False)
-    tables = tables_of(weights * (math.log2(math.e) / math.sqrt(HD)))
+    weights = weights * (math.log2(math.e) / math.sqrt(HD))
     place = jnp.stack([head, core, z % 2, z // 2, head, z, z ^ 1, z ^ 2, z ^ 3])
     place = place.astype(jnp.int32)
-    far, x0, y0, w_pieces, tables, place, w_out = barrier(
-        (far, x0, y0, w_pieces, tables, place, w_out)
+    far, x0, y0, w_pieces, weights, place, w_out = barrier(
+        (far, x0, y0, w_pieces, weights, place, w_out)
     )
 
     same_core = [[i for i in range(8) if i % 2 == k] for k in range(2)]
@@ -631,37 +614,38 @@
     cosine, sine = jnp.cos(angle), jnp.sin(angle)
     cosine = jnp.concatenate([cosine, cosine], -1)
     sine = jnp.concatenate([-sine, sine], -1)
+    w_same, x_rest, y_rest, d_rest, cosine, sine, w_out = barrier(
+        (w_same, x_rest, y_rest, d_rest, cosine, sine, w_out)
+    )
+    w_swap = swapped(w_same, "ctx", 1)
     middle = [(2, 4), (3, 5), (4, 2), (5, 3)]
     outward = [(2, 0), (3, 1), (4, 6), (5, 7)]
     out_near = swapped(w_out, "ctx", 2)
     out_across = lax.ppermute(w_out, "ctx", middle)
-    w_same, x_rest, y_rest, d_rest, cosine, sine, out_near, out_across = barrier(
-        (w_same, x_rest, y_rest, d_rest, cosine, sine, out_near, out_across)
-    )
-    w_swap = swapped(w_same, "ctx", 1)
+    sources = place, [activations] + list(far), (x0, x_rest, y0, y_rest, d_rest), w_same, w_swap
+    (v_pair,) = project(*sources)
+    place, v_pair, out_near, out_across = barrier((place, v_pair, out_near, out_across))
+    v_next = swapped(v_pair, "ctx", 2)
+    v_pair_other = swapped(v_pair, "ctx", 1)
     out_across_next = lax.ppermute(out_near, "ctx", middle)
     out_passed = lax.ppermute(out_across, "ctx", outward)
-    sources = place, [activations] + list(far), (x0, x_rest, y0, y_rest, d_rest), w_same, w_swap
-    (v_pair,) = project(*sources)
-    v_next = swapped(v_pair, "ctx", 2)
-    v_pair_other = swapped(v_pair, "ctx", 1)
-    out_own_swap = swapped(w_out, "ctx", 1)
-    place, v_pair = barrier((place, v_pair))
     mine, theirs = project(place, *sources[1:], (cosine, sine))
-    mine, theirs, v_next, v_pair_other, out_across_next, out_passed, out_own_swap = barrier(
-        (mine, theirs, v_next, v_pair_other, out_across_next, out_passed, out_own_swap)
-    )
-    out_passed_next = lax.ppermute(out_across_next, "ctx", outward)
+    mine, theirs, v_next, v_pair_other = barrier((mine, theirs, v_next, v_pair_other))
     other = swapped(theirs, "ctx", 1)
     v_next_other = swapped(v_next, "ctx", 1)
+    out_own_swap = swapped(w_out, "ctx", 1)
+    other, v_next_other, out_across_next, out_own_swap = barrier(
+        (other, v_next_other, out_across_next, out_own_swap)
+    )
+    out_passed_next = lax.ppermute(out_across_next, "ctx", outward)
     out_near_swap, out_across_swap = swapped(out_near, "ctx", 1), swapped(out_across, "ctx", 1)
     group_rows = lax.dynamic_slice_in_dim(head_mix, GROUP * (ctx // GROUP), GROUP, 0)
     mix = lax.dynamic_index_in_dim(group_rows, ctx % GROUP, 1, keepdims=False)
     out_mine, out_theirs = attend_head(
-        place, mix, mine, other, tables, (v_pair, v_next, v_pair_other, v_next_other)
-    )
-    out_mine, out_theirs, out_passed_next, out_near_swap, out_across_swap = barrier(
-        (out_mine, out_theirs, out_passed_next, out_near_swap, out_across_swap)
+        place, mix, weights, mine, other, (v_pair, v_next, v_pair_other, v_next_other)
+    )
+    out_mine, out_theirs, out_passed, out_passed_next, out_near_swap, out_across_swap = barrier(
+        (out_mine, out_theirs, out_passed, out_passed_next, out_near_swap, out_across_swap)
     )
     out_parts = [w_out, out_own_swap, out_near, out_near_swap, out_across, out_across_swap]
     for part in (out_passed, out_across_next, out_passed_next):

time: 291 us -> 303 us (1.041)
  waiting for transfers between devices: 165 us -> 190 us
  local copies, waits for them, and re-layouts: 33.1 us -> 16 us
  Pallas kernels: 37.7 us -> 41.8 us
    unnamed x88 -> x48, local copies, waits for them, and re-layouts: 25.1 us -> 6.61 us
    ppermute x27, waiting for transfers between devices: 148 us -> 165 us  [swapped(): return lax.ppermute(value, axis, [(i, i ^ mask) for i in range(count)])]
    ppermute x1, waiting for transfers between devices: 16.4 us -> 2.67 us  [per_device_one_head(): out_across = lax.ppermute(w_out, 'ctx', middle)]
    ppermute x1, waiting for transfers between devices: 0.01 us -> 12.1 us  [per_device_one_head(): out_passed_next = lax.ppermute(out_across_next, 'ctx', outward)]
    ppermute x1, waiting for transfers between devices: 0.01 us -> 9.7 us  [per_device_one_head(): out_across_next = lax.ppermute(out_near, 'ctx', middle)]
    ppermute x27, starting transfers between devices: 21 us -> 24.9 us  [swapped(): return lax.ppermute(value, axis, [(i, i ^ mask) for i in range(count)])]
    pallas_call x2, Pallas kernels: 13.6 us -> 17.3 us  [project(): pl.pallas_call(functools.partial(project_kernel, rows, first_col), out_sh...]
  transfers between devices with their start and end apart: 32 -> 32, of which waited for: 15 -> 18; matrix products, arithmetic and copies ran while one was open for 7% -> 7% of each run, Pallas kernels for 10% -> 11%
where the time goes in v7:
time: 303 us; the launch traced here: 302 us
  waiting for transfers between devices  190 us (63%)
  Pallas kernels  41.8 us (14%)
  starting transfers between devices  37.6 us (12%)
  other arithmetic  16.7 us (6%)
  local copies, waits for them, and re-layouts  16 us (5%)
    ppermute x27, waiting for transfers between devices, swapped(): return lax.ppermute(value, axis, [(i, i ^ mask) for i in range(count)])  165 us
    ppermute x27, starting transfers between devices, swapped(): return lax.ppermute(value, axis, [(i, i ^ mask) for i in range(count)])  24.9 us
    pallas_call x2, Pallas kernels, project(): pl.pallas_call(functools.partial(project_kernel, rows, first_col), out_sh...  17.3 us
    pallas_call x1, Pallas kernels, attend_head(): pl.pallas_call(attend_kernel, grid=(count,), out_shape=(out, out), in_spe...  16.7 us
    ppermute x1, waiting for transfers between devices, per_device_one_head(): out_passed_next = lax.ppermute(out_across_next, 'ctx', outward)  12.1 us
    ppermute x1, waiting for transfers between devices, per_device_one_head(): out_across_next = lax.ppermute(out_near, 'ctx', middle)  9.7 us
    pallas_call x1, Pallas kernels, finish(): pl.pallas_call(finish_kernel, in_specs=[whole(pltpu.SMEM)] + [whole(pltpu...  7.89 us
    unnamed x48, local copies, waits for them, and re-layouts  6.61 us
  transfers between devices with their start and end apart: 32, of which 18 were waited for; matrix products, arithmetic and copies ran while one was open for 7% of the time, Pallas kernels for 11%

profile of v7, /device:TPU:17, one launch (start us, length us, event | category | flops | bytes accessed | tf_op | source)
XLA Modules:
  0.0 302.1 jit_solution(6219480057970596620)
XLA Ops:
  0.0 0.8 fusion.11
  0.9 1.9 pad_maximum_fusion.5
  2.8 1.3 collective-permute-start
  4.1 1.3 collective-permute-start.2
  5.4 1.2 collective-permute-start.3
  6.7 1.2 collective-permute-start.4
  8.7 0.9 fusion.15
  9.6 0.9 fusion.14
  11.2 1.2 fusion.13.weights
  12.5 1.4 maximum_bitcast_fusion
  13.8 1.9 pad_maximum_fusion
  15.7 1.9 collective-permute-done.3.refs_4_
  17.7 0.9 collective-permute-done.4.refs_6_
  18.6 7.7 %collective-permute-done.refs_1_ = bf16[272,1024]{1,0:T(8,128)(2,1)S(1)} collective-permute-done((bf16[272,1024]{1,0:T(8,128)(2,1)}, bf16[272,1024]{1,0:T(8,128)(2,1)S(1)}, u32[]{:S(2)}, u32[]{:S(2)}) %collective-permute-start) | collective-permute-done | bytes 557088 | tf_op jit(solution)/shard_map/ppermute | solution.py:566
  26.3 2.0 collective-permute-done.1.refs_2_
  28.4 24.9 %collective-permute-done.2.refs_3_ = bf16[272,1024]{1,0:T(8,128)(2,1)S(1)} collective-permute-done((bf16[272,1024]{1,0:T(8,128)(2,1)}, bf16[272,1024]{1,0:T(8,128)(2,1)S(1)}, u32[]{:S(2)}, u32[]{:S(2)}) %collective-permute-start.2) | collective-permute-done | bytes 557088 | tf_op jit(solution)/shard_map/ppermute | solution.py:566
  53.3 0.8 copy-done.7
  54.1 3.7 %all-to-all-start = ((bf16[4,512,768]{2,1,0:T(8,128)(2,1)}), bf16[4,512,768]{2,1,0:T(8,128)(2,1)S(1)}, u32[]{:S(2)}, u32[]{:S(2)}) async-start(bf16[4,512,768]{2,1,0:T(8,128)(2,1)} %pad_maximum_fusion), calls=%async_computation | async-start | bytes 6291456 | tf_op jit(solution)/shard_map/all_to_all | solution.py:600
  57.8 1.1 slice.44
  58.9 1.1 slice.42
  60.0 1.0 slice.43
  61.5 1.3 collective-permute-start.5
  62.8 1.2 collective-permute-start.6
  65.2 1.9 fusion.3
  67.1 1.0 pad_maximum_fusion.6.refs_11_
  68.1 1.0 pad_maximum_fusion.7.refs_12_
  69.1 66.4 %collective-permute-done.7.refs_8_ = bf16[768,1024]{1,0:T(8,128)(2,1)S(1)} collective-permute-done((bf16[768,1024]{1,0:T(8,128)(2,1)S(1)}, bf16[768,1024]{1,0:T(8,128)(2,1)S(1)}, u32[]{:S(2)}, u32[]{:S(2)}) %collective-permute-start.7) | collective-permute-done | bytes 1572896 | tf_op jit(solution)/shard_map/ppermute | solution.py:566
  135.5 1.1 copy-done.9
  136.6 1.3 copy-done.8
  138.0 3.4 %collective-permute-start.8 = (bf16[4,512,768]{2,1,0:T(8,128)(2,1)S(1)}, bf16[4,512,768]{2,1,0:T(8,128)(2,1)S(1)}, u32[]{:S(2)}, u32[]{:S(2)}) collective-permute-start(bf16[4,512,768]{2,1,0:T(8,128)(2,1)S(1)} %all-to-all-done.refs_9_), channel_id=1, source_target_pairs={{0,4},{4,0},{8,12},{12,8},{16,20},{20,16},{24,28},{28,24},{1,5},{5... | collective-permute-start | bytes 9437192 | tf_op jit(solution)/shard_map/ppermute | solution.py:566
  141.3 1.1 collective-permute-start.9
  142.5 1.9 collective-permute-start.10
  144.4 2.2 collective-permute-done.8.refs_10_
  146.6 1.7 copy-done.2
  148.3 8.0 %shard_map.91.refs_2_ = bf16[4,256,256]{2,1,0:T(8,128)(2,1)} custom-call(s32[9]{0:T(128)} %stack.92.place, bf16[256,1024]{1,0:T(8,128)(2,1)} %refs_0_.3, bf16[272,1024]{1,0:T(8,128)(2,1)} %copy-done.3, bf16[272,1024]{1,0:T(8,128)(2,1)} %copy-done.5, bf16[272,1024]{1,0:T(8,128)(2,1)} %copy-done.7, bf16[256,1024]{1,0:T(8,128)(2,1)} %collective-permute-done.3.refs_4_, ...), custom_call_target="tpu_custom_call" | custom-call | flops 2147483648 | bytes 16777216 | tf_op jit(solution)/shard_map/pallas_call | solution.py:260
  156.4 10.0 %collective-permute-done.9.refs_2_ = bf16[1024,512]{1,0:T(8,128)(2,1)} collective-permute-done((bf16[1024,512]{1,0:T(8,128)(2,1)}, bf16[1024,512]{1,0:T(8,128)(2,1)}, u32[]{:S(2)}, u32[]{:S(2)}) %collective-permute-start.9) | collective-permute-done | bytes 1048608 | tf_op jit(solution)/shard_map/ppermute | solution.py:566
  166.4 2.7 collective-permute-done.10.refs_4_
  169.1 1.2 collective-permute-start.12
  170.3 1.9 collective-permute-start.15
  172.2 9.2 %shard_map.92 = (bf16[4,256,256]{2,1,0:T(8,128)(2,1)}, bf16[4,256,256]{2,1,0:T(8,128)(2,1)}) custom-call(s32[9]{0:T(128)} %stack.92.place, bf16[256,1024]{1,0:T(8,128)(2,1)} %refs_0_.3, bf16[272,1024]{1,0:T(8,128)(2,1)} %copy-done.3, bf16[272,1024]{1,0:T(8,128)(2,1)} %copy-done.5, bf16[272,1024]{1,0:T(8,128)(2,1)} %copy-done.7, ...), custom_call_target="tpu_custom_call" | custom-call | flops 4294967296 | bytes 16777216 | tf_op jit(solution)/shard_map/pallas_call | solution.py:260
  181.6 2.1 collective-permute-start.13
  184.2 2.9 collective-permute-start.17
  187.1 9.7 %collective-permute-done.15.refs_8_ = bf16[1024,512]{1,0:T(8,128)(2,1)} collective-permute-done((bf16[1024,512]{1,0:T(8,128)(2,1)}, bf16[1024,512]{1,0:T(8,128)(2,1)}, u32[]{:S(2)}, u32[]{:S(2)}) %collective-permute-start.15) | collective-permute-done | bytes 1048608 | tf_op jit(solution)/shard_map/ppermute | solution.py:630
  196.8 1.3 collective-permute-start.20
  198.9 0.8 copy-done.23
  199.7 2.3 collective-permute-start.18
  202.6 16.7 %shard_map.93 = (bf16[4,256,512]{2,1,0:T(8,128)(2,1)}, bf16[4,256,512]{2,1,0:T(8,128)(2,1)}) custom-call(s32[9]{0:T(128)} %stack.92.place, f32[4]{0:T(128)} %dynamic-slice_bitcast_fusion.1.mix, f32[66]{0:T(128)} %fusion.13.weights, bf16[4,256,256]{2,1,0:T(8,128)(2,1)} %get-tuple-element.67.refs_0_, bf16[4,256,256]{2,1,0:T(8,128)(2,1)} %copy-done.22, ...), custom_call_target="tpu_custom_call" | custom-call | flops 5368709120 | bytes 16777216 | tf_op jit(solution)/shard_map/pallas_call | solution.py:470
  219.3 12.1 %collective-permute-done.18.refs_10_ = bf16[1024,512]{1,0:T(8,128)(2,1)} collective-permute-done((bf16[1024,512]{1,0:T(8,128)(2,1)}, bf16[1024,512]{1,0:T(8,128)(2,1)}, u32[]{:S(2)}, u32[]{:S(2)}) %collective-permute-start.18) | collective-permute-done | bytes 1048608 | tf_op jit(solution)/shard_map/ppermute | solution.py:640
  231.4 0.8 collective-permute-start.21
  232.8 3.6 %collective-permute-done.21 = bf16[4,256,512]{2,1,0:T(8,128)(2,1)} collective-permute-done((bf16[4,256,512]{2,1,0:T(8,128)(2,1)}, bf16[4,256,512]{2,1,0:T(8,128)(2,1)}, u32[]{:S(2)}, u32[]{:S(2)}) %collective-permute-start.21) | collective-permute-done | bytes 1048608 | tf_op jit(solution)/shard_map/ppermute | solution.py:566
  236.3 1.9 convert_add_fusion
  238.2 0.9 fusion.2
  239.1 2.2 collective-permute-start.22
  241.4 1.1 collective-permute-start.24
  243.2 0.8 dynamic-slice_bitcast_fusion.own
  244.0 7.5 %collective-permute-done.22.r1 = bf16[256,512]{1,0:T(8,128)(2,1)S(1)} collective-permute-done((bf16[256,512]{1,0:T(8,128)(2,1)}, bf16[256,512]{1,0:T(8,128)(2,1)S(1)}, u32[]{:S(2)}, u32[]{:S(2)}) %collective-permute-start.22) | collective-permute-done | bytes 262176 | tf_op jit(solution)/shard_map/ppermute | solution.py:566
  251.5 2.2 collective-permute-done.23.r2
  253.7 12.0 %collective-permute-done.24.r3 = bf16[256,512]{1,0:T(8,128)(2,1)} collective-permute-done((bf16[256,512]{1,0:T(8,128)(2,1)}, bf16[256,512]{1,0:T(8,128)(2,1)}, u32[]{:S(2)}, u32[]{:S(2)}) %collective-permute-start.24) | collective-permute-done | bytes 262176 | tf_op jit(solution)/shard_map/ppermute | solution.py:566
  265.8 7.9 %shard_map.94 = (bf16[256,1024]{1,0:T(8,128)(2,1)}, bf16[256,1024]{1,0:T(8,128)(2,1)}, bf16[256,1024]{1,0:T(8,128)(2,1)}, bf16[256,1024]{1,0:T(8,128)(2,1)}) custom-call(s32[10]{0:T(128)} %concatenate.47.place, f32[256,512]{1,0:T(8,128)} %dynamic-slice_bitcast_fusion.own, bf16[256,512]{1,0:T(8,128)(2,1)} %copy-done.18, ...), custom_call_target="tpu_custom_call" | custom-call | flops 2147483648 | bytes 11534336 | tf_op jit(solution)/shard_map/pallas_call | solution.py:547
  273.7 1.2 collective-permute-start.30
  274.9 1.1 collective-permute-start.29
  276.4 10.7 %collective-permute-done.30 = bf16[256,1024]{1,0:T(8,128)(2,1)S(1)} collective-permute-done((bf16[256,1024]{1,0:T(8,128)(2,1)}, bf16[256,1024]{1,0:T(8,128)(2,1)S(1)}, u32[]{:S(2)}, u32[]{:S(2)}) %collective-permute-start.30) | collective-permute-done | bytes 524320 | tf_op jit(solution)/shard_map/ppermute | solution.py:566
  287.1 12.8 %collective-permute-done.29 = bf16[256,1024]{1,0:T(8,128)(2,1)S(1)} collective-permute-done((bf16[256,1024]{1,0:T(8,128)(2,1)}, bf16[256,1024]{1,0:T(8,128)(2,1)S(1)}, u32[]{:S(2)}, u32[]{:S(2)}) %collective-permute-start.29) | collective-permute-done | bytes 524320 | tf_op jit(solution)/shard_map/ppermute | solution.py:566
  299.9 2.2 add_convert_fusion
  (87 shorter events, 7.2 us)
Async XLA Ops:
  0.0 202.0 %copy-start = (f32[8,4]{0,1:T(4,128)S(1)}, f32[8,4]{0,1:T(4,128)}, u32[]{:S(2)}) copy-start(f32[8,4]{0,1:T(4,128)} %param.15) | copy-start | bytes 388
  0.0 7.9 %copy-start.15 = (bf16[512,1024]{1,0:T(8,128)(2,1)S(1)}, bf16[512,1024]{1,0:T(8,128)(2,1)}, u32[]{:S(2)}) copy-start(bf16[512,1024]{1,0:T(8,128)(2,1)} %param.13) | copy-start | bytes 3145732
  0.0 8.7 %copy-start.16 = (bf16[512,1024]{1,0:T(8,128)(2,1)S(1)}, bf16[512,1024]{1,0:T(8,128)(2,1)}, u32[]{:S(2)}) copy-start(bf16[512,1024]{1,0:T(8,128)(2,1)} %param.12) | copy-start | bytes 3145732
  2.8 6.8 %copy-start.17 = (bf16[512,1024]{1,0:T(8,128)(2,1)S(1)}, bf16[512,1024]{1,0:T(8,128)(2,1)}, u32[]{:S(2)}) copy-start(bf16[512,1024]{1,0:T(8,128)(2,1)} %param.11) | copy-start | bytes 3145732
  2.8 23.5 %collective-permute-start = (bf16[272,1024]{1,0:T(8,128)(2,1)}, bf16[272,1024]{1,0:T(8,128)(2,1)S(1)}, u32[]{:S(2)}, u32[]{:S(2)}) collective-permute-start(bf16[272,1024]{1,0:T(8,128)(2,1)} %pad_maximum_fusion.5), channel_id=1, source_target_pairs={{0,8},{4,12},{8,0},{12,4},{16,24},{20,28},{24,16},{28,20},{1,9},{5... | collective-permute-start | bytes 1671176 | tf_op jit(solution)/shard_map/ppermute | solution.py:566
  4.1 24.3 %collective-permute-start.1 = (bf16[272,1024]{1,0:T(8,128)(2,1)}, bf16[272,1024]{1,0:T(8,128)(2,1)S(1)}, u32[]{:S(2)}, u32[]{:S(2)}) collective-permute-start(bf16[272,1024]{1,0:T(8,128)(2,1)} %pad_maximum_fusion.5), channel_id=1, source_target_pairs={{0,16},{4,20},{8,24},{12,28},{16,0},{20,4},{24,8},{28,12},{1,17},{... | collective-permute-start | bytes 1671176 | tf_op jit(solution)/shard_map/ppermute | solution.py:566
  4.1 49.1 %collective-permute-start.2 = (bf16[272,1024]{1,0:T(8,128)(2,1)}, bf16[272,1024]{1,0:T(8,128)(2,1)S(1)}, u32[]{:S(2)}, u32[]{:S(2)}) collective-permute-start(bf16[272,1024]{1,0:T(8,128)(2,1)} %pad_maximum_fusion.5), channel_id=1, source_target_pairs={{0,24},{4,28},{8,16},{12,20},{16,8},{20,12},{24,0},{28,4},{1,25},{... | collective-permute-start | bytes 1671176 | tf_op jit(solution)/shard_map/ppermute | solution.py:566
  5.4 12.2 %collective-permute-start.3 = (bf16[256,1024]{1,0:T(8,128)(2,1)}, bf16[256,1024]{1,0:T(8,128)(2,1)}, u32[]{:S(2)}, u32[]{:S(2)}) collective-permute-start(bf16[256,1024]{1,0:T(8,128)(2,1)} %refs_0_.3), channel_id=1, source_target_pairs={{0,1},{1,0},{2,3},{3,2},{4,5},{5,4},{6,7},{7,6},{8,9},{9,8},{10,11... | collective-permute-start | bytes 1572872 | tf_op jit(solution)/shard_map/ppermute | solution.py:566
  6.7 11.9 %collective-permute-start.4 = (bf16[256,1024]{1,0:T(8,128)(2,1)}, bf16[256,1024]{1,0:T(8,128)(2,1)}, u32[]{:S(2)}, u32[]{:S(2)}) collective-permute-start(bf16[256,1024]{1,0:T(8,128)(2,1)} %refs_0_.3), channel_id=1, source_target_pairs={{0,2},{1,3},{2,0},{3,1},{4,6},{5,7},{6,4},{7,5},{8,10},{9,11},{10,... | collective-permute-start | bytes 1572872 | tf_op jit(solution)/shard_map/ppermute | solution.py:566
  26.3 27.0 %copy-start.3 = (bf16[272,1024]{1,0:T(8,128)(2,1)}, bf16[272,1024]{1,0:T(8,128)(2,1)S(1)}, u32[]{:S(2)}) copy-start(bf16[272,1024]{1,0:T(8,128)(2,1)S(1)} %collective-permute-done.refs_1_) | copy-start | bytes 1671172
  28.4 24.9 %copy-start.5 = (bf16[272,1024]{1,0:T(8,128)(2,1)}, bf16[272,1024]{1,0:T(8,128)(2,1)S(1)}, u32[]{:S(2)}) copy-start(bf16[272,1024]{1,0:T(8,128)(2,1)S(1)} %collective-permute-done.1.refs_2_) | copy-start | bytes 1671172
  53.3 0.8 copy-start.7
  54.1 83.9 %all-to-all-start = ((bf16[4,512,768]{2,1,0:T(8,128)(2,1)}), bf16[4,512,768]{2,1,0:T(8,128)(2,1)S(1)}, u32[]{:S(2)}, u32[]{:S(2)}) async-start(bf16[4,512,768]{2,1,0:T(8,128)(2,1)} %pad_maximum_fusion), calls=%async_computation | async-start | bytes 6291456 | tf_op jit(solution)/shard_map/all_to_all | solution.py:600
  57.8 2.2 copy-start.6
  57.8 2.2 copy-start.4
  61.5 74.0 %collective-permute-start.5 = (bf16[896,1024]{1,0:T(8,128)(2,1)S(1)}, bf16[896,1024]{1,0:T(8,128)(2,1)S(1)}, u32[]{:S(2)}, u32[]{:S(2)}) collective-permute-start(bf16[896,1024]{1,0:T(8,128)(2,1)S(1)} %get-tuple-element.93), channel_id=1, source_target_pairs={{0,1},{1,0},{2,3},{3,2},{4,5},{5,4},{6,7},{7,6},{8,9},{9,8},{10,11... | collective-permute-start | bytes 5505032 | tf_op jit(solution)/shard_map/ppermute | solution.py:566
  62.8 75.2 %collective-permute-start.6 = (bf16[896,1024]{1,0:T(8,128)(2,1)S(1)}, bf16[896,1024]{1,0:T(8,128)(2,1)}, u32[]{:S(2)}, u32[]{:S(2)}) collective-permute-start(bf16[896,1024]{1,0:T(8,128)(2,1)S(1)} %get-tuple-element.92), channel_id=1, source_target_pairs={{0,2},{1,3},{2,0},{3,1},{4,6},{5,7},{6,4},{7,5},{8,10},{9,11},{10,... | collective-permute-start | bytes 5505032 | tf_op jit(solution)/shard_map/ppermute | solution.py:566
  64.2 71.3 %collective-permute-start.7 = (bf16[768,1024]{1,0:T(8,128)(2,1)S(1)}, bf16[768,1024]{1,0:T(8,128)(2,1)S(1)}, u32[]{:S(2)}, u32[]{:S(2)}) collective-permute-start(bf16[768,1024]{1,0:T(8,128)(2,1)S(1)} %pad_maximum_fusion.4), channel_id=1, source_target_pairs={{0,3},{1,2},{2,1},{3,0},{4,7},{5,6},{6,5},{7,4},{8,11},{9,10},{10,... | collective-permute-start | bytes 4718600 | tf_op jit(solution)/shard_map/ppermute | solution.py:566
  135.5 1.1 copy-start.9
  136.6 1.3 copy-start.8
  138.0 8.7 %copy-start.1 = (bf16[4,512,768]{2,1,0:T(8,128)(2,1)}, bf16[4,512,768]{2,1,0:T(8,128)(2,1)S(1)}, u32[]{:S(2)}) copy-start(bf16[4,512,768]{2,1,0:T(8,128)(2,1)S(1)} %all-to-all-done.refs_9_) | copy-start | bytes 9437188
  138.0 32.3 %copy-start.10 = (bf16[1024,512]{1,0:T(8,128)(2,1)S(1)}, bf16[1024,512]{1,0:T(8,128)(2,1)}, u32[]{:S(2)}) copy-start(bf16[1024,512]{1,0:T(8,128)(2,1)} %refs_0_.4) | copy-start | bytes 3145732
  138.0 8.6 %collective-permute-start.8 = (bf16[4,512,768]{2,1,0:T(8,128)(2,1)S(1)}, bf16[4,512,768]{2,1,0:T(8,128)(2,1)S(1)}, u32[]{:S(2)}, u32[]{:S(2)}) collective-permute-start(bf16[4,512,768]{2,1,0:T(8,128)(2,1)S(1)} %all-to-all-done.refs_9_), channel_id=1, source_target_pairs={{0,4},{4,0},{8,12},{12,8},{16,20},{20,16},{24,28},{28,24},{1,5},{5... | collective-permute-start | bytes 9437192 | tf_op jit(solution)/shard_map/ppermute | solution.py:566
  141.3 25.1 %collective-permute-start.9 = (bf16[1024,512]{1,0:T(8,128)(2,1)}, bf16[1024,512]{1,0:T(8,128)(2,1)}, u32[]{:S(2)}, u32[]{:S(2)}) collective-permute-start(bf16[1024,512]{1,0:T(8,128)(2,1)} %refs_0_.4), channel_id=1, source_target_pairs={{0,8},{4,12},{8,0},{12,4},{16,24},{20,28},{24,16},{28,20},{1,9},{5... | collective-permute-start | bytes 3145736 | tf_op jit(solution)/shard_map/ppermute | solution.py:566
  142.5 26.6 %collective-permute-start.10 = (bf16[1024,512]{1,0:T(8,128)(2,1)}, bf16[1024,512]{1,0:T(8,128)(2,1)}, u32[]{:S(2)}, u32[]{:S(2)}) collective-permute-start(bf16[1024,512]{1,0:T(8,128)(2,1)} %refs_0_.4), channel_id=1, source_target_pairs={{8,16},{12,20},{16,8},{20,12},{9,17},{13,21},{17,9},{21,13},{10,18... | collective-permute-start | bytes 3145736 | tf_op jit(solution)/shard_map/ppermute | solution.py:624
  146.6 1.7 copy-start.2
  169.1 12.6 %collective-permute-start.11 = (bf16[4,256,256]{2,1,0:T(8,128)(2,1)}, bf16[4,256,256]{2,1,0:T(8,128)(2,1)S(1)}, u32[]{:S(2)}, u32[]{:S(2)}) collective-permute-start(bf16[4,256,256]{2,1,0:T(8,128)(2,1)} %shard_map.91.refs_2_), channel_id=1, source_target_pairs={{0,8},{4,12},{8,0},{12,4},{16,24},{20,28},{24,16},{28,20},{1,9},{5... | collective-permute-start | bytes 1572872 | tf_op jit(solution)/shard_map/ppermute | solution.py:566
  169.1 12.6 %collective-permute-start.12 = (bf16[4,256,256]{2,1,0:T(8,128)(2,1)}, bf16[4,256,256]{2,1,0:T(8,128)(2,1)S(1)}, u32[]{:S(2)}, u32[]{:S(2)}) collective-permute-start(bf16[4,256,256]{2,1,0:T(8,128)(2,1)} %shard_map.91.refs_2_), channel_id=1, source_target_pairs={{0,4},{4,0},{8,12},{12,8},{16,20},{20,16},{24,28},{28,24},{1,5},{5... | collective-permute-start | bytes 1572872 | tf_op jit(solution)/shard_map/ppermute | solution.py:566
  170.2 14.0 %collective-permute-start.16 = (bf16[1024,512]{1,0:T(8,128)(2,1)S(1)}, bf16[1024,512]{1,0:T(8,128)(2,1)S(1)}, u32[]{:S(2)}, u32[]{:S(2)}) collective-permute-start(bf16[1024,512]{1,0:T(8,128)(2,1)S(1)} %copy-done.10), channel_id=1, source_target_pairs={{0,4},{4,0},{8,12},{12,8},{16,20},{20,16},{24,28},{28,24},{1,5},{5... | collective-permute-start | bytes 3145736 | tf_op jit(solution)/shard_map/ppermute | solution.py:566
  170.3 26.5 %collective-permute-start.15 = (bf16[1024,512]{1,0:T(8,128)(2,1)}, bf16[1024,512]{1,0:T(8,128)(2,1)}, u32[]{:S(2)}, u32[]{:S(2)}) collective-permute-start(bf16[1024,512]{1,0:T(8,128)(2,1)} %collective-permute-done.9.refs_2_), channel_id=1, source_target_pairs={{8,16},{12,20},{16,8},{20,12},{9,17},{13,21},{17,9},{21,13},{10,18... | collective-permute-start | bytes 3145736 | tf_op jit(solution)/shard_map/ppermute | solution.py:630
  181.6 5.5 %copy-start.20 = (bf16[4,256,256]{2,1,0:T(8,128)(2,1)}, bf16[4,256,256]{2,1,0:T(8,128)(2,1)S(1)}, u32[]{:S(2)}) copy-start(bf16[4,256,256]{2,1,0:T(8,128)(2,1)S(1)} %collective-permute-done.11.refs_3_) | copy-start | bytes 1572868
  181.6 16.5 %copy-start.21 = (bf16[4,256,256]{2,1,0:T(8,128)(2,1)}, bf16[4,256,256]{2,1,0:T(8,128)(2,1)S(1)}, u32[]{:S(2)}) copy-start(bf16[4,256,256]{2,1,0:T(8,128)(2,1)S(1)} %collective-permute-done.12.refs_4_) | copy-start | bytes 1572868
  181.6 16.5 %collective-permute-start.13 = (bf16[4,256,256]{2,1,0:T(8,128)(2,1)}, bf16[4,256,256]{2,1,0:T(8,128)(2,1)S(1)}, u32[]{:S(2)}, u32[]{:S(2)}) collective-permute-start(bf16[4,256,256]{2,1,0:T(8,128)(2,1)} %get-tuple-element.68), channel_id=1, source_target_pairs={{0,4},{4,0},{8,12},{12,8},{16,20},{20,16},{24,28},{28,24},{1,5},{5... | collective-permute-start | bytes 1572872 | tf_op jit(solution)/shard_map/ppermute | solution.py:566
  183.7 14.4 %collective-permute-start.14 = (bf16[4,256,256]{2,1,0:T(8,128)(2,1)S(1)}, bf16[4,256,256]{2,1,0:T(8,128)(2,1)S(1)}, u32[]{:S(2)}, u32[]{:S(2)}) collective-permute-start(bf16[4,256,256]{2,1,0:T(8,128)(2,1)S(1)} %collective-permute-done.11.refs_3_), channel_id=1, source_target_pairs={{0,4},{4,0},{8,12},{12,8},{16,20},{20,16},{24,28},{28,24},{1,5},{5... | collective-permute-start | bytes 1572872 | tf_op jit(solution)/shard_map/ppermute | solution.py:566
  183.8 35.5 %collective-permute-start.19 = (bf16[1024,512]{1,0:T(8,128)(2,1)}, bf16[1024,512]{1,0:T(8,128)(2,1)S(1)}, u32[]{:S(2)}, u32[]{:S(2)}) collective-permute-start(bf16[1024,512]{1,0:T(8,128)(2,1)} %collective-permute-done.9.refs_2_), channel_id=1, source_target_pairs={{0,4},{4,0},{8,12},{12,8},{16,20},{20,16},{24,28},{28,24},{1,5},{5... | collective-permute-start | bytes 3145736 | tf_op jit(solution)/shard_map/ppermute | solution.py:566
  184.2 35.1 %copy-start.11 = (bf16[1024,512]{1,0:T(8,128)(2,1)}, bf16[1024,512]{1,0:T(8,128)(2,1)S(1)}, u32[]{:S(2)}) copy-start(bf16[1024,512]{1,0:T(8,128)(2,1)S(1)} %collective-permute-done.16.refs_1_) | copy-start | bytes 3145732
  184.2 35.1 %collective-permute-start.17 = (bf16[1024,512]{1,0:T(8,128)(2,1)}, bf16[1024,512]{1,0:T(8,128)(2,1)}, u32[]{:S(2)}, u32[]{:S(2)}) collective-permute-start(bf16[1024,512]{1,0:T(8,128)(2,1)} %collective-permute-done.10.refs_4_), channel_id=1, source_target_pairs={{8,0},{12,4},{16,24},{20,28},{9,1},{13,5},{17,25},{21,29},{10,2},{... | collective-permute-start | bytes 3145736 | tf_op jit(solution)/shard_map/ppermute | solution.py:631
  196.8 22.5 %collective-permute-start.20 = (bf16[1024,512]{1,0:T(8,128)(2,1)}, bf16[1024,512]{1,0:T(8,128)(2,1)S(1)}, u32[]{:S(2)}, u32[]{:S(2)}) collective-permute-start(bf16[1024,512]{1,0:T(8,128)(2,1)} %collective-permute-done.10.refs_4_), channel_id=1, source_target_pairs={{0,4},{4,0},{8,12},{12,8},{16,20},{20,16},{24,28},{28,24},{1,5},{5... | collective-permute-start | bytes 3145736 | tf_op jit(solution)/shard_map/ppermute | solution.py:566
  198.1 0.8 copy-start.22
  198.9 0.8 copy-start.23
  199.7 31.7 %collective-permute-start.18 = (bf16[1024,512]{1,0:T(8,128)(2,1)}, bf16[1024,512]{1,0:T(8,128)(2,1)}, u32[]{:S(2)}, u32[]{:S(2)}) collective-permute-start(bf16[1024,512]{1,0:T(8,128)(2,1)} %collective-permute-done.15.refs_8_), channel_id=1, source_target_pairs={{8,0},{12,4},{16,24},{20,28},{9,1},{13,5},{17,25},{21,29},{10,2},{... | collective-permute-start | bytes 3145736 | tf_op jit(solution)/shard_map/ppermute | solution.py:640
  219.3 13.5 %copy-start.12 = (bf16[1024,512]{1,0:T(8,128)(2,1)}, bf16[1024,512]{1,0:T(8,128)(2,1)S(1)}, u32[]{:S(2)}) copy-start(bf16[1024,512]{1,0:T(8,128)(2,1)S(1)} %collective-permute-done.19.refs_3_) | copy-start | bytes 3145732
  219.3 13.4 %copy-start.13 = (bf16[1024,512]{1,0:T(8,128)(2,1)}, bf16[1024,512]{1,0:T(8,128)(2,1)S(1)}, u32[]{:S(2)}) copy-start(bf16[1024,512]{1,0:T(8,128)(2,1)S(1)} %collective-permute-done.20.refs_5_) | copy-start | bytes 3145732
  231.4 4.9 %collective-permute-start.21 = (bf16[4,256,512]{2,1,0:T(8,128)(2,1)}, bf16[4,256,512]{2,1,0:T(8,128)(2,1)}, u32[]{:S(2)}, u32[]{:S(2)}) collective-permute-start(bf16[4,256,512]{2,1,0:T(8,128)(2,1)} %get-tuple-element.79), channel_id=1, source_target_pairs={{0,4},{4,0},{8,12},{12,8},{16,20},{20,16},{24,28},{28,24},{1,5},{5... | collective-permute-start | bytes 3145736 | tf_op jit(solution)/shard_map/ppermute | solution.py:566
  232.3 9.1 %collective-permute-start.26 = (bf16[1024,512]{1,0:T(8,128)(2,1)}, bf16[1024,512]{1,0:T(8,128)(2,1)S(1)}, u32[]{:S(2)}, u32[]{:S(2)}) collective-permute-start(bf16[1024,512]{1,0:T(8,128)(2,1)} %collective-permute-done.15.refs_8_), channel_id=1, source_target_pairs={{0,4},{4,0},{8,12},{12,8},{16,20},{20,16},{24,28},{28,24},{1,5},{5... | collective-permute-start | bytes 3145736 | tf_op jit(solution)/shard_map/ppermute | solution.py:566
  232.3 11.8 %collective-permute-start.25 = (bf16[1024,512]{1,0:T(8,128)(2,1)}, bf16[1024,512]{1,0:T(8,128)(2,1)}, u32[]{:S(2)}, u32[]{:S(2)}) collective-permute-start(bf16[1024,512]{1,0:T(8,128)(2,1)} %collective-permute-done.17.refs_6_), channel_id=1, source_target_pairs={{0,4},{4,0},{8,12},{12,8},{16,20},{20,16},{24,28},{28,24},{1,5},{5... | collective-permute-start | bytes 3145736 | tf_op jit(solution)/shard_map/ppermute | solution.py:566
  232.8 11.3 %collective-permute-start.27 = (bf16[1024,512]{1,0:T(8,128)(2,1)}, bf16[1024,512]{1,0:T(8,128)(2,1)}, u32[]{:S(2)}, u32[]{:S(2)}) collective-permute-start(bf16[1024,512]{1,0:T(8,128)(2,1)} %collective-permute-done.18.refs_10_), channel_id=1, source_target_pairs={{0,4},{4,0},{8,12},{12,8},{16,20},{20,16},{24,28},{28,24},{1,5},{5... | collective-permute-start | bytes 3145736 | tf_op jit(solution)/shard_map/ppermute | solution.py:566
  232.8 9.7 %copy-start.19 = (s32[9]{0:T(128)S(1)}, s32[9]{0:T(128)}, u32[]{:S(2)}) copy-start(s32[9]{0:T(128)} %stack.92.place) | copy-start | bytes 112
  239.1 12.4 %collective-permute-start.22 = (bf16[256,512]{1,0:T(8,128)(2,1)}, bf16[256,512]{1,0:T(8,128)(2,1)S(1)}, u32[]{:S(2)}, u32[]{:S(2)}) collective-permute-start(bf16[256,512]{1,0:T(8,128)(2,1)} %get-tuple-element.91), channel_id=1, source_target_pairs={{0,8},{4,12},{8,0},{12,4},{16,24},{20,28},{24,16},{28,20},{1,9},{5... | collective-permute-start | bytes 786440 | tf_op jit(solution)/shard_map/ppermute | solution.py:566
  241.3 12.4 %collective-permute-start.23 = (bf16[256,512]{1,0:T(8,128)(2,1)}, bf16[256,512]{1,0:T(8,128)(2,1)}, u32[]{:S(2)}, u32[]{:S(2)}) collective-permute-start(bf16[256,512]{1,0:T(8,128)(2,1)} %get-tuple-element.90), channel_id=1, source_target_pairs={{0,16},{4,20},{8,24},{12,28},{16,0},{20,4},{24,8},{28,12},{1,17},{... | collective-permute-start | bytes 786440 | tf_op jit(solution)/shard_map/ppermute | solution.py:566
  241.4 24.4 %copy-start.14 = (bf16[1024,512]{1,0:T(8,128)(2,1)}, bf16[1024,512]{1,0:T(8,128)(2,1)S(1)}, u32[]{:S(2)}) copy-start(bf16[1024,512]{1,0:T(8,128)(2,1)S(1)} %collective-permute-done.26.refs_9_) | copy-start | bytes 3145732
  241.4 24.4 %collective-permute-start.24 = (bf16[256,512]{1,0:T(8,128)(2,1)}, bf16[256,512]{1,0:T(8,128)(2,1)}, u32[]{:S(2)}, u32[]{:S(2)}) collective-permute-start(bf16[256,512]{1,0:T(8,128)(2,1)} %get-tuple-element.89), channel_id=1, source_target_pairs={{0,24},{4,28},{8,16},{12,20},{16,8},{20,12},{24,0},{28,4},{1,25},{... | collective-permute-start | bytes 786440 | tf_op jit(solution)/shard_map/ppermute | solution.py:566
  251.5 14.3 %copy-start.18 = (bf16[256,512]{1,0:T(8,128)(2,1)}, bf16[256,512]{1,0:T(8,128)(2,1)S(1)}, u32[]{:S(2)}) copy-start(bf16[256,512]{1,0:T(8,128)(2,1)S(1)} %collective-permute-done.22.r1) | copy-start | bytes 786436
  273.7 13.4 %collective-permute-start.30 = (bf16[256,1024]{1,0:T(8,128)(2,1)}, bf16[256,1024]{1,0:T(8,128)(2,1)S(1)}, u32[]{:S(2)}, u32[]{:S(2)}) collective-permute-start(bf16[256,1024]{1,0:T(8,128)(2,1)} %get-tuple-element.88), channel_id=1, source_target_pairs={{0,3},{1,2},{2,1},{3,0},{4,7},{5,6},{6,5},{7,4},{8,11},{9,10},{10,... | collective-permute-start | bytes 1572872 | tf_op jit(solution)/shard_map/ppermute | solution.py:566
  274.9 25.0 %collective-permute-start.29 = (bf16[256,1024]{1,0:T(8,128)(2,1)}, bf16[256,1024]{1,0:T(8,128)(2,1)S(1)}, u32[]{:S(2)}, u32[]{:S(2)}) collective-permute-start(bf16[256,1024]{1,0:T(8,128)(2,1)} %get-tuple-element.87), channel_id=1, source_target_pairs={{0,2},{1,3},{2,0},{3,1},{4,6},{5,7},{6,4},{7,5},{8,10},{9,11},{10,... | collective-permute-start | bytes 1572872 | tf_op jit(solution)/shard_map/ppermute | solution.py:566
  276.0 23.9 %collective-permute-start.28 = (bf16[256,1024]{1,0:T(8,128)(2,1)}, bf16[256,1024]{1,0:T(8,128)(2,1)S(1)}, u32[]{:S(2)}, u32[]{:S(2)}) collective-permute-start(bf16[256,1024]{1,0:T(8,128)(2,1)} %get-tuple-element.86), channel_id=1, source_target_pairs={{0,1},{1,0},{2,3},{3,2},{4,5},{5,4},{6,7},{7,6},{8,9},{9,8},{10,11... | collective-permute-start | bytes 1572872 | tf_op jit(solution)/shard_map/ppermute | solution.py:566

commit v8 on v7

--- a/solution.py
+++ b/solution.py
@@ -192,8 +192,8 @@
 
 
 def project_kernel(rows, first_col, place, *refs):
-    a_own, (x0, x_rest, y0, y_rest, d_rest) = refs[:4], refs[4:9]
-    w_same, w_swap = refs[9:11]
+    a_own, (x0, x_rest, y0, y_rest, c_low, c_high) = refs[:4], refs[4:10]
+    w_same, w_swap = refs[10:12]
     abuf, wbuf, acc, sem_a, sem_w = refs[-5:]
     turn, core = place[0], place[1]
     half = w_same.shape[1]
@@ -207,7 +207,8 @@
             pairs = [(first, 0, 0, rows), (others, 0, rows, 3 * rows)]
         else:
             late, mid = 3 * rows, rows // 2
-            pairs = [(y_rest, late, 0, mid), (x_rest, late, mid, mid), (d_rest, 0, rows, 3 * rows)]
+            pairs = [(y_rest, late, 0, mid), (x_rest, late, mid, mid)]
+            pairs += [(c_low, 0, rows, 3 * mid), (c_high, 0, rows + 3 * mid, 3 * mid)]
         return [
             pltpu.make_async_copy(
                 ref.at[pl.ds(source, size)], abuf.at[t, pl.ds(target, size)], sem_a.at[t, n]
@@ -232,11 +233,11 @@
         part = jnp.dot(abuf[t], wbuf[t], preferred_element_type=jnp.float32)
         acc[...] = part if t == 0 else acc[...] + part
     if first_col:
-        v_out = refs[11]
+        v_out = refs[12]
         for b in range(4):
             v_out[place[5 + b]] = acc[b * rows : (b + 1) * rows].astype(jnp.bfloat16)
         return
-    cos_ref, sin_ref, mine, theirs = refs[11:15]
+    cos_ref, sin_ref, mine, theirs = refs[12:16]
     first = core == 0
     for b in range(4):
         total = acc[b * rows : (b + 1) * rows]
@@ -261,7 +262,7 @@
         functools.partial(project_kernel, rows, first_col),
         out_shape=[out] * count,
         in_specs=[whole(pltpu.SMEM)]
-        + [whole(pl.ANY)] * 11
+        + [whole(pl.ANY)] * 12
         + [whole(pltpu.VMEM)] * len(angles),
         out_specs=[whole(pltpu.VMEM)] * count,
         scratch_shapes=[
@@ -597,11 +598,11 @@
     )
 
     same_core = [[i for i in range(8) if i % 2 == k] for k in range(2)]
+    inside = [a[:rows] for a in far]
+    to_x, to_y = jnp.concatenate(inside + [y0[half:]]), jnp.concatenate(inside + [x0[:half]])
+    to_x, to_y, w_pieces = barrier((to_x, to_y, w_pieces))
+    x_rest, y_rest = swapped(to_x, "head", 1), swapped(to_y, "head", 2)
     w_same = lax.all_to_all(w_pieces, "ctx", 0, 0, axis_index_groups=same_core)
-    inner = [a[:rows] for a in far]
-    x_rest = swapped(jnp.concatenate(inner + [y0[half:]]), "head", 1)
-    y_rest = swapped(jnp.concatenate(inner + [x0[:half]]), "head", 2)
-    d_rest = swapped(jnp.concatenate(inner), "head", 3)
     place_of = jnp.stack(
         [
             a[rows, :rows].astype(jnp.float32) * 256.0 + a[rows + 1, :rows].astype(jnp.float32)
@@ -614,17 +615,20 @@
     cosine, sine = jnp.cos(angle), jnp.sin(angle)
     cosine = jnp.concatenate([cosine, cosine], -1)
     sine = jnp.concatenate([-sine, sine], -1)
-    w_same, x_rest, y_rest, d_rest, cosine, sine, w_out = barrier(
-        (w_same, x_rest, y_rest, d_rest, cosine, sine, w_out)
-    )
-    w_swap = swapped(w_same, "ctx", 1)
+    x_rest, y_rest, cosine, sine, w_out = barrier((x_rest, y_rest, cosine, sine, w_out))
+    c_low = swapped(x_rest[: 3 * half], "head", 2)
+    c_high = swapped(y_rest[3 * half : 3 * rows], "head", 1)
     middle = [(2, 4), (3, 5), (4, 2), (5, 3)]
     outward = [(2, 0), (3, 1), (4, 6), (5, 7)]
     out_near = swapped(w_out, "ctx", 2)
     out_across = lax.ppermute(w_out, "ctx", middle)
-    sources = place, [activations] + list(far), (x0, x_rest, y0, y_rest, d_rest), w_same, w_swap
+    c_low, c_high, w_same, out_near, out_across = barrier(
+        (c_low, c_high, w_same, out_near, out_across)
+    )
+    w_swap = swapped(w_same, "ctx", 1)
+    sources = place, [activations] + list(far), (x0, x_rest, y0, y_rest, c_low, c_high), w_same, w_swap
     (v_pair,) = project(*sources)
-    place, v_pair, out_near, out_across = barrier((place, v_pair, out_near, out_across))
+    place, v_pair = barrier((place, v_pair))
     v_next = swapped(v_pair, "ctx", 2)
     v_pair_other = swapped(v_pair, "ctx", 1)
     out_across_next = lax.ppermute(out_near, "ctx", middle)

time: 303 us -> 305 us (level)
    ppermute x27 -> x28, waiting for transfers between devices: 165 us -> 154 us  [swapped(): return lax.ppermute(value, axis, [(i, i ^ mask) for i in range(count)])]
    ppermute x1, waiting for transfers between devices: 2.67 us -> 12.7 us  [per_device_one_head(): out_across = lax.ppermute(w_out, 'ctx', middle)]
    unnamed x48 -> x52, local copies, waits for them, and re-layouts: 6.61 us -> 5.4 us
    ppermute x27 -> x28, starting transfers between devices: 24.9 us -> 24.7 us  [swapped(): return lax.ppermute(value, axis, [(i, i ^ mask) for i in range(count)])]
  transfers between devices with their start and end apart: 32 -> 33, of which waited for: 18 -> 21; matrix products, arithmetic and copies ran while one was open for 7% -> 6% of each run, Pallas kernels for 11% -> 9%
where the time goes in v8:
time: 305 us; the launch traced here: 303 us
  waiting for transfers between devices  189 us (62%)
  Pallas kernels  42.2 us (14%)
  starting transfers between devices  38.5 us (13%)
  other arithmetic  19.7 us (6%)
  local copies, waits for them, and re-layouts  13.8 us (5%)
    ppermute x28, waiting for transfers between devices, swapped(): return lax.ppermute(value, axis, [(i, i ^ mask) for i in range(count)])  154 us
    ppermute x28, starting transfers between devices, swapped(): return lax.ppermute(value, axis, [(i, i ^ mask) for i in range(count)])  24.7 us
    pallas_call x2, Pallas kernels, project(): pl.pallas_call(functools.partial(project_kernel, rows, first_col), out_sh...  17.6 us
    pallas_call x1, Pallas kernels, attend_head(): pl.pallas_call(attend_kernel, grid=(count,), out_shape=(out, out), in_spe...  16.7 us
    ppermute x1, waiting for transfers between devices, per_device_one_head(): out_passed_next = lax.ppermute(out_across_next, 'ctx', outward)  13.5 us
    ppermute x1, waiting for transfers between devices, per_device_one_head(): out_across = lax.ppermute(w_out, 'ctx', middle)  12.7 us
    pallas_call x1, Pallas kernels, finish(): pl.pallas_call(finish_kernel, in_specs=[whole(pltpu.SMEM)] + [whole(pltpu...  7.89 us
    ppermute x1, waiting for transfers between devices, per_device_one_head(): out_across_next = lax.ppermute(out_near, 'ctx', middle)  7.84 us
  transfers between devices with their start and end apart: 33, of which 21 were waited for; matrix products, arithmetic and copies ran while one was open for 6% of the time, Pallas kernels for 9%

profile of v8, /device:TPU:17, one launch (start us, length us, event | category | flops | bytes accessed | tf_op | source)
XLA Modules:
  0.0 303.1 jit_solution(13807004027922309496)
XLA Ops:
  0.0 0.8 fusion.11
  0.9 1.9 pad_maximum_fusion.4
  2.8 1.3 collective-permute-start
  4.1 1.3 collective-permute-start.2
  5.4 1.2 collective-permute-start.3
  6.7 1.2 collective-permute-start.4
  8.7 0.9 fusion.15
  9.6 0.9 fusion.14
  11.2 1.2 fusion.13.weights
  12.4 1.4 maximum_bitcast_fusion
  13.8 1.9 pad_maximum_fusion
  15.7 2.0 collective-permute-done.3.refs_4_
  17.7 0.9 collective-permute-done.4.refs_6_
  18.6 7.7 %collective-permute-done.refs_1_ = bf16[272,1024]{1,0:T(8,128)(2,1)S(1)} collective-permute-done((bf16[272,1024]{1,0:T(8,128)(2,1)}, bf16[272,1024]{1,0:T(8,128)(2,1)S(1)}, u32[]{:S(2)}, u32[]{:S(2)}) %collective-permute-start) | collective-permute-done | bytes 557088 | tf_op jit(solution)/shard_map/ppermute | solution.py:567
  26.3 2.0 collective-permute-done.1.refs_2_
  28.4 24.9 %collective-permute-done.2.refs_3_ = bf16[272,1024]{1,0:T(8,128)(2,1)S(1)} collective-permute-done((bf16[272,1024]{1,0:T(8,128)(2,1)}, bf16[272,1024]{1,0:T(8,128)(2,1)S(1)}, u32[]{:S(2)}, u32[]{:S(2)}) %collective-permute-start.2) | collective-permute-done | bytes 557088 | tf_op jit(solution)/shard_map/ppermute | solution.py:567
  53.3 1.1 slice.50
  54.6 1.0 slice.49
  55.5 2.1 pad_maximum_fusion.3
  57.6 3.7 %all-to-all-start = ((bf16[4,512,768]{2,1,0:T(8,128)(2,1)}), bf16[4,512,768]{2,1,0:T(8,128)(2,1)S(1)}, u32[]{:S(2)}, u32[]{:S(2)}) async-start(bf16[4,512,768]{2,1,0:T(8,128)(2,1)} %pad_maximum_fusion), calls=%async_computation | async-start | bytes 6291456 | tf_op jit(solution)/shard_map/all_to_all | solution.py:605
  61.3 1.3 collective-permute-start.5
  62.6 1.2 collective-permute-start.6
  66.1 1.9 fusion.3
  68.0 1.0 pad_maximum_fusion.5.refs_12_
  69.0 1.0 pad_maximum_fusion.6.refs_13_
  70.1 30.8 %collective-permute-done.5.refs_5_ = bf16[896,1024]{1,0:T(8,128)(2,1)S(1)} collective-permute-done((bf16[896,1024]{1,0:T(8,128)(2,1)}, bf16[896,1024]{1,0:T(8,128)(2,1)S(1)}, u32[]{:S(2)}, u32[]{:S(2)}) %collective-permute-start.5) | collective-permute-done | bytes 1835040 | tf_op jit(solution)/shard_map/ppermute | solution.py:567
  100.8 0.9 collective-permute-done.6.refs_7_
  101.8 0.9 collective-permute-start.9
  102.7 1.9 collective-permute-start.10
  104.7 1.3 collective-permute-start.7
  106.5 13.5 %collective-permute-done.7.refs_8_ = bf16[384,1024]{1,0:T(8,128)(2,1)S(1)} collective-permute-done((bf16[384,1024]{1,0:T(8,128)(2,1)S(1)}, bf16[384,1024]{1,0:T(8,128)(2,1)S(1)}, u32[]{:S(2)}, u32[]{:S(2)}) %collective-permute-start.7) | collective-permute-done | bytes 786464 | tf_op jit(solution)/shard_map/ppermute | solution.py:567
  119.9 1.1 collective-permute-done.8.refs_9_
  121.0 16.2 %collective-permute-done.9.refs_2_ = bf16[1024,512]{1,0:T(8,128)(2,1)S(1)} collective-permute-done((bf16[1024,512]{1,0:T(8,128)(2,1)S(1)}, bf16[1024,512]{1,0:T(8,128)(2,1)S(1)}, u32[]{:S(2)}, u32[]{:S(2)}) %collective-permute-start.9) | collective-permute-done | bytes 1048608 | tf_op jit(solution)/shard_map/ppermute | solution.py:567
  137.2 1.0 copy-done.10
  138.2 12.7 %collective-permute-done.10.refs_4_ = bf16[1024,512]{1,0:T(8,128)(2,1)} collective-permute-done((bf16[1024,512]{1,0:T(8,128)(2,1)S(1)}, bf16[1024,512]{1,0:T(8,128)(2,1)}, u32[]{:S(2)}, u32[]{:S(2)}) %collective-permute-start.10) | collective-permute-done | bytes 1048608 | tf_op jit(solution)/shard_map/ppermute | solution.py:624
  150.9 2.5 collective-permute-start.11
  153.5 5.3 %collective-permute-done.11.refs_11_ = bf16[4,512,768]{2,1,0:T(8,128)(2,1)S(1)} collective-permute-done((bf16[4,512,768]{2,1,0:T(8,128)(2,1)S(1)}, bf16[4,512,768]{2,1,0:T(8,128)(2,1)S(1)}, u32[]{:S(2)}, u32[]{:S(2)}) %collective-permute-start.11) | collective-permute-done | bytes 3145760 | tf_op jit(solution)/shard_map/ppermute | solution.py:567
  158.8 1.7 copy-done.4
  160.4 8.2 %shard_map.91.refs_2_ = bf16[4,256,256]{2,1,0:T(8,128)(2,1)} custom-call(s32[9]{0:T(128)} %stack.92.place, bf16[256,1024]{1,0:T(8,128)(2,1)} %refs_0_.3, bf16[272,1024]{1,0:T(8,128)(2,1)} %copy-done.5, bf16[272,1024]{1,0:T(8,128)(2,1)} %copy-done.6, bf16[272,1024]{1,0:T(8,128)(2,1)} %copy-done.7, bf16[256,1024]{1,0:T(8,128)(2,1)} %collective-permute-done.3.refs_4_, ...), custom_call_target="tpu_custom_call" | custom-call | flops 2147483648 | bytes 16777216 | tf_op jit(solution)/shard_map/pallas_call | solution.py:261
  169.3 3.1 %collective-permute-start.16 = (bf16[1024,512]{1,0:T(8,128)(2,1)}, bf16[1024,512]{1,0:T(8,128)(2,1)}, u32[]{:S(2)}, u32[]{:S(2)}) collective-permute-start(bf16[1024,512]{1,0:T(8,128)(2,1)} %copy-done.10), channel_id=1, source_target_pairs={{8,16},{12,20},{16,8},{20,12},{9,17},{13,21},{17,9},{21,13},{10,18... | collective-permute-start | bytes 3145736 | tf_op jit(solution)/shard_map/ppermute | solution.py:634
  172.4 9.4 %shard_map.92 = (bf16[4,256,256]{2,1,0:T(8,128)(2,1)}, bf16[4,256,256]{2,1,0:T(8,128)(2,1)}) custom-call(s32[9]{0:T(128)} %stack.92.place, bf16[256,1024]{1,0:T(8,128)(2,1)} %refs_0_.3, bf16[272,1024]{1,0:T(8,128)(2,1)} %copy-done.5, bf16[272,1024]{1,0:T(8,128)(2,1)} %copy-done.6, bf16[272,1024]{1,0:T(8,128)(2,1)} %copy-done.7, ...), custom_call_target="tpu_custom_call" | custom-call | flops 4294967296 | bytes 16777216 | tf_op jit(solution)/shard_map/pallas_call | solution.py:261
  182.2 1.2 collective-permute-start.14
  184.1 1.0 copy-done.12
  185.1 2.9 collective-permute-start.18
  188.0 7.8 %collective-permute-done.16.refs_8_ = bf16[1024,512]{1,0:T(8,128)(2,1)} collective-permute-done((bf16[1024,512]{1,0:T(8,128)(2,1)}, bf16[1024,512]{1,0:T(8,128)(2,1)}, u32[]{:S(2)}, u32[]{:S(2)}) %collective-permute-start.16) | collective-permute-done | bytes 1048608 | tf_op jit(solution)/shard_map/ppermute | solution.py:634
  195.9 1.2 collective-permute-start.21
  198.7 2.3 collective-permute-start.19
  201.6 16.7 %shard_map.93 = (bf16[4,256,512]{2,1,0:T(8,128)(2,1)}, bf16[4,256,512]{2,1,0:T(8,128)(2,1)}) custom-call(s32[9]{0:T(128)} %stack.92.place, f32[4]{0:T(128)} %dynamic-slice_bitcast_fusion.1.mix, f32[66]{0:T(128)} %fusion.13.weights, bf16[4,256,256]{2,1,0:T(8,128)(2,1)} %get-tuple-element.75.refs_0_, bf16[4,256,256]{2,1,0:T(8,128)(2,1)} %copy-done.24, ...), custom_call_target="tpu_custom_call" | custom-call | flops 5368709120 | bytes 16777216 | tf_op jit(solution)/shard_map/pallas_call | solution.py:471
  218.3 13.5 %collective-permute-done.19.refs_10_ = bf16[1024,512]{1,0:T(8,128)(2,1)} collective-permute-done((bf16[1024,512]{1,0:T(8,128)(2,1)}, bf16[1024,512]{1,0:T(8,128)(2,1)}, u32[]{:S(2)}, u32[]{:S(2)}) %collective-permute-start.19) | collective-permute-done | bytes 1048608 | tf_op jit(solution)/shard_map/ppermute | solution.py:644
  231.8 1.4 collective-permute-start.22
  233.7 3.6 %collective-permute-done.22 = bf16[4,256,512]{2,1,0:T(8,128)(2,1)} collective-permute-done((bf16[4,256,512]{2,1,0:T(8,128)(2,1)}, bf16[4,256,512]{2,1,0:T(8,128)(2,1)}, u32[]{:S(2)}, u32[]{:S(2)}) %collective-permute-start.22) | collective-permute-done | bytes 1048608 | tf_op jit(solution)/shard_map/ppermute | solution.py:567
  237.3 1.9 convert_add_fusion
  239.2 0.9 fusion.2
  240.1 2.2 collective-permute-start.23
  242.3 0.9 collective-permute-start.24
  244.2 0.8 dynamic-slice_bitcast_fusion.own
  245.0 8.0 %collective-permute-done.23.r1 = bf16[256,512]{1,0:T(8,128)(2,1)S(1)} collective-permute-done((bf16[256,512]{1,0:T(8,128)(2,1)}, bf16[256,512]{1,0:T(8,128)(2,1)S(1)}, u32[]{:S(2)}, u32[]{:S(2)}) %collective-permute-start.23) | collective-permute-done | bytes 262176 | tf_op jit(solution)/shard_map/ppermute | solution.py:567
  253.0 7.0 %collective-permute-done.24.r2 = bf16[256,512]{1,0:T(8,128)(2,1)} collective-permute-done((bf16[256,512]{1,0:T(8,128)(2,1)}, bf16[256,512]{1,0:T(8,128)(2,1)}, u32[]{:S(2)}, u32[]{:S(2)}) %collective-permute-start.24) | collective-permute-done | bytes 262176 | tf_op jit(solution)/shard_map/ppermute | solution.py:567
  260.0 6.8 %collective-permute-done.25.r3 = bf16[256,512]{1,0:T(8,128)(2,1)} collective-permute-done((bf16[256,512]{1,0:T(8,128)(2,1)}, bf16[256,512]{1,0:T(8,128)(2,1)}, u32[]{:S(2)}, u32[]{:S(2)}) %collective-permute-start.25) | collective-permute-done | bytes 262176 | tf_op jit(solution)/shard_map/ppermute | solution.py:567
  266.8 7.9 %shard_map.94 = (bf16[256,1024]{1,0:T(8,128)(2,1)}, bf16[256,1024]{1,0:T(8,128)(2,1)}, bf16[256,1024]{1,0:T(8,128)(2,1)}, bf16[256,1024]{1,0:T(8,128)(2,1)}) custom-call(s32[10]{0:T(128)} %concatenate.43.place, f32[256,512]{1,0:T(8,128)} %dynamic-slice_bitcast_fusion.own, bf16[256,512]{1,0:T(8,128)(2,1)} %copy-done.20, ...), custom_call_target="tpu_custom_call" | custom-call | flops 2147483648 | bytes 11534336 | tf_op jit(solution)/shard_map/pallas_call | solution.py:548
  274.7 2.2 collective-permute-start.31
  277.4 10.7 %collective-permute-done.31 = bf16[256,1024]{1,0:T(8,128)(2,1)S(1)} collective-permute-done((bf16[256,1024]{1,0:T(8,128)(2,1)}, bf16[256,1024]{1,0:T(8,128)(2,1)S(1)}, u32[]{:S(2)}, u32[]{:S(2)}) %collective-permute-start.31) | collective-permute-done | bytes 524320 | tf_op jit(solution)/shard_map/ppermute | solution.py:567
  288.1 12.8 %collective-permute-done.30 = bf16[256,1024]{1,0:T(8,128)(2,1)S(1)} collective-permute-done((bf16[256,1024]{1,0:T(8,128)(2,1)}, bf16[256,1024]{1,0:T(8,128)(2,1)S(1)}, u32[]{:S(2)}, u32[]{:S(2)}) %collective-permute-start.30) | collective-permute-done | bytes 524320 | tf_op jit(solution)/shard_map/ppermute | solution.py:567
  300.9 2.2 add_convert_fusion
  (94 shorter events, 10.5 us)
Async XLA Ops:
  0.0 200.9 %copy-start = (f32[8,4]{0,1:T(4,128)S(1)}, f32[8,4]{0,1:T(4,128)}, u32[]{:S(2)}) copy-start(f32[8,4]{0,1:T(4,128)} %param.15) | copy-start | bytes 388
  0.0 7.9 %copy-start.15 = (bf16[512,1024]{1,0:T(8,128)(2,1)S(1)}, bf16[512,1024]{1,0:T(8,128)(2,1)}, u32[]{:S(2)}) copy-start(bf16[512,1024]{1,0:T(8,128)(2,1)} %param.13) | copy-start | bytes 3145732
  0.0 8.7 %copy-start.16 = (bf16[512,1024]{1,0:T(8,128)(2,1)S(1)}, bf16[512,1024]{1,0:T(8,128)(2,1)}, u32[]{:S(2)}) copy-start(bf16[512,1024]{1,0:T(8,128)(2,1)} %param.12) | copy-start | bytes 3145732
  2.8 6.8 %copy-start.17 = (bf16[512,1024]{1,0:T(8,128)(2,1)S(1)}, bf16[512,1024]{1,0:T(8,128)(2,1)}, u32[]{:S(2)}) copy-start(bf16[512,1024]{1,0:T(8,128)(2,1)} %param.11) | copy-start | bytes 3145732
  2.8 23.5 %collective-permute-start = (bf16[272,1024]{1,0:T(8,128)(2,1)}, bf16[272,1024]{1,0:T(8,128)(2,1)S(1)}, u32[]{:S(2)}, u32[]{:S(2)}) collective-permute-start(bf16[272,1024]{1,0:T(8,128)(2,1)} %pad_maximum_fusion.4), channel_id=1, source_target_pairs={{0,8},{4,12},{8,0},{12,4},{16,24},{20,28},{24,16},{28,20},{1,9},{5... | collective-permute-start | bytes 1671176 | tf_op jit(solution)/shard_map/ppermute | solution.py:567
  4.1 24.3 %collective-permute-start.1 = (bf16[272,1024]{1,0:T(8,128)(2,1)}, bf16[272,1024]{1,0:T(8,128)(2,1)S(1)}, u32[]{:S(2)}, u32[]{:S(2)}) collective-permute-start(bf16[272,1024]{1,0:T(8,128)(2,1)} %pad_maximum_fusion.4), channel_id=1, source_target_pairs={{0,16},{4,20},{8,24},{12,28},{16,0},{20,4},{24,8},{28,12},{1,17},{... | collective-permute-start | bytes 1671176 | tf_op jit(solution)/shard_map/ppermute | solution.py:567
  4.1 49.1 %collective-permute-start.2 = (bf16[272,1024]{1,0:T(8,128)(2,1)}, bf16[272,1024]{1,0:T(8,128)(2,1)S(1)}, u32[]{:S(2)}, u32[]{:S(2)}) collective-permute-start(bf16[272,1024]{1,0:T(8,128)(2,1)} %pad_maximum_fusion.4), channel_id=1, source_target_pairs={{0,24},{4,28},{8,16},{12,20},{16,8},{20,12},{24,0},{28,4},{1,25},{... | collective-permute-start | bytes 1671176 | tf_op jit(solution)/shard_map/ppermute | solution.py:567
  5.4 12.2 %collective-permute-start.3 = (bf16[256,1024]{1,0:T(8,128)(2,1)}, bf16[256,1024]{1,0:T(8,128)(2,1)}, u32[]{:S(2)}, u32[]{:S(2)}) collective-permute-start(bf16[256,1024]{1,0:T(8,128)(2,1)} %refs_0_.3), channel_id=1, source_target_pairs={{0,1},{1,0},{2,3},{3,2},{4,5},{5,4},{6,7},{7,6},{8,9},{9,8},{10,11... | collective-permute-start | bytes 1572872 | tf_op jit(solution)/shard_map/ppermute | solution.py:567
  6.7 11.9 %collective-permute-start.4 = (bf16[256,1024]{1,0:T(8,128)(2,1)}, bf16[256,1024]{1,0:T(8,128)(2,1)}, u32[]{:S(2)}, u32[]{:S(2)}) collective-permute-start(bf16[256,1024]{1,0:T(8,128)(2,1)} %refs_0_.3), channel_id=1, source_target_pairs={{0,2},{1,3},{2,0},{3,1},{4,6},{5,7},{6,4},{7,5},{8,10},{9,11},{10,... | collective-permute-start | bytes 1572872 | tf_op jit(solution)/shard_map/ppermute | solution.py:567
  26.3 28.2 %copy-start.5 = (bf16[272,1024]{1,0:T(8,128)(2,1)}, bf16[272,1024]{1,0:T(8,128)(2,1)S(1)}, u32[]{:S(2)}) copy-start(bf16[272,1024]{1,0:T(8,128)(2,1)S(1)} %collective-permute-done.refs_1_) | copy-start | bytes 1671172
  28.4 26.2 %copy-start.6 = (bf16[272,1024]{1,0:T(8,128)(2,1)}, bf16[272,1024]{1,0:T(8,128)(2,1)S(1)}, u32[]{:S(2)}) copy-start(bf16[272,1024]{1,0:T(8,128)(2,1)S(1)} %collective-permute-done.1.refs_2_) | copy-start | bytes 1671172
  53.3 1.3 copy-start.7
  57.6 93.3 %all-to-all-start = ((bf16[4,512,768]{2,1,0:T(8,128)(2,1)}), bf16[4,512,768]{2,1,0:T(8,128)(2,1)S(1)}, u32[]{:S(2)}, u32[]{:S(2)}) async-start(bf16[4,512,768]{2,1,0:T(8,128)(2,1)} %pad_maximum_fusion), calls=%async_computation | async-start | bytes 6291456 | tf_op jit(solution)/shard_map/all_to_all | solution.py:605
  61.3 39.5 %collective-permute-start.5 = (bf16[896,1024]{1,0:T(8,128)(2,1)}, bf16[896,1024]{1,0:T(8,128)(2,1)S(1)}, u32[]{:S(2)}, u32[]{:S(2)}) collective-permute-start(bf16[896,1024]{1,0:T(8,128)(2,1)} %get-tuple-element.58), channel_id=1, source_target_pairs={{0,1},{1,0},{2,3},{3,2},{4,5},{5,4},{6,7},{7,6},{8,9},{9,8},{10,11... | collective-permute-start | bytes 5505032 | tf_op jit(solution)/shard_map/ppermute | solution.py:567
  62.6 39.2 %collective-permute-start.6 = (bf16[896,1024]{1,0:T(8,128)(2,1)}, bf16[896,1024]{1,0:T(8,128)(2,1)S(1)}, u32[]{:S(2)}, u32[]{:S(2)}) collective-permute-start(bf16[896,1024]{1,0:T(8,128)(2,1)} %get-tuple-element.59), channel_id=1, source_target_pairs={{0,2},{1,3},{2,0},{3,1},{4,6},{5,7},{6,4},{7,5},{8,10},{9,11},{10,... | collective-permute-start | bytes 5505032 | tf_op jit(solution)/shard_map/ppermute | solution.py:567
  66.1 35.6 %copy-start.8 = (bf16[1024,512]{1,0:T(8,128)(2,1)S(1)}, bf16[1024,512]{1,0:T(8,128)(2,1)}, u32[]{:S(2)}) copy-start(bf16[1024,512]{1,0:T(8,128)(2,1)} %refs_0_.4) | copy-start | bytes 3145732
  100.8 36.4 %copy-start.2 = (bf16[896,1024]{1,0:T(8,128)(2,1)}, bf16[896,1024]{1,0:T(8,128)(2,1)S(1)}, u32[]{:S(2)}) copy-start(bf16[896,1024]{1,0:T(8,128)(2,1)S(1)} %collective-permute-done.5.refs_5_) | copy-start | bytes 5505028
  101.8 35.4 %copy-start.3 = (bf16[896,1024]{1,0:T(8,128)(2,1)}, bf16[896,1024]{1,0:T(8,128)(2,1)S(1)}, u32[]{:S(2)}) copy-start(bf16[896,1024]{1,0:T(8,128)(2,1)S(1)} %collective-permute-done.6.refs_7_) | copy-start | bytes 5505028
  101.8 35.4 %collective-permute-start.9 = (bf16[1024,512]{1,0:T(8,128)(2,1)S(1)}, bf16[1024,512]{1,0:T(8,128)(2,1)S(1)}, u32[]{:S(2)}, u32[]{:S(2)}) collective-permute-start(bf16[1024,512]{1,0:T(8,128)(2,1)S(1)} %copy-done.8), channel_id=1, source_target_pairs={{0,8},{4,12},{8,0},{12,4},{16,24},{20,28},{24,16},{28,20},{1,9},{5... | collective-permute-start | bytes 3145736 | tf_op jit(solution)/shard_map/ppermute | solution.py:567
  102.7 48.2 %collective-permute-start.10 = (bf16[1024,512]{1,0:T(8,128)(2,1)S(1)}, bf16[1024,512]{1,0:T(8,128)(2,1)}, u32[]{:S(2)}, u32[]{:S(2)}) collective-permute-start(bf16[1024,512]{1,0:T(8,128)(2,1)S(1)} %copy-done.8), channel_id=1, source_target_pairs={{8,16},{12,20},{16,8},{20,12},{9,17},{13,21},{17,9},{21,13},{10,18... | collective-permute-start | bytes 3145736 | tf_op jit(solution)/shard_map/ppermute | solution.py:624
  104.7 15.2 %collective-permute-start.7 = (bf16[384,1024]{1,0:T(8,128)(2,1)S(1)}, bf16[384,1024]{1,0:T(8,128)(2,1)S(1)}, u32[]{:S(2)}, u32[]{:S(2)}) collective-permute-start(bf16[384,1024]{1,0:T(8,128)(2,1)S(1)} %slice.57), channel_id=1, source_target_pairs={{0,2},{1,3},{2,0},{3,1},{4,6},{5,7},{6,4},{7,5},{8,10},{9,11},{10,... | collective-permute-start | bytes 2359304 | tf_op jit(solution)/shard_map/ppermute | solution.py:567
  106.0 15.0 %collective-permute-start.8 = (bf16[384,1024]{1,0:T(8,128)(2,1)S(1)}, bf16[384,1024]{1,0:T(8,128)(2,1)S(1)}, u32[]{:S(2)}, u32[]{:S(2)}) collective-permute-start(bf16[384,1024]{1,0:T(8,128)(2,1)S(1)} %slice.58), channel_id=1, source_target_pairs={{0,1},{1,0},{2,3},{3,2},{4,5},{5,4},{6,7},{7,6},{8,9},{9,8},{10,11... | collective-permute-start | bytes 2359304 | tf_op jit(solution)/shard_map/ppermute | solution.py:567
  119.9 17.3 %copy-start.18 = (bf16[384,1024]{1,0:T(8,128)(2,1)}, bf16[384,1024]{1,0:T(8,128)(2,1)S(1)}, u32[]{:S(2)}) copy-start(bf16[384,1024]{1,0:T(8,128)(2,1)S(1)} %collective-permute-done.7.refs_8_) | copy-start | bytes 2359300
  121.0 16.2 %copy-start.19 = (bf16[384,1024]{1,0:T(8,128)(2,1)}, bf16[384,1024]{1,0:T(8,128)(2,1)S(1)}, u32[]{:S(2)}) copy-start(bf16[384,1024]{1,0:T(8,128)(2,1)S(1)} %collective-permute-done.8.refs_9_) | copy-start | bytes 2359300
  137.2 1.0 copy-start.10
  150.9 7.8 %copy-start.1 = (bf16[4,512,768]{2,1,0:T(8,128)(2,1)}, bf16[4,512,768]{2,1,0:T(8,128)(2,1)S(1)}, u32[]{:S(2)}) copy-start(bf16[4,512,768]{2,1,0:T(8,128)(2,1)S(1)} %all-to-all-done.refs_10_) | copy-start | bytes 9437188
  150.9 18.2 %copy-start.9 = (bf16[1024,512]{1,0:T(8,128)(2,1)S(1)}, bf16[1024,512]{1,0:T(8,128)(2,1)}, u32[]{:S(2)}) copy-start(bf16[1024,512]{1,0:T(8,128)(2,1)} %refs_0_.4) | copy-start | bytes 3145732
  150.9 7.8 %collective-permute-start.11 = (bf16[4,512,768]{2,1,0:T(8,128)(2,1)S(1)}, bf16[4,512,768]{2,1,0:T(8,128)(2,1)S(1)}, u32[]{:S(2)}, u32[]{:S(2)}) collective-permute-start(bf16[4,512,768]{2,1,0:T(8,128)(2,1)S(1)} %all-to-all-done.refs_10_), channel_id=1, source_target_pairs={{0,4},{4,0},{8,12},{12,8},{16,20},{20,16},{24,28},{28,24},{1,5},{5... | collective-permute-start | bytes 9437192 | tf_op jit(solution)/shard_map/ppermute | solution.py:567
  158.8 1.7 copy-start.4
  168.6 15.5 %copy-start.11 = (bf16[1024,512]{1,0:T(8,128)(2,1)S(1)}, bf16[1024,512]{1,0:T(8,128)(2,1)}, u32[]{:S(2)}) copy-start(bf16[1024,512]{1,0:T(8,128)(2,1)} %copy-done.10) | copy-start | bytes 3145732
  168.6 13.5 %collective-permute-start.12 = (bf16[4,256,256]{2,1,0:T(8,128)(2,1)}, bf16[4,256,256]{2,1,0:T(8,128)(2,1)S(1)}, u32[]{:S(2)}, u32[]{:S(2)}) collective-permute-start(bf16[4,256,256]{2,1,0:T(8,128)(2,1)} %shard_map.91.refs_2_), channel_id=1, source_target_pairs={{0,8},{4,12},{8,0},{12,4},{16,24},{20,28},{24,16},{28,20},{1,9},{5... | collective-permute-start | bytes 1572872 | tf_op jit(solution)/shard_map/ppermute | solution.py:567
  168.7 13.4 %collective-permute-start.13 = (bf16[4,256,256]{2,1,0:T(8,128)(2,1)}, bf16[4,256,256]{2,1,0:T(8,128)(2,1)S(1)}, u32[]{:S(2)}, u32[]{:S(2)}) collective-permute-start(bf16[4,256,256]{2,1,0:T(8,128)(2,1)} %shard_map.91.refs_2_), channel_id=1, source_target_pairs={{0,4},{4,0},{8,12},{12,8},{16,20},{20,16},{24,28},{28,24},{1,5},{5... | collective-permute-start | bytes 1572872 | tf_op jit(solution)/shard_map/ppermute | solution.py:567
  169.2 14.9 %collective-permute-start.17 = (bf16[1024,512]{1,0:T(8,128)(2,1)S(1)}, bf16[1024,512]{1,0:T(8,128)(2,1)S(1)}, u32[]{:S(2)}, u32[]{:S(2)}) collective-permute-start(bf16[1024,512]{1,0:T(8,128)(2,1)S(1)} %copy-done.9), channel_id=1, source_target_pairs={{0,4},{4,0},{8,12},{12,8},{16,20},{20,16},{24,28},{28,24},{1,5},{5... | collective-permute-start | bytes 3145736 | tf_op jit(solution)/shard_map/ppermute | solution.py:567
  169.3 26.6 %collective-permute-start.16 = (bf16[1024,512]{1,0:T(8,128)(2,1)}, bf16[1024,512]{1,0:T(8,128)(2,1)}, u32[]{:S(2)}, u32[]{:S(2)}) collective-permute-start(bf16[1024,512]{1,0:T(8,128)(2,1)} %copy-done.10), channel_id=1, source_target_pairs={{8,16},{12,20},{16,8},{20,12},{9,17},{13,21},{17,9},{21,13},{10,18... | collective-permute-start | bytes 3145736 | tf_op jit(solution)/shard_map/ppermute | solution.py:634
  182.2 19.4 %copy-start.22 = (bf16[4,256,256]{2,1,0:T(8,128)(2,1)}, bf16[4,256,256]{2,1,0:T(8,128)(2,1)S(1)}, u32[]{:S(2)}) copy-start(bf16[4,256,256]{2,1,0:T(8,128)(2,1)S(1)} %collective-permute-done.12.refs_3_) | copy-start | bytes 1572868
  182.2 1.2 copy-start.23
  182.2 14.9 %collective-permute-start.14 = (bf16[4,256,256]{2,1,0:T(8,128)(2,1)}, bf16[4,256,256]{2,1,0:T(8,128)(2,1)S(1)}, u32[]{:S(2)}, u32[]{:S(2)}) collective-permute-start(bf16[4,256,256]{2,1,0:T(8,128)(2,1)} %get-tuple-element.76), channel_id=1, source_target_pairs={{0,4},{4,0},{8,12},{12,8},{16,20},{20,16},{24,28},{28,24},{1,5},{5... | collective-permute-start | bytes 1572872 | tf_op jit(solution)/shard_map/ppermute | solution.py:567
  183.3 13.8 %collective-permute-start.15 = (bf16[4,256,256]{2,1,0:T(8,128)(2,1)S(1)}, bf16[4,256,256]{2,1,0:T(8,128)(2,1)S(1)}, u32[]{:S(2)}, u32[]{:S(2)}) collective-permute-start(bf16[4,256,256]{2,1,0:T(8,128)(2,1)S(1)} %collective-permute-done.12.refs_3_), channel_id=1, source_target_pairs={{0,4},{4,0},{8,12},{12,8},{16,20},{20,16},{24,28},{28,24},{1,5},{5... | collective-permute-start | bytes 1572872 | tf_op jit(solution)/shard_map/ppermute | solution.py:567
  184.1 34.2 %collective-permute-start.20 = (bf16[1024,512]{1,0:T(8,128)(2,1)S(1)}, bf16[1024,512]{1,0:T(8,128)(2,1)S(1)}, u32[]{:S(2)}, u32[]{:S(2)}) collective-permute-start(bf16[1024,512]{1,0:T(8,128)(2,1)S(1)} %copy-done.11), channel_id=1, source_target_pairs={{0,4},{4,0},{8,12},{12,8},{16,20},{20,16},{24,28},{28,24},{1,5},{5... | collective-permute-start | bytes 3145736 | tf_op jit(solution)/shard_map/ppermute | solution.py:567
  184.1 1.0 copy-start.12
  185.1 33.1 %collective-permute-start.18 = (bf16[1024,512]{1,0:T(8,128)(2,1)}, bf16[1024,512]{1,0:T(8,128)(2,1)}, u32[]{:S(2)}, u32[]{:S(2)}) collective-permute-start(bf16[1024,512]{1,0:T(8,128)(2,1)} %collective-permute-done.10.refs_4_), channel_id=1, source_target_pairs={{8,0},{12,4},{16,24},{20,28},{9,1},{13,5},{17,25},{21,29},{10,2},{... | collective-permute-start | bytes 3145736 | tf_op jit(solution)/shard_map/ppermute | solution.py:635
  195.9 22.4 %collective-permute-start.21 = (bf16[1024,512]{1,0:T(8,128)(2,1)}, bf16[1024,512]{1,0:T(8,128)(2,1)}, u32[]{:S(2)}, u32[]{:S(2)}) collective-permute-start(bf16[1024,512]{1,0:T(8,128)(2,1)} %collective-permute-done.10.refs_4_), channel_id=1, source_target_pairs={{0,4},{4,0},{8,12},{12,8},{16,20},{20,16},{24,28},{28,24},{1,5},{5... | collective-permute-start | bytes 3145736 | tf_op jit(solution)/shard_map/ppermute | solution.py:567
  197.1 0.8 copy-start.24
  197.9 0.8 copy-start.25
  198.7 33.1 %collective-permute-start.19 = (bf16[1024,512]{1,0:T(8,128)(2,1)}, bf16[1024,512]{1,0:T(8,128)(2,1)}, u32[]{:S(2)}, u32[]{:S(2)}) collective-permute-start(bf16[1024,512]{1,0:T(8,128)(2,1)} %collective-permute-done.16.refs_8_), channel_id=1, source_target_pairs={{8,0},{12,4},{16,24},{20,28},{9,1},{13,5},{17,25},{21,29},{10,2},{... | collective-permute-start | bytes 3145736 | tf_op jit(solution)/shard_map/ppermute | solution.py:644
  218.3 15.4 %copy-start.13 = (bf16[1024,512]{1,0:T(8,128)(2,1)}, bf16[1024,512]{1,0:T(8,128)(2,1)S(1)}, u32[]{:S(2)}) copy-start(bf16[1024,512]{1,0:T(8,128)(2,1)S(1)} %collective-permute-done.20.refs_3_) | copy-start | bytes 3145732
  231.8 5.5 %collective-permute-start.22 = (bf16[4,256,512]{2,1,0:T(8,128)(2,1)}, bf16[4,256,512]{2,1,0:T(8,128)(2,1)}, u32[]{:S(2)}, u32[]{:S(2)}) collective-permute-start(bf16[4,256,512]{2,1,0:T(8,128)(2,1)} %get-tuple-element.87), channel_id=1, source_target_pairs={{0,4},{4,0},{8,12},{12,8},{16,20},{20,16},{24,28},{28,24},{1,5},{5... | collective-permute-start | bytes 3145736 | tf_op jit(solution)/shard_map/ppermute | solution.py:567
  233.2 10.0 %collective-permute-start.27 = (bf16[1024,512]{1,0:T(8,128)(2,1)}, bf16[1024,512]{1,0:T(8,128)(2,1)S(1)}, u32[]{:S(2)}, u32[]{:S(2)}) collective-permute-start(bf16[1024,512]{1,0:T(8,128)(2,1)} %collective-permute-done.16.refs_8_), channel_id=1, source_target_pairs={{0,4},{4,0},{8,12},{12,8},{16,20},{20,16},{24,28},{28,24},{1,5},{5... | collective-permute-start | bytes 3145736 | tf_op jit(solution)/shard_map/ppermute | solution.py:567
  233.2 11.8 %collective-permute-start.26 = (bf16[1024,512]{1,0:T(8,128)(2,1)}, bf16[1024,512]{1,0:T(8,128)(2,1)}, u32[]{:S(2)}, u32[]{:S(2)}) collective-permute-start(bf16[1024,512]{1,0:T(8,128)(2,1)} %collective-permute-done.18.refs_6_), channel_id=1, source_target_pairs={{0,4},{4,0},{8,12},{12,8},{16,20},{20,16},{24,28},{28,24},{1,5},{5... | collective-permute-start | bytes 3145736 | tf_op jit(solution)/shard_map/ppermute | solution.py:567
  233.7 11.3 %collective-permute-start.28 = (bf16[1024,512]{1,0:T(8,128)(2,1)}, bf16[1024,512]{1,0:T(8,128)(2,1)}, u32[]{:S(2)}, u32[]{:S(2)}) collective-permute-start(bf16[1024,512]{1,0:T(8,128)(2,1)} %collective-permute-done.19.refs_10_), channel_id=1, source_target_pairs={{0,4},{4,0},{8,12},{12,8},{16,20},{20,16},{24,28},{28,24},{1,5},{5... | collective-permute-start | bytes 3145736 | tf_op jit(solution)/shard_map/ppermute | solution.py:567
  233.7 9.9 %copy-start.21 = (s32[9]{0:T(128)S(1)}, s32[9]{0:T(128)}, u32[]{:S(2)}) copy-start(s32[9]{0:T(128)} %stack.92.place) | copy-start | bytes 112
  240.1 12.9 %collective-permute-start.23 = (bf16[256,512]{1,0:T(8,128)(2,1)}, bf16[256,512]{1,0:T(8,128)(2,1)S(1)}, u32[]{:S(2)}, u32[]{:S(2)}) collective-permute-start(bf16[256,512]{1,0:T(8,128)(2,1)} %get-tuple-element.99), channel_id=1, source_target_pairs={{0,8},{4,12},{8,0},{12,4},{16,24},{20,28},{24,16},{28,20},{1,9},{5... | collective-permute-start | bytes 786440 | tf_op jit(solution)/shard_map/ppermute | solution.py:567
  242.3 17.7 %collective-permute-start.24 = (bf16[256,512]{1,0:T(8,128)(2,1)}, bf16[256,512]{1,0:T(8,128)(2,1)}, u32[]{:S(2)}, u32[]{:S(2)}) collective-permute-start(bf16[256,512]{1,0:T(8,128)(2,1)} %get-tuple-element.98), channel_id=1, source_target_pairs={{0,16},{4,20},{8,24},{12,28},{16,0},{20,4},{24,8},{28,12},{1,17},{... | collective-permute-start | bytes 786440 | tf_op jit(solution)/shard_map/ppermute | solution.py:567
  243.2 23.6 %copy-start.14 = (bf16[1024,512]{1,0:T(8,128)(2,1)}, bf16[1024,512]{1,0:T(8,128)(2,1)S(1)}, u32[]{:S(2)}) copy-start(bf16[1024,512]{1,0:T(8,128)(2,1)S(1)} %collective-permute-done.27.refs_9_) | copy-start | bytes 3145732
  243.2 23.5 %collective-permute-start.25 = (bf16[256,512]{1,0:T(8,128)(2,1)}, bf16[256,512]{1,0:T(8,128)(2,1)}, u32[]{:S(2)}, u32[]{:S(2)}) collective-permute-start(bf16[256,512]{1,0:T(8,128)(2,1)} %get-tuple-element.97), channel_id=1, source_target_pairs={{0,24},{4,28},{8,16},{12,20},{16,8},{20,12},{24,0},{28,4},{1,25},{... | collective-permute-start | bytes 786440 | tf_op jit(solution)/shard_map/ppermute | solution.py:567
  253.0 13.8 %copy-start.20 = (bf16[256,512]{1,0:T(8,128)(2,1)}, bf16[256,512]{1,0:T(8,128)(2,1)S(1)}, u32[]{:S(2)}) copy-start(bf16[256,512]{1,0:T(8,128)(2,1)S(1)} %collective-permute-done.23.r1) | copy-start | bytes 786436
  274.7 13.4 %collective-permute-start.31 = (bf16[256,1024]{1,0:T(8,128)(2,1)}, bf16[256,1024]{1,0:T(8,128)(2,1)S(1)}, u32[]{:S(2)}, u32[]{:S(2)}) collective-permute-start(bf16[256,1024]{1,0:T(8,128)(2,1)} %get-tuple-element.96), channel_id=1, source_target_pairs={{0,3},{1,2},{2,1},{3,0},{4,7},{5,6},{6,5},{7,4},{8,11},{9,10},{10,... | collective-permute-start | bytes 1572872 | tf_op jit(solution)/shard_map/ppermute | solution.py:567
  276.9 24.0 %collective-permute-start.30 = (bf16[256,1024]{1,0:T(8,128)(2,1)}, bf16[256,1024]{1,0:T(8,128)(2,1)S(1)}, u32[]{:S(2)}, u32[]{:S(2)}) collective-permute-start(bf16[256,1024]{1,0:T(8,128)(2,1)} %get-tuple-element.95), channel_id=1, source_target_pairs={{0,2},{1,3},{2,0},{3,1},{4,6},{5,7},{6,4},{7,5},{8,10},{9,11},{10,... | collective-permute-start | bytes 1572872 | tf_op jit(solution)/shard_map/ppermute | solution.py:567
  277.1 23.8 %collective-permute-start.29 = (bf16[256,1024]{1,0:T(8,128)(2,1)}, bf16[256,1024]{1,0:T(8,128)(2,1)S(1)}, u32[]{:S(2)}, u32[]{:S(2)}) collective-permute-start(bf16[256,1024]{1,0:T(8,128)(2,1)} %get-tuple-element.94), channel_id=1, source_target_pairs={{0,1},{1,0},{2,3},{3,2},{4,5},{5,4},{6,7},{7,6},{8,9},{9,8},{10,11... | collective-permute-start | bytes 1572872 | tf_op jit(solution)/shard_map/ppermute | solution.py:567

commit v9 on v8

--- a/solution.py
+++ b/solution.py
@@ -622,13 +622,11 @@
     outward = [(2, 0), (3, 1), (4, 6), (5, 7)]
     out_near = swapped(w_out, "ctx", 2)
     out_across = lax.ppermute(w_out, "ctx", middle)
-    c_low, c_high, w_same, out_near, out_across = barrier(
-        (c_low, c_high, w_same, out_near, out_across)
-    )
+    c_low, c_high, w_same = barrier((c_low, c_high, w_same))
     w_swap = swapped(w_same, "ctx", 1)
     sources = place, [activations] + list(far), (x0, x_rest, y0, y_rest, c_low, c_high), w_same, w_swap
     (v_pair,) = project(*sources)
-    place, v_pair = barrier((place, v_pair))
+    place, v_pair, out_near, out_across = barrier((place, v_pair, out_near, out_across))
     v_next = swapped(v_pair, "ctx", 2)
     v_pair_other = swapped(v_pair, "ctx", 1)
     out_across_next = lax.ppermute(out_near, "ctx", middle)
@@ -664,7 +662,6 @@
         )
         for s in (1, 2, 3)
     ]
-
     inner = (z == 1) | (z == 2)
     out_places = jnp.stack(
         [z, z ^ 1, jnp.where(inner, z ^ 3, z ^ 2), jnp.where(inner, z ^ 2, z ^ 3), inner]

time: 305 us -> 294 us (0.964)
  waiting for transfers between devices: 189 us -> 177 us
    ppermute x28, waiting for transfers between devices: 154 us -> 143 us  [swapped(): return lax.ppermute(value, axis, [(i, i ^ mask) for i in range(count)])]
    ppermute x1, waiting for transfers between devices: 12.7 us -> 2.82 us  [per_device_one_head(): out_across = lax.ppermute(w_out, 'ctx', middle)]
    all_to_all x1, waiting for transfers between devices: 0.01 us -> 9.72 us  [per_device_one_head(): w_same = lax.all_to_all(w_pieces, 'ctx', 0, 0, axis_index_groups=same_core)]
  transfers between devices with their start and end apart: 33 -> 33, of which waited for: 21 -> 20; matrix products, arithmetic and copies ran while one was open for 6% -> 6% of each run, Pallas kernels for 9% -> 12%
where the time goes in v9:
time: 294 us; the launch traced here: 292 us
  waiting for transfers between devices  177 us (60%)
  Pallas kernels  42.2 us (14%)
  starting transfers between devices  39.9 us (14%)
  other arithmetic  19.7 us (7%)
  local copies, waits for them, and re-layouts  12.8 us (4%)
    ppermute x28, waiting for transfers between devices, swapped(): return lax.ppermute(value, axis, [(i, i ^ mask) for i in range(count)])  143 us
    ppermute x28, starting transfers between devices, swapped(): return lax.ppermute(value, axis, [(i, i ^ mask) for i in range(count)])  24.8 us
    pallas_call x2, Pallas kernels, project(): pl.pallas_call(functools.partial(project_kernel, rows, first_col), out_sh...  17.6 us
    pallas_call x1, Pallas kernels, attend_head(): pl.pallas_call(attend_kernel, grid=(count,), out_shape=(out, out), in_spe...  16.7 us
    ppermute x1, waiting for transfers between devices, per_device_one_head(): out_passed_next = lax.ppermute(out_across_next, 'ctx', outward)  11.8 us
    all_to_all x1, waiting for transfers between devices, per_device_one_head(): w_same = lax.all_to_all(w_pieces, 'ctx', 0, 0, axis_index_groups=same_core)  9.72 us
    ppermute x1, waiting for transfers between devices, per_device_one_head(): out_across_next = lax.ppermute(out_near, 'ctx', middle)  9.44 us
    pallas_call x1, Pallas kernels, finish(): pl.pallas_call(finish_kernel, in_specs=[whole(pltpu.SMEM)] + [whole(pltpu...  7.89 us
  transfers between devices with their start and end apart: 33, of which 20 were waited for; matrix products, arithmetic and copies ran while one was open for 6% of the time, Pallas kernels for 12%

profile of v9, /device:TPU:17, one launch (start us, length us, event | category | flops | bytes accessed | tf_op | source)
XLA Modules:
  0.0 292.0 jit_solution(1224148181005322286)
XLA Ops:
  0.0 0.8 fusion.11
  0.9 1.9 pad_maximum_fusion.4
  2.8 1.3 collective-permute-start
  4.1 1.3 collective-permute-start.2
  5.4 1.2 collective-permute-start.3
  6.7 1.2 collective-permute-start.4
  8.7 0.9 fusion.15
  9.6 0.9 fusion.14
  11.2 1.2 fusion.13.weights
  12.5 1.4 maximum_bitcast_fusion
  13.8 1.9 pad_maximum_fusion
  15.7 1.9 collective-permute-done.3.refs_4_
  17.7 0.9 collective-permute-done.4.refs_6_
  18.6 7.7 %collective-permute-done.refs_1_ = bf16[272,1024]{1,0:T(8,128)(2,1)S(1)} collective-permute-done((bf16[272,1024]{1,0:T(8,128)(2,1)}, bf16[272,1024]{1,0:T(8,128)(2,1)S(1)}, u32[]{:S(2)}, u32[]{:S(2)}) %collective-permute-start) | collective-permute-done | bytes 557088 | tf_op jit(solution)/shard_map/ppermute | solution.py:567
  26.3 2.0 collective-permute-done.1.refs_2_
  28.4 24.9 %collective-permute-done.2.refs_3_ = bf16[272,1024]{1,0:T(8,128)(2,1)S(1)} collective-permute-done((bf16[272,1024]{1,0:T(8,128)(2,1)}, bf16[272,1024]{1,0:T(8,128)(2,1)S(1)}, u32[]{:S(2)}, u32[]{:S(2)}) %collective-permute-start.2) | collective-permute-done | bytes 557088 | tf_op jit(solution)/shard_map/ppermute | solution.py:567
  53.3 1.1 slice.50
  54.6 1.0 slice.49
  55.5 2.1 pad_maximum_fusion.3
  57.6 3.7 %all-to-all-start = ((bf16[4,512,768]{2,1,0:T(8,128)(2,1)}), bf16[4,512,768]{2,1,0:T(8,128)(2,1)S(1)}, u32[]{:S(2)}, u32[]{:S(2)}) async-start(bf16[4,512,768]{2,1,0:T(8,128)(2,1)} %pad_maximum_fusion), calls=%async_computation | async-start | bytes 6291456 | tf_op jit(solution)/shard_map/all_to_all | solution.py:605
  61.3 1.3 collective-permute-start.5
  62.6 1.2 collective-permute-start.6
  66.1 1.9 fusion.3
  68.0 1.0 pad_maximum_fusion.5.refs_12_
  69.0 1.0 pad_maximum_fusion.6.refs_13_
  70.0 30.8 %collective-permute-done.5.refs_5_ = bf16[896,1024]{1,0:T(8,128)(2,1)S(1)} collective-permute-done((bf16[896,1024]{1,0:T(8,128)(2,1)}, bf16[896,1024]{1,0:T(8,128)(2,1)S(1)}, u32[]{:S(2)}, u32[]{:S(2)}) %collective-permute-start.5) | collective-permute-done | bytes 1835040 | tf_op jit(solution)/shard_map/ppermute | solution.py:567
  100.8 0.9 collective-permute-done.6.refs_7_
  101.8 1.3 collective-permute-start.7
  103.5 14.3 %collective-permute-done.7.refs_8_ = bf16[384,1024]{1,0:T(8,128)(2,1)S(1)} collective-permute-done((bf16[384,1024]{1,0:T(8,128)(2,1)S(1)}, bf16[384,1024]{1,0:T(8,128)(2,1)S(1)}, u32[]{:S(2)}, u32[]{:S(2)}) %collective-permute-start.7) | collective-permute-done | bytes 786464 | tf_op jit(solution)/shard_map/ppermute | solution.py:567
  117.9 0.9 copy-done.16
  118.8 9.7 %all-to-all-done.refs_10_ = bf16[4,512,768]{2,1,0:T(8,128)(2,1)S(1)} async-done(((bf16[4,512,768]{2,1,0:T(8,128)(2,1)}), bf16[4,512,768]{2,1,0:T(8,128)(2,1)S(1)}, u32[]{:S(2)}, u32[]{:S(2)}) %all-to-all-start) | async-done | bytes 3145760 | tf_op jit(solution)/shard_map/all_to_all | solution.py:605
  128.5 1.4 collective-permute-start.9
  129.9 2.0 collective-permute-start.10
  132.0 3.1 %collective-permute-start.11 = (bf16[1024,512]{1,0:T(8,128)(2,1)}, bf16[1024,512]{1,0:T(8,128)(2,1)}, u32[]{:S(2)}, u32[]{:S(2)}) collective-permute-start(bf16[1024,512]{1,0:T(8,128)(2,1)} %refs_0_.4), channel_id=1, source_target_pairs={{8,16},{12,20},{16,8},{20,12},{9,17},{13,21},{17,9},{21,13},{10,18... | collective-permute-start | bytes 3145736 | tf_op jit(solution)/shard_map/ppermute | solution.py:624
  135.2 1.7 copy-done.4
  136.9 8.2 %shard_map.91.refs_2_ = bf16[4,256,256]{2,1,0:T(8,128)(2,1)} custom-call(s32[9]{0:T(128)} %stack.92.place, bf16[256,1024]{1,0:T(8,128)(2,1)} %refs_0_.3, bf16[272,1024]{1,0:T(8,128)(2,1)} %copy-done.5, bf16[272,1024]{1,0:T(8,128)(2,1)} %copy-done.6, bf16[272,1024]{1,0:T(8,128)(2,1)} %copy-done.7, bf16[256,1024]{1,0:T(8,128)(2,1)} %collective-permute-done.3.refs_4_, ...), custom_call_target="tpu_custom_call" | custom-call | flops 2147483648 | bytes 16777216 | tf_op jit(solution)/shard_map/pallas_call | solution.py:261
  145.1 10.6 %collective-permute-done.10.refs_2_ = bf16[1024,512]{1,0:T(8,128)(2,1)} collective-permute-done((bf16[1024,512]{1,0:T(8,128)(2,1)}, bf16[1024,512]{1,0:T(8,128)(2,1)}, u32[]{:S(2)}, u32[]{:S(2)}) %collective-permute-start.10) | collective-permute-done | bytes 1048608 | tf_op jit(solution)/shard_map/ppermute | solution.py:567
  155.7 2.8 collective-permute-done.11.refs_4_
  158.6 1.2 collective-permute-start.13
  159.8 3.1 %collective-permute-start.16 = (bf16[1024,512]{1,0:T(8,128)(2,1)}, bf16[1024,512]{1,0:T(8,128)(2,1)}, u32[]{:S(2)}, u32[]{:S(2)}) collective-permute-start(bf16[1024,512]{1,0:T(8,128)(2,1)} %collective-permute-done.10.refs_2_), channel_id=1, source_target_pairs={{8,16},{12,20},{16,8},{20,12},{9,17},{13,21},{17,9},{21,13},{10,18... | collective-permute-start | bytes 3145736 | tf_op jit(solution)/shard_map/ppermute | solution.py:632
  162.9 9.4 %shard_map.92 = (bf16[4,256,256]{2,1,0:T(8,128)(2,1)}, bf16[4,256,256]{2,1,0:T(8,128)(2,1)}) custom-call(s32[9]{0:T(128)} %stack.92.place, bf16[256,1024]{1,0:T(8,128)(2,1)} %refs_0_.3, bf16[272,1024]{1,0:T(8,128)(2,1)} %copy-done.5, bf16[272,1024]{1,0:T(8,128)(2,1)} %copy-done.6, bf16[272,1024]{1,0:T(8,128)(2,1)} %copy-done.7, ...), custom_call_target="tpu_custom_call" | custom-call | flops 4294967296 | bytes 16777216 | tf_op jit(solution)/shard_map/pallas_call | solution.py:261
  174.0 2.9 collective-permute-start.18
  176.9 9.4 %collective-permute-done.16.refs_8_ = bf16[1024,512]{1,0:T(8,128)(2,1)} collective-permute-done((bf16[1024,512]{1,0:T(8,128)(2,1)}, bf16[1024,512]{1,0:T(8,128)(2,1)}, u32[]{:S(2)}, u32[]{:S(2)}) %collective-permute-start.16) | collective-permute-done | bytes 1048608 | tf_op jit(solution)/shard_map/ppermute | solution.py:632
  186.3 1.3 collective-permute-start.21
  187.6 0.8 copy-done.21
  188.4 0.8 copy-done.22
  189.2 2.3 collective-permute-start.19
  192.1 16.7 %shard_map.93 = (bf16[4,256,512]{2,1,0:T(8,128)(2,1)}, bf16[4,256,512]{2,1,0:T(8,128)(2,1)}) custom-call(s32[9]{0:T(128)} %stack.92.place, f32[4]{0:T(128)} %dynamic-slice_bitcast_fusion.1.mix, f32[66]{0:T(128)} %fusion.13.weights, bf16[4,256,256]{2,1,0:T(8,128)(2,1)} %get-tuple-element.75.refs_0_, bf16[4,256,256]{2,1,0:T(8,128)(2,1)} %copy-done.21, ...), custom_call_target="tpu_custom_call" | custom-call | flops 5368709120 | bytes 16777216 | tf_op jit(solution)/shard_map/pallas_call | solution.py:471
  208.9 11.8 %collective-permute-done.19.refs_10_ = bf16[1024,512]{1,0:T(8,128)(2,1)} collective-permute-done((bf16[1024,512]{1,0:T(8,128)(2,1)}, bf16[1024,512]{1,0:T(8,128)(2,1)}, u32[]{:S(2)}, u32[]{:S(2)}) %collective-permute-start.19) | collective-permute-done | bytes 1048608 | tf_op jit(solution)/shard_map/ppermute | solution.py:642
  220.7 1.3 collective-permute-start.22
  222.5 3.6 %collective-permute-done.22 = bf16[4,256,512]{2,1,0:T(8,128)(2,1)} collective-permute-done((bf16[4,256,512]{2,1,0:T(8,128)(2,1)}, bf16[4,256,512]{2,1,0:T(8,128)(2,1)}, u32[]{:S(2)}, u32[]{:S(2)}) %collective-permute-start.22) | collective-permute-done | bytes 1048608 | tf_op jit(solution)/shard_map/ppermute | solution.py:567
  226.1 1.9 convert_add_fusion
  228.0 0.9 fusion.2
  228.9 2.2 collective-permute-start.23
  231.1 1.0 collective-permute-start.24
  233.0 0.8 dynamic-slice_bitcast_fusion.own
  233.9 8.0 %collective-permute-done.23.r1 = bf16[256,512]{1,0:T(8,128)(2,1)S(1)} collective-permute-done((bf16[256,512]{1,0:T(8,128)(2,1)}, bf16[256,512]{1,0:T(8,128)(2,1)S(1)}, u32[]{:S(2)}, u32[]{:S(2)}) %collective-permute-start.23) | collective-permute-done | bytes 262176 | tf_op jit(solution)/shard_map/ppermute | solution.py:567
  241.8 7.0 %collective-permute-done.24.r2 = bf16[256,512]{1,0:T(8,128)(2,1)} collective-permute-done((bf16[256,512]{1,0:T(8,128)(2,1)}, bf16[256,512]{1,0:T(8,128)(2,1)}, u32[]{:S(2)}, u32[]{:S(2)}) %collective-permute-start.24) | collective-permute-done | bytes 262176 | tf_op jit(solution)/shard_map/ppermute | solution.py:567
  248.8 6.8 %collective-permute-done.25.r3 = bf16[256,512]{1,0:T(8,128)(2,1)} collective-permute-done((bf16[256,512]{1,0:T(8,128)(2,1)}, bf16[256,512]{1,0:T(8,128)(2,1)}, u32[]{:S(2)}, u32[]{:S(2)}) %collective-permute-start.25) | collective-permute-done | bytes 262176 | tf_op jit(solution)/shard_map/ppermute | solution.py:567
  255.6 7.9 %shard_map.94 = (bf16[256,1024]{1,0:T(8,128)(2,1)}, bf16[256,1024]{1,0:T(8,128)(2,1)}, bf16[256,1024]{1,0:T(8,128)(2,1)}, bf16[256,1024]{1,0:T(8,128)(2,1)}) custom-call(s32[10]{0:T(128)} %concatenate.43.place, f32[256,512]{1,0:T(8,128)} %dynamic-slice_bitcast_fusion.own, bf16[256,512]{1,0:T(8,128)(2,1)} %copy-done.17, ...), custom_call_target="tpu_custom_call" | custom-call | flops 2147483648 | bytes 11534336 | tf_op jit(solution)/shard_map/pallas_call | solution.py:548
  263.5 2.2 collective-permute-start.31
  266.2 10.7 %collective-permute-done.31 = bf16[256,1024]{1,0:T(8,128)(2,1)S(1)} collective-permute-done((bf16[256,1024]{1,0:T(8,128)(2,1)}, bf16[256,1024]{1,0:T(8,128)(2,1)S(1)}, u32[]{:S(2)}, u32[]{:S(2)}) %collective-permute-start.31) | collective-permute-done | bytes 524320 | tf_op jit(solution)/shard_map/ppermute | solution.py:567
  276.9 12.8 %collective-permute-done.30 = bf16[256,1024]{1,0:T(8,128)(2,1)S(1)} collective-permute-done((bf16[256,1024]{1,0:T(8,128)(2,1)}, bf16[256,1024]{1,0:T(8,128)(2,1)S(1)}, u32[]{:S(2)}, u32[]{:S(2)}) %collective-permute-start.30) | collective-permute-done | bytes 524320 | tf_op jit(solution)/shard_map/ppermute | solution.py:567
  289.8 2.2 add_convert_fusion
  (88 shorter events, 8.9 us)
Async XLA Ops:
  0.0 191.5 %copy-start = (f32[8,4]{0,1:T(4,128)S(1)}, f32[8,4]{0,1:T(4,128)}, u32[]{:S(2)}) copy-start(f32[8,4]{0,1:T(4,128)} %param.15) | copy-start | bytes 388
  0.0 7.9 %copy-start.13 = (bf16[512,1024]{1,0:T(8,128)(2,1)S(1)}, bf16[512,1024]{1,0:T(8,128)(2,1)}, u32[]{:S(2)}) copy-start(bf16[512,1024]{1,0:T(8,128)(2,1)} %param.13) | copy-start | bytes 3145732
  0.0 8.7 %copy-start.14 = (bf16[512,1024]{1,0:T(8,128)(2,1)S(1)}, bf16[512,1024]{1,0:T(8,128)(2,1)}, u32[]{:S(2)}) copy-start(bf16[512,1024]{1,0:T(8,128)(2,1)} %param.12) | copy-start | bytes 3145732
  2.8 6.8 %copy-start.15 = (bf16[512,1024]{1,0:T(8,128)(2,1)S(1)}, bf16[512,1024]{1,0:T(8,128)(2,1)}, u32[]{:S(2)}) copy-start(bf16[512,1024]{1,0:T(8,128)(2,1)} %param.11) | copy-start | bytes 3145732
  2.8 23.5 %collective-permute-start = (bf16[272,1024]{1,0:T(8,128)(2,1)}, bf16[272,1024]{1,0:T(8,128)(2,1)S(1)}, u32[]{:S(2)}, u32[]{:S(2)}) collective-permute-start(bf16[272,1024]{1,0:T(8,128)(2,1)} %pad_maximum_fusion.4), channel_id=1, source_target_pairs={{0,8},{4,12},{8,0},{12,4},{16,24},{20,28},{24,16},{28,20},{1,9},{5... | collective-permute-start | bytes 1671176 | tf_op jit(solution)/shard_map/ppermute | solution.py:567
  4.1 24.3 %collective-permute-start.1 = (bf16[272,1024]{1,0:T(8,128)(2,1)}, bf16[272,1024]{1,0:T(8,128)(2,1)S(1)}, u32[]{:S(2)}, u32[]{:S(2)}) collective-permute-start(bf16[272,1024]{1,0:T(8,128)(2,1)} %pad_maximum_fusion.4), channel_id=1, source_target_pairs={{0,16},{4,20},{8,24},{12,28},{16,0},{20,4},{24,8},{28,12},{1,17},{... | collective-permute-start | bytes 1671176 | tf_op jit(solution)/shard_map/ppermute | solution.py:567
  4.1 49.1 %collective-permute-start.2 = (bf16[272,1024]{1,0:T(8,128)(2,1)}, bf16[272,1024]{1,0:T(8,128)(2,1)S(1)}, u32[]{:S(2)}, u32[]{:S(2)}) collective-permute-start(bf16[272,1024]{1,0:T(8,128)(2,1)} %pad_maximum_fusion.4), channel_id=1, source_target_pairs={{0,24},{4,28},{8,16},{12,20},{16,8},{20,12},{24,0},{28,4},{1,25},{... | collective-permute-start | bytes 1671176 | tf_op jit(solution)/shard_map/ppermute | solution.py:567
  5.4 12.2 %collective-permute-start.3 = (bf16[256,1024]{1,0:T(8,128)(2,1)}, bf16[256,1024]{1,0:T(8,128)(2,1)}, u32[]{:S(2)}, u32[]{:S(2)}) collective-permute-start(bf16[256,1024]{1,0:T(8,128)(2,1)} %refs_0_.3), channel_id=1, source_target_pairs={{0,1},{1,0},{2,3},{3,2},{4,5},{5,4},{6,7},{7,6},{8,9},{9,8},{10,11... | collective-permute-start | bytes 1572872 | tf_op jit(solution)/shard_map/ppermute | solution.py:567
  6.7 11.9 %collective-permute-start.4 = (bf16[256,1024]{1,0:T(8,128)(2,1)}, bf16[256,1024]{1,0:T(8,128)(2,1)}, u32[]{:S(2)}, u32[]{:S(2)}) collective-permute-start(bf16[256,1024]{1,0:T(8,128)(2,1)} %refs_0_.3), channel_id=1, source_target_pairs={{0,2},{1,3},{2,0},{3,1},{4,6},{5,7},{6,4},{7,5},{8,10},{9,11},{10,... | collective-permute-start | bytes 1572872 | tf_op jit(solution)/shard_map/ppermute | solution.py:567
  26.3 28.2 %copy-start.5 = (bf16[272,1024]{1,0:T(8,128)(2,1)}, bf16[272,1024]{1,0:T(8,128)(2,1)S(1)}, u32[]{:S(2)}) copy-start(bf16[272,1024]{1,0:T(8,128)(2,1)S(1)} %collective-permute-done.refs_1_) | copy-start | bytes 1671172
  28.4 26.2 %copy-start.6 = (bf16[272,1024]{1,0:T(8,128)(2,1)}, bf16[272,1024]{1,0:T(8,128)(2,1)S(1)}, u32[]{:S(2)}) copy-start(bf16[272,1024]{1,0:T(8,128)(2,1)S(1)} %collective-permute-done.1.refs_2_) | copy-start | bytes 1671172
  53.3 1.3 copy-start.7
  57.6 70.9 %all-to-all-start = ((bf16[4,512,768]{2,1,0:T(8,128)(2,1)}), bf16[4,512,768]{2,1,0:T(8,128)(2,1)S(1)}, u32[]{:S(2)}, u32[]{:S(2)}) async-start(bf16[4,512,768]{2,1,0:T(8,128)(2,1)} %pad_maximum_fusion), calls=%async_computation | async-start | bytes 6291456 | tf_op jit(solution)/shard_map/all_to_all | solution.py:605
  61.3 39.5 %collective-permute-start.5 = (bf16[896,1024]{1,0:T(8,128)(2,1)}, bf16[896,1024]{1,0:T(8,128)(2,1)S(1)}, u32[]{:S(2)}, u32[]{:S(2)}) collective-permute-start(bf16[896,1024]{1,0:T(8,128)(2,1)} %get-tuple-element.58), channel_id=1, source_target_pairs={{0,1},{1,0},{2,3},{3,2},{4,5},{5,4},{6,7},{7,6},{8,9},{9,8},{10,11... | collective-permute-start | bytes 5505032 | tf_op jit(solution)/shard_map/ppermute | solution.py:567
  62.6 39.2 %collective-permute-start.6 = (bf16[896,1024]{1,0:T(8,128)(2,1)}, bf16[896,1024]{1,0:T(8,128)(2,1)S(1)}, u32[]{:S(2)}, u32[]{:S(2)}) collective-permute-start(bf16[896,1024]{1,0:T(8,128)(2,1)} %get-tuple-element.59), channel_id=1, source_target_pairs={{0,2},{1,3},{2,0},{3,1},{4,6},{5,7},{6,4},{7,5},{8,10},{9,11},{10,... | collective-permute-start | bytes 5505032 | tf_op jit(solution)/shard_map/ppermute | solution.py:567
  100.8 17.0 %copy-start.2 = (bf16[896,1024]{1,0:T(8,128)(2,1)}, bf16[896,1024]{1,0:T(8,128)(2,1)S(1)}, u32[]{:S(2)}) copy-start(bf16[896,1024]{1,0:T(8,128)(2,1)S(1)} %collective-permute-done.5.refs_5_) | copy-start | bytes 5505028
  101.8 16.1 %copy-start.3 = (bf16[896,1024]{1,0:T(8,128)(2,1)}, bf16[896,1024]{1,0:T(8,128)(2,1)S(1)}, u32[]{:S(2)}) copy-start(bf16[896,1024]{1,0:T(8,128)(2,1)S(1)} %collective-permute-done.6.refs_7_) | copy-start | bytes 5505028
  101.8 16.1 %collective-permute-start.7 = (bf16[384,1024]{1,0:T(8,128)(2,1)S(1)}, bf16[384,1024]{1,0:T(8,128)(2,1)S(1)}, u32[]{:S(2)}, u32[]{:S(2)}) collective-permute-start(bf16[384,1024]{1,0:T(8,128)(2,1)S(1)} %slice.57), channel_id=1, source_target_pairs={{0,2},{1,3},{2,0},{3,1},{4,6},{5,7},{6,4},{7,5},{8,10},{9,11},{10,... | collective-permute-start | bytes 2359304 | tf_op jit(solution)/shard_map/ppermute | solution.py:567
  103.2 15.6 %collective-permute-start.8 = (bf16[384,1024]{1,0:T(8,128)(2,1)S(1)}, bf16[384,1024]{1,0:T(8,128)(2,1)}, u32[]{:S(2)}, u32[]{:S(2)}) collective-permute-start(bf16[384,1024]{1,0:T(8,128)(2,1)S(1)} %slice.58), channel_id=1, source_target_pairs={{0,1},{1,0},{2,3},{3,2},{4,5},{5,4},{6,7},{7,6},{8,9},{9,8},{10,11... | collective-permute-start | bytes 2359304 | tf_op jit(solution)/shard_map/ppermute | solution.py:567
  117.9 0.9 copy-start.16
  128.5 6.7 %copy-start.1 = (bf16[4,512,768]{2,1,0:T(8,128)(2,1)}, bf16[4,512,768]{2,1,0:T(8,128)(2,1)S(1)}, u32[]{:S(2)}) copy-start(bf16[4,512,768]{2,1,0:T(8,128)(2,1)S(1)} %all-to-all-done.refs_10_) | copy-start | bytes 9437188
  128.5 31.2 %copy-start.8 = (bf16[1024,512]{1,0:T(8,128)(2,1)S(1)}, bf16[1024,512]{1,0:T(8,128)(2,1)}, u32[]{:S(2)}) copy-start(bf16[1024,512]{1,0:T(8,128)(2,1)} %refs_0_.4) | copy-start | bytes 3145732
  128.5 6.7 %collective-permute-start.9 = (bf16[4,512,768]{2,1,0:T(8,128)(2,1)S(1)}, bf16[4,512,768]{2,1,0:T(8,128)(2,1)S(1)}, u32[]{:S(2)}, u32[]{:S(2)}) collective-permute-start(bf16[4,512,768]{2,1,0:T(8,128)(2,1)S(1)} %all-to-all-done.refs_10_), channel_id=1, source_target_pairs={{0,4},{4,0},{8,12},{12,8},{16,20},{20,16},{24,28},{28,24},{1,5},{5... | collective-permute-start | bytes 9437192 | tf_op jit(solution)/shard_map/ppermute | solution.py:567
  129.9 25.8 %collective-permute-start.10 = (bf16[1024,512]{1,0:T(8,128)(2,1)}, bf16[1024,512]{1,0:T(8,128)(2,1)}, u32[]{:S(2)}, u32[]{:S(2)}) collective-permute-start(bf16[1024,512]{1,0:T(8,128)(2,1)} %refs_0_.4), channel_id=1, source_target_pairs={{0,8},{4,12},{8,0},{12,4},{16,24},{20,28},{24,16},{28,20},{1,9},{5... | collective-permute-start | bytes 3145736 | tf_op jit(solution)/shard_map/ppermute | solution.py:567
  132.0 26.6 %collective-permute-start.11 = (bf16[1024,512]{1,0:T(8,128)(2,1)}, bf16[1024,512]{1,0:T(8,128)(2,1)}, u32[]{:S(2)}, u32[]{:S(2)}) collective-permute-start(bf16[1024,512]{1,0:T(8,128)(2,1)} %refs_0_.4), channel_id=1, source_target_pairs={{8,16},{12,20},{16,8},{20,12},{9,17},{13,21},{17,9},{21,13},{10,18... | collective-permute-start | bytes 3145736 | tf_op jit(solution)/shard_map/ppermute | solution.py:624
  135.2 1.7 copy-start.4
  158.6 13.8 %collective-permute-start.12 = (bf16[4,256,256]{2,1,0:T(8,128)(2,1)}, bf16[4,256,256]{2,1,0:T(8,128)(2,1)S(1)}, u32[]{:S(2)}, u32[]{:S(2)}) collective-permute-start(bf16[4,256,256]{2,1,0:T(8,128)(2,1)} %shard_map.91.refs_2_), channel_id=1, source_target_pairs={{0,8},{4,12},{8,0},{12,4},{16,24},{20,28},{24,16},{28,20},{1,9},{5... | collective-permute-start | bytes 1572872 | tf_op jit(solution)/shard_map/ppermute | solution.py:567
  158.6 13.8 %collective-permute-start.13 = (bf16[4,256,256]{2,1,0:T(8,128)(2,1)}, bf16[4,256,256]{2,1,0:T(8,128)(2,1)S(1)}, u32[]{:S(2)}, u32[]{:S(2)}) collective-permute-start(bf16[4,256,256]{2,1,0:T(8,128)(2,1)} %shard_map.91.refs_2_), channel_id=1, source_target_pairs={{0,4},{4,0},{8,12},{12,8},{16,20},{20,16},{24,28},{28,24},{1,5},{5... | collective-permute-start | bytes 1572872 | tf_op jit(solution)/shard_map/ppermute | solution.py:567
  159.7 14.2 %collective-permute-start.17 = (bf16[1024,512]{1,0:T(8,128)(2,1)S(1)}, bf16[1024,512]{1,0:T(8,128)(2,1)S(1)}, u32[]{:S(2)}, u32[]{:S(2)}) collective-permute-start(bf16[1024,512]{1,0:T(8,128)(2,1)S(1)} %copy-done.8), channel_id=1, source_target_pairs={{0,4},{4,0},{8,12},{12,8},{16,20},{20,16},{24,28},{28,24},{1,5},{5... | collective-permute-start | bytes 3145736 | tf_op jit(solution)/shard_map/ppermute | solution.py:567
  159.8 26.5 %collective-permute-start.16 = (bf16[1024,512]{1,0:T(8,128)(2,1)}, bf16[1024,512]{1,0:T(8,128)(2,1)}, u32[]{:S(2)}, u32[]{:S(2)}) collective-permute-start(bf16[1024,512]{1,0:T(8,128)(2,1)} %collective-permute-done.10.refs_2_), channel_id=1, source_target_pairs={{8,16},{12,20},{16,8},{20,12},{9,17},{13,21},{17,9},{21,13},{10,18... | collective-permute-start | bytes 3145736 | tf_op jit(solution)/shard_map/ppermute | solution.py:632
  172.4 4.5 %copy-start.19 = (bf16[4,256,256]{2,1,0:T(8,128)(2,1)}, bf16[4,256,256]{2,1,0:T(8,128)(2,1)S(1)}, u32[]{:S(2)}) copy-start(bf16[4,256,256]{2,1,0:T(8,128)(2,1)S(1)} %collective-permute-done.12.refs_3_) | copy-start | bytes 1572868
  172.4 0.8 copy-start.20
  172.4 15.2 %collective-permute-start.14 = (bf16[4,256,256]{2,1,0:T(8,128)(2,1)}, bf16[4,256,256]{2,1,0:T(8,128)(2,1)S(1)}, u32[]{:S(2)}, u32[]{:S(2)}) collective-permute-start(bf16[4,256,256]{2,1,0:T(8,128)(2,1)} %get-tuple-element.76), channel_id=1, source_target_pairs={{0,4},{4,0},{8,12},{12,8},{16,20},{20,16},{24,28},{28,24},{1,5},{5... | collective-permute-start | bytes 1572872 | tf_op jit(solution)/shard_map/ppermute | solution.py:567
  173.2 14.4 %collective-permute-start.15 = (bf16[4,256,256]{2,1,0:T(8,128)(2,1)S(1)}, bf16[4,256,256]{2,1,0:T(8,128)(2,1)S(1)}, u32[]{:S(2)}, u32[]{:S(2)}) collective-permute-start(bf16[4,256,256]{2,1,0:T(8,128)(2,1)S(1)} %collective-permute-done.12.refs_3_), channel_id=1, source_target_pairs={{0,4},{4,0},{8,12},{12,8},{16,20},{20,16},{24,28},{28,24},{1,5},{5... | collective-permute-start | bytes 1572872 | tf_op jit(solution)/shard_map/ppermute | solution.py:567
  173.9 34.9 %collective-permute-start.20 = (bf16[1024,512]{1,0:T(8,128)(2,1)}, bf16[1024,512]{1,0:T(8,128)(2,1)S(1)}, u32[]{:S(2)}, u32[]{:S(2)}) collective-permute-start(bf16[1024,512]{1,0:T(8,128)(2,1)} %collective-permute-done.10.refs_2_), channel_id=1, source_target_pairs={{0,4},{4,0},{8,12},{12,8},{16,20},{20,16},{24,28},{28,24},{1,5},{5... | collective-permute-start | bytes 3145736 | tf_op jit(solution)/shard_map/ppermute | solution.py:567
  174.0 34.8 %copy-start.9 = (bf16[1024,512]{1,0:T(8,128)(2,1)}, bf16[1024,512]{1,0:T(8,128)(2,1)S(1)}, u32[]{:S(2)}) copy-start(bf16[1024,512]{1,0:T(8,128)(2,1)S(1)} %collective-permute-done.17.refs_1_) | copy-start | bytes 3145732
  174.0 34.9 %collective-permute-start.18 = (bf16[1024,512]{1,0:T(8,128)(2,1)}, bf16[1024,512]{1,0:T(8,128)(2,1)}, u32[]{:S(2)}, u32[]{:S(2)}) collective-permute-start(bf16[1024,512]{1,0:T(8,128)(2,1)} %collective-permute-done.11.refs_4_), channel_id=1, source_target_pairs={{8,0},{12,4},{16,24},{20,28},{9,1},{13,5},{17,25},{21,29},{10,2},{... | collective-permute-start | bytes 3145736 | tf_op jit(solution)/shard_map/ppermute | solution.py:633
  186.3 22.5 %collective-permute-start.21 = (bf16[1024,512]{1,0:T(8,128)(2,1)}, bf16[1024,512]{1,0:T(8,128)(2,1)S(1)}, u32[]{:S(2)}, u32[]{:S(2)}) collective-permute-start(bf16[1024,512]{1,0:T(8,128)(2,1)} %collective-permute-done.11.refs_4_), channel_id=1, source_target_pairs={{0,4},{4,0},{8,12},{12,8},{16,20},{20,16},{24,28},{28,24},{1,5},{5... | collective-permute-start | bytes 3145736 | tf_op jit(solution)/shard_map/ppermute | solution.py:567
  187.6 0.8 copy-start.21
  188.4 0.8 copy-start.22
  189.2 31.5 %collective-permute-start.19 = (bf16[1024,512]{1,0:T(8,128)(2,1)}, bf16[1024,512]{1,0:T(8,128)(2,1)}, u32[]{:S(2)}, u32[]{:S(2)}) collective-permute-start(bf16[1024,512]{1,0:T(8,128)(2,1)} %collective-permute-done.16.refs_8_), channel_id=1, source_target_pairs={{8,0},{12,4},{16,24},{20,28},{9,1},{13,5},{17,25},{21,29},{10,2},{... | collective-permute-start | bytes 3145736 | tf_op jit(solution)/shard_map/ppermute | solution.py:642
  208.8 13.7 %copy-start.10 = (bf16[1024,512]{1,0:T(8,128)(2,1)}, bf16[1024,512]{1,0:T(8,128)(2,1)S(1)}, u32[]{:S(2)}) copy-start(bf16[1024,512]{1,0:T(8,128)(2,1)S(1)} %collective-permute-done.20.refs_3_) | copy-start | bytes 3145732
  208.9 13.7 %copy-start.11 = (bf16[1024,512]{1,0:T(8,128)(2,1)}, bf16[1024,512]{1,0:T(8,128)(2,1)S(1)}, u32[]{:S(2)}) copy-start(bf16[1024,512]{1,0:T(8,128)(2,1)S(1)} %collective-permute-done.21.refs_5_) | copy-start | bytes 3145732
  220.7 5.4 %collective-permute-start.22 = (bf16[4,256,512]{2,1,0:T(8,128)(2,1)}, bf16[4,256,512]{2,1,0:T(8,128)(2,1)}, u32[]{:S(2)}, u32[]{:S(2)}) collective-permute-start(bf16[4,256,512]{2,1,0:T(8,128)(2,1)} %get-tuple-element.87), channel_id=1, source_target_pairs={{0,4},{4,0},{8,12},{12,8},{16,20},{20,16},{24,28},{28,24},{1,5},{5... | collective-permute-start | bytes 3145736 | tf_op jit(solution)/shard_map/ppermute | solution.py:567
  222.0 10.0 %collective-permute-start.27 = (bf16[1024,512]{1,0:T(8,128)(2,1)}, bf16[1024,512]{1,0:T(8,128)(2,1)S(1)}, u32[]{:S(2)}, u32[]{:S(2)}) collective-permute-start(bf16[1024,512]{1,0:T(8,128)(2,1)} %collective-permute-done.16.refs_8_), channel_id=1, source_target_pairs={{0,4},{4,0},{8,12},{12,8},{16,20},{20,16},{24,28},{28,24},{1,5},{5... | collective-permute-start | bytes 3145736 | tf_op jit(solution)/shard_map/ppermute | solution.py:567
  222.0 11.8 %collective-permute-start.26 = (bf16[1024,512]{1,0:T(8,128)(2,1)}, bf16[1024,512]{1,0:T(8,128)(2,1)}, u32[]{:S(2)}, u32[]{:S(2)}) collective-permute-start(bf16[1024,512]{1,0:T(8,128)(2,1)} %collective-permute-done.18.refs_6_), channel_id=1, source_target_pairs={{0,4},{4,0},{8,12},{12,8},{16,20},{20,16},{24,28},{28,24},{1,5},{5... | collective-permute-start | bytes 3145736 | tf_op jit(solution)/shard_map/ppermute | solution.py:567
  222.5 11.3 %collective-permute-start.28 = (bf16[1024,512]{1,0:T(8,128)(2,1)}, bf16[1024,512]{1,0:T(8,128)(2,1)}, u32[]{:S(2)}, u32[]{:S(2)}) collective-permute-start(bf16[1024,512]{1,0:T(8,128)(2,1)} %collective-permute-done.19.refs_10_), channel_id=1, source_target_pairs={{0,4},{4,0},{8,12},{12,8},{16,20},{20,16},{24,28},{28,24},{1,5},{5... | collective-permute-start | bytes 3145736 | tf_op jit(solution)/shard_map/ppermute | solution.py:567
  222.5 9.9 %copy-start.18 = (s32[9]{0:T(128)S(1)}, s32[9]{0:T(128)}, u32[]{:S(2)}) copy-start(s32[9]{0:T(128)} %stack.92.place) | copy-start | bytes 112
  228.9 12.9 %collective-permute-start.23 = (bf16[256,512]{1,0:T(8,128)(2,1)}, bf16[256,512]{1,0:T(8,128)(2,1)S(1)}, u32[]{:S(2)}, u32[]{:S(2)}) collective-permute-start(bf16[256,512]{1,0:T(8,128)(2,1)} %get-tuple-element.99), channel_id=1, source_target_pairs={{0,8},{4,12},{8,0},{12,4},{16,24},{20,28},{24,16},{28,20},{1,9},{5... | collective-permute-start | bytes 786440 | tf_op jit(solution)/shard_map/ppermute | solution.py:567
  231.1 17.7 %collective-permute-start.24 = (bf16[256,512]{1,0:T(8,128)(2,1)}, bf16[256,512]{1,0:T(8,128)(2,1)}, u32[]{:S(2)}, u32[]{:S(2)}) collective-permute-start(bf16[256,512]{1,0:T(8,128)(2,1)} %get-tuple-element.98), channel_id=1, source_target_pairs={{0,16},{4,20},{8,24},{12,28},{16,0},{20,4},{24,8},{28,12},{1,17},{... | collective-permute-start | bytes 786440 | tf_op jit(solution)/shard_map/ppermute | solution.py:567
  232.1 23.6 %copy-start.12 = (bf16[1024,512]{1,0:T(8,128)(2,1)}, bf16[1024,512]{1,0:T(8,128)(2,1)S(1)}, u32[]{:S(2)}) copy-start(bf16[1024,512]{1,0:T(8,128)(2,1)S(1)} %collective-permute-done.27.refs_9_) | copy-start | bytes 3145732
  232.1 23.5 %collective-permute-start.25 = (bf16[256,512]{1,0:T(8,128)(2,1)}, bf16[256,512]{1,0:T(8,128)(2,1)}, u32[]{:S(2)}, u32[]{:S(2)}) collective-permute-start(bf16[256,512]{1,0:T(8,128)(2,1)} %get-tuple-element.97), channel_id=1, source_target_pairs={{0,24},{4,28},{8,16},{12,20},{16,8},{20,12},{24,0},{28,4},{1,25},{... | collective-permute-start | bytes 786440 | tf_op jit(solution)/shard_map/ppermute | solution.py:567
  241.8 13.8 %copy-start.17 = (bf16[256,512]{1,0:T(8,128)(2,1)}, bf16[256,512]{1,0:T(8,128)(2,1)S(1)}, u32[]{:S(2)}) copy-start(bf16[256,512]{1,0:T(8,128)(2,1)S(1)} %collective-permute-done.23.r1) | copy-start | bytes 786436
  263.5 13.4 %collective-permute-start.31 = (bf16[256,1024]{1,0:T(8,128)(2,1)}, bf16[256,1024]{1,0:T(8,128)(2,1)S(1)}, u32[]{:S(2)}, u32[]{:S(2)}) collective-permute-start(bf16[256,1024]{1,0:T(8,128)(2,1)} %get-tuple-element.96), channel_id=1, source_target_pairs={{0,3},{1,2},{2,1},{3,0},{4,7},{5,6},{6,5},{7,4},{8,11},{9,10},{10,... | collective-permute-start | bytes 1572872 | tf_op jit(solution)/shard_map/ppermute | solution.py:567
  265.7 24.0 %collective-permute-start.30 = (bf16[256,1024]{1,0:T(8,128)(2,1)}, bf16[256,1024]{1,0:T(8,128)(2,1)S(1)}, u32[]{:S(2)}, u32[]{:S(2)}) collective-permute-start(bf16[256,1024]{1,0:T(8,128)(2,1)} %get-tuple-element.95), channel_id=1, source_target_pairs={{0,2},{1,3},{2,0},{3,1},{4,6},{5,7},{6,4},{7,5},{8,10},{9,11},{10,... | collective-permute-start | bytes 1572872 | tf_op jit(solution)/shard_map/ppermute | solution.py:567
  266.0 23.8 %collective-permute-start.29 = (bf16[256,1024]{1,0:T(8,128)(2,1)}, bf16[256,1024]{1,0:T(8,128)(2,1)S(1)}, u32[]{:S(2)}, u32[]{:S(2)}) collective-permute-start(bf16[256,1024]{1,0:T(8,128)(2,1)} %get-tuple-element.94), channel_id=1, source_target_pairs={{0,1},{1,0},{2,3},{3,2},{4,5},{5,4},{6,7},{7,6},{8,9},{9,8},{10,11... | collective-permute-start | bytes 1572872 | tf_op jit(solution)/shard_map/ppermute | solution.py:567

commit v10 on v9

--- a/solution.py
+++ b/solution.py
@@ -615,18 +615,20 @@
     cosine, sine = jnp.cos(angle), jnp.sin(angle)
     cosine = jnp.concatenate([cosine, cosine], -1)
     sine = jnp.concatenate([-sine, sine], -1)
-    x_rest, y_rest, cosine, sine, w_out = barrier((x_rest, y_rest, cosine, sine, w_out))
-    c_low = swapped(x_rest[: 3 * half], "head", 2)
-    c_high = swapped(y_rest[3 * half : 3 * rows], "head", 1)
     middle = [(2, 4), (3, 5), (4, 2), (5, 3)]
     outward = [(2, 0), (3, 1), (4, 6), (5, 7)]
     out_near = swapped(w_out, "ctx", 2)
+    x_rest, y_rest, cosine, sine, out_near, w_out = barrier(
+        (x_rest, y_rest, cosine, sine, out_near, w_out)
+    )
+    c_low = swapped(x_rest[: 3 * half], "head", 2)
+    c_high = swapped(y_rest[3 * half : 3 * rows], "head", 1)
     out_across = lax.ppermute(w_out, "ctx", middle)
-    c_low, c_high, w_same = barrier((c_low, c_high, w_same))
+    c_low, c_high, w_same, out_across = barrier((c_low, c_high, w_same, out_across))
     w_swap = swapped(w_same, "ctx", 1)
     sources = place, [activations] + list(far), (x0, x_rest, y0, y_rest, c_low, c_high), w_same, w_swap
     (v_pair,) = project(*sources)
-    place, v_pair, out_near, out_across = barrier((place, v_pair, out_near, out_across))
+    place, v_pair = barrier((place, v_pair))
     v_next = swapped(v_pair, "ctx", 2)
     v_pair_other = swapped(v_pair, "ctx", 1)
     out_across_next = lax.ppermute(out_near, "ctx", middle)
@@ -635,10 +637,10 @@
     mine, theirs, v_next, v_pair_other = barrier((mine, theirs, v_next, v_pair_other))
     other = swapped(theirs, "ctx", 1)
     v_next_other = swapped(v_next, "ctx", 1)
+    other, v_next_other, out_across_next, out_passed = barrier(
+        (other, v_next_other, out_across_next, out_passed)
+    )
     out_own_swap = swapped(w_out, "ctx", 1)
-    other, v_next_other, out_across_next, out_own_swap = barrier(
-        (other, v_next_other, out_across_next, out_own_swap)
-    )
     out_passed_next = lax.ppermute(out_across_next, "ctx", outward)
     out_near_swap, out_across_swap = swapped(out_near, "ctx", 1), swapped(out_across, "ctx", 1)
     group_rows = lax.dynamic_slice_in_dim(head_mix, GROUP * (ctx // GROUP), GROUP, 0)
@@ -646,8 +648,8 @@
     out_mine, out_theirs = attend_head(
         place, mix, weights, mine, other, (v_pair, v_next, v_pair_other, v_next_other)
     )
-    out_mine, out_theirs, out_passed, out_passed_next, out_near_swap, out_across_swap = barrier(
-        (out_mine, out_theirs, out_passed, out_passed_next, out_near_swap, out_across_swap)
+    out_mine, out_theirs, out_passed_next, out_own_swap, out_near_swap, out_across_swap = barrier(
+        (out_mine, out_theirs, out_passed_next, out_own_swap, out_near_swap, out_across_swap)
     )
     out_parts = [w_out, out_own_swap, out_near, out_near_swap, out_across, out_across_swap]
     for part in (out_passed, out_across_next, out_passed_next):

time: 294 us -> 312 us (1.061)
  waiting for transfers between devices: 177 us -> 194 us
    ppermute x28, waiting for transfers between devices: 143 us -> 170 us  [swapped(): return lax.ppermute(value, axis, [(i, i ^ mask) for i in range(count)])]
    all_to_all x1, waiting for transfers between devices: 9.72 us -> 0.01 us  [per_device_one_head(): w_same = lax.all_to_all(w_pieces, 'ctx', 0, 0, axis_index_groups=same_core)]
    ppermute x1, waiting for transfers between devices: 11.8 us -> 4.55 us  [per_device_one_head(): out_passed_next = lax.ppermute(out_across_next, 'ctx', outward)]
    ppermute x1, waiting for transfers between devices: 0.01 us -> 5.82 us  [per_device_one_head(): out_passed = lax.ppermute(out_across, 'ctx', outward)]
  transfers between devices with their start and end apart: 33 -> 33, of which waited for: 20 -> 19; matrix products, arithmetic and copies ran while one was open for 6% -> 6% of each run, Pallas kernels for 12% -> 8%
where the time goes in v10:
time: 312 us
  waiting for transfers between devices  194 us (62%)
  starting transfers between devices  42.8 us (14%)
  Pallas kernels  42.2 us (14%)
  other arithmetic  19.6 us (6%)
  local copies, waits for them, and re-layouts  12.6 us (4%)
    ppermute x28, waiting for transfers between devices, swapped(): return lax.ppermute(value, axis, [(i, i ^ mask) for i in range(count)])  170 us
    ppermute x28, starting transfers between devices, swapped(): return lax.ppermute(value, axis, [(i, i ^ mask) for i in range(count)])  25.9 us
    pallas_call x2, Pallas kernels, project(): pl.pallas_call(functools.partial(project_kernel, rows, first_col), out_sh...  17.6 us
    pallas_call x1, Pallas kernels, attend_head(): pl.pallas_call(attend_kernel, grid=(count,), out_shape=(out, out), in_spe...  16.7 us
    ppermute x1, waiting for transfers between devices, per_device_one_head(): out_across_next = lax.ppermute(out_near, 'ctx', middle)  10.2 us
    pallas_call x1, Pallas kernels, finish(): pl.pallas_call(finish_kernel, in_specs=[whole(pltpu.SMEM)] + [whole(pltpu...  7.94 us
  transfers between devices with their start and end apart: 33, of which 19 were waited for; matrix products, arithmetic and copies ran while one was open for 6% of the time, Pallas kernels for 8%

profile of v10, /device:TPU:17, one launch (start us, length us, event | category | flops | bytes accessed | tf_op | source)
XLA Modules:
  0.0 311.6 jit_solution(7691996051719743107)
XLA Ops:
  0.0 0.8 fusion.11
  0.9 1.9 pad_maximum_fusion.4
  2.8 1.3 collective-permute-start
  4.1 1.3 collective-permute-start.2
  5.4 1.2 collective-permute-start.3
  6.6 1.2 collective-permute-start.4
  8.7 0.9 fusion.15
  9.5 0.9 fusion.14
  11.2 1.2 fusion.13.weights
  12.4 1.4 maximum_bitcast_fusion
  13.8 1.9 pad_maximum_fusion
  15.7 2.0 collective-permute-done.3.refs_4_
  17.6 0.9 collective-permute-done.4.refs_6_
  18.6 7.7 %collective-permute-done.refs_1_ = bf16[272,1024]{1,0:T(8,128)(2,1)S(1)} collective-permute-done((bf16[272,1024]{1,0:T(8,128)(2,1)}, bf16[272,1024]{1,0:T(8,128)(2,1)S(1)}, u32[]{:S(2)}, u32[]{:S(2)}) %collective-permute-start) | collective-permute-done | bytes 557088 | tf_op jit(solution)/shard_map/ppermute | solution.py:567
  26.3 2.0 collective-permute-done.1.refs_2_
  28.4 24.9 %collective-permute-done.2.refs_3_ = bf16[272,1024]{1,0:T(8,128)(2,1)S(1)} collective-permute-done((bf16[272,1024]{1,0:T(8,128)(2,1)}, bf16[272,1024]{1,0:T(8,128)(2,1)S(1)}, u32[]{:S(2)}, u32[]{:S(2)}) %collective-permute-start.2) | collective-permute-done | bytes 557088 | tf_op jit(solution)/shard_map/ppermute | solution.py:567
  53.3 1.1 slice.50
  54.6 1.0 slice.49
  55.5 2.1 pad_maximum_fusion.3
  57.6 3.7 %all-to-all-start = ((bf16[4,512,768]{2,1,0:T(8,128)(2,1)}), bf16[4,512,768]{2,1,0:T(8,128)(2,1)S(1)}, u32[]{:S(2)}, u32[]{:S(2)}) async-start(bf16[4,512,768]{2,1,0:T(8,128)(2,1)} %pad_maximum_fusion), calls=%async_computation | async-start | bytes 6291456 | tf_op jit(solution)/shard_map/all_to_all | solution.py:605
  61.3 1.3 collective-permute-start.5
  62.6 1.2 collective-permute-start.6
  63.8 1.1 collective-permute-start.7
  67.2 1.9 fusion.3
  69.1 1.0 pad_maximum_fusion.5.refs_12_
  70.1 1.0 pad_maximum_fusion.6.refs_13_
  71.1 63.4 %collective-permute-done.7.refs_2_ = bf16[1024,512]{1,0:T(8,128)(2,1)} collective-permute-done((bf16[1024,512]{1,0:T(8,128)(2,1)}, bf16[1024,512]{1,0:T(8,128)(2,1)}, u32[]{:S(2)}, u32[]{:S(2)}) %collective-permute-start.7) | collective-permute-done | bytes 1048608 | tf_op jit(solution)/shard_map/ppermute | solution.py:567
  134.5 1.9 collective-permute-start.10
  136.5 1.3 collective-permute-start.8
  137.9 1.3 collective-permute-start.9
  139.2 13.6 %collective-permute-done.8.refs_8_ = bf16[384,1024]{1,0:T(8,128)(2,1)S(1)} collective-permute-done((bf16[384,1024]{1,0:T(8,128)(2,1)S(1)}, bf16[384,1024]{1,0:T(8,128)(2,1)S(1)}, u32[]{:S(2)}, u32[]{:S(2)}) %collective-permute-start.8) | collective-permute-done | bytes 786464 | tf_op jit(solution)/shard_map/ppermute | solution.py:567
  152.7 1.1 collective-permute-done.9.refs_9_
  153.8 0.9 copy-done.17
  154.7 3.5 %collective-permute-done.10.refs_4_ = bf16[1024,512]{1,0:T(8,128)(2,1)} collective-permute-done((bf16[1024,512]{1,0:T(8,128)(2,1)S(1)}, bf16[1024,512]{1,0:T(8,128)(2,1)}, u32[]{:S(2)}, u32[]{:S(2)}) %collective-permute-start.10) | collective-permute-done | bytes 1048608 | tf_op jit(solution)/shard_map/ppermute | solution.py:626
  158.2 3.9 %collective-permute-start.11 = (bf16[4,512,768]{2,1,0:T(8,128)(2,1)S(1)}, bf16[4,512,768]{2,1,0:T(8,128)(2,1)S(1)}, u32[]{:S(2)}, u32[]{:S(2)}) collective-permute-start(bf16[4,512,768]{2,1,0:T(8,128)(2,1)S(1)} %all-to-all-done.refs_10_), channel_id=1, source_target_pairs={{0,4},{4,0},{8,12},{12,8},{16,20},{20,16},{24,28},{28,24},{1,5},{5... | collective-permute-start | bytes 9437192 | tf_op jit(solution)/shard_map/ppermute | solution.py:567
  162.1 5.3 %collective-permute-done.11.refs_11_ = bf16[4,512,768]{2,1,0:T(8,128)(2,1)S(1)} collective-permute-done((bf16[4,512,768]{2,1,0:T(8,128)(2,1)S(1)}, bf16[4,512,768]{2,1,0:T(8,128)(2,1)S(1)}, u32[]{:S(2)}, u32[]{:S(2)}) %collective-permute-start.11) | collective-permute-done | bytes 3145760 | tf_op jit(solution)/shard_map/ppermute | solution.py:567
  167.4 1.7 copy-done.4
  169.1 8.2 %shard_map.91.refs_2_ = bf16[4,256,256]{2,1,0:T(8,128)(2,1)} custom-call(s32[9]{0:T(128)} %stack.92.place, bf16[256,1024]{1,0:T(8,128)(2,1)} %refs_0_.3, bf16[272,1024]{1,0:T(8,128)(2,1)} %copy-done.5, bf16[272,1024]{1,0:T(8,128)(2,1)} %copy-done.6, bf16[272,1024]{1,0:T(8,128)(2,1)} %copy-done.7, bf16[256,1024]{1,0:T(8,128)(2,1)} %collective-permute-done.3.refs_4_, ...), custom_call_target="tpu_custom_call" | custom-call | flops 2147483648 | bytes 16777216 | tf_op jit(solution)/shard_map/pallas_call | solution.py:261
  177.8 1.9 collective-permute-start.16
  179.7 4.3 %collective-permute-start.17 = (bf16[1024,512]{1,0:T(8,128)(2,1)}, bf16[1024,512]{1,0:T(8,128)(2,1)}, u32[]{:S(2)}, u32[]{:S(2)}) collective-permute-start(bf16[1024,512]{1,0:T(8,128)(2,1)} %collective-permute-done.10.refs_4_), channel_id=1, source_target_pairs={{8,0},{12,4},{16,24},{20,28},{9,1},{13,5},{17,25},{21,29},{10,2},{... | collective-permute-start | bytes 3145736 | tf_op jit(solution)/shard_map/ppermute | solution.py:635
  184.0 9.4 %shard_map.92 = (bf16[4,256,256]{2,1,0:T(8,128)(2,1)}, bf16[4,256,256]{2,1,0:T(8,128)(2,1)}) custom-call(s32[9]{0:T(128)} %stack.92.place, bf16[256,1024]{1,0:T(8,128)(2,1)} %refs_0_.3, bf16[272,1024]{1,0:T(8,128)(2,1)} %copy-done.5, bf16[272,1024]{1,0:T(8,128)(2,1)} %copy-done.6, bf16[272,1024]{1,0:T(8,128)(2,1)} %copy-done.7, ...), custom_call_target="tpu_custom_call" | custom-call | flops 4294967296 | bytes 16777216 | tf_op jit(solution)/shard_map/pallas_call | solution.py:261
  194.3 10.2 %collective-permute-done.16.refs_8_ = bf16[1024,512]{1,0:T(8,128)(2,1)} collective-permute-done((bf16[1024,512]{1,0:T(8,128)(2,1)}, bf16[1024,512]{1,0:T(8,128)(2,1)}, u32[]{:S(2)}, u32[]{:S(2)}) %collective-permute-start.16) | collective-permute-done | bytes 1048608 | tf_op jit(solution)/shard_map/ppermute | solution.py:634
  204.5 1.1 collective-permute-start.20
  205.6 5.8 %collective-permute-done.17.refs_6_ = bf16[1024,512]{1,0:T(8,128)(2,1)} collective-permute-done((bf16[1024,512]{1,0:T(8,128)(2,1)}, bf16[1024,512]{1,0:T(8,128)(2,1)}, u32[]{:S(2)}, u32[]{:S(2)}) %collective-permute-start.17) | collective-permute-done | bytes 1048608 | tf_op jit(solution)/shard_map/ppermute | solution.py:635
  211.4 0.9 collective-permute-start.21
  213.1 0.8 copy-done.23
  213.9 5.1 %collective-permute-start.18 = (bf16[1024,512]{1,0:T(8,128)(2,1)}, bf16[1024,512]{1,0:T(8,128)(2,1)}, u32[]{:S(2)}, u32[]{:S(2)}) collective-permute-start(bf16[1024,512]{1,0:T(8,128)(2,1)} %collective-permute-done.16.refs_8_), channel_id=1, source_target_pairs={{8,0},{12,4},{16,24},{20,28},{9,1},{13,5},{17,25},{21,29},{10,2},{... | collective-permute-start | bytes 3145736 | tf_op jit(solution)/shard_map/ppermute | solution.py:644
  219.6 16.7 %shard_map.93 = (bf16[4,256,512]{2,1,0:T(8,128)(2,1)}, bf16[4,256,512]{2,1,0:T(8,128)(2,1)}) custom-call(s32[9]{0:T(128)} %stack.92.place, f32[4]{0:T(128)} %dynamic-slice_bitcast_fusion.1.mix, f32[66]{0:T(128)} %fusion.13.weights, bf16[4,256,256]{2,1,0:T(8,128)(2,1)} %get-tuple-element.75.refs_0_, bf16[4,256,256]{2,1,0:T(8,128)(2,1)} %copy-done.22, ...), custom_call_target="tpu_custom_call" | custom-call | flops 5368709120 | bytes 16777216 | tf_op jit(solution)/shard_map/pallas_call | solution.py:471
  236.3 4.5 %collective-permute-done.18.refs_10_ = bf16[1024,512]{1,0:T(8,128)(2,1)} collective-permute-done((bf16[1024,512]{1,0:T(8,128)(2,1)}, bf16[1024,512]{1,0:T(8,128)(2,1)}, u32[]{:S(2)}, u32[]{:S(2)}) %collective-permute-start.18) | collective-permute-done | bytes 1048608 | tf_op jit(solution)/shard_map/ppermute | solution.py:644
  240.9 0.8 collective-permute-start.22
  242.2 3.6 %collective-permute-done.22 = bf16[4,256,512]{2,1,0:T(8,128)(2,1)} collective-permute-done((bf16[4,256,512]{2,1,0:T(8,128)(2,1)}, bf16[4,256,512]{2,1,0:T(8,128)(2,1)}, u32[]{:S(2)}, u32[]{:S(2)}) %collective-permute-start.22) | collective-permute-done | bytes 1048608 | tf_op jit(solution)/shard_map/ppermute | solution.py:567
  245.8 1.9 convert_add_fusion
  247.6 1.0 fusion.2
  248.6 2.2 collective-permute-start.23
  250.8 1.2 collective-permute-start.25
  252.5 0.8 dynamic-slice_bitcast_fusion.own
  253.4 7.3 %collective-permute-done.23.r1 = bf16[256,512]{1,0:T(8,128)(2,1)S(1)} collective-permute-done((bf16[256,512]{1,0:T(8,128)(2,1)}, bf16[256,512]{1,0:T(8,128)(2,1)S(1)}, u32[]{:S(2)}, u32[]{:S(2)}) %collective-permute-start.23) | collective-permute-done | bytes 262176 | tf_op jit(solution)/shard_map/ppermute | solution.py:567
  260.6 2.2 collective-permute-done.24.r2
  262.9 12.4 %collective-permute-done.25.r3 = bf16[256,512]{1,0:T(8,128)(2,1)} collective-permute-done((bf16[256,512]{1,0:T(8,128)(2,1)}, bf16[256,512]{1,0:T(8,128)(2,1)}, u32[]{:S(2)}, u32[]{:S(2)}) %collective-permute-start.25) | collective-permute-done | bytes 262176 | tf_op jit(solution)/shard_map/ppermute | solution.py:567
  275.2 7.9 %shard_map.94 = (bf16[256,1024]{1,0:T(8,128)(2,1)}, bf16[256,1024]{1,0:T(8,128)(2,1)}, bf16[256,1024]{1,0:T(8,128)(2,1)}, bf16[256,1024]{1,0:T(8,128)(2,1)}) custom-call(s32[10]{0:T(128)} %concatenate.43.place, f32[256,512]{1,0:T(8,128)} %dynamic-slice_bitcast_fusion.own, bf16[256,512]{1,0:T(8,128)(2,1)} %copy-done.18, ...), custom_call_target="tpu_custom_call" | custom-call | flops 2147483648 | bytes 11534336 | tf_op jit(solution)/shard_map/pallas_call | solution.py:548
  283.2 2.2 collective-permute-start.31
  285.9 10.7 %collective-permute-done.31 = bf16[256,1024]{1,0:T(8,128)(2,1)S(1)} collective-permute-done((bf16[256,1024]{1,0:T(8,128)(2,1)}, bf16[256,1024]{1,0:T(8,128)(2,1)S(1)}, u32[]{:S(2)}, u32[]{:S(2)}) %collective-permute-start.31) | collective-permute-done | bytes 524320 | tf_op jit(solution)/shard_map/ppermute | solution.py:567
  296.6 12.8 %collective-permute-done.30 = bf16[256,1024]{1,0:T(8,128)(2,1)S(1)} collective-permute-done((bf16[256,1024]{1,0:T(8,128)(2,1)}, bf16[256,1024]{1,0:T(8,128)(2,1)S(1)}, u32[]{:S(2)}, u32[]{:S(2)}) %collective-permute-start.30) | collective-permute-done | bytes 524320 | tf_op jit(solution)/shard_map/ppermute | solution.py:567
  309.4 2.2 add_convert_fusion
  (90 shorter events, 8.5 us)
Async XLA Ops:
  0.0 219.0 %copy-start = (f32[8,4]{0,1:T(4,128)S(1)}, f32[8,4]{0,1:T(4,128)}, u32[]{:S(2)}) copy-start(f32[8,4]{0,1:T(4,128)} %param.15) | copy-start | bytes 388
  0.0 7.9 %copy-start.13 = (bf16[512,1024]{1,0:T(8,128)(2,1)S(1)}, bf16[512,1024]{1,0:T(8,128)(2,1)}, u32[]{:S(2)}) copy-start(bf16[512,1024]{1,0:T(8,128)(2,1)} %param.13) | copy-start | bytes 3145732
  0.0 8.7 %copy-start.14 = (bf16[512,1024]{1,0:T(8,128)(2,1)S(1)}, bf16[512,1024]{1,0:T(8,128)(2,1)}, u32[]{:S(2)}) copy-start(bf16[512,1024]{1,0:T(8,128)(2,1)} %param.12) | copy-start | bytes 3145732
  2.8 6.8 %copy-start.15 = (bf16[512,1024]{1,0:T(8,128)(2,1)S(1)}, bf16[512,1024]{1,0:T(8,128)(2,1)}, u32[]{:S(2)}) copy-start(bf16[512,1024]{1,0:T(8,128)(2,1)} %param.11) | copy-start | bytes 3145732
  2.8 23.5 %collective-permute-start = (bf16[272,1024]{1,0:T(8,128)(2,1)}, bf16[272,1024]{1,0:T(8,128)(2,1)S(1)}, u32[]{:S(2)}, u32[]{:S(2)}) collective-permute-start(bf16[272,1024]{1,0:T(8,128)(2,1)} %pad_maximum_fusion.4), channel_id=1, source_target_pairs={{0,8},{4,12},{8,0},{12,4},{16,24},{20,28},{24,16},{28,20},{1,9},{5... | collective-permute-start | bytes 1671176 | tf_op jit(solution)/shard_map/ppermute | solution.py:567
  4.1 24.3 %collective-permute-start.1 = (bf16[272,1024]{1,0:T(8,128)(2,1)}, bf16[272,1024]{1,0:T(8,128)(2,1)S(1)}, u32[]{:S(2)}, u32[]{:S(2)}) collective-permute-start(bf16[272,1024]{1,0:T(8,128)(2,1)} %pad_maximum_fusion.4), channel_id=1, source_target_pairs={{0,16},{4,20},{8,24},{12,28},{16,0},{20,4},{24,8},{28,12},{1,17},{... | collective-permute-start | bytes 1671176 | tf_op jit(solution)/shard_map/ppermute | solution.py:567
  4.1 49.1 %collective-permute-start.2 = (bf16[272,1024]{1,0:T(8,128)(2,1)}, bf16[272,1024]{1,0:T(8,128)(2,1)S(1)}, u32[]{:S(2)}, u32[]{:S(2)}) collective-permute-start(bf16[272,1024]{1,0:T(8,128)(2,1)} %pad_maximum_fusion.4), channel_id=1, source_target_pairs={{0,24},{4,28},{8,16},{12,20},{16,8},{20,12},{24,0},{28,4},{1,25},{... | collective-permute-start | bytes 1671176 | tf_op jit(solution)/shard_map/ppermute | solution.py:567
  5.4 12.2 %collective-permute-start.3 = (bf16[256,1024]{1,0:T(8,128)(2,1)}, bf16[256,1024]{1,0:T(8,128)(2,1)}, u32[]{:S(2)}, u32[]{:S(2)}) collective-permute-start(bf16[256,1024]{1,0:T(8,128)(2,1)} %refs_0_.3), channel_id=1, source_target_pairs={{0,1},{1,0},{2,3},{3,2},{4,5},{5,4},{6,7},{7,6},{8,9},{9,8},{10,11... | collective-permute-start | bytes 1572872 | tf_op jit(solution)/shard_map/ppermute | solution.py:567
  6.6 11.9 %collective-permute-start.4 = (bf16[256,1024]{1,0:T(8,128)(2,1)}, bf16[256,1024]{1,0:T(8,128)(2,1)}, u32[]{:S(2)}, u32[]{:S(2)}) collective-permute-start(bf16[256,1024]{1,0:T(8,128)(2,1)} %refs_0_.3), channel_id=1, source_target_pairs={{0,2},{1,3},{2,0},{3,1},{4,6},{5,7},{6,4},{7,5},{8,10},{9,11},{10,... | collective-permute-start | bytes 1572872 | tf_op jit(solution)/shard_map/ppermute | solution.py:567
  26.3 28.2 %copy-start.5 = (bf16[272,1024]{1,0:T(8,128)(2,1)}, bf16[272,1024]{1,0:T(8,128)(2,1)S(1)}, u32[]{:S(2)}) copy-start(bf16[272,1024]{1,0:T(8,128)(2,1)S(1)} %collective-permute-done.refs_1_) | copy-start | bytes 1671172
  28.4 26.2 %copy-start.6 = (bf16[272,1024]{1,0:T(8,128)(2,1)}, bf16[272,1024]{1,0:T(8,128)(2,1)S(1)}, u32[]{:S(2)}) copy-start(bf16[272,1024]{1,0:T(8,128)(2,1)S(1)} %collective-permute-done.1.refs_2_) | copy-start | bytes 1671172
  53.3 1.3 copy-start.7
  57.6 100.6 %all-to-all-start = ((bf16[4,512,768]{2,1,0:T(8,128)(2,1)}), bf16[4,512,768]{2,1,0:T(8,128)(2,1)S(1)}, u32[]{:S(2)}, u32[]{:S(2)}) async-start(bf16[4,512,768]{2,1,0:T(8,128)(2,1)} %pad_maximum_fusion), calls=%async_computation | async-start | bytes 6291456 | tf_op jit(solution)/shard_map/all_to_all | solution.py:605
  61.3 73.2 %collective-permute-start.5 = (bf16[896,1024]{1,0:T(8,128)(2,1)}, bf16[896,1024]{1,0:T(8,128)(2,1)S(1)}, u32[]{:S(2)}, u32[]{:S(2)}) collective-permute-start(bf16[896,1024]{1,0:T(8,128)(2,1)} %get-tuple-element.58), channel_id=1, source_target_pairs={{0,1},{1,0},{2,3},{3,2},{4,5},{5,4},{6,7},{7,6},{8,9},{9,8},{10,11... | collective-permute-start | bytes 5505032 | tf_op jit(solution)/shard_map/ppermute | solution.py:567
  62.6 71.9 %collective-permute-start.6 = (bf16[896,1024]{1,0:T(8,128)(2,1)}, bf16[896,1024]{1,0:T(8,128)(2,1)S(1)}, u32[]{:S(2)}, u32[]{:S(2)}) collective-permute-start(bf16[896,1024]{1,0:T(8,128)(2,1)} %get-tuple-element.59), channel_id=1, source_target_pairs={{0,2},{1,3},{2,0},{3,1},{4,6},{5,7},{6,4},{7,5},{8,10},{9,11},{10,... | collective-permute-start | bytes 5505032 | tf_op jit(solution)/shard_map/ppermute | solution.py:567
  63.8 70.7 %collective-permute-start.7 = (bf16[1024,512]{1,0:T(8,128)(2,1)}, bf16[1024,512]{1,0:T(8,128)(2,1)}, u32[]{:S(2)}, u32[]{:S(2)}) collective-permute-start(bf16[1024,512]{1,0:T(8,128)(2,1)} %refs_0_.4), channel_id=1, source_target_pairs={{0,8},{4,12},{8,0},{12,4},{16,24},{20,28},{24,16},{28,20},{1,9},{5... | collective-permute-start | bytes 3145736 | tf_op jit(solution)/shard_map/ppermute | solution.py:567
  67.2 67.3 %copy-start.8 = (bf16[1024,512]{1,0:T(8,128)(2,1)S(1)}, bf16[1024,512]{1,0:T(8,128)(2,1)}, u32[]{:S(2)}) copy-start(bf16[1024,512]{1,0:T(8,128)(2,1)} %refs_0_.4) | copy-start | bytes 3145732
  134.5 19.3 %copy-start.2 = (bf16[896,1024]{1,0:T(8,128)(2,1)}, bf16[896,1024]{1,0:T(8,128)(2,1)S(1)}, u32[]{:S(2)}) copy-start(bf16[896,1024]{1,0:T(8,128)(2,1)S(1)} %collective-permute-done.5.refs_5_) | copy-start | bytes 5505028
  134.5 19.3 %copy-start.3 = (bf16[896,1024]{1,0:T(8,128)(2,1)}, bf16[896,1024]{1,0:T(8,128)(2,1)S(1)}, u32[]{:S(2)}) copy-start(bf16[896,1024]{1,0:T(8,128)(2,1)S(1)} %collective-permute-done.6.refs_7_) | copy-start | bytes 5505028
  134.5 23.7 %collective-permute-start.10 = (bf16[1024,512]{1,0:T(8,128)(2,1)S(1)}, bf16[1024,512]{1,0:T(8,128)(2,1)}, u32[]{:S(2)}, u32[]{:S(2)}) collective-permute-start(bf16[1024,512]{1,0:T(8,128)(2,1)S(1)} %copy-done.8), channel_id=1, source_target_pairs={{8,16},{12,20},{16,8},{20,12},{9,17},{13,21},{17,9},{21,13},{10,18... | collective-permute-start | bytes 3145736 | tf_op jit(solution)/shard_map/ppermute | solution.py:626
  136.5 16.2 %collective-permute-start.8 = (bf16[384,1024]{1,0:T(8,128)(2,1)S(1)}, bf16[384,1024]{1,0:T(8,128)(2,1)S(1)}, u32[]{:S(2)}, u32[]{:S(2)}) collective-permute-start(bf16[384,1024]{1,0:T(8,128)(2,1)S(1)} %slice.57), channel_id=1, source_target_pairs={{0,2},{1,3},{2,0},{3,1},{4,6},{5,7},{6,4},{7,5},{8,10},{9,11},{10,... | collective-permute-start | bytes 2359304 | tf_op jit(solution)/shard_map/ppermute | solution.py:567
  137.9 15.9 %collective-permute-start.9 = (bf16[384,1024]{1,0:T(8,128)(2,1)S(1)}, bf16[384,1024]{1,0:T(8,128)(2,1)S(1)}, u32[]{:S(2)}, u32[]{:S(2)}) collective-permute-start(bf16[384,1024]{1,0:T(8,128)(2,1)S(1)} %slice.58), channel_id=1, source_target_pairs={{0,1},{1,0},{2,3},{3,2},{4,5},{5,4},{6,7},{7,6},{8,9},{9,8},{10,11... | collective-permute-start | bytes 2359304 | tf_op jit(solution)/shard_map/ppermute | solution.py:567
  152.7 1.1 copy-start.16
  153.8 0.9 copy-start.17
  158.2 9.2 %copy-start.1 = (bf16[4,512,768]{2,1,0:T(8,128)(2,1)}, bf16[4,512,768]{2,1,0:T(8,128)(2,1)S(1)}, u32[]{:S(2)}) copy-start(bf16[4,512,768]{2,1,0:T(8,128)(2,1)S(1)} %all-to-all-done.refs_10_) | copy-start | bytes 9437188
  158.2 9.2 %collective-permute-start.11 = (bf16[4,512,768]{2,1,0:T(8,128)(2,1)S(1)}, bf16[4,512,768]{2,1,0:T(8,128)(2,1)S(1)}, u32[]{:S(2)}, u32[]{:S(2)}) collective-permute-start(bf16[4,512,768]{2,1,0:T(8,128)(2,1)S(1)} %all-to-all-done.refs_10_), channel_id=1, source_target_pairs={{0,4},{4,0},{8,12},{12,8},{16,20},{20,16},{24,28},{28,24},{1,5},{5... | collective-permute-start | bytes 9437192 | tf_op jit(solution)/shard_map/ppermute | solution.py:567
  167.4 1.7 copy-start.4
  177.3 16.7 %copy-start.9 = (bf16[1024,512]{1,0:T(8,128)(2,1)S(1)}, bf16[1024,512]{1,0:T(8,128)(2,1)}, u32[]{:S(2)}) copy-start(bf16[1024,512]{1,0:T(8,128)(2,1)} %refs_0_.4) | copy-start | bytes 3145732
  177.3 16.1 %collective-permute-start.12 = (bf16[4,256,256]{2,1,0:T(8,128)(2,1)}, bf16[4,256,256]{2,1,0:T(8,128)(2,1)S(1)}, u32[]{:S(2)}, u32[]{:S(2)}) collective-permute-start(bf16[4,256,256]{2,1,0:T(8,128)(2,1)} %shard_map.91.refs_2_), channel_id=1, source_target_pairs={{0,8},{4,12},{8,0},{12,4},{16,24},{20,28},{24,16},{28,20},{1,9},{5... | collective-permute-start | bytes 1572872 | tf_op jit(solution)/shard_map/ppermute | solution.py:567
  177.4 16.0 %collective-permute-start.13 = (bf16[4,256,256]{2,1,0:T(8,128)(2,1)}, bf16[4,256,256]{2,1,0:T(8,128)(2,1)S(1)}, u32[]{:S(2)}, u32[]{:S(2)}) collective-permute-start(bf16[4,256,256]{2,1,0:T(8,128)(2,1)} %shard_map.91.refs_2_), channel_id=1, source_target_pairs={{0,4},{4,0},{8,12},{12,8},{16,20},{20,16},{24,28},{28,24},{1,5},{5... | collective-permute-start | bytes 1572872 | tf_op jit(solution)/shard_map/ppermute | solution.py:567
  177.8 26.7 %collective-permute-start.16 = (bf16[1024,512]{1,0:T(8,128)(2,1)}, bf16[1024,512]{1,0:T(8,128)(2,1)}, u32[]{:S(2)}, u32[]{:S(2)}) collective-permute-start(bf16[1024,512]{1,0:T(8,128)(2,1)} %collective-permute-done.7.refs_2_), channel_id=1, source_target_pairs={{8,16},{12,20},{16,8},{20,12},{9,17},{13,21},{17,9},{21,13},{10,18... | collective-permute-start | bytes 3145736 | tf_op jit(solution)/shard_map/ppermute | solution.py:634
  179.7 31.7 %collective-permute-start.17 = (bf16[1024,512]{1,0:T(8,128)(2,1)}, bf16[1024,512]{1,0:T(8,128)(2,1)}, u32[]{:S(2)}, u32[]{:S(2)}) collective-permute-start(bf16[1024,512]{1,0:T(8,128)(2,1)} %collective-permute-done.10.refs_4_), channel_id=1, source_target_pairs={{8,0},{12,4},{16,24},{20,28},{9,1},{13,5},{17,25},{21,29},{10,2},{... | collective-permute-start | bytes 3145736 | tf_op jit(solution)/shard_map/ppermute | solution.py:635
  193.4 0.9 copy-start.20
  193.4 18.9 %copy-start.21 = (bf16[4,256,256]{2,1,0:T(8,128)(2,1)}, bf16[4,256,256]{2,1,0:T(8,128)(2,1)S(1)}, u32[]{:S(2)}) copy-start(bf16[4,256,256]{2,1,0:T(8,128)(2,1)S(1)} %collective-permute-done.13.refs_4_) | copy-start | bytes 1572868
  193.4 18.9 %collective-permute-start.14 = (bf16[4,256,256]{2,1,0:T(8,128)(2,1)}, bf16[4,256,256]{2,1,0:T(8,128)(2,1)S(1)}, u32[]{:S(2)}, u32[]{:S(2)}) collective-permute-start(bf16[4,256,256]{2,1,0:T(8,128)(2,1)} %get-tuple-element.76), channel_id=1, source_target_pairs={{0,4},{4,0},{8,12},{12,8},{16,20},{20,16},{24,28},{28,24},{1,5},{5... | collective-permute-start | bytes 1572872 | tf_op jit(solution)/shard_map/ppermute | solution.py:567
  193.8 18.5 %collective-permute-start.15 = (bf16[4,256,256]{2,1,0:T(8,128)(2,1)S(1)}, bf16[4,256,256]{2,1,0:T(8,128)(2,1)S(1)}, u32[]{:S(2)}, u32[]{:S(2)}) collective-permute-start(bf16[4,256,256]{2,1,0:T(8,128)(2,1)S(1)} %collective-permute-done.12.refs_3_), channel_id=1, source_target_pairs={{0,4},{4,0},{8,12},{12,8},{16,20},{20,16},{24,28},{28,24},{1,5},{5... | collective-permute-start | bytes 1572872 | tf_op jit(solution)/shard_map/ppermute | solution.py:567
  194.0 42.3 %collective-permute-start.19 = (bf16[1024,512]{1,0:T(8,128)(2,1)S(1)}, bf16[1024,512]{1,0:T(8,128)(2,1)S(1)}, u32[]{:S(2)}, u32[]{:S(2)}) collective-permute-start(bf16[1024,512]{1,0:T(8,128)(2,1)S(1)} %copy-done.9), channel_id=1, source_target_pairs={{0,4},{4,0},{8,12},{12,8},{16,20},{20,16},{24,28},{28,24},{1,5},{5... | collective-permute-start | bytes 3145736 | tf_op jit(solution)/shard_map/ppermute | solution.py:567
  204.5 31.8 %collective-permute-start.20 = (bf16[1024,512]{1,0:T(8,128)(2,1)}, bf16[1024,512]{1,0:T(8,128)(2,1)S(1)}, u32[]{:S(2)}, u32[]{:S(2)}) collective-permute-start(bf16[1024,512]{1,0:T(8,128)(2,1)} %collective-permute-done.7.refs_2_), channel_id=1, source_target_pairs={{0,4},{4,0},{8,12},{12,8},{16,20},{20,16},{24,28},{28,24},{1,5},{5... | collective-permute-start | bytes 3145736 | tf_op jit(solution)/shard_map/ppermute | solution.py:567
  211.4 24.9 %collective-permute-start.21 = (bf16[1024,512]{1,0:T(8,128)(2,1)}, bf16[1024,512]{1,0:T(8,128)(2,1)}, u32[]{:S(2)}, u32[]{:S(2)}) collective-permute-start(bf16[1024,512]{1,0:T(8,128)(2,1)} %collective-permute-done.10.refs_4_), channel_id=1, source_target_pairs={{0,4},{4,0},{8,12},{12,8},{16,20},{20,16},{24,28},{28,24},{1,5},{5... | collective-permute-start | bytes 3145736 | tf_op jit(solution)/shard_map/ppermute | solution.py:567
  212.3 0.8 copy-start.22
  213.1 0.8 copy-start.23
  213.9 27.0 %collective-permute-start.18 = (bf16[1024,512]{1,0:T(8,128)(2,1)}, bf16[1024,512]{1,0:T(8,128)(2,1)}, u32[]{:S(2)}, u32[]{:S(2)}) collective-permute-start(bf16[1024,512]{1,0:T(8,128)(2,1)} %collective-permute-done.16.refs_8_), channel_id=1, source_target_pairs={{8,0},{12,4},{16,24},{20,28},{9,1},{13,5},{17,25},{21,29},{10,2},{... | collective-permute-start | bytes 3145736 | tf_op jit(solution)/shard_map/ppermute | solution.py:644
  236.3 5.9 %copy-start.10 = (bf16[1024,512]{1,0:T(8,128)(2,1)}, bf16[1024,512]{1,0:T(8,128)(2,1)S(1)}, u32[]{:S(2)}) copy-start(bf16[1024,512]{1,0:T(8,128)(2,1)S(1)} %collective-permute-done.19.refs_1_) | copy-start | bytes 3145732
  236.3 5.9 %copy-start.11 = (bf16[1024,512]{1,0:T(8,128)(2,1)}, bf16[1024,512]{1,0:T(8,128)(2,1)S(1)}, u32[]{:S(2)}) copy-start(bf16[1024,512]{1,0:T(8,128)(2,1)S(1)} %collective-permute-done.20.refs_3_) | copy-start | bytes 3145732
  240.9 4.9 %collective-permute-start.22 = (bf16[4,256,512]{2,1,0:T(8,128)(2,1)}, bf16[4,256,512]{2,1,0:T(8,128)(2,1)}, u32[]{:S(2)}, u32[]{:S(2)}) collective-permute-start(bf16[4,256,512]{2,1,0:T(8,128)(2,1)} %get-tuple-element.87), channel_id=1, source_target_pairs={{0,4},{4,0},{8,12},{12,8},{16,20},{20,16},{24,28},{28,24},{1,5},{5... | collective-permute-start | bytes 3145736 | tf_op jit(solution)/shard_map/ppermute | solution.py:567
  241.7 9.1 %collective-permute-start.26 = (bf16[1024,512]{1,0:T(8,128)(2,1)}, bf16[1024,512]{1,0:T(8,128)(2,1)S(1)}, u32[]{:S(2)}, u32[]{:S(2)}) collective-permute-start(bf16[1024,512]{1,0:T(8,128)(2,1)} %collective-permute-done.17.refs_6_), channel_id=1, source_target_pairs={{0,4},{4,0},{8,12},{12,8},{16,20},{20,16},{24,28},{28,24},{1,5},{5... | collective-permute-start | bytes 3145736 | tf_op jit(solution)/shard_map/ppermute | solution.py:567
  241.7 11.7 %collective-permute-start.27 = (bf16[1024,512]{1,0:T(8,128)(2,1)}, bf16[1024,512]{1,0:T(8,128)(2,1)}, u32[]{:S(2)}, u32[]{:S(2)}) collective-permute-start(bf16[1024,512]{1,0:T(8,128)(2,1)} %collective-permute-done.16.refs_8_), channel_id=1, source_target_pairs={{0,4},{4,0},{8,12},{12,8},{16,20},{20,16},{24,28},{28,24},{1,5},{5... | collective-permute-start | bytes 3145736 | tf_op jit(solution)/shard_map/ppermute | solution.py:567
  242.2 11.2 %collective-permute-start.28 = (bf16[1024,512]{1,0:T(8,128)(2,1)}, bf16[1024,512]{1,0:T(8,128)(2,1)}, u32[]{:S(2)}, u32[]{:S(2)}) collective-permute-start(bf16[1024,512]{1,0:T(8,128)(2,1)} %collective-permute-done.18.refs_10_), channel_id=1, source_target_pairs={{0,4},{4,0},{8,12},{12,8},{16,20},{20,16},{24,28},{28,24},{1,5},{5... | collective-permute-start | bytes 3145736 | tf_op jit(solution)/shard_map/ppermute | solution.py:567
  242.2 9.8 %copy-start.19 = (s32[9]{0:T(128)S(1)}, s32[9]{0:T(128)}, u32[]{:S(2)}) copy-start(s32[9]{0:T(128)} %stack.92.place) | copy-start | bytes 112
  248.6 12.1 %collective-permute-start.23 = (bf16[256,512]{1,0:T(8,128)(2,1)}, bf16[256,512]{1,0:T(8,128)(2,1)S(1)}, u32[]{:S(2)}, u32[]{:S(2)}) collective-permute-start(bf16[256,512]{1,0:T(8,128)(2,1)} %get-tuple-element.99), channel_id=1, source_target_pairs={{0,8},{4,12},{8,0},{12,4},{16,24},{20,28},{24,16},{28,20},{1,9},{5... | collective-permute-start | bytes 786440 | tf_op jit(solution)/shard_map/ppermute | solution.py:567
  250.8 12.1 %collective-permute-start.24 = (bf16[256,512]{1,0:T(8,128)(2,1)}, bf16[256,512]{1,0:T(8,128)(2,1)}, u32[]{:S(2)}, u32[]{:S(2)}) collective-permute-start(bf16[256,512]{1,0:T(8,128)(2,1)} %get-tuple-element.98), channel_id=1, source_target_pairs={{0,16},{4,20},{8,24},{12,28},{16,0},{20,4},{24,8},{28,12},{1,17},{... | collective-permute-start | bytes 786440 | tf_op jit(solution)/shard_map/ppermute | solution.py:567
  250.8 24.5 %copy-start.12 = (bf16[1024,512]{1,0:T(8,128)(2,1)}, bf16[1024,512]{1,0:T(8,128)(2,1)S(1)}, u32[]{:S(2)}) copy-start(bf16[1024,512]{1,0:T(8,128)(2,1)S(1)} %collective-permute-done.26.refs_7_) | copy-start | bytes 3145732
  250.8 24.4 %collective-permute-start.25 = (bf16[256,512]{1,0:T(8,128)(2,1)}, bf16[256,512]{1,0:T(8,128)(2,1)}, u32[]{:S(2)}, u32[]{:S(2)}) collective-permute-start(bf16[256,512]{1,0:T(8,128)(2,1)} %get-tuple-element.97), channel_id=1, source_target_pairs={{0,24},{4,28},{8,16},{12,20},{16,8},{20,12},{24,0},{28,4},{1,25},{... | collective-permute-start | bytes 786440 | tf_op jit(solution)/shard_map/ppermute | solution.py:567
  260.6 14.6 %copy-start.18 = (bf16[256,512]{1,0:T(8,128)(2,1)}, bf16[256,512]{1,0:T(8,128)(2,1)S(1)}, u32[]{:S(2)}) copy-start(bf16[256,512]{1,0:T(8,128)(2,1)S(1)} %collective-permute-done.23.r1) | copy-start | bytes 786436
  283.2 13.4 %collective-permute-start.31 = (bf16[256,1024]{1,0:T(8,128)(2,1)}, bf16[256,1024]{1,0:T(8,128)(2,1)S(1)}, u32[]{:S(2)}, u32[]{:S(2)}) collective-permute-start(bf16[256,1024]{1,0:T(8,128)(2,1)} %get-tuple-element.96), channel_id=1, source_target_pairs={{0,3},{1,2},{2,1},{3,0},{4,7},{5,6},{6,5},{7,4},{8,11},{9,10},{10,... | collective-permute-start | bytes 1572872 | tf_op jit(solution)/shard_map/ppermute | solution.py:567
  285.4 24.0 %collective-permute-start.30 = (bf16[256,1024]{1,0:T(8,128)(2,1)}, bf16[256,1024]{1,0:T(8,128)(2,1)S(1)}, u32[]{:S(2)}, u32[]{:S(2)}) collective-permute-start(bf16[256,1024]{1,0:T(8,128)(2,1)} %get-tuple-element.95), channel_id=1, source_target_pairs={{0,2},{1,3},{2,0},{3,1},{4,6},{5,7},{6,4},{7,5},{8,10},{9,11},{10,... | collective-permute-start | bytes 1572872 | tf_op jit(solution)/shard_map/ppermute | solution.py:567
  285.6 23.8 %collective-permute-start.29 = (bf16[256,1024]{1,0:T(8,128)(2,1)}, bf16[256,1024]{1,0:T(8,128)(2,1)S(1)}, u32[]{:S(2)}, u32[]{:S(2)}) collective-permute-start(bf16[256,1024]{1,0:T(8,128)(2,1)} %get-tuple-element.94), channel_id=1, source_target_pairs={{0,1},{1,0},{2,3},{3,2},{4,5},{5,4},{6,7},{7,6},{8,9},{9,8},{10,11... | collective-permute-start | bytes 1572872 | tf_op jit(solution)/shard_map/ppermute | solution.py:567

commit v11 on v9

--- a/solution.py
+++ b/solution.py
@@ -498,31 +498,18 @@
     )(place, mix, weights, mine, other, *values)
 
 
-def finish_kernel(place, own, r1, r2, r3, gain, *refs):
-    w_parts, outs = refs[:12], refs[12:16]
-    normed, w_buf, sem = refs[16:]
-    width = w_parts[0].shape[1]
-    core, head, inner = place[1], place[0], place[9]
-
-    def copy_w(n, source):
-        side = core if n % 2 == 0 else 1 - core
-        cols = pl.ds(pl.multiple_of(side * width, width), width)
-        target = w_buf.at[lax.bitwise_xor(place[5 + n // 2], head), :, cols]
-        return pltpu.make_async_copy(w_parts[source], target, sem.at[n])
-
-    for n in range(4):
-        copy_w(n, n).start()
-    for n in range(4, 8):
-        straight = n if n < 6 else n + 2
-
-        @pl.when(inner == 1)
-        def _():
-            copy_w(n, straight).start()
-
-        @pl.when(inner == 0)
-        def _():
-            copy_w(n, straight + 2).start()
-
+def finish_kernel(place, own, r1, r2, r3, gain, w_any, o0, o1, o2, o3, normed, w_buf, sem):
+    blocks, _, width = w_buf.shape
+    per = blocks // 4
+    order = [(t, i) for t in (3, 2, 1, 0) for i in range(per)]
+
+    def copy_w(n):
+        t, i = order[n]
+        source = per * lax.bitwise_xor(place[0], t) + i
+        return pltpu.make_async_copy(w_any.at[source], w_buf.at[n], sem.at[n])
+
+    for n in range(blocks):
+        copy_w(n).start()
     near = own[...] + r1[...].astype(jnp.float32)
     far = r2[...].astype(jnp.float32) + r3[...].astype(jnp.float32)
     low = place[3] == 0
@@ -534,32 +521,32 @@
         normed[:, g * HD : (g + 1) * HD] = (
             x * scale * gain[:, g * HD : (g + 1) * HD]
         ).astype(jnp.bfloat16)
-    for n in range(8):
-        copy_w(n, n).wait()
-    for t in (3, 2, 1, 0):
-        outs[t][...] = jnp.dot(
-            normed[...], w_buf[t], preferred_element_type=jnp.float32
+    for n in range(blocks):
+        t, i = order[n]
+        copy_w(n).wait()
+        (o0, o1, o2, o3)[t][:, i * width : (i + 1) * width] = jnp.dot(
+            normed[...], w_buf[n], preferred_element_type=jnp.float32
         ).astype(jnp.bfloat16)
 
 
-def finish(place, own, r1, r2, r3, gain, w_parts):
+def finish(place, own, r1, r2, r3, gain, w_all):
     rows = own.shape[0]
-    depth, width = w_parts[0].shape
+    blocks, depth, width = w_all.shape
     return pl.pallas_call(
         finish_kernel,
-        in_specs=[whole(pltpu.SMEM)] + [whole(pltpu.VMEM)] * 5 + [whole(pl.ANY)] * 12,
+        in_specs=[whole(pltpu.SMEM)] + [whole(pltpu.VMEM)] * 5 + [whole(pl.ANY)],
         out_specs=[whole(pltpu.VMEM)] * 4,
-        out_shape=[jax.ShapeDtypeStruct((rows, 2 * width), jnp.bfloat16)] * 4,
+        out_shape=[jax.ShapeDtypeStruct((rows, blocks // 4 * width), jnp.bfloat16)] * 4,
         scratch_shapes=[
             pltpu.VMEM((rows, depth), jnp.bfloat16),
-            pltpu.VMEM((4, depth, 2 * width), jnp.bfloat16),
-            pltpu.SemaphoreType.DMA((8,)),
+            pltpu.VMEM((blocks, depth, width), jnp.bfloat16),
+            pltpu.SemaphoreType.DMA((blocks,)),
         ],
         compiler_params=kernel_params(56),
         cost_estimate=pl.CostEstimate(
-            flops=2 * rows * depth * 8 * width, bytes_accessed=11 * 2**20, transcendentals=0
+            flops=2 * rows * depth * blocks * width, bytes_accessed=11 * 2**20, transcendentals=0
         ),
-    )(place, own, r1, r2, r3, gain, *w_parts)
+    )(place, own, r1, r2, r3, gain, w_all)
 
 
 def swapped(value, axis, mask):
@@ -618,40 +605,23 @@
     x_rest, y_rest, cosine, sine, w_out = barrier((x_rest, y_rest, cosine, sine, w_out))
     c_low = swapped(x_rest[: 3 * half], "head", 2)
     c_high = swapped(y_rest[3 * half : 3 * rows], "head", 1)
-    middle = [(2, 4), (3, 5), (4, 2), (5, 3)]
-    outward = [(2, 0), (3, 1), (4, 6), (5, 7)]
-    out_near = swapped(w_out, "ctx", 2)
-    out_across = lax.ppermute(w_out, "ctx", middle)
-    c_low, c_high, w_same = barrier((c_low, c_high, w_same))
+    c_low, c_high, w_same, w_out = barrier((c_low, c_high, w_same, w_out))
+    w_all = lax.all_gather(w_out, "ctx", axis=0)
     w_swap = swapped(w_same, "ctx", 1)
     sources = place, [activations] + list(far), (x0, x_rest, y0, y_rest, c_low, c_high), w_same, w_swap
     (v_pair,) = project(*sources)
-    place, v_pair, out_near, out_across = barrier((place, v_pair, out_near, out_across))
+    place, v_pair = barrier((place, v_pair))
     v_next = swapped(v_pair, "ctx", 2)
     v_pair_other = swapped(v_pair, "ctx", 1)
-    out_across_next = lax.ppermute(out_near, "ctx", middle)
-    out_passed = lax.ppermute(out_across, "ctx", outward)
     mine, theirs = project(place, *sources[1:], (cosine, sine))
     mine, theirs, v_next, v_pair_other = barrier((mine, theirs, v_next, v_pair_other))
     other = swapped(theirs, "ctx", 1)
     v_next_other = swapped(v_next, "ctx", 1)
-    out_own_swap = swapped(w_out, "ctx", 1)
-    other, v_next_other, out_across_next, out_own_swap = barrier(
-        (other, v_next_other, out_across_next, out_own_swap)
-    )
-    out_passed_next = lax.ppermute(out_across_next, "ctx", outward)
-    out_near_swap, out_across_swap = swapped(out_near, "ctx", 1), swapped(out_across, "ctx", 1)
     group_rows = lax.dynamic_slice_in_dim(head_mix, GROUP * (ctx // GROUP), GROUP, 0)
     mix = lax.dynamic_index_in_dim(group_rows, ctx % GROUP, 1, keepdims=False)
     out_mine, out_theirs = attend_head(
         place, mix, weights, mine, other, (v_pair, v_next, v_pair_other, v_next_other)
     )
-    out_mine, out_theirs, out_passed, out_passed_next, out_near_swap, out_across_swap = barrier(
-        (out_mine, out_theirs, out_passed, out_passed_next, out_near_swap, out_across_swap)
-    )
-    out_parts = [w_out, out_own_swap, out_near, out_near_swap, out_across, out_across_swap]
-    for part in (out_passed, out_across_next, out_passed_next):
-        out_parts += [part, swapped(part, "ctx", 1)]
     summed = out_mine.astype(jnp.float32) + swapped(out_theirs, "ctx", 1).astype(jnp.float32)
     own = lax.dynamic_index_in_dim(summed, z, 0, keepdims=False)
     r1, r2, r3 = [
@@ -662,12 +632,7 @@
         )
         for s in (1, 2, 3)
     ]
-    inner = (z == 1) | (z == 2)
-    out_places = jnp.stack(
-        [z, z ^ 1, jnp.where(inner, z ^ 3, z ^ 2), jnp.where(inner, z ^ 2, z ^ 3), inner]
-    )
-    where = jnp.concatenate([place[:5], out_places.astype(jnp.int32)])
-    shares = finish(where, own, r1, r2, r3, out_gain.reshape(1, -1), out_parts)
+    shares = finish(place, own, r1, r2, r3, out_gain.reshape(1, -1), w_all)
     total = shares[0].astype(jnp.float32)
     for t in (1, 2, 3):
         total = total + swapped(shares[t], "head", t).astype(jnp.float32)

time: 294 us -> 303 us (1.031)
  starting transfers between devices: 39.9 us -> 25.8 us
  between operations: 0.36 us -> 13.6 us
  waiting for transfers between devices: 177 us -> 189 us
    ppermute x28 -> x21, waiting for transfers between devices: 143 us -> 180 us  [swapped(): return lax.ppermute(value, axis, [(i, i ^ mask) for i in range(count)])]
    ppermute x4 -> x0, waiting for transfers between devices: 24.1 us -> none  [the longest x1 11.8 us: per_device_one_head(): out_passed_next = lax.ppermute(out_across_next, 'ctx', outward)]
    ppermute x4 -> x0, starting transfers between devices: 11.4 us -> none  [the longest x1 3.13 us: per_device_one_head(): out_across = lax.ppermute(w_out, 'ctx', middle)]
    ppermute x28 -> x21, starting transfers between devices: 24.8 us -> 22.1 us  [swapped(): return lax.ppermute(value, axis, [(i, i ^ mask) for i in range(count)])]
  transfers between devices with their start and end apart: 33 -> 23, of which waited for: 20 -> 19; matrix products, arithmetic and copies ran while one was open for 6% -> 6% of each run, Pallas kernels for 12% -> 12%
where the time goes in v11:
time: 303 us; the launch traced here: 302 us
  waiting for transfers between devices  189 us (62%)
  Pallas kernels  41.8 us (14%)
  starting transfers between devices  25.8 us (9%)
  other arithmetic  19.4 us (6%)
  between operations  13.6 us (4%)
  local copies, waits for them, and re-layouts  12 us (4%)
    ppermute x21, waiting for transfers between devices, swapped(): return lax.ppermute(value, axis, [(i, i ^ mask) for i in range(count)])  180 us
    ppermute x21, starting transfers between devices, swapped(): return lax.ppermute(value, axis, [(i, i ^ mask) for i in range(count)])  22.1 us
    pallas_call x2, Pallas kernels, project(): pl.pallas_call(functools.partial(project_kernel, rows, first_col), out_sh...  18.1 us
    pallas_call x1, Pallas kernels, attend_head(): pl.pallas_call(attend_kernel, grid=(count,), out_shape=(out, out), in_spe...  16.7 us
    all_to_all x1, waiting for transfers between devices, per_device_one_head(): w_same = lax.all_to_all(w_pieces, 'ctx', 0, 0, axis_index_groups=same_core)  9.65 us
    pallas_call x1, Pallas kernels, finish(): pl.pallas_call(finish_kernel, in_specs=[whole(pltpu.SMEM)] + [whole(pltpu...  7.01 us
  transfers between devices with their start and end apart: 23, of which 19 were waited for; matrix products, arithmetic and copies ran while one was open for 6% of the time, Pallas kernels for 12%

profile of v11, /device:TPU:17, one launch (start us, length us, event | category | flops | bytes accessed | tf_op | source)
XLA Modules:
  0.0 301.8 jit_solution(4066791114146294111)
XLA Ops:
  6.5 0.8 fusion.11
  7.4 1.9 pad_maximum_fusion.4
  9.3 1.3 collective-permute-start
  10.6 1.3 collective-permute-start.2
  11.9 1.2 collective-permute-start.3
  13.2 1.2 collective-permute-start.4
  14.4 0.8 fusion.16
  15.2 0.9 fusion.15
  16.0 0.9 fusion.14
  17.1 0.7 stack.78.place
  17.7 1.2 fusion.13.weights
  18.9 1.4 maximum_bitcast_fusion
  20.3 1.9 pad_maximum_fusion
  22.2 2.0 collective-permute-done.3.refs_4_
  24.2 0.9 collective-permute-done.4.refs_6_
  25.1 7.7 %collective-permute-done.refs_1_ = bf16[272,1024]{1,0:T(8,128)(2,1)S(1)} collective-permute-done((bf16[272,1024]{1,0:T(8,128)(2,1)}, bf16[272,1024]{1,0:T(8,128)(2,1)S(1)}, u32[]{:S(2)}, u32[]{:S(2)}) %collective-permute-start) | collective-permute-done | bytes 557088 | tf_op jit(solution)/shard_map/ppermute | solution.py:554
  32.8 2.0 collective-permute-done.1.refs_2_
  34.9 24.9 %collective-permute-done.2.refs_3_ = bf16[272,1024]{1,0:T(8,128)(2,1)S(1)} collective-permute-done((bf16[272,1024]{1,0:T(8,128)(2,1)}, bf16[272,1024]{1,0:T(8,128)(2,1)S(1)}, u32[]{:S(2)}, u32[]{:S(2)}) %collective-permute-start.2) | collective-permute-done | bytes 557088 | tf_op jit(solution)/shard_map/ppermute | solution.py:554
  59.8 1.1 slice.47
  61.1 1.0 slice.46
  62.0 2.1 pad_maximum_fusion.3
  64.1 3.7 %all-to-all-start = ((bf16[4,512,768]{2,1,0:T(8,128)(2,1)}), bf16[4,512,768]{2,1,0:T(8,128)(2,1)S(1)}, u32[]{:S(2)}, u32[]{:S(2)}) async-start(bf16[4,512,768]{2,1,0:T(8,128)(2,1)} %pad_maximum_fusion), calls=%async_computation | async-start | bytes 6291456 | tf_op jit(solution)/shard_map/all_to_all | solution.py:592
  67.9 1.3 collective-permute-start.5
  69.1 1.2 collective-permute-start.6
  70.4 0.8 convert_add_fusion.1
  71.2 0.8 convert_add_fusion.2
  71.9 0.8 convert_add_fusion.3
  72.7 1.9 fusion.3
  74.6 1.0 pad_maximum_fusion.5.refs_12_
  75.6 1.0 pad_maximum_fusion.6.refs_13_
  76.6 30.8 %collective-permute-done.5.refs_5_ = bf16[896,1024]{1,0:T(8,128)(2,1)S(1)} collective-permute-done((bf16[896,1024]{1,0:T(8,128)(2,1)}, bf16[896,1024]{1,0:T(8,128)(2,1)S(1)}, u32[]{:S(2)}, u32[]{:S(2)}) %collective-permute-start.5) | collective-permute-done | bytes 1835040 | tf_op jit(solution)/shard_map/ppermute | solution.py:554
  107.4 0.9 collective-permute-done.6.refs_7_
  108.4 1.3 collective-permute-start.7
  110.1 14.3 %collective-permute-done.7.refs_8_ = bf16[384,1024]{1,0:T(8,128)(2,1)S(1)} collective-permute-done((bf16[384,1024]{1,0:T(8,128)(2,1)S(1)}, bf16[384,1024]{1,0:T(8,128)(2,1)S(1)}, u32[]{:S(2)}, u32[]{:S(2)}) %collective-permute-start.7) | collective-permute-done | bytes 786464 | tf_op jit(solution)/shard_map/ppermute | solution.py:554
  124.5 0.9 copy-done.11
  125.4 9.6 %all-to-all-done.refs_10_ = bf16[4,512,768]{2,1,0:T(8,128)(2,1)S(1)} async-done(((bf16[4,512,768]{2,1,0:T(8,128)(2,1)}), bf16[4,512,768]{2,1,0:T(8,128)(2,1)S(1)}, u32[]{:S(2)}, u32[]{:S(2)}) %all-to-all-start) | async-done | bytes 3145760 | tf_op jit(solution)/shard_map/all_to_all | solution.py:592
  135.1 1.5 collective-permute-start.9
  136.5 5.3 %collective-permute-done.9.refs_11_ = bf16[4,512,768]{2,1,0:T(8,128)(2,1)S(1)} collective-permute-done((bf16[4,512,768]{2,1,0:T(8,128)(2,1)S(1)}, bf16[4,512,768]{2,1,0:T(8,128)(2,1)S(1)}, u32[]{:S(2)}, u32[]{:S(2)}) %collective-permute-start.9) | collective-permute-done | bytes 3145760 | tf_op jit(solution)/shard_map/ppermute | solution.py:554
  141.8 1.7 copy-done.4
  143.5 8.5 %shard_map.91.refs_2_ = bf16[4,256,256]{2,1,0:T(8,128)(2,1)} custom-call(s32[9]{0:T(128)} %stack.78.place, bf16[256,1024]{1,0:T(8,128)(2,1)} %refs_0_.3, bf16[272,1024]{1,0:T(8,128)(2,1)} %copy-done.5, bf16[272,1024]{1,0:T(8,128)(2,1)} %copy-done.6, bf16[272,1024]{1,0:T(8,128)(2,1)} %copy-done.7, bf16[256,1024]{1,0:T(8,128)(2,1)} %collective-permute-done.3.refs_4_, ...), custom_call_target="tpu_custom_call" | custom-call | flops 2147483648 | bytes 16777216 | tf_op jit(solution)/shard_map/pallas_call | solution.py:261
  152.0 2.2 collective-permute-start.10
  154.2 0.7 collective-permute-start.11
  154.8 9.6 %shard_map.92 = (bf16[4,256,256]{2,1,0:T(8,128)(2,1)}, bf16[4,256,256]{2,1,0:T(8,128)(2,1)}) custom-call(s32[9]{0:T(128)} %stack.78.place, bf16[256,1024]{1,0:T(8,128)(2,1)} %refs_0_.3, bf16[272,1024]{1,0:T(8,128)(2,1)} %copy-done.5, bf16[272,1024]{1,0:T(8,128)(2,1)} %copy-done.6, bf16[272,1024]{1,0:T(8,128)(2,1)} %copy-done.7, ...), custom_call_target="tpu_custom_call" | custom-call | flops 4294967296 | bytes 16777216 | tf_op jit(solution)/shard_map/pallas_call | solution.py:261
  164.4 40.8 %collective-permute-done.10.refs_3_ = bf16[4,256,256]{2,1,0:T(8,128)(2,1)S(1)} collective-permute-done((bf16[4,256,256]{2,1,0:T(8,128)(2,1)}, bf16[4,256,256]{2,1,0:T(8,128)(2,1)S(1)}, u32[]{:S(2)}, u32[]{:S(2)}) %collective-permute-start.10) | collective-permute-done | bytes 524320 | tf_op jit(solution)/shard_map/ppermute | solution.py:554
  205.2 0.7 collective-permute-start.12
  206.5 1.1 collective-permute-done.12.refs_1_
  207.7 0.6 collective-permute-done.13.refs_5_
  208.4 0.8 copy-done.18
  209.2 16.7 %shard_map.93 = (bf16[4,256,512]{2,1,0:T(8,128)(2,1)}, bf16[4,256,512]{2,1,0:T(8,128)(2,1)}) custom-call(s32[9]{0:T(128)} %stack.78.place, f32[4]{0:T(128)} %dynamic-slice_bitcast_fusion.1.mix, f32[66]{0:T(128)} %fusion.13.weights, bf16[4,256,256]{2,1,0:T(8,128)(2,1)} %get-tuple-element.64.refs_0_, bf16[4,256,256]{2,1,0:T(8,128)(2,1)} %copy-done.17, ...), custom_call_target="tpu_custom_call" | custom-call | flops 5368709120 | bytes 16777216 | tf_op jit(solution)/shard_map/pallas_call | solution.py:471
  226.4 2.5 collective-permute-done.14
  228.9 1.6 convert_add_fusion
  230.5 0.8 fusion.2
  231.3 2.9 collective-permute-start.15
  234.5 0.9 collective-permute-start.17
  235.3 0.8 dynamic-slice_bitcast_fusion.own
  236.2 8.6 %collective-permute-done.15.r1 = bf16[256,512]{1,0:T(8,128)(2,1)S(1)} collective-permute-done((bf16[256,512]{1,0:T(8,128)(2,1)}, bf16[256,512]{1,0:T(8,128)(2,1)S(1)}, u32[]{:S(2)}, u32[]{:S(2)}) %collective-permute-start.15) | collective-permute-done | bytes 262176 | tf_op jit(solution)/shard_map/ppermute | solution.py:554
  244.7 2.0 collective-permute-done.16.r2
  246.7 11.6 %collective-permute-done.17.r3 = bf16[256,512]{1,0:T(8,128)(2,1)S(1)} collective-permute-done((bf16[256,512]{1,0:T(8,128)(2,1)S(1)}, bf16[256,512]{1,0:T(8,128)(2,1)S(1)}, u32[]{:S(2)}, u32[]{:S(2)}) %collective-permute-start.17) | collective-permute-done | bytes 262176 | tf_op jit(solution)/shard_map/ppermute | solution.py:554
  258.3 0.7 copy-done.14
  259.0 7.0 %shard_map.94 = (bf16[256,1024]{1,0:T(8,128)(2,1)}, bf16[256,1024]{1,0:T(8,128)(2,1)}, bf16[256,1024]{1,0:T(8,128)(2,1)}, bf16[256,1024]{1,0:T(8,128)(2,1)}) custom-call(s32[9]{0:T(128)} %stack.78.place, f32[256,512]{1,0:T(8,128)} %dynamic-slice_bitcast_fusion.own, bf16[256,512]{1,0:T(8,128)(2,1)} %copy-done.12, bf16[256,512]{1,0:T(8,128)(2,1)} %copy-done.13, ...), custom_call_target="tpu_custom_call" | custom-call | flops 2147483648 | bytes 11534336 | tf_op jit(solution)/shard_map/pallas_call | solution.py:535
  266.0 2.9 collective-permute-start.20
  269.3 10.9 %collective-permute-done.20 = bf16[256,1024]{1,0:T(8,128)(2,1)S(1)} collective-permute-done((bf16[256,1024]{1,0:T(8,128)(2,1)}, bf16[256,1024]{1,0:T(8,128)(2,1)S(1)}, u32[]{:S(2)}, u32[]{:S(2)}) %collective-permute-start.20) | collective-permute-done | bytes 524320 | tf_op jit(solution)/shard_map/ppermute | solution.py:554
  280.2 12.5 %collective-permute-done.19 = bf16[256,1024]{1,0:T(8,128)(2,1)S(1)} collective-permute-done((bf16[256,1024]{1,0:T(8,128)(2,1)}, bf16[256,1024]{1,0:T(8,128)(2,1)S(1)}, u32[]{:S(2)}, u32[]{:S(2)}) %collective-permute-start.19) | collective-permute-done | bytes 524320 | tf_op jit(solution)/shard_map/ppermute | solution.py:554
  292.8 2.2 add_convert_fusion
  (60 shorter events, 2.8 us)
Async XLA Ops:
  6.5 199.4 %copy-start = (f32[8,4]{0,1:T(4,128)S(1)}, f32[8,4]{0,1:T(4,128)}, u32[]{:S(2)}) copy-start(f32[8,4]{0,1:T(4,128)} %param.15) | copy-start | bytes 388
  6.5 7.9 %copy-start.8 = (bf16[512,1024]{1,0:T(8,128)(2,1)S(1)}, bf16[512,1024]{1,0:T(8,128)(2,1)}, u32[]{:S(2)}) copy-start(bf16[512,1024]{1,0:T(8,128)(2,1)} %param.13) | copy-start | bytes 3145732
  6.5 8.6 %copy-start.9 = (bf16[512,1024]{1,0:T(8,128)(2,1)S(1)}, bf16[512,1024]{1,0:T(8,128)(2,1)}, u32[]{:S(2)}) copy-start(bf16[512,1024]{1,0:T(8,128)(2,1)} %param.12) | copy-start | bytes 3145732
  9.3 6.8 %copy-start.10 = (bf16[512,1024]{1,0:T(8,128)(2,1)S(1)}, bf16[512,1024]{1,0:T(8,128)(2,1)}, u32[]{:S(2)}) copy-start(bf16[512,1024]{1,0:T(8,128)(2,1)} %param.11) | copy-start | bytes 3145732
  9.3 23.5 %collective-permute-start = (bf16[272,1024]{1,0:T(8,128)(2,1)}, bf16[272,1024]{1,0:T(8,128)(2,1)S(1)}, u32[]{:S(2)}, u32[]{:S(2)}) collective-permute-start(bf16[272,1024]{1,0:T(8,128)(2,1)} %pad_maximum_fusion.4), channel_id=1, source_target_pairs={{0,8},{4,12},{8,0},{12,4},{16,24},{20,28},{24,16},{28,20},{1,9},{5... | collective-permute-start | bytes 1671176 | tf_op jit(solution)/shard_map/ppermute | solution.py:554
  10.6 24.3 %collective-permute-start.1 = (bf16[272,1024]{1,0:T(8,128)(2,1)}, bf16[272,1024]{1,0:T(8,128)(2,1)S(1)}, u32[]{:S(2)}, u32[]{:S(2)}) collective-permute-start(bf16[272,1024]{1,0:T(8,128)(2,1)} %pad_maximum_fusion.4), channel_id=1, source_target_pairs={{0,16},{4,20},{8,24},{12,28},{16,0},{20,4},{24,8},{28,12},{1,17},{... | collective-permute-start | bytes 1671176 | tf_op jit(solution)/shard_map/ppermute | solution.py:554
  10.6 49.1 %collective-permute-start.2 = (bf16[272,1024]{1,0:T(8,128)(2,1)}, bf16[272,1024]{1,0:T(8,128)(2,1)S(1)}, u32[]{:S(2)}, u32[]{:S(2)}) collective-permute-start(bf16[272,1024]{1,0:T(8,128)(2,1)} %pad_maximum_fusion.4), channel_id=1, source_target_pairs={{0,24},{4,28},{8,16},{12,20},{16,8},{20,12},{24,0},{28,4},{1,25},{... | collective-permute-start | bytes 1671176 | tf_op jit(solution)/shard_map/ppermute | solution.py:554
  11.9 12.2 %collective-permute-start.3 = (bf16[256,1024]{1,0:T(8,128)(2,1)}, bf16[256,1024]{1,0:T(8,128)(2,1)}, u32[]{:S(2)}, u32[]{:S(2)}) collective-permute-start(bf16[256,1024]{1,0:T(8,128)(2,1)} %refs_0_.3), channel_id=1, source_target_pairs={{0,1},{1,0},{2,3},{3,2},{4,5},{5,4},{6,7},{7,6},{8,9},{9,8},{10,11... | collective-permute-start | bytes 1572872 | tf_op jit(solution)/shard_map/ppermute | solution.py:554
  13.2 11.9 %collective-permute-start.4 = (bf16[256,1024]{1,0:T(8,128)(2,1)}, bf16[256,1024]{1,0:T(8,128)(2,1)}, u32[]{:S(2)}, u32[]{:S(2)}) collective-permute-start(bf16[256,1024]{1,0:T(8,128)(2,1)} %refs_0_.3), channel_id=1, source_target_pairs={{0,2},{1,3},{2,0},{3,1},{4,6},{5,7},{6,4},{7,5},{8,10},{9,11},{10,... | collective-permute-start | bytes 1572872 | tf_op jit(solution)/shard_map/ppermute | solution.py:554
  32.8 28.2 %copy-start.5 = (bf16[272,1024]{1,0:T(8,128)(2,1)}, bf16[272,1024]{1,0:T(8,128)(2,1)S(1)}, u32[]{:S(2)}) copy-start(bf16[272,1024]{1,0:T(8,128)(2,1)S(1)} %collective-permute-done.refs_1_) | copy-start | bytes 1671172
  34.9 26.2 %copy-start.6 = (bf16[272,1024]{1,0:T(8,128)(2,1)}, bf16[272,1024]{1,0:T(8,128)(2,1)S(1)}, u32[]{:S(2)}) copy-start(bf16[272,1024]{1,0:T(8,128)(2,1)S(1)} %collective-permute-done.1.refs_2_) | copy-start | bytes 1671172
  59.8 1.3 copy-start.7
  64.1 70.9 %all-to-all-start = ((bf16[4,512,768]{2,1,0:T(8,128)(2,1)}), bf16[4,512,768]{2,1,0:T(8,128)(2,1)S(1)}, u32[]{:S(2)}, u32[]{:S(2)}) async-start(bf16[4,512,768]{2,1,0:T(8,128)(2,1)} %pad_maximum_fusion), calls=%async_computation | async-start | bytes 6291456 | tf_op jit(solution)/shard_map/all_to_all | solution.py:592
  67.8 190.5 %all-gather.3.cloned.1.call-start = ((), (), s32[]{:S(2)}) async-start(), calls=%async_computation.1 | async-start | bytes 9437184 | tf_op jit(solution)/shard_map/all_gather | solution.py:609
  67.9 39.6 %collective-permute-start.5 = (bf16[896,1024]{1,0:T(8,128)(2,1)}, bf16[896,1024]{1,0:T(8,128)(2,1)S(1)}, u32[]{:S(2)}, u32[]{:S(2)}) collective-permute-start(bf16[896,1024]{1,0:T(8,128)(2,1)} %get-tuple-element.47), channel_id=1, source_target_pairs={{0,1},{1,0},{2,3},{3,2},{4,5},{5,4},{6,7},{7,6},{8,9},{9,8},{10,11... | collective-permute-start | bytes 5505032 | tf_op jit(solution)/shard_map/ppermute | solution.py:554
  69.1 39.2 %collective-permute-start.6 = (bf16[896,1024]{1,0:T(8,128)(2,1)}, bf16[896,1024]{1,0:T(8,128)(2,1)S(1)}, u32[]{:S(2)}, u32[]{:S(2)}) collective-permute-start(bf16[896,1024]{1,0:T(8,128)(2,1)} %get-tuple-element.48), channel_id=1, source_target_pairs={{0,2},{1,3},{2,0},{3,1},{4,6},{5,7},{6,4},{7,5},{8,10},{9,11},{10,... | collective-permute-start | bytes 5505032 | tf_op jit(solution)/shard_map/ppermute | solution.py:554
  107.4 17.0 %copy-start.2 = (bf16[896,1024]{1,0:T(8,128)(2,1)}, bf16[896,1024]{1,0:T(8,128)(2,1)S(1)}, u32[]{:S(2)}) copy-start(bf16[896,1024]{1,0:T(8,128)(2,1)S(1)} %collective-permute-done.5.refs_5_) | copy-start | bytes 5505028
  108.4 16.1 %copy-start.3 = (bf16[896,1024]{1,0:T(8,128)(2,1)}, bf16[896,1024]{1,0:T(8,128)(2,1)S(1)}, u32[]{:S(2)}) copy-start(bf16[896,1024]{1,0:T(8,128)(2,1)S(1)} %collective-permute-done.6.refs_7_) | copy-start | bytes 5505028
  108.4 16.1 %collective-permute-start.7 = (bf16[384,1024]{1,0:T(8,128)(2,1)S(1)}, bf16[384,1024]{1,0:T(8,128)(2,1)S(1)}, u32[]{:S(2)}, u32[]{:S(2)}) collective-permute-start(bf16[384,1024]{1,0:T(8,128)(2,1)S(1)} %slice.54), channel_id=1, source_target_pairs={{0,2},{1,3},{2,0},{3,1},{4,6},{5,7},{6,4},{7,5},{8,10},{9,11},{10,... | collective-permute-start | bytes 2359304 | tf_op jit(solution)/shard_map/ppermute | solution.py:554
  109.8 15.6 %collective-permute-start.8 = (bf16[384,1024]{1,0:T(8,128)(2,1)S(1)}, bf16[384,1024]{1,0:T(8,128)(2,1)}, u32[]{:S(2)}, u32[]{:S(2)}) collective-permute-start(bf16[384,1024]{1,0:T(8,128)(2,1)S(1)} %slice.55), channel_id=1, source_target_pairs={{0,1},{1,0},{2,3},{3,2},{4,5},{5,4},{6,7},{7,6},{8,9},{9,8},{10,11... | collective-permute-start | bytes 2359304 | tf_op jit(solution)/shard_map/ppermute | solution.py:554
  124.5 0.9 copy-start.11
  135.0 6.8 %copy-start.1 = (bf16[4,512,768]{2,1,0:T(8,128)(2,1)}, bf16[4,512,768]{2,1,0:T(8,128)(2,1)S(1)}, u32[]{:S(2)}) copy-start(bf16[4,512,768]{2,1,0:T(8,128)(2,1)S(1)} %all-to-all-done.refs_10_) | copy-start | bytes 9437188
  135.1 6.8 %collective-permute-start.9 = (bf16[4,512,768]{2,1,0:T(8,128)(2,1)S(1)}, bf16[4,512,768]{2,1,0:T(8,128)(2,1)S(1)}, u32[]{:S(2)}, u32[]{:S(2)}) collective-permute-start(bf16[4,512,768]{2,1,0:T(8,128)(2,1)S(1)} %all-to-all-done.refs_10_), channel_id=1, source_target_pairs={{0,4},{4,0},{8,12},{12,8},{16,20},{20,16},{24,28},{28,24},{1,5},{5... | collective-permute-start | bytes 9437192 | tf_op jit(solution)/shard_map/ppermute | solution.py:554
  141.8 1.7 copy-start.4
  152.0 53.2 %collective-permute-start.10 = (bf16[4,256,256]{2,1,0:T(8,128)(2,1)}, bf16[4,256,256]{2,1,0:T(8,128)(2,1)S(1)}, u32[]{:S(2)}, u32[]{:S(2)}) collective-permute-start(bf16[4,256,256]{2,1,0:T(8,128)(2,1)} %shard_map.91.refs_2_), channel_id=1, source_target_pairs={{0,8},{4,12},{8,0},{12,4},{16,24},{20,28},{24,16},{28,20},{1,9},{5... | collective-permute-start | bytes 1572872 | tf_op jit(solution)/shard_map/ppermute | solution.py:554
  154.2 51.1 %collective-permute-start.11 = (bf16[4,256,256]{2,1,0:T(8,128)(2,1)}, bf16[4,256,256]{2,1,0:T(8,128)(2,1)S(1)}, u32[]{:S(2)}, u32[]{:S(2)}) collective-permute-start(bf16[4,256,256]{2,1,0:T(8,128)(2,1)} %shard_map.91.refs_2_), channel_id=1, source_target_pairs={{0,4},{4,0},{8,12},{12,8},{16,20},{20,16},{24,28},{28,24},{1,5},{5... | collective-permute-start | bytes 1572872 | tf_op jit(solution)/shard_map/ppermute | solution.py:554
  205.2 3.0 copy-start.15
  205.2 3.0 copy-start.16
  205.2 2.4 collective-permute-start.12
  205.9 2.3 collective-permute-start.13
  207.7 0.8 copy-start.17
  208.4 0.8 copy-start.18
  225.9 2.9 collective-permute-start.14
  231.3 13.5 %collective-permute-start.15 = (bf16[256,512]{1,0:T(8,128)(2,1)}, bf16[256,512]{1,0:T(8,128)(2,1)S(1)}, u32[]{:S(2)}, u32[]{:S(2)}) collective-permute-start(bf16[256,512]{1,0:T(8,128)(2,1)} %get-tuple-element.77), channel_id=1, source_target_pairs={{0,8},{4,12},{8,0},{12,4},{16,24},{20,28},{24,16},{28,20},{1,9},{5... | collective-permute-start | bytes 786440 | tf_op jit(solution)/shard_map/ppermute | solution.py:554
  234.2 12.5 %collective-permute-start.16 = (bf16[256,512]{1,0:T(8,128)(2,1)S(1)}, bf16[256,512]{1,0:T(8,128)(2,1)S(1)}, u32[]{:S(2)}, u32[]{:S(2)}) collective-permute-start(bf16[256,512]{1,0:T(8,128)(2,1)S(1)} %get-tuple-element.76), channel_id=1, source_target_pairs={{0,16},{4,20},{8,24},{12,28},{16,0},{20,4},{24,8},{28,12},{1,17},{... | collective-permute-start | bytes 786440 | tf_op jit(solution)/shard_map/ppermute | solution.py:554
  234.5 23.8 %collective-permute-start.17 = (bf16[256,512]{1,0:T(8,128)(2,1)S(1)}, bf16[256,512]{1,0:T(8,128)(2,1)S(1)}, u32[]{:S(2)}, u32[]{:S(2)}) collective-permute-start(bf16[256,512]{1,0:T(8,128)(2,1)S(1)} %get-tuple-element.75), channel_id=1, source_target_pairs={{0,24},{4,28},{8,16},{12,20},{16,8},{20,12},{24,0},{28,4},{1,25},{... | collective-permute-start | bytes 786440 | tf_op jit(solution)/shard_map/ppermute | solution.py:554
  244.7 13.6 %copy-start.12 = (bf16[256,512]{1,0:T(8,128)(2,1)}, bf16[256,512]{1,0:T(8,128)(2,1)S(1)}, u32[]{:S(2)}) copy-start(bf16[256,512]{1,0:T(8,128)(2,1)S(1)} %collective-permute-done.15.r1) | copy-start | bytes 786436
  246.7 11.6 %copy-start.13 = (bf16[256,512]{1,0:T(8,128)(2,1)}, bf16[256,512]{1,0:T(8,128)(2,1)S(1)}, u32[]{:S(2)}) copy-start(bf16[256,512]{1,0:T(8,128)(2,1)S(1)} %collective-permute-done.16.r2) | copy-start | bytes 786436
  258.3 0.7 copy-start.14
  266.0 14.2 %collective-permute-start.20 = (bf16[256,1024]{1,0:T(8,128)(2,1)}, bf16[256,1024]{1,0:T(8,128)(2,1)S(1)}, u32[]{:S(2)}, u32[]{:S(2)}) collective-permute-start(bf16[256,1024]{1,0:T(8,128)(2,1)} %get-tuple-element.74), channel_id=1, source_target_pairs={{0,3},{1,2},{2,1},{3,0},{4,7},{5,6},{6,5},{7,4},{8,11},{9,10},{10,... | collective-permute-start | bytes 1572872 | tf_op jit(solution)/shard_map/ppermute | solution.py:554
  268.9 23.8 %collective-permute-start.19 = (bf16[256,1024]{1,0:T(8,128)(2,1)}, bf16[256,1024]{1,0:T(8,128)(2,1)S(1)}, u32[]{:S(2)}, u32[]{:S(2)}) collective-permute-start(bf16[256,1024]{1,0:T(8,128)(2,1)} %get-tuple-element.73), channel_id=1, source_target_pairs={{0,2},{1,3},{2,0},{3,1},{4,6},{5,7},{6,4},{7,5},{8,10},{9,11},{10,... | collective-permute-start | bytes 1572872 | tf_op jit(solution)/shard_map/ppermute | solution.py:554
  269.2 23.6 %collective-permute-start.18 = (bf16[256,1024]{1,0:T(8,128)(2,1)}, bf16[256,1024]{1,0:T(8,128)(2,1)S(1)}, u32[]{:S(2)}, u32[]{:S(2)}) collective-permute-start(bf16[256,1024]{1,0:T(8,128)(2,1)} %get-tuple-element.72), channel_id=1, source_target_pairs={{0,1},{1,0},{2,3},{3,2},{4,5},{5,4},{6,7},{7,6},{8,9},{9,8},{10,11... | collective-permute-start | bytes 1572872 | tf_op jit(solution)/shard_map/ppermute | solution.py:554
Sparse Core Ops, SparseCore 0:
  135.2 94.4 all-gather.2

commit v12 on v9

--- a/solution.py
+++ b/solution.py
@@ -192,29 +192,29 @@
 
 
 def project_kernel(rows, first_col, place, *refs):
-    a_own, (x0, x_rest, y0, y_rest, c_low, c_high) = refs[:4], refs[4:10]
-    w_same, w_swap = refs[10:12]
+    a_own, a_x, a_y = refs[:4], refs[4:9], refs[9:14]
+    w_same, w_swap = refs[14:16]
     abuf, wbuf, acc, sem_a, sem_w = refs[-5:]
     turn, core = place[0], place[1]
     half = w_same.shape[1]
     width = wbuf.shape[2]
 
     def copies_a(t):
-        if t == 0:
-            pairs = [(a_own[b], 0, b * rows, rows) for b in range(4)]
-        elif t < 3:
-            first, others = ((x0, x_rest), (y0, y_rest))[t - 1]
-            pairs = [(first, 0, 0, rows), (others, 0, rows, 3 * rows)]
-        else:
-            late, mid = 3 * rows, rows // 2
-            pairs = [(y_rest, late, 0, mid), (x_rest, late, mid, mid)]
-            pairs += [(c_low, 0, rows, 3 * mid), (c_high, 0, rows + 3 * mid, 3 * mid)]
-        return [
-            pltpu.make_async_copy(
-                ref.at[pl.ds(source, size)], abuf.at[t, pl.ds(target, size)], sem_a.at[t, n]
-            )
-            for n, (ref, source, target, size) in enumerate(pairs)
-        ]
+        out = []
+        for b in range(4):
+            if t < 3:
+                source = (a_own, a_x, a_y)[t][b].at[pl.ds(0, rows)]
+                target = abuf.at[t, pl.ds(b * rows, rows)]
+                out.append(pltpu.make_async_copy(source, target, sem_a.at[t, b]))
+                continue
+            mid = rows // 2
+            late = pl.ds(rows if b < 3 else 0, mid)
+            for n, part in enumerate((a_y, a_x)):
+                target = abuf.at[t, pl.ds(b * rows + n * mid, mid)]
+                out.append(
+                    pltpu.make_async_copy(part[b + 1].at[late], target, sem_a.at[t + n, b])
+                )
+        return out
 
     def copies_w(t):
         out = []
@@ -233,11 +233,11 @@
         part = jnp.dot(abuf[t], wbuf[t], preferred_element_type=jnp.float32)
         acc[...] = part if t == 0 else acc[...] + part
     if first_col:
-        v_out = refs[12]
+        v_out = refs[16]
         for b in range(4):
             v_out[place[5 + b]] = acc[b * rows : (b + 1) * rows].astype(jnp.bfloat16)
         return
-    cos_ref, sin_ref, mine, theirs = refs[12:16]
+    cos_ref, sin_ref, mine, theirs = refs[16:20]
     first = core == 0
     for b in range(4):
         total = acc[b * rows : (b + 1) * rows]
@@ -262,14 +262,14 @@
         functools.partial(project_kernel, rows, first_col),
         out_shape=[out] * count,
         in_specs=[whole(pltpu.SMEM)]
-        + [whole(pl.ANY)] * 12
+        + [whole(pl.ANY)] * 16
         + [whole(pltpu.VMEM)] * len(angles),
         out_specs=[whole(pltpu.VMEM)] * count,
         scratch_shapes=[
             pltpu.VMEM((4, 4 * rows, depth), jnp.bfloat16),
             pltpu.VMEM((4, depth, width), jnp.bfloat16),
             pltpu.VMEM((4 * rows, width), jnp.float32),
-            pltpu.SemaphoreType.DMA((4, 4)),
+            pltpu.SemaphoreType.DMA((5, 4)),
             pltpu.SemaphoreType.DMA((4, 2)),
         ],
         compiler_params=kernel_params(56),
@@ -587,26 +587,41 @@
     digits = jnp.pad(digits, ((0, 14), (0, activations.shape[1] - rows)))
     block = jnp.concatenate([activations, digits])
     w_pieces = jnp.stack([columns(target) for target in range(4)])
-    far = [swapped(block, "ctx", 2 * s) for s in (1, 2, 3)]
+    middle = [(2, 4), (3, 5), (4, 2), (5, 3)]
+    outward = [(2, 0), (3, 1), (4, 6), (5, 7)]
+    inner = (z == 1) | (z == 2)
+
+    def plane(piece, x_before, y_before):
+        to_x = jnp.concatenate([piece[:rows], y_before[half:rows]])
+        to_y = jnp.concatenate([piece[:rows], x_before[:half]])
+        return swapped(to_x, "head", 1), swapped(to_y, "head", 2)
+
+    near = swapped(block, "ctx", 2)
+    across = lax.ppermute(block, "ctx", middle)
     x0, y0 = swapped(activations, "head", 1), swapped(activations, "head", 2)
     weights = lax.dynamic_index_in_dim(conv_kernel, ctx, 0, keepdims=False)
     weights = weights * (math.log2(math.e) / math.sqrt(HD))
-    place = jnp.stack([head, core, z % 2, z // 2, head, z, z ^ 1, z ^ 2, z ^ 3])
-    place = place.astype(jnp.int32)
-    far, x0, y0, w_pieces, weights, place, w_out = barrier(
-        (far, x0, y0, w_pieces, weights, place, w_out)
-    )
-
+    order = [z, z ^ 1, jnp.where(inner, z ^ 3, z ^ 2), jnp.where(inner, z ^ 2, z ^ 3)]
+    place = jnp.stack([head, core, z % 2, z // 2, head] + order).astype(jnp.int32)
+    near, across, x0, y0, w_pieces, weights, place, w_out = barrier(
+        (near, across, x0, y0, w_pieces, weights, place, w_out)
+    )
     same_core = [[i for i in range(8) if i % 2 == k] for k in range(2)]
-    inside = [a[:rows] for a in far]
-    to_x, to_y = jnp.concatenate(inside + [y0[half:]]), jnp.concatenate(inside + [x0[:half]])
-    to_x, to_y, w_pieces = barrier((to_x, to_y, w_pieces))
-    x_rest, y_rest = swapped(to_x, "head", 1), swapped(to_y, "head", 2)
     w_same = lax.all_to_all(w_pieces, "ctx", 0, 0, axis_index_groups=same_core)
+    across_next = lax.ppermute(near, "ctx", middle)
+    passed = lax.ppermute(across, "ctx", outward)
+    x1, y1 = plane(near, x0, y0)
+    across_next, passed, x1, y1 = barrier((across_next, passed, x1, y1))
+    far_a = across + passed
+    passed_next = lax.ppermute(across_next, "ctx", outward)
+    x2, y2 = plane(far_a, x1, y1)
+    passed_next, x2, y2 = barrier((passed_next, x2, y2))
+    far_b = across_next + passed_next
+    x3, y3 = plane(far_b, x2, y2)
     place_of = jnp.stack(
         [
             a[rows, :rows].astype(jnp.float32) * 256.0 + a[rows + 1, :rows].astype(jnp.float32)
-            for a in [block] + far
+            for a in (block, near, far_a, far_b)
         ]
     )
     exponents = jnp.arange(HD // 2, dtype=jnp.float32) * (2.0 / HD)
@@ -615,16 +630,14 @@
     cosine, sine = jnp.cos(angle), jnp.sin(angle)
     cosine = jnp.concatenate([cosine, cosine], -1)
     sine = jnp.concatenate([-sine, sine], -1)
-    x_rest, y_rest, cosine, sine, w_out = barrier((x_rest, y_rest, cosine, sine, w_out))
-    c_low = swapped(x_rest[: 3 * half], "head", 2)
-    c_high = swapped(y_rest[3 * half : 3 * rows], "head", 1)
-    middle = [(2, 4), (3, 5), (4, 2), (5, 3)]
-    outward = [(2, 0), (3, 1), (4, 6), (5, 7)]
+    x3, y3, cosine, sine, w_out = barrier((x3, y3, cosine, sine, w_out))
+    x4, y4 = swapped(y3[half:rows], "head", 1), swapped(x3[:half], "head", 2)
     out_near = swapped(w_out, "ctx", 2)
     out_across = lax.ppermute(w_out, "ctx", middle)
-    c_low, c_high, w_same = barrier((c_low, c_high, w_same))
+    x4, y4, w_same = barrier((x4, y4, w_same))
     w_swap = swapped(w_same, "ctx", 1)
-    sources = place, [activations] + list(far), (x0, x_rest, y0, y_rest, c_low, c_high), w_same, w_swap
+    planes = (x0, x1, x2, x3, x4, y0, y1, y2, y3, y4)
+    sources = place, (activations, near, far_a, far_b), planes, w_same, w_swap
     (v_pair,) = project(*sources)
     place, v_pair, out_near, out_across = barrier((place, v_pair, out_near, out_across))
     v_next = swapped(v_pair, "ctx", 2)
@@ -662,11 +675,7 @@
         )
         for s in (1, 2, 3)
     ]
-    inner = (z == 1) | (z == 2)
-    out_places = jnp.stack(
-        [z, z ^ 1, jnp.where(inner, z ^ 3, z ^ 2), jnp.where(inner, z ^ 2, z ^ 3), inner]
-    )
-    where = jnp.concatenate([place[:5], out_places.astype(jnp.int32)])
+    where = jnp.concatenate([place, inner.astype(jnp.int32)[None]])
     shares = finish(where, own, r1, r2, r3, out_gain.reshape(1, -1), out_parts)
     total = shares[0].astype(jnp.float32)
     for t in (1, 2, 3):

time: 294 us -> 317 us (1.078)
  starting transfers between devices: 39.9 us -> 54.1 us
  waiting for transfers between devices: 177 us -> 186 us
    ppermute x0 -> x4, waiting for transfers between devices: none -> 80.4 us  [the longest x1 71.6 us: per_device_one_head(): across_next = lax.ppermute(near, 'ctx', middle)]
    ppermute x28 -> x30, waiting for transfers between devices: 143 us -> 81.7 us  [swapped(): return lax.ppermute(value, axis, [(i, i ^ mask) for i in range(count)])]
    all_to_all x1, waiting for transfers between devices: 9.72 us -> 0.01 us  [per_device_one_head(): w_same = lax.all_to_all(w_pieces, 'ctx', 0, 0, axis_index_groups=same_core)]
    ppermute x0 -> x4, starting transfers between devices: none -> 7.6 us  [the longest x1 3.05 us: per_device_one_head(): across_next = lax.ppermute(near, 'ctx', middle)]
    ppermute x28 -> x30, starting transfers between devices: 24.8 us -> 30.9 us  [swapped(): return lax.ppermute(value, axis, [(i, i ^ mask) for i in range(count)])]
  transfers between devices with their start and end apart: 33 -> 39, of which waited for: 20 -> 21; matrix products, arithmetic and copies ran while one was open for 6% -> 6% of each run, Pallas kernels for 12% -> 12%
where the time goes in v12:
time: 317 us; the launch traced here: 315 us
  waiting for transfers between devices  186 us (59%)
  starting transfers between devices  54.1 us (17%)
  Pallas kernels  44.7 us (14%)
  other arithmetic  18.5 us (6%)
  local copies, waits for them, and re-layouts  12.1 us (4%)
    ppermute x30, waiting for transfers between devices, swapped(): return lax.ppermute(value, axis, [(i, i ^ mask) for i in range(count)])  81.7 us
    ppermute x1, waiting for transfers between devices, per_device_one_head(): across_next = lax.ppermute(near, 'ctx', middle)  71.6 us
    ppermute x30, starting transfers between devices, swapped(): return lax.ppermute(value, axis, [(i, i ^ mask) for i in range(count)])  30.9 us
    pallas_call x2, Pallas kernels, project(): pl.pallas_call(functools.partial(project_kernel, rows, first_col), out_sh...  20 us
    pallas_call x1, Pallas kernels, attend_head(): pl.pallas_call(attend_kernel, grid=(count,), out_shape=(out, out), in_spe...  16.7 us
    ppermute x1, waiting for transfers between devices, per_device_one_head(): out_passed_next = lax.ppermute(out_across_next, 'ctx', outward)  13 us
    ppermute x1, waiting for transfers between devices, per_device_one_head(): passed_next = lax.ppermute(across_next, 'ctx', outward)  8.76 us
    ppermute x1, waiting for transfers between devices, per_device_one_head(): out_across_next = lax.ppermute(out_near, 'ctx', middle)  8.24 us
  transfers between devices with their start and end apart: 39, of which 21 were waited for; matrix products, arithmetic and copies ran while one was open for 6% of the time, Pallas kernels for 12%

profile of v12, /device:TPU:17, one launch (start us, length us, event | category | flops | bytes accessed | tf_op | source)
XLA Modules:
  0.0 315.5 jit_solution(2985851890461087010)
XLA Ops:
  0.8 2.0 pad_maximum_fusion.7
  2.8 1.3 collective-permute-start
  4.1 1.9 collective-permute-start.1
  6.0 1.3 collective-permute-start.2
  7.3 1.2 collective-permute-start.3
  9.3 0.9 fusion.19
  10.2 0.9 fusion.18
  11.8 1.3 fusion.17.weights
  13.1 1.4 maximum_bitcast_fusion
  14.5 1.9 pad_maximum_fusion
  16.4 2.5 collective-permute-done.2.refs_4_
  18.9 0.9 collective-permute-done.3.refs_9_
  19.8 0.8 copy-done.14
  20.8 3.7 %all-to-all-start = ((bf16[4,512,768]{2,1,0:T(8,128)(2,1)}), bf16[4,512,768]{2,1,0:T(8,128)(2,1)S(1)}, u32[]{:S(2)}, u32[]{:S(2)}) async-start(bf16[4,512,768]{2,1,0:T(8,128)(2,1)} %pad_maximum_fusion), calls=%async_computation | async-start | bytes 6291456 | tf_op jit(solution)/shard_map/all_to_all | solution.py:610
  24.6 1.2 slice-done
  26.6 1.2 collective-permute-start.7
  27.8 3.1 collective-permute-start.4
  30.9 1.3 collective-permute-start.5
  32.2 71.6 %collective-permute-done.4 = bf16[272,1024]{1,0:T(8,128)(2,1)S(1)} collective-permute-done((bf16[272,1024]{1,0:T(8,128)(2,1)S(1)}, bf16[272,1024]{1,0:T(8,128)(2,1)S(1)}, u32[]{:S(2)}, u32[]{:S(2)}) %collective-permute-start.4) | collective-permute-done | bytes 557088 | tf_op jit(solution)/shard_map/ppermute | solution.py:611
  103.9 1.7 add.86.refs_2_
  106.6 1.2 collective-permute-start.10
  107.9 1.3 collective-permute-start.8
  109.2 8.8 %collective-permute-done.8 = bf16[272,1024]{1,0:T(8,128)(2,1)S(1)} collective-permute-done((bf16[272,1024]{1,0:T(8,128)(2,1)S(1)}, bf16[272,1024]{1,0:T(8,128)(2,1)S(1)}, u32[]{:S(2)}, u32[]{:S(2)}) %collective-permute-start.8) | collective-permute-done | bytes 557088 | tf_op jit(solution)/shard_map/ppermute | solution.py:616
  118.0 4.0 %collective-permute-done.9.refs_6_ = bf16[384,1024]{1,0:T(8,128)(2,1)S(1)} collective-permute-done((bf16[384,1024]{1,0:T(8,128)(2,1)S(1)}, bf16[384,1024]{1,0:T(8,128)(2,1)S(1)}, u32[]{:S(2)}, u32[]{:S(2)}) %collective-permute-start.9) | collective-permute-done | bytes 786464 | tf_op jit(solution)/shard_map/ppermute | solution.py:567
  124.4 1.2 collective-permute-start.12
  125.7 1.9 fusion.3
  127.6 1.0 pad_maximum_fusion.8.refs_16_
  128.6 1.0 pad_maximum_fusion.9.refs_17_
  129.6 9.2 %collective-permute-done.11.refs_7_ = bf16[384,1024]{1,0:T(8,128)(2,1)S(1)} collective-permute-done((bf16[384,1024]{1,0:T(8,128)(2,1)S(1)}, bf16[384,1024]{1,0:T(8,128)(2,1)S(1)}, u32[]{:S(2)}, u32[]{:S(2)}) %collective-permute-start.11) | collective-permute-done | bytes 786464 | tf_op jit(solution)/shard_map/ppermute | solution.py:567
  139.0 1.1 collective-permute-start.13
  140.1 1.3 collective-permute-start.14
  141.4 4.4 %collective-permute-done.13.refs_8_ = bf16[128,1024]{1,0:T(8,128)(2,1)S(1)} collective-permute-done((bf16[128,1024]{1,0:T(8,128)(2,1)S(1)}, bf16[128,1024]{1,0:T(8,128)(2,1)S(1)}, u32[]{:S(2)}, u32[]{:S(2)}) %collective-permute-start.13) | collective-permute-done | bytes 262176 | tf_op jit(solution)/shard_map/ppermute | solution.py:567
  146.6 7.0 %collective-permute-start.15 = (bf16[4,512,768]{2,1,0:T(8,128)(2,1)S(1)}, bf16[4,512,768]{2,1,0:T(8,128)(2,1)S(1)}, u32[]{:S(2)}, u32[]{:S(2)}) collective-permute-start(bf16[4,512,768]{2,1,0:T(8,128)(2,1)S(1)} %all-to-all-done.refs_14_), channel_id=1, source_target_pairs={{0,4},{4,0},{8,12},{12,8},{16,20},{20,16},{24,28},{28,24},{1,5},{5... | collective-permute-start | bytes 9437192 | tf_op jit(solution)/shard_map/ppermute | solution.py:567
  153.6 3.6 %collective-permute-start.17 = (bf16[1024,512]{1,0:T(8,128)(2,1)}, bf16[1024,512]{1,0:T(8,128)(2,1)}, u32[]{:S(2)}, u32[]{:S(2)}) collective-permute-start(bf16[1024,512]{1,0:T(8,128)(2,1)} %refs_0_.4), channel_id=1, source_target_pairs={{8,16},{12,20},{16,8},{20,12},{9,17},{13,21},{17,9},{21,13},{10,18... | collective-permute-start | bytes 3145736 | tf_op jit(solution)/shard_map/ppermute | solution.py:636
  157.3 1.6 collective-permute-done.15.refs_15_
  158.9 1.7 copy-done.4
  160.6 9.4 %shard_map.91.refs_2_ = bf16[4,256,256]{2,1,0:T(8,128)(2,1)} custom-call(s32[9]{0:T(128)} %stack.78.place, bf16[256,1024]{1,0:T(8,128)(2,1)} %refs_0_.3, bf16[272,1024]{1,0:T(8,128)(2,1)} %copy-done.5, bf16[272,1024]{1,0:T(8,128)(2,1)} %copy-done.2, bf16[272,1024]{1,0:T(8,128)(2,1)} %copy-done.3, bf16[256,1024]{1,0:T(8,128)(2,1)} %copy-done.13, ...), custom_call_target="tpu_custom_call" | custom-call | flops 2147483648 | bytes 16777216 | tf_op jit(solution)/shard_map/pallas_call | solution.py:261
  170.0 8.7 %collective-permute-done.16.refs_2_ = bf16[1024,512]{1,0:T(8,128)(2,1)} collective-permute-done((bf16[1024,512]{1,0:T(8,128)(2,1)}, bf16[1024,512]{1,0:T(8,128)(2,1)}, u32[]{:S(2)}, u32[]{:S(2)}) %collective-permute-start.16) | collective-permute-done | bytes 1048608 | tf_op jit(solution)/shard_map/ppermute | solution.py:567
  178.7 2.1 collective-permute-done.17.refs_4_
  180.8 0.9 collective-permute-start.19
  181.8 3.4 %collective-permute-start.22 = (bf16[1024,512]{1,0:T(8,128)(2,1)}, bf16[1024,512]{1,0:T(8,128)(2,1)}, u32[]{:S(2)}, u32[]{:S(2)}) collective-permute-start(bf16[1024,512]{1,0:T(8,128)(2,1)} %collective-permute-done.16.refs_2_), channel_id=1, source_target_pairs={{8,16},{12,20},{16,8},{20,12},{9,17},{13,21},{17,9},{21,13},{10,18... | collective-permute-start | bytes 3145736 | tf_op jit(solution)/shard_map/ppermute | solution.py:645
  185.1 10.6 %shard_map.92 = (bf16[4,256,256]{2,1,0:T(8,128)(2,1)}, bf16[4,256,256]{2,1,0:T(8,128)(2,1)}) custom-call(s32[9]{0:T(128)} %stack.78.place, bf16[256,1024]{1,0:T(8,128)(2,1)} %refs_0_.3, bf16[272,1024]{1,0:T(8,128)(2,1)} %copy-done.5, bf16[272,1024]{1,0:T(8,128)(2,1)} %copy-done.2, bf16[272,1024]{1,0:T(8,128)(2,1)} %copy-done.3, ...), custom_call_target="tpu_custom_call" | custom-call | flops 4294967296 | bytes 16777216 | tf_op jit(solution)/shard_map/pallas_call | solution.py:261
  197.4 2.6 collective-permute-start.24
  200.0 8.2 %collective-permute-done.22.refs_8_ = bf16[1024,512]{1,0:T(8,128)(2,1)} collective-permute-done((bf16[1024,512]{1,0:T(8,128)(2,1)}, bf16[1024,512]{1,0:T(8,128)(2,1)}, u32[]{:S(2)}, u32[]{:S(2)}) %collective-permute-start.22) | collective-permute-done | bytes 1048608 | tf_op jit(solution)/shard_map/ppermute | solution.py:645
  208.3 1.3 collective-permute-start.27
  210.4 0.8 copy-done.29
  211.2 2.3 collective-permute-start.25
  214.1 16.7 %shard_map.93 = (bf16[4,256,512]{2,1,0:T(8,128)(2,1)}, bf16[4,256,512]{2,1,0:T(8,128)(2,1)}) custom-call(s32[9]{0:T(128)} %stack.78.place, f32[4]{0:T(128)} %dynamic-slice_bitcast_fusion.1.mix, f32[66]{0:T(128)} %fusion.17.weights, bf16[4,256,256]{2,1,0:T(8,128)(2,1)} %get-tuple-element.81.refs_0_, bf16[4,256,256]{2,1,0:T(8,128)(2,1)} %copy-done.28, ...), custom_call_target="tpu_custom_call" | custom-call | flops 5368709120 | bytes 16777216 | tf_op jit(solution)/shard_map/pallas_call | solution.py:471
  230.8 13.0 %collective-permute-done.25.refs_10_ = bf16[1024,512]{1,0:T(8,128)(2,1)} collective-permute-done((bf16[1024,512]{1,0:T(8,128)(2,1)}, bf16[1024,512]{1,0:T(8,128)(2,1)}, u32[]{:S(2)}, u32[]{:S(2)}) %collective-permute-start.25) | collective-permute-done | bytes 1048608 | tf_op jit(solution)/shard_map/ppermute | solution.py:655
  243.8 1.3 collective-permute-start.28
  245.7 3.6 %collective-permute-done.28 = bf16[4,256,512]{2,1,0:T(8,128)(2,1)} collective-permute-done((bf16[4,256,512]{2,1,0:T(8,128)(2,1)}, bf16[4,256,512]{2,1,0:T(8,128)(2,1)}, u32[]{:S(2)}, u32[]{:S(2)}) %collective-permute-start.28) | collective-permute-done | bytes 1048608 | tf_op jit(solution)/shard_map/ppermute | solution.py:567
  249.3 1.9 convert_add_fusion
  251.2 1.0 fusion.2
  252.1 2.2 collective-permute-start.29
  254.3 1.2 collective-permute-start.30
  256.5 0.8 dynamic-slice_bitcast_fusion.own
  257.3 7.8 %collective-permute-done.29.r1 = bf16[256,512]{1,0:T(8,128)(2,1)S(1)} collective-permute-done((bf16[256,512]{1,0:T(8,128)(2,1)}, bf16[256,512]{1,0:T(8,128)(2,1)S(1)}, u32[]{:S(2)}, u32[]{:S(2)}) %collective-permute-start.29) | collective-permute-done | bytes 262176 | tf_op jit(solution)/shard_map/ppermute | solution.py:567
  265.1 7.2 %collective-permute-done.30.r2 = bf16[256,512]{1,0:T(8,128)(2,1)} collective-permute-done((bf16[256,512]{1,0:T(8,128)(2,1)}, bf16[256,512]{1,0:T(8,128)(2,1)}, u32[]{:S(2)}, u32[]{:S(2)}) %collective-permute-start.30) | collective-permute-done | bytes 262176 | tf_op jit(solution)/shard_map/ppermute | solution.py:567
  272.3 6.8 %collective-permute-done.31.r3 = bf16[256,512]{1,0:T(8,128)(2,1)} collective-permute-done((bf16[256,512]{1,0:T(8,128)(2,1)}, bf16[256,512]{1,0:T(8,128)(2,1)}, u32[]{:S(2)}, u32[]{:S(2)}) %collective-permute-start.31) | collective-permute-done | bytes 262176 | tf_op jit(solution)/shard_map/ppermute | solution.py:567
  279.1 8.0 %shard_map.94 = (bf16[256,1024]{1,0:T(8,128)(2,1)}, bf16[256,1024]{1,0:T(8,128)(2,1)}, bf16[256,1024]{1,0:T(8,128)(2,1)}, bf16[256,1024]{1,0:T(8,128)(2,1)}) custom-call(s32[10]{0:T(128)} %pad_add_fusion.place, f32[256,512]{1,0:T(8,128)} %dynamic-slice_bitcast_fusion.own, bf16[256,512]{1,0:T(8,128)(2,1)} %copy-done.24, ...), custom_call_target="tpu_custom_call" | custom-call | flops 2147483648 | bytes 11534336 | tf_op jit(solution)/shard_map/pallas_call | solution.py:548
  287.0 1.9 collective-permute-start.37
  289.8 10.7 %collective-permute-done.37 = bf16[256,1024]{1,0:T(8,128)(2,1)S(1)} collective-permute-done((bf16[256,1024]{1,0:T(8,128)(2,1)}, bf16[256,1024]{1,0:T(8,128)(2,1)S(1)}, u32[]{:S(2)}, u32[]{:S(2)}) %collective-permute-start.37) | collective-permute-done | bytes 524320 | tf_op jit(solution)/shard_map/ppermute | solution.py:567
  300.5 12.8 %collective-permute-done.36 = bf16[256,1024]{1,0:T(8,128)(2,1)S(1)} collective-permute-done((bf16[256,1024]{1,0:T(8,128)(2,1)}, bf16[256,1024]{1,0:T(8,128)(2,1)S(1)}, u32[]{:S(2)}, u32[]{:S(2)}) %collective-permute-start.36) | collective-permute-done | bytes 524320 | tf_op jit(solution)/shard_map/ppermute | solution.py:567
  313.3 2.2 add_convert_fusion
  (125 shorter events, 13.1 us)
Async XLA Ops:
  0.0 213.4 %copy-start = (f32[8,4]{0,1:T(4,128)S(1)}, f32[8,4]{0,1:T(4,128)}, u32[]{:S(2)}) copy-start(f32[8,4]{0,1:T(4,128)} %param.15) | copy-start | bytes 388
  0.0 8.6 %copy-start.20 = (bf16[512,1024]{1,0:T(8,128)(2,1)S(1)}, bf16[512,1024]{1,0:T(8,128)(2,1)}, u32[]{:S(2)}) copy-start(bf16[512,1024]{1,0:T(8,128)(2,1)} %param.13) | copy-start | bytes 3145732
  0.8 8.5 %copy-start.21 = (bf16[512,1024]{1,0:T(8,128)(2,1)S(1)}, bf16[512,1024]{1,0:T(8,128)(2,1)}, u32[]{:S(2)}) copy-start(bf16[512,1024]{1,0:T(8,128)(2,1)} %param.12) | copy-start | bytes 3145732
  2.8 7.4 %copy-start.22 = (bf16[512,1024]{1,0:T(8,128)(2,1)S(1)}, bf16[512,1024]{1,0:T(8,128)(2,1)}, u32[]{:S(2)}) copy-start(bf16[512,1024]{1,0:T(8,128)(2,1)} %param.11) | copy-start | bytes 3145732
  2.8 17.0 %collective-permute-start = (bf16[272,1024]{1,0:T(8,128)(2,1)}, bf16[272,1024]{1,0:T(8,128)(2,1)S(1)}, u32[]{:S(2)}, u32[]{:S(2)}) collective-permute-start(bf16[272,1024]{1,0:T(8,128)(2,1)} %pad_maximum_fusion.7), channel_id=1, source_target_pairs={{0,8},{4,12},{8,0},{12,4},{16,24},{20,28},{24,16},{28,20},{1,9},{5... | collective-permute-start | bytes 1671176 | tf_op jit(solution)/shard_map/ppermute | solution.py:567
  4.1 15.7 %collective-permute-start.1 = (bf16[272,1024]{1,0:T(8,128)(2,1)}, bf16[272,1024]{1,0:T(8,128)(2,1)}, u32[]{:S(2)}, u32[]{:S(2)}) collective-permute-start(bf16[272,1024]{1,0:T(8,128)(2,1)} %pad_maximum_fusion.7), channel_id=1, source_target_pairs={{8,16},{12,20},{16,8},{20,12},{9,17},{13,21},{17,9},{21,13},{10,18... | collective-permute-start | bytes 1671176 | tf_op jit(solution)/shard_map/ppermute | solution.py:600
  6.0 12.9 %collective-permute-start.2 = (bf16[256,1024]{1,0:T(8,128)(2,1)}, bf16[256,1024]{1,0:T(8,128)(2,1)S(1)}, u32[]{:S(2)}, u32[]{:S(2)}) collective-permute-start(bf16[256,1024]{1,0:T(8,128)(2,1)} %refs_0_.3), channel_id=1, source_target_pairs={{0,1},{1,0},{2,3},{3,2},{4,5},{5,4},{6,7},{7,6},{8,9},{9,8},{10,11... | collective-permute-start | bytes 1572872 | tf_op jit(solution)/shard_map/ppermute | solution.py:567
  7.3 12.5 %collective-permute-start.3 = (bf16[256,1024]{1,0:T(8,128)(2,1)}, bf16[256,1024]{1,0:T(8,128)(2,1)S(1)}, u32[]{:S(2)}, u32[]{:S(2)}) collective-permute-start(bf16[256,1024]{1,0:T(8,128)(2,1)} %refs_0_.3), channel_id=1, source_target_pairs={{0,2},{1,3},{2,0},{3,1},{4,6},{5,7},{6,4},{7,5},{8,10},{9,11},{10,... | collective-permute-start | bytes 1572872 | tf_op jit(solution)/shard_map/ppermute | solution.py:567
  20.8 125.8 %all-to-all-start = ((bf16[4,512,768]{2,1,0:T(8,128)(2,1)}), bf16[4,512,768]{2,1,0:T(8,128)(2,1)S(1)}, u32[]{:S(2)}, u32[]{:S(2)}) async-start(bf16[4,512,768]{2,1,0:T(8,128)(2,1)} %pad_maximum_fusion), calls=%async_computation | async-start | bytes 6291456 | tf_op jit(solution)/shard_map/all_to_all | solution.py:610
  24.5 1.2 slice-start
  24.5 1.3 slice-start.1
  24.5 1.3 slice-start.2
  24.5 3.3 %copy-start.6 = (bf16[272,1024]{1,0:T(8,128)(2,1)S(1)}, bf16[272,1024]{1,0:T(8,128)(2,1)}, u32[]{:S(2)}) copy-start(bf16[272,1024]{1,0:T(8,128)(2,1)} %copy-done.5) | copy-start | bytes 1671172
  26.1 77.8 %collective-permute-start.6 = (bf16[384,1024]{1,0:T(8,128)(2,1)S(1)}, bf16[384,1024]{1,0:T(8,128)(2,1)S(1)}, u32[]{:S(2)}, u32[]{:S(2)}) collective-permute-start(bf16[384,1024]{1,0:T(8,128)(2,1)S(1)} %get-tuple-element.123), channel_id=1, source_target_pairs={{0,1},{1,0},{2,3},{3,2},{4,5},{5,4},{6,7},{7,6},{8,9},{9,8},{10,11... | collective-permute-start | bytes 2359304 | tf_op jit(solution)/shard_map/ppermute | solution.py:567
  26.6 77.3 %collective-permute-start.7 = (bf16[384,1024]{1,0:T(8,128)(2,1)S(1)}, bf16[384,1024]{1,0:T(8,128)(2,1)S(1)}, u32[]{:S(2)}, u32[]{:S(2)}) collective-permute-start(bf16[384,1024]{1,0:T(8,128)(2,1)S(1)} %get-tuple-element.122), channel_id=1, source_target_pairs={{0,2},{1,3},{2,0},{3,1},{4,6},{5,7},{6,4},{7,5},{8,10},{9,11},{10,... | collective-permute-start | bytes 2359304 | tf_op jit(solution)/shard_map/ppermute | solution.py:567
  27.8 76.0 %collective-permute-start.4 = (bf16[272,1024]{1,0:T(8,128)(2,1)S(1)}, bf16[272,1024]{1,0:T(8,128)(2,1)S(1)}, u32[]{:S(2)}, u32[]{:S(2)}) collective-permute-start(bf16[272,1024]{1,0:T(8,128)(2,1)S(1)} %copy-done.6), channel_id=1, source_target_pairs={{8,16},{12,20},{16,8},{20,12},{9,17},{13,21},{17,9},{21,13},{10,18... | collective-permute-start | bytes 1671176 | tf_op jit(solution)/shard_map/ppermute | solution.py:611
  30.9 73.0 %collective-permute-start.5 = (bf16[272,1024]{1,0:T(8,128)(2,1)}, bf16[272,1024]{1,0:T(8,128)(2,1)S(1)}, u32[]{:S(2)}, u32[]{:S(2)}) collective-permute-start(bf16[272,1024]{1,0:T(8,128)(2,1)} %collective-permute-done.1), channel_id=1, source_target_pairs={{8,0},{12,4},{16,24},{20,28},{9,1},{13,5},{17,25},{21,29},{10,2},{... | collective-permute-start | bytes 1671176 | tf_op jit(solution)/shard_map/ppermute | solution.py:612
  103.9 1.8 copy-start.7
  103.9 1.8 copy-start.8
  105.6 3.6 %copy-start.2 = (bf16[272,1024]{1,0:T(8,128)(2,1)}, bf16[272,1024]{1,0:T(8,128)(2,1)S(1)}, u32[]{:S(2)}) copy-start(bf16[272,1024]{1,0:T(8,128)(2,1)S(1)} %add.86.refs_2_) | copy-start | bytes 1671172
  105.9 16.1 %collective-permute-start.9 = (bf16[384,1024]{1,0:T(8,128)(2,1)S(1)}, bf16[384,1024]{1,0:T(8,128)(2,1)S(1)}, u32[]{:S(2)}, u32[]{:S(2)}) collective-permute-start(bf16[384,1024]{1,0:T(8,128)(2,1)S(1)} %get-tuple-element.121), channel_id=1, source_target_pairs={{0,1},{1,0},{2,3},{3,2},{4,5},{5,4},{6,7},{7,6},{8,9},{9,8},{10,11... | collective-permute-start | bytes 2359304 | tf_op jit(solution)/shard_map/ppermute | solution.py:567
  106.6 16.0 %collective-permute-start.10 = (bf16[384,1024]{1,0:T(8,128)(2,1)S(1)}, bf16[384,1024]{1,0:T(8,128)(2,1)S(1)}, u32[]{:S(2)}, u32[]{:S(2)}) collective-permute-start(bf16[384,1024]{1,0:T(8,128)(2,1)S(1)} %get-tuple-element.120), channel_id=1, source_target_pairs={{0,2},{1,3},{2,0},{3,1},{4,6},{5,7},{6,4},{7,5},{8,10},{9,11},{10,... | collective-permute-start | bytes 2359304 | tf_op jit(solution)/shard_map/ppermute | solution.py:567
  107.9 10.1 %collective-permute-start.8 = (bf16[272,1024]{1,0:T(8,128)(2,1)S(1)}, bf16[272,1024]{1,0:T(8,128)(2,1)S(1)}, u32[]{:S(2)}, u32[]{:S(2)}) collective-permute-start(bf16[272,1024]{1,0:T(8,128)(2,1)S(1)} %collective-permute-done.4), channel_id=1, source_target_pairs={{8,0},{12,4},{16,24},{20,28},{9,1},{13,5},{17,25},{21,29},{10,2},{... | collective-permute-start | bytes 1671176 | tf_op jit(solution)/shard_map/ppermute | solution.py:616
  122.8 2.8 copy-start.3
  123.7 15.1 %collective-permute-start.11 = (bf16[384,1024]{1,0:T(8,128)(2,1)S(1)}, bf16[384,1024]{1,0:T(8,128)(2,1)S(1)}, u32[]{:S(2)}, u32[]{:S(2)}) collective-permute-start(bf16[384,1024]{1,0:T(8,128)(2,1)S(1)} %get-tuple-element.119), channel_id=1, source_target_pairs={{0,1},{1,0},{2,3},{3,2},{4,5},{5,4},{6,7},{7,6},{8,9},{9,8},{10,11... | collective-permute-start | bytes 2359304 | tf_op jit(solution)/shard_map/ppermute | solution.py:567
  124.4 14.6 %collective-permute-start.12 = (bf16[384,1024]{1,0:T(8,128)(2,1)S(1)}, bf16[384,1024]{1,0:T(8,128)(2,1)S(1)}, u32[]{:S(2)}, u32[]{:S(2)}) collective-permute-start(bf16[384,1024]{1,0:T(8,128)(2,1)S(1)} %get-tuple-element.118), channel_id=1, source_target_pairs={{0,2},{1,3},{2,0},{3,1},{4,6},{5,7},{6,4},{7,5},{8,10},{9,11},{10,... | collective-permute-start | bytes 2359304 | tf_op jit(solution)/shard_map/ppermute | solution.py:567
  138.8 7.0 %copy-start.11 = (bf16[384,1024]{1,0:T(8,128)(2,1)}, bf16[384,1024]{1,0:T(8,128)(2,1)S(1)}, u32[]{:S(2)}) copy-start(bf16[384,1024]{1,0:T(8,128)(2,1)S(1)} %collective-permute-done.11.refs_7_) | copy-start | bytes 2359300
  139.0 6.9 %copy-start.12 = (bf16[384,1024]{1,0:T(8,128)(2,1)}, bf16[384,1024]{1,0:T(8,128)(2,1)S(1)}, u32[]{:S(2)}) copy-start(bf16[384,1024]{1,0:T(8,128)(2,1)S(1)} %collective-permute-done.12.refs_12_) | copy-start | bytes 2359300
  139.0 6.9 %collective-permute-start.13 = (bf16[128,1024]{1,0:T(8,128)(2,1)S(1)}, bf16[128,1024]{1,0:T(8,128)(2,1)S(1)}, u32[]{:S(2)}, u32[]{:S(2)}) collective-permute-start(bf16[128,1024]{1,0:T(8,128)(2,1)S(1)} %slice.73), channel_id=1, source_target_pairs={{0,1},{1,0},{2,3},{3,2},{4,5},{5,4},{6,7},{7,6},{8,9},{9,8},{10,11... | collective-permute-start | bytes 786440 | tf_op jit(solution)/shard_map/ppermute | solution.py:567
  140.1 6.5 %collective-permute-start.14 = (bf16[128,1024]{1,0:T(8,128)(2,1)S(1)}, bf16[128,1024]{1,0:T(8,128)(2,1)}, u32[]{:S(2)}, u32[]{:S(2)}) collective-permute-start(bf16[128,1024]{1,0:T(8,128)(2,1)S(1)} %slice.74), channel_id=1, source_target_pairs={{0,2},{1,3},{2,0},{3,1},{4,6},{5,7},{6,4},{7,5},{8,10},{9,11},{10,... | collective-permute-start | bytes 786440 | tf_op jit(solution)/shard_map/ppermute | solution.py:567
  145.9 13.0 %copy-start.23 = (bf16[128,1024]{1,0:T(8,128)(2,1)}, bf16[128,1024]{1,0:T(8,128)(2,1)S(1)}, u32[]{:S(2)}) copy-start(bf16[128,1024]{1,0:T(8,128)(2,1)S(1)} %collective-permute-done.13.refs_8_) | copy-start | bytes 786436
  146.6 12.3 %copy-start.1 = (bf16[4,512,768]{2,1,0:T(8,128)(2,1)}, bf16[4,512,768]{2,1,0:T(8,128)(2,1)S(1)}, u32[]{:S(2)}) copy-start(bf16[4,512,768]{2,1,0:T(8,128)(2,1)S(1)} %all-to-all-done.refs_14_) | copy-start | bytes 9437188
  146.6 35.1 %copy-start.15 = (bf16[1024,512]{1,0:T(8,128)(2,1)S(1)}, bf16[1024,512]{1,0:T(8,128)(2,1)}, u32[]{:S(2)}) copy-start(bf16[1024,512]{1,0:T(8,128)(2,1)} %refs_0_.4) | copy-start | bytes 3145732
  146.6 12.3 %collective-permute-start.15 = (bf16[4,512,768]{2,1,0:T(8,128)(2,1)S(1)}, bf16[4,512,768]{2,1,0:T(8,128)(2,1)S(1)}, u32[]{:S(2)}, u32[]{:S(2)}) collective-permute-start(bf16[4,512,768]{2,1,0:T(8,128)(2,1)S(1)} %all-to-all-done.refs_14_), channel_id=1, source_target_pairs={{0,4},{4,0},{8,12},{12,8},{16,20},{20,16},{24,28},{28,24},{1,5},{5... | collective-permute-start | bytes 9437192 | tf_op jit(solution)/shard_map/ppermute | solution.py:567
  153.6 25.1 %collective-permute-start.16 = (bf16[1024,512]{1,0:T(8,128)(2,1)}, bf16[1024,512]{1,0:T(8,128)(2,1)}, u32[]{:S(2)}, u32[]{:S(2)}) collective-permute-start(bf16[1024,512]{1,0:T(8,128)(2,1)} %refs_0_.4), channel_id=1, source_target_pairs={{0,8},{4,12},{8,0},{12,4},{16,24},{20,28},{24,16},{28,20},{1,9},{5... | collective-permute-start | bytes 3145736 | tf_op jit(solution)/shard_map/ppermute | solution.py:567
  153.6 27.2 %collective-permute-start.17 = (bf16[1024,512]{1,0:T(8,128)(2,1)}, bf16[1024,512]{1,0:T(8,128)(2,1)}, u32[]{:S(2)}, u32[]{:S(2)}) collective-permute-start(bf16[1024,512]{1,0:T(8,128)(2,1)} %refs_0_.4), channel_id=1, source_target_pairs={{8,16},{12,20},{16,8},{20,12},{9,17},{13,21},{17,9},{21,13},{10,18... | collective-permute-start | bytes 3145736 | tf_op jit(solution)/shard_map/ppermute | solution.py:636
  158.9 1.7 copy-start.4
  180.8 14.9 %collective-permute-start.18 = (bf16[4,256,256]{2,1,0:T(8,128)(2,1)}, bf16[4,256,256]{2,1,0:T(8,128)(2,1)S(1)}, u32[]{:S(2)}, u32[]{:S(2)}) collective-permute-start(bf16[4,256,256]{2,1,0:T(8,128)(2,1)} %shard_map.91.refs_2_), channel_id=1, source_target_pairs={{0,8},{4,12},{8,0},{12,4},{16,24},{20,28},{24,16},{28,20},{1,9},{5... | collective-permute-start | bytes 1572872 | tf_op jit(solution)/shard_map/ppermute | solution.py:567
  180.8 15.0 %collective-permute-start.19 = (bf16[4,256,256]{2,1,0:T(8,128)(2,1)}, bf16[4,256,256]{2,1,0:T(8,128)(2,1)S(1)}, u32[]{:S(2)}, u32[]{:S(2)}) collective-permute-start(bf16[4,256,256]{2,1,0:T(8,128)(2,1)} %shard_map.91.refs_2_), channel_id=1, source_target_pairs={{0,4},{4,0},{8,12},{12,8},{16,20},{20,16},{24,28},{28,24},{1,5},{5... | collective-permute-start | bytes 1572872 | tf_op jit(solution)/shard_map/ppermute | solution.py:567
  181.7 15.7 %collective-permute-start.23 = (bf16[1024,512]{1,0:T(8,128)(2,1)S(1)}, bf16[1024,512]{1,0:T(8,128)(2,1)S(1)}, u32[]{:S(2)}, u32[]{:S(2)}) collective-permute-start(bf16[1024,512]{1,0:T(8,128)(2,1)S(1)} %copy-done.15), channel_id=1, source_target_pairs={{0,4},{4,0},{8,12},{12,8},{16,20},{20,16},{24,28},{28,24},{1,5},{5... | collective-permute-start | bytes 3145736 | tf_op jit(solution)/shard_map/ppermute | solution.py:567
  181.8 26.5 %collective-permute-start.22 = (bf16[1024,512]{1,0:T(8,128)(2,1)}, bf16[1024,512]{1,0:T(8,128)(2,1)}, u32[]{:S(2)}, u32[]{:S(2)}) collective-permute-start(bf16[1024,512]{1,0:T(8,128)(2,1)} %collective-permute-done.16.refs_2_), channel_id=1, source_target_pairs={{8,16},{12,20},{16,8},{20,12},{9,17},{13,21},{17,9},{21,13},{10,18... | collective-permute-start | bytes 3145736 | tf_op jit(solution)/shard_map/ppermute | solution.py:645
  195.8 4.3 %copy-start.26 = (bf16[4,256,256]{2,1,0:T(8,128)(2,1)}, bf16[4,256,256]{2,1,0:T(8,128)(2,1)S(1)}, u32[]{:S(2)}) copy-start(bf16[4,256,256]{2,1,0:T(8,128)(2,1)S(1)} %collective-permute-done.18.refs_3_) | copy-start | bytes 1572868
  195.8 13.7 %collective-permute-start.20 = (bf16[4,256,256]{2,1,0:T(8,128)(2,1)}, bf16[4,256,256]{2,1,0:T(8,128)(2,1)S(1)}, u32[]{:S(2)}, u32[]{:S(2)}) collective-permute-start(bf16[4,256,256]{2,1,0:T(8,128)(2,1)} %get-tuple-element.82), channel_id=1, source_target_pairs={{0,4},{4,0},{8,12},{12,8},{16,20},{20,16},{24,28},{28,24},{1,5},{5... | collective-permute-start | bytes 1572872 | tf_op jit(solution)/shard_map/ppermute | solution.py:567
  196.7 12.9 %collective-permute-start.21 = (bf16[4,256,256]{2,1,0:T(8,128)(2,1)S(1)}, bf16[4,256,256]{2,1,0:T(8,128)(2,1)S(1)}, u32[]{:S(2)}, u32[]{:S(2)}) collective-permute-start(bf16[4,256,256]{2,1,0:T(8,128)(2,1)S(1)} %collective-permute-done.18.refs_3_), channel_id=1, source_target_pairs={{0,4},{4,0},{8,12},{12,8},{16,20},{20,16},{24,28},{28,24},{1,5},{5... | collective-permute-start | bytes 1572872 | tf_op jit(solution)/shard_map/ppermute | solution.py:567
  197.4 33.4 %collective-permute-start.26 = (bf16[1024,512]{1,0:T(8,128)(2,1)}, bf16[1024,512]{1,0:T(8,128)(2,1)S(1)}, u32[]{:S(2)}, u32[]{:S(2)}) collective-permute-start(bf16[1024,512]{1,0:T(8,128)(2,1)} %collective-permute-done.16.refs_2_), channel_id=1, source_target_pairs={{0,4},{4,0},{8,12},{12,8},{16,20},{20,16},{24,28},{28,24},{1,5},{5... | collective-permute-start | bytes 3145736 | tf_op jit(solution)/shard_map/ppermute | solution.py:567
  197.4 33.3 %copy-start.16 = (bf16[1024,512]{1,0:T(8,128)(2,1)}, bf16[1024,512]{1,0:T(8,128)(2,1)S(1)}, u32[]{:S(2)}) copy-start(bf16[1024,512]{1,0:T(8,128)(2,1)S(1)} %collective-permute-done.23.refs_1_) | copy-start | bytes 3145732
  197.4 33.4 %collective-permute-start.24 = (bf16[1024,512]{1,0:T(8,128)(2,1)}, bf16[1024,512]{1,0:T(8,128)(2,1)}, u32[]{:S(2)}, u32[]{:S(2)}) collective-permute-start(bf16[1024,512]{1,0:T(8,128)(2,1)} %collective-permute-done.17.refs_4_), channel_id=1, source_target_pairs={{8,0},{12,4},{16,24},{20,28},{9,1},{13,5},{17,25},{21,29},{10,2},{... | collective-permute-start | bytes 3145736 | tf_op jit(solution)/shard_map/ppermute | solution.py:646
  208.3 22.5 %collective-permute-start.27 = (bf16[1024,512]{1,0:T(8,128)(2,1)}, bf16[1024,512]{1,0:T(8,128)(2,1)S(1)}, u32[]{:S(2)}, u32[]{:S(2)}) collective-permute-start(bf16[1024,512]{1,0:T(8,128)(2,1)} %collective-permute-done.17.refs_4_), channel_id=1, source_target_pairs={{0,4},{4,0},{8,12},{12,8},{16,20},{20,16},{24,28},{28,24},{1,5},{5... | collective-permute-start | bytes 3145736 | tf_op jit(solution)/shard_map/ppermute | solution.py:567
  211.2 32.7 %collective-permute-start.25 = (bf16[1024,512]{1,0:T(8,128)(2,1)}, bf16[1024,512]{1,0:T(8,128)(2,1)}, u32[]{:S(2)}, u32[]{:S(2)}) collective-permute-start(bf16[1024,512]{1,0:T(8,128)(2,1)} %collective-permute-done.22.refs_8_), channel_id=1, source_target_pairs={{8,0},{12,4},{16,24},{20,28},{9,1},{13,5},{17,25},{21,29},{10,2},{... | collective-permute-start | bytes 3145736 | tf_op jit(solution)/shard_map/ppermute | solution.py:655
  230.8 14.9 %copy-start.17 = (bf16[1024,512]{1,0:T(8,128)(2,1)}, bf16[1024,512]{1,0:T(8,128)(2,1)S(1)}, u32[]{:S(2)}) copy-start(bf16[1024,512]{1,0:T(8,128)(2,1)S(1)} %collective-permute-done.26.refs_3_) | copy-start | bytes 3145732
  230.8 14.9 %copy-start.18 = (bf16[1024,512]{1,0:T(8,128)(2,1)}, bf16[1024,512]{1,0:T(8,128)(2,1)S(1)}, u32[]{:S(2)}) copy-start(bf16[1024,512]{1,0:T(8,128)(2,1)S(1)} %collective-permute-done.27.refs_5_) | copy-start | bytes 3145732
  243.8 5.4 %collective-permute-start.28 = (bf16[4,256,512]{2,1,0:T(8,128)(2,1)}, bf16[4,256,512]{2,1,0:T(8,128)(2,1)}, u32[]{:S(2)}, u32[]{:S(2)}) collective-permute-start(bf16[4,256,512]{2,1,0:T(8,128)(2,1)} %get-tuple-element.93), channel_id=1, source_target_pairs={{0,4},{4,0},{8,12},{12,8},{16,20},{20,16},{24,28},{28,24},{1,5},{5... | collective-permute-start | bytes 3145736 | tf_op jit(solution)/shard_map/ppermute | solution.py:567
  245.2 10.3 %collective-permute-start.33 = (bf16[1024,512]{1,0:T(8,128)(2,1)}, bf16[1024,512]{1,0:T(8,128)(2,1)S(1)}, u32[]{:S(2)}, u32[]{:S(2)}) collective-permute-start(bf16[1024,512]{1,0:T(8,128)(2,1)} %collective-permute-done.22.refs_8_), channel_id=1, source_target_pairs={{0,4},{4,0},{8,12},{12,8},{16,20},{20,16},{24,28},{28,24},{1,5},{5... | collective-permute-start | bytes 3145736 | tf_op jit(solution)/shard_map/ppermute | solution.py:567
  245.2 12.1 %collective-permute-start.32 = (bf16[1024,512]{1,0:T(8,128)(2,1)}, bf16[1024,512]{1,0:T(8,128)(2,1)}, u32[]{:S(2)}, u32[]{:S(2)}) collective-permute-start(bf16[1024,512]{1,0:T(8,128)(2,1)} %collective-permute-done.24.refs_6_), channel_id=1, source_target_pairs={{0,4},{4,0},{8,12},{12,8},{16,20},{20,16},{24,28},{28,24},{1,5},{5... | collective-permute-start | bytes 3145736 | tf_op jit(solution)/shard_map/ppermute | solution.py:567
  245.7 11.6 %collective-permute-start.34 = (bf16[1024,512]{1,0:T(8,128)(2,1)}, bf16[1024,512]{1,0:T(8,128)(2,1)}, u32[]{:S(2)}, u32[]{:S(2)}) collective-permute-start(bf16[1024,512]{1,0:T(8,128)(2,1)} %collective-permute-done.25.refs_10_), channel_id=1, source_target_pairs={{0,4},{4,0},{8,12},{12,8},{16,20},{20,16},{24,28},{28,24},{1,5},{5... | collective-permute-start | bytes 3145736 | tf_op jit(solution)/shard_map/ppermute | solution.py:567
  251.1 4.7 %copy-start.25 = (s32[9]{0:T(128)S(1)}, s32[9]{0:T(128)}, u32[]{:S(2)}) copy-start(s32[9]{0:T(128)} %stack.78.place) | copy-start | bytes 112
  252.1 12.9 %collective-permute-start.29 = (bf16[256,512]{1,0:T(8,128)(2,1)}, bf16[256,512]{1,0:T(8,128)(2,1)S(1)}, u32[]{:S(2)}, u32[]{:S(2)}) collective-permute-start(bf16[256,512]{1,0:T(8,128)(2,1)} %get-tuple-element.105), channel_id=1, source_target_pairs={{0,8},{4,12},{8,0},{12,4},{16,24},{20,28},{24,16},{28,20},{1,9},{5... | collective-permute-start | bytes 786440 | tf_op jit(solution)/shard_map/ppermute | solution.py:567
  254.3 18.0 %collective-permute-start.30 = (bf16[256,512]{1,0:T(8,128)(2,1)}, bf16[256,512]{1,0:T(8,128)(2,1)}, u32[]{:S(2)}, u32[]{:S(2)}) collective-permute-start(bf16[256,512]{1,0:T(8,128)(2,1)} %get-tuple-element.104), channel_id=1, source_target_pairs={{0,16},{4,20},{8,24},{12,28},{16,0},{20,4},{24,8},{28,12},{1,17},{... | collective-permute-start | bytes 786440 | tf_op jit(solution)/shard_map/ppermute | solution.py:567
  255.5 23.6 %copy-start.19 = (bf16[1024,512]{1,0:T(8,128)(2,1)}, bf16[1024,512]{1,0:T(8,128)(2,1)S(1)}, u32[]{:S(2)}) copy-start(bf16[1024,512]{1,0:T(8,128)(2,1)S(1)} %collective-permute-done.33.refs_9_) | copy-start | bytes 3145732
  255.5 23.5 %collective-permute-start.31 = (bf16[256,512]{1,0:T(8,128)(2,1)}, bf16[256,512]{1,0:T(8,128)(2,1)}, u32[]{:S(2)}, u32[]{:S(2)}) collective-permute-start(bf16[256,512]{1,0:T(8,128)(2,1)} %get-tuple-element.103), channel_id=1, source_target_pairs={{0,24},{4,28},{8,16},{12,20},{16,8},{20,12},{24,0},{28,4},{1,25},{... | collective-permute-start | bytes 786440 | tf_op jit(solution)/shard_map/ppermute | solution.py:567
  265.1 14.0 %copy-start.24 = (bf16[256,512]{1,0:T(8,128)(2,1)}, bf16[256,512]{1,0:T(8,128)(2,1)S(1)}, u32[]{:S(2)}) copy-start(bf16[256,512]{1,0:T(8,128)(2,1)S(1)} %collective-permute-done.29.r1) | copy-start | bytes 786436
  287.0 13.4 %collective-permute-start.37 = (bf16[256,1024]{1,0:T(8,128)(2,1)}, bf16[256,1024]{1,0:T(8,128)(2,1)S(1)}, u32[]{:S(2)}, u32[]{:S(2)}) collective-permute-start(bf16[256,1024]{1,0:T(8,128)(2,1)} %get-tuple-element.102), channel_id=1, source_target_pairs={{0,3},{1,2},{2,1},{3,0},{4,7},{5,6},{6,5},{7,4},{8,11},{9,10},{10,... | collective-permute-start | bytes 1572872 | tf_op jit(solution)/shard_map/ppermute | solution.py:567
  289.0 24.3 %collective-permute-start.36 = (bf16[256,1024]{1,0:T(8,128)(2,1)}, bf16[256,1024]{1,0:T(8,128)(2,1)S(1)}, u32[]{:S(2)}, u32[]{:S(2)}) collective-permute-start(bf16[256,1024]{1,0:T(8,128)(2,1)} %get-tuple-element.101), channel_id=1, source_target_pairs={{0,2},{1,3},{2,0},{3,1},{4,6},{5,7},{6,4},{7,5},{8,10},{9,11},{10,... | collective-permute-start | bytes 1572872 | tf_op jit(solution)/shard_map/ppermute | solution.py:567
  289.2 24.1 %collective-permute-start.35 = (bf16[256,1024]{1,0:T(8,128)(2,1)}, bf16[256,1024]{1,0:T(8,128)(2,1)S(1)}, u32[]{:S(2)}, u32[]{:S(2)}) collective-permute-start(bf16[256,1024]{1,0:T(8,128)(2,1)} %get-tuple-element.100), channel_id=1, source_target_pairs={{0,1},{1,0},{2,3},{3,2},{4,5},{5,4},{6,7},{7,6},{8,9},{9,8},{10,11... | collective-permute-start | bytes 1572872 | tf_op jit(solution)/shard_map/ppermute | solution.py:567
  (8 other events, 7.0 us)

commit v13 on v12

--- a/solution.py
+++ b/solution.py
@@ -607,11 +607,11 @@
         (near, across, x0, y0, w_pieces, weights, place, w_out)
     )
     same_core = [[i for i in range(8) if i % 2 == k] for k in range(2)]
-    w_same = lax.all_to_all(w_pieces, "ctx", 0, 0, axis_index_groups=same_core)
     across_next = lax.ppermute(near, "ctx", middle)
     passed = lax.ppermute(across, "ctx", outward)
     x1, y1 = plane(near, x0, y0)
-    across_next, passed, x1, y1 = barrier((across_next, passed, x1, y1))
+    across_next, passed, x1, y1, w_pieces = barrier((across_next, passed, x1, y1, w_pieces))
+    w_same = lax.all_to_all(w_pieces, "ctx", 0, 0, axis_index_groups=same_core)
     far_a = across + passed
     passed_next = lax.ppermute(across_next, "ctx", outward)
     x2, y2 = plane(far_a, x1, y1)

time: 317 us -> 282 us (0.89)
  waiting for transfers between devices: 186 us -> 150 us
    ppermute x1, waiting for transfers between devices: 71.6 us -> 9.3 us  [per_device_one_head(): across_next = lax.ppermute(near, 'ctx', middle)]
    ppermute x1, waiting for transfers between devices: 8.76 us -> 35.5 us  [per_device_one_head(): passed_next = lax.ppermute(across_next, 'ctx', outward)]
  transfers between devices with their start and end apart: 39 -> 39, of which waited for: 21 -> 22; matrix products, arithmetic and copies ran while one was open for 6% -> 8% of each run, Pallas kernels for 12% -> 13%
where the time goes in v13:
time: 282 us; the launch traced here: 281 us
  waiting for transfers between devices  150 us (53%)
  starting transfers between devices  53.9 us (19%)
  Pallas kernels  44.6 us (16%)
  other arithmetic  19 us (7%)
  local copies, waits for them, and re-layouts  12.6 us (4%)
    ppermute x30, waiting for transfers between devices, swapped(): return lax.ppermute(value, axis, [(i, i ^ mask) for i in range(count)])  80.4 us
    ppermute x1, waiting for transfers between devices, per_device_one_head(): passed_next = lax.ppermute(across_next, 'ctx', outward)  35.5 us
    ppermute x30, starting transfers between devices, swapped(): return lax.ppermute(value, axis, [(i, i ^ mask) for i in range(count)])  29.2 us
    pallas_call x2, Pallas kernels, project(): pl.pallas_call(functools.partial(project_kernel, rows, first_col), out_sh...  20 us
    pallas_call x1, Pallas kernels, attend_head(): pl.pallas_call(attend_kernel, grid=(count,), out_shape=(out, out), in_spe...  16.7 us
    ppermute x1, waiting for transfers between devices, per_device_one_head(): out_passed_next = lax.ppermute(out_across_next, 'ctx', outward)  13.2 us
    ppermute x1, waiting for transfers between devices, per_device_one_head(): across_next = lax.ppermute(near, 'ctx', middle)  9.3 us
    ppermute x1, waiting for transfers between devices, per_device_one_head(): out_across_next = lax.ppermute(out_near, 'ctx', middle)  8.55 us
  transfers between devices with their start and end apart: 39, of which 22 were waited for; matrix products, arithmetic and copies ran while one was open for 8% of the time, Pallas kernels for 13%

profile of v13, /device:TPU:17, one launch (start us, length us, event | category | flops | bytes accessed | tf_op | source)
XLA Modules:
  0.0 280.8 jit_solution(11876308710066580260)
XLA Ops:
  0.8 2.0 pad_maximum_fusion.7
  2.8 1.3 collective-permute-start
  4.1 1.9 collective-permute-start.1
  6.0 1.3 collective-permute-start.2
  7.3 1.2 collective-permute-start.3
  9.3 0.9 fusion.19
  10.2 0.9 fusion.18
  11.8 1.3 fusion.17.weights
  13.1 1.4 maximum_bitcast_fusion
  14.5 1.9 pad_maximum_fusion
  16.4 2.5 collective-permute-done.2.refs_4_
  18.9 0.9 collective-permute-done.3.refs_9_
  21.1 1.2 collective-permute-start.7
  22.3 3.0 %collective-permute-start.4 = (bf16[272,1024]{1,0:T(8,128)(2,1)S(1)}, bf16[272,1024]{1,0:T(8,128)(2,1)S(1)}, u32[]{:S(2)}, u32[]{:S(2)}) collective-permute-start(bf16[272,1024]{1,0:T(8,128)(2,1)S(1)} %collective-permute-done.refs_1_), channel_id=1, source_target_pairs={{8,16},{12,20},{16,8},{20,12},{9,17},{13,21},{17,9},{21,13},{10,18... | collective-permute-start | bytes 1671176 | tf_op jit(solution)/shard_map/ppermute | solution.py:610
  25.4 1.3 collective-permute-start.5
  26.7 9.3 %collective-permute-done.4 = bf16[272,1024]{1,0:T(8,128)(2,1)S(1)} collective-permute-done((bf16[272,1024]{1,0:T(8,128)(2,1)S(1)}, bf16[272,1024]{1,0:T(8,128)(2,1)S(1)}, u32[]{:S(2)}, u32[]{:S(2)}) %collective-permute-start.4) | collective-permute-done | bytes 557088 | tf_op jit(solution)/shard_map/ppermute | solution.py:610
  36.2 1.5 collective-permute-done.6.refs_5_
  38.1 5.2 %all-to-all-start = ((bf16[4,512,768]{2,1,0:T(8,128)(2,1)}), bf16[4,512,768]{2,1,0:T(8,128)(2,1)S(1)}, u32[]{:S(2)}, u32[]{:S(2)}) async-start(bf16[4,512,768]{2,1,0:T(8,128)(2,1)} %pad_maximum_fusion), calls=%async_computation | async-start | bytes 6291456 | tf_op jit(solution)/shard_map/all_to_all | solution.py:614
  43.2 1.4 add.86.refs_2_
  44.7 1.1 slice.63
  45.9 1.0 slice.62
  47.1 0.9 collective-permute-start.9
  48.2 3.1 %collective-permute-start.8 = (bf16[272,1024]{1,0:T(8,128)(2,1)S(1)}, bf16[272,1024]{1,0:T(8,128)(2,1)S(1)}, u32[]{:S(2)}, u32[]{:S(2)}) collective-permute-start(bf16[272,1024]{1,0:T(8,128)(2,1)S(1)} %copy-done.21), channel_id=1, source_target_pairs={{8,0},{12,4},{16,24},{20,28},{9,1},{13,5},{17,25},{21,29},{10,2},{... | collective-permute-start | bytes 1671176 | tf_op jit(solution)/shard_map/ppermute | solution.py:616
  52.1 35.5 %collective-permute-done.8 = bf16[272,1024]{1,0:T(8,128)(2,1)S(1)} collective-permute-done((bf16[272,1024]{1,0:T(8,128)(2,1)S(1)}, bf16[272,1024]{1,0:T(8,128)(2,1)S(1)}, u32[]{:S(2)}, u32[]{:S(2)}) %collective-permute-start.8) | collective-permute-done | bytes 557088 | tf_op jit(solution)/shard_map/ppermute | solution.py:616
  89.9 1.9 fusion.3
  91.8 1.0 pad_maximum_fusion.8.refs_16_
  92.8 1.0 pad_maximum_fusion.9.refs_17_
  93.8 10.1 %collective-permute-done.11.refs_7_ = bf16[384,1024]{1,0:T(8,128)(2,1)S(1)} collective-permute-done((bf16[384,1024]{1,0:T(8,128)(2,1)S(1)}, bf16[384,1024]{1,0:T(8,128)(2,1)S(1)}, u32[]{:S(2)}, u32[]{:S(2)}) %collective-permute-start.11) | collective-permute-done | bytes 786464 | tf_op jit(solution)/shard_map/ppermute | solution.py:567
  104.2 1.0 collective-permute-start.13
  105.4 5.7 %collective-permute-done.13.refs_8_ = bf16[128,1024]{1,0:T(8,128)(2,1)S(1)} collective-permute-done((bf16[128,1024]{1,0:T(8,128)(2,1)S(1)}, bf16[128,1024]{1,0:T(8,128)(2,1)S(1)}, u32[]{:S(2)}, u32[]{:S(2)}) %collective-permute-start.13) | collective-permute-done | bytes 262176 | tf_op jit(solution)/shard_map/ppermute | solution.py:567
  111.9 7.1 %collective-permute-start.15 = (bf16[4,512,768]{2,1,0:T(8,128)(2,1)S(1)}, bf16[4,512,768]{2,1,0:T(8,128)(2,1)S(1)}, u32[]{:S(2)}, u32[]{:S(2)}) collective-permute-start(bf16[4,512,768]{2,1,0:T(8,128)(2,1)S(1)} %all-to-all-done.refs_14_), channel_id=1, source_target_pairs={{0,4},{4,0},{8,12},{12,8},{16,20},{20,16},{24,28},{28,24},{1,5},{5... | collective-permute-start | bytes 9437192 | tf_op jit(solution)/shard_map/ppermute | solution.py:567
  119.0 2.2 collective-permute-start.16
  121.2 1.9 collective-permute-start.17
  123.1 1.2 collective-permute-done.15.refs_15_
  124.3 1.7 copy-done.4
  126.0 9.4 %shard_map.91.refs_2_ = bf16[4,256,256]{2,1,0:T(8,128)(2,1)} custom-call(s32[9]{0:T(128)} %stack.78.place, bf16[256,1024]{1,0:T(8,128)(2,1)} %refs_0_.3, bf16[272,1024]{1,0:T(8,128)(2,1)} %copy-done.5, bf16[272,1024]{1,0:T(8,128)(2,1)} %copy-done.2, bf16[272,1024]{1,0:T(8,128)(2,1)} %copy-done.3, bf16[256,1024]{1,0:T(8,128)(2,1)} %copy-done.10, ...), custom_call_target="tpu_custom_call" | custom-call | flops 2147483648 | bytes 16777216 | tf_op jit(solution)/shard_map/pallas_call | solution.py:261
  135.4 9.6 %collective-permute-done.16.refs_2_ = bf16[1024,512]{1,0:T(8,128)(2,1)} collective-permute-done((bf16[1024,512]{1,0:T(8,128)(2,1)}, bf16[1024,512]{1,0:T(8,128)(2,1)}, u32[]{:S(2)}, u32[]{:S(2)}) %collective-permute-start.16) | collective-permute-done | bytes 1048608 | tf_op jit(solution)/shard_map/ppermute | solution.py:567
  145.0 2.8 %collective-permute-done.17.refs_4_ = bf16[1024,512]{1,0:T(8,128)(2,1)} collective-permute-done((bf16[1024,512]{1,0:T(8,128)(2,1)}, bf16[1024,512]{1,0:T(8,128)(2,1)}, u32[]{:S(2)}, u32[]{:S(2)}) %collective-permute-start.17) | collective-permute-done | bytes 1048608 | tf_op jit(solution)/shard_map/ppermute | solution.py:636
  147.8 1.2 collective-permute-start.19
  149.1 1.9 collective-permute-start.22
  151.0 10.6 %shard_map.92 = (bf16[4,256,256]{2,1,0:T(8,128)(2,1)}, bf16[4,256,256]{2,1,0:T(8,128)(2,1)}) custom-call(s32[9]{0:T(128)} %stack.78.place, bf16[256,1024]{1,0:T(8,128)(2,1)} %refs_0_.3, bf16[272,1024]{1,0:T(8,128)(2,1)} %copy-done.5, bf16[272,1024]{1,0:T(8,128)(2,1)} %copy-done.2, bf16[272,1024]{1,0:T(8,128)(2,1)} %copy-done.3, ...), custom_call_target="tpu_custom_call" | custom-call | flops 4294967296 | bytes 16777216 | tf_op jit(solution)/shard_map/pallas_call | solution.py:261
  161.6 0.8 collective-permute-start.20
  162.9 4.1 %collective-permute-start.24 = (bf16[1024,512]{1,0:T(8,128)(2,1)}, bf16[1024,512]{1,0:T(8,128)(2,1)}, u32[]{:S(2)}, u32[]{:S(2)}) collective-permute-start(bf16[1024,512]{1,0:T(8,128)(2,1)} %collective-permute-done.17.refs_4_), channel_id=1, source_target_pairs={{8,0},{12,4},{16,24},{20,28},{9,1},{13,5},{17,25},{21,29},{10,2},{... | collective-permute-start | bytes 3145736 | tf_op jit(solution)/shard_map/ppermute | solution.py:646
  167.0 8.6 %collective-permute-done.22.refs_8_ = bf16[1024,512]{1,0:T(8,128)(2,1)} collective-permute-done((bf16[1024,512]{1,0:T(8,128)(2,1)}, bf16[1024,512]{1,0:T(8,128)(2,1)}, u32[]{:S(2)}, u32[]{:S(2)}) %collective-permute-start.22) | collective-permute-done | bytes 1048608 | tf_op jit(solution)/shard_map/ppermute | solution.py:645
  175.6 1.3 collective-permute-start.27
  178.4 2.3 collective-permute-start.25
  181.4 16.7 %shard_map.93 = (bf16[4,256,512]{2,1,0:T(8,128)(2,1)}, bf16[4,256,512]{2,1,0:T(8,128)(2,1)}) custom-call(s32[9]{0:T(128)} %stack.78.place, f32[4]{0:T(128)} %dynamic-slice_bitcast_fusion.1.mix, f32[66]{0:T(128)} %fusion.17.weights, bf16[4,256,256]{2,1,0:T(8,128)(2,1)} %get-tuple-element.83.refs_0_, bf16[4,256,256]{2,1,0:T(8,128)(2,1)} %copy-done.28, ...), custom_call_target="tpu_custom_call" | custom-call | flops 5368709120 | bytes 16777216 | tf_op jit(solution)/shard_map/pallas_call | solution.py:471
  198.1 13.2 %collective-permute-done.25.refs_10_ = bf16[1024,512]{1,0:T(8,128)(2,1)} collective-permute-done((bf16[1024,512]{1,0:T(8,128)(2,1)}, bf16[1024,512]{1,0:T(8,128)(2,1)}, u32[]{:S(2)}, u32[]{:S(2)}) %collective-permute-start.25) | collective-permute-done | bytes 1048608 | tf_op jit(solution)/shard_map/ppermute | solution.py:655
  211.3 0.8 collective-permute-start.28
  212.7 3.6 %collective-permute-done.28 = bf16[4,256,512]{2,1,0:T(8,128)(2,1)} collective-permute-done((bf16[4,256,512]{2,1,0:T(8,128)(2,1)}, bf16[4,256,512]{2,1,0:T(8,128)(2,1)}, u32[]{:S(2)}, u32[]{:S(2)}) %collective-permute-start.28) | collective-permute-done | bytes 1048608 | tf_op jit(solution)/shard_map/ppermute | solution.py:567
  216.3 1.9 convert_add_fusion
  218.1 1.0 fusion.2
  219.1 2.2 collective-permute-start.29
  221.3 1.2 collective-permute-start.31
  223.2 0.8 dynamic-slice_bitcast_fusion.own
  224.0 7.2 %collective-permute-done.29.r1 = bf16[256,512]{1,0:T(8,128)(2,1)S(1)} collective-permute-done((bf16[256,512]{1,0:T(8,128)(2,1)}, bf16[256,512]{1,0:T(8,128)(2,1)S(1)}, u32[]{:S(2)}, u32[]{:S(2)}) %collective-permute-start.29) | collective-permute-done | bytes 262176 | tf_op jit(solution)/shard_map/ppermute | solution.py:567
  231.2 2.2 collective-permute-done.30.r2
  233.4 12.4 %collective-permute-done.31.r3 = bf16[256,512]{1,0:T(8,128)(2,1)} collective-permute-done((bf16[256,512]{1,0:T(8,128)(2,1)}, bf16[256,512]{1,0:T(8,128)(2,1)}, u32[]{:S(2)}, u32[]{:S(2)}) %collective-permute-start.31) | collective-permute-done | bytes 262176 | tf_op jit(solution)/shard_map/ppermute | solution.py:567
  245.8 7.9 %shard_map.94 = (bf16[256,1024]{1,0:T(8,128)(2,1)}, bf16[256,1024]{1,0:T(8,128)(2,1)}, bf16[256,1024]{1,0:T(8,128)(2,1)}, bf16[256,1024]{1,0:T(8,128)(2,1)}) custom-call(s32[10]{0:T(128)} %pad_add_fusion.place, f32[256,512]{1,0:T(8,128)} %dynamic-slice_bitcast_fusion.own, bf16[256,512]{1,0:T(8,128)(2,1)} %copy-done.24, ...), custom_call_target="tpu_custom_call" | custom-call | flops 2147483648 | bytes 11534336 | tf_op jit(solution)/shard_map/pallas_call | solution.py:548
  254.0 1.4 collective-permute-start.36
  255.4 1.0 collective-permute-start.35
  256.5 10.8 %collective-permute-done.37 = bf16[256,1024]{1,0:T(8,128)(2,1)S(1)} collective-permute-done((bf16[256,1024]{1,0:T(8,128)(2,1)}, bf16[256,1024]{1,0:T(8,128)(2,1)S(1)}, u32[]{:S(2)}, u32[]{:S(2)}) %collective-permute-start.37) | collective-permute-done | bytes 524320 | tf_op jit(solution)/shard_map/ppermute | solution.py:567
  267.2 11.4 %collective-permute-done.36 = bf16[256,1024]{1,0:T(8,128)(2,1)S(1)} collective-permute-done((bf16[256,1024]{1,0:T(8,128)(2,1)}, bf16[256,1024]{1,0:T(8,128)(2,1)S(1)}, u32[]{:S(2)}, u32[]{:S(2)}) %collective-permute-start.36) | collective-permute-done | bytes 524320 | tf_op jit(solution)/shard_map/ppermute | solution.py:567
  278.6 2.2 add_convert_fusion
  (122 shorter events, 13.1 us)
Async XLA Ops:
  0.0 180.7 %copy-start = (f32[8,4]{0,1:T(4,128)S(1)}, f32[8,4]{0,1:T(4,128)}, u32[]{:S(2)}) copy-start(f32[8,4]{0,1:T(4,128)} %param.15) | copy-start | bytes 388
  0.0 8.5 %copy-start.17 = (bf16[512,1024]{1,0:T(8,128)(2,1)S(1)}, bf16[512,1024]{1,0:T(8,128)(2,1)}, u32[]{:S(2)}) copy-start(bf16[512,1024]{1,0:T(8,128)(2,1)} %param.13) | copy-start | bytes 3145732
  0.8 8.5 %copy-start.18 = (bf16[512,1024]{1,0:T(8,128)(2,1)S(1)}, bf16[512,1024]{1,0:T(8,128)(2,1)}, u32[]{:S(2)}) copy-start(bf16[512,1024]{1,0:T(8,128)(2,1)} %param.12) | copy-start | bytes 3145732
  2.8 7.4 %copy-start.19 = (bf16[512,1024]{1,0:T(8,128)(2,1)S(1)}, bf16[512,1024]{1,0:T(8,128)(2,1)}, u32[]{:S(2)}) copy-start(bf16[512,1024]{1,0:T(8,128)(2,1)} %param.11) | copy-start | bytes 3145732
  2.8 17.0 %collective-permute-start = (bf16[272,1024]{1,0:T(8,128)(2,1)}, bf16[272,1024]{1,0:T(8,128)(2,1)S(1)}, u32[]{:S(2)}, u32[]{:S(2)}) collective-permute-start(bf16[272,1024]{1,0:T(8,128)(2,1)} %pad_maximum_fusion.7), channel_id=1, source_target_pairs={{0,8},{4,12},{8,0},{12,4},{16,24},{20,28},{24,16},{28,20},{1,9},{5... | collective-permute-start | bytes 1671176 | tf_op jit(solution)/shard_map/ppermute | solution.py:567
  4.1 15.7 %collective-permute-start.1 = (bf16[272,1024]{1,0:T(8,128)(2,1)}, bf16[272,1024]{1,0:T(8,128)(2,1)}, u32[]{:S(2)}, u32[]{:S(2)}) collective-permute-start(bf16[272,1024]{1,0:T(8,128)(2,1)} %pad_maximum_fusion.7), channel_id=1, source_target_pairs={{8,16},{12,20},{16,8},{20,12},{9,17},{13,21},{17,9},{21,13},{10,18... | collective-permute-start | bytes 1671176 | tf_op jit(solution)/shard_map/ppermute | solution.py:600
  6.0 12.9 %collective-permute-start.2 = (bf16[256,1024]{1,0:T(8,128)(2,1)}, bf16[256,1024]{1,0:T(8,128)(2,1)S(1)}, u32[]{:S(2)}, u32[]{:S(2)}) collective-permute-start(bf16[256,1024]{1,0:T(8,128)(2,1)} %refs_0_.3), channel_id=1, source_target_pairs={{0,1},{1,0},{2,3},{3,2},{4,5},{5,4},{6,7},{7,6},{8,9},{9,8},{10,11... | collective-permute-start | bytes 1572872 | tf_op jit(solution)/shard_map/ppermute | solution.py:567
  7.3 12.5 %collective-permute-start.3 = (bf16[256,1024]{1,0:T(8,128)(2,1)}, bf16[256,1024]{1,0:T(8,128)(2,1)S(1)}, u32[]{:S(2)}, u32[]{:S(2)}) collective-permute-start(bf16[256,1024]{1,0:T(8,128)(2,1)} %refs_0_.3), channel_id=1, source_target_pairs={{0,2},{1,3},{2,0},{3,1},{4,6},{5,7},{6,4},{7,5},{8,10},{9,11},{10,... | collective-permute-start | bytes 1572872 | tf_op jit(solution)/shard_map/ppermute | solution.py:567
  18.9 1.2 copy-start.10
  19.8 2.5 copy-start.5
  20.6 17.1 %collective-permute-start.6 = (bf16[384,1024]{1,0:T(8,128)(2,1)S(1)}, bf16[384,1024]{1,0:T(8,128)(2,1)}, u32[]{:S(2)}, u32[]{:S(2)}) collective-permute-start(bf16[384,1024]{1,0:T(8,128)(2,1)S(1)} %get-tuple-element.125), channel_id=1, source_target_pairs={{0,1},{1,0},{2,3},{3,2},{4,5},{5,4},{6,7},{7,6},{8,9},{9,8},{10,11... | collective-permute-start | bytes 2359304 | tf_op jit(solution)/shard_map/ppermute | solution.py:567
  21.1 17.0 %collective-permute-start.7 = (bf16[384,1024]{1,0:T(8,128)(2,1)S(1)}, bf16[384,1024]{1,0:T(8,128)(2,1)}, u32[]{:S(2)}, u32[]{:S(2)}) collective-permute-start(bf16[384,1024]{1,0:T(8,128)(2,1)S(1)} %get-tuple-element.124), channel_id=1, source_target_pairs={{0,2},{1,3},{2,0},{3,1},{4,6},{5,7},{6,4},{7,5},{8,10},{9,11},{10,... | collective-permute-start | bytes 2359304 | tf_op jit(solution)/shard_map/ppermute | solution.py:567
  22.3 13.7 %collective-permute-start.4 = (bf16[272,1024]{1,0:T(8,128)(2,1)S(1)}, bf16[272,1024]{1,0:T(8,128)(2,1)S(1)}, u32[]{:S(2)}, u32[]{:S(2)}) collective-permute-start(bf16[272,1024]{1,0:T(8,128)(2,1)S(1)} %collective-permute-done.refs_1_), channel_id=1, source_target_pairs={{8,16},{12,20},{16,8},{20,12},{9,17},{13,21},{17,9},{21,13},{10,18... | collective-permute-start | bytes 1671176 | tf_op jit(solution)/shard_map/ppermute | solution.py:610
  25.4 10.8 %collective-permute-start.5 = (bf16[272,1024]{1,0:T(8,128)(2,1)}, bf16[272,1024]{1,0:T(8,128)(2,1)S(1)}, u32[]{:S(2)}, u32[]{:S(2)}) collective-permute-start(bf16[272,1024]{1,0:T(8,128)(2,1)} %collective-permute-done.1), channel_id=1, source_target_pairs={{8,0},{12,4},{16,24},{20,28},{9,1},{13,5},{17,25},{21,29},{10,2},{... | collective-permute-start | bytes 1671176 | tf_op jit(solution)/shard_map/ppermute | solution.py:611
  36.0 1.7 copy-start.20
  36.2 1.5 copy-start.22
  38.1 73.9 %all-to-all-start = ((bf16[4,512,768]{2,1,0:T(8,128)(2,1)}), bf16[4,512,768]{2,1,0:T(8,128)(2,1)S(1)}, u32[]{:S(2)}, u32[]{:S(2)}) async-start(bf16[4,512,768]{2,1,0:T(8,128)(2,1)} %pad_maximum_fusion), calls=%async_computation | async-start | bytes 6291456 | tf_op jit(solution)/shard_map/all_to_all | solution.py:614
  44.7 7.4 %copy-start.2 = (bf16[272,1024]{1,0:T(8,128)(2,1)}, bf16[272,1024]{1,0:T(8,128)(2,1)S(1)}, u32[]{:S(2)}) copy-start(bf16[272,1024]{1,0:T(8,128)(2,1)S(1)} %add.86.refs_2_) | copy-start | bytes 1671172
  45.8 2.3 copy-start.21
  47.1 40.5 %collective-permute-start.9 = (bf16[384,1024]{1,0:T(8,128)(2,1)S(1)}, bf16[384,1024]{1,0:T(8,128)(2,1)S(1)}, u32[]{:S(2)}, u32[]{:S(2)}) collective-permute-start(bf16[384,1024]{1,0:T(8,128)(2,1)S(1)} %get-tuple-element.123), channel_id=1, source_target_pairs={{0,1},{1,0},{2,3},{3,2},{4,5},{5,4},{6,7},{7,6},{8,9},{9,8},{10,11... | collective-permute-start | bytes 2359304 | tf_op jit(solution)/shard_map/ppermute | solution.py:567
  48.0 39.7 %collective-permute-start.10 = (bf16[384,1024]{1,0:T(8,128)(2,1)S(1)}, bf16[384,1024]{1,0:T(8,128)(2,1)S(1)}, u32[]{:S(2)}, u32[]{:S(2)}) collective-permute-start(bf16[384,1024]{1,0:T(8,128)(2,1)S(1)} %get-tuple-element.122), channel_id=1, source_target_pairs={{0,2},{1,3},{2,0},{3,1},{4,6},{5,7},{6,4},{7,5},{8,10},{9,11},{10,... | collective-permute-start | bytes 2359304 | tf_op jit(solution)/shard_map/ppermute | solution.py:567
  48.2 39.4 %collective-permute-start.8 = (bf16[272,1024]{1,0:T(8,128)(2,1)S(1)}, bf16[272,1024]{1,0:T(8,128)(2,1)S(1)}, u32[]{:S(2)}, u32[]{:S(2)}) collective-permute-start(bf16[272,1024]{1,0:T(8,128)(2,1)S(1)} %copy-done.21), channel_id=1, source_target_pairs={{8,0},{12,4},{16,24},{20,28},{9,1},{13,5},{17,25},{21,29},{10,2},{... | collective-permute-start | bytes 1671176 | tf_op jit(solution)/shard_map/ppermute | solution.py:616
  87.8 2.0 copy-start.3
  89.0 14.9 %collective-permute-start.11 = (bf16[384,1024]{1,0:T(8,128)(2,1)S(1)}, bf16[384,1024]{1,0:T(8,128)(2,1)S(1)}, u32[]{:S(2)}, u32[]{:S(2)}) collective-permute-start(bf16[384,1024]{1,0:T(8,128)(2,1)S(1)} %get-tuple-element.121), channel_id=1, source_target_pairs={{0,1},{1,0},{2,3},{3,2},{4,5},{5,4},{6,7},{7,6},{8,9},{9,8},{10,11... | collective-permute-start | bytes 2359304 | tf_op jit(solution)/shard_map/ppermute | solution.py:567
  89.8 14.4 %collective-permute-start.12 = (bf16[384,1024]{1,0:T(8,128)(2,1)S(1)}, bf16[384,1024]{1,0:T(8,128)(2,1)S(1)}, u32[]{:S(2)}, u32[]{:S(2)}) collective-permute-start(bf16[384,1024]{1,0:T(8,128)(2,1)S(1)} %get-tuple-element.120), channel_id=1, source_target_pairs={{0,2},{1,3},{2,0},{3,1},{4,6},{5,7},{6,4},{7,5},{8,10},{9,11},{10,... | collective-permute-start | bytes 2359304 | tf_op jit(solution)/shard_map/ppermute | solution.py:567
  103.9 7.2 %copy-start.8 = (bf16[384,1024]{1,0:T(8,128)(2,1)}, bf16[384,1024]{1,0:T(8,128)(2,1)S(1)}, u32[]{:S(2)}) copy-start(bf16[384,1024]{1,0:T(8,128)(2,1)S(1)} %collective-permute-done.11.refs_7_) | copy-start | bytes 2359300
  104.2 7.0 %copy-start.9 = (bf16[384,1024]{1,0:T(8,128)(2,1)}, bf16[384,1024]{1,0:T(8,128)(2,1)S(1)}, u32[]{:S(2)}) copy-start(bf16[384,1024]{1,0:T(8,128)(2,1)S(1)} %collective-permute-done.12.refs_12_) | copy-start | bytes 2359300
  104.2 7.0 %collective-permute-start.13 = (bf16[128,1024]{1,0:T(8,128)(2,1)S(1)}, bf16[128,1024]{1,0:T(8,128)(2,1)S(1)}, u32[]{:S(2)}, u32[]{:S(2)}) collective-permute-start(bf16[128,1024]{1,0:T(8,128)(2,1)S(1)} %slice.73), channel_id=1, source_target_pairs={{0,1},{1,0},{2,3},{3,2},{4,5},{5,4},{6,7},{7,6},{8,9},{9,8},{10,11... | collective-permute-start | bytes 786440 | tf_op jit(solution)/shard_map/ppermute | solution.py:567
  105.2 6.7 %collective-permute-start.14 = (bf16[128,1024]{1,0:T(8,128)(2,1)S(1)}, bf16[128,1024]{1,0:T(8,128)(2,1)}, u32[]{:S(2)}, u32[]{:S(2)}) collective-permute-start(bf16[128,1024]{1,0:T(8,128)(2,1)S(1)} %slice.74), channel_id=1, source_target_pairs={{0,2},{1,3},{2,0},{3,1},{4,6},{5,7},{6,4},{7,5},{8,10},{9,11},{10,... | collective-permute-start | bytes 786440 | tf_op jit(solution)/shard_map/ppermute | solution.py:567
  111.1 13.1 %copy-start.23 = (bf16[128,1024]{1,0:T(8,128)(2,1)}, bf16[128,1024]{1,0:T(8,128)(2,1)S(1)}, u32[]{:S(2)}) copy-start(bf16[128,1024]{1,0:T(8,128)(2,1)S(1)} %collective-permute-done.13.refs_8_) | copy-start | bytes 786436
  111.9 12.3 %copy-start.1 = (bf16[4,512,768]{2,1,0:T(8,128)(2,1)}, bf16[4,512,768]{2,1,0:T(8,128)(2,1)S(1)}, u32[]{:S(2)}) copy-start(bf16[4,512,768]{2,1,0:T(8,128)(2,1)S(1)} %all-to-all-done.refs_14_) | copy-start | bytes 9437188
  111.9 37.1 %copy-start.12 = (bf16[1024,512]{1,0:T(8,128)(2,1)S(1)}, bf16[1024,512]{1,0:T(8,128)(2,1)}, u32[]{:S(2)}) copy-start(bf16[1024,512]{1,0:T(8,128)(2,1)} %refs_0_.4) | copy-start | bytes 3145732
  111.9 12.3 %collective-permute-start.15 = (bf16[4,512,768]{2,1,0:T(8,128)(2,1)S(1)}, bf16[4,512,768]{2,1,0:T(8,128)(2,1)S(1)}, u32[]{:S(2)}, u32[]{:S(2)}) collective-permute-start(bf16[4,512,768]{2,1,0:T(8,128)(2,1)S(1)} %all-to-all-done.refs_14_), channel_id=1, source_target_pairs={{0,4},{4,0},{8,12},{12,8},{16,20},{20,16},{24,28},{28,24},{1,5},{5... | collective-permute-start | bytes 9437192 | tf_op jit(solution)/shard_map/ppermute | solution.py:567
  119.0 26.0 %collective-permute-start.16 = (bf16[1024,512]{1,0:T(8,128)(2,1)}, bf16[1024,512]{1,0:T(8,128)(2,1)}, u32[]{:S(2)}, u32[]{:S(2)}) collective-permute-start(bf16[1024,512]{1,0:T(8,128)(2,1)} %refs_0_.4), channel_id=1, source_target_pairs={{0,8},{4,12},{8,0},{12,4},{16,24},{20,28},{24,16},{28,20},{1,9},{5... | collective-permute-start | bytes 3145736 | tf_op jit(solution)/shard_map/ppermute | solution.py:567
  121.2 26.6 %collective-permute-start.17 = (bf16[1024,512]{1,0:T(8,128)(2,1)}, bf16[1024,512]{1,0:T(8,128)(2,1)}, u32[]{:S(2)}, u32[]{:S(2)}) collective-permute-start(bf16[1024,512]{1,0:T(8,128)(2,1)} %refs_0_.4), channel_id=1, source_target_pairs={{8,16},{12,20},{16,8},{20,12},{9,17},{13,21},{17,9},{21,13},{10,18... | collective-permute-start | bytes 3145736 | tf_op jit(solution)/shard_map/ppermute | solution.py:636
  124.3 1.7 copy-start.4
  147.8 13.8 %collective-permute-start.18 = (bf16[4,256,256]{2,1,0:T(8,128)(2,1)}, bf16[4,256,256]{2,1,0:T(8,128)(2,1)S(1)}, u32[]{:S(2)}, u32[]{:S(2)}) collective-permute-start(bf16[4,256,256]{2,1,0:T(8,128)(2,1)} %shard_map.91.refs_2_), channel_id=1, source_target_pairs={{0,8},{4,12},{8,0},{12,4},{16,24},{20,28},{24,16},{28,20},{1,9},{5... | collective-permute-start | bytes 1572872 | tf_op jit(solution)/shard_map/ppermute | solution.py:567
  147.8 13.8 %collective-permute-start.19 = (bf16[4,256,256]{2,1,0:T(8,128)(2,1)}, bf16[4,256,256]{2,1,0:T(8,128)(2,1)S(1)}, u32[]{:S(2)}, u32[]{:S(2)}) collective-permute-start(bf16[4,256,256]{2,1,0:T(8,128)(2,1)} %shard_map.91.refs_2_), channel_id=1, source_target_pairs={{0,4},{4,0},{8,12},{12,8},{16,20},{20,16},{24,28},{28,24},{1,5},{5... | collective-permute-start | bytes 1572872 | tf_op jit(solution)/shard_map/ppermute | solution.py:567
  149.0 14.0 %collective-permute-start.23 = (bf16[1024,512]{1,0:T(8,128)(2,1)S(1)}, bf16[1024,512]{1,0:T(8,128)(2,1)S(1)}, u32[]{:S(2)}, u32[]{:S(2)}) collective-permute-start(bf16[1024,512]{1,0:T(8,128)(2,1)S(1)} %copy-done.12), channel_id=1, source_target_pairs={{0,4},{4,0},{8,12},{12,8},{16,20},{20,16},{24,28},{28,24},{1,5},{5... | collective-permute-start | bytes 3145736 | tf_op jit(solution)/shard_map/ppermute | solution.py:567
  149.1 26.5 %collective-permute-start.22 = (bf16[1024,512]{1,0:T(8,128)(2,1)}, bf16[1024,512]{1,0:T(8,128)(2,1)}, u32[]{:S(2)}, u32[]{:S(2)}) collective-permute-start(bf16[1024,512]{1,0:T(8,128)(2,1)} %collective-permute-done.16.refs_2_), channel_id=1, source_target_pairs={{8,16},{12,20},{16,8},{20,12},{9,17},{13,21},{17,9},{21,13},{10,18... | collective-permute-start | bytes 3145736 | tf_op jit(solution)/shard_map/ppermute | solution.py:645
  161.6 5.4 %copy-start.26 = (bf16[4,256,256]{2,1,0:T(8,128)(2,1)}, bf16[4,256,256]{2,1,0:T(8,128)(2,1)S(1)}, u32[]{:S(2)}) copy-start(bf16[4,256,256]{2,1,0:T(8,128)(2,1)S(1)} %collective-permute-done.18.refs_3_) | copy-start | bytes 1572868
  161.6 15.2 %copy-start.27 = (bf16[4,256,256]{2,1,0:T(8,128)(2,1)}, bf16[4,256,256]{2,1,0:T(8,128)(2,1)S(1)}, u32[]{:S(2)}) copy-start(bf16[4,256,256]{2,1,0:T(8,128)(2,1)S(1)} %collective-permute-done.19.refs_4_) | copy-start | bytes 1572868
  161.6 15.2 %collective-permute-start.20 = (bf16[4,256,256]{2,1,0:T(8,128)(2,1)}, bf16[4,256,256]{2,1,0:T(8,128)(2,1)S(1)}, u32[]{:S(2)}, u32[]{:S(2)}) collective-permute-start(bf16[4,256,256]{2,1,0:T(8,128)(2,1)} %get-tuple-element.84), channel_id=1, source_target_pairs={{0,4},{4,0},{8,12},{12,8},{16,20},{20,16},{24,28},{28,24},{1,5},{5... | collective-permute-start | bytes 1572872 | tf_op jit(solution)/shard_map/ppermute | solution.py:567
  162.4 14.4 %collective-permute-start.21 = (bf16[4,256,256]{2,1,0:T(8,128)(2,1)S(1)}, bf16[4,256,256]{2,1,0:T(8,128)(2,1)S(1)}, u32[]{:S(2)}, u32[]{:S(2)}) collective-permute-start(bf16[4,256,256]{2,1,0:T(8,128)(2,1)S(1)} %collective-permute-done.18.refs_3_), channel_id=1, source_target_pairs={{0,4},{4,0},{8,12},{12,8},{16,20},{20,16},{24,28},{28,24},{1,5},{5... | collective-permute-start | bytes 1572872 | tf_op jit(solution)/shard_map/ppermute | solution.py:567
  162.5 35.5 %collective-permute-start.26 = (bf16[1024,512]{1,0:T(8,128)(2,1)}, bf16[1024,512]{1,0:T(8,128)(2,1)S(1)}, u32[]{:S(2)}, u32[]{:S(2)}) collective-permute-start(bf16[1024,512]{1,0:T(8,128)(2,1)} %collective-permute-done.16.refs_2_), channel_id=1, source_target_pairs={{0,4},{4,0},{8,12},{12,8},{16,20},{20,16},{24,28},{28,24},{1,5},{5... | collective-permute-start | bytes 3145736 | tf_op jit(solution)/shard_map/ppermute | solution.py:567
  162.9 35.1 %copy-start.13 = (bf16[1024,512]{1,0:T(8,128)(2,1)}, bf16[1024,512]{1,0:T(8,128)(2,1)S(1)}, u32[]{:S(2)}) copy-start(bf16[1024,512]{1,0:T(8,128)(2,1)S(1)} %collective-permute-done.23.refs_1_) | copy-start | bytes 3145732
  162.9 35.1 %collective-permute-start.24 = (bf16[1024,512]{1,0:T(8,128)(2,1)}, bf16[1024,512]{1,0:T(8,128)(2,1)}, u32[]{:S(2)}, u32[]{:S(2)}) collective-permute-start(bf16[1024,512]{1,0:T(8,128)(2,1)} %collective-permute-done.17.refs_4_), channel_id=1, source_target_pairs={{8,0},{12,4},{16,24},{20,28},{9,1},{13,5},{17,25},{21,29},{10,2},{... | collective-permute-start | bytes 3145736 | tf_op jit(solution)/shard_map/ppermute | solution.py:646
  175.6 22.5 %collective-permute-start.27 = (bf16[1024,512]{1,0:T(8,128)(2,1)}, bf16[1024,512]{1,0:T(8,128)(2,1)S(1)}, u32[]{:S(2)}, u32[]{:S(2)}) collective-permute-start(bf16[1024,512]{1,0:T(8,128)(2,1)} %collective-permute-done.17.refs_4_), channel_id=1, source_target_pairs={{0,4},{4,0},{8,12},{12,8},{16,20},{20,16},{24,28},{28,24},{1,5},{5... | collective-permute-start | bytes 3145736 | tf_op jit(solution)/shard_map/ppermute | solution.py:567
  178.4 32.9 %collective-permute-start.25 = (bf16[1024,512]{1,0:T(8,128)(2,1)}, bf16[1024,512]{1,0:T(8,128)(2,1)}, u32[]{:S(2)}, u32[]{:S(2)}) collective-permute-start(bf16[1024,512]{1,0:T(8,128)(2,1)} %collective-permute-done.22.refs_8_), channel_id=1, source_target_pairs={{8,0},{12,4},{16,24},{20,28},{9,1},{13,5},{17,25},{21,29},{10,2},{... | collective-permute-start | bytes 3145736 | tf_op jit(solution)/shard_map/ppermute | solution.py:655
  198.1 14.6 %copy-start.14 = (bf16[1024,512]{1,0:T(8,128)(2,1)}, bf16[1024,512]{1,0:T(8,128)(2,1)S(1)}, u32[]{:S(2)}) copy-start(bf16[1024,512]{1,0:T(8,128)(2,1)S(1)} %collective-permute-done.26.refs_3_) | copy-start | bytes 3145732
  198.1 14.6 %copy-start.15 = (bf16[1024,512]{1,0:T(8,128)(2,1)}, bf16[1024,512]{1,0:T(8,128)(2,1)S(1)}, u32[]{:S(2)}) copy-start(bf16[1024,512]{1,0:T(8,128)(2,1)S(1)} %collective-permute-done.27.refs_5_) | copy-start | bytes 3145732
  211.3 4.9 %collective-permute-start.28 = (bf16[4,256,512]{2,1,0:T(8,128)(2,1)}, bf16[4,256,512]{2,1,0:T(8,128)(2,1)}, u32[]{:S(2)}, u32[]{:S(2)}) collective-permute-start(bf16[4,256,512]{2,1,0:T(8,128)(2,1)} %get-tuple-element.95), channel_id=1, source_target_pairs={{0,4},{4,0},{8,12},{12,8},{16,20},{20,16},{24,28},{28,24},{1,5},{5... | collective-permute-start | bytes 3145736 | tf_op jit(solution)/shard_map/ppermute | solution.py:567
  212.2 9.2 %collective-permute-start.33 = (bf16[1024,512]{1,0:T(8,128)(2,1)}, bf16[1024,512]{1,0:T(8,128)(2,1)S(1)}, u32[]{:S(2)}, u32[]{:S(2)}) collective-permute-start(bf16[1024,512]{1,0:T(8,128)(2,1)} %collective-permute-done.22.refs_8_), channel_id=1, source_target_pairs={{0,4},{4,0},{8,12},{12,8},{16,20},{20,16},{24,28},{28,24},{1,5},{5... | collective-permute-start | bytes 3145736 | tf_op jit(solution)/shard_map/ppermute | solution.py:567
  212.2 11.8 %collective-permute-start.32 = (bf16[1024,512]{1,0:T(8,128)(2,1)}, bf16[1024,512]{1,0:T(8,128)(2,1)}, u32[]{:S(2)}, u32[]{:S(2)}) collective-permute-start(bf16[1024,512]{1,0:T(8,128)(2,1)} %collective-permute-done.24.refs_6_), channel_id=1, source_target_pairs={{0,4},{4,0},{8,12},{12,8},{16,20},{20,16},{24,28},{28,24},{1,5},{5... | collective-permute-start | bytes 3145736 | tf_op jit(solution)/shard_map/ppermute | solution.py:567
  212.7 11.3 %collective-permute-start.34 = (bf16[1024,512]{1,0:T(8,128)(2,1)}, bf16[1024,512]{1,0:T(8,128)(2,1)}, u32[]{:S(2)}, u32[]{:S(2)}) collective-permute-start(bf16[1024,512]{1,0:T(8,128)(2,1)} %collective-permute-done.25.refs_10_), channel_id=1, source_target_pairs={{0,4},{4,0},{8,12},{12,8},{16,20},{20,16},{24,28},{28,24},{1,5},{5... | collective-permute-start | bytes 3145736 | tf_op jit(solution)/shard_map/ppermute | solution.py:567
  218.1 4.4 %copy-start.25 = (s32[9]{0:T(128)S(1)}, s32[9]{0:T(128)}, u32[]{:S(2)}) copy-start(s32[9]{0:T(128)} %stack.78.place) | copy-start | bytes 112
  219.1 12.0 %collective-permute-start.29 = (bf16[256,512]{1,0:T(8,128)(2,1)}, bf16[256,512]{1,0:T(8,128)(2,1)S(1)}, u32[]{:S(2)}, u32[]{:S(2)}) collective-permute-start(bf16[256,512]{1,0:T(8,128)(2,1)} %get-tuple-element.107), channel_id=1, source_target_pairs={{0,8},{4,12},{8,0},{12,4},{16,24},{20,28},{24,16},{28,20},{1,9},{5... | collective-permute-start | bytes 786440 | tf_op jit(solution)/shard_map/ppermute | solution.py:567
  221.3 12.1 %collective-permute-start.30 = (bf16[256,512]{1,0:T(8,128)(2,1)}, bf16[256,512]{1,0:T(8,128)(2,1)}, u32[]{:S(2)}, u32[]{:S(2)}) collective-permute-start(bf16[256,512]{1,0:T(8,128)(2,1)} %get-tuple-element.106), channel_id=1, source_target_pairs={{0,16},{4,20},{8,24},{12,28},{16,0},{20,4},{24,8},{28,12},{1,17},{... | collective-permute-start | bytes 786440 | tf_op jit(solution)/shard_map/ppermute | solution.py:567
  221.3 24.5 %copy-start.16 = (bf16[1024,512]{1,0:T(8,128)(2,1)}, bf16[1024,512]{1,0:T(8,128)(2,1)S(1)}, u32[]{:S(2)}) copy-start(bf16[1024,512]{1,0:T(8,128)(2,1)S(1)} %collective-permute-done.33.refs_9_) | copy-start | bytes 3145732
  221.3 24.4 %collective-permute-start.31 = (bf16[256,512]{1,0:T(8,128)(2,1)}, bf16[256,512]{1,0:T(8,128)(2,1)}, u32[]{:S(2)}, u32[]{:S(2)}) collective-permute-start(bf16[256,512]{1,0:T(8,128)(2,1)} %get-tuple-element.105), channel_id=1, source_target_pairs={{0,24},{4,28},{8,16},{12,20},{16,8},{20,12},{24,0},{28,4},{1,25},{... | collective-permute-start | bytes 786440 | tf_op jit(solution)/shard_map/ppermute | solution.py:567
  231.2 14.6 %copy-start.24 = (bf16[256,512]{1,0:T(8,128)(2,1)}, bf16[256,512]{1,0:T(8,128)(2,1)S(1)}, u32[]{:S(2)}) copy-start(bf16[256,512]{1,0:T(8,128)(2,1)S(1)} %collective-permute-done.29.r1) | copy-start | bytes 786436
  253.7 13.5 %collective-permute-start.37 = (bf16[256,1024]{1,0:T(8,128)(2,1)}, bf16[256,1024]{1,0:T(8,128)(2,1)S(1)}, u32[]{:S(2)}, u32[]{:S(2)}) collective-permute-start(bf16[256,1024]{1,0:T(8,128)(2,1)} %get-tuple-element.104), channel_id=1, source_target_pairs={{0,3},{1,2},{2,1},{3,0},{4,7},{5,6},{6,5},{7,4},{8,11},{9,10},{10,... | collective-permute-start | bytes 1572872 | tf_op jit(solution)/shard_map/ppermute | solution.py:567
  254.0 24.6 %collective-permute-start.36 = (bf16[256,1024]{1,0:T(8,128)(2,1)}, bf16[256,1024]{1,0:T(8,128)(2,1)S(1)}, u32[]{:S(2)}, u32[]{:S(2)}) collective-permute-start(bf16[256,1024]{1,0:T(8,128)(2,1)} %get-tuple-element.103), channel_id=1, source_target_pairs={{0,2},{1,3},{2,0},{3,1},{4,6},{5,7},{6,4},{7,5},{8,10},{9,11},{10,... | collective-permute-start | bytes 1572872 | tf_op jit(solution)/shard_map/ppermute | solution.py:567
  255.4 23.2 %collective-permute-start.35 = (bf16[256,1024]{1,0:T(8,128)(2,1)}, bf16[256,1024]{1,0:T(8,128)(2,1)S(1)}, u32[]{:S(2)}, u32[]{:S(2)}) collective-permute-start(bf16[256,1024]{1,0:T(8,128)(2,1)} %get-tuple-element.102), channel_id=1, source_target_pairs={{0,1},{1,0},{2,3},{3,2},{4,5},{5,4},{6,7},{7,6},{8,9},{9,8},{10,11... | collective-permute-start | bytes 1572872 | tf_op jit(solution)/shard_map/ppermute | solution.py:567
  (5 other events, 4.4 us)

commit v14 on v13

--- a/solution.py
+++ b/solution.py
@@ -192,29 +192,30 @@
 
 
 def project_kernel(rows, first_col, place, *refs):
-    a_own, a_x, a_y = refs[:4], refs[4:9], refs[9:14]
-    w_same, w_swap = refs[14:16]
+    a_own, a_x, a_y, corners = refs[:4], refs[4:7], refs[7:10], refs[10:12]
+    w_same, w_swap = refs[12:14]
     abuf, wbuf, acc, sem_a, sem_w = refs[-5:]
     turn, core = place[0], place[1]
     half = w_same.shape[1]
     width = wbuf.shape[2]
 
     def copies_a(t):
-        out = []
-        for b in range(4):
-            if t < 3:
-                source = (a_own, a_x, a_y)[t][b].at[pl.ds(0, rows)]
-                target = abuf.at[t, pl.ds(b * rows, rows)]
-                out.append(pltpu.make_async_copy(source, target, sem_a.at[t, b]))
-                continue
-            mid = rows // 2
-            late = pl.ds(rows if b < 3 else 0, mid)
-            for n, part in enumerate((a_y, a_x)):
-                target = abuf.at[t, pl.ds(b * rows + n * mid, mid)]
-                out.append(
-                    pltpu.make_async_copy(part[b + 1].at[late], target, sem_a.at[t + n, b])
-                )
-        return out
+        mid = rows // 2
+        if t == 0:
+            pairs = [(a_own[b], 0, b * rows, rows) for b in range(4)]
+        elif t < 3:
+            c0, c1, c2 = (a_x, a_y)[t - 1]
+            pairs = [(c0, 0, 0, rows), (c1, 0, rows, rows), (c2, 0, 2 * rows, 2 * rows)]
+        else:
+            pairs = [(a_y[1], rows, 0, mid), (a_x[1], rows, mid, mid)]
+            pairs += [(a_y[2], 2 * rows, rows, mid), (a_x[2], 2 * rows, rows + mid, mid)]
+            pairs += [(corners[0], 0, 2 * rows, rows), (corners[1], 0, 3 * rows, rows)]
+        return [
+            pltpu.make_async_copy(
+                ref.at[pl.ds(source, size)], abuf.at[t, pl.ds(target, size)], sem_a.at[t, n]
+            )
+            for n, (ref, source, target, size) in enumerate(pairs)
+        ]
 
     def copies_w(t):
         out = []
@@ -233,11 +234,11 @@
         part = jnp.dot(abuf[t], wbuf[t], preferred_element_type=jnp.float32)
         acc[...] = part if t == 0 else acc[...] + part
     if first_col:
-        v_out = refs[16]
+        v_out = refs[14]
         for b in range(4):
             v_out[place[5 + b]] = acc[b * rows : (b + 1) * rows].astype(jnp.bfloat16)
         return
-    cos_ref, sin_ref, mine, theirs = refs[16:20]
+    cos_ref, sin_ref, mine, theirs = refs[14:18]
     first = core == 0
     for b in range(4):
         total = acc[b * rows : (b + 1) * rows]
@@ -262,14 +263,14 @@
         functools.partial(project_kernel, rows, first_col),
         out_shape=[out] * count,
         in_specs=[whole(pltpu.SMEM)]
-        + [whole(pl.ANY)] * 16
+        + [whole(pl.ANY)] * 14
         + [whole(pltpu.VMEM)] * len(angles),
         out_specs=[whole(pltpu.VMEM)] * count,
         scratch_shapes=[
             pltpu.VMEM((4, 4 * rows, depth), jnp.bfloat16),
             pltpu.VMEM((4, depth, width), jnp.bfloat16),
             pltpu.VMEM((4 * rows, width), jnp.float32),
-            pltpu.SemaphoreType.DMA((5, 4)),
+            pltpu.SemaphoreType.DMA((4, 6)),
             pltpu.SemaphoreType.DMA((4, 2)),
         ],
         compiler_params=kernel_params(56),
@@ -591,9 +592,12 @@
     outward = [(2, 0), (3, 1), (4, 6), (5, 7)]
     inner = (z == 1) | (z == 2)
 
-    def plane(piece, x_before, y_before):
-        to_x = jnp.concatenate([piece[:rows], y_before[half:rows]])
-        to_y = jnp.concatenate([piece[:rows], x_before[:half]])
+    ends = [(0, 6), (1, 7), (6, 0), (7, 1)]
+
+    def plane(pieces, x_before, y_before):
+        pieces = [piece[:rows] for piece in pieces]
+        to_x = jnp.concatenate(pieces + [y_before[half:rows]])
+        to_y = jnp.concatenate(pieces + [x_before[:half]])
         return swapped(to_x, "head", 1), swapped(to_y, "head", 2)
 
     near = swapped(block, "ctx", 2)
@@ -609,15 +613,14 @@
     same_core = [[i for i in range(8) if i % 2 == k] for k in range(2)]
     across_next = lax.ppermute(near, "ctx", middle)
     passed = lax.ppermute(across, "ctx", outward)
-    x1, y1 = plane(near, x0, y0)
-    across_next, passed, x1, y1, w_pieces = barrier((across_next, passed, x1, y1, w_pieces))
+    straight = lax.ppermute(block, "ctx", ends)
+    x1, y1 = plane([near], x0, y0)
+    across_next, passed, straight, x1, y1, w_pieces = barrier(
+        (across_next, passed, straight, x1, y1, w_pieces)
+    )
     w_same = lax.all_to_all(w_pieces, "ctx", 0, 0, axis_index_groups=same_core)
-    far_a = across + passed
-    passed_next = lax.ppermute(across_next, "ctx", outward)
-    x2, y2 = plane(far_a, x1, y1)
-    passed_next, x2, y2 = barrier((passed_next, x2, y2))
-    far_b = across_next + passed_next
-    x3, y3 = plane(far_b, x2, y2)
+    far_a, far_b = across + passed, across_next + straight
+    x2, y2 = plane([far_a, far_b], x1, y1)
     place_of = jnp.stack(
         [
             a[rows, :rows].astype(jnp.float32) * 256.0 + a[rows + 1, :rows].astype(jnp.float32)
@@ -630,16 +633,20 @@
     cosine, sine = jnp.cos(angle), jnp.sin(angle)
     cosine = jnp.concatenate([cosine, cosine], -1)
     sine = jnp.concatenate([-sine, sine], -1)
-    x3, y3, cosine, sine, w_out = barrier((x3, y3, cosine, sine, w_out))
-    x4, y4 = swapped(y3[half:rows], "head", 1), swapped(x3[:half], "head", 2)
+    x2, y2, cosine, sine, w_out = barrier((x2, y2, cosine, sine, w_out))
+    c_low = swapped(x2[:rows], "head", 2)
+    c_high = swapped(y2[rows : 2 * rows], "head", 1)
     out_near = swapped(w_out, "ctx", 2)
     out_across = lax.ppermute(w_out, "ctx", middle)
-    x4, y4, w_same = barrier((x4, y4, w_same))
+    out_ends = lax.ppermute(w_out, "ctx", ends)
+    c_low, c_high, w_same = barrier((c_low, c_high, w_same))
     w_swap = swapped(w_same, "ctx", 1)
-    planes = (x0, x1, x2, x3, x4, y0, y1, y2, y3, y4)
+    planes = (x0, x1, x2, y0, y1, y2, c_low, c_high)
     sources = place, (activations, near, far_a, far_b), planes, w_same, w_swap
     (v_pair,) = project(*sources)
-    place, v_pair, out_near, out_across = barrier((place, v_pair, out_near, out_across))
+    place, v_pair, out_near, out_across, out_ends = barrier(
+        (place, v_pair, out_near, out_across, out_ends)
+    )
     v_next = swapped(v_pair, "ctx", 2)
     v_pair_other = swapped(v_pair, "ctx", 1)
     out_across_next = lax.ppermute(out_near, "ctx", middle)
@@ -648,23 +655,21 @@
     mine, theirs, v_next, v_pair_other = barrier((mine, theirs, v_next, v_pair_other))
     other = swapped(theirs, "ctx", 1)
     v_next_other = swapped(v_next, "ctx", 1)
-    out_own_swap = swapped(w_out, "ctx", 1)
-    other, v_next_other, out_across_next, out_own_swap = barrier(
-        (other, v_next_other, out_across_next, out_own_swap)
-    )
-    out_passed_next = lax.ppermute(out_across_next, "ctx", outward)
-    out_near_swap, out_across_swap = swapped(out_near, "ctx", 1), swapped(out_across, "ctx", 1)
+    out_own_swap, out_near_swap = swapped(w_out, "ctx", 1), swapped(out_near, "ctx", 1)
+    out_across_swap, out_ends_swap = swapped(out_across, "ctx", 1), swapped(out_ends, "ctx", 1)
     group_rows = lax.dynamic_slice_in_dim(head_mix, GROUP * (ctx // GROUP), GROUP, 0)
     mix = lax.dynamic_index_in_dim(group_rows, ctx % GROUP, 1, keepdims=False)
     out_mine, out_theirs = attend_head(
         place, mix, weights, mine, other, (v_pair, v_next, v_pair_other, v_next_other)
     )
-    out_mine, out_theirs, out_passed, out_passed_next, out_near_swap, out_across_swap = barrier(
-        (out_mine, out_theirs, out_passed, out_passed_next, out_near_swap, out_across_swap)
-    )
+    out_mine, out_theirs, out_passed, out_across_next, *swaps = barrier(
+        (out_mine, out_theirs, out_passed, out_across_next)
+        + (out_own_swap, out_near_swap, out_across_swap, out_ends_swap)
+    )
+    out_own_swap, out_near_swap, out_across_swap, out_ends_swap = swaps
     out_parts = [w_out, out_own_swap, out_near, out_near_swap, out_across, out_across_swap]
-    for part in (out_passed, out_across_next, out_passed_next):
-        out_parts += [part, swapped(part, "ctx", 1)]
+    out_parts += [p for w in (out_passed, out_across_next) for p in (w, swapped(w, "ctx", 1))]
+    out_parts += [out_ends, out_ends_swap]
     summed = out_mine.astype(jnp.float32) + swapped(out_theirs, "ctx", 1).astype(jnp.float32)
     own = lax.dynamic_index_in_dim(summed, z, 0, keepdims=False)
     r1, r2, r3 = [

time: 282 us -> 290 us (1.028)
  waiting for transfers between devices: 150 us -> 168 us
  starting transfers between devices: 53.9 us -> 44.9 us
    ppermute x2, waiting for transfers between devices: 48.8 us -> 0.01 us  [the longest x1 0.01 us: per_device_one_head(): out_ends = lax.ppermute(w_out, 'ctx', ends)]
    ppermute x1, waiting for transfers between devices: 2.85 us -> 25.3 us  [per_device_one_head(): out_across = lax.ppermute(w_out, 'ctx', middle)]
    all_to_all x1, waiting for transfers between devices: 0.01 us -> 20.5 us  [per_device_one_head(): w_same = lax.all_to_all(w_pieces, 'ctx', 0, 0, axis_index_groups=same_core)]
    ppermute x30 -> x28, waiting for transfers between devices: 80.4 us -> 95 us  [swapped(): return lax.ppermute(value, axis, [(i, i ^ mask) for i in range(count)])]
    ppermute x1, waiting for transfers between devices: 9.3 us -> 23.8 us  [per_device_one_head(): across_next = lax.ppermute(near, 'ctx', middle)]
    ppermute x1, waiting for transfers between devices: 8.55 us -> 0.01 us  [per_device_one_head(): out_across_next = lax.ppermute(out_near, 'ctx', middle)]
    ppermute x30 -> x28, starting transfers between devices: 29.2 us -> 23.2 us  [swapped(): return lax.ppermute(value, axis, [(i, i ^ mask) for i in range(count)])]
    ppermute x1, waiting for transfers between devices: 0.01 us -> 3.42 us  [per_device_one_head(): out_passed = lax.ppermute(out_across, 'ctx', outward)]
  transfers between devices with their start and end apart: 39 -> 37, of which waited for: 22 -> 17; matrix products, arithmetic and copies ran while one was open for 8% -> 8% of each run, Pallas kernels for 13% -> 12%
where the time goes in v14:
time: 290 us; the launch traced here: 289 us
  waiting for transfers between devices  168 us (58%)
  starting transfers between devices  44.9 us (15%)
  Pallas kernels  43.9 us (15%)
  other arithmetic  19.1 us (7%)
  local copies, waits for them, and re-layouts  13.1 us (5%)
    ppermute x28, waiting for transfers between devices, swapped(): return lax.ppermute(value, axis, [(i, i ^ mask) for i in range(count)])  95 us
    ppermute x1, waiting for transfers between devices, per_device_one_head(): out_across = lax.ppermute(w_out, 'ctx', middle)  25.3 us
    ppermute x1, waiting for transfers between devices, per_device_one_head(): across_next = lax.ppermute(near, 'ctx', middle)  23.8 us
    ppermute x28, starting transfers between devices, swapped(): return lax.ppermute(value, axis, [(i, i ^ mask) for i in range(count)])  23.2 us
    all_to_all x1, waiting for transfers between devices, per_device_one_head(): w_same = lax.all_to_all(w_pieces, 'ctx', 0, 0, axis_index_groups=same_core)  20.5 us
    pallas_call x2, Pallas kernels, project(): pl.pallas_call(functools.partial(project_kernel, rows, first_col), out_sh...  19.3 us
    pallas_call x1, Pallas kernels, attend_head(): pl.pallas_call(attend_kernel, grid=(count,), out_shape=(out, out), in_spe...  16.7 us
    pallas_call x1, Pallas kernels, finish(): pl.pallas_call(finish_kernel, in_specs=[whole(pltpu.SMEM)] + [whole(pltpu...  7.9 us
  transfers between devices with their start and end apart: 37, of which 17 were waited for; matrix products, arithmetic and copies ran while one was open for 8% of the time, Pallas kernels for 12%

profile of v14, /device:TPU:17, one launch (start us, length us, event | category | flops | bytes accessed | tf_op | source)
XLA Modules:
  0.0 289.4 jit_solution(8412492698638782337)
XLA Ops:
  0.0 0.8 fusion.15
  0.8 2.0 pad_maximum_fusion.6
  2.8 1.3 collective-permute-start
  4.1 1.9 collective-permute-start.1
  6.0 1.3 collective-permute-start.2
  7.3 1.2 collective-permute-start.3
  8.5 0.8 fusion.20
  9.3 0.9 fusion.19
  10.2 0.9 fusion.18
  11.9 1.3 fusion.17.weights
  13.2 1.4 maximum_bitcast_fusion
  14.6 1.9 pad_maximum_fusion
  16.5 2.4 collective-permute-done.2.refs_4_
  18.9 0.9 collective-permute-done.3.refs_7_
  21.1 1.2 collective-permute-start.8
  23.0 3.0 %collective-permute-start.4 = (bf16[272,1024]{1,0:T(8,128)(2,1)S(1)}, bf16[272,1024]{1,0:T(8,128)(2,1)S(1)}, u32[]{:S(2)}, u32[]{:S(2)}) collective-permute-start(bf16[272,1024]{1,0:T(8,128)(2,1)S(1)} %collective-permute-done.refs_1_), channel_id=1, source_target_pairs={{8,16},{12,20},{16,8},{20,12},{9,17},{13,21},{17,9},{21,13},{10,18... | collective-permute-start | bytes 1671176 | tf_op jit(solution)/shard_map/ppermute | solution.py:614
  26.1 1.4 collective-permute-start.5
  27.5 23.8 %collective-permute-done.4 = bf16[272,1024]{1,0:T(8,128)(2,1)S(1)} collective-permute-done((bf16[272,1024]{1,0:T(8,128)(2,1)S(1)}, bf16[272,1024]{1,0:T(8,128)(2,1)S(1)}, u32[]{:S(2)}, u32[]{:S(2)}) %collective-permute-start.4) | collective-permute-done | bytes 557088 | tf_op jit(solution)/shard_map/ppermute | solution.py:614
  51.3 0.8 copy-done.20
  52.3 4.5 %all-to-all-start = ((bf16[4,512,768]{2,1,0:T(8,128)(2,1)}), bf16[4,512,768]{2,1,0:T(8,128)(2,1)S(1)}, u32[]{:S(2)}, u32[]{:S(2)}) async-start(bf16[4,512,768]{2,1,0:T(8,128)(2,1)} %pad_maximum_fusion), calls=%async_computation | async-start | bytes 6291456 | tf_op jit(solution)/shard_map/all_to_all | solution.py:621
  56.8 1.5 add.86.refs_2_
  58.3 1.2 slice.55
  59.8 1.1 slice.54
  61.3 1.0 collective-permute-start.9
  63.4 1.9 fusion.3
  65.3 1.0 pad_maximum_fusion.7.refs_14_
  66.3 1.0 pad_maximum_fusion.8.refs_15_
  67.3 23.3 %collective-permute-done.9.refs_6_ = bf16[640,1024]{1,0:T(8,128)(2,1)S(1)} collective-permute-done((bf16[640,1024]{1,0:T(8,128)(2,1)S(1)}, bf16[640,1024]{1,0:T(8,128)(2,1)S(1)}, u32[]{:S(2)}, u32[]{:S(2)}) %collective-permute-start.9) | collective-permute-done | bytes 1310752 | tf_op jit(solution)/shard_map/ppermute | solution.py:568
  92.2 10.5 %collective-permute-done.11.refs_10_ = bf16[256,1024]{1,0:T(8,128)(2,1)S(1)} collective-permute-done((bf16[256,1024]{1,0:T(8,128)(2,1)S(1)}, bf16[256,1024]{1,0:T(8,128)(2,1)S(1)}, u32[]{:S(2)}, u32[]{:S(2)}) %collective-permute-start.11) | collective-permute-done | bytes 524320 | tf_op jit(solution)/shard_map/ppermute | solution.py:568
  102.7 0.8 copy-done.23
  103.5 20.5 %all-to-all-done.refs_12_ = bf16[4,512,768]{2,1,0:T(8,128)(2,1)S(1)} async-done(((bf16[4,512,768]{2,1,0:T(8,128)(2,1)}), bf16[4,512,768]{2,1,0:T(8,128)(2,1)S(1)}, u32[]{:S(2)}, u32[]{:S(2)}) %all-to-all-start) | async-done | bytes 3145760 | tf_op jit(solution)/shard_map/all_to_all | solution.py:621
  124.0 1.4 collective-permute-start.13
  125.4 2.1 collective-permute-start.14
  127.5 3.1 %collective-permute-start.15 = (bf16[1024,512]{1,0:T(8,128)(2,1)}, bf16[1024,512]{1,0:T(8,128)(2,1)}, u32[]{:S(2)}, u32[]{:S(2)}) collective-permute-start(bf16[1024,512]{1,0:T(8,128)(2,1)} %refs_0_.4), channel_id=1, source_target_pairs={{8,16},{12,20},{16,8},{20,12},{9,17},{13,21},{17,9},{21,13},{10,18... | collective-permute-start | bytes 3145736 | tf_op jit(solution)/shard_map/ppermute | solution.py:640
  130.6 1.7 collective-permute-start.16
  132.3 1.7 copy-done.4
  134.0 9.1 %shard_map.91.refs_2_ = bf16[4,256,256]{2,1,0:T(8,128)(2,1)} custom-call(s32[9]{0:T(128)} %stack.78.place, bf16[256,1024]{1,0:T(8,128)(2,1)} %refs_0_.3, bf16[272,1024]{1,0:T(8,128)(2,1)} %copy-done.7, bf16[272,1024]{1,0:T(8,128)(2,1)} %copy-done.2, bf16[272,1024]{1,0:T(8,128)(2,1)} %copy-done.3, bf16[256,1024]{1,0:T(8,128)(2,1)} %copy-done.8, ...), custom_call_target="tpu_custom_call" | custom-call | flops 2147483648 | bytes 16777216 | tf_op jit(solution)/shard_map/pallas_call | solution.py:262
  143.1 8.2 %collective-permute-done.14.refs_2_ = bf16[1024,512]{1,0:T(8,128)(2,1)} collective-permute-done((bf16[1024,512]{1,0:T(8,128)(2,1)}, bf16[1024,512]{1,0:T(8,128)(2,1)}, u32[]{:S(2)}, u32[]{:S(2)}) %collective-permute-start.14) | collective-permute-done | bytes 1048608 | tf_op jit(solution)/shard_map/ppermute | solution.py:568
  151.3 25.3 %collective-permute-done.15.refs_4_ = bf16[1024,512]{1,0:T(8,128)(2,1)} collective-permute-done((bf16[1024,512]{1,0:T(8,128)(2,1)}, bf16[1024,512]{1,0:T(8,128)(2,1)}, u32[]{:S(2)}, u32[]{:S(2)}) %collective-permute-start.15) | collective-permute-done | bytes 1048608 | tf_op jit(solution)/shard_map/ppermute | solution.py:640
  176.6 1.2 collective-permute-start.18
  177.9 10.2 %shard_map.92 = (bf16[4,256,256]{2,1,0:T(8,128)(2,1)}, bf16[4,256,256]{2,1,0:T(8,128)(2,1)}) custom-call(s32[9]{0:T(128)} %stack.78.place, bf16[256,1024]{1,0:T(8,128)(2,1)} %refs_0_.3, bf16[272,1024]{1,0:T(8,128)(2,1)} %copy-done.7, bf16[272,1024]{1,0:T(8,128)(2,1)} %copy-done.2, bf16[272,1024]{1,0:T(8,128)(2,1)} %copy-done.3, bf16[256,1024]{1,0:T(8,128)(2,1)} %copy-done.8, ...), custom_call_target="tpu_custom_call" | custom-call | flops 4294967296 | bytes 16777216 | tf_op jit(solution)/shard_map/pallas_call | solution.py:262
  188.1 0.9 collective-permute-done.17.refs_3_
  189.1 2.2 collective-permute-start.19
  191.3 3.1 %collective-permute-start.22 = (bf16[1024,512]{1,0:T(8,128)(2,1)}, bf16[1024,512]{1,0:T(8,128)(2,1)}, u32[]{:S(2)}, u32[]{:S(2)}) collective-permute-start(bf16[1024,512]{1,0:T(8,128)(2,1)} %collective-permute-done.14.refs_2_), channel_id=1, source_target_pairs={{8,16},{12,20},{16,8},{20,12},{9,17},{13,21},{17,9},{21,13},{10,18... | collective-permute-start | bytes 3145736 | tf_op jit(solution)/shard_map/ppermute | solution.py:652
  194.4 0.8 collective-permute-start.24
  195.2 2.3 collective-permute-start.21
  197.5 0.8 copy-done.28
  199.4 16.7 %shard_map.93 = (bf16[4,256,512]{2,1,0:T(8,128)(2,1)}, bf16[4,256,512]{2,1,0:T(8,128)(2,1)}) custom-call(s32[9]{0:T(128)} %stack.78.place, f32[4]{0:T(128)} %dynamic-slice_bitcast_fusion.1.mix, f32[66]{0:T(128)} %fusion.17.weights, bf16[4,256,256]{2,1,0:T(8,128)(2,1)} %get-tuple-element.78.refs_0_, bf16[4,256,256]{2,1,0:T(8,128)(2,1)} %collective-permute-done.19.refs_1_, ...), custom_call_target="tpu_custom_call" | custom-call | flops 5368709120 | bytes 16777216 | tf_op jit(solution)/shard_map/pallas_call | solution.py:472
  216.1 3.4 %collective-permute-done.21.refs_6_ = bf16[1024,512]{1,0:T(8,128)(2,1)} collective-permute-done((bf16[1024,512]{1,0:T(8,128)(2,1)}, bf16[1024,512]{1,0:T(8,128)(2,1)}, u32[]{:S(2)}, u32[]{:S(2)}) %collective-permute-start.21) | collective-permute-done | bytes 1048608 | tf_op jit(solution)/shard_map/ppermute | solution.py:653
  220.9 2.7 collective-permute-done.27
  223.6 1.9 convert_add_fusion
  225.4 1.0 fusion.2
  226.4 2.2 collective-permute-start.28
  228.6 1.2 collective-permute-start.30
  230.4 0.8 dynamic-slice_bitcast_fusion.own
  231.2 7.5 %collective-permute-done.28.r1 = bf16[256,512]{1,0:T(8,128)(2,1)S(1)} collective-permute-done((bf16[256,512]{1,0:T(8,128)(2,1)}, bf16[256,512]{1,0:T(8,128)(2,1)S(1)}, u32[]{:S(2)}, u32[]{:S(2)}) %collective-permute-start.28) | collective-permute-done | bytes 262176 | tf_op jit(solution)/shard_map/ppermute | solution.py:568
  238.7 2.2 collective-permute-done.29.r2
  240.9 12.1 %collective-permute-done.30.r3 = bf16[256,512]{1,0:T(8,128)(2,1)} collective-permute-done((bf16[256,512]{1,0:T(8,128)(2,1)}, bf16[256,512]{1,0:T(8,128)(2,1)}, u32[]{:S(2)}, u32[]{:S(2)}) %collective-permute-start.30) | collective-permute-done | bytes 262176 | tf_op jit(solution)/shard_map/ppermute | solution.py:568
  253.0 7.9 %shard_map.94 = (bf16[256,1024]{1,0:T(8,128)(2,1)}, bf16[256,1024]{1,0:T(8,128)(2,1)}, bf16[256,1024]{1,0:T(8,128)(2,1)}, bf16[256,1024]{1,0:T(8,128)(2,1)}) custom-call(s32[10]{0:T(128)} %pad_add_fusion.place, f32[256,512]{1,0:T(8,128)} %dynamic-slice_bitcast_fusion.own, bf16[256,512]{1,0:T(8,128)(2,1)} %copy-done.24, ...), custom_call_target="tpu_custom_call" | custom-call | flops 2147483648 | bytes 11534336 | tf_op jit(solution)/shard_map/pallas_call | solution.py:549
  261.0 1.0 collective-permute-start.35
  261.9 1.2 collective-permute-start.34
  263.7 10.7 %collective-permute-done.35 = bf16[256,1024]{1,0:T(8,128)(2,1)S(1)} collective-permute-done((bf16[256,1024]{1,0:T(8,128)(2,1)}, bf16[256,1024]{1,0:T(8,128)(2,1)S(1)}, u32[]{:S(2)}, u32[]{:S(2)}) %collective-permute-start.35) | collective-permute-done | bytes 524320 | tf_op jit(solution)/shard_map/ppermute | solution.py:568
  274.4 12.8 %collective-permute-done.34 = bf16[256,1024]{1,0:T(8,128)(2,1)S(1)} collective-permute-done((bf16[256,1024]{1,0:T(8,128)(2,1)}, bf16[256,1024]{1,0:T(8,128)(2,1)S(1)}, u32[]{:S(2)}, u32[]{:S(2)}) %collective-permute-start.34) | collective-permute-done | bytes 524320 | tf_op jit(solution)/shard_map/ppermute | solution.py:568
  287.2 2.2 add_convert_fusion
  (113 shorter events, 10.1 us)
Async XLA Ops:
  0.0 198.7 %copy-start = (f32[8,4]{0,1:T(4,128)S(1)}, f32[8,4]{0,1:T(4,128)}, u32[]{:S(2)}) copy-start(f32[8,4]{0,1:T(4,128)} %param.15) | copy-start | bytes 388
  0.0 8.5 %copy-start.15 = (bf16[512,1024]{1,0:T(8,128)(2,1)S(1)}, bf16[512,1024]{1,0:T(8,128)(2,1)}, u32[]{:S(2)}) copy-start(bf16[512,1024]{1,0:T(8,128)(2,1)} %param.13) | copy-start | bytes 3145732
  0.8 8.5 %copy-start.16 = (bf16[512,1024]{1,0:T(8,128)(2,1)S(1)}, bf16[512,1024]{1,0:T(8,128)(2,1)}, u32[]{:S(2)}) copy-start(bf16[512,1024]{1,0:T(8,128)(2,1)} %param.12) | copy-start | bytes 3145732
  2.8 7.4 %copy-start.17 = (bf16[512,1024]{1,0:T(8,128)(2,1)S(1)}, bf16[512,1024]{1,0:T(8,128)(2,1)}, u32[]{:S(2)}) copy-start(bf16[512,1024]{1,0:T(8,128)(2,1)} %param.11) | copy-start | bytes 3145732
  2.8 17.0 %collective-permute-start = (bf16[272,1024]{1,0:T(8,128)(2,1)}, bf16[272,1024]{1,0:T(8,128)(2,1)S(1)}, u32[]{:S(2)}, u32[]{:S(2)}) collective-permute-start(bf16[272,1024]{1,0:T(8,128)(2,1)} %pad_maximum_fusion.6), channel_id=1, source_target_pairs={{0,8},{4,12},{8,0},{12,4},{16,24},{20,28},{24,16},{28,20},{1,9},{5... | collective-permute-start | bytes 1671176 | tf_op jit(solution)/shard_map/ppermute | solution.py:568
  4.1 15.7 %collective-permute-start.1 = (bf16[272,1024]{1,0:T(8,128)(2,1)}, bf16[272,1024]{1,0:T(8,128)(2,1)}, u32[]{:S(2)}, u32[]{:S(2)}) collective-permute-start(bf16[272,1024]{1,0:T(8,128)(2,1)} %pad_maximum_fusion.6), channel_id=1, source_target_pairs={{8,16},{12,20},{16,8},{20,12},{9,17},{13,21},{17,9},{21,13},{10,18... | collective-permute-start | bytes 1671176 | tf_op jit(solution)/shard_map/ppermute | solution.py:604
  6.0 12.9 %collective-permute-start.2 = (bf16[256,1024]{1,0:T(8,128)(2,1)}, bf16[256,1024]{1,0:T(8,128)(2,1)S(1)}, u32[]{:S(2)}, u32[]{:S(2)}) collective-permute-start(bf16[256,1024]{1,0:T(8,128)(2,1)} %refs_0_.3), channel_id=1, source_target_pairs={{0,1},{1,0},{2,3},{3,2},{4,5},{5,4},{6,7},{7,6},{8,9},{9,8},{10,11... | collective-permute-start | bytes 1572872 | tf_op jit(solution)/shard_map/ppermute | solution.py:568
  7.3 12.5 %collective-permute-start.3 = (bf16[256,1024]{1,0:T(8,128)(2,1)}, bf16[256,1024]{1,0:T(8,128)(2,1)S(1)}, u32[]{:S(2)}, u32[]{:S(2)}) collective-permute-start(bf16[256,1024]{1,0:T(8,128)(2,1)} %refs_0_.3), channel_id=1, source_target_pairs={{0,2},{1,3},{2,0},{3,1},{4,6},{5,7},{6,4},{7,5},{8,10},{9,11},{10,... | collective-permute-start | bytes 1572872 | tf_op jit(solution)/shard_map/ppermute | solution.py:568
  18.9 1.2 copy-start.8
  19.8 3.2 %copy-start.7 = (bf16[272,1024]{1,0:T(8,128)(2,1)}, bf16[272,1024]{1,0:T(8,128)(2,1)S(1)}, u32[]{:S(2)}) copy-start(bf16[272,1024]{1,0:T(8,128)(2,1)S(1)} %collective-permute-done.refs_1_) | copy-start | bytes 1671172
  20.6 30.7 %collective-permute-start.7 = (bf16[384,1024]{1,0:T(8,128)(2,1)S(1)}, bf16[384,1024]{1,0:T(8,128)(2,1)}, u32[]{:S(2)}, u32[]{:S(2)}) collective-permute-start(bf16[384,1024]{1,0:T(8,128)(2,1)S(1)} %get-tuple-element.117), channel_id=1, source_target_pairs={{0,1},{1,0},{2,3},{3,2},{4,5},{5,4},{6,7},{7,6},{8,9},{9,8},{10,11... | collective-permute-start | bytes 2359304 | tf_op jit(solution)/shard_map/ppermute | solution.py:568
  21.1 31.2 %collective-permute-start.8 = (bf16[384,1024]{1,0:T(8,128)(2,1)S(1)}, bf16[384,1024]{1,0:T(8,128)(2,1)}, u32[]{:S(2)}, u32[]{:S(2)}) collective-permute-start(bf16[384,1024]{1,0:T(8,128)(2,1)S(1)} %get-tuple-element.116), channel_id=1, source_target_pairs={{0,2},{1,3},{2,0},{3,1},{4,6},{5,7},{6,4},{7,5},{8,10},{9,11},{10,... | collective-permute-start | bytes 2359304 | tf_op jit(solution)/shard_map/ppermute | solution.py:568
  22.3 5.2 %collective-permute-start.6 = (bf16[272,1024]{1,0:T(8,128)(2,1)}, bf16[272,1024]{1,0:T(8,128)(2,1)S(1)}, u32[]{:S(2)}, u32[]{:S(2)}) collective-permute-start(bf16[272,1024]{1,0:T(8,128)(2,1)} %pad_maximum_fusion.6), channel_id=1, source_target_pairs={{0,24},{4,28},{24,0},{28,4},{1,25},{5,29},{25,1},{29,5},{2,26},{6,... | collective-permute-start | bytes 1671176 | tf_op jit(solution)/shard_map/ppermute | solution.py:616
  23.0 28.3 %collective-permute-start.4 = (bf16[272,1024]{1,0:T(8,128)(2,1)S(1)}, bf16[272,1024]{1,0:T(8,128)(2,1)S(1)}, u32[]{:S(2)}, u32[]{:S(2)}) collective-permute-start(bf16[272,1024]{1,0:T(8,128)(2,1)S(1)} %collective-permute-done.refs_1_), channel_id=1, source_target_pairs={{8,16},{12,20},{16,8},{20,12},{9,17},{13,21},{17,9},{21,13},{10,18... | collective-permute-start | bytes 1671176 | tf_op jit(solution)/shard_map/ppermute | solution.py:614
  26.1 25.2 %collective-permute-start.5 = (bf16[272,1024]{1,0:T(8,128)(2,1)}, bf16[272,1024]{1,0:T(8,128)(2,1)S(1)}, u32[]{:S(2)}, u32[]{:S(2)}) collective-permute-start(bf16[272,1024]{1,0:T(8,128)(2,1)} %collective-permute-done.1), channel_id=1, source_target_pairs={{8,0},{12,4},{16,24},{20,28},{9,1},{13,5},{17,25},{21,29},{10,2},{... | collective-permute-start | bytes 1671176 | tf_op jit(solution)/shard_map/ppermute | solution.py:615
  27.5 23.8 %copy-start.18 = (bf16[272,1024]{1,0:T(8,128)(2,1)}, bf16[272,1024]{1,0:T(8,128)(2,1)S(1)}, u32[]{:S(2)}) copy-start(bf16[272,1024]{1,0:T(8,128)(2,1)S(1)} %collective-permute-done.6) | copy-start | bytes 1671172
  51.3 0.8 copy-start.20
  51.3 1.0 copy-start.22
  52.3 71.7 %all-to-all-start = ((bf16[4,512,768]{2,1,0:T(8,128)(2,1)}), bf16[4,512,768]{2,1,0:T(8,128)(2,1)S(1)}, u32[]{:S(2)}, u32[]{:S(2)}) async-start(bf16[4,512,768]{2,1,0:T(8,128)(2,1)} %pad_maximum_fusion), calls=%async_computation | async-start | bytes 6291456 | tf_op jit(solution)/shard_map/all_to_all | solution.py:621
  56.8 2.7 copy-start.19
  56.8 2.7 copy-start.21
  58.3 5.0 %copy-start.2 = (bf16[272,1024]{1,0:T(8,128)(2,1)}, bf16[272,1024]{1,0:T(8,128)(2,1)S(1)}, u32[]{:S(2)}) copy-start(bf16[272,1024]{1,0:T(8,128)(2,1)S(1)} %add.86.refs_2_) | copy-start | bytes 1671172
  59.7 3.6 %copy-start.3 = (bf16[272,1024]{1,0:T(8,128)(2,1)}, bf16[272,1024]{1,0:T(8,128)(2,1)S(1)}, u32[]{:S(2)}) copy-start(bf16[272,1024]{1,0:T(8,128)(2,1)S(1)} %add.87.refs_3_) | copy-start | bytes 1671172
  61.3 29.3 %collective-permute-start.9 = (bf16[640,1024]{1,0:T(8,128)(2,1)S(1)}, bf16[640,1024]{1,0:T(8,128)(2,1)S(1)}, u32[]{:S(2)}, u32[]{:S(2)}) collective-permute-start(bf16[640,1024]{1,0:T(8,128)(2,1)S(1)} %get-tuple-element.103), channel_id=1, source_target_pairs={{0,1},{1,0},{2,3},{3,2},{4,5},{5,4},{6,7},{7,6},{8,9},{9,8},{10,11... | collective-permute-start | bytes 3932168 | tf_op jit(solution)/shard_map/ppermute | solution.py:568
  62.3 28.9 %collective-permute-start.10 = (bf16[640,1024]{1,0:T(8,128)(2,1)S(1)}, bf16[640,1024]{1,0:T(8,128)(2,1)S(1)}, u32[]{:S(2)}, u32[]{:S(2)}) collective-permute-start(bf16[640,1024]{1,0:T(8,128)(2,1)S(1)} %get-tuple-element.102), channel_id=1, source_target_pairs={{0,2},{1,3},{2,0},{3,1},{4,6},{5,7},{6,4},{7,5},{8,10},{9,11},{10,... | collective-permute-start | bytes 3932168 | tf_op jit(solution)/shard_map/ppermute | solution.py:568
  90.6 12.1 %copy-start.5 = (bf16[640,1024]{1,0:T(8,128)(2,1)}, bf16[640,1024]{1,0:T(8,128)(2,1)S(1)}, u32[]{:S(2)}) copy-start(bf16[640,1024]{1,0:T(8,128)(2,1)S(1)} %collective-permute-done.9.refs_6_) | copy-start | bytes 3932164
  91.3 11.4 %copy-start.6 = (bf16[640,1024]{1,0:T(8,128)(2,1)}, bf16[640,1024]{1,0:T(8,128)(2,1)S(1)}, u32[]{:S(2)}) copy-start(bf16[640,1024]{1,0:T(8,128)(2,1)S(1)} %collective-permute-done.10.refs_9_) | copy-start | bytes 3932164
  91.3 11.3 %collective-permute-start.11 = (bf16[256,1024]{1,0:T(8,128)(2,1)S(1)}, bf16[256,1024]{1,0:T(8,128)(2,1)S(1)}, u32[]{:S(2)}, u32[]{:S(2)}) collective-permute-start(bf16[256,1024]{1,0:T(8,128)(2,1)S(1)} %slice.62), channel_id=1, source_target_pairs={{0,2},{1,3},{2,0},{3,1},{4,6},{5,7},{6,4},{7,5},{8,10},{9,11},{10,... | collective-permute-start | bytes 1572872 | tf_op jit(solution)/shard_map/ppermute | solution.py:568
  91.6 11.8 %collective-permute-start.12 = (bf16[256,1024]{1,0:T(8,128)(2,1)S(1)}, bf16[256,1024]{1,0:T(8,128)(2,1)}, u32[]{:S(2)}, u32[]{:S(2)}) collective-permute-start(bf16[256,1024]{1,0:T(8,128)(2,1)S(1)} %slice.63), channel_id=1, source_target_pairs={{0,1},{1,0},{2,3},{3,2},{4,5},{5,4},{6,7},{7,6},{8,9},{9,8},{10,11... | collective-permute-start | bytes 1572872 | tf_op jit(solution)/shard_map/ppermute | solution.py:568
  102.7 0.8 copy-start.23
  124.0 8.3 %copy-start.1 = (bf16[4,512,768]{2,1,0:T(8,128)(2,1)}, bf16[4,512,768]{2,1,0:T(8,128)(2,1)S(1)}, u32[]{:S(2)}) copy-start(bf16[4,512,768]{2,1,0:T(8,128)(2,1)S(1)} %all-to-all-done.refs_12_) | copy-start | bytes 9437188
  124.0 53.8 %copy-start.10 = (bf16[1024,512]{1,0:T(8,128)(2,1)S(1)}, bf16[1024,512]{1,0:T(8,128)(2,1)}, u32[]{:S(2)}) copy-start(bf16[1024,512]{1,0:T(8,128)(2,1)} %refs_0_.4) | copy-start | bytes 3145732
  124.0 8.3 %collective-permute-start.13 = (bf16[4,512,768]{2,1,0:T(8,128)(2,1)S(1)}, bf16[4,512,768]{2,1,0:T(8,128)(2,1)S(1)}, u32[]{:S(2)}, u32[]{:S(2)}) collective-permute-start(bf16[4,512,768]{2,1,0:T(8,128)(2,1)S(1)} %all-to-all-done.refs_12_), channel_id=1, source_target_pairs={{0,4},{4,0},{8,12},{12,8},{16,20},{20,16},{24,28},{28,24},{1,5},{5... | collective-permute-start | bytes 9437192 | tf_op jit(solution)/shard_map/ppermute | solution.py:568
  125.4 25.9 %collective-permute-start.14 = (bf16[1024,512]{1,0:T(8,128)(2,1)}, bf16[1024,512]{1,0:T(8,128)(2,1)}, u32[]{:S(2)}, u32[]{:S(2)}) collective-permute-start(bf16[1024,512]{1,0:T(8,128)(2,1)} %refs_0_.4), channel_id=1, source_target_pairs={{0,8},{4,12},{8,0},{12,4},{16,24},{20,28},{24,16},{28,20},{1,9},{5... | collective-permute-start | bytes 3145736 | tf_op jit(solution)/shard_map/ppermute | solution.py:568
  127.5 49.1 %collective-permute-start.15 = (bf16[1024,512]{1,0:T(8,128)(2,1)}, bf16[1024,512]{1,0:T(8,128)(2,1)}, u32[]{:S(2)}, u32[]{:S(2)}) collective-permute-start(bf16[1024,512]{1,0:T(8,128)(2,1)} %refs_0_.4), channel_id=1, source_target_pairs={{8,16},{12,20},{16,8},{20,12},{9,17},{13,21},{17,9},{21,13},{10,18... | collective-permute-start | bytes 3145736 | tf_op jit(solution)/shard_map/ppermute | solution.py:640
  130.6 46.0 %collective-permute-start.16 = (bf16[1024,512]{1,0:T(8,128)(2,1)}, bf16[1024,512]{1,0:T(8,128)(2,1)}, u32[]{:S(2)}, u32[]{:S(2)}) collective-permute-start(bf16[1024,512]{1,0:T(8,128)(2,1)} %refs_0_.4), channel_id=1, source_target_pairs={{0,24},{4,28},{24,0},{28,4},{1,25},{5,29},{25,1},{29,5},{2,26},{6,... | collective-permute-start | bytes 3145736 | tf_op jit(solution)/shard_map/ppermute | solution.py:641
  132.3 1.7 copy-start.4
  176.6 12.5 %collective-permute-start.17 = (bf16[4,256,256]{2,1,0:T(8,128)(2,1)}, bf16[4,256,256]{2,1,0:T(8,128)(2,1)S(1)}, u32[]{:S(2)}, u32[]{:S(2)}) collective-permute-start(bf16[4,256,256]{2,1,0:T(8,128)(2,1)} %shard_map.91.refs_2_), channel_id=1, source_target_pairs={{0,8},{4,12},{8,0},{12,4},{16,24},{20,28},{24,16},{28,20},{1,9},{5... | collective-permute-start | bytes 1572872 | tf_op jit(solution)/shard_map/ppermute | solution.py:568
  176.6 12.5 %collective-permute-start.18 = (bf16[4,256,256]{2,1,0:T(8,128)(2,1)}, bf16[4,256,256]{2,1,0:T(8,128)(2,1)S(1)}, u32[]{:S(2)}, u32[]{:S(2)}) collective-permute-start(bf16[4,256,256]{2,1,0:T(8,128)(2,1)} %shard_map.91.refs_2_), channel_id=1, source_target_pairs={{0,4},{4,0},{8,12},{12,8},{16,20},{20,16},{24,28},{28,24},{1,5},{5... | collective-permute-start | bytes 1572872 | tf_op jit(solution)/shard_map/ppermute | solution.py:568
  177.8 17.4 %collective-permute-start.23 = (bf16[1024,512]{1,0:T(8,128)(2,1)S(1)}, bf16[1024,512]{1,0:T(8,128)(2,1)S(1)}, u32[]{:S(2)}, u32[]{:S(2)}) collective-permute-start(bf16[1024,512]{1,0:T(8,128)(2,1)S(1)} %copy-done.10), channel_id=1, source_target_pairs={{0,4},{4,0},{8,12},{12,8},{16,20},{20,16},{24,28},{28,24},{1,5},{5... | collective-permute-start | bytes 3145736 | tf_op jit(solution)/shard_map/ppermute | solution.py:568
  189.0 8.4 %copy-start.26 = (bf16[4,256,256]{2,1,0:T(8,128)(2,1)}, bf16[4,256,256]{2,1,0:T(8,128)(2,1)S(1)}, u32[]{:S(2)}) copy-start(bf16[4,256,256]{2,1,0:T(8,128)(2,1)S(1)} %collective-permute-done.17.refs_3_) | copy-start | bytes 1572868
  189.1 8.4 %copy-start.27 = (bf16[4,256,256]{2,1,0:T(8,128)(2,1)}, bf16[4,256,256]{2,1,0:T(8,128)(2,1)S(1)}, u32[]{:S(2)}) copy-start(bf16[4,256,256]{2,1,0:T(8,128)(2,1)S(1)} %collective-permute-done.18.refs_4_) | copy-start | bytes 1572868
  189.1 8.4 %collective-permute-start.19 = (bf16[4,256,256]{2,1,0:T(8,128)(2,1)}, bf16[4,256,256]{2,1,0:T(8,128)(2,1)}, u32[]{:S(2)}, u32[]{:S(2)}) collective-permute-start(bf16[4,256,256]{2,1,0:T(8,128)(2,1)} %get-tuple-element.79), channel_id=1, source_target_pairs={{0,4},{4,0},{8,12},{12,8},{16,20},{20,16},{24,28},{28,24},{1,5},{5... | collective-permute-start | bytes 1572872 | tf_op jit(solution)/shard_map/ppermute | solution.py:568
  191.2 6.3 %collective-permute-start.20 = (bf16[4,256,256]{2,1,0:T(8,128)(2,1)S(1)}, bf16[4,256,256]{2,1,0:T(8,128)(2,1)S(1)}, u32[]{:S(2)}, u32[]{:S(2)}) collective-permute-start(bf16[4,256,256]{2,1,0:T(8,128)(2,1)S(1)} %collective-permute-done.17.refs_3_), channel_id=1, source_target_pairs={{0,4},{4,0},{8,12},{12,8},{16,20},{20,16},{24,28},{28,24},{1,5},{5... | collective-permute-start | bytes 1572872 | tf_op jit(solution)/shard_map/ppermute | solution.py:568
  191.3 28.2 %collective-permute-start.22 = (bf16[1024,512]{1,0:T(8,128)(2,1)}, bf16[1024,512]{1,0:T(8,128)(2,1)}, u32[]{:S(2)}, u32[]{:S(2)}) collective-permute-start(bf16[1024,512]{1,0:T(8,128)(2,1)} %collective-permute-done.14.refs_2_), channel_id=1, source_target_pairs={{8,16},{12,20},{16,8},{20,12},{9,17},{13,21},{17,9},{21,13},{10,18... | collective-permute-start | bytes 3145736 | tf_op jit(solution)/shard_map/ppermute | solution.py:652
  194.4 25.1 %collective-permute-start.24 = (bf16[1024,512]{1,0:T(8,128)(2,1)}, bf16[1024,512]{1,0:T(8,128)(2,1)S(1)}, u32[]{:S(2)}, u32[]{:S(2)}) collective-permute-start(bf16[1024,512]{1,0:T(8,128)(2,1)} %collective-permute-done.14.refs_2_), channel_id=1, source_target_pairs={{0,4},{4,0},{8,12},{12,8},{16,20},{20,16},{24,28},{28,24},{1,5},{5... | collective-permute-start | bytes 3145736 | tf_op jit(solution)/shard_map/ppermute | solution.py:568
  195.2 20.9 %copy-start.11 = (bf16[1024,512]{1,0:T(8,128)(2,1)}, bf16[1024,512]{1,0:T(8,128)(2,1)S(1)}, u32[]{:S(2)}) copy-start(bf16[1024,512]{1,0:T(8,128)(2,1)S(1)} %collective-permute-done.23.refs_1_) | copy-start | bytes 3145732
  195.2 24.3 %collective-permute-start.21 = (bf16[1024,512]{1,0:T(8,128)(2,1)}, bf16[1024,512]{1,0:T(8,128)(2,1)}, u32[]{:S(2)}, u32[]{:S(2)}) collective-permute-start(bf16[1024,512]{1,0:T(8,128)(2,1)} %collective-permute-done.15.refs_4_), channel_id=1, source_target_pairs={{8,0},{12,4},{16,24},{20,28},{9,1},{13,5},{17,25},{21,29},{10,2},{... | collective-permute-start | bytes 3145736 | tf_op jit(solution)/shard_map/ppermute | solution.py:653
  197.4 22.1 %collective-permute-start.25 = (bf16[1024,512]{1,0:T(8,128)(2,1)}, bf16[1024,512]{1,0:T(8,128)(2,1)S(1)}, u32[]{:S(2)}, u32[]{:S(2)}) collective-permute-start(bf16[1024,512]{1,0:T(8,128)(2,1)} %collective-permute-done.15.refs_4_), channel_id=1, source_target_pairs={{0,4},{4,0},{8,12},{12,8},{16,20},{20,16},{24,28},{28,24},{1,5},{5... | collective-permute-start | bytes 3145736 | tf_op jit(solution)/shard_map/ppermute | solution.py:568
  198.3 21.3 %collective-permute-start.26 = (bf16[1024,512]{1,0:T(8,128)(2,1)}, bf16[1024,512]{1,0:T(8,128)(2,1)}, u32[]{:S(2)}, u32[]{:S(2)}) collective-permute-start(bf16[1024,512]{1,0:T(8,128)(2,1)} %collective-permute-done.16.refs_10_), channel_id=1, source_target_pairs={{0,4},{4,0},{8,12},{12,8},{16,20},{20,16},{24,28},{28,24},{1,5},{5... | collective-permute-start | bytes 3145736 | tf_op jit(solution)/shard_map/ppermute | solution.py:568
  219.5 1.2 copy-start.12
  219.5 1.3 copy-start.13
  219.5 4.0 %collective-permute-start.27 = (bf16[4,256,512]{2,1,0:T(8,128)(2,1)}, bf16[4,256,512]{2,1,0:T(8,128)(2,1)}, u32[]{:S(2)}, u32[]{:S(2)}) collective-permute-start(bf16[4,256,512]{2,1,0:T(8,128)(2,1)} %get-tuple-element.88), channel_id=1, source_target_pairs={{0,4},{4,0},{8,12},{12,8},{16,20},{20,16},{24,28},{28,24},{1,5},{5... | collective-permute-start | bytes 3145736 | tf_op jit(solution)/shard_map/ppermute | solution.py:568
  220.2 11.0 %collective-permute-start.31 = (bf16[1024,512]{1,0:T(8,128)(2,1)}, bf16[1024,512]{1,0:T(8,128)(2,1)S(1)}, u32[]{:S(2)}, u32[]{:S(2)}) collective-permute-start(bf16[1024,512]{1,0:T(8,128)(2,1)} %collective-permute-done.21.refs_6_), channel_id=1, source_target_pairs={{0,4},{4,0},{8,12},{12,8},{16,20},{20,16},{24,28},{28,24},{1,5},{5... | collective-permute-start | bytes 3145736 | tf_op jit(solution)/shard_map/ppermute | solution.py:568
  220.3 10.9 %collective-permute-start.32 = (bf16[1024,512]{1,0:T(8,128)(2,1)}, bf16[1024,512]{1,0:T(8,128)(2,1)}, u32[]{:S(2)}, u32[]{:S(2)}) collective-permute-start(bf16[1024,512]{1,0:T(8,128)(2,1)} %collective-permute-done.22.refs_8_), channel_id=1, source_target_pairs={{0,4},{4,0},{8,12},{12,8},{16,20},{20,16},{24,28},{28,24},{1,5},{5... | collective-permute-start | bytes 3145736 | tf_op jit(solution)/shard_map/ppermute | solution.py:568
  225.4 4.4 %copy-start.25 = (s32[9]{0:T(128)S(1)}, s32[9]{0:T(128)}, u32[]{:S(2)}) copy-start(s32[9]{0:T(128)} %stack.78.place) | copy-start | bytes 112
  226.4 12.3 %collective-permute-start.28 = (bf16[256,512]{1,0:T(8,128)(2,1)}, bf16[256,512]{1,0:T(8,128)(2,1)S(1)}, u32[]{:S(2)}, u32[]{:S(2)}) collective-permute-start(bf16[256,512]{1,0:T(8,128)(2,1)} %get-tuple-element.101), channel_id=1, source_target_pairs={{0,8},{4,12},{8,0},{12,4},{16,24},{20,28},{24,16},{28,20},{1,9},{5... | collective-permute-start | bytes 786440 | tf_op jit(solution)/shard_map/ppermute | solution.py:568
  228.6 12.4 %collective-permute-start.29 = (bf16[256,512]{1,0:T(8,128)(2,1)}, bf16[256,512]{1,0:T(8,128)(2,1)}, u32[]{:S(2)}, u32[]{:S(2)}) collective-permute-start(bf16[256,512]{1,0:T(8,128)(2,1)} %get-tuple-element.100), channel_id=1, source_target_pairs={{0,16},{4,20},{8,24},{12,28},{16,0},{20,4},{24,8},{28,12},{1,17},{... | collective-permute-start | bytes 786440 | tf_op jit(solution)/shard_map/ppermute | solution.py:568
  228.6 24.5 %collective-permute-start.30 = (bf16[256,512]{1,0:T(8,128)(2,1)}, bf16[256,512]{1,0:T(8,128)(2,1)}, u32[]{:S(2)}, u32[]{:S(2)}) collective-permute-start(bf16[256,512]{1,0:T(8,128)(2,1)} %get-tuple-element.99), channel_id=1, source_target_pairs={{0,24},{4,28},{8,16},{12,20},{16,8},{20,12},{24,0},{28,4},{1,25},{... | collective-permute-start | bytes 786440 | tf_op jit(solution)/shard_map/ppermute | solution.py:568
  231.2 21.8 %copy-start.14 = (bf16[1024,512]{1,0:T(8,128)(2,1)}, bf16[1024,512]{1,0:T(8,128)(2,1)S(1)}, u32[]{:S(2)}) copy-start(bf16[1024,512]{1,0:T(8,128)(2,1)S(1)} %collective-permute-done.31.refs_7_) | copy-start | bytes 3145732
  238.7 14.3 %copy-start.24 = (bf16[256,512]{1,0:T(8,128)(2,1)}, bf16[256,512]{1,0:T(8,128)(2,1)S(1)}, u32[]{:S(2)}) copy-start(bf16[256,512]{1,0:T(8,128)(2,1)S(1)} %collective-permute-done.28.r1) | copy-start | bytes 786436
  261.0 13.5 %collective-permute-start.35 = (bf16[256,1024]{1,0:T(8,128)(2,1)}, bf16[256,1024]{1,0:T(8,128)(2,1)S(1)}, u32[]{:S(2)}, u32[]{:S(2)}) collective-permute-start(bf16[256,1024]{1,0:T(8,128)(2,1)} %get-tuple-element.98), channel_id=1, source_target_pairs={{0,3},{1,2},{2,1},{3,0},{4,7},{5,6},{6,5},{7,4},{8,11},{9,10},{10,... | collective-permute-start | bytes 1572872 | tf_op jit(solution)/shard_map/ppermute | solution.py:568
  261.9 25.3 %collective-permute-start.34 = (bf16[256,1024]{1,0:T(8,128)(2,1)}, bf16[256,1024]{1,0:T(8,128)(2,1)S(1)}, u32[]{:S(2)}, u32[]{:S(2)}) collective-permute-start(bf16[256,1024]{1,0:T(8,128)(2,1)} %get-tuple-element.97), channel_id=1, source_target_pairs={{0,2},{1,3},{2,0},{3,1},{4,6},{5,7},{6,4},{7,5},{8,10},{9,11},{10,... | collective-permute-start | bytes 1572872 | tf_op jit(solution)/shard_map/ppermute | solution.py:568
  263.2 24.0 %collective-permute-start.33 = (bf16[256,1024]{1,0:T(8,128)(2,1)}, bf16[256,1024]{1,0:T(8,128)(2,1)S(1)}, u32[]{:S(2)}, u32[]{:S(2)}) collective-permute-start(bf16[256,1024]{1,0:T(8,128)(2,1)} %get-tuple-element.96), channel_id=1, source_target_pairs={{0,1},{1,0},{2,3},{3,2},{4,5},{5,4},{6,7},{7,6},{8,9},{9,8},{10,11... | collective-permute-start | bytes 1572872 | tf_op jit(solution)/shard_map/ppermute | solution.py:568
  (2 other events, 1.6 us)

commit v15 on v13

--- a/solution.py
+++ b/solution.py
@@ -498,7 +498,7 @@
     )(place, mix, weights, mine, other, *values)
 
 
-def finish_kernel(place, own, r1, r2, r3, gain, *refs):
+def finish_kernel(place, own, parts, gain, *refs):
     w_parts, outs = refs[:12], refs[12:16]
     normed, w_buf, sem = refs[16:]
     width = w_parts[0].shape[1]
@@ -523,8 +523,8 @@
         def _():
             copy_w(n, straight + 2).start()
 
-    near = own[...] + r1[...].astype(jnp.float32)
-    far = r2[...].astype(jnp.float32) + r3[...].astype(jnp.float32)
+    near = own[...] + parts[place[6]].astype(jnp.float32)
+    far = parts[place[7]].astype(jnp.float32) + parts[place[8]].astype(jnp.float32)
     low = place[3] == 0
     for g in range(2 * GROUP):
         cols = slice((g % GROUP) * HD, (g % GROUP + 1) * HD)
@@ -542,12 +542,12 @@
         ).astype(jnp.bfloat16)
 
 
-def finish(place, own, r1, r2, r3, gain, w_parts):
+def finish(place, own, parts, gain, w_parts):
     rows = own.shape[0]
     depth, width = w_parts[0].shape
     return pl.pallas_call(
         finish_kernel,
-        in_specs=[whole(pltpu.SMEM)] + [whole(pltpu.VMEM)] * 5 + [whole(pl.ANY)] * 12,
+        in_specs=[whole(pltpu.SMEM)] + [whole(pltpu.VMEM)] * 3 + [whole(pl.ANY)] * 12,
         out_specs=[whole(pltpu.VMEM)] * 4,
         out_shape=[jax.ShapeDtypeStruct((rows, 2 * width), jnp.bfloat16)] * 4,
         scratch_shapes=[
@@ -559,7 +559,7 @@
         cost_estimate=pl.CostEstimate(
             flops=2 * rows * depth * 8 * width, bytes_accessed=11 * 2**20, transcendentals=0
         ),
-    )(place, own, r1, r2, r3, gain, *w_parts)
+    )(place, own, parts, gain, *w_parts)
 
 
 def swapped(value, axis, mask):
@@ -667,16 +667,11 @@
         out_parts += [part, swapped(part, "ctx", 1)]
     summed = out_mine.astype(jnp.float32) + swapped(out_theirs, "ctx", 1).astype(jnp.float32)
     own = lax.dynamic_index_in_dim(summed, z, 0, keepdims=False)
-    r1, r2, r3 = [
-        swapped(
-            lax.dynamic_index_in_dim(summed, z ^ s, 0, keepdims=False).astype(jnp.bfloat16),
-            "ctx",
-            2 * s,
-        )
-        for s in (1, 2, 3)
-    ]
+    parts = lax.all_to_all(
+        summed.astype(jnp.bfloat16), "ctx", 0, 0, axis_index_groups=same_core
+    )
     where = jnp.concatenate([place, inner.astype(jnp.int32)[None]])
-    shares = finish(where, own, r1, r2, r3, out_gain.reshape(1, -1), out_parts)
+    shares = finish(where, own, parts, out_gain.reshape(1, -1), out_parts)
     total = shares[0].astype(jnp.float32)
     for t in (1, 2, 3):
         total = total + swapped(shares[t], "head", t).astype(jnp.float32)

time: 282 us -> 288 us (1.021); the launches traced: 281 us -> 283 us
    ppermute x30 -> x27, waiting for transfers between devices: 80.4 us -> 61.6 us  [swapped(): return lax.ppermute(value, axis, [(i, i ^ mask) for i in range(count)])]
    all_to_all x0 -> x1, waiting for transfers between devices: none -> 16.2 us  [per_device_one_head(): lax.all_to_all(summed.astype(jnp.bfloat16), 'ctx', 0, 0, axis_index_group...]
    all_to_all x0 -> x1, starting transfers between devices: none -> 6.21 us  [per_device_one_head(): lax.all_to_all(summed.astype(jnp.bfloat16), 'ctx', 0, 0, axis_index_group...]
    ppermute x30 -> x27, starting transfers between devices: 29.2 us -> 26.3 us  [swapped(): return lax.ppermute(value, axis, [(i, i ^ mask) for i in range(count)])]
  transfers between devices with their start and end apart: 39 -> 37, of which waited for: 22 -> 23; matrix products, arithmetic and copies ran while one was open for 8% -> 7% of each run, Pallas kernels for 13% -> 13%
where the time goes in v15:
time: 288 us; the launch traced here: 283 us
  waiting for transfers between devices  148 us (51%)
  starting transfers between devices  55.5 us (19%)
  Pallas kernels  44.8 us (16%)
  other arithmetic  19.8 us (7%)
  local copies, waits for them, and re-layouts  13.8 us (5%)
    ppermute x27, waiting for transfers between devices, swapped(): return lax.ppermute(value, axis, [(i, i ^ mask) for i in range(count)])  61.6 us
    ppermute x1, waiting for transfers between devices, per_device_one_head(): passed_next = lax.ppermute(across_next, 'ctx', outward)  35.5 us
    ppermute x27, starting transfers between devices, swapped(): return lax.ppermute(value, axis, [(i, i ^ mask) for i in range(count)])  26.3 us
    pallas_call x2, Pallas kernels, project(): pl.pallas_call(functools.partial(project_kernel, rows, first_col), out_sh...  20 us
    pallas_call x1, Pallas kernels, attend_head(): pl.pallas_call(attend_kernel, grid=(count,), out_shape=(out, out), in_spe...  16.7 us
    all_to_all x1, waiting for transfers between devices, per_device_one_head(): lax.all_to_all(summed.astype(jnp.bfloat16), 'ctx', 0, 0, axis_index_group...  16.2 us
    ppermute x1, waiting for transfers between devices, per_device_one_head(): out_passed_next = lax.ppermute(out_across_next, 'ctx', outward)  13.4 us
    ppermute x1, waiting for transfers between devices, per_device_one_head(): across_next = lax.ppermute(near, 'ctx', middle)  9.29 us
  transfers between devices with their start and end apart: 37, of which 23 were waited for; matrix products, arithmetic and copies ran while one was open for 7% of the time, Pallas kernels for 13%

profile of v15, /device:TPU:17, one launch (start us, length us, event | category | flops | bytes accessed | tf_op | source)
XLA Modules:
  0.0 282.6 jit_solution(13822658694758573477)
XLA Ops:
  0.8 2.0 pad_maximum_fusion.7
  2.8 1.3 collective-permute-start
  4.1 1.9 collective-permute-start.1
  6.0 1.3 collective-permute-start.2
  7.3 1.2 collective-permute-start.3
  9.3 0.9 fusion.15
  10.2 0.9 fusion.14
  11.9 1.2 multiply_bitcast_fusion.weights
  13.1 1.4 maximum_bitcast_fusion
  14.5 1.9 pad_maximum_fusion
  16.4 2.5 collective-permute-done.2.refs_4_
  18.9 0.9 collective-permute-done.3.refs_9_
  21.1 1.2 collective-permute-start.7
  22.3 3.1 %collective-permute-start.4 = (bf16[272,1024]{1,0:T(8,128)(2,1)S(1)}, bf16[272,1024]{1,0:T(8,128)(2,1)S(1)}, u32[]{:S(2)}, u32[]{:S(2)}) collective-permute-start(bf16[272,1024]{1,0:T(8,128)(2,1)S(1)} %collective-permute-done.refs_1_), channel_id=1, source_target_pairs={{8,16},{12,20},{16,8},{20,12},{9,17},{13,21},{17,9},{21,13},{10,18... | collective-permute-start | bytes 1671176 | tf_op jit(solution)/shard_map/ppermute | solution.py:610
  25.4 1.3 collective-permute-start.5
  26.7 9.3 %collective-permute-done.4 = bf16[272,1024]{1,0:T(8,128)(2,1)S(1)} collective-permute-done((bf16[272,1024]{1,0:T(8,128)(2,1)S(1)}, bf16[272,1024]{1,0:T(8,128)(2,1)S(1)}, u32[]{:S(2)}, u32[]{:S(2)}) %collective-permute-start.4) | collective-permute-done | bytes 557088 | tf_op jit(solution)/shard_map/ppermute | solution.py:610
  36.2 1.5 collective-permute-done.6.refs_5_
  38.1 5.1 %all-to-all-start = ((bf16[4,512,768]{2,1,0:T(8,128)(2,1)}), bf16[4,512,768]{2,1,0:T(8,128)(2,1)S(1)}, u32[]{:S(2)}, u32[]{:S(2)}) async-start(bf16[4,512,768]{2,1,0:T(8,128)(2,1)} %pad_maximum_fusion), calls=%async_computation | async-start | bytes 6291456 | tf_op jit(solution)/shard_map/all_to_all | solution.py:614
  43.2 1.4 add.77.refs_2_
  44.7 1.1 slice.63
  45.8 1.0 slice.62
  47.0 0.9 collective-permute-start.9
  48.2 3.1 %collective-permute-start.8 = (bf16[272,1024]{1,0:T(8,128)(2,1)S(1)}, bf16[272,1024]{1,0:T(8,128)(2,1)S(1)}, u32[]{:S(2)}, u32[]{:S(2)}) collective-permute-start(bf16[272,1024]{1,0:T(8,128)(2,1)S(1)} %copy-done.22), channel_id=1, source_target_pairs={{8,0},{12,4},{16,24},{20,28},{9,1},{13,5},{17,25},{21,29},{10,2},{... | collective-permute-start | bytes 1671176 | tf_op jit(solution)/shard_map/ppermute | solution.py:616
  52.1 35.5 %collective-permute-done.8 = bf16[272,1024]{1,0:T(8,128)(2,1)S(1)} collective-permute-done((bf16[272,1024]{1,0:T(8,128)(2,1)S(1)}, bf16[272,1024]{1,0:T(8,128)(2,1)S(1)}, u32[]{:S(2)}, u32[]{:S(2)}) %collective-permute-start.8) | collective-permute-done | bytes 557088 | tf_op jit(solution)/shard_map/ppermute | solution.py:616
  89.9 1.9 fusion
  91.8 1.0 pad_maximum_fusion.8.refs_16_
  92.8 1.0 pad_maximum_fusion.9.refs_17_
  93.8 10.2 %collective-permute-done.11.refs_7_ = bf16[384,1024]{1,0:T(8,128)(2,1)S(1)} collective-permute-done((bf16[384,1024]{1,0:T(8,128)(2,1)S(1)}, bf16[384,1024]{1,0:T(8,128)(2,1)S(1)}, u32[]{:S(2)}, u32[]{:S(2)}) %collective-permute-start.11) | collective-permute-done | bytes 786464 | tf_op jit(solution)/shard_map/ppermute | solution.py:567
  104.2 1.0 collective-permute-start.13
  105.4 5.8 %collective-permute-done.13.refs_8_ = bf16[128,1024]{1,0:T(8,128)(2,1)S(1)} collective-permute-done((bf16[128,1024]{1,0:T(8,128)(2,1)S(1)}, bf16[128,1024]{1,0:T(8,128)(2,1)S(1)}, u32[]{:S(2)}, u32[]{:S(2)}) %collective-permute-start.13) | collective-permute-done | bytes 262176 | tf_op jit(solution)/shard_map/ppermute | solution.py:567
  111.2 0.8 collective-permute-done.14.refs_13_
  112.0 7.0 %collective-permute-start.15 = (bf16[4,512,768]{2,1,0:T(8,128)(2,1)S(1)}, bf16[4,512,768]{2,1,0:T(8,128)(2,1)S(1)}, u32[]{:S(2)}, u32[]{:S(2)}) collective-permute-start(bf16[4,512,768]{2,1,0:T(8,128)(2,1)S(1)} %all-to-all-done.refs_14_), channel_id=1, source_target_pairs={{0,4},{4,0},{8,12},{12,8},{16,20},{20,16},{24,28},{28,24},{1,5},{5... | collective-permute-start | bytes 9437192 | tf_op jit(solution)/shard_map/ppermute | solution.py:567
  119.0 2.2 collective-permute-start.16
  121.2 1.9 collective-permute-start.17
  123.1 1.2 collective-permute-done.15.refs_15_
  124.3 1.7 copy-done.5
  126.0 9.4 %shard_map.91.refs_2_ = bf16[4,256,256]{2,1,0:T(8,128)(2,1)} custom-call(s32[9]{0:T(128)} %stack.78.place, bf16[256,1024]{1,0:T(8,128)(2,1)} %refs_0_.3, bf16[272,1024]{1,0:T(8,128)(2,1)} %copy-done.6, bf16[272,1024]{1,0:T(8,128)(2,1)} %copy-done.2, bf16[272,1024]{1,0:T(8,128)(2,1)} %copy-done.3, bf16[256,1024]{1,0:T(8,128)(2,1)} %copy-done.11, ...), custom_call_target="tpu_custom_call" | custom-call | flops 2147483648 | bytes 16777216 | tf_op jit(solution)/shard_map/pallas_call | solution.py:261
  135.4 9.6 %collective-permute-done.16.refs_2_ = bf16[1024,512]{1,0:T(8,128)(2,1)} collective-permute-done((bf16[1024,512]{1,0:T(8,128)(2,1)}, bf16[1024,512]{1,0:T(8,128)(2,1)}, u32[]{:S(2)}, u32[]{:S(2)}) %collective-permute-start.16) | collective-permute-done | bytes 1048608 | tf_op jit(solution)/shard_map/ppermute | solution.py:567
  145.0 2.8 %collective-permute-done.17.refs_4_ = bf16[1024,512]{1,0:T(8,128)(2,1)} collective-permute-done((bf16[1024,512]{1,0:T(8,128)(2,1)}, bf16[1024,512]{1,0:T(8,128)(2,1)}, u32[]{:S(2)}, u32[]{:S(2)}) %collective-permute-start.17) | collective-permute-done | bytes 1048608 | tf_op jit(solution)/shard_map/ppermute | solution.py:636
  147.8 1.2 collective-permute-start.19
  149.1 1.9 collective-permute-start.22
  151.0 10.6 %shard_map.92 = (bf16[4,256,256]{2,1,0:T(8,128)(2,1)}, bf16[4,256,256]{2,1,0:T(8,128)(2,1)}) custom-call(s32[9]{0:T(128)} %stack.78.place, bf16[256,1024]{1,0:T(8,128)(2,1)} %refs_0_.3, bf16[272,1024]{1,0:T(8,128)(2,1)} %copy-done.6, bf16[272,1024]{1,0:T(8,128)(2,1)} %copy-done.2, bf16[272,1024]{1,0:T(8,128)(2,1)} %copy-done.3, ...), custom_call_target="tpu_custom_call" | custom-call | flops 4294967296 | bytes 16777216 | tf_op jit(solution)/shard_map/pallas_call | solution.py:261
  162.9 1.0 copy-done.14
  163.9 2.4 collective-permute-start.24
  166.4 9.1 %collective-permute-done.22.refs_8_ = bf16[1024,512]{1,0:T(8,128)(2,1)S(1)} collective-permute-done((bf16[1024,512]{1,0:T(8,128)(2,1)}, bf16[1024,512]{1,0:T(8,128)(2,1)S(1)}, u32[]{:S(2)}, u32[]{:S(2)}) %collective-permute-start.22) | collective-permute-done | bytes 1048608 | tf_op jit(solution)/shard_map/ppermute | solution.py:645
  175.5 1.3 collective-permute-start.27
  178.3 2.3 collective-permute-start.25
  181.2 16.7 %shard_map.93 = (bf16[4,256,512]{2,1,0:T(8,128)(2,1)}, bf16[4,256,512]{2,1,0:T(8,128)(2,1)}) custom-call(s32[9]{0:T(128)} %stack.78.place, f32[4]{0:T(128)} %dynamic-slice_bitcast_fusion.1.mix, f32[66]{0:T(128)} %multiply_bitcast_fusion.weights, bf16[4,256,256]{2,1,0:T(8,128)(2,1)} %get-tuple-element.83.refs_0_, bf16[4,256,256]{2,1,0:T(8,128)(2,1)} %copy-done.28, ...), custom_call_target="tpu_custom_call" | custom-call | flops 5368709120 | bytes 16777216 | tf_op jit(solution)/shard_map/pallas_call | solution.py:471
  198.0 13.4 %collective-permute-done.25.refs_10_ = bf16[1024,512]{1,0:T(8,128)(2,1)} collective-permute-done((bf16[1024,512]{1,0:T(8,128)(2,1)S(1)}, bf16[1024,512]{1,0:T(8,128)(2,1)}, u32[]{:S(2)}, u32[]{:S(2)}) %collective-permute-start.25) | collective-permute-done | bytes 1048608 | tf_op jit(solution)/shard_map/ppermute | solution.py:655
  211.3 0.8 collective-permute-start.28
  212.2 2.5 collective-permute-done.28
  214.7 2.7 fusion.13
  217.4 6.2 %all-to-all-start.1 = ((bf16[4,256,512]{2,1,0:T(8,128)(2,1)}), bf16[4,256,512]{2,1,0:T(8,128)(2,1)S(1)}, u32[]{:S(2)}, u32[]{:S(2)}) async-start(bf16[4,256,512]{2,1,0:T(8,128)(2,1)} %get-tuple-element.105), calls=%async_computation.1 | async-start | bytes 2097152 | tf_op jit(solution)/shard_map/all_to_all | solution.py:670
  225.4 0.8 dynamic-slice_bitcast_fusion.own
  226.9 1.5 collective-permute-done.29.refs_7_
  228.4 1.5 collective-permute-done.31.refs_11_
  229.9 16.2 %all-to-all-done.1.parts = bf16[4,256,512]{2,1,0:T(8,128)(2,1)S(1)} async-done(((bf16[4,256,512]{2,1,0:T(8,128)(2,1)}), bf16[4,256,512]{2,1,0:T(8,128)(2,1)S(1)}, u32[]{:S(2)}, u32[]{:S(2)}) %all-to-all-start.1) | async-done | bytes 1048608 | tf_op jit(solution)/shard_map/all_to_all | solution.py:670
  246.1 1.0 copy-done.4
  247.1 8.1 %shard_map.94 = (bf16[256,1024]{1,0:T(8,128)(2,1)}, bf16[256,1024]{1,0:T(8,128)(2,1)}, bf16[256,1024]{1,0:T(8,128)(2,1)}, bf16[256,1024]{1,0:T(8,128)(2,1)}) custom-call(s32[10]{0:T(128)} %pad_add_fusion.place, f32[256,512]{1,0:T(8,128)} %dynamic-slice_bitcast_fusion.own, bf16[4,256,512]{2,1,0:T(8,128)(2,1)} %copy-done.4, f32[1,1024]{1,0:T(1,128)} %bitcast.24, ...), custom_call_target="tpu_custom_call" | custom-call | flops 2147483648 | bytes 11534336 | tf_op jit(solution)/shard_map/pallas_call | solution.py:548
  255.7 1.3 collective-permute-start.33
  257.0 1.0 collective-permute-start.32
  258.0 10.8 %collective-permute-done.34 = bf16[256,1024]{1,0:T(8,128)(2,1)S(1)} collective-permute-done((bf16[256,1024]{1,0:T(8,128)(2,1)}, bf16[256,1024]{1,0:T(8,128)(2,1)S(1)}, u32[]{:S(2)}, u32[]{:S(2)}) %collective-permute-start.34) | collective-permute-done | bytes 524320 | tf_op jit(solution)/shard_map/ppermute | solution.py:567
  268.7 11.6 %collective-permute-done.33 = bf16[256,1024]{1,0:T(8,128)(2,1)S(1)} collective-permute-done((bf16[256,1024]{1,0:T(8,128)(2,1)}, bf16[256,1024]{1,0:T(8,128)(2,1)S(1)}, u32[]{:S(2)}, u32[]{:S(2)}) %collective-permute-start.33) | collective-permute-done | bytes 524320 | tf_op jit(solution)/shard_map/ppermute | solution.py:567
  280.4 2.2 add_convert_fusion
  (117 shorter events, 14.6 us)
Async XLA Ops:
  0.0 180.6 %copy-start = (f32[8,4]{0,1:T(4,128)S(1)}, f32[8,4]{0,1:T(4,128)}, u32[]{:S(2)}) copy-start(f32[8,4]{0,1:T(4,128)} %param.15) | copy-start | bytes 388
  0.0 8.5 %copy-start.18 = (bf16[512,1024]{1,0:T(8,128)(2,1)S(1)}, bf16[512,1024]{1,0:T(8,128)(2,1)}, u32[]{:S(2)}) copy-start(bf16[512,1024]{1,0:T(8,128)(2,1)} %param.13) | copy-start | bytes 3145732
  0.8 8.5 %copy-start.19 = (bf16[512,1024]{1,0:T(8,128)(2,1)S(1)}, bf16[512,1024]{1,0:T(8,128)(2,1)}, u32[]{:S(2)}) copy-start(bf16[512,1024]{1,0:T(8,128)(2,1)} %param.12) | copy-start | bytes 3145732
  2.8 7.4 %copy-start.20 = (bf16[512,1024]{1,0:T(8,128)(2,1)S(1)}, bf16[512,1024]{1,0:T(8,128)(2,1)}, u32[]{:S(2)}) copy-start(bf16[512,1024]{1,0:T(8,128)(2,1)} %param.11) | copy-start | bytes 3145732
  2.8 17.0 %collective-permute-start = (bf16[272,1024]{1,0:T(8,128)(2,1)}, bf16[272,1024]{1,0:T(8,128)(2,1)S(1)}, u32[]{:S(2)}, u32[]{:S(2)}) collective-permute-start(bf16[272,1024]{1,0:T(8,128)(2,1)} %pad_maximum_fusion.7), channel_id=1, source_target_pairs={{0,8},{4,12},{8,0},{12,4},{16,24},{20,28},{24,16},{28,20},{1,9},{5... | collective-permute-start | bytes 1671176 | tf_op jit(solution)/shard_map/ppermute | solution.py:567
  4.1 15.7 %collective-permute-start.1 = (bf16[272,1024]{1,0:T(8,128)(2,1)}, bf16[272,1024]{1,0:T(8,128)(2,1)}, u32[]{:S(2)}, u32[]{:S(2)}) collective-permute-start(bf16[272,1024]{1,0:T(8,128)(2,1)} %pad_maximum_fusion.7), channel_id=1, source_target_pairs={{8,16},{12,20},{16,8},{20,12},{9,17},{13,21},{17,9},{21,13},{10,18... | collective-permute-start | bytes 1671176 | tf_op jit(solution)/shard_map/ppermute | solution.py:600
  6.0 12.9 %collective-permute-start.2 = (bf16[256,1024]{1,0:T(8,128)(2,1)}, bf16[256,1024]{1,0:T(8,128)(2,1)S(1)}, u32[]{:S(2)}, u32[]{:S(2)}) collective-permute-start(bf16[256,1024]{1,0:T(8,128)(2,1)} %refs_0_.3), channel_id=1, source_target_pairs={{0,1},{1,0},{2,3},{3,2},{4,5},{5,4},{6,7},{7,6},{8,9},{9,8},{10,11... | collective-permute-start | bytes 1572872 | tf_op jit(solution)/shard_map/ppermute | solution.py:567
  7.3 12.5 %collective-permute-start.3 = (bf16[256,1024]{1,0:T(8,128)(2,1)}, bf16[256,1024]{1,0:T(8,128)(2,1)S(1)}, u32[]{:S(2)}, u32[]{:S(2)}) collective-permute-start(bf16[256,1024]{1,0:T(8,128)(2,1)} %refs_0_.3), channel_id=1, source_target_pairs={{0,2},{1,3},{2,0},{3,1},{4,6},{5,7},{6,4},{7,5},{8,10},{9,11},{10,... | collective-permute-start | bytes 1572872 | tf_op jit(solution)/shard_map/ppermute | solution.py:567
  18.9 1.2 copy-start.11
  19.8 2.5 copy-start.6
  20.6 17.1 %collective-permute-start.6 = (bf16[384,1024]{1,0:T(8,128)(2,1)S(1)}, bf16[384,1024]{1,0:T(8,128)(2,1)}, u32[]{:S(2)}, u32[]{:S(2)}) collective-permute-start(bf16[384,1024]{1,0:T(8,128)(2,1)S(1)} %get-tuple-element.124), channel_id=1, source_target_pairs={{0,1},{1,0},{2,3},{3,2},{4,5},{5,4},{6,7},{7,6},{8,9},{9,8},{10,11... | collective-permute-start | bytes 2359304 | tf_op jit(solution)/shard_map/ppermute | solution.py:567
  21.1 17.0 %collective-permute-start.7 = (bf16[384,1024]{1,0:T(8,128)(2,1)S(1)}, bf16[384,1024]{1,0:T(8,128)(2,1)}, u32[]{:S(2)}, u32[]{:S(2)}) collective-permute-start(bf16[384,1024]{1,0:T(8,128)(2,1)S(1)} %get-tuple-element.123), channel_id=1, source_target_pairs={{0,2},{1,3},{2,0},{3,1},{4,6},{5,7},{6,4},{7,5},{8,10},{9,11},{10,... | collective-permute-start | bytes 2359304 | tf_op jit(solution)/shard_map/ppermute | solution.py:567
  22.3 13.7 %collective-permute-start.4 = (bf16[272,1024]{1,0:T(8,128)(2,1)S(1)}, bf16[272,1024]{1,0:T(8,128)(2,1)S(1)}, u32[]{:S(2)}, u32[]{:S(2)}) collective-permute-start(bf16[272,1024]{1,0:T(8,128)(2,1)S(1)} %collective-permute-done.refs_1_), channel_id=1, source_target_pairs={{8,16},{12,20},{16,8},{20,12},{9,17},{13,21},{17,9},{21,13},{10,18... | collective-permute-start | bytes 1671176 | tf_op jit(solution)/shard_map/ppermute | solution.py:610
  25.4 10.8 %collective-permute-start.5 = (bf16[272,1024]{1,0:T(8,128)(2,1)}, bf16[272,1024]{1,0:T(8,128)(2,1)S(1)}, u32[]{:S(2)}, u32[]{:S(2)}) collective-permute-start(bf16[272,1024]{1,0:T(8,128)(2,1)} %collective-permute-done.1), channel_id=1, source_target_pairs={{8,0},{12,4},{16,24},{20,28},{9,1},{13,5},{17,25},{21,29},{10,2},{... | collective-permute-start | bytes 1671176 | tf_op jit(solution)/shard_map/ppermute | solution.py:611
  36.0 1.7 copy-start.21
  36.2 1.5 copy-start.23
  38.1 73.9 %all-to-all-start = ((bf16[4,512,768]{2,1,0:T(8,128)(2,1)}), bf16[4,512,768]{2,1,0:T(8,128)(2,1)S(1)}, u32[]{:S(2)}, u32[]{:S(2)}) async-start(bf16[4,512,768]{2,1,0:T(8,128)(2,1)} %pad_maximum_fusion), calls=%async_computation | async-start | bytes 6291456 | tf_op jit(solution)/shard_map/all_to_all | solution.py:614
  44.6 7.4 %copy-start.2 = (bf16[272,1024]{1,0:T(8,128)(2,1)}, bf16[272,1024]{1,0:T(8,128)(2,1)S(1)}, u32[]{:S(2)}) copy-start(bf16[272,1024]{1,0:T(8,128)(2,1)S(1)} %add.77.refs_2_) | copy-start | bytes 1671172
  45.8 2.4 copy-start.22
  47.0 40.5 %collective-permute-start.9 = (bf16[384,1024]{1,0:T(8,128)(2,1)S(1)}, bf16[384,1024]{1,0:T(8,128)(2,1)S(1)}, u32[]{:S(2)}, u32[]{:S(2)}) collective-permute-start(bf16[384,1024]{1,0:T(8,128)(2,1)S(1)} %get-tuple-element.122), channel_id=1, source_target_pairs={{0,1},{1,0},{2,3},{3,2},{4,5},{5,4},{6,7},{7,6},{8,9},{9,8},{10,11... | collective-permute-start | bytes 2359304 | tf_op jit(solution)/shard_map/ppermute | solution.py:567
  47.9 39.7 %collective-permute-start.10 = (bf16[384,1024]{1,0:T(8,128)(2,1)S(1)}, bf16[384,1024]{1,0:T(8,128)(2,1)S(1)}, u32[]{:S(2)}, u32[]{:S(2)}) collective-permute-start(bf16[384,1024]{1,0:T(8,128)(2,1)S(1)} %get-tuple-element.121), channel_id=1, source_target_pairs={{0,2},{1,3},{2,0},{3,1},{4,6},{5,7},{6,4},{7,5},{8,10},{9,11},{10,... | collective-permute-start | bytes 2359304 | tf_op jit(solution)/shard_map/ppermute | solution.py:567
  48.2 39.4 %collective-permute-start.8 = (bf16[272,1024]{1,0:T(8,128)(2,1)S(1)}, bf16[272,1024]{1,0:T(8,128)(2,1)S(1)}, u32[]{:S(2)}, u32[]{:S(2)}) collective-permute-start(bf16[272,1024]{1,0:T(8,128)(2,1)S(1)} %copy-done.22), channel_id=1, source_target_pairs={{8,0},{12,4},{16,24},{20,28},{9,1},{13,5},{17,25},{21,29},{10,2},{... | collective-permute-start | bytes 1671176 | tf_op jit(solution)/shard_map/ppermute | solution.py:616
  87.6 0.9 copy-start.7
  87.6 1.2 copy-start.8
  87.8 2.0 copy-start.3
  89.0 14.9 %collective-permute-start.11 = (bf16[384,1024]{1,0:T(8,128)(2,1)S(1)}, bf16[384,1024]{1,0:T(8,128)(2,1)S(1)}, u32[]{:S(2)}, u32[]{:S(2)}) collective-permute-start(bf16[384,1024]{1,0:T(8,128)(2,1)S(1)} %get-tuple-element.120), channel_id=1, source_target_pairs={{0,1},{1,0},{2,3},{3,2},{4,5},{5,4},{6,7},{7,6},{8,9},{9,8},{10,11... | collective-permute-start | bytes 2359304 | tf_op jit(solution)/shard_map/ppermute | solution.py:567
  89.8 14.4 %collective-permute-start.12 = (bf16[384,1024]{1,0:T(8,128)(2,1)S(1)}, bf16[384,1024]{1,0:T(8,128)(2,1)S(1)}, u32[]{:S(2)}, u32[]{:S(2)}) collective-permute-start(bf16[384,1024]{1,0:T(8,128)(2,1)S(1)} %get-tuple-element.119), channel_id=1, source_target_pairs={{0,2},{1,3},{2,0},{3,1},{4,6},{5,7},{6,4},{7,5},{8,10},{9,11},{10,... | collective-permute-start | bytes 2359304 | tf_op jit(solution)/shard_map/ppermute | solution.py:567
  103.9 7.2 %copy-start.9 = (bf16[384,1024]{1,0:T(8,128)(2,1)}, bf16[384,1024]{1,0:T(8,128)(2,1)S(1)}, u32[]{:S(2)}) copy-start(bf16[384,1024]{1,0:T(8,128)(2,1)S(1)} %collective-permute-done.11.refs_7_) | copy-start | bytes 2359300
  104.2 7.0 %copy-start.10 = (bf16[384,1024]{1,0:T(8,128)(2,1)}, bf16[384,1024]{1,0:T(8,128)(2,1)S(1)}, u32[]{:S(2)}) copy-start(bf16[384,1024]{1,0:T(8,128)(2,1)S(1)} %collective-permute-done.12.refs_12_) | copy-start | bytes 2359300
  104.2 6.9 %collective-permute-start.13 = (bf16[128,1024]{1,0:T(8,128)(2,1)S(1)}, bf16[128,1024]{1,0:T(8,128)(2,1)S(1)}, u32[]{:S(2)}, u32[]{:S(2)}) collective-permute-start(bf16[128,1024]{1,0:T(8,128)(2,1)S(1)} %slice.73), channel_id=1, source_target_pairs={{0,1},{1,0},{2,3},{3,2},{4,5},{5,4},{6,7},{7,6},{8,9},{9,8},{10,11... | collective-permute-start | bytes 786440 | tf_op jit(solution)/shard_map/ppermute | solution.py:567
  105.2 6.7 %collective-permute-start.14 = (bf16[128,1024]{1,0:T(8,128)(2,1)S(1)}, bf16[128,1024]{1,0:T(8,128)(2,1)}, u32[]{:S(2)}, u32[]{:S(2)}) collective-permute-start(bf16[128,1024]{1,0:T(8,128)(2,1)S(1)} %slice.74), channel_id=1, source_target_pairs={{0,2},{1,3},{2,0},{3,1},{4,6},{5,7},{6,4},{7,5},{8,10},{9,11},{10,... | collective-permute-start | bytes 786440 | tf_op jit(solution)/shard_map/ppermute | solution.py:567
  111.2 13.1 %copy-start.24 = (bf16[128,1024]{1,0:T(8,128)(2,1)}, bf16[128,1024]{1,0:T(8,128)(2,1)S(1)}, u32[]{:S(2)}) copy-start(bf16[128,1024]{1,0:T(8,128)(2,1)S(1)} %collective-permute-done.13.refs_8_) | copy-start | bytes 786436
  112.0 12.3 %copy-start.1 = (bf16[4,512,768]{2,1,0:T(8,128)(2,1)}, bf16[4,512,768]{2,1,0:T(8,128)(2,1)S(1)}, u32[]{:S(2)}) copy-start(bf16[4,512,768]{2,1,0:T(8,128)(2,1)S(1)} %all-to-all-done.refs_14_) | copy-start | bytes 9437188
  112.0 37.0 %copy-start.13 = (bf16[1024,512]{1,0:T(8,128)(2,1)S(1)}, bf16[1024,512]{1,0:T(8,128)(2,1)}, u32[]{:S(2)}) copy-start(bf16[1024,512]{1,0:T(8,128)(2,1)} %refs_0_.4) | copy-start | bytes 3145732
  112.0 12.3 %collective-permute-start.15 = (bf16[4,512,768]{2,1,0:T(8,128)(2,1)S(1)}, bf16[4,512,768]{2,1,0:T(8,128)(2,1)S(1)}, u32[]{:S(2)}, u32[]{:S(2)}) collective-permute-start(bf16[4,512,768]{2,1,0:T(8,128)(2,1)S(1)} %all-to-all-done.refs_14_), channel_id=1, source_target_pairs={{0,4},{4,0},{8,12},{12,8},{16,20},{20,16},{24,28},{28,24},{1,5},{5... | collective-permute-start | bytes 9437192 | tf_op jit(solution)/shard_map/ppermute | solution.py:567
  119.0 26.0 %collective-permute-start.16 = (bf16[1024,512]{1,0:T(8,128)(2,1)}, bf16[1024,512]{1,0:T(8,128)(2,1)}, u32[]{:S(2)}, u32[]{:S(2)}) collective-permute-start(bf16[1024,512]{1,0:T(8,128)(2,1)} %refs_0_.4), channel_id=1, source_target_pairs={{0,8},{4,12},{8,0},{12,4},{16,24},{20,28},{24,16},{28,20},{1,9},{5... | collective-permute-start | bytes 3145736 | tf_op jit(solution)/shard_map/ppermute | solution.py:567
  121.2 26.6 %collective-permute-start.17 = (bf16[1024,512]{1,0:T(8,128)(2,1)}, bf16[1024,512]{1,0:T(8,128)(2,1)}, u32[]{:S(2)}, u32[]{:S(2)}) collective-permute-start(bf16[1024,512]{1,0:T(8,128)(2,1)} %refs_0_.4), channel_id=1, source_target_pairs={{8,16},{12,20},{16,8},{20,12},{9,17},{13,21},{17,9},{21,13},{10,18... | collective-permute-start | bytes 3145736 | tf_op jit(solution)/shard_map/ppermute | solution.py:636
  124.3 1.7 copy-start.5
  147.8 13.8 %collective-permute-start.18 = (bf16[4,256,256]{2,1,0:T(8,128)(2,1)}, bf16[4,256,256]{2,1,0:T(8,128)(2,1)S(1)}, u32[]{:S(2)}, u32[]{:S(2)}) collective-permute-start(bf16[4,256,256]{2,1,0:T(8,128)(2,1)} %shard_map.91.refs_2_), channel_id=1, source_target_pairs={{0,8},{4,12},{8,0},{12,4},{16,24},{20,28},{24,16},{28,20},{1,9},{5... | collective-permute-start | bytes 1572872 | tf_op jit(solution)/shard_map/ppermute | solution.py:567
  147.8 13.8 %collective-permute-start.19 = (bf16[4,256,256]{2,1,0:T(8,128)(2,1)}, bf16[4,256,256]{2,1,0:T(8,128)(2,1)S(1)}, u32[]{:S(2)}, u32[]{:S(2)}) collective-permute-start(bf16[4,256,256]{2,1,0:T(8,128)(2,1)} %shard_map.91.refs_2_), channel_id=1, source_target_pairs={{0,4},{4,0},{8,12},{12,8},{16,20},{20,16},{24,28},{28,24},{1,5},{5... | collective-permute-start | bytes 1572872 | tf_op jit(solution)/shard_map/ppermute | solution.py:567
  149.0 14.0 %collective-permute-start.23 = (bf16[1024,512]{1,0:T(8,128)(2,1)S(1)}, bf16[1024,512]{1,0:T(8,128)(2,1)S(1)}, u32[]{:S(2)}, u32[]{:S(2)}) collective-permute-start(bf16[1024,512]{1,0:T(8,128)(2,1)S(1)} %copy-done.13), channel_id=1, source_target_pairs={{0,4},{4,0},{8,12},{12,8},{16,20},{20,16},{24,28},{28,24},{1,5},{5... | collective-permute-start | bytes 3145736 | tf_op jit(solution)/shard_map/ppermute | solution.py:567
  149.1 26.4 %collective-permute-start.22 = (bf16[1024,512]{1,0:T(8,128)(2,1)}, bf16[1024,512]{1,0:T(8,128)(2,1)S(1)}, u32[]{:S(2)}, u32[]{:S(2)}) collective-permute-start(bf16[1024,512]{1,0:T(8,128)(2,1)} %collective-permute-done.16.refs_2_), channel_id=1, source_target_pairs={{8,16},{12,20},{16,8},{20,12},{9,17},{13,21},{17,9},{21,13},{10,18... | collective-permute-start | bytes 3145736 | tf_op jit(solution)/shard_map/ppermute | solution.py:645
  161.6 15.1 %copy-start.26 = (bf16[4,256,256]{2,1,0:T(8,128)(2,1)}, bf16[4,256,256]{2,1,0:T(8,128)(2,1)S(1)}, u32[]{:S(2)}) copy-start(bf16[4,256,256]{2,1,0:T(8,128)(2,1)S(1)} %collective-permute-done.18.refs_3_) | copy-start | bytes 1572868
  161.6 15.1 %copy-start.27 = (bf16[4,256,256]{2,1,0:T(8,128)(2,1)}, bf16[4,256,256]{2,1,0:T(8,128)(2,1)S(1)}, u32[]{:S(2)}) copy-start(bf16[4,256,256]{2,1,0:T(8,128)(2,1)S(1)} %collective-permute-done.19.refs_4_) | copy-start | bytes 1572868
  161.7 15.1 %collective-permute-start.20 = (bf16[4,256,256]{2,1,0:T(8,128)(2,1)}, bf16[4,256,256]{2,1,0:T(8,128)(2,1)S(1)}, u32[]{:S(2)}, u32[]{:S(2)}) collective-permute-start(bf16[4,256,256]{2,1,0:T(8,128)(2,1)} %get-tuple-element.84), channel_id=1, source_target_pairs={{0,4},{4,0},{8,12},{12,8},{16,20},{20,16},{24,28},{28,24},{1,5},{5... | collective-permute-start | bytes 1572872 | tf_op jit(solution)/shard_map/ppermute | solution.py:567
  162.4 14.3 %collective-permute-start.21 = (bf16[4,256,256]{2,1,0:T(8,128)(2,1)S(1)}, bf16[4,256,256]{2,1,0:T(8,128)(2,1)S(1)}, u32[]{:S(2)}, u32[]{:S(2)}) collective-permute-start(bf16[4,256,256]{2,1,0:T(8,128)(2,1)S(1)} %collective-permute-done.18.refs_3_), channel_id=1, source_target_pairs={{0,4},{4,0},{8,12},{12,8},{16,20},{20,16},{24,28},{28,24},{1,5},{5... | collective-permute-start | bytes 1572872 | tf_op jit(solution)/shard_map/ppermute | solution.py:567
  162.5 35.4 %collective-permute-start.26 = (bf16[1024,512]{1,0:T(8,128)(2,1)}, bf16[1024,512]{1,0:T(8,128)(2,1)S(1)}, u32[]{:S(2)}, u32[]{:S(2)}) collective-permute-start(bf16[1024,512]{1,0:T(8,128)(2,1)} %collective-permute-done.16.refs_2_), channel_id=1, source_target_pairs={{0,4},{4,0},{8,12},{12,8},{16,20},{20,16},{24,28},{28,24},{1,5},{5... | collective-permute-start | bytes 3145736 | tf_op jit(solution)/shard_map/ppermute | solution.py:567
  162.9 1.0 copy-start.14
  163.9 34.0 %collective-permute-start.24 = (bf16[1024,512]{1,0:T(8,128)(2,1)}, bf16[1024,512]{1,0:T(8,128)(2,1)S(1)}, u32[]{:S(2)}, u32[]{:S(2)}) collective-permute-start(bf16[1024,512]{1,0:T(8,128)(2,1)} %collective-permute-done.17.refs_4_), channel_id=1, source_target_pairs={{8,0},{12,4},{16,24},{20,28},{9,1},{13,5},{17,25},{21,29},{10,2},{... | collective-permute-start | bytes 3145736 | tf_op jit(solution)/shard_map/ppermute | solution.py:646
  175.5 22.4 %copy-start.15 = (bf16[1024,512]{1,0:T(8,128)(2,1)}, bf16[1024,512]{1,0:T(8,128)(2,1)S(1)}, u32[]{:S(2)}) copy-start(bf16[1024,512]{1,0:T(8,128)(2,1)S(1)} %collective-permute-done.22.refs_8_) | copy-start | bytes 3145732
  175.5 22.5 %collective-permute-start.27 = (bf16[1024,512]{1,0:T(8,128)(2,1)}, bf16[1024,512]{1,0:T(8,128)(2,1)}, u32[]{:S(2)}, u32[]{:S(2)}) collective-permute-start(bf16[1024,512]{1,0:T(8,128)(2,1)} %collective-permute-done.17.refs_4_), channel_id=1, source_target_pairs={{0,4},{4,0},{8,12},{12,8},{16,20},{20,16},{24,28},{28,24},{1,5},{5... | collective-permute-start | bytes 3145736 | tf_op jit(solution)/shard_map/ppermute | solution.py:567
  178.3 33.0 %collective-permute-start.25 = (bf16[1024,512]{1,0:T(8,128)(2,1)S(1)}, bf16[1024,512]{1,0:T(8,128)(2,1)}, u32[]{:S(2)}, u32[]{:S(2)}) collective-permute-start(bf16[1024,512]{1,0:T(8,128)(2,1)S(1)} %collective-permute-done.22.refs_8_), channel_id=1, source_target_pairs={{8,0},{12,4},{16,24},{20,28},{9,1},{13,5},{17,25},{21,29},{10,2},{... | collective-permute-start | bytes 3145736 | tf_op jit(solution)/shard_map/ppermute | solution.py:655
  197.9 14.3 %copy-start.17 = (bf16[1024,512]{1,0:T(8,128)(2,1)}, bf16[1024,512]{1,0:T(8,128)(2,1)S(1)}, u32[]{:S(2)}) copy-start(bf16[1024,512]{1,0:T(8,128)(2,1)S(1)} %collective-permute-done.24.refs_6_) | copy-start | bytes 3145732
  197.9 14.2 %copy-start.16 = (bf16[1024,512]{1,0:T(8,128)(2,1)}, bf16[1024,512]{1,0:T(8,128)(2,1)S(1)}, u32[]{:S(2)}) copy-start(bf16[1024,512]{1,0:T(8,128)(2,1)S(1)} %collective-permute-done.26.refs_3_) | copy-start | bytes 3145732
  211.3 3.3 %collective-permute-start.28 = (bf16[4,256,512]{2,1,0:T(8,128)(2,1)}, bf16[4,256,512]{2,1,0:T(8,128)(2,1)S(1)}, u32[]{:S(2)}, u32[]{:S(2)}) collective-permute-start(bf16[4,256,512]{2,1,0:T(8,128)(2,1)} %get-tuple-element.95), channel_id=1, source_target_pairs={{0,4},{4,0},{8,12},{12,8},{16,20},{20,16},{24,28},{28,24},{1,5},{5... | collective-permute-start | bytes 3145736 | tf_op jit(solution)/shard_map/ppermute | solution.py:567
  217.4 7.4 %copy-start.25 = (s32[9]{0:T(128)S(1)}, s32[9]{0:T(128)}, u32[]{:S(2)}) copy-start(s32[9]{0:T(128)} %stack.78.place) | copy-start | bytes 112
  217.4 28.7 %all-to-all-start.1 = ((bf16[4,256,512]{2,1,0:T(8,128)(2,1)}), bf16[4,256,512]{2,1,0:T(8,128)(2,1)S(1)}, u32[]{:S(2)}, u32[]{:S(2)}) async-start(bf16[4,256,512]{2,1,0:T(8,128)(2,1)} %get-tuple-element.105), calls=%async_computation.1 | async-start | bytes 2097152 | tf_op jit(solution)/shard_map/all_to_all | solution.py:670
  223.6 3.3 %collective-permute-start.30 = (bf16[1024,512]{1,0:T(8,128)(2,1)}, bf16[1024,512]{1,0:T(8,128)(2,1)}, u32[]{:S(2)}, u32[]{:S(2)}) collective-permute-start(bf16[1024,512]{1,0:T(8,128)(2,1)} %copy-done.15), channel_id=1, source_target_pairs={{0,4},{4,0},{8,12},{12,8},{16,20},{20,16},{24,28},{28,24},{1,5},{5... | collective-permute-start | bytes 3145736 | tf_op jit(solution)/shard_map/ppermute | solution.py:567
  224.2 4.1 %collective-permute-start.29 = (bf16[1024,512]{1,0:T(8,128)(2,1)}, bf16[1024,512]{1,0:T(8,128)(2,1)}, u32[]{:S(2)}, u32[]{:S(2)}) collective-permute-start(bf16[1024,512]{1,0:T(8,128)(2,1)} %copy-done.17), channel_id=1, source_target_pairs={{0,4},{4,0},{8,12},{12,8},{16,20},{20,16},{24,28},{28,24},{1,5},{5... | collective-permute-start | bytes 3145736 | tf_op jit(solution)/shard_map/ppermute | solution.py:567
  224.2 5.6 %collective-permute-start.31 = (bf16[1024,512]{1,0:T(8,128)(2,1)}, bf16[1024,512]{1,0:T(8,128)(2,1)}, u32[]{:S(2)}, u32[]{:S(2)}) collective-permute-start(bf16[1024,512]{1,0:T(8,128)(2,1)} %collective-permute-done.25.refs_10_), channel_id=1, source_target_pairs={{0,4},{4,0},{8,12},{12,8},{16,20},{20,16},{24,28},{28,24},{1,5},{5... | collective-permute-start | bytes 3145736 | tf_op jit(solution)/shard_map/ppermute | solution.py:567
  246.1 1.0 copy-start.4
  255.3 13.5 %collective-permute-start.34 = (bf16[256,1024]{1,0:T(8,128)(2,1)}, bf16[256,1024]{1,0:T(8,128)(2,1)S(1)}, u32[]{:S(2)}, u32[]{:S(2)}) collective-permute-start(bf16[256,1024]{1,0:T(8,128)(2,1)} %get-tuple-element.104), channel_id=1, source_target_pairs={{0,3},{1,2},{2,1},{3,0},{4,7},{5,6},{6,5},{7,4},{8,11},{9,10},{10,... | collective-permute-start | bytes 1572872 | tf_op jit(solution)/shard_map/ppermute | solution.py:567
  255.7 24.7 %collective-permute-start.33 = (bf16[256,1024]{1,0:T(8,128)(2,1)}, bf16[256,1024]{1,0:T(8,128)(2,1)S(1)}, u32[]{:S(2)}, u32[]{:S(2)}) collective-permute-start(bf16[256,1024]{1,0:T(8,128)(2,1)} %get-tuple-element.103), channel_id=1, source_target_pairs={{0,2},{1,3},{2,0},{3,1},{4,6},{5,7},{6,4},{7,5},{8,10},{9,11},{10,... | collective-permute-start | bytes 1572872 | tf_op jit(solution)/shard_map/ppermute | solution.py:567
  257.0 23.4 %collective-permute-start.32 = (bf16[256,1024]{1,0:T(8,128)(2,1)}, bf16[256,1024]{1,0:T(8,128)(2,1)S(1)}, u32[]{:S(2)}, u32[]{:S(2)}) collective-permute-start(bf16[256,1024]{1,0:T(8,128)(2,1)} %get-tuple-element.102), channel_id=1, source_target_pairs={{0,1},{1,0},{2,3},{3,2},{4,5},{5,4},{6,7},{7,6},{8,9},{9,8},{10,11... | collective-permute-start | bytes 1572872 | tf_op jit(solution)/shard_map/ppermute | solution.py:567
  (3 other events, 2.4 us)
